TPU v7x, 32 devices: a whole 2x2x4 slice. The times are simulated.
32 devices in a mesh: dp: 8 (over z, x), tensor: 4 (over y, core).
Axes of the slice: x: 2, y: 2, z: 4, core: 2. Of those that a mesh axis runs over, the one named last changes fastest.
Arguments:
- inputs: bfloat16 [16, 1024, 1024], P('dp', 'tensor'), may hold values from -6 to 6
- lengths: int32 [16], P('dp'), may hold values from 1 to 1024, as said below
- w_query: bfloat16 [1024, 1024], P('dp', 'tensor'), may hold values from -0.1875 to 0.1875
- w_key: bfloat16 [1024, 1024], P('dp', 'tensor'), may hold values from -0.1875 to 0.1875
- w_value: bfloat16 [1024, 1024], P('dp', 'tensor'), may hold values from -0.1875 to 0.1875
- w_out: bfloat16 [1024, 1024], P('tensor', 'dp'), may hold values from -4 to 4
- w_up: bfloat16 [1024, 4096], P('dp', 'tensor'), may hold values from -0.1875 to 0.1875
- w_down: bfloat16 [4096, 1024], P('tensor', 'dp'), may hold values from -0.09375 to 0.09375
- b_query: float32 [1024], P('tensor'), may hold values from -3 to 3
- b_value: float32 [1024], P('tensor'), may hold values from -3 to 3
- b_out: float32 [1024], replicated, may hold values from -3 to 3
- b_up: float32 [4096], P('tensor'), may hold values from -3 to 3
- b_down: float32 [1024], replicated, may hold values from -3 to 3
- first_gain: float32 [1024], replicated, may hold values from 0.5 to 1.5
- first_shift: float32 [1024], replicated, may hold values from -3 to 3
- second_gain: float32 [1024], replicated, may hold values from 0.5 to 1.5
- second_shift: float32 [1024], replicated, may hold values from -3 to 3
- cotangent: bfloat16 [16, 1024, 1024], P('dp', 'tensor'), may hold values from -6 to 6
Outputs:
- output: bfloat16 [16, 1024, 1024], P('dp', 'tensor')
- input_grad: bfloat16 [16, 1024, 1024], P('dp', 'tensor')
- w_query_grad: float32 [1024, 1024], P('dp', 'tensor')
- w_key_grad: float32 [1024, 1024], P('dp', 'tensor')
- w_value_grad: float32 [1024, 1024], P('dp', 'tensor')
- w_out_grad: float32 [1024, 1024], P('tensor', 'dp')
- w_up_grad: float32 [1024, 4096], P('dp', 'tensor')
- w_down_grad: float32 [4096, 1024], P('tensor', 'dp')
- b_query_grad: float32 [1024], replicated
- b_value_grad: float32 [1024], replicated
- b_out_grad: float32 [1024], replicated
- b_up_grad: float32 [4096], replicated
- b_down_grad: float32 [1024], replicated
- first_gain_grad: float32 [1024], replicated
- first_shift_grad: float32 [1024], replicated
- second_gain_grad: float32 [1024], replicated
- second_shift_grad: float32 [1024], replicated
Inputs may be any that keep to these rules, and one draw needn't show every extreme that they name: `lengths`: in each aligned block of 2 sequences (those of one index of dp) one sequence, drawn from the seed, has the full length 1024; positions at or past a sequence's length are padding.
All inputs are finite; a program needn't handle non-finite values.
Results may differ from a plain program's by a relative error of at most 0.02.
Values may be sent and summed in bfloat16 or wider, within the bound.
No kernel may reach another device: no remote copies, remote signals or barrier semaphores. Data moves between devices by JAX's collectives and lax.ppermute only.
A program may use at most 128 MiB of HBM per device.

v0:
```python
import math

import jax
import jax.numpy as jnp
from jax import lax
from jax.sharding import PartitionSpec as P

D = 1024
HEADS = 16
FF = 4096
ROWS_BLOCK = 512


NORM_EPS = 1e-12
MASKED = -1000000000.0


def normalize(summed, norm_gain, norm_shift):
    centre = jnp.mean(summed, axis=-1, keepdims=True)
    centred = summed - centre
    spread = jnp.mean(centred * centred, axis=-1, keepdims=True)
    return centred * lax.rsqrt(spread + NORM_EPS) * norm_gain + norm_shift


def exact_gelu(values_in):
    return jax.nn.gelu(values_in, approximate=False)


def matmul(factor_one, factor_two):
    return jnp.dot(factor_one, factor_two, preferred_element_type=jnp.float32)


def matmul_tn(factor_one, factor_two):
    return lax.dot_general(
        factor_one, factor_two, (((0,), (0,)), ((), ())), preferred_element_type=jnp.float32
    )


def matmul_nt(factor_one, factor_two):
    return lax.dot_general(
        factor_one, factor_two, (((1,), (1,)), ((), ())), preferred_element_type=jnp.float32
    )


def fetch_weights(w_query, w_key, w_value, w_out, w_up, w_down):
    return (
        lax.all_gather(w_query, "dp", axis=0, tiled=True),
        lax.all_gather(w_key, "dp", axis=0, tiled=True),
        lax.all_gather(w_value, "dp", axis=0, tiled=True),
        lax.all_gather(w_out, "dp", axis=1, tiled=True),
        lax.all_gather(w_up, "dp", axis=0, tiled=True),
        lax.all_gather(w_down, "dp", axis=1, tiled=True),
    )


def block_scores(query_block, key_seq, visible, head_count, scaling):
    row_count = query_block.shape[0]
    head_size = key_seq.shape[1] // head_count
    query_heads = query_block.reshape(row_count, head_count, head_size)
    key_heads = key_seq.reshape(key_seq.shape[0], head_count, head_size)
    scores = (
        jnp.einsum("qhe,khe->hqk", query_heads, key_heads, preferred_element_type=jnp.float32)
        * scaling
    )
    return jnp.where(visible[None, None, :], scores, MASKED)


def attention_forward(queries, keys_all, values_all, lengths, head_count):
    seq_count, seq_len, head_dims = queries.shape
    per_seq = seq_len // ROWS_BLOCK
    head_size = head_dims // head_count
    scaling = 1.0 / math.sqrt(head_size)
    positions = jnp.arange(seq_len, dtype=jnp.int32)

    def attention_one_block(block_id):
        seq_id = block_id // per_seq
        row_start = block_id % per_seq * ROWS_BLOCK
        query_block = lax.dynamic_slice(
            queries, (seq_id, row_start, 0), (1, ROWS_BLOCK, head_dims)
        )[0]
        key_seq = lax.dynamic_index_in_dim(keys_all, seq_id, 0, keepdims=False)
        value_seq = lax.dynamic_index_in_dim(values_all, seq_id, 0, keepdims=False)
        visible = positions < lengths[seq_id]
        scores = block_scores(query_block, key_seq, visible, head_count, scaling)
        row_peak = jnp.max(scores, axis=-1, keepdims=True)
        weights = jnp.exp(scores - row_peak)
        row_total = jnp.sum(weights, axis=-1, keepdims=True)
        attention = (weights / row_total).astype(jnp.bfloat16)
        value_heads = value_seq.reshape(seq_len, head_count, head_size)
        context = jnp.einsum(
            "hqk,khe->qhe", attention, value_heads, preferred_element_type=jnp.float32
        )
        log_total = (row_peak + jnp.log(row_total))[..., 0]
        return (context.reshape(ROWS_BLOCK, head_dims).astype(jnp.bfloat16), log_total)

    context, log_totals = lax.map(
        attention_one_block, jnp.arange(seq_count * per_seq, dtype=jnp.int32)
    )
    return (context.reshape(seq_count, seq_len, head_dims), log_totals)


def attention_backward(
    queries, keys_all, values_all, grad_context, log_totals, lengths, head_count
):
    seq_count, seq_len, head_dims = queries.shape
    per_seq = seq_len // ROWS_BLOCK
    head_size = head_dims // head_count
    scaling = 1.0 / math.sqrt(head_size)
    positions = jnp.arange(seq_len, dtype=jnp.int32)

    def one_sequence(seq_id):
        query_seq = lax.dynamic_index_in_dim(queries, seq_id, 0, keepdims=False)
        key_seq = lax.dynamic_index_in_dim(keys_all, seq_id, 0, keepdims=False)
        value_seq = lax.dynamic_index_in_dim(values_all, seq_id, 0, keepdims=False)
        grad_seq = lax.dynamic_index_in_dim(grad_context, seq_id, 0, keepdims=False)
        visible = positions < lengths[seq_id]
        key_heads = key_seq.reshape(seq_len, head_count, head_size)
        value_heads = value_seq.reshape(seq_len, head_count, head_size)

        def one_one_block(carry, part_id):
            key_acc, value_acc = carry
            row_start = part_id * ROWS_BLOCK
            query_block = lax.dynamic_slice_in_dim(query_seq, row_start, ROWS_BLOCK, 0)
            grad_block = lax.dynamic_slice_in_dim(grad_seq, row_start, ROWS_BLOCK, 0)
            log_block = log_totals[seq_id * per_seq + part_id]
            scores = block_scores(query_block, key_seq, visible, head_count, scaling)
            attention = jnp.exp(scores - log_block[..., None])
            grad_heads = grad_block.reshape(ROWS_BLOCK, head_count, head_size)
            query_heads = query_block.reshape(ROWS_BLOCK, head_count, head_size)
            grad_probs = jnp.einsum(
                "qhe,khe->hqk", grad_heads, value_heads, preferred_element_type=jnp.float32
            )
            inner = jnp.sum(attention * grad_probs, axis=-1, keepdims=True)
            grad_scores = (attention * (grad_probs - inner)).astype(jnp.bfloat16)
            grad_query = (
                jnp.einsum(
                    "hqk,khe->qhe", grad_scores, key_heads, preferred_element_type=jnp.float32
                )
                * scaling
            )
            key_acc = (
                key_acc
                + jnp.einsum(
                    "hqk,qhe->khe", grad_scores, query_heads, preferred_element_type=jnp.float32
                )
                * scaling
            )
            value_acc = value_acc + jnp.einsum(
                "hqk,qhe->khe",
                attention.astype(jnp.bfloat16),
                grad_heads,
                preferred_element_type=jnp.float32,
            )
            return (
                (key_acc, value_acc),
                grad_query.reshape(ROWS_BLOCK, head_dims).astype(jnp.bfloat16),
            )

        zero_acc = jnp.zeros((seq_len, head_count, head_size), jnp.float32)
        (key_acc, value_acc), grad_query = lax.scan(
            one_one_block, (zero_acc, zero_acc), jnp.arange(per_seq, dtype=jnp.int32)
        )
        return (
            grad_query.reshape(seq_len, head_dims),
            key_acc.reshape(seq_len, head_dims).astype(jnp.bfloat16),
            value_acc.reshape(seq_len, head_dims).astype(jnp.bfloat16),
        )

    return lax.map(one_sequence, jnp.arange(seq_count, dtype=jnp.int32))


def shards(
    inputs,
    lengths,
    w_query,
    w_key,
    w_value,
    w_out,
    w_up,
    w_down,
    b_query,
    b_value,
    b_out,
    b_up,
    b_down,
    first_gain,
    first_shift,
    second_gain,
    second_shift,
    cotangent,
):
    head_count = HEADS // lax.axis_size("tensor")
    weights_now = fetch_weights(w_query, w_key, w_value, w_out, w_up, w_down)
    full_query, full_key, full_value, full_out, full_up, full_down = weights_now
    gathered = lax.all_gather(inputs, "tensor", axis=1, tiled=True)
    seq_count, seq_len, model_width = gathered.shape
    token_rows = gathered.reshape(seq_count * seq_len, model_width)
    head_dims = full_query.shape[1]
    queries = (
        (matmul(token_rows, full_query) + b_query)
        .astype(jnp.bfloat16)
        .reshape(seq_count, seq_len, head_dims)
    )
    keys_all = (
        matmul(token_rows, full_key).astype(jnp.bfloat16).reshape(seq_count, seq_len, head_dims)
    )
    values_all = (
        (matmul(token_rows, full_value) + b_value)
        .astype(jnp.bfloat16)
        .reshape(seq_count, seq_len, head_dims)
    )
    context, log_totals = attention_forward(queries, keys_all, values_all, lengths, head_count)
    context_rows = context.reshape(seq_count * seq_len, head_dims)
    partial_value = matmul(context_rows, full_out).reshape(seq_count, seq_len, model_width)
    attended = lax.psum_scatter(
        partial_value.astype(jnp.bfloat16), "tensor", scatter_dimension=1, tiled=True
    ).astype(jnp.float32)
    residual_one = inputs.astype(jnp.float32) + attended + b_out
    normed, first_back = jax.vjp(normalize, residual_one, first_gain, first_shift)
    spread_rows = lax.all_gather(normed.astype(jnp.bfloat16), "tensor", axis=1, tiled=True)
    first_rows = spread_rows.reshape(seq_count * seq_len, model_width)
    hidden = matmul(first_rows, full_up) + b_up
    active, gelu_back = jax.vjp(exact_gelu, hidden)
    active_low = active.astype(jnp.bfloat16)
    partial_two = matmul(active_low, full_down).reshape(seq_count, seq_len, model_width)
    branch = lax.psum_scatter(
        partial_two.astype(jnp.bfloat16), "tensor", scatter_dimension=1, tiled=True
    ).astype(jnp.float32)
    residual_two = normed + branch + b_down
    final, second_back = jax.vjp(normalize, residual_two, second_gain, second_shift)
    output = final.astype(jnp.bfloat16)
    weights_now = fetch_weights(w_query, w_key, w_value, w_out, w_up, w_down)
    full_query, full_key, full_value, full_out, full_up, full_down = weights_now
    grad_second, second_gain_grad, second_shift_grad = second_back(cotangent.astype(jnp.float32))
    b_down_grad = jnp.sum(grad_second, axis=(0, 1))
    grad_rows = lax.all_gather(
        grad_second.astype(jnp.bfloat16), "tensor", axis=1, tiled=True
    ).reshape(seq_count * seq_len, model_width)
    w_down_grad = matmul_tn(active_low, grad_rows)
    grad_active = matmul_nt(grad_rows, full_down)
    grad_hidden = gelu_back(grad_active)[0].astype(jnp.bfloat16)
    w_up_grad = matmul_tn(first_rows, grad_hidden)
    b_up_part = jnp.sum(grad_hidden.astype(jnp.float32), axis=0)
    back_first = matmul_nt(grad_hidden, full_up).reshape(seq_count, seq_len, model_width)
    grad_normed = grad_second + lax.psum_scatter(
        back_first.astype(jnp.bfloat16), "tensor", scatter_dimension=1, tiled=True
    ).astype(jnp.float32)
    grad_first, first_gain_grad, first_shift_grad = first_back(grad_normed)
    b_out_grad = jnp.sum(grad_first, axis=(0, 1))
    grad_attended = lax.all_gather(
        grad_first.astype(jnp.bfloat16), "tensor", axis=1, tiled=True
    ).reshape(seq_count * seq_len, model_width)
    w_out_grad = matmul_tn(context_rows, grad_attended)
    grad_context = (
        matmul_nt(grad_attended, full_out)
        .astype(jnp.bfloat16)
        .reshape(seq_count, seq_len, head_dims)
    )
    grad_queries, grad_keys, grad_values = attention_backward(
        queries, keys_all, values_all, grad_context, log_totals, lengths, head_count
    )
    query_rows = grad_queries.reshape(seq_count * seq_len, head_dims)
    key_grad_rows = grad_keys.reshape(seq_count * seq_len, head_dims)
    value_grad_rows = grad_values.reshape(seq_count * seq_len, head_dims)
    w_query_grad = matmul_tn(token_rows, query_rows)
    w_key_grad = matmul_tn(token_rows, key_grad_rows)
    w_value_grad = matmul_tn(token_rows, value_grad_rows)
    b_query_part = jnp.sum(query_rows.astype(jnp.float32), axis=0)
    b_value_part = jnp.sum(value_grad_rows.astype(jnp.float32), axis=0)
    back_inputs = (
        matmul_nt(query_rows, full_query)
        + matmul_nt(key_grad_rows, full_key)
        + matmul_nt(value_grad_rows, full_value)
    ).reshape(seq_count, seq_len, model_width)
    input_grad = (
        grad_first
        + lax.psum_scatter(
            back_inputs.astype(jnp.bfloat16), "tensor", scatter_dimension=1, tiled=True
        ).astype(jnp.float32)
    ).astype(jnp.bfloat16)
    w_query_grad, w_key_grad, w_value_grad, w_out_grad, w_up_grad, w_down_grad = (
        lax.psum_scatter(w_query_grad, "dp", scatter_dimension=0, tiled=True),
        lax.psum_scatter(w_key_grad, "dp", scatter_dimension=0, tiled=True),
        lax.psum_scatter(w_value_grad, "dp", scatter_dimension=0, tiled=True),
        lax.psum_scatter(w_out_grad, "dp", scatter_dimension=1, tiled=True),
        lax.psum_scatter(w_up_grad, "dp", scatter_dimension=0, tiled=True),
        lax.psum_scatter(w_down_grad, "dp", scatter_dimension=1, tiled=True),
    )
    tensor_pos = lax.axis_index("tensor")

    def placed_in(vector, full_len):
        return lax.dynamic_update_slice(
            jnp.zeros((full_len,), jnp.float32), vector, (tensor_pos * vector.shape[0],)
        )

    smalls = lax.psum(
        (
            placed_in(b_query_part, D),
            placed_in(b_value_part, D),
            b_out_grad,
            placed_in(b_up_part, FF),
            b_down_grad,
            first_gain_grad,
            first_shift_grad,
            second_gain_grad,
            second_shift_grad,
        ),
        ("dp", "tensor"),
    )
    return (
        output,
        input_grad,
        w_query_grad,
        w_key_grad,
        w_value_grad,
        w_out_grad,
        w_up_grad,
        w_down_grad,
        smalls[0],
        smalls[1],
        smalls[2],
        smalls[3],
        smalls[4],
        smalls[5],
        smalls[6],
        smalls[7],
        smalls[8],
    )


def solution(mesh):
    placed = (
        P("dp", "tensor", None),
        P("dp"),
        P("dp", "tensor"),
        P("dp", "tensor"),
        P("dp", "tensor"),
        P("tensor", "dp"),
        P("dp", "tensor"),
        P("tensor", "dp"),
        P("tensor"),
        P("tensor"),
        P(),
        P("tensor"),
        P(),
        P(),
        P(),
        P(),
        P(),
        P("dp", "tensor", None),
    )
    return jax.shard_map(
        shards,
        mesh=mesh,
        in_specs=placed,
        out_specs=(
            P("dp", "tensor", None),
            P("dp", "tensor", None),
            P("dp", "tensor"),
            P("dp", "tensor"),
            P("dp", "tensor"),
            P("tensor", "dp"),
            P("dp", "tensor"),
            P("tensor", "dp"),
            P(),
            P(),
            P(),
            P(),
            P(),
            P(),
            P(),
            P(),
            P(),
        ),
        check_vma=False,
    )
```

profile of v0, /device:TPU:0, one launch (start us, length us, event | category | flops | bytes accessed | tf_op | source)
XLA Modules:
  0.0 1155.1 jit_solution(15563760866401505360)
XLA Ops:
  8.8 33.2 %all_gather.38 = bf16[1024,256]{1,0:T(8,128)(2,1)S(1)} all-gather(bf16[128,256]{1,0:T(8,128)(2,1)} %param.26), channel_id=1, replica_groups=mesh['dp'=8,'tensor'=4] {'dp'}, dimensions={0}, use_global_device_ids=true | all-gather | bytes 589824 | tf_op jit(solution)/shard_map/all_gather | solution.py:47
  42.0 33.6 %all_gather.39 = bf16[1024,256]{1,0:T(8,128)(2,1)} all-gather(bf16[128,256]{1,0:T(8,128)(2,1)} %param.27), channel_id=1, replica_groups=mesh['dp'=8,'tensor'=4] {'dp'}, dimensions={0}, use_global_device_ids=true | all-gather | bytes 589824 | tf_op jit(solution)/shard_map/all_gather | solution.py:48
  75.6 31.7 %all_gather.37 = bf16[1024,256]{1,0:T(8,128)(2,1)S(1)} all-gather(bf16[128,256]{1,0:T(8,128)(2,1)} %param.28), channel_id=1, replica_groups=mesh['dp'=8,'tensor'=4] {'dp'}, dimensions={0}, use_global_device_ids=true | all-gather | bytes 589824 | tf_op jit(solution)/shard_map/all_gather | solution.py:49
  107.3 28.4 %all_gather.40 = bf16[256,1024]{1,0:T(8,128)(2,1)} all-gather(bf16[256,128]{1,0:T(8,128)(2,1)} %param.29), channel_id=1, replica_groups=mesh['dp'=8,'tensor'=4] {'dp'}, dimensions={1}, use_global_device_ids=true | all-gather | bytes 589824 | tf_op jit(solution)/shard_map/all_gather | solution.py:50
  135.7 4.4 fusion.31
  141.7 4.5 convolution_convert_fusion.4
  146.2 2.3 copy.52
  148.5 4.4 fusion.32
  152.9 2.3 copy.51
  155.2 50.7 %while.48 = (s32[]{:T(128)}, bf16[4,512,256]{2,1,0:T(8,128)(2,1)S(1)}, f32[4,4,512]{2,1,0:T(4,128)S(1)}, s32[4]{0:T(128)S(1)}, bf16[2,1024,256]{1,2,0:T(8,128)(2...) while((s32[]{:T(128)}, ...), condition=%wide.region_3.4_spmd.clone, body=%wide.region_0.3_spmd.clone.sunk | while | flops 562166784 | bytes 30478792 | solution.py:96
  163.1 2.0 fusion.127
  165.2 2.5 fusion.128
  175.8 2.0 fusion.127
  177.8 2.5 fusion.128
  188.5 2.0 fusion.127
  190.5 2.5 fusion.128
  201.2 2.0 fusion.127
  203.2 2.5 fusion.128
  205.9 4.7 convolution_convert_fusion.2
  211.6 43.0 %reduce-scatter.11.cloned.1.call-done = bf16[2,256,1024]{2,1,0:T(8,128)(2,1)} async-done(((bf16[2,1024,1024]{2,1,0:T(8,128)(2,1)}), bf16[2,256,1024]{2,1,0:T(8,128)(2,1)}) %reduce-scatter.11.cloned.1.call-update) | async-done | bytes 1048592 | tf_op jit(solution)/shard_map/reduce_scatter | solution.py:215
  261.8 34.9 %all-gather.9.cloned.1.call-done = bf16[2,1024,1024]{2,1,0:T(8,128)(2,1)} async-done(((bf16[2,256,1024]{2,1,0:T(8,128)(2,1)}), bf16[2,1024,1024]{2,1,0:T(8,128)(2,1)}) %all-gather.9.cloned.1.call-update) | async-done | bytes 4194320 | tf_op jit(solution)/shard_map/all_gather | solution.py:220
  296.7 26.3 %multiply_convert_fusion.1 = (bf16[2048,1024]{1,0:T(8,128)(2,1)}, f32[2048,1024]{1,0:T(8,128)}, f32[2048,1024]{1,0:T(8,128)}) fusion(f32[1024]{0:T(1024)S(1)} %copy-done.41, bf16[2048,1024]{1,0:T(8,128)(2,1)} %bitcast.222, bf16[1024,1024]{1,0:T(8,128)(2,1)} %all-gather.11.cloned.1.call-done), kind=kOutput, calls=%fused_computation.49 | convolution fusion | flops 4433379328 | bytes 27267072 | tf_op jit(solution)/shard_map/dot_general | solution.py:30
  323.0 26.4 %all-gather.13.cloned.1.call-done = bf16[1024,1024]{1,0:T(8,128)(2,1)} async-done(((bf16[1024,128]{1,0:T(8,128)(2,1)}), bf16[1024,1024]{1,0:T(8,128)(2,1)}) %all-gather.13.cloned.1.call-update) | async-done | bytes 2097168 | tf_op jit(solution)/shard_map/all_gather | solution.py:52
  349.4 9.4 convolution_convert_fusion.1
  359.3 42.2 %reduce-scatter.13.cloned.1.call-done = bf16[2,256,1024]{2,1,0:T(8,128)(2,1)} async-done(((bf16[2,1024,1024]{2,1,0:T(8,128)(2,1)}), bf16[2,256,1024]{2,1,0:T(8,128)(2,1)}) %reduce-scatter.13.cloned.1.call-update) | async-done | bytes 1048592 | tf_op jit(solution)/shard_map/reduce_scatter | solution.py:226
  401.5 2.3 fusion.46
  410.2 34.6 %all-gather.15.cloned.1.call-done = bf16[2,1024,1024]{2,1,0:T(8,128)(2,1)} async-done(((bf16[2,256,1024]{2,1,0:T(8,128)(2,1)}), bf16[2,1024,1024]{2,1,0:T(8,128)(2,1)}) %all-gather.15.cloned.1.call-update) | async-done | bytes 4194320 | tf_op jit(solution)/shard_map/all_gather | solution.py:236
  444.8 14.0 %convert_reduce_fusion = (f32[1024]{0:T(1024)}, bf16[2048,1024]{1,0:T(8,128)(2,1)S(1)}) fusion(f32[2048,1024]{1,0:T(8,128)} %get-tuple-element.615, f32[2048,1024]{1,0:T(8,128)} %get-tuple-element.629, f32[1024]{0:T(1024)S(1)} %copy-done.41, bf16[2048,1024]{1,0:T(8,128)(2,1)} %bitcast.224, bf16[1024,1024]{1,0:T(8,128)(2,1)} %all-gather.13.cloned.1.call-done), kind=kOutput, calls=%fused_computation.46 | convolution fusion | flops 4330617856 | bytes 27271168 | tf_op jit(solution)/shard_map/dot_general | solution.py:40
  458.8 6.3 convolution_convert_fusion
  465.2 44.6 %reduce-scatter.15.cloned.1.call-done = bf16[2,256,1024]{2,1,0:T(8,128)(2,1)} async-done(((bf16[2,1024,1024]{2,1,0:T(8,128)(2,1)}), bf16[2,256,1024]{2,1,0:T(8,128)(2,1)}) %reduce-scatter.15.cloned.1.call-update) | async-done | bytes 1048592 | tf_op jit(solution)/shard_map/reduce_scatter | solution.py:245
  509.8 4.0 multiply_reduce_fusion.1
  518.5 34.2 %all-gather.17.cloned.1.call-done = bf16[2,1024,1024]{2,1,0:T(8,128)(2,1)} async-done(((bf16[2,256,1024]{2,1,0:T(8,128)(2,1)}), bf16[2,1024,1024]{2,1,0:T(8,128)(2,1)}) %all-gather.17.cloned.1.call-update) | async-done | bytes 4194320 | tf_op jit(solution)/shard_map/all_gather | solution.py:250
  552.7 4.5 convolution_convert_fusion.3
  557.2 89.3 %while.50 = (s32[]{:T(128)}, bf16[2,1024,256]{2,1,0:T(8,128)(2,1)}, bf16[2,1024,256]{1,2,0:T(8,128)(2,1)}, bf16[2,1024,256]{1,2,0:T(8,128)(2,1)}, s32[2]{0:T(128...) while((s32[]{:T(128)}, bf16[2,1024,256]{2,1,0:T(8,128)(2,1)}, ...), condition=%wide.region_19.20_spmd.clone, body=%wide.region_15.19_spmd.clone.sunk | while | flops 1375730688 | bytes 118289368 | solution.py:169
  568.0 29.0 %while.51 = (s32[]{:T(128)}, f32[1024,4,64]{0,2,1:T(8,128)S(1)}, f32[1024,4,64]{0,2,1:T(8,128)}, bf16[2,512,256]{2,1,0:T(8,128)(2,1)}, s32[2]{0:T(128)S(1)}, /*i...) while((s32[]{:T(128)}, f32[1024,4,64]{0,2,1:T(8,128)S(1)}, ...), condition=%wide.region_18.18_spmd.clone, body=%wide.region_16.17_spmd.clone.sunk | while | flops 1375205376 | bytes 80538984 | solution.py:160
  572.3 2.0 fusion.142
  574.3 2.7 multiply_reduce_fusion.6
  577.0 2.2 multiply_convert_fusion.3
  586.8 2.0 fusion.142
  588.8 2.7 multiply_reduce_fusion.6
  591.5 2.2 multiply_convert_fusion.3
  612.6 29.0 %while.51 = (s32[]{:T(128)}, f32[1024,4,64]{0,2,1:T(8,128)S(1)}, f32[1024,4,64]{0,2,1:T(8,128)}, bf16[2,512,256]{2,1,0:T(8,128)(2,1)}, s32[2]{0:T(128)S(1)}, /*i...) while((s32[]{:T(128)}, f32[1024,4,64]{0,2,1:T(8,128)S(1)}, ...), condition=%wide.region_18.18_spmd.clone, body=%wide.region_16.17_spmd.clone.sunk | while | flops 1375205376 | bytes 80538984 | solution.py:160
  616.9 2.0 fusion.142
  619.0 2.7 multiply_reduce_fusion.6
  621.7 2.2 multiply_convert_fusion.3
  631.4 2.0 fusion.142
  633.5 2.7 multiply_reduce_fusion.6
  636.2 2.2 multiply_convert_fusion.3
  646.5 4.8 convolution_bitcast_fusion.1
  651.6 4.5 convolution_bitcast_fusion.2
  656.1 4.5 convolution_bitcast_fusion
  662.8 2.4 fusion.50
  666.5 3.5 add_convert_fusion
  670.0 10.1 fusion.52
  680.5 10.1 fusion.53
  690.8 4.9 fusion.51
  698.3 40.7 %all-reduce = (f32[1024]{0:T(1024)}, f32[1024]{0:T(1024)}, f32[1024]{0:T(1024)}, f32[4096]{0:T(1024)}, f32[1024]{0:T(1024)}, /*index=5*/f32[1024]{0:T(1024)}, f32[1024]{0:T(1024)}, f32[1024]{0:T(1024)}, f32[1024]{0:T(1024)}) all-reduce(f32[1024]{0:T(1024)S(1)} %dynamic_update_slice.39, ...), channel_id=1, replica_groups=mesh['dp'=8,'tensor'=4] {'dp','tensor'}, use_global_device_ids=true, to_apply=%region_28.29 | all-reduce | flops 12288 | bytes 98304 | tf_op jit(solution)/shard_map/psum | solution.py:296
  740.7 41.7 %reduce-scatter.19.cloned.1.call-done = f32[128,256]{0,1:T(8,128)} async-done(((f32[1024,256]{0,1:T(8,128)}), f32[128,256]{0,1:T(8,128)}) %reduce-scatter.19.cloned.1.call-update) | async-done | bytes 131088 | tf_op jit(solution)/shard_map/reduce_scatter | solution.py:282
  784.1 65.1 %reduce-scatter.23.cloned.1.call-done = f32[128,256]{0,1:T(8,128)} async-done(((f32[1024,256]{0,1:T(8,128)}), f32[128,256]{0,1:T(8,128)}) %reduce-scatter.23.cloned.1.call-update) | async-done | bytes 131088 | tf_op jit(solution)/shard_map/reduce_scatter | solution.py:284
  850.8 44.2 %reduce-scatter.17.cloned.1.call-done = bf16[2,256,1024]{2,1,0:T(8,128)(2,1)} async-done(((bf16[2,1024,1024]{2,1,0:T(8,128)(2,1)}), bf16[2,256,1024]{2,1,0:T(8,128)(2,1)}) %reduce-scatter.17.cloned.1.call-update) | async-done | bytes 1048592 | tf_op jit(solution)/shard_map/reduce_scatter | solution.py:277
  895.0 2.5 add_convert_fusion.2
  897.5 90.0 %reduce-scatter.27.cloned.1.call-done = f32[128,1024]{1,0:T(8,128)} async-done(((f32[1024,1024]{1,0:T(8,128)}), f32[128,1024]{1,0:T(8,128)}) %reduce-scatter.27.cloned.1.call-update) | async-done | bytes 524304 | tf_op jit(solution)/shard_map/reduce_scatter | solution.py:286
  987.5 92.0 %reduce-scatter.29.cloned.1.call-done = f32[1024,128]{1,0:T(8,128)} async-done(((f32[1024,1024]{1,0:T(8,128)}), f32[1024,128]{1,0:T(8,128)}) %reduce-scatter.29.cloned.1.call-update) | async-done | bytes 524304 | tf_op jit(solution)/shard_map/reduce_scatter | solution.py:287
  1079.5 68.1 %reduce-scatter.25.cloned.1.call-done = f32[256,128]{1,0:T(8,128)} async-done(((f32[256,1024]{1,0:T(8,128)}), f32[256,128]{1,0:T(8,128)}) %reduce-scatter.25.cloned.1.call-update) | async-done | bytes 131088 | tf_op jit(solution)/shard_map/reduce_scatter | solution.py:285
  (290 shorter events, 105.9 us)
Async XLA Ops:
  8.0 127.7 %all-gather.7.cloned.1.call-start = ((), (), s32[]{:S(2)}) async-start(), calls=%async_computation.10 | async-start | bytes 5242880 | tf_op jit(solution)/shard_map/all_gather | solution.py:195
  8.8 245.8 %reduce-scatter.11.cloned.1.call-start = ((), (), s32[]{:S(2)}) async-start(), calls=%async_computation.11 | async-start | bytes 5242880 | tf_op jit(solution)/shard_map/reduce_scatter | solution.py:215
  42.0 106.4 %copy-start.17 = (bf16[1024,256]{1,0:T(8,128)(2,1)}, bf16[1024,256]{1,0:T(8,128)(2,1)S(1)}, u32[]{:S(2)}) copy-start(bf16[1024,256]{1,0:T(8,128)(2,1)S(1)} %all_gather.38) | copy-start | bytes 1572868
  107.3 32.8 %copy-start.19 = (bf16[1024,256]{1,0:T(8,128)(2,1)}, bf16[1024,256]{1,0:T(8,128)(2,1)S(1)}, u32[]{:S(2)}) copy-start(bf16[1024,256]{1,0:T(8,128)(2,1)S(1)} %all_gather.37) | copy-start | bytes 1572868
  141.6 6.8 copy-start.42
  148.5 6.7 copy-start.43
  205.9 4.8 copy-start.11
  205.9 48.6 %copy-start = (bf16[2,256,1024]{2,1,0:T(8,128)(2,1)S(1)}, bf16[2,256,1024]{2,1,0:T(8,128)(2,1)}, u32[]{:S(2)}) copy-start(bf16[2,256,1024]{2,1,0:T(8,128)(2,1)} %param.24) | copy-start | bytes 3145732
  205.9 48.6 %copy-start.25 = (f32[1024]{0:T(1024)S(1)}, f32[1024]{0:T(1024)}, u32[]{:S(2)}) copy-start(f32[1024]{0:T(1024)} %param.34) | copy-start | bytes 12292
  210.7 47.4 %copy-start.26 = (f32[1024]{0:T(1024)S(1)}, f32[1024]{0:T(1024)}, u32[]{:S(2)}) copy-start(f32[1024]{0:T(1024)} %param.37) | copy-start | bytes 12292
  210.7 47.4 %copy-start.33 = (f32[1024]{0:T(1024)S(1)}, f32[1024]{0:T(1024)}, u32[]{:S(2)}) copy-start(f32[1024]{0:T(1024)} %param.38) | copy-start | bytes 12292
  210.7 51.1 %all-gather.11.cloned.1.call-start = ((), (), s32[]{:S(2)}) async-start(), calls=%async_computation.13 | async-start | bytes 2359296 | tf_op jit(solution)/shard_map/all_gather | solution.py:51
  211.3 85.5 %copy-start.41 = (f32[1024]{0:T(1024)S(1)}, f32[1024]{0:T(1024)}, u32[]{:S(2)}) copy-start(f32[1024]{0:T(1024)} %param.35) | copy-start | bytes 12292
  211.3 85.4 %all-gather.9.cloned.1.call-start = ((), (), s32[]{:S(2)}) async-start(), calls=%async_computation.12 | async-start | bytes 5242880 | tf_op jit(solution)/shard_map/all_gather | solution.py:220
  254.5 3.6 copy-start.3
  259.7 89.7 %all-gather.13.cloned.1.call-start = ((), (), s32[]{:S(2)}) async-start(), calls=%async_computation.14 | async-start | bytes 2359296 | tf_op jit(solution)/shard_map/all_gather | solution.py:52
  260.3 141.2 %reduce-scatter.13.cloned.1.call-start = ((), (), s32[]{:S(2)}) async-start(), calls=%async_computation.15 | async-start | bytes 5242880 | tf_op jit(solution)/shard_map/reduce_scatter | solution.py:226
  358.8 42.7 %copy-start.39 = (f32[1024]{0:T(1024)S(1)}, f32[1024]{0:T(1024)}, u32[]{:S(2)}) copy-start(f32[1024]{0:T(1024)} %param.36) | copy-start | bytes 12292
  358.8 45.4 %copy-start.29 = (f32[1024]{0:T(1024)S(1)}, f32[1024]{0:T(1024)}, u32[]{:S(2)}) copy-start(f32[1024]{0:T(1024)} %param.39) | copy-start | bytes 12292
  358.8 46.9 %copy-start.37 = (f32[1024]{0:T(1024)S(1)}, f32[1024]{0:T(1024)}, u32[]{:S(2)}) copy-start(f32[1024]{0:T(1024)} %param.40) | copy-start | bytes 12292
  358.8 85.9 %all-gather.15.cloned.1.call-start = ((), (), s32[]{:S(2)}) async-start(), calls=%async_computation.16 | async-start | bytes 5242880 | tf_op jit(solution)/shard_map/all_gather | solution.py:236
  401.5 2.7 copy-start.15
  407.6 1.4 copy-start.4
  410.1 99.7 %reduce-scatter.15.cloned.1.call-start = ((), (), s32[]{:S(2)}) async-start(), calls=%async_computation.17 | async-start | bytes 5242880 | tf_op jit(solution)/shard_map/reduce_scatter | solution.py:245
  444.8 14.0 %copy-start.40 = (bf16[1024,1024]{1,0:T(8,128)(2,1)S(1)}, bf16[1024,1024]{1,0:T(8,128)(2,1)}, u32[]{:S(2)}) copy-start(bf16[1024,1024]{1,0:T(8,128)(2,1)} %all-gather.11.cloned.1.call-done) | copy-start | bytes 6291460
  458.8 6.3 copy-start.44
  465.1 87.5 %all-gather.17.cloned.1.call-start = ((), (), s32[]{:S(2)}) async-start(), calls=%async_computation.18 | async-start | bytes 5242880 | tf_op jit(solution)/shard_map/all_gather | solution.py:250
  509.8 4.1 copy-start.5
  509.8 4.1 copy-start.16
  515.1 1.3 copy-start.8
  515.1 37.6 %copy-start.21 = (bf16[256,1024]{1,0:T(8,128)(2,1)S(1)}, bf16[256,1024]{1,0:T(8,128)(2,1)}, u32[]{:S(2)}) copy-start(bf16[256,1024]{1,0:T(8,128)(2,1)} %all_gather.40) | copy-start | bytes 1572868
  515.1 42.1 %copy-start.27 = (f32[2,256]{1,0:T(2,128)}, f32[2,256]{1,0:T(2,128)S(1)}, u32[]{:S(2)}) copy-start(f32[2,256]{1,0:T(2,128)S(1)} %negate_multiply_fusion.1) | copy-start | bytes 6148
  518.3 220.8 %reduce-scatter.21.cloned.1.call-start = ((), (), s32[]{:S(2)}) async-start(), calls=%async_computation.21 | async-start | bytes 1179648 | tf_op jit(solution)/shard_map/reduce_scatter | solution.py:283
  557.2 6.7 copy-start.1
  574.3 2.7 copy-start.7
  588.8 2.7 copy-start.7
  597.0 3.4 copy-start.12
  597.0 3.4 copy-start.22
  597.0 4.8 copy-start.2
  601.8 6.7 copy-start.1
  619.0 2.7 copy-start.7
  633.5 2.7 copy-start.7
  641.6 3.4 copy-start.12
  641.6 3.4 copy-start.22
  641.6 4.8 copy-start.2
  646.5 5.1 copy-start.10
  651.3 4.9 copy-start.14
  651.3 131.1 %reduce-scatter.19.cloned.1.call-start = ((), (), s32[]{:S(2)}) async-start(), calls=%async_computation.20 | async-start | bytes 1179648 | tf_op jit(solution)/shard_map/reduce_scatter | solution.py:282
  656.1 4.7 copy-start.24
  656.1 193.1 %reduce-scatter.23.cloned.1.call-start = ((), (), s32[]{:S(2)}) async-start(), calls=%async_computation.22 | async-start | bytes 1179648 | tf_op jit(solution)/shard_map/reduce_scatter | solution.py:284
  660.7 234.3 %reduce-scatter.17.cloned.1.call-start = ((), (), s32[]{:S(2)}) async-start(), calls=%async_computation.19 | async-start | bytes 5242880 | tf_op jit(solution)/shard_map/reduce_scatter | solution.py:277
  662.8 2.4 copy-start.18
  670.0 317.5 %reduce-scatter.27.cloned.1.call-start = ((), (), s32[]{:S(2)}) async-start(), calls=%async_computation.24 | async-start | bytes 4718592 | tf_op jit(solution)/shard_map/reduce_scatter | solution.py:286
  680.2 399.3 %reduce-scatter.29.cloned.1.call-start = ((), (), s32[]{:S(2)}) async-start(), calls=%async_computation.25 | async-start | bytes 4718592 | tf_op jit(solution)/shard_map/reduce_scatter | solution.py:287
  690.6 456.9 %reduce-scatter.25.cloned.1.call-start = ((), (), s32[]{:S(2)}) async-start(), calls=%async_computation.23 | async-start | bytes 1179648 | tf_op jit(solution)/shard_map/reduce_scatter | solution.py:285
  690.7 5.1 copy-start.38
  690.7 7.6 copy-start.30
  690.7 7.6 copy-start.31
  690.7 7.6 copy-start.32
  690.7 7.6 copy-start.34
  690.7 7.6 copy-start.35
  690.7 7.6 copy-start.36
  690.8 204.3 %copy-start.9 = (f32[2,256,1024]{2,1,0:T(8,128)S(1)}, f32[2,256,1024]{2,1,0:T(8,128)}, u32[]{:S(2)}) copy-start(f32[2,256,1024]{2,1,0:T(8,128)} %copy-done.8) | copy-start | bytes 6291460
  690.8 204.2 %copy-start.28 = (f32[2,256]{1,0:T(2,128)S(1)}, f32[2,256]{1,0:T(2,128)}, u32[]{:S(2)}) copy-start(f32[2,256]{1,0:T(2,128)} %copy-done.27) | copy-start | bytes 6148
  (9 other events, 11.1 us)
Sparse Core Ops, SparseCore 0:
  10.4 37.1 all-gather.6
  210.8 43.6 reduce-scatter.10
  410.2 34.4 all-gather.14
  465.3 44.5 reduce-scatter.14
Sparse Core Ops, SparseCore 1:
  213.3 48.4 all-gather.10
  263.9 32.8 all-gather.8
  298.8 50.5 all-gather.12
  358.9 42.6 reduce-scatter.12
  518.3 34.3 all-gather.16
  651.4 64.1 reduce-scatter.20
  719.4 63.0 reduce-scatter.18
  786.1 63.0 reduce-scatter.22
  851.5 43.4 reduce-scatter.16
  899.7 87.8 reduce-scatter.26
  991.6 87.9 reduce-scatter.28
  1083.9 63.6 reduce-scatter.24
where the time goes:
time: 1160 us
  waiting for transfers between devices  664 us (57%)
  matrix products  174 us (15%)
  blocking collectives  168 us (14%)
  local copies, waits for them, and re-layouts  62.3 us (5%)
  other arithmetic  47.2 us (4%)
  loops' own time  21.7 us (2%)
  between operations  16.3 us (1%)
    reduce_scatter x1, waiting for transfers between devices, shards(): lax.psum_scatter(w_down_grad, 'dp', scatter_dimension=1, tiled=True)  92 us
    reduce_scatter x1, waiting for transfers between devices, shards(): lax.psum_scatter(w_up_grad, 'dp', scatter_dimension=0, tiled=True)  90 us
    reduce_scatter x1, waiting for transfers between devices, shards(): lax.psum_scatter(w_out_grad, 'dp', scatter_dimension=1, tiled=True)  68.1 us
    reduce_scatter x1, waiting for transfers between devices, shards(): lax.psum_scatter(w_value_grad, 'dp', scatter_dimension=0, tiled=True)  65.1 us
    dot_general x6, matrix products, matmul(): return jnp.dot(factor_one, factor_two, preferred_element_type=jnp.float32)  53.8 us
    reduce_scatter x1, waiting for transfers between devices, shards(): lax.psum_scatter(back_first.astype(jnp.bfloat16), 'tensor', scatter_dimen...  44.6 us
    reduce_scatter x1, waiting for transfers between devices, shards(): lax.psum_scatter(back_inputs.astype(jnp.bfloat16), 'tensor', scatter_dime...  44.2 us
    reduce_scatter x1, waiting for transfers between devices, shards(): lax.psum_scatter(partial_value.astype(jnp.bfloat16), 'tensor', scatter_di...  43 us
  transfers between devices with their start and end apart: 16, of which 14 were waited for; matrix products, arithmetic and copies ran while one was open for 7% of the time, Pallas kernels for 0%

commit v1 on v0

v1 whole, which is shorter than its diff:
```python
import math

import jax
import jax.numpy as jnp
from jax import lax
from jax.experimental import pallas as pl
from jax.experimental.pallas import tpu as pltpu
from jax.sharding import PartitionSpec as P

HEADS = 16
NORM_EPS = 1e-12
MASKED = -1000000000.0
MIB = 1024 * 1024
VMEM_LIMIT = 40 * MIB

F32 = jnp.float32
BF16 = jnp.bfloat16

CORE = 1
ACROSS = 2


def dot(one, two):
    return lax.dot_general(one, two, (((1,), (0,)), ((), ())), preferred_element_type=F32)


def dot_nt(one, two):
    return lax.dot_general(one, two, (((1,), (1,)), ((), ())), preferred_element_type=F32)


def dot_tn(one, two):
    return lax.dot_general(one, two, (((0,), (0,)), ((), ())), preferred_element_type=F32)


def shape(dims, kind):
    return jax.ShapeDtypeStruct(dims, kind)


def whole_call(kernel, outs, args, flops, name, scratch=()):
    moved = sum(math.prod(a.shape) * a.dtype.itemsize for a in (*args, *outs))
    return pl.pallas_call(
        kernel,
        out_shape=tuple(outs),
        in_specs=[pl.BlockSpec(memory_space=pltpu.VMEM)] * len(args),
        out_specs=tuple([pl.BlockSpec(memory_space=pltpu.VMEM)] * len(outs)),
        scratch_shapes=list(scratch),
        compiler_params=pltpu.CompilerParams(vmem_limit_bytes=VMEM_LIMIT),
        cost_estimate=pl.CostEstimate(flops=flops, bytes_accessed=moved, transcendentals=0),
        name=name,
    )(*args)


def swap_tensor(array, bit):
    size = lax.axis_size("tensor")
    return lax.ppermute(array, "tensor", [(i, i ^ bit) for i in range(size)])


def swap_dp(array, bit):
    size = lax.axis_size("dp")
    return lax.ppermute(array, "dp", [(i, i ^ bit) for i in range(size)])


def gather_dp(rows):
    size = lax.axis_size("dp")
    place = lax.axis_index("dp")
    step = size // 2
    level = 0
    block = rows.shape
    held = rows
    while step >= 1:
        other = swap_dp(held, step)
        low = (place & step) == 0
        held = jnp.where(
            low, jnp.stack([held, other], axis=level), jnp.stack([other, held], axis=level)
        )
        level += 1
        step //= 2
    return held.reshape((size * block[0],) + block[1:])


def scatter_dp(total):
    size = lax.axis_size("dp")
    place = lax.axis_index("dp")
    levels = size.bit_length() - 1
    rows = total.shape[0] // size
    held = total.reshape((2,) * levels + (rows,) + total.shape[1:])
    for level in range(levels):
        axis = levels - 1 - level
        bit = (place >> level) & 1
        mine = lax.dynamic_index_in_dim(held, bit, axis, keepdims=False)
        theirs = lax.dynamic_index_in_dim(held, 1 - bit, axis, keepdims=False)
        held = mine.astype(F32) + swap_dp(theirs.astype(BF16), 1 << level).astype(F32)
    return held


def sum_all(vector):
    step = 1
    while step < lax.axis_size("tensor"):
        vector = vector + swap_tensor(vector, step)
        step *= 2
    step = 1
    while step < lax.axis_size("dp"):
        vector = vector + swap_dp(vector, step)
        step *= 2
    return vector


def project_inputs(x_own, x_across, w_mine, w_other, b_mine, b_other):
    rows, width = x_own.shape
    third = w_mine.shape[1] // 3

    def kernel(x0, x1, wm, wo, bm, bo, mine_ref, other_ref, send_ref):
        tokens = jnp.concatenate([x0[...], x1[...]], axis=0)
        mine = (dot(tokens, wm[...]) + bm[...]).astype(BF16)
        other = (dot(tokens, wo[...]) + bo[...]).astype(BF16)
        mine_ref[...] = mine
        other_ref[...] = other
        send_ref[:, : 2 * third] = other[:, third:]
        send_ref[:, 2 * third :] = mine[:, third:]

    outs = [
        shape((2 * rows, 3 * third), BF16),
        shape((2 * rows, 3 * third), BF16),
        shape((2 * rows, 4 * third), BF16),
    ]
    flops = 2 * 2 * rows * width * 6 * third
    return whole_call(
        kernel, outs, [x_own, x_across, w_mine, w_other, b_mine, b_other], flops, "project_inputs"
    )


def attention_forward(mine, other, far, bias_row, wout_mine, wout_other, head_size):
    rows = mine.shape[0]
    third = mine.shape[1] // 3
    heads = third // head_size
    block = rows // 2
    width = wout_mine.shape[0]
    scaling = 1.0 / math.sqrt(head_size)

    def kernel(mine_ref, other_ref, far_ref, bias_ref, wm, wo, cm_ref, co_ref, own_ref, across_ref, acc):
        lane_head = lax.broadcasted_iota(jnp.int32, (1, third), 1) // head_size
        acc[...] = jnp.zeros_like(acc)
        bias = bias_ref[...]

        def one_head(head, carry):
            inside = lane_head == head
            for group, ref in enumerate((mine_ref, other_ref)):
                base = 2 * third * group
                keys = jnp.concatenate(
                    [ref[:, third : 2 * third], far_ref[:, base : base + third]], axis=0
                )
                vals = jnp.concatenate(
                    [ref[:, 2 * third :], far_ref[:, base + third : base + 2 * third]], axis=0
                )
                for part in range(2):
                    span = slice(part * block, (part + 1) * block)
                    query = jnp.where(inside, ref[span, :third] * scaling, 0.0).astype(BF16)
                    scores = dot_nt(query, keys) + bias
                    peak = jnp.max(scores, axis=-1, keepdims=True)
                    weights = jnp.exp(scores - peak)
                    total = jnp.sum(weights, axis=-1, keepdims=True)
                    found = dot(weights.astype(BF16), vals) * (1.0 / total)
                    acc[group, span, :] += jnp.where(inside, found, 0.0)
            return carry

        lax.fori_loop(0, heads, one_head, 0)
        ctx_mine = acc[0].astype(BF16)
        ctx_other = acc[1].astype(BF16)
        cm_ref[...] = ctx_mine
        co_ref[...] = ctx_other
        part_sum = dot_nt(ctx_mine, wm[...]) + dot_nt(ctx_other, wo[...])
        own_ref[...] = part_sum[:block]
        across_ref[...] = part_sum[block:].astype(BF16)

    outs = [
        shape((rows, third), BF16),
        shape((rows, third), BF16),
        shape((block, width), F32),
        shape((block, width), BF16),
    ]
    flops = 2 * 2 * 2 * rows * 2 * rows * third * heads * 2
    return whole_call(
        kernel,
        outs,
        [mine, other, far, bias_row, wout_mine, wout_other],
        flops,
        "attention_forward",
        [pltpu.VMEM((2, rows, third), F32)],
    )


def attention_backward(mine, other, far, bias_column, ga_own, ga_across, wout_mine, wout_other, head_size):
    rows = mine.shape[0]
    third = mine.shape[1] // 3
    heads = third // head_size
    block = rows // 2
    keys_count = 2 * rows
    scaling = 1.0 / math.sqrt(head_size)

    def kernel(
        mine_ref, other_ref, far_ref, bias_ref, g0, g1, wm, wo,
        dq_ref, keep_ref, send_ref, grad_ctx, keys_t, dq_t, dkv,
    ):
        lane_head = lax.broadcasted_iota(jnp.int32, (1, third), 1) // head_size
        grad_rows = jnp.concatenate([g0[...], g1[...]], axis=0)
        grad_ctx[0] = dot(grad_rows, wm[...]).astype(BF16)
        grad_ctx[1] = dot(grad_rows, wo[...]).astype(BF16)
        dkv[...] = jnp.zeros_like(dkv)
        for group, ref in enumerate((mine_ref, other_ref)):
            base = 2 * third * group
            keys_t[group, :, :rows] = ref[:, third : 2 * third].T
            keys_t[group, :, rows:] = far_ref[:, base : base + third].T
        bias = bias_ref[...]

        def one_head(head, carry):
            inside = lane_head == head
            start = pl.multiple_of(head * head_size, head_size)
            for group, ref in enumerate((mine_ref, other_ref)):
                base = 2 * third * group
                keys = jnp.concatenate(
                    [ref[:, third : 2 * third], far_ref[:, base : base + third]], axis=0
                )
                vals = jnp.concatenate(
                    [ref[:, 2 * third :], far_ref[:, base + third : base + 2 * third]], axis=0
                )
                head_keys_t = keys_t[group, pl.ds(start, head_size), :]
                for part in range(2):
                    span = slice(part * block, (part + 1) * block)
                    query = jnp.where(inside, ref[span, :third] * scaling, 0.0).astype(BF16)
                    grad = jnp.where(inside, grad_ctx[group, span, :], 0.0).astype(BF16)
                    scores = dot_nt(keys, query) + bias
                    peak = jnp.max(scores, axis=0, keepdims=True)
                    weights = jnp.exp(scores - peak)
                    total = jnp.sum(weights, axis=0, keepdims=True)
                    probs = weights * (1.0 / total)
                    grad_probs = dot_nt(vals, grad)
                    inner = jnp.sum(probs * grad_probs, axis=0, keepdims=True)
                    grad_scores = (probs * (grad_probs - inner)).astype(BF16)
                    dkv[group, 1] += dot(probs.astype(BF16), grad)
                    dkv[group, 0] += dot(grad_scores, query)
                    dq_t[group, pl.ds(start, head_size), span] = dot(head_keys_t, grad_scores)
            return carry

        lax.fori_loop(0, heads, one_head, 0)
        for group in range(2):
            dq_ref[:, group * third : (group + 1) * third] = (dq_t[group].T * scaling).astype(BF16)
            for kind in range(2):
                at = (2 * group + kind) * third
                keep_ref[:, at : at + third] = dkv[group, kind, :rows]
                away = (2 * (1 - group) + kind) * third
                send_ref[:, away : away + third] = dkv[group, kind, rows:].astype(BF16)

    outs = [
        shape((rows, 2 * third), BF16),
        shape((rows, 4 * third), F32),
        shape((rows, 4 * third), BF16),
    ]
    flops = 5 * 2 * 2 * rows * keys_count * third * heads
    return whole_call(
        kernel,
        outs,
        [mine, other, far, bias_column, ga_own, ga_across, wout_mine, wout_other],
        flops,
        "attention_backward",
        [
            pltpu.VMEM((2, rows, third), BF16),
            pltpu.VMEM((2, third, keys_count), BF16),
            pltpu.VMEM((2, third, rows), F32),
            pltpu.VMEM((2, 2, keys_count, third), F32),
        ],
    )


def project_back(dq, keep, got, w_mine, w_other):
    rows = dq.shape[0]
    third = dq.shape[1] // 2
    block = rows // 2
    width = w_mine.shape[0]

    def kernel(dq_ref, keep_ref, got_ref, wm, wo, gm_ref, go_ref, own_ref, across_ref, sums_ref):
        dkv = (keep_ref[...] + got_ref[...].astype(F32)).astype(BF16)
        grad_mine = jnp.concatenate([dq_ref[:, :third], dkv[:, : 2 * third]], axis=1)
        grad_other = jnp.concatenate([dq_ref[:, third:], dkv[:, 2 * third :]], axis=1)
        gm_ref[...] = grad_mine
        go_ref[...] = grad_other
        back = dot_nt(grad_mine, wm[...]) + dot_nt(grad_other, wo[...])
        own_ref[...] = back[:block]
        across_ref[...] = back[block:].astype(BF16)
        sums_ref[0:1, :] = jnp.sum(grad_mine.astype(F32), axis=0, keepdims=True)
        sums_ref[1:2, :] = jnp.sum(grad_other.astype(F32), axis=0, keepdims=True)

    outs = [
        shape((rows, 3 * third), BF16),
        shape((rows, 3 * third), BF16),
        shape((block, width), F32),
        shape((block, width), BF16),
        shape((2, 3 * third), F32),
    ]
    flops = 2 * rows * width * 6 * third
    return whole_call(kernel, outs, [dq, keep, got, w_mine, w_other], flops, "project_back")


def moments(summed):
    centre = jnp.mean(summed, axis=-1, keepdims=True)
    centred = summed - centre
    spread = jnp.mean(centred * centred, axis=-1, keepdims=True)
    back = lax.rsqrt(spread + NORM_EPS)
    return centred * back, back


def first_norm(x_own, part, got, b_out, gain, shift):
    dims = x_own.shape

    def kernel(x_ref, p_ref, r_ref, b_ref, g_ref, s_ref, summed_ref, normed_ref, low_ref):
        summed = x_ref[...].astype(F32) + (p_ref[...] + r_ref[...].astype(F32)) + b_ref[...]
        unit, _ = moments(summed)
        normed = unit * g_ref[...] + s_ref[...]
        summed_ref[...] = summed
        normed_ref[...] = normed
        low_ref[...] = normed.astype(BF16)

    outs = [shape(dims, F32), shape(dims, F32), shape(dims, BF16)]
    return whole_call(
        kernel, outs, [x_own, part, got, b_out, gain, shift], 20 * math.prod(dims), "first_norm"
    )


def second_norm(normed, part, got, cotangent, b_down, gain, shift):
    dims = normed.shape

    def kernel(n_ref, p_ref, r_ref, c_ref, b_ref, g_ref, s_ref, out_ref, grad_ref, low_ref, sums_ref):
        summed = n_ref[...] + (p_ref[...] + r_ref[...].astype(F32)) + b_ref[...]
        unit, back = moments(summed)
        out_ref[...] = (unit * g_ref[...] + s_ref[...]).astype(BF16)
        cot = c_ref[...].astype(F32)
        scaled = cot * g_ref[...]
        grad = back * (
            scaled
            - jnp.mean(scaled, axis=-1, keepdims=True)
            - unit * jnp.mean(scaled * unit, axis=-1, keepdims=True)
        )
        grad_ref[...] = grad
        low_ref[...] = grad.astype(BF16)
        sums_ref[0:1, :] = jnp.sum(cot * unit, axis=0, keepdims=True)
        sums_ref[1:2, :] = jnp.sum(cot, axis=0, keepdims=True)
        sums_ref[2:3, :] = jnp.sum(grad, axis=0, keepdims=True)

    outs = [shape(dims, BF16), shape(dims, F32), shape(dims, BF16), shape((3, dims[1]), F32)]
    return whole_call(
        kernel,
        outs,
        [normed, part, got, cotangent, b_down, gain, shift],
        40 * math.prod(dims),
        "second_norm",
    )


def first_norm_back(summed, grad_second, part, got, gain):
    dims = summed.shape

    def kernel(z_ref, gs_ref, p_ref, r_ref, g_ref, grad_ref, low_ref, sums_ref):
        unit, back = moments(z_ref[...])
        grad_normed = gs_ref[...] + (p_ref[...] + r_ref[...].astype(F32))
        scaled = grad_normed * g_ref[...]
        grad = back * (
            scaled
            - jnp.mean(scaled, axis=-1, keepdims=True)
            - unit * jnp.mean(scaled * unit, axis=-1, keepdims=True)
        )
        grad_ref[...] = grad
        low_ref[...] = grad.astype(BF16)
        sums_ref[0:1, :] = jnp.sum(grad_normed * unit, axis=0, keepdims=True)
        sums_ref[1:2, :] = jnp.sum(grad_normed, axis=0, keepdims=True)
        sums_ref[2:3, :] = jnp.sum(grad, axis=0, keepdims=True)

    outs = [shape(dims, F32), shape(dims, BF16), shape((3, dims[1]), F32)]
    return whole_call(
        kernel, outs, [summed, grad_second, part, got, gain], 40 * math.prod(dims), "first_norm_back"
    )


def streamed_call(kernel, grid, outs, out_specs, args, in_specs, flops, name, scratch):
    moved = sum(math.prod(a.shape) * a.dtype.itemsize for a in (*args, *outs))
    return pl.pallas_call(
        kernel,
        grid=grid,
        out_shape=tuple(outs),
        in_specs=in_specs,
        out_specs=tuple(out_specs),
        scratch_shapes=list(scratch),
        compiler_params=pltpu.CompilerParams(
            vmem_limit_bytes=VMEM_LIMIT, dimension_semantics=("arbitrary",)
        ),
        cost_estimate=pl.CostEstimate(flops=flops, bytes_accessed=moved, transcendentals=0),
        name=name,
    )(*args)


def const_spec(dims):
    return pl.BlockSpec(dims, lambda i: (0,) * len(dims))


def feed_forward(n_own, n_across, up_mine, up_other, down_mine, down_other, b_mine, b_other):
    block, width = n_own.shape
    rows = 2 * block
    hidden = up_mine.shape[1]
    tile = min(256, hidden)
    steps = hidden // tile

    def kernel(
        n0, n1, um, uo, dm, do, bm, bo,
        am_ref, ao_ref, sm_ref, so_ref, own_ref, across_ref, tokens, acc,
    ):
        step = pl.program_id(0)

        @pl.when(step == 0)
        def _():
            tokens[:block] = n0[...]
            tokens[block:] = n1[...]
            acc[...] = jnp.zeros_like(acc)

        total = acc[...]
        for u, d, b, a_ref, s_ref in ((um, dm, bm, am_ref, sm_ref), (uo, do, bo, ao_ref, so_ref)):
            hid = dot(tokens[...], u[...]) + b[...]
            half = 0.5 * (1.0 + lax.erf(hid * (1.0 / math.sqrt(2.0))))
            bell = jnp.exp(hid * hid * -0.5) * (1.0 / math.sqrt(2.0 * math.pi))
            active = (hid * half).astype(BF16)
            a_ref[...] = active
            s_ref[...] = (half + hid * bell).astype(BF16)
            total = total + dot_nt(active, d[...])
        acc[...] = total

        @pl.when(step == steps - 1)
        def _():
            own_ref[...] = acc[:block]
            across_ref[...] = acc[block:].astype(BF16)

    column = pl.BlockSpec((width, tile), lambda i: (0, i))
    bias = pl.BlockSpec((1, tile), lambda i: (0, i))
    made = pl.BlockSpec((rows, tile), lambda i: (0, i))
    outs = [shape((rows, hidden), BF16)] * 4 + [shape((block, width), F32), shape((block, width), BF16)]
    return streamed_call(
        kernel,
        (steps,),
        outs,
        [made] * 4 + [const_spec((block, width))] * 2,
        [n_own, n_across, up_mine, up_other, down_mine, down_other, b_mine, b_other],
        [const_spec((block, width))] * 2 + [column] * 4 + [bias] * 2,
        2 * 2 * rows * width * 2 * hidden,
        "feed_forward",
        [pltpu.VMEM((rows, width), BF16), pltpu.VMEM((rows, width), F32)],
    )


def feed_forward_back(g_own, g_across, up_mine, up_other, down_mine, down_other, slope_mine, slope_other):
    block, width = g_own.shape
    rows = 2 * block
    hidden = up_mine.shape[1]
    tile = min(256, hidden)
    steps = hidden // tile

    def kernel(
        g0, g1, um, uo, dm, do, sm, so,
        gm_ref, go_ref, own_ref, across_ref, bm_ref, bo_ref, grads, acc,
    ):
        step = pl.program_id(0)

        @pl.when(step == 0)
        def _():
            grads[:block] = g0[...]
            grads[block:] = g1[...]
            acc[...] = jnp.zeros_like(acc)

        total = acc[...]
        for u, d, s, g_ref, b_ref in ((um, dm, sm, gm_ref, bm_ref), (uo, do, so, go_ref, bo_ref)):
            grad_hidden = (dot(grads[...], d[...]) * s[...].astype(F32)).astype(BF16)
            g_ref[...] = grad_hidden
            b_ref[...] = jnp.sum(grad_hidden.astype(F32), axis=0, keepdims=True)
            total = total + dot_nt(grad_hidden, u[...])
        acc[...] = total

        @pl.when(step == steps - 1)
        def _():
            own_ref[...] = acc[:block]
            across_ref[...] = acc[block:].astype(BF16)

    column = pl.BlockSpec((width, tile), lambda i: (0, i))
    bias = pl.BlockSpec((1, tile), lambda i: (0, i))
    made = pl.BlockSpec((rows, tile), lambda i: (0, i))
    outs = (
        [shape((rows, hidden), BF16)] * 2
        + [shape((block, width), F32), shape((block, width), BF16)]
        + [shape((1, hidden), F32)] * 2
    )
    return streamed_call(
        kernel,
        (steps,),
        outs,
        [made] * 2 + [const_spec((block, width))] * 2 + [bias] * 2,
        [g_own, g_across, up_mine, up_other, down_mine, down_other, slope_mine, slope_other],
        [const_spec((block, width))] * 2 + [column] * 4 + [made] * 2,
        2 * 2 * rows * width * 2 * hidden,
        "feed_forward_back",
        [pltpu.VMEM((rows, width), BF16), pltpu.VMEM((rows, width), F32)],
    )


def weight_grad(ones, mine, other):
    kept = sum(dot_tn(a, b) for a, b in zip(ones, mine))
    sent = sum(dot_tn(a, b) for a, b in zip(ones, other))
    kept = kept + swap_tensor(sent.astype(BF16), CORE).astype(F32)
    return scatter_dp(kept)


def shards(
    inputs,
    lengths,
    w_query,
    w_key,
    w_value,
    w_out,
    w_up,
    w_down,
    b_query,
    b_value,
    b_out,
    b_up,
    b_down,
    first_gain,
    first_shift,
    second_gain,
    second_shift,
    cotangent,
):
    seq_count, block, width = inputs.shape
    tensor_size = lax.axis_size("tensor")
    seq_len = block * tensor_size
    place = lax.axis_index("tensor")
    head_dims = w_query.shape[1]
    head_size = width // HEADS
    seqs = range(seq_count)
    row = lambda vector: vector.reshape(1, -1)

    x_own = [inputs[s] for s in seqs]
    x_across = [swap_tensor(x_own[s], ACROSS) for s in seqs]

    qkv_mine = gather_dp(jnp.concatenate([w_query, w_key, w_value], axis=1))
    qkv_other = swap_tensor(qkv_mine, CORE)
    out_mine = gather_dp(w_out.T)
    out_other = swap_tensor(out_mine, CORE)
    up_mine = gather_dp(w_up)
    up_other = swap_tensor(up_mine, CORE)
    down_mine = gather_dp(w_down.T)
    down_other = swap_tensor(down_mine, CORE)

    biases = jnp.concatenate([b_query, jnp.zeros_like(b_query), b_value, b_up])
    biases_other = swap_tensor(biases, CORE)
    qkv_bias_mine, up_bias_mine = row(biases[: 3 * head_dims]), row(biases[3 * head_dims :])
    qkv_bias_other = row(biases_other[: 3 * head_dims])
    up_bias_other = row(biases_other[3 * head_dims :])
    b_out_row, b_down_row = row(b_out), row(b_down)
    gain_one, shift_one = row(first_gain), row(first_shift)
    gain_two, shift_two = row(second_gain), row(second_shift)

    order = jnp.stack([place, place ^ ACROSS, place ^ CORE, place ^ CORE ^ ACROSS])
    positions = (order[:, None] * block + jnp.arange(block, dtype=jnp.int32)[None, :]).reshape(-1)
    masks = [jnp.where(positions < lengths[s], 0.0, MASKED).astype(F32) for s in seqs]

    projected = [
        project_inputs(x_own[s], x_across[s], qkv_mine, qkv_other, qkv_bias_mine, qkv_bias_other)
        for s in seqs
    ]
    far = [swap_tensor(projected[s][2], CORE) for s in seqs]
    attended = [
        attention_forward(
            projected[s][0], projected[s][1], far[s], masks[s].reshape(1, seq_len),
            out_mine, out_other, head_size,
        )
        for s in seqs
    ]
    attended_got = [swap_tensor(attended[s][3], ACROSS) for s in seqs]
    one = [
        first_norm(x_own[s], attended[s][2], attended_got[s], b_out_row, gain_one, shift_one)
        for s in seqs
    ]
    normed_across = [swap_tensor(one[s][2], ACROSS) for s in seqs]
    fed = [
        feed_forward(
            one[s][2], normed_across[s], up_mine, up_other, down_mine, down_other,
            up_bias_mine, up_bias_other,
        )
        for s in seqs
    ]
    branch_got = [swap_tensor(fed[s][5], ACROSS) for s in seqs]
    two = [
        second_norm(
            one[s][1], fed[s][4], branch_got[s], cotangent[s], b_down_row, gain_two, shift_two
        )
        for s in seqs
    ]
    grad_across = [swap_tensor(two[s][2], ACROSS) for s in seqs]
    fed_back = [
        feed_forward_back(
            two[s][2], grad_across[s], up_mine, up_other, down_mine, down_other, fed[s][2], fed[s][3]
        )
        for s in seqs
    ]
    back_got = [swap_tensor(fed_back[s][3], ACROSS) for s in seqs]
    one_back = [
        first_norm_back(one[s][0], two[s][1], fed_back[s][2], back_got[s], gain_one) for s in seqs
    ]
    first_across = [swap_tensor(one_back[s][1], ACROSS) for s in seqs]

    grad_rows = [jnp.concatenate([two[s][2], grad_across[s]]) for s in seqs]
    down_grad = weight_grad(grad_rows, [fed[s][0] for s in seqs], [fed[s][1] for s in seqs])
    normed_rows = [jnp.concatenate([one[s][2], normed_across[s]]) for s in seqs]
    up_grad = weight_grad(normed_rows, [fed_back[s][0] for s in seqs], [fed_back[s][1] for s in seqs])

    attended_back = [
        attention_backward(
            projected[s][0], projected[s][1], far[s], masks[s].reshape(seq_len, 1),
            one_back[s][1], first_across[s], out_mine, out_other, head_size,
        )
        for s in seqs
    ]
    first_rows = [jnp.concatenate([one_back[s][1], first_across[s]]) for s in seqs]
    out_grad = weight_grad(first_rows, [attended[s][0] for s in seqs], [attended[s][1] for s in seqs])

    far_back = [swap_tensor(attended_back[s][2], CORE) for s in seqs]
    back = [
        project_back(attended_back[s][0], attended_back[s][1], far_back[s], qkv_mine, qkv_other)
        for s in seqs
    ]
    input_got = [swap_tensor(back[s][3], ACROSS) for s in seqs]
    input_grad = jnp.stack(
        [
            (one_back[s][0] + (back[s][2] + input_got[s].astype(F32))).astype(BF16)
            for s in seqs
        ]
    )
    token_rows = [jnp.concatenate([x_own[s], x_across[s]]) for s in seqs]
    qkv_grad = weight_grad(token_rows, [back[s][0] for s in seqs], [back[s][1] for s in seqs])

    def placed_in(part_mine, part_other):
        size = part_mine.shape[0]
        empty = jnp.zeros((tensor_size * size,), F32)
        empty = lax.dynamic_update_slice(empty, part_mine, (place * size,))
        return lax.dynamic_update_slice(empty, part_other, ((place ^ CORE) * size,))

    hidden = up_mine.shape[1]
    early = sum_all(
        jnp.concatenate(
            [
                sum(two[s][3] for s in seqs).reshape(-1),
                sum(one_back[s][2] for s in seqs).reshape(-1),
                placed_in(
                    sum(fed_back[s][4] for s in seqs).reshape(-1),
                    sum(fed_back[s][5] for s in seqs).reshape(-1),
                ),
            ]
        )
    )
    sums = sum(back[s][4] for s in seqs)
    late = sum_all(
        jnp.concatenate(
            [
                placed_in(sums[0, :head_dims], sums[1, :head_dims]),
                placed_in(sums[0, 2 * head_dims :], sums[1, 2 * head_dims :]),
            ]
        )
    )
    vectors = [early[i * width : (i + 1) * width] for i in range(6)]
    second_gain_grad, second_shift_grad, b_down_grad = vectors[:3]
    first_gain_grad, first_shift_grad, b_out_grad = vectors[3:]
    b_up_grad = early[6 * width : 6 * width + tensor_size * hidden]
    b_query_grad, b_value_grad = late[:width], late[width:]

    output = jnp.stack([two[s][0] for s in seqs])
    return (
        output,
        input_grad,
        qkv_grad[:, :head_dims],
        qkv_grad[:, head_dims : 2 * head_dims],
        qkv_grad[:, 2 * head_dims :],
        out_grad.T,
        up_grad,
        down_grad.T,
        b_query_grad,
        b_value_grad,
        b_out_grad,
        b_up_grad,
        b_down_grad,
        first_gain_grad,
        first_shift_grad,
        second_gain_grad,
        second_shift_grad,
    )


def solution(mesh):
    placed = (
        P("dp", "tensor", None),
        P("dp"),
        P("dp", "tensor"),
        P("dp", "tensor"),
        P("dp", "tensor"),
        P("tensor", "dp"),
        P("dp", "tensor"),
        P("tensor", "dp"),
        P("tensor"),
        P("tensor"),
        P(),
        P("tensor"),
        P(),
        P(),
        P(),
        P(),
        P(),
        P("dp", "tensor", None),
    )
    return jax.shard_map(
        shards,
        mesh=mesh,
        in_specs=placed,
        out_specs=(
            P("dp", "tensor", None),
            P("dp", "tensor", None),
            P("dp", "tensor"),
            P("dp", "tensor"),
            P("dp", "tensor"),
            P("tensor", "dp"),
            P("dp", "tensor"),
            P("tensor", "dp"),
            P(),
            P(),
            P(),
            P(),
            P(),
            P(),
            P(),
            P(),
            P(),
        ),
        check_vma=False,
    )
```

time: 1160 us -> 562 us (0.48)
  waiting for transfers between devices: 664 us -> 170 us
  blocking collectives: 168 us -> 0 us
  Pallas kernels: 0 us -> 139 us
  matrix products: 174 us -> 40.9 us
  starting transfers between devices: 1.94 us -> 69.1 us
  local copies, waits for them, and re-layouts: 62.3 us -> 85.8 us
  loops' own time: 21.7 us -> 0 us
  between operations: 16.3 us -> 2.23 us
    reduce_scatter x10 -> x0, waiting for transfers between devices: 531 us -> none  [the longest x1 92 us: shards(): lax.psum_scatter(w_down_grad, 'dp', scatter_dimension=1, tiled=True)]
    ppermute x0 -> x63, waiting for transfers between devices: none -> 170 us  [the longest x30 135 us: swap_dp(): return lax.ppermute(array, 'dp', [(i, i ^ bit) for i in range(size)])]
    pallas_call x0 -> x18, Pallas kernels: none -> 139 us  [the longest x14 95 us: whole_call(): pl.pallas_call(kernel, out_shape=tuple(outs), in_specs=[pl.BlockSpec(memo...]
    dot_general x46 -> x16, matrix products: 174 us -> 40.9 us  [dot_tn(): lax.dot_general(one, two, (((0,), (0,)), ((), ())), preferred_element_typ...]
    all_gather x6 -> x0, waiting for transfers between devices: 132 us -> none  [the longest x1 34.9 us: shards(): lax.all_gather(normed.astype(jnp.bfloat16), 'tensor', axis=1, tiled=True)]
    all_gather x4 -> x0, blocking collectives: 127 us -> none  [the longest x1 33.6 us: fetch_weights(): lax.all_gather(w_key, 'dp', axis=0, tiled=True)]
    ppermute x0 -> x63, starting transfers between devices: none -> 69.1 us  [the longest x30 47.2 us: swap_dp(): return lax.ppermute(array, 'dp', [(i, i ^ bit) for i in range(size)])]
    unnamed x80 -> x279, local copies, waits for them, and re-layouts: 13.9 us -> 56.1 us
  transfers between devices with their start and end apart: 16 -> 63, of which waited for: 14 -> 25; matrix products, arithmetic and copies ran while one was open for 7% -> 23% of each run, Pallas kernels for 0% -> 25%
where the time goes in v1:
time: 562 us; the launch traced here: 555 us
  waiting for transfers between devices  170 us (30%)
  Pallas kernels  139 us (25%)
  local copies, waits for them, and re-layouts  85.8 us (15%)
  starting transfers between devices  69.1 us (12%)
  other arithmetic  48.2 us (9%)
  matrix products  40.9 us (7%)
    ppermute x30, waiting for transfers between devices, swap_dp(): return lax.ppermute(array, 'dp', [(i, i ^ bit) for i in range(size)])  135 us
    pallas_call x14, Pallas kernels, whole_call(): pl.pallas_call(kernel, out_shape=tuple(outs), in_specs=[pl.BlockSpec(memo...  95 us
    unnamed x279, local copies, waits for them, and re-layouts  56.1 us
    ppermute x30, starting transfers between devices, swap_dp(): return lax.ppermute(array, 'dp', [(i, i ^ bit) for i in range(size)])  47.2 us
    pallas_call x4, Pallas kernels, streamed_call(): pl.pallas_call(kernel, grid=grid, out_shape=tuple(outs), in_specs=in_spec...  43.5 us
    dot_general x16, matrix products, dot_tn(): lax.dot_general(one, two, (((0,), (0,)), ((), ())), preferred_element_typ...  40.9 us
    ppermute x33, waiting for transfers between devices, swap_tensor(): return lax.ppermute(array, 'tensor', [(i, i ^ bit) for i in range(size)])  35.2 us
    ppermute x33, starting transfers between devices, swap_tensor(): return lax.ppermute(array, 'tensor', [(i, i ^ bit) for i in range(size)])  22 us
  transfers between devices with their start and end apart: 63, of which 25 were waited for; matrix products, arithmetic and copies ran while one was open for 23% of the time, Pallas kernels for 25%

profile of v1, /device:TPU:0, one launch (start us, length us, event | category | flops | bytes accessed | tf_op | source)
XLA Modules:
  0.0 554.8 jit_solution(1876498054901874533)
XLA Ops:
  3.2 4.0 collective-permute-start.1
  7.2 9.1 %collective-permute-done.1 = bf16[128,768]{1,0:T(8,128)(2,1)S(1)} collective-permute-done((bf16[128,768]{1,0:T(8,128)(2,1)S(1)}, bf16[128,768]{1,0:T(8,128)(2,1)S(1)}, u32[]{:S(2)}, u32[]{:S(2)}) %collective-permute-start.1) | collective-permute-done | bytes 196640 | tf_op jit(solution)/shard_map/ppermute | solution.py:60
  17.2 2.2 slice_bitcast_fusion.3
  21.0 5.8 %collective-permute-done.2 = bf16[2,128,768]{2,1,0:T(8,128)(2,1)S(1)} collective-permute-done((bf16[2,128,768]{2,1,0:T(8,128)(2,1)S(1)}, bf16[2,128,768]{2,1,0:T(8,128)(2,1)S(1)}, u32[]{:S(2)}, u32[]{:S(2)}) %collective-permute-start.2) | collective-permute-done | bytes 393248 | tf_op jit(solution)/shard_map/ppermute | solution.py:60
  28.4 3.4 collective-permute-start.7
  35.2 9.7 %collective-permute-done.3 = bf16[2,2,128,768]{3,2,0,1:T(8,128)(2,1)S(1)} collective-permute-done((bf16[2,2,128,768]{3,2,0,1:T(8,128)(2,1)S(1)}, bf16[2,2,128,768]{3,2,0,1:T(8,128)(2,1)S(1)}, u32[]{:S(2)}, u32[]{:S(2)}) %collective-permute-start.3) | collective-permute-done | bytes 786464 | tf_op jit(solution)/shard_map/ppermute | solution.py:60
  48.4 4.2 collective-permute-start.17
  59.7 5.0 collective-permute-done.17
  68.2 11.4 %collective-permute-done.14 = bf16[2,128,1024]{1,2,0:T(8,128)(2,1)S(1)} collective-permute-done((bf16[2,128,1024]{1,2,0:T(8,128)(2,1)S(1)}, bf16[2,128,1024]{1,2,0:T(8,128)(2,1)S(1)}, u32[]{:S(2)}, u32[]{:S(2)}) %collective-permute-start.14) | collective-permute-done | bytes 524320 | tf_op jit(solution)/shard_map/ppermute | solution.py:60
  82.2 6.8 %collective-permute-done.18 = bf16[2,128,1024]{1,2,0:T(8,128)(2,1)S(1)} collective-permute-done((bf16[2,128,1024]{1,2,0:T(8,128)(2,1)S(1)}, bf16[2,128,1024]{1,2,0:T(8,128)(2,1)S(1)}, u32[]{:S(2)}, u32[]{:S(2)}) %collective-permute-start.18) | collective-permute-done | bytes 524320 | tf_op jit(solution)/shard_map/ppermute | solution.py:60
  91.7 2.0 fusion.70
  94.2 4.0 project_inputs.3
  100.9 29.7 %collective-permute-done.9 = bf16[2,2,128,256]{2,3,0,1:T(8,128)(2,1)S(1)} collective-permute-done((bf16[2,2,128,256]{2,3,0,1:T(8,128)(2,1)S(1)}, bf16[2,2,128,256]{2,3,0,1:T(8,128)(2,1)S(1)}, u32[]{:S(2)}, u32[]{:S(2)}) %collective-permute-start.9) | collective-permute-done | bytes 262176 | tf_op jit(solution)/shard_map/ppermute | solution.py:60
  131.5 2.0 copy.53
  136.6 4.0 project_inputs.2
  142.9 3.2 maximum_select_fusion
  146.1 4.3 copy.59
  150.4 4.1 maximum_select_fusion.1
  154.5 4.0 copy.60
  162.3 10.1 %attention_forward.3 = (bf16[512,256]{1,0:T(8,128)(2,1)S(1)}, bf16[512,256]{1,0:T(8,128)(2,1)S(1)}, f32[256,1024]{1,0:T(8,128)S(1)}, bf16[256,1024]{1,0:T(8,128)(2,1)S(1)}) custom-call(bf16[512,768]{1,0:T(8,128)(2,1)S(1)} %copy-done.90, bf16[512,768]{1,0:T(8,128)(2,1)S(1)} %copy-done.93, bf16[512,1024]{1,0:T(8,128)(2,1)} %collective-permute-done.23.far_ref, ...), custom_call_target="tpu_custom_call" | custom-call | flops 8589934592 | bytes 5771264 | tf_op jit(solution)/shard_map/attention_forward/pallas_call | solution.py:41
  174.6 10.3 %attention_forward.2 = (bf16[512,256]{1,0:T(8,128)(2,1)S(1)}, bf16[512,256]{1,0:T(8,128)(2,1)S(1)}, f32[256,1024]{1,0:T(8,128)S(1)}, bf16[256,1024]{1,0:T(8,128)(2,1)S(1)}) custom-call(bf16[512,768]{1,0:T(8,128)(2,1)S(1)} %copy-done.84, bf16[512,768]{1,0:T(8,128)(2,1)S(1)} %copy-done.87, bf16[512,1024]{1,0:T(8,128)(2,1)} %collective-permute-done.6.far_ref, ...), custom_call_target="tpu_custom_call" | custom-call | flops 8589934592 | bytes 5771264 | tf_op jit(solution)/shard_map/attention_forward/pallas_call | solution.py:41
  191.2 10.0 %collective-permute-done.11.r_ref = bf16[256,1024]{1,0:T(8,128)(2,1)S(1)} collective-permute-done((bf16[256,1024]{1,0:T(8,128)(2,1)S(1)}, bf16[256,1024]{1,0:T(8,128)(2,1)S(1)}, u32[]{:S(2)}, u32[]{:S(2)}) %collective-permute-start.11) | collective-permute-done | bytes 524320 | tf_op jit(solution)/shard_map/ppermute | solution.py:55
  204.3 8.1 %collective-permute-done.25.n1 = bf16[256,1024]{1,0:T(8,128)(2,1)S(1)} collective-permute-done((bf16[256,1024]{1,0:T(8,128)(2,1)S(1)}, bf16[256,1024]{1,0:T(8,128)(2,1)S(1)}, u32[]{:S(2)}, u32[]{:S(2)}) %collective-permute-start.25) | collective-permute-done | bytes 524320 | tf_op jit(solution)/shard_map/ppermute | solution.py:55
  212.4 11.5 %feed_forward.3 = (bf16[512,1024]{1,0:T(8,128)(2,1)S(1)}, bf16[512,1024]{1,0:T(8,128)(2,1)S(1)}, bf16[512,1024]{1,0:T(8,128)(2,1)S(1)}, bf16[512,1024]{1,0:T(8,1...) custom-call(bf16[256,1024]{1,0:T(8,128)(2,1)S(1)} %get-tuple-element.107.n0, ...), custom_call_target="tpu_custom_call" | custom-call | flops 4294967296 | bytes 15212544 | tf_op jit(solution)/shard_map/feed_forward/pallas_call | solution.py:384
  227.1 12.0 %feed_forward.2 = (bf16[512,1024]{1,0:T(8,128)(2,1)S(1)}, bf16[512,1024]{1,0:T(8,128)(2,1)S(1)}, bf16[512,1024]{1,0:T(8,128)(2,1)S(1)}, bf16[512,1024]{1,0:T(8,1...) custom-call(bf16[256,1024]{1,0:T(8,128)(2,1)S(1)} %get-tuple-element.97.n0, ...), custom_call_target="tpu_custom_call" | custom-call | flops 4294967296 | bytes 15212544 | tf_op jit(solution)/shard_map/feed_forward/pallas_call | solution.py:384
  252.1 3.0 second_norm.3
  257.2 3.3 second_norm.2
  264.6 2.4 pad_maximum_fusion
  268.9 2.3 collective-permute-done.32.g1
  273.7 9.9 %feed_forward_back.3 = (bf16[512,1024]{1,0:T(8,128)(2,1)S(1)}, bf16[512,1024]{1,0:T(8,128)(2,1)S(1)}, f32[256,1024]{1,0:T(8,128)S(1)}, bf16[256,1024]{1,0:T(8,12...) custom-call(bf16[256,1024]{1,0:T(8,128)(2,1)} %get-tuple-element.127.g0, ...), custom_call_target="tpu_custom_call" | custom-call | flops 4294967296 | bytes 15212544 | tf_op jit(solution)/shard_map/feed_forward_back/pallas_call | solution.py:384
  284.7 10.1 %feed_forward_back.2 = (bf16[512,1024]{1,0:T(8,128)(2,1)S(1)}, bf16[512,1024]{1,0:T(8,128)(2,1)S(1)}, f32[256,1024]{1,0:T(8,128)S(1)}, bf16[256,1024]{1,0:T(8,12...) custom-call(bf16[256,1024]{1,0:T(8,128)(2,1)} %get-tuple-element.113.g0, ...), custom_call_target="tpu_custom_call" | custom-call | flops 4294967296 | bytes 15212544 | tf_op jit(solution)/shard_map/feed_forward_back/pallas_call | solution.py:384
  297.3 2.7 add_convert_fusion.1
  300.0 3.3 fusion.35
  307.7 2.8 add_convert_fusion
  316.4 5.0 fusion.36
  323.5 3.3 fusion.38
  326.9 9.3 %collective-permute-done.59 = f32[10240]{0:T(1024)S(1)} collective-permute-done((f32[10240]{0:T(1024)S(1)}, f32[10240]{0:T(1024)S(1)}, u32[]{:S(2)}, u32[]{:S(2)}) %collective-permute-start.59) | collective-permute-done | bytes 40992 | tf_op jit(solution)/shard_map/ppermute | solution.py:55
  340.2 2.1 collective-permute-start.61
  342.3 1.9 collective-permute-done.61
  344.2 4.2 collective-permute-start.62
  351.2 23.6 %attention_backward.3 = (bf16[512,512]{1,0:T(8,128)(2,1)S(1)}, f32[512,1024]{1,0:T(8,128)S(1)}, bf16[512,1024]{1,0:T(8,128)(2,1)}) custom-call(bf16[512,768]{1,0:T(8,128)(2,1)S(1)} %copy-done.91, bf16[512,768]{1,0:T(8,128)(2,1)S(1)} %copy-done.94, bf16[512,1024]{1,0:T(8,128)(2,1)} %collective-permute-done.23.far_ref, f32[1024,1]{1,0:T(8,128)S(1)} %bitcast.219, ...), custom_call_target="tpu_custom_call" | custom-call | flops 10737418240 | bytes 8392704 | tf_op jit(solution)/shard_map/attention_backward/pallas_call | solution.py:41
  386.1 23.8 %attention_backward.2 = (bf16[512,512]{1,0:T(8,128)(2,1)S(1)}, f32[512,1024]{1,0:T(8,128)S(1)}, bf16[512,1024]{1,0:T(8,128)(2,1)}) custom-call(bf16[512,768]{1,0:T(8,128)(2,1)S(1)} %copy-done.85, bf16[512,768]{1,0:T(8,128)(2,1)S(1)} %copy-done.88, bf16[512,1024]{1,0:T(8,128)(2,1)} %collective-permute-done.6.far_ref, f32[1024,1]{1,0:T(8,128)S(1)} %bitcast.218, ...), custom_call_target="tpu_custom_call" | custom-call | flops 10737418240 | bytes 8392704 | tf_op jit(solution)/shard_map/attention_backward/pallas_call | solution.py:41
  412.9 2.1 copy.65
  417.6 4.9 fusion.39
  422.6 3.4 collective-permute-start.44
  427.3 2.9 collective-permute-done.44
  430.9 4.0 project_back.3
  437.7 3.9 project_back.2
  441.6 2.9 fusion.4
  444.6 3.5 add_convert_fusion.2
  448.1 2.8 convert_add_fusion.1
  455.1 5.7 %convert_add_fusion = f32[1024,1024]{1,0:T(8,128)S(1)} fusion(bf16[1024,1024]{1,0:T(8,128)(2,1)} %collective-permute-done.49, f32[1024,1024]{1,0:T(8,128)} %fusion.38, f32[1024,1024]{1,0:T(8,128)} %fusion.39), kind=kLoop, calls=%fused_computation | loop fusion | flops 3145728 | bytes 14680064 | tf_op jit(solution)/shard_map/add | solution.py:511
  462.1 4.0 fusion.6
  467.4 4.0 fusion.5
  471.4 6.8 %collective-permute-done.55 = f32[2048]{0:T(1024)S(1)} collective-permute-done((f32[2048]{0:T(1024)S(1)}, f32[2048]{0:T(1024)S(1)}, u32[]{:S(2)}, u32[]{:S(2)}) %collective-permute-start.55) | collective-permute-done | bytes 8224 | tf_op jit(solution)/shard_map/ppermute | solution.py:60
  478.5 3.4 collective-permute-done.56
  487.5 2.4 copy.74
  493.4 3.8 collective-permute-done.31
  503.4 2.2 convert_add_fusion.2
  507.2 9.1 %collective-permute-done.50 = bf16[2,2,128,1024]{2,3,0,1:T(8,128)(2,1)S(1)} collective-permute-done((bf16[2,2,128,1024]{2,3,0,1:T(8,128)(2,1)}, bf16[2,2,128,1024]{2,3,0,1:T(8,128)(2,1)S(1)}, u32[]{:S(2)}, u32[]{:S(2)}) %collective-permute-start.50) | collective-permute-done | bytes 1048608 | tf_op jit(solution)/shard_map/ppermute | solution.py:60
  516.5 2.0 collective-permute-start.51
  518.8 11.5 %collective-permute-done.38 = bf16[2,2,128,768]{3,2,0,1:T(8,128)(2,1)S(1)} collective-permute-done((bf16[2,2,128,768]{3,2,0,1:T(8,128)(2,1)S(1)}, bf16[2,2,128,768]{3,2,0,1:T(8,128)(2,1)S(1)}, u32[]{:S(2)}, u32[]{:S(2)}) %collective-permute-start.38) | collective-permute-done | bytes 786464 | tf_op jit(solution)/shard_map/ppermute | solution.py:60
  533.8 10.9 %collective-permute-done.39 = bf16[2,128,768]{2,1,0:T(8,128)(2,1)S(1)} collective-permute-done((bf16[2,128,768]{2,1,0:T(8,128)(2,1)S(1)}, bf16[2,128,768]{2,1,0:T(8,128)(2,1)S(1)}, u32[]{:S(2)}, u32[]{:S(2)}) %collective-permute-start.39) | collective-permute-done | bytes 393248 | tf_op jit(solution)/shard_map/ppermute | solution.py:60
  545.8 7.9 %collective-permute-done.40 = bf16[128,768]{1,0:T(8,128)(2,1)S(1)} collective-permute-done((bf16[128,768]{1,0:T(8,128)(2,1)S(1)}, bf16[128,768]{1,0:T(8,128)(2,1)S(1)}, u32[]{:S(2)}, u32[]{:S(2)}) %collective-permute-start.40) | collective-permute-done | bytes 196640 | tf_op jit(solution)/shard_map/ppermute | solution.py:60
  (490 shorter events, 154.4 us)
Async XLA Ops:
  3.2 13.1 %collective-permute-start.1 = (bf16[128,768]{1,0:T(8,128)(2,1)S(1)}, bf16[128,768]{1,0:T(8,128)(2,1)S(1)}, u32[]{:S(2)}, u32[]{:S(2)}) collective-permute-start(bf16[128,768]{1,0:T(8,128)(2,1)S(1)} %constant_dynamic-update-slice_fusion), channel_id=1, source_target_pairs={{0,16},{4,20},{8,24},{12,28},{16,0},{20,4},{24,8},{28,12},{1,17},{... | collective-permute-start | bytes 589832 | tf_op jit(solution)/shard_map/ppermute | solution.py:60
  16.4 10.4 %collective-permute-start.2 = (bf16[2,128,768]{2,1,0:T(8,128)(2,1)S(1)}, bf16[2,128,768]{2,1,0:T(8,128)(2,1)S(1)}, u32[]{:S(2)}, u32[]{:S(2)}) collective-permute-start(bf16[2,128,768]{2,1,0:T(8,128)(2,1)S(1)} %maximum_select_fusion.14), channel_id=1, source_target_pairs={{0,8},{4,12},{8,0},{12,4},{16,24},{20,28},{24,16},{28,20},{1,9},{5... | collective-permute-start | bytes 1179656 | tf_op jit(solution)/shard_map/ppermute | solution.py:60
  19.5 74.2 %collective-permute-start.22 = (bf16[256,1024]{1,0:T(8,128)(2,1)}, bf16[256,1024]{1,0:T(8,128)(2,1)}, u32[]{:S(2)}, u32[]{:S(2)}) collective-permute-start(bf16[256,1024]{1,0:T(8,128)(2,1)} %get-tuple-element.168.x0.x_ref), channel_id=1, source_target_pairs={{0,2},{1,3},{2,0},{3,1},{4,6},{5,7},{6,4},{7,5},{8,10},{9,11},{10,... | collective-permute-start | bytes 1572872 | tf_op jit(solution)/shard_map/ppermute | solution.py:55
  27.0 18.0 %collective-permute-start.3 = (bf16[2,2,128,768]{3,2,0,1:T(8,128)(2,1)S(1)}, bf16[2,2,128,768]{3,2,0,1:T(8,128)(2,1)S(1)}, u32[]{:S(2)}, u32[]{:S(2)}) collective-permute-start(bf16[2,2,128,768]{3,2,0,1:T(8,128)(2,1)S(1)} %maximum_select_fusion.8), channel_id=1, source_target_pairs={{0,4},{4,0},{8,12},{12,8},{16,20},{20,16},{24,28},{28,24},{1,5},{5... | collective-permute-start | bytes 2359304 | tf_op jit(solution)/shard_map/ppermute | solution.py:60
  28.3 19.4 %collective-permute-start.5 = (f32[1792]{0:T(1024)S(1)}, f32[1792]{0:T(1024)S(1)}, u32[]{:S(2)}, u32[]{:S(2)}) collective-permute-start(f32[1792]{0:T(1024)S(1)} %pad_maximum_fusion.9), channel_id=1, source_target_pairs={{0,1},{1,0},{2,3},{3,2},{4,5},{5,4},{6,7},{7,6},{8,9},{9,8},{10,11... | collective-permute-start | bytes 21512 | tf_op jit(solution)/shard_map/ppermute | solution.py:55
  28.4 24.2 %collective-permute-start.7 = (bf16[128,256]{0,1:T(8,128)(2,1)S(1)}, bf16[128,256]{0,1:T(8,128)(2,1)}, u32[]{:S(2)}, u32[]{:S(2)}) collective-permute-start(bf16[128,256]{0,1:T(8,128)(2,1)S(1)} %bitcast.276), channel_id=1, source_target_pairs={{0,16},{4,20},{8,24},{12,28},{16,0},{20,4},{24,8},{28,12},{1,17},{... | collective-permute-start | bytes 196616 | tf_op jit(solution)/shard_map/ppermute | solution.py:60
  32.9 24.1 %collective-permute-start.13 = (bf16[128,1024]{0,1:T(8,128)(2,1)S(1)}, bf16[128,1024]{0,1:T(8,128)(2,1)}, u32[]{:S(2)}, u32[]{:S(2)}) collective-permute-start(bf16[128,1024]{0,1:T(8,128)(2,1)S(1)} %copy.54), channel_id=1, source_target_pairs={{0,16},{4,20},{8,24},{12,28},{16,0},{20,4},{24,8},{28,12},{1,17},{... | collective-permute-start | bytes 786440 | tf_op jit(solution)/shard_map/ppermute | solution.py:60
  47.5 46.7 %collective-permute-start.4 = (bf16[1024,768]{1,0:T(8,128)(2,1)S(1)}, bf16[1024,768]{1,0:T(8,128)(2,1)S(1)}, u32[]{:S(2)}, u32[]{:S(2)}) collective-permute-start(bf16[1024,768]{1,0:T(8,128)(2,1)S(1)} %bitcast.198), channel_id=1, source_target_pairs={{0,1},{1,0},{2,3},{3,2},{4,5},{5,4},{6,7},{7,6},{8,9},{9,8},{10,11... | collective-permute-start | bytes 4718600 | tf_op jit(solution)/shard_map/ppermute | solution.py:55
  48.4 16.3 %collective-permute-start.17 = (bf16[128,1024]{0,1:T(8,128)(2,1)S(1)}, bf16[128,1024]{0,1:T(8,128)(2,1)S(1)}, u32[]{:S(2)}, u32[]{:S(2)}) collective-permute-start(bf16[128,1024]{0,1:T(8,128)(2,1)S(1)} %bitcast.255), channel_id=1, source_target_pairs={{0,16},{4,20},{8,24},{12,28},{16,0},{20,4},{24,8},{28,12},{1,17},{... | collective-permute-start | bytes 786440 | tf_op jit(solution)/shard_map/ppermute | solution.py:60
  52.6 84.0 %collective-permute-start = (bf16[256,1024]{1,0:T(8,128)(2,1)}, bf16[256,1024]{1,0:T(8,128)(2,1)}, u32[]{:S(2)}, u32[]{:S(2)}) collective-permute-start(bf16[256,1024]{1,0:T(8,128)(2,1)} %get-tuple-element.167.x0.x_ref), channel_id=1, source_target_pairs={{0,2},{1,3},{2,0},{3,1},{4,6},{5,7},{6,4},{7,5},{8,10},{9,11},{10,... | collective-permute-start | bytes 1572872 | tf_op jit(solution)/shard_map/ppermute | solution.py:55
  57.0 9.4 %collective-permute-start.8 = (bf16[2,128,256]{1,2,0:T(8,128)(2,1)S(1)}, bf16[2,128,256]{1,2,0:T(8,128)(2,1)S(1)}, u32[]{:S(2)}, u32[]{:S(2)}) collective-permute-start(bf16[2,128,256]{1,2,0:T(8,128)(2,1)S(1)} %maximum_select_fusion.18), channel_id=1, source_target_pairs={{0,8},{4,12},{8,0},{12,4},{16,24},{20,28},{24,16},{28,20},{1,9},{5... | collective-permute-start | bytes 393224 | tf_op jit(solution)/shard_map/ppermute | solution.py:60
  64.7 14.9 %collective-permute-start.14 = (bf16[2,128,1024]{1,2,0:T(8,128)(2,1)S(1)}, bf16[2,128,1024]{1,2,0:T(8,128)(2,1)S(1)}, u32[]{:S(2)}, u32[]{:S(2)}) collective-permute-start(bf16[2,128,1024]{1,2,0:T(8,128)(2,1)S(1)} %maximum_select_fusion.10), channel_id=1, source_target_pairs={{0,8},{4,12},{8,0},{12,4},{16,24},{20,28},{24,16},{28,20},{1,9},{5... | collective-permute-start | bytes 1572872 | tf_op jit(solution)/shard_map/ppermute | solution.py:60
  66.5 22.5 %collective-permute-start.18 = (bf16[2,128,1024]{1,2,0:T(8,128)(2,1)S(1)}, bf16[2,128,1024]{1,2,0:T(8,128)(2,1)S(1)}, u32[]{:S(2)}, u32[]{:S(2)}) collective-permute-start(bf16[2,128,1024]{1,2,0:T(8,128)(2,1)S(1)} %maximum_select_fusion.12), channel_id=1, source_target_pairs={{0,8},{4,12},{8,0},{12,4},{16,24},{20,28},{24,16},{28,20},{1,9},{5... | collective-permute-start | bytes 1572872 | tf_op jit(solution)/shard_map/ppermute | solution.py:60
  80.7 62.2 %collective-permute-start.15 = (bf16[2,2,128,1024]{2,3,0,1:T(8,128)(2,1)}, bf16[2,2,128,1024]{2,3,0,1:T(8,128)(2,1)}, u32[]{:S(2)}, u32[]{:S(2)}) collective-permute-start(bf16[2,2,128,1024]{2,3,0,1:T(8,128)(2,1)} %maximum_select_fusion.4), channel_id=1, source_target_pairs={{0,4},{4,0},{8,12},{12,8},{16,20},{20,16},{24,28},{28,24},{1,5},{5... | collective-permute-start | bytes 3145736 | tf_op jit(solution)/shard_map/ppermute | solution.py:60
  90.2 60.2 %collective-permute-start.19 = (bf16[2,2,128,1024]{2,3,0,1:T(8,128)(2,1)}, bf16[2,2,128,1024]{2,3,0,1:T(8,128)(2,1)}, u32[]{:S(2)}, u32[]{:S(2)}) collective-permute-start(bf16[2,2,128,1024]{2,3,0,1:T(8,128)(2,1)} %maximum_select_fusion.6), channel_id=1, source_target_pairs={{0,4},{4,0},{8,12},{12,8},{16,20},{20,16},{24,28},{28,24},{1,5},{5... | collective-permute-start | bytes 3145736 | tf_op jit(solution)/shard_map/ppermute | solution.py:60
  93.7 36.9 %collective-permute-start.9 = (bf16[2,2,128,256]{2,3,0,1:T(8,128)(2,1)S(1)}, bf16[2,2,128,256]{2,3,0,1:T(8,128)(2,1)S(1)}, u32[]{:S(2)}, u32[]{:S(2)}) collective-permute-start(bf16[2,2,128,256]{2,3,0,1:T(8,128)(2,1)S(1)} %maximum_select_fusion.16), channel_id=1, source_target_pairs={{0,4},{4,0},{8,12},{12,8},{16,20},{20,16},{24,28},{28,24},{1,5},{5... | collective-permute-start | bytes 786440 | tf_op jit(solution)/shard_map/ppermute | solution.py:60
  100.1 58.9 %collective-permute-start.23 = (bf16[512,1024]{1,0:T(8,128)(2,1)}, bf16[512,1024]{1,0:T(8,128)(2,1)}, u32[]{:S(2)}, u32[]{:S(2)}) collective-permute-start(bf16[512,1024]{1,0:T(8,128)(2,1)} %get-tuple-element.103), channel_id=1, source_target_pairs={{0,1},{1,0},{2,3},{3,2},{4,5},{5,4},{6,7},{7,6},{8,9},{9,8},{10,11... | collective-permute-start | bytes 3145736 | tf_op jit(solution)/shard_map/ppermute | solution.py:55
  133.6 25.4 %collective-permute-start.10 = (bf16[1024,256]{1,0:T(8,128)(2,1)}, bf16[1024,256]{1,0:T(8,128)(2,1)}, u32[]{:S(2)}, u32[]{:S(2)}) collective-permute-start(bf16[1024,256]{1,0:T(8,128)(2,1)} %bitcast.213), channel_id=1, source_target_pairs={{0,1},{1,0},{2,3},{3,2},{4,5},{5,4},{6,7},{7,6},{8,9},{9,8},{10,11... | collective-permute-start | bytes 1572872 | tf_op jit(solution)/shard_map/ppermute | solution.py:55
  142.4 32.2 %collective-permute-start.6 = (bf16[512,1024]{1,0:T(8,128)(2,1)}, bf16[512,1024]{1,0:T(8,128)(2,1)}, u32[]{:S(2)}, u32[]{:S(2)}) collective-permute-start(bf16[512,1024]{1,0:T(8,128)(2,1)} %get-tuple-element.93), channel_id=1, source_target_pairs={{0,1},{1,0},{2,3},{3,2},{4,5},{5,4},{6,7},{7,6},{8,9},{9,8},{10,11... | collective-permute-start | bytes 3145736 | tf_op jit(solution)/shard_map/ppermute | solution.py:55
  150.4 53.9 %collective-permute-start.16 = (bf16[1024,1024]{1,0:T(8,128)(2,1)}, bf16[1024,1024]{1,0:T(8,128)(2,1)}, u32[]{:S(2)}, u32[]{:S(2)}) collective-permute-start(bf16[1024,1024]{1,0:T(8,128)(2,1)} %bitcast.203), channel_id=1, source_target_pairs={{0,1},{1,0},{2,3},{3,2},{4,5},{5,4},{6,7},{7,6},{8,9},{9,8},{10,11... | collective-permute-start | bytes 6291464 | tf_op jit(solution)/shard_map/ppermute | solution.py:55
  158.5 45.8 %collective-permute-start.20 = (bf16[1024,1024]{1,0:T(8,128)(2,1)}, bf16[1024,1024]{1,0:T(8,128)(2,1)S(1)}, u32[]{:S(2)}, u32[]{:S(2)}) collective-permute-start(bf16[1024,1024]{1,0:T(8,128)(2,1)} %bitcast.208), channel_id=1, source_target_pairs={{0,1},{1,0},{2,3},{3,2},{4,5},{5,4},{6,7},{7,6},{8,9},{9,8},{10,11... | collective-permute-start | bytes 6291464 | tf_op jit(solution)/shard_map/ppermute | solution.py:55
  173.1 13.9 %collective-permute-start.24 = (bf16[256,1024]{1,0:T(8,128)(2,1)S(1)}, bf16[256,1024]{1,0:T(8,128)(2,1)S(1)}, u32[]{:S(2)}, u32[]{:S(2)}) collective-permute-start(bf16[256,1024]{1,0:T(8,128)(2,1)S(1)} %get-tuple-element.105), channel_id=1, source_target_pairs={{0,2},{1,3},{2,0},{3,1},{4,6},{5,7},{6,4},{7,5},{8,10},{9,11},{10,... | collective-permute-start | bytes 1572872 | tf_op jit(solution)/shard_map/ppermute | solution.py:55
  186.3 14.8 %collective-permute-start.11 = (bf16[256,1024]{1,0:T(8,128)(2,1)S(1)}, bf16[256,1024]{1,0:T(8,128)(2,1)S(1)}, u32[]{:S(2)}, u32[]{:S(2)}) collective-permute-start(bf16[256,1024]{1,0:T(8,128)(2,1)S(1)} %get-tuple-element.95), channel_id=1, source_target_pairs={{0,2},{1,3},{2,0},{3,1},{4,6},{5,7},{6,4},{7,5},{8,10},{9,11},{10,... | collective-permute-start | bytes 1572872 | tf_op jit(solution)/shard_map/ppermute | solution.py:55
  189.7 34.3 %copy-start.51 = (bf16[256,1024]{1,0:T(8,128)(2,1)}, bf16[256,1024]{1,0:T(8,128)(2,1)S(1)}, u32[]{:S(2)}) copy-start(bf16[256,1024]{1,0:T(8,128)(2,1)S(1)} %get-tuple-element.107.n0) | copy-start | bytes 1572868
  189.7 22.7 %collective-permute-start.25 = (bf16[256,1024]{1,0:T(8,128)(2,1)S(1)}, bf16[256,1024]{1,0:T(8,128)(2,1)S(1)}, u32[]{:S(2)}, u32[]{:S(2)}) collective-permute-start(bf16[256,1024]{1,0:T(8,128)(2,1)S(1)} %get-tuple-element.107.n0), channel_id=1, source_target_pairs={{0,2},{1,3},{2,0},{3,1},{4,6},{5,7},{6,4},{7,5},{8,10},{9,11},{10,... | collective-permute-start | bytes 1572872 | tf_op jit(solution)/shard_map/ppermute | solution.py:55
  203.8 23.3 %collective-permute-start.12 = (bf16[256,1024]{1,0:T(8,128)(2,1)S(1)}, bf16[256,1024]{1,0:T(8,128)(2,1)S(1)}, u32[]{:S(2)}, u32[]{:S(2)}) collective-permute-start(bf16[256,1024]{1,0:T(8,128)(2,1)S(1)} %get-tuple-element.97.n0), channel_id=1, source_target_pairs={{0,2},{1,3},{2,0},{3,1},{4,6},{5,7},{6,4},{7,5},{8,10},{9,11},{10,... | collective-permute-start | bytes 1572872 | tf_op jit(solution)/shard_map/ppermute | solution.py:55
  226.1 24.7 %collective-permute-start.26 = (bf16[256,1024]{1,0:T(8,128)(2,1)}, bf16[256,1024]{1,0:T(8,128)(2,1)}, u32[]{:S(2)}, u32[]{:S(2)}) collective-permute-start(bf16[256,1024]{1,0:T(8,128)(2,1)} %get-tuple-element.109), channel_id=1, source_target_pairs={{0,2},{1,3},{2,0},{3,1},{4,6},{5,7},{6,4},{7,5},{8,10},{9,11},{10,... | collective-permute-start | bytes 1572872 | tf_op jit(solution)/shard_map/ppermute | solution.py:55
  244.2 12.9 %collective-permute-start.21 = (bf16[256,1024]{1,0:T(8,128)(2,1)}, bf16[256,1024]{1,0:T(8,128)(2,1)}, u32[]{:S(2)}, u32[]{:S(2)}) collective-permute-start(bf16[256,1024]{1,0:T(8,128)(2,1)} %get-tuple-element.99), channel_id=1, source_target_pairs={{0,2},{1,3},{2,0},{3,1},{4,6},{5,7},{6,4},{7,5},{8,10},{9,11},{10,... | collective-permute-start | bytes 1572872 | tf_op jit(solution)/shard_map/ppermute | solution.py:55
  256.1 15.2 %collective-permute-start.32 = (bf16[256,1024]{1,0:T(8,128)(2,1)}, bf16[256,1024]{1,0:T(8,128)(2,1)}, u32[]{:S(2)}, u32[]{:S(2)}) collective-permute-start(bf16[256,1024]{1,0:T(8,128)(2,1)} %get-tuple-element.127.g0), channel_id=1, source_target_pairs={{0,2},{1,3},{2,0},{3,1},{4,6},{5,7},{6,4},{7,5},{8,10},{9,11},{10,... | collective-permute-start | bytes 1572872 | tf_op jit(solution)/shard_map/ppermute | solution.py:55
  262.2 22.4 %collective-permute-start.27 = (bf16[256,1024]{1,0:T(8,128)(2,1)}, bf16[256,1024]{1,0:T(8,128)(2,1)}, u32[]{:S(2)}, u32[]{:S(2)}) collective-permute-start(bf16[256,1024]{1,0:T(8,128)(2,1)} %get-tuple-element.113.g0), channel_id=1, source_target_pairs={{0,2},{1,3},{2,0},{3,1},{4,6},{5,7},{6,4},{7,5},{8,10},{9,11},{10,... | collective-permute-start | bytes 1572872 | tf_op jit(solution)/shard_map/ppermute | solution.py:55
  283.7 26.8 %collective-permute-start.33 = (bf16[256,1024]{1,0:T(8,128)(2,1)S(1)}, bf16[256,1024]{1,0:T(8,128)(2,1)S(1)}, u32[]{:S(2)}, u32[]{:S(2)}) collective-permute-start(bf16[256,1024]{1,0:T(8,128)(2,1)S(1)} %get-tuple-element.131), channel_id=1, source_target_pairs={{0,2},{1,3},{2,0},{3,1},{4,6},{5,7},{6,4},{7,5},{8,10},{9,11},{10,... | collective-permute-start | bytes 1572872 | tf_op jit(solution)/shard_map/ppermute | solution.py:55
  294.8 18.4 %collective-permute-start.28 = (bf16[256,1024]{1,0:T(8,128)(2,1)S(1)}, bf16[256,1024]{1,0:T(8,128)(2,1)S(1)}, u32[]{:S(2)}, u32[]{:S(2)}) collective-permute-start(bf16[256,1024]{1,0:T(8,128)(2,1)S(1)} %get-tuple-element.117), channel_id=1, source_target_pairs={{0,2},{1,3},{2,0},{3,1},{4,6},{5,7},{6,4},{7,5},{8,10},{9,11},{10,... | collective-permute-start | bytes 1572872 | tf_op jit(solution)/shard_map/ppermute | solution.py:55
  300.0 148.2 %collective-permute-start.45 = (bf16[1024,1024]{1,0:T(8,128)(2,1)}, bf16[1024,1024]{1,0:T(8,128)(2,1)}, u32[]{:S(2)}, u32[]{:S(2)}) collective-permute-start(bf16[1024,1024]{1,0:T(8,128)(2,1)} %add_convert_fusion.1), channel_id=1, source_target_pairs={{0,1},{1,0},{2,3},{3,2},{4,5},{5,4},{6,7},{7,6},{8,9},{9,8},{10,11... | collective-permute-start | bytes 6291464 | tf_op jit(solution)/shard_map/ppermute | solution.py:55
  315.9 6.4 %collective-permute-start.58 = (f32[10240]{0:T(1024)S(1)}, f32[10240]{0:T(1024)S(1)}, u32[]{:S(2)}, u32[]{:S(2)}) collective-permute-start(f32[10240]{0:T(1024)S(1)} %pad_maximum_fusion.8), channel_id=1, source_target_pairs={{0,1},{1,0},{2,3},{3,2},{4,5},{5,4},{6,7},{7,6},{8,9},{9,8},{10,11... | collective-permute-start | bytes 122888 | tf_op jit(solution)/shard_map/ppermute | solution.py:55
  321.4 27.0 %collective-permute-start.34 = (bf16[256,1024]{1,0:T(8,128)(2,1)S(1)}, bf16[256,1024]{1,0:T(8,128)(2,1)S(1)}, u32[]{:S(2)}, u32[]{:S(2)}) collective-permute-start(bf16[256,1024]{1,0:T(8,128)(2,1)S(1)} %copy-done.57), channel_id=1, source_target_pairs={{0,2},{1,3},{2,0},{3,1},{4,6},{5,7},{6,4},{7,5},{8,10},{9,11},{10,... | collective-permute-start | bytes 1572872 | tf_op jit(solution)/shard_map/ppermute | solution.py:55
  322.3 13.9 %collective-permute-start.59 = (f32[10240]{0:T(1024)S(1)}, f32[10240]{0:T(1024)S(1)}, u32[]{:S(2)}, u32[]{:S(2)}) collective-permute-start(f32[10240]{0:T(1024)S(1)} %fusion.27), channel_id=1, source_target_pairs={{0,2},{1,3},{2,0},{3,1},{4,6},{5,7},{6,4},{7,5},{8,10},{9,11},{10,... | collective-permute-start | bytes 122888 | tf_op jit(solution)/shard_map/ppermute | solution.py:55
  336.2 4.0 collective-permute-start.60
  337.7 12.8 %collective-permute-start.29 = (bf16[256,1024]{1,0:T(8,128)(2,1)S(1)}, bf16[256,1024]{1,0:T(8,128)(2,1)S(1)}, u32[]{:S(2)}, u32[]{:S(2)}) collective-permute-start(bf16[256,1024]{1,0:T(8,128)(2,1)S(1)} %copy-done.54), channel_id=1, source_target_pairs={{0,2},{1,3},{2,0},{3,1},{4,6},{5,7},{6,4},{7,5},{8,10},{9,11},{10,... | collective-permute-start | bytes 1572872 | tf_op jit(solution)/shard_map/ppermute | solution.py:55
  340.2 4.0 collective-permute-start.61
  344.2 78.3 %collective-permute-start.62 = (f32[10240]{0:T(1024)S(1)}, f32[10240]{0:T(1024)S(1)}, u32[]{:S(2)}, u32[]{:S(2)}) collective-permute-start(f32[10240]{0:T(1024)S(1)} %add.283), channel_id=1, source_target_pairs={{0,16},{4,20},{8,24},{12,28},{16,0},{20,4},{24,8},{28,12},{1,17},{... | collective-permute-start | bytes 122888 | tf_op jit(solution)/shard_map/ppermute | solution.py:60
  351.1 24.7 %collective-permute-start.41 = (bf16[1024,256]{1,0:T(8,128)(2,1)S(1)}, bf16[1024,256]{1,0:T(8,128)(2,1)S(1)}, u32[]{:S(2)}, u32[]{:S(2)}) collective-permute-start(bf16[1024,256]{1,0:T(8,128)(2,1)S(1)} %fusion.1), channel_id=1, source_target_pairs={{0,1},{1,0},{2,3},{3,2},{4,5},{5,4},{6,7},{7,6},{8,9},{9,8},{10,11... | collective-permute-start | bytes 1572872 | tf_op jit(solution)/shard_map/ppermute | solution.py:55
  374.8 56.1 %collective-permute-start.35 = (bf16[512,1024]{1,0:T(8,128)(2,1)}, bf16[512,1024]{1,0:T(8,128)(2,1)}, u32[]{:S(2)}, u32[]{:S(2)}) collective-permute-start(bf16[512,1024]{1,0:T(8,128)(2,1)} %get-tuple-element.136), channel_id=1, source_target_pairs={{0,1},{1,0},{2,3},{3,2},{4,5},{5,4},{6,7},{7,6},{8,9},{9,8},{10,11... | collective-permute-start | bytes 3145736 | tf_op jit(solution)/shard_map/ppermute | solution.py:55
  378.3 36.7 %collective-permute-start.42 = (bf16[2,2,128,256]{2,3,0,1:T(8,128)(2,1)}, bf16[2,2,128,256]{2,3,0,1:T(8,128)(2,1)S(1)}, u32[]{:S(2)}, u32[]{:S(2)}) collective-permute-start(bf16[2,2,128,256]{2,3,0,1:T(8,128)(2,1)} %bitcast.282), channel_id=1, source_target_pairs={{0,4},{4,0},{8,12},{12,8},{16,20},{20,16},{24,28},{28,24},{1,5},{5... | collective-permute-start | bytes 786440 | tf_op jit(solution)/shard_map/ppermute | solution.py:60
  412.1 25.6 %collective-permute-start.30 = (bf16[512,1024]{1,0:T(8,128)(2,1)}, bf16[512,1024]{1,0:T(8,128)(2,1)}, u32[]{:S(2)}, u32[]{:S(2)}) collective-permute-start(bf16[512,1024]{1,0:T(8,128)(2,1)} %get-tuple-element.122), channel_id=1, source_target_pairs={{0,1},{1,0},{2,3},{3,2},{4,5},{5,4},{6,7},{7,6},{8,9},{9,8},{10,11... | collective-permute-start | bytes 3145736 | tf_op jit(solution)/shard_map/ppermute | solution.py:55
  416.1 6.4 %collective-permute-start.43 = (bf16[2,128,256]{1,2,0:T(8,128)(2,1)S(1)}, bf16[2,128,256]{1,2,0:T(8,128)(2,1)S(1)}, u32[]{:S(2)}, u32[]{:S(2)}) collective-permute-start(bf16[2,128,256]{1,2,0:T(8,128)(2,1)S(1)} %fusion.17), channel_id=1, source_target_pairs={{0,8},{4,12},{8,0},{12,4},{16,24},{20,28},{24,16},{28,20},{1,9},{5... | collective-permute-start | bytes 393224 | tf_op jit(solution)/shard_map/ppermute | solution.py:60
  422.5 32.6 %collective-permute-start.49 = (bf16[1024,1024]{1,0:T(8,128)(2,1)}, bf16[1024,1024]{1,0:T(8,128)(2,1)}, u32[]{:S(2)}, u32[]{:S(2)}) collective-permute-start(bf16[1024,1024]{1,0:T(8,128)(2,1)} %add_convert_fusion), channel_id=1, source_target_pairs={{0,1},{1,0},{2,3},{3,2},{4,5},{5,4},{6,7},{7,6},{8,9},{9,8},{10,11... | collective-permute-start | bytes 6291464 | tf_op jit(solution)/shard_map/ppermute | solution.py:55
  422.6 7.6 %collective-permute-start.44 = (bf16[128,256]{0,1:T(8,128)(2,1)S(1)}, bf16[128,256]{0,1:T(8,128)(2,1)S(1)}, u32[]{:S(2)}, u32[]{:S(2)}) collective-permute-start(bf16[128,256]{0,1:T(8,128)(2,1)S(1)} %fusion.19), channel_id=1, source_target_pairs={{0,16},{4,20},{8,24},{12,28},{16,0},{20,4},{24,8},{28,12},{1,17},{... | collective-permute-start | bytes 196616 | tf_op jit(solution)/shard_map/ppermute | solution.py:60
  436.8 55.2 %collective-permute-start.36 = (bf16[256,1024]{1,0:T(8,128)(2,1)}, bf16[256,1024]{1,0:T(8,128)(2,1)}, u32[]{:S(2)}, u32[]{:S(2)}) collective-permute-start(bf16[256,1024]{1,0:T(8,128)(2,1)} %get-tuple-element.138), channel_id=1, source_target_pairs={{0,2},{1,3},{2,0},{3,1},{4,6},{5,7},{6,4},{7,5},{8,10},{9,11},{10,... | collective-permute-start | bytes 1572872 | tf_op jit(solution)/shard_map/ppermute | solution.py:55
  448.1 55.2 %collective-permute-start.37 = (bf16[1024,768]{1,0:T(8,128)(2,1)}, bf16[1024,768]{1,0:T(8,128)(2,1)}, u32[]{:S(2)}, u32[]{:S(2)}) collective-permute-start(bf16[1024,768]{1,0:T(8,128)(2,1)} %add_convert_fusion.2), channel_id=1, source_target_pairs={{0,1},{1,0},{2,3},{3,2},{4,5},{5,4},{6,7},{7,6},{8,9},{9,8},{10,11... | collective-permute-start | bytes 4718600 | tf_op jit(solution)/shard_map/ppermute | solution.py:55
  452.3 47.4 %collective-permute-start.46 = (bf16[2,2,128,1024]{3,2,0,1:T(8,128)(2,1)}, bf16[2,2,128,1024]{3,2,0,1:T(8,128)(2,1)}, u32[]{:S(2)}, u32[]{:S(2)}) collective-permute-start(bf16[2,2,128,1024]{3,2,0,1:T(8,128)(2,1)} %fusion.2), channel_id=1, source_target_pairs={{0,4},{4,0},{8,12},{12,8},{16,20},{20,16},{24,28},{28,24},{1,5},{5... | collective-permute-start | bytes 3145736 | tf_op jit(solution)/shard_map/ppermute | solution.py:60
  454.9 6.0 %collective-permute-start.53 = (f32[2048]{0:T(1024)S(1)}, f32[2048]{0:T(1024)S(1)}, u32[]{:S(2)}, u32[]{:S(2)}) collective-permute-start(f32[2048]{0:T(1024)S(1)} %pad_maximum_fusion.10), channel_id=1, source_target_pairs={{0,1},{1,0},{2,3},{3,2},{4,5},{5,4},{6,7},{7,6},{8,9},{9,8},{10,11... | collective-permute-start | bytes 24584 | tf_op jit(solution)/shard_map/ppermute | solution.py:55
  460.9 5.3 collective-permute-start.54
  466.1 12.1 %collective-permute-start.55 = (f32[2048]{0:T(1024)S(1)}, f32[2048]{0:T(1024)S(1)}, u32[]{:S(2)}, u32[]{:S(2)}) collective-permute-start(f32[2048]{0:T(1024)S(1)} %add.270), channel_id=1, source_target_pairs={{0,4},{4,0},{8,12},{12,8},{16,20},{20,16},{24,28},{28,24},{1,5},{5... | collective-permute-start | bytes 24584 | tf_op jit(solution)/shard_map/ppermute | solution.py:60
  478.3 3.7 collective-permute-start.56
  481.9 8.0 %collective-permute-start.57 = (f32[2048]{0:T(1024)S(1)}, f32[2048]{0:T(1024)S(1)}, u32[]{:S(2)}, u32[]{:S(2)}) collective-permute-start(f32[2048]{0:T(1024)S(1)} %add.272), channel_id=1, source_target_pairs={{0,16},{4,20},{8,24},{12,28},{16,0},{20,4},{24,8},{28,12},{1,17},{... | collective-permute-start | bytes 24584 | tf_op jit(solution)/shard_map/ppermute | solution.py:60
  484.5 12.7 %collective-permute-start.31 = (bf16[256,1024]{1,0:T(8,128)(2,1)}, bf16[256,1024]{1,0:T(8,128)(2,1)}, u32[]{:S(2)}, u32[]{:S(2)}) collective-permute-start(bf16[256,1024]{1,0:T(8,128)(2,1)} %get-tuple-element.124), channel_id=1, source_target_pairs={{0,2},{1,3},{2,0},{3,1},{4,6},{5,7},{6,4},{7,5},{8,10},{9,11},{10,... | collective-permute-start | bytes 1572872 | tf_op jit(solution)/shard_map/ppermute | solution.py:55
  489.9 26.4 %collective-permute-start.50 = (bf16[2,2,128,1024]{2,3,0,1:T(8,128)(2,1)}, bf16[2,2,128,1024]{2,3,0,1:T(8,128)(2,1)S(1)}, u32[]{:S(2)}, u32[]{:S(2)}) collective-permute-start(bf16[2,2,128,1024]{2,3,0,1:T(8,128)(2,1)} %bitcast.274), channel_id=1, source_target_pairs={{0,4},{4,0},{8,12},{12,8},{16,20},{20,16},{24,28},{28,24},{1,5},{5... | collective-permute-start | bytes 3145736 | tf_op jit(solution)/shard_map/ppermute | solution.py:60
  501.5 17.0 %collective-permute-start.47 = (bf16[2,128,1024]{2,1,0:T(8,128)(2,1)S(1)}, bf16[2,128,1024]{2,1,0:T(8,128)(2,1)S(1)}, u32[]{:S(2)}, u32[]{:S(2)}) collective-permute-start(bf16[2,128,1024]{2,1,0:T(8,128)(2,1)S(1)} %fusion.9), channel_id=1, source_target_pairs={{0,8},{4,12},{8,0},{12,4},{16,24},{20,28},{24,16},{28,20},{1,9},{5... | collective-permute-start | bytes 1572872 | tf_op jit(solution)/shard_map/ppermute | solution.py:60
  505.6 24.7 %collective-permute-start.38 = (bf16[2,2,128,768]{3,2,0,1:T(8,128)(2,1)S(1)}, bf16[2,2,128,768]{3,2,0,1:T(8,128)(2,1)S(1)}, u32[]{:S(2)}, u32[]{:S(2)}) collective-permute-start(bf16[2,2,128,768]{3,2,0,1:T(8,128)(2,1)S(1)} %fusion.3), channel_id=1, source_target_pairs={{0,4},{4,0},{8,12},{12,8},{16,20},{20,16},{24,28},{28,24},{1,5},{5... | collective-permute-start | bytes 2359304 | tf_op jit(solution)/shard_map/ppermute | solution.py:60
  516.5 15.9 %collective-permute-start.51 = (bf16[2,128,1024]{1,2,0:T(8,128)(2,1)S(1)}, bf16[2,128,1024]{1,2,0:T(8,128)(2,1)S(1)}, u32[]{:S(2)}, u32[]{:S(2)}) collective-permute-start(bf16[2,128,1024]{1,2,0:T(8,128)(2,1)S(1)} %fusion.10), channel_id=1, source_target_pairs={{0,8},{4,12},{8,0},{12,4},{16,24},{20,28},{24,16},{28,20},{1,9},{5... | collective-permute-start | bytes 1572872 | tf_op jit(solution)/shard_map/ppermute | solution.py:60
  518.7 14.2 %collective-permute-start.48 = (bf16[128,1024]{1,0:T(8,128)(2,1)S(1)}, bf16[128,1024]{1,0:T(8,128)(2,1)S(1)}, u32[]{:S(2)}, u32[]{:S(2)}) collective-permute-start(bf16[128,1024]{1,0:T(8,128)(2,1)S(1)} %fusion.14), channel_id=1, source_target_pairs={{0,16},{4,20},{8,24},{12,28},{16,0},{20,4},{24,8},{28,12},{1,17},{... | collective-permute-start | bytes 786440 | tf_op jit(solution)/shard_map/ppermute | solution.py:60
  530.6 14.1 %collective-permute-start.39 = (bf16[2,128,768]{2,1,0:T(8,128)(2,1)S(1)}, bf16[2,128,768]{2,1,0:T(8,128)(2,1)S(1)}, u32[]{:S(2)}, u32[]{:S(2)}) collective-permute-start(bf16[2,128,768]{2,1,0:T(8,128)(2,1)S(1)} %fusion.13), channel_id=1, source_target_pairs={{0,8},{4,12},{8,0},{12,4},{16,24},{20,28},{24,16},{28,20},{1,9},{5... | collective-permute-start | bytes 1179656 | tf_op jit(solution)/shard_map/ppermute | solution.py:60
  532.6 12.4 %collective-permute-start.52 = (bf16[128,1024]{0,1:T(8,128)(2,1)S(1)}, bf16[128,1024]{0,1:T(8,128)(2,1)S(1)}, u32[]{:S(2)}, u32[]{:S(2)}) collective-permute-start(bf16[128,1024]{0,1:T(8,128)(2,1)S(1)} %fusion.15), channel_id=1, source_target_pairs={{0,16},{4,20},{8,24},{12,28},{16,0},{20,4},{24,8},{28,12},{1,17},{... | collective-permute-start | bytes 786440 | tf_op jit(solution)/shard_map/ppermute | solution.py:60
  544.8 9.0 %collective-permute-start.40 = (bf16[128,768]{1,0:T(8,128)(2,1)S(1)}, bf16[128,768]{1,0:T(8,128)(2,1)S(1)}, u32[]{:S(2)}, u32[]{:S(2)}) collective-permute-start(bf16[128,768]{1,0:T(8,128)(2,1)S(1)} %fusion.16), channel_id=1, source_target_pairs={{0,16},{4,20},{8,24},{12,28},{16,0},{20,4},{24,8},{28,12},{1,17},{... | collective-permute-start | bytes 589832 | tf_op jit(solution)/shard_map/ppermute | solution.py:60
  (131 other events, 760.2 us)

commit v2 on v1

--- a/solution.py
+++ b/solution.py
@@ -11,7 +11,7 @@
 NORM_EPS = 1e-12
 MASKED = -1000000000.0
 MIB = 1024 * 1024
-VMEM_LIMIT = 40 * MIB
+VMEM_LIMIT = 32 * MIB
 
 F32 = jnp.float32
 BF16 = jnp.bfloat16
@@ -28,26 +28,51 @@
     return lax.dot_general(one, two, (((1,), (1,)), ((), ())), preferred_element_type=F32)
 
 
-def dot_tn(one, two):
-    return lax.dot_general(one, two, (((0,), (0,)), ((), ())), preferred_element_type=F32)
-
-
 def shape(dims, kind):
     return jax.ShapeDtypeStruct(dims, kind)
 
 
-def whole_call(kernel, outs, args, flops, name, scratch=()):
+def after(kernel, count, deps):
+    def body(*refs):
+        kernel(*refs[:count], *refs[count + len(deps) :])
+
+    return body
+
+
+def whole_call(kernel, outs, args, flops, name, scratch=(), deps=()):
     moved = sum(math.prod(a.shape) * a.dtype.itemsize for a in (*args, *outs))
     return pl.pallas_call(
-        kernel,
+        after(kernel, len(args), deps),
         out_shape=tuple(outs),
-        in_specs=[pl.BlockSpec(memory_space=pltpu.VMEM)] * len(args),
+        in_specs=[pl.BlockSpec(memory_space=pltpu.VMEM)] * len(args)
+        + [pl.BlockSpec(memory_space=pl.ANY)] * len(deps),
         out_specs=tuple([pl.BlockSpec(memory_space=pltpu.VMEM)] * len(outs)),
         scratch_shapes=list(scratch),
         compiler_params=pltpu.CompilerParams(vmem_limit_bytes=VMEM_LIMIT),
         cost_estimate=pl.CostEstimate(flops=flops, bytes_accessed=moved, transcendentals=0),
         name=name,
-    )(*args)
+    )(*args, *deps)
+
+
+def streamed_call(kernel, grid, outs, out_specs, args, in_specs, flops, name, scratch, deps=()):
+    moved = sum(math.prod(a.shape) * a.dtype.itemsize for a in (*args, *outs))
+    return pl.pallas_call(
+        after(kernel, len(args), deps),
+        grid=grid,
+        out_shape=tuple(outs),
+        in_specs=list(in_specs) + [pl.BlockSpec(memory_space=pl.ANY)] * len(deps),
+        out_specs=tuple(out_specs),
+        scratch_shapes=list(scratch),
+        compiler_params=pltpu.CompilerParams(
+            vmem_limit_bytes=VMEM_LIMIT, dimension_semantics=("arbitrary",)
+        ),
+        cost_estimate=pl.CostEstimate(flops=flops, bytes_accessed=moved, transcendentals=0),
+        name=name,
+    )(*args, *deps)
+
+
+def const_spec(dims):
+    return pl.BlockSpec(dims, lambda i: (0,) * len(dims))
 
 
 def swap_tensor(array, bit):
@@ -60,37 +85,83 @@
     return lax.ppermute(array, "dp", [(i, i ^ bit) for i in range(size)])
 
 
-def gather_dp(rows):
+def pack(parts, name, deps=()):
+    def kernel(*refs):
+        at = 0
+        for ref in refs[:-1]:
+            refs[-1][:, at : at + ref.shape[1]] = ref[...]
+            at += ref.shape[1]
+
+    out = shape((parts[0].shape[0], sum(p.shape[1] for p in parts)), parts[0].dtype)
+    return whole_call(kernel, [out], parts, 0, name, deps=deps)[0]
+
+
+def gather_far(rows):
+    pieces = [(rows, [0])]
+    step = lax.axis_size("dp") // 2
+    while step > 1:
+        if len(pieces) > 2:
+            pieces = [merged(pieces)]
+        pieces += [(swap_dp(p, step), [o ^ step for o in offsets]) for p, offsets in pieces]
+        step //= 2
+    return pieces
+
+
+def merged(pieces):
+    return (
+        jnp.concatenate([p for p, _ in pieces], axis=0),
+        [o for _, offsets in pieces for o in offsets],
+    )
+
+
+def gather_near(pieces):
+    return [(swap_dp(p, 1), [o ^ 1 for o in offsets]) for p, offsets in pieces]
+
+
+def assemble(pieces, dp_place, name, deps=()):
+    rows = pieces[0][0].shape[0] // len(pieces[0][1])
+    width = pieces[0][0].shape[1]
     size = lax.axis_size("dp")
-    place = lax.axis_index("dp")
-    step = size // 2
-    level = 0
-    block = rows.shape
-    held = rows
-    while step >= 1:
-        other = swap_dp(held, step)
-        low = (place & step) == 0
-        held = jnp.where(
-            low, jnp.stack([held, other], axis=level), jnp.stack([other, held], axis=level)
-        )
-        level += 1
-        step //= 2
-    return held.reshape((size * block[0],) + block[1:])
-
-
-def scatter_dp(total):
-    size = lax.axis_size("dp")
-    place = lax.axis_index("dp")
-    levels = size.bit_length() - 1
-    rows = total.shape[0] // size
-    held = total.reshape((2,) * levels + (rows,) + total.shape[1:])
-    for level in range(levels):
-        axis = levels - 1 - level
-        bit = (place >> level) & 1
-        mine = lax.dynamic_index_in_dim(held, bit, axis, keepdims=False)
-        theirs = lax.dynamic_index_in_dim(held, 1 - bit, axis, keepdims=False)
-        held = mine.astype(F32) + swap_dp(theirs.astype(BF16), 1 << level).astype(F32)
-    return held
+
+    def kernel(*refs):
+        place = refs[0][0]
+        for ref, (_, offsets) in zip(refs[1:-1], pieces):
+            for i, offset in enumerate(offsets):
+                start = pl.multiple_of((place ^ offset) * rows, rows)
+                refs[-1][pl.ds(start, rows), :] = ref[i * rows : (i + 1) * rows, :]
+
+    arrays = [p for p, _ in pieces]
+    out = shape((size * rows, width), BF16)
+    moved = 2 * size * rows * width * 2
+    return pl.pallas_call(
+        after(kernel, 1 + len(arrays), deps),
+        out_shape=out,
+        in_specs=[pl.BlockSpec(memory_space=pltpu.SMEM)]
+        + [pl.BlockSpec(memory_space=pltpu.VMEM)] * len(arrays)
+        + [pl.BlockSpec(memory_space=pl.ANY)] * len(deps),
+        out_specs=pl.BlockSpec(memory_space=pltpu.VMEM),
+        compiler_params=pltpu.CompilerParams(vmem_limit_bytes=VMEM_LIMIT),
+        cost_estimate=pl.CostEstimate(flops=0, bytes_accessed=moved, transcendentals=0),
+        name=name,
+    )(dp_place, *arrays, *deps)
+
+
+def halving_order(size, bits):
+    order = [0]
+    for bit in reversed(bits):
+        order = order + [o ^ (1 << bit) for o in order]
+    return order
+
+
+def scatter_dp(kept, got, bits):
+    arrivals = [got]
+    total = kept + got.astype(F32)
+    for bit in bits:
+        half = total.shape[0] // 2
+        came = swap_dp(total[half:].astype(BF16), 1 << bit)
+        arrivals.append(came)
+        total = total[:half] + came.astype(F32)
+    return total, arrivals
 
 
 def sum_all(vector):
@@ -107,12 +178,12 @@
 
 def project_inputs(x_own, x_across, w_mine, w_other, b_mine, b_other):
     rows, width = x_own.shape
-    third = w_mine.shape[1] // 3
+    third = w_mine.shape[1] // 4
 
     def kernel(x0, x1, wm, wo, bm, bo, mine_ref, other_ref, send_ref):
         tokens = jnp.concatenate([x0[...], x1[...]], axis=0)
-        mine = (dot(tokens, wm[...]) + bm[...]).astype(BF16)
-        other = (dot(tokens, wo[...]) + bo[...]).astype(BF16)
+        mine = (dot(tokens, wm[:, : 3 * third]) + bm[...]).astype(BF16)
+        other = (dot(tokens, wo[:, : 3 * third]) + bo[...]).astype(BF16)
         mine_ref[...] = mine
         other_ref[...] = other
         send_ref[:, : 2 * third] = other[:, third:]
@@ -129,12 +200,12 @@
     )
 
 
-def attention_forward(mine, other, far, bias_row, wout_mine, wout_other, head_size):
+def attention_forward(mine, other, far, bias_row, w_mine, w_other, head_size, deps):
     rows = mine.shape[0]
     third = mine.shape[1] // 3
     heads = third // head_size
     block = rows // 2
-    width = wout_mine.shape[0]
+    width = w_mine.shape[0]
     scaling = 1.0 / math.sqrt(head_size)
 
     def kernel(mine_ref, other_ref, far_ref, bias_ref, wm, wo, cm_ref, co_ref, own_ref, across_ref, acc):
@@ -168,7 +239,7 @@
         ctx_other = acc[1].astype(BF16)
         cm_ref[...] = ctx_mine
         co_ref[...] = ctx_other
-        part_sum = dot_nt(ctx_mine, wm[...]) + dot_nt(ctx_other, wo[...])
+        part_sum = dot_nt(ctx_mine, wm[:, 3 * third :]) + dot_nt(ctx_other, wo[:, 3 * third :])
         own_ref[...] = part_sum[:block]
         across_ref[...] = part_sum[block:].astype(BF16)
 
@@ -182,14 +253,15 @@
     return whole_call(
         kernel,
         outs,
-        [mine, other, far, bias_row, wout_mine, wout_other],
+        [mine, other, far, bias_row, w_mine, w_other],
         flops,
         "attention_forward",
         [pltpu.VMEM((2, rows, third), F32)],
-    )
-
-
-def attention_backward(mine, other, far, bias_column, ga_own, ga_across, wout_mine, wout_other, head_size):
+        deps,
+    )
+
+
+def attention_backward(mine, other, far, bias_column, ga_own, ga_across, w_mine, w_other, head_size, deps):
     rows = mine.shape[0]
     third = mine.shape[1] // 3
     heads = third // head_size
@@ -203,8 +275,8 @@
     ):
         lane_head = lax.broadcasted_iota(jnp.int32, (1, third), 1) // head_size
         grad_rows = jnp.concatenate([g0[...], g1[...]], axis=0)
-        grad_ctx[0] = dot(grad_rows, wm[...]).astype(BF16)
-        grad_ctx[1] = dot(grad_rows, wo[...]).astype(BF16)
+        grad_ctx[0] = dot(grad_rows, wm[:, 3 * third :]).astype(BF16)
+        grad_ctx[1] = dot(grad_rows, wo[:, 3 * third :]).astype(BF16)
         dkv[...] = jnp.zeros_like(dkv)
         for group, ref in enumerate((mine_ref, other_ref)):
             base = 2 * third * group
@@ -259,7 +331,7 @@
     return whole_call(
         kernel,
         outs,
-        [mine, other, far, bias_column, ga_own, ga_across, wout_mine, wout_other],
+        [mine, other, far, bias_column, ga_own, ga_across, w_mine, w_other],
         flops,
         "attention_backward",
         [
@@ -268,10 +340,11 @@
             pltpu.VMEM((2, third, rows), F32),
             pltpu.VMEM((2, 2, keys_count, third), F32),
         ],
-    )
-
-
-def project_back(dq, keep, got, w_mine, w_other):
+        deps,
+    )
+
+
+def project_back(dq, keep, got, w_mine, w_other, deps):
     rows = dq.shape[0]
     third = dq.shape[1] // 2
     block = rows // 2
@@ -283,7 +356,7 @@
         grad_other = jnp.concatenate([dq_ref[:, third:], dkv[:, 2 * third :]], axis=1)
         gm_ref[...] = grad_mine
         go_ref[...] = grad_other
-        back = dot_nt(grad_mine, wm[...]) + dot_nt(grad_other, wo[...])
+        back = dot_nt(grad_mine, wm[:, : 3 * third]) + dot_nt(grad_other, wo[:, : 3 * third])
         own_ref[...] = back[:block]
         across_ref[...] = back[block:].astype(BF16)
         sums_ref[0:1, :] = jnp.sum(grad_mine.astype(F32), axis=0, keepdims=True)
@@ -297,7 +370,9 @@
         shape((2, 3 * third), F32),
     ]
     flops = 2 * rows * width * 6 * third
-    return whole_call(kernel, outs, [dq, keep, got, w_mine, w_other], flops, "project_back")
+    return whole_call(
+        kernel, outs, [dq, keep, got, w_mine, w_other], flops, "project_back", deps=deps
+    )
 
 
 def moments(summed):
@@ -379,31 +454,10 @@
     )
 
 
-def streamed_call(kernel, grid, outs, out_specs, args, in_specs, flops, name, scratch):
-    moved = sum(math.prod(a.shape) * a.dtype.itemsize for a in (*args, *outs))
-    return pl.pallas_call(
-        kernel,
-        grid=grid,
-        out_shape=tuple(outs),
-        in_specs=in_specs,
-        out_specs=tuple(out_specs),
-        scratch_shapes=list(scratch),
-        compiler_params=pltpu.CompilerParams(
-            vmem_limit_bytes=VMEM_LIMIT, dimension_semantics=("arbitrary",)
-        ),
-        cost_estimate=pl.CostEstimate(flops=flops, bytes_accessed=moved, transcendentals=0),
-        name=name,
-    )(*args)
-
-
-def const_spec(dims):
-    return pl.BlockSpec(dims, lambda i: (0,) * len(dims))
-
-
-def feed_forward(n_own, n_across, up_mine, up_other, down_mine, down_other, b_mine, b_other):
+def feed_forward(n_own, n_across, w_mine, w_other, b_mine, b_other):
     block, width = n_own.shape
     rows = 2 * block
-    hidden = up_mine.shape[1]
+    hidden = w_mine.shape[1] // 2
     tile = min(256, hidden)
     steps = hidden // tile
 
@@ -436,6 +490,7 @@
             across_ref[...] = acc[block:].astype(BF16)
 
     column = pl.BlockSpec((width, tile), lambda i: (0, i))
+    later = pl.BlockSpec((width, tile), lambda i: (0, steps + i))
     bias = pl.BlockSpec((1, tile), lambda i: (0, i))
     made = pl.BlockSpec((rows, tile), lambda i: (0, i))
     outs = [shape((rows, hidden), BF16)] * 4 + [shape((block, width), F32), shape((block, width), BF16)]
@@ -444,18 +499,18 @@
         (steps,),
         outs,
         [made] * 4 + [const_spec((block, width))] * 2,
-        [n_own, n_across, up_mine, up_other, down_mine, down_other, b_mine, b_other],
-        [const_spec((block, width))] * 2 + [column] * 4 + [bias] * 2,
+        [n_own, n_across, w_mine, w_other, w_mine, w_other, b_mine, b_other],
+        [const_spec((block, width))] * 2 + [column] * 2 + [later] * 2 + [bias] * 2,
         2 * 2 * rows * width * 2 * hidden,
         "feed_forward",
         [pltpu.VMEM((rows, width), BF16), pltpu.VMEM((rows, width), F32)],
     )
 
 
-def feed_forward_back(g_own, g_across, up_mine, up_other, down_mine, down_other, slope_mine, slope_other):
+def feed_forward_back(g_own, g_across, w_mine, w_other, slope_mine, slope_other):
     block, width = g_own.shape
     rows = 2 * block
-    hidden = up_mine.shape[1]
+    hidden = w_mine.shape[1] // 2
     tile = min(256, hidden)
     steps = hidden // tile
 
@@ -485,6 +540,7 @@
             across_ref[...] = acc[block:].astype(BF16)
 
     column = pl.BlockSpec((width, tile), lambda i: (0, i))
+    later = pl.BlockSpec((width, tile), lambda i: (0, steps + i))
     bias = pl.BlockSpec((1, tile), lambda i: (0, i))
     made = pl.BlockSpec((rows, tile), lambda i: (0, i))
     outs = (
@@ -497,19 +553,55 @@
         (steps,),
         outs,
         [made] * 2 + [const_spec((block, width))] * 2 + [bias] * 2,
-        [g_own, g_across, up_mine, up_other, down_mine, down_other, slope_mine, slope_other],
-        [const_spec((block, width))] * 2 + [column] * 4 + [made] * 2,
+        [g_own, g_across, w_mine, w_other, w_mine, w_other, slope_mine, slope_other],
+        [const_spec((block, width))] * 2 + [column] * 2 + [later] * 2 + [made] * 2,
         2 * 2 * rows * width * 2 * hidden,
         "feed_forward_back",
         [pltpu.VMEM((rows, width), BF16), pltpu.VMEM((rows, width), F32)],
     )
 
 
-def weight_grad(ones, mine, other):
-    kept = sum(dot_tn(a, b) for a, b in zip(ones, mine))
-    sent = sum(dot_tn(a, b) for a, b in zip(ones, other))
-    kept = kept + swap_tensor(sent.astype(BF16), CORE).astype(F32)
-    return scatter_dp(kept)
+def weight_grad(ones, mine, other, dp_place, bits, first, count, tile, name):
+    block, width = ones[0].shape
+    rows = 2 * block
+    tile = min(tile, count)
+    size = lax.axis_size("dp")
+    share = width // size
+    order = halving_order(size, bits)
+
+    def kernel(place_ref, a0, a1, a2, a3, m0, m1, o0, o1, mine_ref, other_ref, turned, full):
+        @pl.when(pl.program_id(0) == 0)
+        def _():
+            for i, ref in enumerate((a0, a1, a2, a3)):
+                turned[:, i * block : (i + 1) * block] = ref[...].T
+
+        place = place_ref[0]
+        for one, two, out_ref in ((m0, m1, mine_ref), (o0, o1, other_ref)):
+            full[...] = dot(turned[:, :rows], one[...]) + dot(turned[:, rows:], two[...])
+            for i, offset in enumerate(order):
+                start = pl.multiple_of((place ^ offset) * share, share)
+                out_ref[i * share : (i + 1) * share, :] = full[pl.ds(start, share), :].astype(
+                    out_ref.dtype
+                )
+
+    base = first // tile
+    column = pl.BlockSpec((rows, tile), lambda i: (0, base + i))
+    made = pl.BlockSpec((width, tile), lambda i: (0, i))
+    return streamed_call(
+        kernel,
+        (count // tile,),
+        [shape((width, count), F32), shape((width, count), BF16)],
+        [made] * 2,
+        [dp_place, *ones, *mine, *other],
+        [pl.BlockSpec(memory_space=pltpu.SMEM)] + [const_spec((block, width))] * 4 + [column] * 4,
+        2 * 2 * rows * width * 2 * count,
+        name,
+        [pltpu.VMEM((width, 2 * rows), BF16), pltpu.VMEM((width, tile), F32)],
+    )
+
+
+def reduced(made, bits):
+    return scatter_dp(made[0], swap_tensor(made[1], CORE), bits)
 
 
 def shards(
@@ -538,20 +630,28 @@
     place = lax.axis_index("tensor")
     head_dims = w_query.shape[1]
     head_size = width // HEADS
+    hidden = w_up.shape[1]
     seqs = range(seq_count)
     row = lambda vector: vector.reshape(1, -1)
 
     x_own = [inputs[s] for s in seqs]
     x_across = [swap_tensor(x_own[s], ACROSS) for s in seqs]
 
-    qkv_mine = gather_dp(jnp.concatenate([w_query, w_key, w_value], axis=1))
-    qkv_other = swap_tensor(qkv_mine, CORE)
-    out_mine = gather_dp(w_out.T)
-    out_other = swap_tensor(out_mine, CORE)
-    up_mine = gather_dp(w_up)
-    up_other = swap_tensor(up_mine, CORE)
-    down_mine = gather_dp(w_down.T)
-    down_other = swap_tensor(down_mine, CORE)
+    dp_place = lax.axis_index("dp").astype(jnp.int32).reshape(1)
+    pieces = gather_far(pack([w_query, w_key, w_value, w_out.T], "pack_attention"))
+    far_last = pieces[-1][0]
+    pieces += gather_near(pieces)
+    att_mine = assemble(pieces, dp_place, "assemble_attention")
+    att_other = swap_tensor(att_mine, CORE)
+    fed_pieces = [merged(gather_far(pack([w_up, w_down.T], "pack_feed", [far_last])))]
+    (held, offsets) = fed_pieces[0]
+    cut = held.shape[0] // 2
+    halves = [(held[:cut], offsets[: len(offsets) // 2]), (held[cut:], offsets[len(offsets) // 2 :])]
+    near = gather_near(halves)
+    ffw_mine = assemble([*halves, *near], dp_place, "assemble_feed")
+    ffw_other = assemble(
+        [(swap_tensor(p, CORE), o) for p, o in [*fed_pieces, *near]], dp_place, "assemble_feed_other"
+    )
 
     biases = jnp.concatenate([b_query, jnp.zeros_like(b_query), b_value, b_up])
     biases_other = swap_tensor(biases, CORE)
@@ -567,14 +667,14 @@
     masks = [jnp.where(positions < lengths[s], 0.0, MASKED).astype(F32) for s in seqs]
 
     projected = [
-        project_inputs(x_own[s], x_across[s], qkv_mine, qkv_other, qkv_bias_mine, qkv_bias_other)
+        project_inputs(x_own[s], x_across[s], att_mine, att_other, qkv_bias_mine, qkv_bias_other)
         for s in seqs
     ]
     far = [swap_tensor(projected[s][2], CORE) for s in seqs]
     attended = [
         attention_forward(
             projected[s][0], projected[s][1], far[s], masks[s].reshape(1, seq_len),
-            out_mine, out_other, head_size,
+            att_mine, att_other, head_size, [held] if s == 0 else [near[0][0]],
         )
         for s in seqs
     ]
@@ -586,8 +686,7 @@
     normed_across = [swap_tensor(one[s][2], ACROSS) for s in seqs]
     fed = [
         feed_forward(
-            one[s][2], normed_across[s], up_mine, up_other, down_mine, down_other,
-            up_bias_mine, up_bias_other,
+            one[s][2], normed_across[s], ffw_mine, ffw_other, up_bias_mine, up_bias_other,
         )
         for s in seqs
     ]
@@ -601,7 +700,7 @@
     grad_across = [swap_tensor(two[s][2], ACROSS) for s in seqs]
     fed_back = [
         feed_forward_back(
-            two[s][2], grad_across[s], up_mine, up_other, down_mine, down_other, fed[s][2], fed[s][3]
+            two[s][2], grad_across[s], ffw_mine, ffw_other, fed[s][2], fed[s][3]
         )
         for s in seqs
     ]
@@ -610,36 +709,6 @@
         first_norm_back(one[s][0], two[s][1], fed_back[s][2], back_got[s], gain_one) for s in seqs
     ]
     first_across = [swap_tensor(one_back[s][1], ACROSS) for s in seqs]
-
-    grad_rows = [jnp.concatenate([two[s][2], grad_across[s]]) for s in seqs]
-    down_grad = weight_grad(grad_rows, [fed[s][0] for s in seqs], [fed[s][1] for s in seqs])
-    normed_rows = [jnp.concatenate([one[s][2], normed_across[s]]) for s in seqs]
-    up_grad = weight_grad(normed_rows, [fed_back[s][0] for s in seqs], [fed_back[s][1] for s in seqs])
-
-    attended_back = [
-        attention_backward(
-            projected[s][0], projected[s][1], far[s], masks[s].reshape(seq_len, 1),
-            one_back[s][1], first_across[s], out_mine, out_other, head_size,
-        )
-        for s in seqs
-    ]
-    first_rows = [jnp.concatenate([one_back[s][1], first_across[s]]) for s in seqs]
-    out_grad = weight_grad(first_rows, [attended[s][0] for s in seqs], [attended[s][1] for s in seqs])
-
-    far_back = [swap_tensor(attended_back[s][2], CORE) for s in seqs]
-    back = [
-        project_back(attended_back[s][0], attended_back[s][1], far_back[s], qkv_mine, qkv_other)
-        for s in seqs
-    ]
-    input_got = [swap_tensor(back[s][3], ACROSS) for s in seqs]
-    input_grad = jnp.stack(
-        [
-            (one_back[s][0] + (back[s][2] + input_got[s].astype(F32))).astype(BF16)
-            for s in seqs
-        ]
-    )
-    token_rows = [jnp.concatenate([x_own[s], x_across[s]]) for s in seqs]
-    qkv_grad = weight_grad(token_rows, [back[s][0] for s in seqs], [back[s][1] for s in seqs])
 
     def placed_in(part_mine, part_other):
         size = part_mine.shape[0]
@@ -647,7 +716,38 @@
         empty = lax.dynamic_update_slice(empty, part_mine, (place * size,))
         return lax.dynamic_update_slice(empty, part_other, ((place ^ CORE) * size,))
 
-    hidden = up_mine.shape[1]
+    levels = range(lax.axis_size("dp").bit_length() - 1)
+    near_first = list(levels)
+    far_first = [1, 0, *levels[2:]] if len(near_first) > 1 else near_first
+
+    def pairs(own, across):
+        return [part for s in seqs for part in (own[s], across[s])]
+
+    down_grad, down_came = reduced(
+        weight_grad(
+            pairs([two[s][2] for s in seqs], grad_across),
+            [fed[s][0] for s in seqs], [fed[s][1] for s in seqs],
+            dp_place, near_first, 0, hidden, 256, "w_down_grad",
+        ),
+        near_first,
+    )
+    up_grad, up_came = reduced(
+        weight_grad(
+            pairs([one[s][2] for s in seqs], normed_across),
+            [fed_back[s][0] for s in seqs], [fed_back[s][1] for s in seqs],
+            dp_place, far_first, 0, hidden, 256, "w_up_grad",
+        ),
+        far_first,
+    )
+    out_grad, out_came = reduced(
+        weight_grad(
+            pairs([one_back[s][1] for s in seqs], first_across),
+            [attended[s][0] for s in seqs], [attended[s][1] for s in seqs],
+            dp_place, near_first, 0, head_dims, 256, "w_out_grad",
+        ),
+        near_first,
+    )
+
     early = sum_all(
         jnp.concatenate(
             [
@@ -660,6 +760,46 @@
             ]
         )
     )
+
+    attended_back = [
+        attention_backward(
+            projected[s][0], projected[s][1], far[s], masks[s].reshape(seq_len, 1),
+            one_back[s][1], first_across[s], att_mine, att_other, head_size,
+            [down_came[1], up_came[0]] if s == 0 else [down_came[2], up_came[1], out_came[0]],
+        )
+        for s in seqs
+    ]
+    far_back = [swap_tensor(attended_back[s][2], CORE) for s in seqs]
+    back = [
+        project_back(
+            attended_back[s][0], attended_back[s][1], far_back[s], att_mine, att_other,
+            [down_came[-1], up_came[2], out_came[1]] if s == 0 else [up_came[-1], out_came[2], early],
+        )
+        for s in seqs
+    ]
+    input_got = [swap_tensor(back[s][3], ACROSS) for s in seqs]
+    input_grad = jnp.stack(
+        [
+            (one_back[s][0] + (back[s][2] + input_got[s].astype(F32))).astype(BF16)
+            for s in seqs
+        ]
+    )
+    part_cols = 3 * head_dims // 2
+    qkv_grad = jnp.concatenate(
+        [
+            reduced(
+                weight_grad(
+                    pairs(x_own, x_across),
+                    [back[s][0] for s in seqs], [back[s][1] for s in seqs],
+                    dp_place, bits, i * part_cols, part_cols, part_cols, "w_qkv_grad",
+                ),
+                bits,
+            )[0]
+            for i, bits in enumerate((near_first, far_first))
+        ],
+        axis=1,
+    )
+
     sums = sum(back[s][4] for s in seqs)
     late = sum_all(
         jnp.concatenate(

time: 562 us -> 557 us (level)
  waiting for transfers between devices: 170 us -> 222 us
  matrix products: 40.9 us -> 0 us
  other arithmetic: 48.2 us -> 20.9 us
  Pallas kernels: 139 us -> 165 us
  local copies, waits for them, and re-layouts: 85.8 us -> 72.2 us
    ppermute x33 -> x34, waiting for transfers between devices: 35.2 us -> 101 us  [swap_tensor(): return lax.ppermute(array, 'tensor', [(i, i ^ bit) for i in range(size)])]
    dot_general x16 -> x0, matrix products: 40.9 us -> none  [dot_tn(): lax.dot_general(one, two, (((0,), (0,)), ((), ())), preferred_element_typ...]
    pallas_call x18 -> x28, Pallas kernels: 139 us -> 165 us  [the longest x16 94.1 us: whole_call(): pl.pallas_call(after(kernel, len(args), deps), out_shape=tuple(outs), in_...]
    select_n x20 -> x0, other arithmetic: 20 us -> none  [gather_dp(): jnp.where(low, jnp.stack([held, other], axis=level), jnp.stack([other, he...]
    ppermute x30 -> x33, waiting for transfers between devices: 135 us -> 121 us  [swap_dp(): return lax.ppermute(array, 'dp', [(i, i ^ bit) for i in range(size)])]
    select_n x4 -> x0, local copies, waits for them, and re-layouts: 10.4 us -> none  [gather_dp(): jnp.where(low, jnp.stack([held, other], axis=level), jnp.stack([other, he...]
    dynamic_slice x6 -> x0, local copies, waits for them, and re-layouts: 6.24 us -> none  [the longest x4 5 us: scatter_dp(): mine = lax.dynamic_index_in_dim(held, bit, axis, keepdims=False)]
    unnamed x279 -> x253, local copies, waits for them, and re-layouts: 56.1 us -> 61.6 us
  transfers between devices with their start and end apart: 63 -> 67, of which waited for: 25 -> 31; matrix products, arithmetic and copies ran while one was open for 23% -> 7% of each run, Pallas kernels for 25% -> 27%
where the time goes in v2:
time: 557 us; the launch traced here: 551 us
  waiting for transfers between devices  222 us (40%)
  Pallas kernels  165 us (30%)
  local copies, waits for them, and re-layouts  72.2 us (13%)
  starting transfers between devices  69.3 us (12%)
  other arithmetic  20.9 us (4%)
    ppermute x33, waiting for transfers between devices, swap_dp(): return lax.ppermute(array, 'dp', [(i, i ^ bit) for i in range(size)])  121 us
    ppermute x34, waiting for transfers between devices, swap_tensor(): return lax.ppermute(array, 'tensor', [(i, i ^ bit) for i in range(size)])  101 us
    pallas_call x16, Pallas kernels, whole_call(): pl.pallas_call(after(kernel, len(args), deps), out_shape=tuple(outs), in_...  94.1 us
    pallas_call x9, Pallas kernels, streamed_call(): pl.pallas_call(after(kernel, len(args), deps), grid=grid, out_shape=tuple...  67.6 us
    unnamed x253, local copies, waits for them, and re-layouts  61.6 us
    ppermute x33, starting transfers between devices, swap_dp(): return lax.ppermute(array, 'dp', [(i, i ^ bit) for i in range(size)])  45.8 us
    ppermute x34, starting transfers between devices, swap_tensor(): return lax.ppermute(array, 'tensor', [(i, i ^ bit) for i in range(size)])  23.5 us
  transfers between devices with their start and end apart: 67, of which 31 were waited for; matrix products, arithmetic and copies ran while one was open for 7% of the time, Pallas kernels for 27%

profile of v2, /device:TPU:0, one launch (start us, length us, event | category | flops | bytes accessed | tf_op | source)
XLA Modules:
  0.0 551.2 jit_solution(12974478904023339863)
XLA Ops:
  4.1 4.1 collective-permute-start.1
  9.8 10.5 %collective-permute-done.1.refs_2_ = bf16[128,1024]{1,0:T(8,128)(2,1)S(1)} collective-permute-done((bf16[128,1024]{1,0:T(8,128)(2,1)S(1)}, bf16[128,1024]{1,0:T(8,128)(2,1)S(1)}, u32[]{:S(2)}, u32[]{:S(2)}) %collective-permute-start.1) | collective-permute-done | bytes 262176 | tf_op jit(solution)/shard_map/ppermute | solution.py:85
  24.4 3.3 collective-permute-done.3.refs_4_.refs_2_
  30.8 10.5 %collective-permute-done.6.refs_7_ = bf16[128,1024]{1,0:T(8,128)(2,1)S(1)} collective-permute-done((bf16[128,1024]{1,0:T(8,128)(2,1)S(1)}, bf16[128,1024]{1,0:T(8,128)(2,1)S(1)}, u32[]{:S(2)}, u32[]{:S(2)}) %collective-permute-start.6) | collective-permute-done | bytes 262176 | tf_op jit(solution)/shard_map/ppermute | solution.py:85
  42.8 2.9 collective-permute-done.7.refs_8_
  51.6 3.4 collective-permute-start.11
  55.6 2.1 slice_bitcast_fusion.3
  59.2 19.5 %collective-permute-done.11 = bf16[128,2048]{1,0:T(8,128)(2,1)S(1)} collective-permute-done((bf16[128,2048]{1,0:T(8,128)(2,1)S(1)}, bf16[128,2048]{1,0:T(8,128)(2,1)S(1)}, u32[]{:S(2)}, u32[]{:S(2)}) %collective-permute-start.11) | collective-permute-done | bytes 524320 | tf_op jit(solution)/shard_map/ppermute | solution.py:85
  82.3 10.3 %collective-permute-done.13 = bf16[128,2048]{1,0:T(8,128)(2,1)S(1)} collective-permute-done((bf16[128,2048]{1,0:T(8,128)(2,1)S(1)}, bf16[128,2048]{1,0:T(8,128)(2,1)S(1)}, u32[]{:S(2)}, u32[]{:S(2)}) %collective-permute-start.13) | collective-permute-done | bytes 524320 | tf_op jit(solution)/shard_map/ppermute | solution.py:85
  95.0 4.5 project_inputs.2
  104.9 11.1 %collective-permute-done.22.refs_1_.refs_4_ = bf16[256,1024]{1,0:T(8,128)(2,1)} collective-permute-done((bf16[256,1024]{1,0:T(8,128)(2,1)}, bf16[256,1024]{1,0:T(8,128)(2,1)}, u32[]{:S(2)}, u32[]{:S(2)}) %collective-permute-start.22) | collective-permute-done | bytes 524320 | tf_op jit(solution)/shard_map/ppermute | solution.py:80
  116.0 3.7 project_inputs.3
  120.7 7.0 %collective-permute-done.17.refs_4_ = bf16[256,2048]{1,0:T(8,128)(2,1)} collective-permute-done((bf16[256,2048]{1,0:T(8,128)(2,1)}, bf16[256,2048]{1,0:T(8,128)(2,1)}, u32[]{:S(2)}, u32[]{:S(2)}) %collective-permute-start.17) | collective-permute-done | bytes 1048608 | tf_op jit(solution)/shard_map/ppermute | solution.py:85
  127.7 10.7 %attention_forward.2 = (bf16[512,256]{1,0:T(8,128)(2,1)S(1)}, bf16[512,256]{1,0:T(8,128)(2,1)S(1)}, f32[256,1024]{1,0:T(8,128)S(1)}, bf16[256,1024]{1,0:T(8,128)(2,1)S(1)}) custom-call(bf16[512,768]{1,0:T(8,128)(2,1)S(1)} %copy-done.96, bf16[512,768]{1,0:T(8,128)(2,1)S(1)} %copy-done.99, bf16[512,1024]{1,0:T(8,128)(2,1)} %collective-permute-done.10.refs_2_, ...), custom_call_target="tpu_custom_call" | custom-call | flops 8589934592 | bytes 8916992 | tf_op jit(solution)/shard_map/attention_forward/pallas_call | solution.py:44
  140.7 11.1 %attention_forward.3 = (bf16[512,256]{1,0:T(8,128)(2,1)S(1)}, bf16[512,256]{1,0:T(8,128)(2,1)S(1)}, f32[256,1024]{1,0:T(8,128)S(1)}, bf16[256,1024]{1,0:T(8,128)(2,1)S(1)}) custom-call(bf16[512,768]{1,0:T(8,128)(2,1)S(1)} %get-tuple-element.111.refs_0_, bf16[512,768]{1,0:T(8,128)(2,1)S(1)} %get-tuple-element.112.refs_1_, ...), custom_call_target="tpu_custom_call" | custom-call | flops 8589934592 | bytes 8916992 | tf_op jit(solution)/shard_map/attention_forward/pallas_call | solution.py:44
  155.6 11.7 %collective-permute-done.24.refs_2_ = bf16[256,1024]{1,0:T(8,128)(2,1)S(1)} collective-permute-done((bf16[256,1024]{1,0:T(8,128)(2,1)S(1)}, bf16[256,1024]{1,0:T(8,128)(2,1)S(1)}, u32[]{:S(2)}, u32[]{:S(2)}) %collective-permute-start.24) | collective-permute-done | bytes 524320 | tf_op jit(solution)/shard_map/ppermute | solution.py:80
  170.4 2.4 assemble_feed.1.refs_2_.refs_4_
  173.2 5.3 collective-permute-done.15.refs_1_.refs_2_
  178.5 10.3 %feed_forward.2 = (bf16[512,1024]{1,0:T(8,128)(2,1)S(1)}, bf16[512,1024]{1,0:T(8,128)(2,1)S(1)}, bf16[512,1024]{1,0:T(8,128)(2,1)S(1)}, bf16[512,1024]{1,0:T(8,1...) custom-call(bf16[256,1024]{1,0:T(8,128)(2,1)S(1)} %get-tuple-element.107.refs_0_.refs_1_, ...), custom_call_target="tpu_custom_call" | custom-call | flops 4294967296 | bytes 23601152 | tf_op jit(solution)/shard_map/feed_forward/pallas_call | solution.py:59
  190.2 10.7 %feed_forward.3 = (bf16[512,1024]{1,0:T(8,128)(2,1)S(1)}, bf16[512,1024]{1,0:T(8,128)(2,1)S(1)}, bf16[512,1024]{1,0:T(8,128)(2,1)S(1)}, bf16[512,1024]{1,0:T(8,1...) custom-call(bf16[256,1024]{1,0:T(8,128)(2,1)S(1)} %get-tuple-element.117.refs_0_.refs_3_, ...), custom_call_target="tpu_custom_call" | custom-call | flops 4294967296 | bytes 23601152 | tf_op jit(solution)/shard_map/feed_forward/pallas_call | solution.py:59
  208.0 9.8 %collective-permute-done.26.refs_2_ = bf16[256,1024]{1,0:T(8,128)(2,1)S(1)} collective-permute-done((bf16[256,1024]{1,0:T(8,128)(2,1)S(1)}, bf16[256,1024]{1,0:T(8,128)(2,1)S(1)}, u32[]{:S(2)}, u32[]{:S(2)}) %collective-permute-start.26) | collective-permute-done | bytes 524320 | tf_op jit(solution)/shard_map/ppermute | solution.py:80
  222.1 6.9 %collective-permute-done.27.refs_1_.refs_2_ = bf16[256,1024]{1,0:T(8,128)(2,1)S(1)} collective-permute-done((bf16[256,1024]{1,0:T(8,128)(2,1)S(1)}, bf16[256,1024]{1,0:T(8,128)(2,1)S(1)}, u32[]{:S(2)}, u32[]{:S(2)}) %collective-permute-start.27) | collective-permute-done | bytes 524320 | tf_op jit(solution)/shard_map/ppermute | solution.py:80
  229.0 8.6 %collective-permute-done.30.refs_4_.refs_1_ = bf16[256,1024]{1,0:T(8,128)(2,1)S(1)} collective-permute-done((bf16[256,1024]{1,0:T(8,128)(2,1)S(1)}, bf16[256,1024]{1,0:T(8,128)(2,1)S(1)}, u32[]{:S(2)}, u32[]{:S(2)}) %collective-permute-start.30) | collective-permute-done | bytes 524320 | tf_op jit(solution)/shard_map/ppermute | solution.py:80
  241.3 8.3 %w_down_grad.1 = (f32[1024,1024]{1,0:T(8,128)S(1)}, bf16[1024,1024]{1,0:T(8,128)(2,1)}) custom-call(s32[1]{0:T(128)} %bitcast.1.refs_0_, bf16[256,1024]{1,0:T(8,128)(2,1)S(1)} %get-tuple-element.123.refs_0_.refs_1_, bf16[256,1024]{1,0:T(8,128)(2,1)S(1)} %collective-permute-done.27.refs_1_.refs_2_, bf16[256,1024]{1,0:T(8,128)(2,1)S(1)} %get-tuple-element.130.refs_3_.refs_0_, ...), custom_call_target="tpu_custom_call" | custom-call | flops 4294967296 | bytes 12582916 | tf_op jit(solution)/shard_map/w_down_grad/pallas_call | solution.py:59
  249.6 2.0 copy-done
  252.6 10.0 %feed_forward_back.2 = (bf16[512,1024]{1,0:T(8,128)(2,1)S(1)}, bf16[512,1024]{1,0:T(8,128)(2,1)S(1)}, f32[256,1024]{1,0:T(8,128)S(1)}, bf16[256,1024]{1,0:T(8,12...) custom-call(bf16[256,1024]{1,0:T(8,128)(2,1)S(1)} %copy-done.40, ...), custom_call_target="tpu_custom_call" | custom-call | flops 4294967296 | bytes 23601152 | tf_op jit(solution)/shard_map/feed_forward_back/pallas_call | solution.py:59
  263.6 10.1 %feed_forward_back.3 = (bf16[512,1024]{1,0:T(8,128)(2,1)S(1)}, bf16[512,1024]{1,0:T(8,128)(2,1)S(1)}, f32[256,1024]{1,0:T(8,128)S(1)}, bf16[256,1024]{1,0:T(8,12...) custom-call(bf16[256,1024]{1,0:T(8,128)(2,1)S(1)} %get-tuple-element.130.refs_3_.refs_0_, ...), custom_call_target="tpu_custom_call" | custom-call | flops 4294967296 | bytes 23601152 | tf_op jit(solution)/shard_map/feed_forward_back/pallas_call | solution.py:59
  273.7 8.3 %w_up_grad.1 = (f32[1024,1024]{1,0:T(8,128)S(1)}, bf16[1024,1024]{1,0:T(8,128)(2,1)}) custom-call(s32[1]{0:T(128)} %bitcast.1.refs_0_, bf16[256,1024]{1,0:T(8,128)(2,1)S(1)} %copy-done.28, bf16[256,1024]{1,0:T(8,128)(2,1)S(1)} %copy-done.30, bf16[256,1024]{1,0:T(8,128)(2,1)S(1)} %copy-done.32, bf16[256,1024]{1,0:T(8,128)(2,1)S(1)} %copy-done.34, ...), custom_call_target="tpu_custom_call" | custom-call | flops 4294967296 | bytes 12582916 | tf_op jit(solution)/shard_map/w_up_grad/pallas_call | solution.py:59
  282.0 2.0 copy-done.1
  287.4 12.3 %collective-permute-done.28.refs_3_ = bf16[256,1024]{1,0:T(8,128)(2,1)} collective-permute-done((bf16[256,1024]{1,0:T(8,128)(2,1)}, bf16[256,1024]{1,0:T(8,128)(2,1)}, u32[]{:S(2)}, u32[]{:S(2)}) %collective-permute-start.28) | collective-permute-done | bytes 524320 | tf_op jit(solution)/shard_map/ppermute | solution.py:80
  303.3 2.0 first_norm_back.2
  306.4 3.5 collective-permute-done.39.refs_3_
  312.7 1.6 collective-permute-start.29
  316.4 23.0 %collective-permute-done.48 = f32[10240]{0:T(1024)S(1)} collective-permute-done((f32[10240]{0:T(1024)S(1)}, f32[10240]{0:T(1024)S(1)}, u32[]{:S(2)}, u32[]{:S(2)}) %collective-permute-start.48) | collective-permute-done | bytes 40992 | tf_op jit(solution)/shard_map/ppermute | solution.py:80
  340.8 2.5 collective-permute-done.49
  343.4 1.7 collective-permute-start.50
  347.4 2.5 collective-permute-start.51
  355.0 2.5 w_out_grad.1
  357.7 4.1 convert_add_fusion.1
  363.4 2.6 convert_add_fusion
  369.8 23.3 %collective-permute-done.42.refs_7_ = bf16[512,256]{1,0:T(8,128)(2,1)S(1)} collective-permute-done((bf16[512,256]{1,0:T(8,128)(2,1)S(1)}, bf16[512,256]{1,0:T(8,128)(2,1)S(1)}, u32[]{:S(2)}, u32[]{:S(2)}) %collective-permute-start.42) | collective-permute-done | bytes 262176 | tf_op jit(solution)/shard_map/ppermute | solution.py:85
  394.1 1.8 collective-permute-start.35
  398.1 24.4 %attention_backward.2 = (bf16[512,512]{1,0:T(8,128)(2,1)S(1)}, f32[512,1024]{1,0:T(8,128)S(1)}, bf16[512,1024]{1,0:T(8,128)(2,1)}) custom-call(bf16[512,768]{1,0:T(8,128)(2,1)S(1)} %copy-done.97, bf16[512,768]{1,0:T(8,128)(2,1)S(1)} %copy-done.100, bf16[512,1024]{1,0:T(8,128)(2,1)} %collective-permute-done.10.refs_2_, f32[1024,1]{1,0:T(8,128)S(1)} %bitcast.59, ...), custom_call_target="tpu_custom_call" | custom-call | flops 10737418240 | bytes 11538432 | tf_op jit(solution)/shard_map/attention_backward/pallas_call | solution.py:44
  424.8 23.8 %attention_backward.3 = (bf16[512,512]{1,0:T(8,128)(2,1)S(1)}, f32[512,1024]{1,0:T(8,128)S(1)}, bf16[512,1024]{1,0:T(8,128)(2,1)}) custom-call(bf16[512,768]{1,0:T(8,128)(2,1)S(1)} %copy-done.102, bf16[512,768]{1,0:T(8,128)(2,1)S(1)} %copy-done.104, bf16[512,1024]{1,0:T(8,128)(2,1)S(1)} %copy-done.69, f32[1024,1]{1,0:T(8,128)S(1)} %bitcast.58, ...), custom_call_target="tpu_custom_call" | custom-call | flops 10737418240 | bytes 11538432 | tf_op jit(solution)/shard_map/attention_backward/pallas_call | solution.py:44
  450.6 2.5 collective-permute-start.36
  454.4 1.8 slice.328
  456.6 10.2 %collective-permute-done.61 = bf16[128,256]{1,0:T(8,128)(2,1)S(1)} collective-permute-done((bf16[128,256]{1,0:T(8,128)(2,1)S(1)}, bf16[128,256]{1,0:T(8,128)(2,1)S(1)}, u32[]{:S(2)}, u32[]{:S(2)}) %collective-permute-start.61) | collective-permute-done | bytes 65568 | tf_op jit(solution)/shard_map/ppermute | solution.py:85
  467.4 1.7 copy.43
  469.1 3.4 collective-permute-done.36.refs_5_
  472.5 1.6 copy-done.6
  475.1 3.9 project_back.2
  481.8 4.8 project_back.3
  493.9 2.0 slice_add_fusion.7
  498.3 8.6 %collective-permute-done.63 = f32[2048]{0:T(1024)S(1)} collective-permute-done((f32[2048]{0:T(1024)S(1)}, f32[2048]{0:T(1024)S(1)}, u32[]{:S(2)}, u32[]{:S(2)}) %collective-permute-start.63) | collective-permute-done | bytes 8224 | tf_op jit(solution)/shard_map/ppermute | solution.py:80
  509.8 3.7 w_qkv_grad.3
  513.7 3.8 w_qkv_grad.2
  518.1 2.1 collective-permute-start.66
  523.8 1.7 collective-permute-start.58
  528.1 5.8 %collective-permute-done.58 = bf16[512,384]{1,0:T(8,128)(2,1)S(1)} collective-permute-done((bf16[512,384]{1,0:T(8,128)(2,1)S(1)}, bf16[512,384]{1,0:T(8,128)(2,1)S(1)}, u32[]{:S(2)}, u32[]{:S(2)}) %collective-permute-start.58) | collective-permute-done | bytes 393248 | tf_op jit(solution)/shard_map/ppermute | solution.py:85
  537.4 2.5 collective-permute-done.59
  539.9 2.3 collective-permute-start.60
  543.2 2.1 collective-permute-start.56
  545.3 2.5 collective-permute-done.60
  547.8 2.1 collective-permute-done.56
  (438 shorter events, 127.1 us)
Async XLA Ops:
  4.1 16.1 %collective-permute-start.1 = (bf16[128,1024]{1,0:T(8,128)(2,1)S(1)}, bf16[128,1024]{1,0:T(8,128)(2,1)S(1)}, u32[]{:S(2)}, u32[]{:S(2)}) collective-permute-start(bf16[128,1024]{1,0:T(8,128)(2,1)S(1)} %pack_attention.1.refs_1_), channel_id=1, source_target_pairs={{0,16},{4,20},{8,24},{12,28},{16,0},{20,4},{24,8},{28,12},{1,17},{... | collective-permute-start | bytes 786440 | tf_op jit(solution)/shard_map/ppermute | solution.py:85
  8.3 14.7 %collective-permute-start.2 = (bf16[128,1024]{1,0:T(8,128)(2,1)S(1)}, bf16[128,1024]{1,0:T(8,128)(2,1)S(1)}, u32[]{:S(2)}, u32[]{:S(2)}) collective-permute-start(bf16[128,1024]{1,0:T(8,128)(2,1)S(1)} %pack_attention.1.refs_1_), channel_id=1, source_target_pairs={{0,8},{4,12},{8,0},{12,4},{16,24},{20,28},{24,16},{28,20},{1,9},{5... | collective-permute-start | bytes 786440 | tf_op jit(solution)/shard_map/ppermute | solution.py:85
  20.3 7.4 %collective-permute-start.3 = (bf16[128,1024]{1,0:T(8,128)(2,1)S(1)}, bf16[128,1024]{1,0:T(8,128)(2,1)S(1)}, u32[]{:S(2)}, u32[]{:S(2)}) collective-permute-start(bf16[128,1024]{1,0:T(8,128)(2,1)S(1)} %collective-permute-done.1.refs_2_), channel_id=1, source_target_pairs={{0,8},{4,12},{8,0},{12,4},{16,24},{20,28},{24,16},{28,20},{1,9},{5... | collective-permute-start | bytes 786440 | tf_op jit(solution)/shard_map/ppermute | solution.py:85
  20.9 9.2 %collective-permute-start.4 = (bf16[128,1024]{1,0:T(8,128)(2,1)S(1)}, bf16[128,1024]{1,0:T(8,128)(2,1)S(1)}, u32[]{:S(2)}, u32[]{:S(2)}) collective-permute-start(bf16[128,1024]{1,0:T(8,128)(2,1)S(1)} %pack_attention.1.refs_1_), channel_id=1, source_target_pairs={{0,4},{4,0},{8,12},{12,8},{16,20},{20,16},{24,28},{28,24},{1,5},{5... | collective-permute-start | bytes 786440 | tf_op jit(solution)/shard_map/ppermute | solution.py:85
  22.4 19.7 %collective-permute-start.5 = (bf16[128,1024]{1,0:T(8,128)(2,1)S(1)}, bf16[128,1024]{1,0:T(8,128)(2,1)S(1)}, u32[]{:S(2)}, u32[]{:S(2)}) collective-permute-start(bf16[128,1024]{1,0:T(8,128)(2,1)S(1)} %collective-permute-done.1.refs_2_), channel_id=1, source_target_pairs={{0,4},{4,0},{8,12},{12,8},{16,20},{20,16},{24,28},{28,24},{1,5},{5... | collective-permute-start | bytes 786440 | tf_op jit(solution)/shard_map/ppermute | solution.py:85
  22.9 18.4 %collective-permute-start.6 = (bf16[128,1024]{1,0:T(8,128)(2,1)S(1)}, bf16[128,1024]{1,0:T(8,128)(2,1)S(1)}, u32[]{:S(2)}, u32[]{:S(2)}) collective-permute-start(bf16[128,1024]{1,0:T(8,128)(2,1)S(1)} %collective-permute-done.2.refs_3_), channel_id=1, source_target_pairs={{0,4},{4,0},{8,12},{12,8},{16,20},{20,16},{24,28},{28,24},{1,5},{5... | collective-permute-start | bytes 786440 | tf_op jit(solution)/shard_map/ppermute | solution.py:85
  27.7 18.0 %collective-permute-start.7 = (bf16[128,1024]{1,0:T(8,128)(2,1)S(1)}, bf16[128,1024]{1,0:T(8,128)(2,1)S(1)}, u32[]{:S(2)}, u32[]{:S(2)}) collective-permute-start(bf16[128,1024]{1,0:T(8,128)(2,1)S(1)} %collective-permute-done.3.refs_4_.refs_2_), channel_id=1, source_target_pairs={{0,4},{4,0},{8,12},{12,8},{16,20},{20,16},{24,28},{28,24},{1,5},{5... | collective-permute-start | bytes 786440 | tf_op jit(solution)/shard_map/ppermute | solution.py:85
  50.4 44.6 %collective-permute-start.8 = (bf16[1024,1024]{1,0:T(8,128)(2,1)S(1)}, bf16[1024,1024]{1,0:T(8,128)(2,1)}, u32[]{:S(2)}, u32[]{:S(2)}) collective-permute-start(bf16[1024,1024]{1,0:T(8,128)(2,1)S(1)} %assemble_attention.1.refs_2_.refs_4_.refs_6_.refs_3_), channel_id=1, source_target_pairs={{0,1},{1,0},{2,3},{3,2},{4,5},{5,4},{6,7},{7,6},{8,9},{9,8},{10,11... | collective-permute-start | bytes 6291464 | tf_op jit(solution)/shard_map/ppermute | solution.py:80
  51.6 27.1 %collective-permute-start.11 = (bf16[128,2048]{1,0:T(8,128)(2,1)S(1)}, bf16[128,2048]{1,0:T(8,128)(2,1)S(1)}, u32[]{:S(2)}, u32[]{:S(2)}) collective-permute-start(bf16[128,2048]{1,0:T(8,128)(2,1)S(1)} %pack_feed.1), channel_id=1, source_target_pairs={{0,16},{4,20},{8,24},{12,28},{16,0},{20,4},{24,8},{28,12},{1,17},{... | collective-permute-start | bytes 1572872 | tf_op jit(solution)/shard_map/ppermute | solution.py:85
  55.1 23.6 %collective-permute-start.9 = (f32[1792]{0:T(1024)S(1)}, f32[1792]{0:T(1024)S(1)}, u32[]{:S(2)}, u32[]{:S(2)}) collective-permute-start(f32[1792]{0:T(1024)S(1)} %pad_maximum_fusion.6), channel_id=1, source_target_pairs={{0,1},{1,0},{2,3},{3,2},{4,5},{5,4},{6,7},{7,6},{8,9},{9,8},{10,11... | collective-permute-start | bytes 21512 | tf_op jit(solution)/shard_map/ppermute | solution.py:80
  55.3 26.0 %collective-permute-start.12 = (bf16[128,2048]{1,0:T(8,128)(2,1)S(1)}, bf16[128,2048]{1,0:T(8,128)(2,1)S(1)}, u32[]{:S(2)}, u32[]{:S(2)}) collective-permute-start(bf16[128,2048]{1,0:T(8,128)(2,1)S(1)} %pack_feed.1), channel_id=1, source_target_pairs={{0,8},{4,12},{8,0},{12,4},{16,24},{20,28},{24,16},{28,20},{1,9},{5... | collective-permute-start | bytes 1572872 | tf_op jit(solution)/shard_map/ppermute | solution.py:85
  57.7 37.3 %collective-permute-start = (bf16[256,1024]{1,0:T(8,128)(2,1)S(1)}, bf16[256,1024]{1,0:T(8,128)(2,1)S(1)}, u32[]{:S(2)}, u32[]{:S(2)}) collective-permute-start(bf16[256,1024]{1,0:T(8,128)(2,1)S(1)} %get-tuple-element.221.refs_0_.refs_1_), channel_id=1, source_target_pairs={{0,2},{1,3},{2,0},{3,1},{4,6},{5,7},{6,4},{7,5},{8,10},{9,11},{10,... | collective-permute-start | bytes 1572872 | tf_op jit(solution)/shard_map/ppermute | solution.py:80
  78.7 13.9 %collective-permute-start.13 = (bf16[128,2048]{1,0:T(8,128)(2,1)S(1)}, bf16[128,2048]{1,0:T(8,128)(2,1)S(1)}, u32[]{:S(2)}, u32[]{:S(2)}) collective-permute-start(bf16[128,2048]{1,0:T(8,128)(2,1)S(1)} %collective-permute-done.11), channel_id=1, source_target_pairs={{0,8},{4,12},{8,0},{12,4},{16,24},{20,28},{24,16},{28,20},{1,9},{5... | collective-permute-start | bytes 1572872 | tf_op jit(solution)/shard_map/ppermute | solution.py:85
  79.8 40.8 %collective-permute-start.16 = (bf16[256,2048]{1,0:T(8,128)(2,1)}, bf16[256,2048]{1,0:T(8,128)(2,1)}, u32[]{:S(2)}, u32[]{:S(2)}) collective-permute-start(bf16[256,2048]{1,0:T(8,128)(2,1)} %pad_maximum_fusion.1.refs_1_), channel_id=1, source_target_pairs={{0,4},{4,0},{8,12},{12,8},{16,20},{20,16},{24,28},{28,24},{1,5},{5... | collective-permute-start | bytes 3145736 | tf_op jit(solution)/shard_map/ppermute | solution.py:85
  93.5 34.2 %collective-permute-start.17 = (bf16[256,2048]{1,0:T(8,128)(2,1)}, bf16[256,2048]{1,0:T(8,128)(2,1)}, u32[]{:S(2)}, u32[]{:S(2)}) collective-permute-start(bf16[256,2048]{1,0:T(8,128)(2,1)} %constant_dynamic-update-slice_fusion.refs_2_), channel_id=1, source_target_pairs={{0,4},{4,0},{8,12},{12,8},{16,20},{20,16},{24,28},{28,24},{1,5},{5... | collective-permute-start | bytes 3145736 | tf_op jit(solution)/shard_map/ppermute | solution.py:85
  101.3 26.4 %collective-permute-start.10 = (bf16[512,1024]{1,0:T(8,128)(2,1)}, bf16[512,1024]{1,0:T(8,128)(2,1)}, u32[]{:S(2)}, u32[]{:S(2)}) collective-permute-start(bf16[512,1024]{1,0:T(8,128)(2,1)} %get-tuple-element.103), channel_id=1, source_target_pairs={{0,1},{1,0},{2,3},{3,2},{4,5},{5,4},{6,7},{7,6},{8,9},{9,8},{10,11... | collective-permute-start | bytes 3145736 | tf_op jit(solution)/shard_map/ppermute | solution.py:80
  101.3 14.7 %collective-permute-start.22 = (bf16[256,1024]{1,0:T(8,128)(2,1)}, bf16[256,1024]{1,0:T(8,128)(2,1)}, u32[]{:S(2)}, u32[]{:S(2)}) collective-permute-start(bf16[256,1024]{1,0:T(8,128)(2,1)} %get-tuple-element.222.refs_0_.refs_3_), channel_id=1, source_target_pairs={{0,2},{1,3},{2,0},{3,1},{4,6},{5,7},{6,4},{7,5},{8,10},{9,11},{10,... | collective-permute-start | bytes 1572872 | tf_op jit(solution)/shard_map/ppermute | solution.py:80
  119.8 20.9 %collective-permute-start.23 = (bf16[512,1024]{1,0:T(8,128)(2,1)S(1)}, bf16[512,1024]{1,0:T(8,128)(2,1)S(1)}, u32[]{:S(2)}, u32[]{:S(2)}) collective-permute-start(bf16[512,1024]{1,0:T(8,128)(2,1)S(1)} %get-tuple-element.113), channel_id=1, source_target_pairs={{0,1},{1,0},{2,3},{3,2},{4,5},{5,4},{6,7},{7,6},{8,9},{9,8},{10,11... | collective-permute-start | bytes 3145736 | tf_op jit(solution)/shard_map/ppermute | solution.py:80
  120.1 52.8 %collective-permute-start.18 = (bf16[512,2048]{1,0:T(8,128)(2,1)S(1)}, bf16[512,2048]{1,0:T(8,128)(2,1)S(1)}, u32[]{:S(2)}, u32[]{:S(2)}) collective-permute-start(bf16[512,2048]{1,0:T(8,128)(2,1)S(1)} %pad_maximum_fusion.refs_6_), channel_id=1, source_target_pairs={{0,1},{1,0},{2,3},{3,2},{4,5},{5,4},{6,7},{7,6},{8,9},{9,8},{10,11... | collective-permute-start | bytes 6291464 | tf_op jit(solution)/shard_map/ppermute | solution.py:80
  120.6 52.2 %collective-permute-start.19 = (bf16[256,2048]{1,0:T(8,128)(2,1)}, bf16[256,2048]{1,0:T(8,128)(2,1)S(1)}, u32[]{:S(2)}, u32[]{:S(2)}) collective-permute-start(bf16[256,2048]{1,0:T(8,128)(2,1)} %collective-permute-done.16.refs_3_.refs_6_), channel_id=1, source_target_pairs={{0,1},{1,0},{2,3},{3,2},{4,5},{5,4},{6,7},{7,6},{8,9},{9,8},{10,11... | collective-permute-start | bytes 3145736 | tf_op jit(solution)/shard_map/ppermute | solution.py:80
  127.7 45.1 %collective-permute-start.20 = (bf16[256,2048]{1,0:T(8,128)(2,1)}, bf16[256,2048]{1,0:T(8,128)(2,1)S(1)}, u32[]{:S(2)}, u32[]{:S(2)}) collective-permute-start(bf16[256,2048]{1,0:T(8,128)(2,1)} %collective-permute-done.17.refs_4_), channel_id=1, source_target_pairs={{0,1},{1,0},{2,3},{3,2},{4,5},{5,4},{6,7},{7,6},{8,9},{9,8},{10,11... | collective-permute-start | bytes 3145736 | tf_op jit(solution)/shard_map/ppermute | solution.py:80
  139.1 14.3 %collective-permute-start.14 = (bf16[256,1024]{1,0:T(8,128)(2,1)S(1)}, bf16[256,1024]{1,0:T(8,128)(2,1)S(1)}, u32[]{:S(2)}, u32[]{:S(2)}) collective-permute-start(bf16[256,1024]{1,0:T(8,128)(2,1)S(1)} %get-tuple-element.105), channel_id=1, source_target_pairs={{0,2},{1,3},{2,0},{3,1},{4,6},{5,7},{6,4},{7,5},{8,10},{9,11},{10,... | collective-permute-start | bytes 1572872 | tf_op jit(solution)/shard_map/ppermute | solution.py:80
  152.5 14.8 %collective-permute-start.24 = (bf16[256,1024]{1,0:T(8,128)(2,1)S(1)}, bf16[256,1024]{1,0:T(8,128)(2,1)S(1)}, u32[]{:S(2)}, u32[]{:S(2)}) collective-permute-start(bf16[256,1024]{1,0:T(8,128)(2,1)S(1)} %get-tuple-element.115), channel_id=1, source_target_pairs={{0,2},{1,3},{2,0},{3,1},{4,6},{5,7},{6,4},{7,5},{8,10},{9,11},{10,... | collective-permute-start | bytes 1572872 | tf_op jit(solution)/shard_map/ppermute | solution.py:80
  154.0 24.5 %collective-permute-start.15 = (bf16[256,1024]{1,0:T(8,128)(2,1)S(1)}, bf16[256,1024]{1,0:T(8,128)(2,1)S(1)}, u32[]{:S(2)}, u32[]{:S(2)}) collective-permute-start(bf16[256,1024]{1,0:T(8,128)(2,1)S(1)} %get-tuple-element.107.refs_0_.refs_1_), channel_id=1, source_target_pairs={{0,2},{1,3},{2,0},{3,1},{4,6},{5,7},{6,4},{7,5},{8,10},{9,11},{10,... | collective-permute-start | bytes 1572872 | tf_op jit(solution)/shard_map/ppermute | solution.py:80
  169.9 20.4 %collective-permute-start.25 = (bf16[256,1024]{1,0:T(8,128)(2,1)S(1)}, bf16[256,1024]{1,0:T(8,128)(2,1)S(1)}, u32[]{:S(2)}, u32[]{:S(2)}) collective-permute-start(bf16[256,1024]{1,0:T(8,128)(2,1)S(1)} %get-tuple-element.117.refs_0_.refs_3_), channel_id=1, source_target_pairs={{0,2},{1,3},{2,0},{3,1},{4,6},{5,7},{6,4},{7,5},{8,10},{9,11},{10,... | collective-permute-start | bytes 1572872 | tf_op jit(solution)/shard_map/ppermute | solution.py:80
  189.7 14.8 %collective-permute-start.21 = (bf16[256,1024]{1,0:T(8,128)(2,1)S(1)}, bf16[256,1024]{1,0:T(8,128)(2,1)S(1)}, u32[]{:S(2)}, u32[]{:S(2)}) collective-permute-start(bf16[256,1024]{1,0:T(8,128)(2,1)S(1)} %get-tuple-element.109), channel_id=1, source_target_pairs={{0,2},{1,3},{2,0},{3,1},{4,6},{5,7},{6,4},{7,5},{8,10},{9,11},{10,... | collective-permute-start | bytes 1572872 | tf_op jit(solution)/shard_map/ppermute | solution.py:80
  202.9 14.9 %collective-permute-start.26 = (bf16[256,1024]{1,0:T(8,128)(2,1)S(1)}, bf16[256,1024]{1,0:T(8,128)(2,1)S(1)}, u32[]{:S(2)}, u32[]{:S(2)}) collective-permute-start(bf16[256,1024]{1,0:T(8,128)(2,1)S(1)} %get-tuple-element.119), channel_id=1, source_target_pairs={{0,2},{1,3},{2,0},{3,1},{4,6},{5,7},{6,4},{7,5},{8,10},{9,11},{10,... | collective-permute-start | bytes 1572872 | tf_op jit(solution)/shard_map/ppermute | solution.py:80
  207.4 21.6 %collective-permute-start.27 = (bf16[256,1024]{1,0:T(8,128)(2,1)S(1)}, bf16[256,1024]{1,0:T(8,128)(2,1)S(1)}, u32[]{:S(2)}, u32[]{:S(2)}) collective-permute-start(bf16[256,1024]{1,0:T(8,128)(2,1)S(1)} %get-tuple-element.123.refs_0_.refs_1_), channel_id=1, source_target_pairs={{0,2},{1,3},{2,0},{3,1},{4,6},{5,7},{6,4},{7,5},{8,10},{9,11},{10,... | collective-permute-start | bytes 1572872 | tf_op jit(solution)/shard_map/ppermute | solution.py:80
  220.6 17.0 %collective-permute-start.30 = (bf16[256,1024]{1,0:T(8,128)(2,1)S(1)}, bf16[256,1024]{1,0:T(8,128)(2,1)S(1)}, u32[]{:S(2)}, u32[]{:S(2)}) collective-permute-start(bf16[256,1024]{1,0:T(8,128)(2,1)S(1)} %get-tuple-element.130.refs_3_.refs_0_), channel_id=1, source_target_pairs={{0,2},{1,3},{2,0},{3,1},{4,6},{5,7},{6,4},{7,5},{8,10},{9,11},{10,... | collective-permute-start | bytes 1572872 | tf_op jit(solution)/shard_map/ppermute | solution.py:80
  251.5 106.1 %collective-permute-start.31 = (bf16[1024,1024]{1,0:T(8,128)(2,1)}, bf16[1024,1024]{1,0:T(8,128)(2,1)}, u32[]{:S(2)}, u32[]{:S(2)}) collective-permute-start(bf16[1024,1024]{1,0:T(8,128)(2,1)} %get-tuple-element.136), channel_id=1, source_target_pairs={{0,1},{1,0},{2,3},{3,2},{4,5},{5,4},{6,7},{7,6},{8,9},{9,8},{10,11... | collective-permute-start | bytes 6291464 | tf_op jit(solution)/shard_map/ppermute | solution.py:80
  284.0 79.4 %collective-permute-start.33 = (bf16[1024,1024]{1,0:T(8,128)(2,1)}, bf16[1024,1024]{1,0:T(8,128)(2,1)}, u32[]{:S(2)}, u32[]{:S(2)}) collective-permute-start(bf16[1024,1024]{1,0:T(8,128)(2,1)} %get-tuple-element.143), channel_id=1, source_target_pairs={{0,1},{1,0},{2,3},{3,2},{4,5},{5,4},{6,7},{7,6},{8,9},{9,8},{10,11... | collective-permute-start | bytes 6291464 | tf_op jit(solution)/shard_map/ppermute | solution.py:80
  284.6 15.1 %collective-permute-start.28 = (bf16[256,1024]{1,0:T(8,128)(2,1)}, bf16[256,1024]{1,0:T(8,128)(2,1)}, u32[]{:S(2)}, u32[]{:S(2)}) collective-permute-start(bf16[256,1024]{1,0:T(8,128)(2,1)} %get-tuple-element.127), channel_id=1, source_target_pairs={{0,2},{1,3},{2,0},{3,1},{4,6},{5,7},{6,4},{7,5},{8,10},{9,11},{10,... | collective-permute-start | bytes 1572872 | tf_op jit(solution)/shard_map/ppermute | solution.py:80
  286.1 23.8 %collective-permute-start.39 = (bf16[256,1024]{1,0:T(8,128)(2,1)}, bf16[256,1024]{1,0:T(8,128)(2,1)S(1)}, u32[]{:S(2)}, u32[]{:S(2)}) collective-permute-start(bf16[256,1024]{1,0:T(8,128)(2,1)} %get-tuple-element.151), channel_id=1, source_target_pairs={{0,2},{1,3},{2,0},{3,1},{4,6},{5,7},{6,4},{7,5},{8,10},{9,11},{10,... | collective-permute-start | bytes 1572872 | tf_op jit(solution)/shard_map/ppermute | solution.py:80
  312.7 37.2 %collective-permute-start.29 = (bf16[256,1024]{1,0:T(8,128)(2,1)}, bf16[256,1024]{1,0:T(8,128)(2,1)}, u32[]{:S(2)}, u32[]{:S(2)}) collective-permute-start(bf16[256,1024]{1,0:T(8,128)(2,1)} %copy-done.89), channel_id=1, source_target_pairs={{0,2},{1,3},{2,0},{3,1},{4,6},{5,7},{6,4},{7,5},{8,10},{9,11},{10,... | collective-permute-start | bytes 1572872 | tf_op jit(solution)/shard_map/ppermute | solution.py:80
  314.3 35.6 %collective-permute-start.40 = (bf16[256,1024]{1,0:T(8,128)(2,1)}, bf16[256,1024]{1,0:T(8,128)(2,1)S(1)}, u32[]{:S(2)}, u32[]{:S(2)}) collective-permute-start(bf16[256,1024]{1,0:T(8,128)(2,1)} %copy-done.86), channel_id=1, source_target_pairs={{0,2},{1,3},{2,0},{3,1},{4,6},{5,7},{6,4},{7,5},{8,10},{9,11},{10,... | collective-permute-start | bytes 1572872 | tf_op jit(solution)/shard_map/ppermute | solution.py:80
  314.8 24.6 %collective-permute-start.48 = (f32[10240]{0:T(1024)S(1)}, f32[10240]{0:T(1024)S(1)}, u32[]{:S(2)}, u32[]{:S(2)}) collective-permute-start(f32[10240]{0:T(1024)S(1)} %fusion.7), channel_id=1, source_target_pairs={{0,2},{1,3},{2,0},{3,1},{4,6},{5,7},{6,4},{7,5},{8,10},{9,11},{10,... | collective-permute-start | bytes 122888 | tf_op jit(solution)/shard_map/ppermute | solution.py:80
  343.4 4.0 collective-permute-start.50
  347.4 21.2 %collective-permute-start.51 = (f32[10240]{0:T(1024)S(1)}, f32[10240]{0:T(1024)S(1)}, u32[]{:S(2)}, u32[]{:S(2)}) collective-permute-start(f32[10240]{0:T(1024)S(1)} %add.191), channel_id=1, source_target_pairs={{0,16},{4,20},{8,24},{12,28},{16,0},{20,4},{24,8},{28,12},{1,17},{... | collective-permute-start | bytes 122888 | tf_op jit(solution)/shard_map/ppermute | solution.py:85
  357.6 9.1 %collective-permute-start.41 = (bf16[1024,256]{1,0:T(8,128)(2,1)S(1)}, bf16[1024,256]{1,0:T(8,128)(2,1)S(1)}, u32[]{:S(2)}, u32[]{:S(2)}) collective-permute-start(bf16[1024,256]{1,0:T(8,128)(2,1)S(1)} %get-tuple-element.158), channel_id=1, source_target_pairs={{0,1},{1,0},{2,3},{3,2},{4,5},{5,4},{6,7},{7,6},{8,9},{9,8},{10,11... | collective-permute-start | bytes 1572872 | tf_op jit(solution)/shard_map/ppermute | solution.py:80
  361.9 31.7 %collective-permute-start.32 = (bf16[512,1024]{1,0:T(8,128)(2,1)S(1)}, bf16[512,1024]{1,0:T(8,128)(2,1)S(1)}, u32[]{:S(2)}, u32[]{:S(2)}) collective-permute-start(bf16[512,1024]{1,0:T(8,128)(2,1)S(1)} %slice.323), channel_id=1, source_target_pairs={{0,4},{4,0},{8,12},{12,8},{16,20},{20,16},{24,28},{28,24},{1,5},{5... | collective-permute-start | bytes 3145736 | tf_op jit(solution)/shard_map/ppermute | solution.py:85
  366.3 29.7 %collective-permute-start.37 = (bf16[512,1024]{1,0:T(8,128)(2,1)S(1)}, bf16[512,1024]{1,0:T(8,128)(2,1)S(1)}, u32[]{:S(2)}, u32[]{:S(2)}) collective-permute-start(bf16[512,1024]{1,0:T(8,128)(2,1)S(1)} %slice.322), channel_id=1, source_target_pairs={{0,8},{4,12},{8,0},{12,4},{16,24},{20,28},{24,16},{28,20},{1,9},{5... | collective-permute-start | bytes 3145736 | tf_op jit(solution)/shard_map/ppermute | solution.py:85
  366.8 26.3 %collective-permute-start.42 = (bf16[512,256]{1,0:T(8,128)(2,1)S(1)}, bf16[512,256]{1,0:T(8,128)(2,1)S(1)}, u32[]{:S(2)}, u32[]{:S(2)}) collective-permute-start(bf16[512,256]{1,0:T(8,128)(2,1)S(1)} %slice.329), channel_id=1, source_target_pairs={{0,4},{4,0},{8,12},{12,8},{16,20},{20,16},{24,28},{28,24},{1,5},{5... | collective-permute-start | bytes 786440 | tf_op jit(solution)/shard_map/ppermute | solution.py:85
  393.2 55.9 %collective-permute-start.46 = (bf16[256,256]{1,0:T(8,128)(2,1)S(1)}, bf16[256,256]{1,0:T(8,128)(2,1)S(1)}, u32[]{:S(2)}, u32[]{:S(2)}) collective-permute-start(bf16[256,256]{1,0:T(8,128)(2,1)S(1)} %slice.333), channel_id=1, source_target_pairs={{0,8},{4,12},{8,0},{12,4},{16,24},{20,28},{24,16},{28,20},{1,9},{5... | collective-permute-start | bytes 393224 | tf_op jit(solution)/shard_map/ppermute | solution.py:85
  394.1 30.6 %collective-permute-start.35 = (bf16[256,1024]{1,0:T(8,128)(2,1)S(1)}, bf16[256,1024]{1,0:T(8,128)(2,1)S(1)}, u32[]{:S(2)}, u32[]{:S(2)}) collective-permute-start(bf16[256,1024]{1,0:T(8,128)(2,1)S(1)} %slice.325), channel_id=1, source_target_pairs={{0,8},{4,12},{8,0},{12,4},{16,24},{20,28},{24,16},{28,20},{1,9},{5... | collective-permute-start | bytes 1572872 | tf_op jit(solution)/shard_map/ppermute | solution.py:85
  396.5 56.6 %collective-permute-start.38 = (bf16[256,1024]{1,0:T(8,128)(2,1)S(1)}, bf16[256,1024]{1,0:T(8,128)(2,1)S(1)}, u32[]{:S(2)}, u32[]{:S(2)}) collective-permute-start(bf16[256,1024]{1,0:T(8,128)(2,1)S(1)} %slice.324), channel_id=1, source_target_pairs={{0,4},{4,0},{8,12},{12,8},{16,20},{20,16},{24,28},{28,24},{1,5},{5... | collective-permute-start | bytes 1572872 | tf_op jit(solution)/shard_map/ppermute | solution.py:85
  424.7 47.8 %collective-permute-start.34 = (bf16[512,1024]{1,0:T(8,128)(2,1)}, bf16[512,1024]{1,0:T(8,128)(2,1)}, u32[]{:S(2)}, u32[]{:S(2)}) collective-permute-start(bf16[512,1024]{1,0:T(8,128)(2,1)} %get-tuple-element.146), channel_id=1, source_target_pairs={{0,1},{1,0},{2,3},{3,2},{4,5},{5,4},{6,7},{7,6},{8,9},{9,8},{10,11... | collective-permute-start | bytes 3145736 | tf_op jit(solution)/shard_map/ppermute | solution.py:80
  448.6 33.1 %collective-permute-start.44 = (bf16[512,1024]{1,0:T(8,128)(2,1)}, bf16[512,1024]{1,0:T(8,128)(2,1)}, u32[]{:S(2)}, u32[]{:S(2)}) collective-permute-start(bf16[512,1024]{1,0:T(8,128)(2,1)} %get-tuple-element.164), channel_id=1, source_target_pairs={{0,1},{1,0},{2,3},{3,2},{4,5},{5,4},{6,7},{7,6},{8,9},{9,8},{10,11... | collective-permute-start | bytes 3145736 | tf_op jit(solution)/shard_map/ppermute | solution.py:80
  449.2 17.6 %collective-permute-start.61 = (bf16[128,256]{1,0:T(8,128)(2,1)S(1)}, bf16[128,256]{1,0:T(8,128)(2,1)S(1)}, u32[]{:S(2)}, u32[]{:S(2)}) collective-permute-start(bf16[128,256]{1,0:T(8,128)(2,1)S(1)} %slice.336), channel_id=1, source_target_pairs={{0,16},{4,20},{8,24},{12,28},{16,0},{20,4},{24,8},{28,12},{1,17},{... | collective-permute-start | bytes 196616 | tf_op jit(solution)/shard_map/ppermute | solution.py:85
  450.6 21.9 %collective-permute-start.36 = (bf16[128,1024]{1,0:T(8,128)(2,1)}, bf16[128,1024]{1,0:T(8,128)(2,1)}, u32[]{:S(2)}, u32[]{:S(2)}) collective-permute-start(bf16[128,1024]{1,0:T(8,128)(2,1)} %slice.330), channel_id=1, source_target_pairs={{0,16},{4,20},{8,24},{12,28},{16,0},{20,4},{24,8},{28,12},{1,17},{... | collective-permute-start | bytes 786440 | tf_op jit(solution)/shard_map/ppermute | solution.py:85
  456.2 25.5 %collective-permute-start.45 = (bf16[128,1024]{1,0:T(8,128)(2,1)}, bf16[128,1024]{1,0:T(8,128)(2,1)}, u32[]{:S(2)}, u32[]{:S(2)}) collective-permute-start(bf16[128,1024]{1,0:T(8,128)(2,1)} %slice.328), channel_id=1, source_target_pairs={{0,16},{4,20},{8,24},{12,28},{16,0},{20,4},{24,8},{28,12},{1,17},{... | collective-permute-start | bytes 786440 | tf_op jit(solution)/shard_map/ppermute | solution.py:85
  491.8 28.5 %collective-permute-start.43 = (bf16[256,1024]{1,0:T(8,128)(2,1)}, bf16[256,1024]{1,0:T(8,128)(2,1)}, u32[]{:S(2)}, u32[]{:S(2)}) collective-permute-start(bf16[256,1024]{1,0:T(8,128)(2,1)} %copy-done.94), channel_id=1, source_target_pairs={{0,2},{1,3},{2,0},{3,1},{4,6},{5,7},{6,4},{7,5},{8,10},{9,11},{10,... | collective-permute-start | bytes 1572872 | tf_op jit(solution)/shard_map/ppermute | solution.py:80
  493.4 13.6 %collective-permute-start.63 = (f32[2048]{0:T(1024)S(1)}, f32[2048]{0:T(1024)S(1)}, u32[]{:S(2)}, u32[]{:S(2)}) collective-permute-start(f32[2048]{0:T(1024)S(1)} %fusion.6), channel_id=1, source_target_pairs={{0,2},{1,3},{2,0},{3,1},{4,6},{5,7},{6,4},{7,5},{8,10},{9,11},{10,... | collective-permute-start | bytes 24584 | tf_op jit(solution)/shard_map/ppermute | solution.py:80
  496.8 26.4 %collective-permute-start.52 = (bf16[256,1024]{1,0:T(8,128)(2,1)}, bf16[256,1024]{1,0:T(8,128)(2,1)S(1)}, u32[]{:S(2)}, u32[]{:S(2)}) collective-permute-start(bf16[256,1024]{1,0:T(8,128)(2,1)} %get-tuple-element.174), channel_id=1, source_target_pairs={{0,2},{1,3},{2,0},{3,1},{4,6},{5,7},{6,4},{7,5},{8,10},{9,11},{10,... | collective-permute-start | bytes 1572872 | tf_op jit(solution)/shard_map/ppermute | solution.py:80
  507.0 6.6 %collective-permute-start.64 = (f32[2048]{0:T(1024)S(1)}, f32[2048]{0:T(1024)S(1)}, u32[]{:S(2)}, u32[]{:S(2)}) collective-permute-start(f32[2048]{0:T(1024)S(1)} %add.211), channel_id=1, source_target_pairs={{0,4},{4,0},{8,12},{12,8},{16,20},{20,16},{24,28},{28,24},{1,5},{5... | collective-permute-start | bytes 24584 | tf_op jit(solution)/shard_map/ppermute | solution.py:85
  513.5 10.1 %collective-permute-start.57 = (bf16[1024,384]{1,0:T(8,128)(2,1)S(1)}, bf16[1024,384]{1,0:T(8,128)(2,1)S(1)}, u32[]{:S(2)}, u32[]{:S(2)}) collective-permute-start(bf16[1024,384]{1,0:T(8,128)(2,1)S(1)} %get-tuple-element.182), channel_id=1, source_target_pairs={{0,1},{1,0},{2,3},{3,2},{4,5},{5,4},{6,7},{7,6},{8,9},{9,8},{10,11... | collective-permute-start | bytes 2359304 | tf_op jit(solution)/shard_map/ppermute | solution.py:80
  513.6 4.5 collective-permute-start.65
  517.5 7.9 %collective-permute-start.53 = (bf16[1024,384]{1,0:T(8,128)(2,1)S(1)}, bf16[1024,384]{1,0:T(8,128)(2,1)S(1)}, u32[]{:S(2)}, u32[]{:S(2)}) collective-permute-start(bf16[1024,384]{1,0:T(8,128)(2,1)S(1)} %get-tuple-element.180), channel_id=1, source_target_pairs={{0,1},{1,0},{2,3},{3,2},{4,5},{5,4},{6,7},{7,6},{8,9},{9,8},{10,11... | collective-permute-start | bytes 2359304 | tf_op jit(solution)/shard_map/ppermute | solution.py:80
  518.1 4.6 collective-permute-start.66
  523.8 10.1 %collective-permute-start.58 = (bf16[512,384]{1,0:T(8,128)(2,1)S(1)}, bf16[512,384]{1,0:T(8,128)(2,1)S(1)}, u32[]{:S(2)}, u32[]{:S(2)}) collective-permute-start(bf16[512,384]{1,0:T(8,128)(2,1)S(1)} %slice.326), channel_id=1, source_target_pairs={{0,8},{4,12},{8,0},{12,4},{16,24},{20,28},{24,16},{28,20},{1,9},{5... | collective-permute-start | bytes 1179656 | tf_op jit(solution)/shard_map/ppermute | solution.py:85
  525.6 10.7 %collective-permute-start.54 = (bf16[512,384]{1,0:T(8,128)(2,1)S(1)}, bf16[512,384]{1,0:T(8,128)(2,1)S(1)}, u32[]{:S(2)}, u32[]{:S(2)}) collective-permute-start(bf16[512,384]{1,0:T(8,128)(2,1)S(1)} %slice.327), channel_id=1, source_target_pairs={{0,4},{4,0},{8,12},{12,8},{16,20},{20,16},{24,28},{28,24},{1,5},{5... | collective-permute-start | bytes 1179656 | tf_op jit(solution)/shard_map/ppermute | solution.py:85
  534.0 5.8 %collective-permute-start.59 = (bf16[256,384]{1,0:T(8,128)(2,1)S(1)}, bf16[256,384]{1,0:T(8,128)(2,1)S(1)}, u32[]{:S(2)}, u32[]{:S(2)}) collective-permute-start(bf16[256,384]{1,0:T(8,128)(2,1)S(1)} %slice.331), channel_id=1, source_target_pairs={{0,4},{4,0},{8,12},{12,8},{16,20},{20,16},{24,28},{28,24},{1,5},{5... | collective-permute-start | bytes 589832 | tf_op jit(solution)/shard_map/ppermute | solution.py:85
  536.5 6.6 %collective-permute-start.55 = (bf16[256,384]{1,0:T(8,128)(2,1)S(1)}, bf16[256,384]{1,0:T(8,128)(2,1)S(1)}, u32[]{:S(2)}, u32[]{:S(2)}) collective-permute-start(bf16[256,384]{1,0:T(8,128)(2,1)S(1)} %slice.332), channel_id=1, source_target_pairs={{0,8},{4,12},{8,0},{12,4},{16,24},{20,28},{24,16},{28,20},{1,9},{5... | collective-permute-start | bytes 589832 | tf_op jit(solution)/shard_map/ppermute | solution.py:85
  539.9 7.9 %collective-permute-start.60 = (bf16[128,384]{1,0:T(8,128)(2,1)S(1)}, bf16[128,384]{1,0:T(8,128)(2,1)S(1)}, u32[]{:S(2)}, u32[]{:S(2)}) collective-permute-start(bf16[128,384]{1,0:T(8,128)(2,1)S(1)} %slice.334), channel_id=1, source_target_pairs={{0,16},{4,20},{8,24},{12,28},{16,0},{20,4},{24,8},{28,12},{1,17},{... | collective-permute-start | bytes 294920 | tf_op jit(solution)/shard_map/ppermute | solution.py:85
  543.2 6.7 %collective-permute-start.56 = (bf16[128,384]{1,0:T(8,128)(2,1)S(1)}, bf16[128,384]{1,0:T(8,128)(2,1)S(1)}, u32[]{:S(2)}, u32[]{:S(2)}) collective-permute-start(bf16[128,384]{1,0:T(8,128)(2,1)S(1)} %slice.335), channel_id=1, source_target_pairs={{0,16},{4,20},{8,24},{12,28},{16,0},{20,4},{24,8},{28,12},{1,17},{... | collective-permute-start | bytes 294920 | tf_op jit(solution)/shard_map/ppermute | solution.py:85
  (125 other events, 854.2 us)

commit v3 on v2

--- a/solution.py
+++ b/solution.py
@@ -11,7 +11,8 @@
 NORM_EPS = 1e-12
 MASKED = -1000000000.0
 MIB = 1024 * 1024
-VMEM_LIMIT = 32 * MIB
+VMEM_LIMIT = 56 * MIB
+UNDERSTATED = 1000
 
 F32 = jnp.float32
 BF16 = jnp.bfloat16
@@ -49,7 +50,9 @@
         out_specs=tuple([pl.BlockSpec(memory_space=pltpu.VMEM)] * len(outs)),
         scratch_shapes=list(scratch),
         compiler_params=pltpu.CompilerParams(vmem_limit_bytes=VMEM_LIMIT),
-        cost_estimate=pl.CostEstimate(flops=flops, bytes_accessed=moved, transcendentals=0),
+        cost_estimate=pl.CostEstimate(
+            flops=flops // UNDERSTATED, bytes_accessed=moved // UNDERSTATED, transcendentals=0
+        ),
         name=name,
     )(*args, *deps)
 
@@ -66,7 +69,9 @@
         compiler_params=pltpu.CompilerParams(
             vmem_limit_bytes=VMEM_LIMIT, dimension_semantics=("arbitrary",)
         ),
-        cost_estimate=pl.CostEstimate(flops=flops, bytes_accessed=moved, transcendentals=0),
+        cost_estimate=pl.CostEstimate(
+            flops=flops // UNDERSTATED, bytes_accessed=moved // UNDERSTATED, transcendentals=0
+        ),
         name=name,
     )(*args, *deps)
 
@@ -116,6 +121,10 @@
 
 def gather_near(pieces):
     return [(swap_dp(p, 1), [o ^ 1 for o in offsets]) for p, offsets in pieces]
+
+
+def other_core(pieces):
+    return [(swap_tensor(p, CORE), offsets) for p, offsets in pieces]
 
 
 def assemble(pieces, dp_place, name, deps=()):
@@ -141,7 +150,9 @@
         + [pl.BlockSpec(memory_space=pl.ANY)] * len(deps),
         out_specs=pl.BlockSpec(memory_space=pltpu.VMEM),
         compiler_params=pltpu.CompilerParams(vmem_limit_bytes=VMEM_LIMIT),
-        cost_estimate=pl.CostEstimate(flops=0, bytes_accessed=moved, transcendentals=0),
+        cost_estimate=pl.CostEstimate(
+            flops=0, bytes_accessed=moved // UNDERSTATED, transcendentals=0
+        ),
         name=name,
     )(dp_place, *arrays, *deps)
 
@@ -176,7 +187,7 @@
     return vector
 
 
-def project_inputs(x_own, x_across, w_mine, w_other, b_mine, b_other):
+def project_inputs(x_own, x_across, w_mine, w_other, b_mine, b_other, deps):
     rows, width = x_own.shape
     third = w_mine.shape[1] // 4
 
@@ -196,7 +207,12 @@
     ]
     flops = 2 * 2 * rows * width * 6 * third
     return whole_call(
-        kernel, outs, [x_own, x_across, w_mine, w_other, b_mine, b_other], flops, "project_inputs"
+        kernel,
+        outs,
+        [x_own, x_across, w_mine, w_other, b_mine, b_other],
+        flops,
+        "project_inputs",
+        deps=deps,
     )
 
 
@@ -271,7 +287,7 @@
 
     def kernel(
         mine_ref, other_ref, far_ref, bias_ref, g0, g1, wm, wo,
-        dq_ref, keep_ref, send_ref, grad_ctx, keys_t, dq_t, dkv,
+        dq_ref, keep_ref, send_ref, sums_ref, grad_ctx, keys_t, dq_t, dkv,
     ):
         lane_head = lax.broadcasted_iota(jnp.int32, (1, third), 1) // head_size
         grad_rows = jnp.concatenate([g0[...], g1[...]], axis=0)
@@ -315,7 +331,12 @@
 
         lax.fori_loop(0, heads, one_head, 0)
         for group in range(2):
-            dq_ref[:, group * third : (group + 1) * third] = (dq_t[group].T * scaling).astype(BF16)
+            grad_query = (dq_t[group].T * scaling).astype(BF16)
+            dq_ref[:, group * third : (group + 1) * third] = grad_query
+            sums_ref[group : group + 1, :third] = jnp.sum(
+                grad_query.astype(F32), axis=0, keepdims=True
+            )
+            sums_ref[group : group + 1, third:] = jnp.sum(dkv[group, 1], axis=0, keepdims=True)
             for kind in range(2):
                 at = (2 * group + kind) * third
                 keep_ref[:, at : at + third] = dkv[group, kind, :rows]
@@ -326,6 +347,7 @@
         shape((rows, 2 * third), BF16),
         shape((rows, 4 * third), F32),
         shape((rows, 4 * third), BF16),
+        shape((2, 2 * third), F32),
     ]
     flops = 5 * 2 * 2 * rows * keys_count * third * heads
     return whole_call(
@@ -350,24 +372,21 @@
     block = rows // 2
     width = w_mine.shape[0]
 
-    def kernel(dq_ref, keep_ref, got_ref, wm, wo, gm_ref, go_ref, own_ref, across_ref, sums_ref):
+    def kernel(dq_ref, keep_ref, got_ref, wm, wo, gm_ref, go_ref, own_ref, across_ref):
         dkv = (keep_ref[...] + got_ref[...].astype(F32)).astype(BF16)
         grad_mine = jnp.concatenate([dq_ref[:, :third], dkv[:, : 2 * third]], axis=1)
         grad_other = jnp.concatenate([dq_ref[:, third:], dkv[:, 2 * third :]], axis=1)
-        gm_ref[...] = grad_mine
-        go_ref[...] = grad_other
+        gm_ref[...] = dkv[:, : 2 * third]
+        go_ref[...] = dkv[:, 2 * third :]
         back = dot_nt(grad_mine, wm[:, : 3 * third]) + dot_nt(grad_other, wo[:, : 3 * third])
         own_ref[...] = back[:block]
         across_ref[...] = back[block:].astype(BF16)
-        sums_ref[0:1, :] = jnp.sum(grad_mine.astype(F32), axis=0, keepdims=True)
-        sums_ref[1:2, :] = jnp.sum(grad_other.astype(F32), axis=0, keepdims=True)
 
     outs = [
-        shape((rows, 3 * third), BF16),
-        shape((rows, 3 * third), BF16),
+        shape((rows, 2 * third), BF16),
+        shape((rows, 2 * third), BF16),
         shape((block, width), F32),
         shape((block, width), BF16),
-        shape((2, 3 * third), F32),
     ]
     flops = 2 * rows * width * 6 * third
     return whole_call(
@@ -430,7 +449,7 @@
     )
 
 
-def first_norm_back(summed, grad_second, part, got, gain):
+def first_norm_back(summed, grad_second, part, got, gain, deps):
     dims = summed.shape
 
     def kernel(z_ref, gs_ref, p_ref, r_ref, g_ref, grad_ref, low_ref, sums_ref):
@@ -450,7 +469,12 @@
 
     outs = [shape(dims, F32), shape(dims, BF16), shape((3, dims[1]), F32)]
     return whole_call(
-        kernel, outs, [summed, grad_second, part, got, gain], 40 * math.prod(dims), "first_norm_back"
+        kernel,
+        outs,
+        [summed, grad_second, part, got, gain],
+        40 * math.prod(dims),
+        "first_norm_back",
+        deps=deps,
     )
 
 
@@ -561,10 +585,10 @@
     )
 
 
-def weight_grad(ones, mine, other, dp_place, bits, first, count, tile, name):
+def weight_grad(ones, mine, other, dp_place, bits, count, name, other_first=0, deps=()):
     block, width = ones[0].shape
     rows = 2 * block
-    tile = min(tile, count)
+    tile = min(256, count)
     size = lax.axis_size("dp")
     share = width // size
     order = halving_order(size, bits)
@@ -584,8 +608,9 @@
                     out_ref.dtype
                 )
 
-    base = first // tile
-    column = pl.BlockSpec((rows, tile), lambda i: (0, base + i))
+    base = other_first // tile
+    column = pl.BlockSpec((rows, tile), lambda i: (0, i))
+    other_column = pl.BlockSpec((rows, tile), lambda i: (0, base + i))
     made = pl.BlockSpec((width, tile), lambda i: (0, i))
     return streamed_call(
         kernel,
@@ -593,10 +618,11 @@
         [shape((width, count), F32), shape((width, count), BF16)],
         [made] * 2,
         [dp_place, *ones, *mine, *other],
-        [pl.BlockSpec(memory_space=pltpu.SMEM)] + [const_spec((block, width))] * 4 + [column] * 4,
+        [pl.BlockSpec(memory_space=pltpu.SMEM)] + [const_spec((block, width))] * 4 + [column] * 2 + [other_column] * 2,
         2 * 2 * rows * width * 2 * count,
         name,
         [pltpu.VMEM((width, 2 * rows), BF16), pltpu.VMEM((width, tile), F32)],
+        deps,
     )
 
 
@@ -638,20 +664,20 @@
     x_across = [swap_tensor(x_own[s], ACROSS) for s in seqs]
 
     dp_place = lax.axis_index("dp").astype(jnp.int32).reshape(1)
-    pieces = gather_far(pack([w_query, w_key, w_value, w_out.T], "pack_attention"))
-    far_last = pieces[-1][0]
-    pieces += gather_near(pieces)
-    att_mine = assemble(pieces, dp_place, "assemble_attention")
-    att_other = swap_tensor(att_mine, CORE)
-    fed_pieces = [merged(gather_far(pack([w_up, w_down.T], "pack_feed", [far_last])))]
-    (held, offsets) = fed_pieces[0]
-    cut = held.shape[0] // 2
-    halves = [(held[:cut], offsets[: len(offsets) // 2]), (held[cut:], offsets[len(offsets) // 2 :])]
-    near = gather_near(halves)
-    ffw_mine = assemble([*halves, *near], dp_place, "assemble_feed")
-    ffw_other = assemble(
-        [(swap_tensor(p, CORE), o) for p, o in [*fed_pieces, *near]], dp_place, "assemble_feed_other"
-    )
+    att_far = gather_far(pack([w_query, w_key, w_value, w_out.T], "pack_attention"))
+    att_pieces = att_far + gather_near(att_far)
+    ffw_far = gather_far(pack([w_up, w_down.T], "pack_feed", [p for p, _ in att_far[1:2]]))
+    ffw_near = gather_near(ffw_far)
+    ffw_pieces = ffw_far + ffw_near
+    started = [p for p, _ in ffw_far[1:2]] + x_across
+    att_mine = assemble(att_pieces, dp_place, "assemble_attention", started)
+    att_other = assemble(
+        other_core(att_pieces), dp_place, "assemble_attention_other", [p for p, _ in ffw_far[2:3]]
+    )
+    ffw_mine = assemble(ffw_pieces, dp_place, "assemble_feed")
+    ffw_other = assemble(other_core(ffw_pieces), dp_place, "assemble_feed_other")
+    project_waits = [[], [p for p, _ in ffw_near[:1]]]
+    waits = [[p for p, _ in ffw_far[3:]], [p for p, _ in ffw_near[1:2]]]
 
     biases = jnp.concatenate([b_query, jnp.zeros_like(b_query), b_value, b_up])
     biases_other = swap_tensor(biases, CORE)
@@ -667,14 +693,17 @@
     masks = [jnp.where(positions < lengths[s], 0.0, MASKED).astype(F32) for s in seqs]
 
     projected = [
-        project_inputs(x_own[s], x_across[s], att_mine, att_other, qkv_bias_mine, qkv_bias_other)
+        project_inputs(
+            x_own[s], x_across[s], att_mine, att_other, qkv_bias_mine, qkv_bias_other,
+            project_waits[s] if s < 2 else [],
+        )
         for s in seqs
     ]
     far = [swap_tensor(projected[s][2], CORE) for s in seqs]
     attended = [
         attention_forward(
             projected[s][0], projected[s][1], far[s], masks[s].reshape(1, seq_len),
-            att_mine, att_other, head_size, [held] if s == 0 else [near[0][0]],
+            att_mine, att_other, head_size, waits[s] if s < 2 else [],
         )
         for s in seqs
     ]
@@ -705,11 +734,6 @@
         for s in seqs
     ]
     back_got = [swap_tensor(fed_back[s][3], ACROSS) for s in seqs]
-    one_back = [
-        first_norm_back(one[s][0], two[s][1], fed_back[s][2], back_got[s], gain_one) for s in seqs
-    ]
-    first_across = [swap_tensor(one_back[s][1], ACROSS) for s in seqs]
-
     def placed_in(part_mine, part_other):
         size = part_mine.shape[0]
         empty = jnp.zeros((tensor_size * size,), F32)
@@ -723,32 +747,77 @@
     def pairs(own, across):
         return [part for s in seqs for part in (own[s], across[s])]
 
-    down_grad, down_came = reduced(
-        weight_grad(
-            pairs([two[s][2] for s in seqs], grad_across),
-            [fed[s][0] for s in seqs], [fed[s][1] for s in seqs],
-            dp_place, near_first, 0, hidden, 256, "w_down_grad",
-        ),
-        near_first,
-    )
-    up_grad, up_came = reduced(
-        weight_grad(
-            pairs([one[s][2] for s in seqs], normed_across),
-            [fed_back[s][0] for s in seqs], [fed_back[s][1] for s in seqs],
-            dp_place, far_first, 0, hidden, 256, "w_up_grad",
-        ),
-        far_first,
-    )
+    def norm_back(s, deps):
+        return first_norm_back(
+            one[s][0], two[s][1], fed_back[s][2], back_got[s], gain_one, deps
+        )
+
+    down_made = weight_grad(
+        pairs([two[s][2] for s in seqs], grad_across),
+        [fed[s][0] for s in seqs], [fed[s][1] for s in seqs],
+        dp_place, near_first, hidden, "w_down_grad", deps=[fed_back[-1][2]],
+    )
+    one_back = [norm_back(s, [down_made[1]]) for s in seqs]
+    up_made = weight_grad(
+        pairs([one[s][2] for s in seqs], normed_across),
+        [fed_back[s][0] for s in seqs], [fed_back[s][1] for s in seqs],
+        dp_place, far_first, hidden, "w_up_grad", deps=[one_back[s][1] for s in seqs],
+    )
+    first_across = [swap_tensor(one_back[s][1], ACROSS) for s in seqs]
+    down_grad, down_came = reduced(down_made, near_first)
+    up_grad, up_came = reduced(up_made, far_first)
+
+    def backward(s, deps):
+        return attention_backward(
+            projected[s][0], projected[s][1], far[s], masks[s].reshape(seq_len, 1),
+            one_back[s][1], first_across[s], att_mine, att_other, head_size, deps,
+        )
+
+    attended_back = [backward(0, [down_came[0], up_made[1]])]
     out_grad, out_came = reduced(
         weight_grad(
             pairs([one_back[s][1] for s in seqs], first_across),
             [attended[s][0] for s in seqs], [attended[s][1] for s in seqs],
-            dp_place, near_first, 0, head_dims, 256, "w_out_grad",
+            dp_place, near_first, head_dims, "w_out_grad", deps=[attended_back[0][3]],
         ),
         near_first,
     )
 
-    early = sum_all(
+    attended_back += [backward(s, [down_came[1], up_came[1], out_came[0]]) for s in seqs[1:]]
+    far_back = [swap_tensor(attended_back[s][2], CORE) for s in seqs]
+    back = [
+        project_back(
+            attended_back[s][0], attended_back[s][1], far_back[s], att_mine, att_other,
+            [down_came[2], up_came[2], out_came[1]] if s == 0 else [out_came[2]],
+        )
+        for s in seqs
+    ]
+    input_got = [swap_tensor(back[s][3], ACROSS) for s in seqs]
+    input_grad = jnp.stack(
+        [
+            (one_back[s][0] + (back[s][2] + input_got[s].astype(F32))).astype(BF16)
+            for s in seqs
+        ]
+    )
+    tokens = pairs(x_own, x_across)
+    grad_queries = [attended_back[s][0] for s in seqs]
+    query_grad, _ = reduced(
+        weight_grad(
+            tokens, grad_queries, grad_queries, dp_place, far_first, head_dims, "w_query_grad",
+            head_dims, [far_back[0]],
+        ),
+        far_first,
+    )
+    both_grad, _ = reduced(
+        weight_grad(
+            tokens, [back[s][0] for s in seqs], [back[s][1] for s in seqs],
+            dp_place, near_first, 2 * head_dims, "w_key_value_grad",
+        ),
+        near_first,
+    )
+
+    sums = sum(attended_back[s][3] for s in seqs)
+    small = sum_all(
         jnp.concatenate(
             [
                 sum(two[s][3] for s in seqs).reshape(-1),
@@ -757,71 +826,24 @@
                     sum(fed_back[s][4] for s in seqs).reshape(-1),
                     sum(fed_back[s][5] for s in seqs).reshape(-1),
                 ),
+                placed_in(sums[0, :head_dims], sums[1, :head_dims]),
+                placed_in(sums[0, head_dims:], sums[1, head_dims:]),
             ]
         )
     )
-
-    attended_back = [
-        attention_backward(
-            projected[s][0], projected[s][1], far[s], masks[s].reshape(seq_len, 1),
-            one_back[s][1], first_across[s], att_mine, att_other, head_size,
-            [down_came[1], up_came[0]] if s == 0 else [down_came[2], up_came[1], out_came[0]],
-        )
-        for s in seqs
-    ]
-    far_back = [swap_tensor(attended_back[s][2], CORE) for s in seqs]
-    back = [
-        project_back(
-            attended_back[s][0], attended_back[s][1], far_back[s], att_mine, att_other,
-            [down_came[-1], up_came[2], out_came[1]] if s == 0 else [up_came[-1], out_came[2], early],
-        )
-        for s in seqs
-    ]
-    input_got = [swap_tensor(back[s][3], ACROSS) for s in seqs]
-    input_grad = jnp.stack(
-        [
-            (one_back[s][0] + (back[s][2] + input_got[s].astype(F32))).astype(BF16)
-            for s in seqs
-        ]
-    )
-    part_cols = 3 * head_dims // 2
-    qkv_grad = jnp.concatenate(
-        [
-            reduced(
-                weight_grad(
-                    pairs(x_own, x_across),
-                    [back[s][0] for s in seqs], [back[s][1] for s in seqs],
-                    dp_place, bits, i * part_cols, part_cols, part_cols, "w_qkv_grad",
-                ),
-                bits,
-            )[0]
-            for i, bits in enumerate((near_first, far_first))
-        ],
-        axis=1,
-    )
-
-    sums = sum(back[s][4] for s in seqs)
-    late = sum_all(
-        jnp.concatenate(
-            [
-                placed_in(sums[0, :head_dims], sums[1, :head_dims]),
-                placed_in(sums[0, 2 * head_dims :], sums[1, 2 * head_dims :]),
-            ]
-        )
-    )
-    vectors = [early[i * width : (i + 1) * width] for i in range(6)]
+    vectors = [small[i * width : (i + 1) * width] for i in range(6)]
     second_gain_grad, second_shift_grad, b_down_grad = vectors[:3]
     first_gain_grad, first_shift_grad, b_out_grad = vectors[3:]
-    b_up_grad = early[6 * width : 6 * width + tensor_size * hidden]
-    b_query_grad, b_value_grad = late[:width], late[width:]
+    b_up_grad = small[6 * width : 6 * width + tensor_size * hidden]
+    b_query_grad, b_value_grad = small[-2 * width : -width], small[-width:]
 
     output = jnp.stack([two[s][0] for s in seqs])
     return (
         output,
         input_grad,
-        qkv_grad[:, :head_dims],
-        qkv_grad[:, head_dims : 2 * head_dims],
-        qkv_grad[:, 2 * head_dims :],
+        query_grad,
+        both_grad[:, :head_dims],
+        both_grad[:, head_dims:],
         out_grad.T,
         up_grad,
         down_grad.T,

time: 557 us -> 487 us (0.87)
  waiting for transfers between devices: 222 us -> 130 us
  Pallas kernels: 165 us -> 226 us
  local copies, waits for them, and re-layouts: 72.2 us -> 41.6 us
  starting transfers between devices: 69.3 us -> 61.7 us
    ppermute x34 -> x44, waiting for transfers between devices: 101 us -> 31.9 us  [swap_tensor(): return lax.ppermute(array, 'tensor', [(i, i ^ bit) for i in range(size)])]
    unnamed x253 -> x176, local copies, waits for them, and re-layouts: 61.6 us -> 27.1 us
    pallas_call x16, Pallas kernels: 94.1 us -> 128 us  [whole_call(): pl.pallas_call(after(kernel, len(args), deps), out_shape=tuple(outs), in_...]
    ppermute x33 -> x32, waiting for transfers between devices: 121 us -> 98.3 us  [swap_dp(): return lax.ppermute(array, 'dp', [(i, i ^ bit) for i in range(size)])]
    pallas_call x9, Pallas kernels: 67.6 us -> 83.4 us  [streamed_call(): pl.pallas_call(after(kernel, len(args), deps), grid=grid, out_shape=tuple...]
    pallas_call x3 -> x4, Pallas kernels: 2.86 us -> 14.9 us  [assemble(): pl.pallas_call(after(kernel, 1 + len(arrays), deps), out_shape=out, in_sp...]
    ppermute x33 -> x32, starting transfers between devices: 45.8 us -> 40.9 us  [swap_dp(): return lax.ppermute(array, 'dp', [(i, i ^ bit) for i in range(size)])]
    ppermute x34 -> x44, starting transfers between devices: 23.5 us -> 20.8 us  [swap_tensor(): return lax.ppermute(array, 'tensor', [(i, i ^ bit) for i in range(size)])]
  transfers between devices with their start and end apart: 67 -> 76, of which waited for: 31 -> 23; matrix products, arithmetic and copies ran while one was open for 7% -> 8% of each run, Pallas kernels for 27% -> 45%
where the time goes in v3:
time: 487 us; the launch traced here: 482 us
  Pallas kernels  226 us (46%)
  waiting for transfers between devices  130 us (27%)
  starting transfers between devices  61.7 us (13%)
  local copies, waits for them, and re-layouts  41.6 us (9%)
  other arithmetic  20.2 us (4%)
    pallas_call x16, Pallas kernels, whole_call(): pl.pallas_call(after(kernel, len(args), deps), out_shape=tuple(outs), in_...  128 us
    ppermute x32, waiting for transfers between devices, swap_dp(): return lax.ppermute(array, 'dp', [(i, i ^ bit) for i in range(size)])  98.3 us
    pallas_call x9, Pallas kernels, streamed_call(): pl.pallas_call(after(kernel, len(args), deps), grid=grid, out_shape=tuple...  83.4 us
    ppermute x32, starting transfers between devices, swap_dp(): return lax.ppermute(array, 'dp', [(i, i ^ bit) for i in range(size)])  40.9 us
    ppermute x44, waiting for transfers between devices, swap_tensor(): return lax.ppermute(array, 'tensor', [(i, i ^ bit) for i in range(size)])  31.9 us
    unnamed x176, local copies, waits for them, and re-layouts  27.1 us
    ppermute x44, starting transfers between devices, swap_tensor(): return lax.ppermute(array, 'tensor', [(i, i ^ bit) for i in range(size)])  20.8 us
    pallas_call x4, Pallas kernels, assemble(): pl.pallas_call(after(kernel, 1 + len(arrays), deps), out_shape=out, in_sp...  14.9 us
  transfers between devices with their start and end apart: 76, of which 23 were waited for; matrix products, arithmetic and copies ran while one was open for 8% of the time, Pallas kernels for 45%

profile of v3, /device:TPU:0, one launch (start us, length us, event | category | flops | bytes accessed | tf_op | source)
XLA Modules:
  0.0 481.8 jit_solution(17431793888920616145)
XLA Ops:
  0.7 1.6 copy.39
  2.2 1.7 pack_attention.1.refs_1_
  3.9 4.1 collective-permute-start.1
  8.0 1.6 collective-permute-start.2
  13.1 1.6 collective-permute-start
  15.2 5.1 %collective-permute-done.1.refs_2_ = bf16[128,1024]{1,0:T(8,128)(2,1)S(1)} collective-permute-done((bf16[128,1024]{1,0:T(8,128)(2,1)}, bf16[128,1024]{1,0:T(8,128)(2,1)S(1)}, u32[]{:S(2)}, u32[]{:S(2)}) %collective-permute-start.1) | collective-permute-done | bytes 262176 | tf_op jit(solution)/shard_map/ppermute | solution.py:90
  23.5 1.8 copy.40
  25.3 1.9 pack_feed.1.refs_1_
  29.0 2.2 collective-permute-start.8
  31.3 1.8 collective-permute-start.18
  33.1 5.6 %collective-permute-done.9.refs_11_.refs_1_.refs_4_ = bf16[256,1024]{1,0:T(8,128)(2,1)S(1)} collective-permute-done((bf16[256,1024]{1,0:T(8,128)(2,1)S(1)}, bf16[256,1024]{1,0:T(8,128)(2,1)S(1)}, u32[]{:S(2)}, u32[]{:S(2)}) %collective-permute-start.9) | collective-permute-done | bytes 524320 | tf_op jit(solution)/shard_map/ppermute | solution.py:85
  41.3 13.5 %collective-permute-done.8.refs_9_.refs_2_ = bf16[128,2048]{1,0:T(8,128)(2,1)S(1)} collective-permute-done((bf16[128,2048]{1,0:T(8,128)(2,1)}, bf16[128,2048]{1,0:T(8,128)(2,1)S(1)}, u32[]{:S(2)}, u32[]{:S(2)}) %collective-permute-start.8) | collective-permute-done | bytes 524320 | tf_op jit(solution)/shard_map/ppermute | solution.py:90
  57.3 3.0 assemble_attention.1.refs_2_.refs_4_.refs_6_.refs_3_
  60.4 3.0 assemble_attention_other.1.refs_3_.refs_5_.refs_7_.refs_4_
  63.4 5.6 %project_inputs.3 = (bf16[512,768]{1,0:T(8,128)(2,1)}, bf16[512,768]{1,0:T(8,128)(2,1)}, bf16[512,1024]{1,0:T(8,128)(2,1)}) custom-call(bf16[256,1024]{1,0:T(8,128)(2,1)} %copy-done, bf16[256,1024]{1,0:T(8,128)(2,1)} %copy-done.7, bf16[1024,1024]{1,0:T(8,128)(2,1)} %assemble_attention.1.refs_2_.refs_4_.refs_6_.refs_3_, ...), custom_call_target="tpu_custom_call" | custom-call | flops 1610612 | bytes 7870 | tf_op jit(solution)/shard_map/project_inputs/pallas_call | solution.py:45
  69.4 5.6 %project_inputs.2 = (bf16[512,768]{1,0:T(8,128)(2,1)}, bf16[512,768]{1,0:T(8,128)(2,1)}, bf16[512,1024]{1,0:T(8,128)(2,1)}) custom-call(bf16[256,1024]{1,0:T(8,128)(2,1)} %copy-done.1, bf16[256,1024]{1,0:T(8,128)(2,1)} %copy-done.8, bf16[1024,1024]{1,0:T(8,128)(2,1)} %assemble_attention.1.refs_2_.refs_4_.refs_6_.refs_3_, ...), custom_call_target="tpu_custom_call" | custom-call | flops 1610612 | bytes 7870 | tf_op jit(solution)/shard_map/project_inputs/pallas_call | solution.py:45
  79.9 9.6 %collective-permute-done.25.refs_6_ = bf16[128,2048]{1,0:T(8,128)(2,1)} collective-permute-done((bf16[128,2048]{1,0:T(8,128)(2,1)S(1)}, bf16[128,2048]{1,0:T(8,128)(2,1)}, u32[]{:S(2)}, u32[]{:S(2)}) %collective-permute-start.25) | collective-permute-done | bytes 524320 | tf_op jit(solution)/shard_map/ppermute | solution.py:90
  91.9 12.9 %attention_forward.3 = (bf16[512,256]{1,0:T(8,128)(2,1)}, bf16[512,256]{1,0:T(8,128)(2,1)}, f32[256,1024]{1,0:T(8,128)}, bf16[256,1024]{1,0:T(8,128)(2,1)}) custom-call(bf16[512,768]{1,0:T(8,128)(2,1)} %get-tuple-element.111.refs_0_, bf16[512,768]{1,0:T(8,128)(2,1)} %get-tuple-element.112.refs_1_, bf16[512,1024]{1,0:T(8,128)(2,1)} %copy-done.16, ...), custom_call_target="tpu_custom_call" | custom-call | flops 8589934 | bytes 8916 | tf_op jit(solution)/shard_map/attention_forward/pallas_call | solution.py:45
  108.0 12.7 %attention_forward.2 = (bf16[512,256]{1,0:T(8,128)(2,1)}, bf16[512,256]{1,0:T(8,128)(2,1)}, f32[256,1024]{1,0:T(8,128)}, bf16[256,1024]{1,0:T(8,128)(2,1)}) custom-call(bf16[512,768]{1,0:T(8,128)(2,1)} %get-tuple-element.101.refs_0_, bf16[512,768]{1,0:T(8,128)(2,1)} %get-tuple-element.102.refs_1_, bf16[512,1024]{1,0:T(8,128)(2,1)} %copy-done.13, ...), custom_call_target="tpu_custom_call" | custom-call | flops 8589934 | bytes 8916 | tf_op jit(solution)/shard_map/attention_forward/pallas_call | solution.py:45
  122.8 3.3 first_norm.3
  126.6 8.8 %collective-permute-done.27.refs_8_ = bf16[128,2048]{1,0:T(8,128)(2,1)S(1)} collective-permute-done((bf16[128,2048]{1,0:T(8,128)(2,1)}, bf16[128,2048]{1,0:T(8,128)(2,1)S(1)}, u32[]{:S(2)}, u32[]{:S(2)}) %collective-permute-start.27) | collective-permute-done | bytes 524320 | tf_op jit(solution)/shard_map/ppermute | solution.py:90
  136.5 3.2 first_norm.2
  141.6 4.5 assemble_feed.1.refs_2_.refs_4_
  147.8 4.5 assemble_feed_other.1.refs_3_.refs_5_
  153.1 12.4 %feed_forward.3 = (bf16[512,1024]{1,0:T(8,128)(2,1)}, bf16[512,1024]{1,0:T(8,128)(2,1)}, bf16[512,1024]{1,0:T(8,128)(2,1)}, bf16[512,1024]{1,0:T(8,128)(2,1)}, f...) custom-call(bf16[256,1024]{1,0:T(8,128)(2,1)} %get-tuple-element.117.refs_0_.refs_3_, bf16[256,1024]{1,0:T(8,128)(2,1)} %copy-done.25, ...), custom_call_target="tpu_custom_call" | custom-call | flops 4294967 | bytes 23601 | tf_op jit(solution)/shard_map/feed_forward/pallas_call | solution.py:62
  167.3 12.8 %feed_forward.2 = (bf16[512,1024]{1,0:T(8,128)(2,1)}, bf16[512,1024]{1,0:T(8,128)(2,1)}, bf16[512,1024]{1,0:T(8,128)(2,1)}, bf16[512,1024]{1,0:T(8,128)(2,1)}, f...) custom-call(bf16[256,1024]{1,0:T(8,128)(2,1)} %get-tuple-element.107.refs_0_.refs_1_, bf16[256,1024]{1,0:T(8,128)(2,1)} %copy-done.26, ...), custom_call_target="tpu_custom_call" | custom-call | flops 4294967 | bytes 23601 | tf_op jit(solution)/shard_map/feed_forward/pallas_call | solution.py:62
  183.2 4.0 second_norm.3
  188.0 7.2 %collective-permute-done.36.refs_2_ = bf16[256,1024]{1,0:T(8,128)(2,1)S(1)} collective-permute-done((bf16[256,1024]{1,0:T(8,128)(2,1)}, bf16[256,1024]{1,0:T(8,128)(2,1)S(1)}, u32[]{:S(2)}, u32[]{:S(2)}) %collective-permute-start.36) | collective-permute-done | bytes 524320 | tf_op jit(solution)/shard_map/ppermute | solution.py:85
  196.0 4.0 second_norm.2
  201.3 5.2 %collective-permute-done.43.refs_1_.refs_4_ = bf16[256,1024]{1,0:T(8,128)(2,1)S(1)} collective-permute-done((bf16[256,1024]{1,0:T(8,128)(2,1)}, bf16[256,1024]{1,0:T(8,128)(2,1)S(1)}, u32[]{:S(2)}, u32[]{:S(2)}) %collective-permute-start.43) | collective-permute-done | bytes 524320 | tf_op jit(solution)/shard_map/ppermute | solution.py:85
  207.3 11.4 %feed_forward_back.3 = (bf16[512,1024]{1,0:T(8,128)(2,1)}, bf16[512,1024]{1,0:T(8,128)(2,1)}, f32[256,1024]{1,0:T(8,128)}, bf16[256,1024]{1,0:T(8,128)(2,1)}, f32[1,1024]{1,0:T(1,128)}, /*index=5*/f32[1,1024]{1,0:T(1,128)}) custom-call(bf16[256,1024]{1,0:T(8,128)(2,1)} %get-tuple-element.128.refs_0_.refs_3_, bf16[256,1024]{1,0:T(8,128)(2,1)} %copy-done.27, ...), custom_call_target="tpu_custom_call" | custom-call | flops 4294967 | bytes 23601 | tf_op jit(solution)/shard_map/feed_forward_back/pallas_call | solution.py:62
  220.7 11.4 %feed_forward_back.2 = (bf16[512,1024]{1,0:T(8,128)(2,1)}, bf16[512,1024]{1,0:T(8,128)(2,1)}, f32[256,1024]{1,0:T(8,128)}, bf16[256,1024]{1,0:T(8,128)(2,1)}, f32[1,1024]{1,0:T(1,128)}, /*index=5*/f32[1,1024]{1,0:T(1,128)}) custom-call(bf16[256,1024]{1,0:T(8,128)(2,1)} %get-tuple-element.123.refs_0_.refs_1_, bf16[256,1024]{1,0:T(8,128)(2,1)} %copy-done.28, ...), custom_call_target="tpu_custom_call" | custom-call | flops 4294967 | bytes 23601 | tf_op jit(solution)/shard_map/feed_forward_back/pallas_call | solution.py:62
  233.0 9.7 %w_down_grad.1 = (f32[1024,1024]{1,0:T(8,128)}, bf16[1024,1024]{1,0:T(8,128)(2,1)}) custom-call(s32[1]{0:T(128)} %bitcast.1.refs_0_, bf16[256,1024]{1,0:T(8,128)(2,1)} %get-tuple-element.123.refs_0_.refs_1_, bf16[256,1024]{1,0:T(8,128)(2,1)} %copy-done.28, bf16[256,1024]{1,0:T(8,128)(2,1)} %get-tuple-element.128.refs_0_.refs_3_, ...), custom_call_target="tpu_custom_call" | custom-call | flops 4294967 | bytes 12582 | tf_op jit(solution)/shard_map/w_down_grad/pallas_call | solution.py:62
  243.5 4.0 first_norm_back.3
  248.3 3.9 first_norm_back.2
  252.2 10.0 %w_up_grad.1 = (f32[1024,1024]{1,0:T(8,128)}, bf16[1024,1024]{1,0:T(8,128)(2,1)}) custom-call(s32[1]{0:T(128)} %bitcast.1.refs_0_, bf16[256,1024]{1,0:T(8,128)(2,1)} %get-tuple-element.107.refs_0_.refs_1_, bf16[256,1024]{1,0:T(8,128)(2,1)} %copy-done.26, bf16[256,1024]{1,0:T(8,128)(2,1)} %get-tuple-element.117.refs_0_.refs_3_, bf16[256,1024]{1,0:T(8,128)(2,1)} %copy-done.25, ...), custom_call_target="tpu_custom_call" | custom-call | flops 4294967 | bytes 12582 | tf_op jit(solution)/shard_map/w_up_grad/pallas_call | solution.py:62
  265.8 11.8 %collective-permute-done.44.refs_5_.refs_2_ = bf16[256,1024]{1,0:T(8,128)(2,1)} collective-permute-done((bf16[256,1024]{1,0:T(8,128)(2,1)S(1)}, bf16[256,1024]{1,0:T(8,128)(2,1)}, u32[]{:S(2)}, u32[]{:S(2)}) %collective-permute-start.44) | collective-permute-done | bytes 524320 | tf_op jit(solution)/shard_map/ppermute | solution.py:85
  278.9 26.1 %attention_backward.2 = (bf16[512,512]{1,0:T(8,128)(2,1)}, f32[512,1024]{1,0:T(8,128)}, bf16[512,1024]{1,0:T(8,128)(2,1)}, f32[2,512]{1,0:T(2,128)}) custom-call(bf16[512,768]{1,0:T(8,128)(2,1)} %get-tuple-element.101.refs_0_, bf16[512,768]{1,0:T(8,128)(2,1)} %get-tuple-element.102.refs_1_, bf16[512,1024]{1,0:T(8,128)(2,1)} %copy-done.13, ...), custom_call_target="tpu_custom_call" | custom-call | flops 10737418 | bytes 11542 | tf_op jit(solution)/shard_map/attention_backward/pallas_call | solution.py:45
  305.1 4.6 w_out_grad.1
  309.7 3.0 convert_add_fusion.1
  315.5 2.6 convert_add_fusion
  318.2 2.0 copy-done.2
  326.3 19.1 %collective-permute-done.55.refs_7_ = bf16[512,256]{1,0:T(8,128)(2,1)S(1)} collective-permute-done((bf16[512,256]{1,0:T(8,128)(2,1)S(1)}, bf16[512,256]{1,0:T(8,128)(2,1)S(1)}, u32[]{:S(2)}, u32[]{:S(2)}) %collective-permute-start.55) | collective-permute-done | bytes 262176 | tf_op jit(solution)/shard_map/ppermute | solution.py:90
  347.0 26.2 %attention_backward.3 = (bf16[512,512]{1,0:T(8,128)(2,1)}, f32[512,1024]{1,0:T(8,128)}, bf16[512,1024]{1,0:T(8,128)(2,1)}, f32[2,512]{1,0:T(2,128)}) custom-call(bf16[512,768]{1,0:T(8,128)(2,1)} %get-tuple-element.111.refs_0_, bf16[512,768]{1,0:T(8,128)(2,1)} %get-tuple-element.112.refs_1_, bf16[512,1024]{1,0:T(8,128)(2,1)} %copy-done.16, ...), custom_call_target="tpu_custom_call" | custom-call | flops 10737418 | bytes 11542 | tf_op jit(solution)/shard_map/attention_backward/pallas_call | solution.py:45
  375.2 3.0 collective-permute-start.68
  379.3 2.2 slice_add_fusion.1
  387.7 4.4 w_query_grad.1
  392.7 1.6 collective-permute-start.74
  394.3 1.7 slice_add_fusion
  396.5 2.2 collective-permute-done.74
  400.7 2.0 collective-permute-start.70
  402.6 7.0 %collective-permute-done.75 = f32[12288]{0:T(1024)S(1)} collective-permute-done((f32[12288]{0:T(1024)S(1)}, f32[12288]{0:T(1024)S(1)}, u32[]{:S(2)}, u32[]{:S(2)}) %collective-permute-start.75) | collective-permute-done | bytes 49184 | tf_op jit(solution)/shard_map/ppermute | solution.py:90
  412.6 6.3 %project_back.2 = (bf16[512,512]{1,0:T(8,128)(2,1)}, bf16[512,512]{1,0:T(8,128)(2,1)}, f32[256,1024]{1,0:T(8,128)}, bf16[256,1024]{1,0:T(8,128)(2,1)}) custom-call(bf16[512,512]{1,0:T(8,128)(2,1)} %get-tuple-element.148.refs_0_.refs_5_.refs_7_, f32[512,1024]{1,0:T(8,128)} %get-tuple-element.149.refs_1_, bf16[512,1024]{1,0:T(8,128)(2,1)} %copy-done.15, ...), custom_call_target="tpu_custom_call" | custom-call | flops 1610612 | bytes 10485 | tf_op jit(solution)/shard_map/project_back/pallas_call | solution.py:45
  418.9 6.2 %project_back.3 = (bf16[512,512]{1,0:T(8,128)(2,1)}, bf16[512,512]{1,0:T(8,128)(2,1)}, f32[256,1024]{1,0:T(8,128)}, bf16[256,1024]{1,0:T(8,128)(2,1)}) custom-call(bf16[512,512]{1,0:T(8,128)(2,1)} %get-tuple-element.163.refs_0_.refs_6_.refs_8_, f32[512,1024]{1,0:T(8,128)} %get-tuple-element.164.refs_1_, bf16[512,1024]{1,0:T(8,128)(2,1)} %collective-permute-done.57.refs_2_, ...), custom_call_target="tpu_custom_call" | custom-call | flops 1610612 | bytes 10485 | tf_op jit(solution)/shard_map/project_back/pallas_call | solution.py:45
  425.1 6.7 %w_key_value_grad.1 = (f32[1024,512]{1,0:T(8,128)}, bf16[1024,512]{1,0:T(8,128)(2,1)}) custom-call(s32[1]{0:T(128)} %bitcast.1.refs_0_, bf16[256,1024]{1,0:T(8,128)(2,1)} %copy-done.1, bf16[256,1024]{1,0:T(8,128)(2,1)} %copy-done.8, bf16[256,1024]{1,0:T(8,128)(2,1)} %copy-done, bf16[256,1024]{1,0:T(8,128)(2,1)} %copy-done.7, ...), custom_call_target="tpu_custom_call" | custom-call | flops 2147483 | bytes 7340 | tf_op jit(solution)/shard_map/w_key_value_grad/pallas_call | solution.py:62
  436.2 12.1 %collective-permute-done.69 = bf16[128,1024]{1,0:T(8,128)(2,1)} collective-permute-done((bf16[128,1024]{1,0:T(8,128)(2,1)}, bf16[128,1024]{1,0:T(8,128)(2,1)}, u32[]{:S(2)}, u32[]{:S(2)}) %collective-permute-start.69) | collective-permute-done | bytes 262176 | tf_op jit(solution)/shard_map/ppermute | solution.py:90
  448.3 1.8 slice_add_fusion.6
  450.3 1.7 convert_add_fusion.2
  453.5 1.9 collective-permute-done.63
  457.3 8.3 %collective-permute-done.65 = bf16[512,512]{1,0:T(8,128)(2,1)S(1)} collective-permute-done((bf16[512,512]{1,0:T(8,128)(2,1)S(1)}, bf16[512,512]{1,0:T(8,128)(2,1)S(1)}, u32[]{:S(2)}, u32[]{:S(2)}) %collective-permute-start.65) | collective-permute-done | bytes 524320 | tf_op jit(solution)/shard_map/ppermute | solution.py:90
  465.9 1.9 collective-permute-start.66
  469.1 4.1 collective-permute-done.66
  473.3 2.2 collective-permute-start.67
  476.5 4.1 collective-permute-done.67
  (370 shorter events, 87.7 us)
Async XLA Ops:
  3.9 16.3 %collective-permute-start.1 = (bf16[128,1024]{1,0:T(8,128)(2,1)}, bf16[128,1024]{1,0:T(8,128)(2,1)S(1)}, u32[]{:S(2)}, u32[]{:S(2)}) collective-permute-start(bf16[128,1024]{1,0:T(8,128)(2,1)} %pack_attention.1.refs_1_), channel_id=1, source_target_pairs={{0,16},{4,20},{8,24},{12,28},{16,0},{20,4},{24,8},{28,12},{1,17},{... | collective-permute-start | bytes 786440 | tf_op jit(solution)/shard_map/ppermute | solution.py:90
  8.0 12.5 %collective-permute-start.2 = (bf16[128,1024]{1,0:T(8,128)(2,1)}, bf16[128,1024]{1,0:T(8,128)(2,1)}, u32[]{:S(2)}, u32[]{:S(2)}) collective-permute-start(bf16[128,1024]{1,0:T(8,128)(2,1)} %pack_attention.1.refs_1_), channel_id=1, source_target_pairs={{0,8},{4,12},{8,0},{12,4},{16,24},{20,28},{24,16},{28,20},{1,9},{5... | collective-permute-start | bytes 786440 | tf_op jit(solution)/shard_map/ppermute | solution.py:90
  9.6 12.4 %collective-permute-start.4 = (bf16[128,1024]{1,0:T(8,128)(2,1)}, bf16[128,1024]{1,0:T(8,128)(2,1)S(1)}, u32[]{:S(2)}, u32[]{:S(2)}) collective-permute-start(bf16[128,1024]{1,0:T(8,128)(2,1)} %pack_attention.1.refs_1_), channel_id=1, source_target_pairs={{0,4},{4,0},{8,12},{12,8},{16,20},{20,16},{24,28},{28,24},{1,5},{5... | collective-permute-start | bytes 786440 | tf_op jit(solution)/shard_map/ppermute | solution.py:90
  13.1 18.2 %collective-permute-start = (bf16[256,1024]{1,0:T(8,128)(2,1)S(1)}, bf16[256,1024]{1,0:T(8,128)(2,1)S(1)}, u32[]{:S(2)}, u32[]{:S(2)}) collective-permute-start(bf16[256,1024]{1,0:T(8,128)(2,1)S(1)} %get-tuple-element.221.refs_0_.refs_1_), channel_id=1, source_target_pairs={{0,2},{1,3},{2,0},{3,1},{4,6},{5,7},{6,4},{7,5},{8,10},{9,11},{10,... | collective-permute-start | bytes 1572872 | tf_op jit(solution)/shard_map/ppermute | solution.py:85
  14.7 24.0 %collective-permute-start.9 = (bf16[256,1024]{1,0:T(8,128)(2,1)S(1)}, bf16[256,1024]{1,0:T(8,128)(2,1)S(1)}, u32[]{:S(2)}, u32[]{:S(2)}) collective-permute-start(bf16[256,1024]{1,0:T(8,128)(2,1)S(1)} %get-tuple-element.222.refs_0_.refs_3_), channel_id=1, source_target_pairs={{0,2},{1,3},{2,0},{3,1},{4,6},{5,7},{6,4},{7,5},{8,10},{9,11},{10,... | collective-permute-start | bytes 1572872 | tf_op jit(solution)/shard_map/ppermute | solution.py:85
  20.5 8.4 %collective-permute-start.3 = (bf16[128,1024]{1,0:T(8,128)(2,1)S(1)}, bf16[128,1024]{1,0:T(8,128)(2,1)S(1)}, u32[]{:S(2)}, u32[]{:S(2)}) collective-permute-start(bf16[128,1024]{1,0:T(8,128)(2,1)S(1)} %collective-permute-done.1.refs_2_), channel_id=1, source_target_pairs={{0,8},{4,12},{8,0},{12,4},{16,24},{20,28},{24,16},{28,20},{1,9},{5... | collective-permute-start | bytes 786440 | tf_op jit(solution)/shard_map/ppermute | solution.py:90
  22.0 9.2 %collective-permute-start.5 = (bf16[128,1024]{1,0:T(8,128)(2,1)S(1)}, bf16[128,1024]{1,0:T(8,128)(2,1)}, u32[]{:S(2)}, u32[]{:S(2)}) collective-permute-start(bf16[128,1024]{1,0:T(8,128)(2,1)S(1)} %collective-permute-done.1.refs_2_), channel_id=1, source_target_pairs={{0,4},{4,0},{8,12},{12,8},{16,20},{20,16},{24,28},{28,24},{1,5},{5... | collective-permute-start | bytes 786440 | tf_op jit(solution)/shard_map/ppermute | solution.py:90
  27.2 11.6 %collective-permute-start.6 = (bf16[128,1024]{1,0:T(8,128)(2,1)}, bf16[128,1024]{1,0:T(8,128)(2,1)}, u32[]{:S(2)}, u32[]{:S(2)}) collective-permute-start(bf16[128,1024]{1,0:T(8,128)(2,1)} %collective-permute-done.2.refs_3_), channel_id=1, source_target_pairs={{0,4},{4,0},{8,12},{12,8},{16,20},{20,16},{24,28},{28,24},{1,5},{5... | collective-permute-start | bytes 786440 | tf_op jit(solution)/shard_map/ppermute | solution.py:90
  29.0 25.8 %collective-permute-start.8 = (bf16[128,2048]{1,0:T(8,128)(2,1)}, bf16[128,2048]{1,0:T(8,128)(2,1)S(1)}, u32[]{:S(2)}, u32[]{:S(2)}) collective-permute-start(bf16[128,2048]{1,0:T(8,128)(2,1)} %pack_feed.1.refs_1_), channel_id=1, source_target_pairs={{0,16},{4,20},{8,24},{12,28},{16,0},{20,4},{24,8},{28,12},{1,17},{... | collective-permute-start | bytes 1572872 | tf_op jit(solution)/shard_map/ppermute | solution.py:90
  31.2 8.0 %collective-permute-start.11 = (bf16[128,1024]{1,0:T(8,128)(2,1)}, bf16[128,1024]{1,0:T(8,128)(2,1)S(1)}, u32[]{:S(2)}, u32[]{:S(2)}) collective-permute-start(bf16[128,1024]{1,0:T(8,128)(2,1)} %copy-done.37), channel_id=1, source_target_pairs={{0,1},{1,0},{2,3},{3,2},{4,5},{5,4},{6,7},{7,6},{8,9},{9,8},{10,11... | collective-permute-start | bytes 786440 | tf_op jit(solution)/shard_map/ppermute | solution.py:85
  31.3 24.7 %collective-permute-start.18 = (bf16[128,2048]{1,0:T(8,128)(2,1)}, bf16[128,2048]{1,0:T(8,128)(2,1)S(1)}, u32[]{:S(2)}, u32[]{:S(2)}) collective-permute-start(bf16[128,2048]{1,0:T(8,128)(2,1)} %pack_feed.1.refs_1_), channel_id=1, source_target_pairs={{0,8},{4,12},{8,0},{12,4},{16,24},{20,28},{24,16},{28,20},{1,9},{5... | collective-permute-start | bytes 1572872 | tf_op jit(solution)/shard_map/ppermute | solution.py:90
  39.2 15.6 %collective-permute-start.7 = (bf16[128,1024]{1,0:T(8,128)(2,1)}, bf16[128,1024]{1,0:T(8,128)(2,1)}, u32[]{:S(2)}, u32[]{:S(2)}) collective-permute-start(bf16[128,1024]{1,0:T(8,128)(2,1)} %copy-done.63), channel_id=1, source_target_pairs={{0,4},{4,0},{8,12},{12,8},{16,20},{20,16},{24,28},{28,24},{1,5},{5... | collective-permute-start | bytes 786440 | tf_op jit(solution)/shard_map/ppermute | solution.py:90
  40.5 22.9 %collective-permute-start.24 = (bf16[128,2048]{1,0:T(8,128)(2,1)}, bf16[128,2048]{1,0:T(8,128)(2,1)}, u32[]{:S(2)}, u32[]{:S(2)}) collective-permute-start(bf16[128,2048]{1,0:T(8,128)(2,1)} %pack_feed.1.refs_1_), channel_id=1, source_target_pairs={{0,4},{4,0},{8,12},{12,8},{16,20},{20,16},{24,28},{28,24},{1,5},{5... | collective-permute-start | bytes 1572872 | tf_op jit(solution)/shard_map/ppermute | solution.py:90
  41.3 19.0 %collective-permute-start.13 = (bf16[128,1024]{1,0:T(8,128)(2,1)}, bf16[128,1024]{1,0:T(8,128)(2,1)}, u32[]{:S(2)}, u32[]{:S(2)}) collective-permute-start(bf16[128,1024]{1,0:T(8,128)(2,1)} %copy-done.63), channel_id=1, source_target_pairs={{0,1},{1,0},{2,3},{3,2},{4,5},{5,4},{6,7},{7,6},{8,9},{9,8},{10,11... | collective-permute-start | bytes 786440 | tf_op jit(solution)/shard_map/ppermute | solution.py:85
  69.0 22.0 %collective-permute-start.37 = (bf16[512,1024]{1,0:T(8,128)(2,1)}, bf16[512,1024]{1,0:T(8,128)(2,1)S(1)}, u32[]{:S(2)}, u32[]{:S(2)}) collective-permute-start(bf16[512,1024]{1,0:T(8,128)(2,1)} %get-tuple-element.113), channel_id=1, source_target_pairs={{0,1},{1,0},{2,3},{3,2},{4,5},{5,4},{6,7},{7,6},{8,9},{9,8},{10,11... | collective-permute-start | bytes 3145736 | tf_op jit(solution)/shard_map/ppermute | solution.py:85
  75.0 31.9 %collective-permute-start.20 = (bf16[512,1024]{1,0:T(8,128)(2,1)}, bf16[512,1024]{1,0:T(8,128)(2,1)S(1)}, u32[]{:S(2)}, u32[]{:S(2)}) collective-permute-start(bf16[512,1024]{1,0:T(8,128)(2,1)} %get-tuple-element.103), channel_id=1, source_target_pairs={{0,1},{1,0},{2,3},{3,2},{4,5},{5,4},{6,7},{7,6},{8,9},{9,8},{10,11... | collective-permute-start | bytes 3145736 | tf_op jit(solution)/shard_map/ppermute | solution.py:85
  75.2 14.2 %collective-permute-start.25 = (bf16[128,2048]{1,0:T(8,128)(2,1)S(1)}, bf16[128,2048]{1,0:T(8,128)(2,1)}, u32[]{:S(2)}, u32[]{:S(2)}) collective-permute-start(bf16[128,2048]{1,0:T(8,128)(2,1)S(1)} %copy-done.18), channel_id=1, source_target_pairs={{0,4},{4,0},{8,12},{12,8},{16,20},{20,16},{24,28},{28,24},{1,5},{5... | collective-permute-start | bytes 1572872 | tf_op jit(solution)/shard_map/ppermute | solution.py:90
  76.7 28.1 %collective-permute-start.21 = (bf16[128,2048]{1,0:T(8,128)(2,1)S(1)}, bf16[128,2048]{1,0:T(8,128)(2,1)}, u32[]{:S(2)}, u32[]{:S(2)}) collective-permute-start(bf16[128,2048]{1,0:T(8,128)(2,1)S(1)} %copy-done.18), channel_id=1, source_target_pairs={{0,8},{4,12},{8,0},{12,4},{16,24},{20,28},{24,16},{28,20},{1,9},{5... | collective-permute-start | bytes 1572872 | tf_op jit(solution)/shard_map/ppermute | solution.py:90
  79.9 40.9 %collective-permute-start.28 = (bf16[128,2048]{1,0:T(8,128)(2,1)}, bf16[128,2048]{1,0:T(8,128)(2,1)S(1)}, u32[]{:S(2)}, u32[]{:S(2)}) collective-permute-start(bf16[128,2048]{1,0:T(8,128)(2,1)} %pack_feed.1.refs_1_), channel_id=1, source_target_pairs={{0,1},{1,0},{2,3},{3,2},{4,5},{5,4},{6,7},{7,6},{8,9},{9,8},{10,11... | collective-permute-start | bytes 1572872 | tf_op jit(solution)/shard_map/ppermute | solution.py:85
  89.5 31.4 %collective-permute-start.26 = (bf16[128,2048]{1,0:T(8,128)(2,1)S(1)}, bf16[128,2048]{1,0:T(8,128)(2,1)S(1)}, u32[]{:S(2)}, u32[]{:S(2)}) collective-permute-start(bf16[128,2048]{1,0:T(8,128)(2,1)S(1)} %copy-done.20), channel_id=1, source_target_pairs={{0,4},{4,0},{8,12},{12,8},{16,20},{20,16},{24,28},{28,24},{1,5},{5... | collective-permute-start | bytes 1572872 | tf_op jit(solution)/shard_map/ppermute | solution.py:90
  91.0 30.5 %collective-permute-start.29 = (bf16[128,2048]{1,0:T(8,128)(2,1)S(1)}, bf16[128,2048]{1,0:T(8,128)(2,1)S(1)}, u32[]{:S(2)}, u32[]{:S(2)}) collective-permute-start(bf16[128,2048]{1,0:T(8,128)(2,1)S(1)} %copy-done.18), channel_id=1, source_target_pairs={{0,1},{1,0},{2,3},{3,2},{4,5},{5,4},{6,7},{7,6},{8,9},{9,8},{10,11... | collective-permute-start | bytes 1572872 | tf_op jit(solution)/shard_map/ppermute | solution.py:85
  104.9 17.1 %collective-permute-start.38 = (bf16[256,1024]{1,0:T(8,128)(2,1)}, bf16[256,1024]{1,0:T(8,128)(2,1)S(1)}, u32[]{:S(2)}, u32[]{:S(2)}) collective-permute-start(bf16[256,1024]{1,0:T(8,128)(2,1)} %get-tuple-element.115), channel_id=1, source_target_pairs={{0,2},{1,3},{2,0},{3,1},{4,6},{5,7},{6,4},{7,5},{8,10},{9,11},{10,... | collective-permute-start | bytes 1572872 | tf_op jit(solution)/shard_map/ppermute | solution.py:85
  107.0 19.1 %collective-permute-start.30 = (bf16[128,2048]{1,0:T(8,128)(2,1)S(1)}, bf16[128,2048]{1,0:T(8,128)(2,1)S(1)}, u32[]{:S(2)}, u32[]{:S(2)}) collective-permute-start(bf16[128,2048]{1,0:T(8,128)(2,1)S(1)} %copy-done.20), channel_id=1, source_target_pairs={{0,1},{1,0},{2,3},{3,2},{4,5},{5,4},{6,7},{7,6},{8,9},{9,8},{10,11... | collective-permute-start | bytes 1572872 | tf_op jit(solution)/shard_map/ppermute | solution.py:85
  120.8 14.5 %collective-permute-start.27 = (bf16[128,2048]{1,0:T(8,128)(2,1)}, bf16[128,2048]{1,0:T(8,128)(2,1)S(1)}, u32[]{:S(2)}, u32[]{:S(2)}) collective-permute-start(bf16[128,2048]{1,0:T(8,128)(2,1)} %collective-permute-done.21.refs_6_.refs_4_), channel_id=1, source_target_pairs={{0,4},{4,0},{8,12},{12,8},{16,20},{20,16},{24,28},{28,24},{1,5},{5... | collective-permute-start | bytes 1572872 | tf_op jit(solution)/shard_map/ppermute | solution.py:90
  121.5 14.2 %collective-permute-start.22 = (bf16[256,1024]{1,0:T(8,128)(2,1)}, bf16[256,1024]{1,0:T(8,128)(2,1)S(1)}, u32[]{:S(2)}, u32[]{:S(2)}) collective-permute-start(bf16[256,1024]{1,0:T(8,128)(2,1)} %get-tuple-element.105), channel_id=1, source_target_pairs={{0,2},{1,3},{2,0},{3,1},{4,6},{5,7},{6,4},{7,5},{8,10},{9,11},{10,... | collective-permute-start | bytes 1572872 | tf_op jit(solution)/shard_map/ppermute | solution.py:85
  122.0 17.8 %collective-permute-start.31 = (bf16[128,2048]{1,0:T(8,128)(2,1)}, bf16[128,2048]{1,0:T(8,128)(2,1)S(1)}, u32[]{:S(2)}, u32[]{:S(2)}) collective-permute-start(bf16[128,2048]{1,0:T(8,128)(2,1)} %collective-permute-done.21.refs_6_.refs_4_), channel_id=1, source_target_pairs={{0,1},{1,0},{2,3},{3,2},{4,5},{5,4},{6,7},{7,6},{8,9},{9,8},{10,11... | collective-permute-start | bytes 1572872 | tf_op jit(solution)/shard_map/ppermute | solution.py:85
  126.0 20.0 %collective-permute-start.33 = (bf16[128,2048]{1,0:T(8,128)(2,1)}, bf16[128,2048]{1,0:T(8,128)(2,1)S(1)}, u32[]{:S(2)}, u32[]{:S(2)}) collective-permute-start(bf16[128,2048]{1,0:T(8,128)(2,1)} %collective-permute-done.25.refs_6_), channel_id=1, source_target_pairs={{0,1},{1,0},{2,3},{3,2},{4,5},{5,4},{6,7},{7,6},{8,9},{9,8},{10,11... | collective-permute-start | bytes 1572872 | tf_op jit(solution)/shard_map/ppermute | solution.py:85
  126.1 20.0 %collective-permute-start.34 = (bf16[128,2048]{1,0:T(8,128)(2,1)S(1)}, bf16[128,2048]{1,0:T(8,128)(2,1)S(1)}, u32[]{:S(2)}, u32[]{:S(2)}) collective-permute-start(bf16[128,2048]{1,0:T(8,128)(2,1)S(1)} %collective-permute-done.26.refs_7_), channel_id=1, source_target_pairs={{0,1},{1,0},{2,3},{3,2},{4,5},{5,4},{6,7},{7,6},{8,9},{9,8},{10,11... | collective-permute-start | bytes 1572872 | tf_op jit(solution)/shard_map/ppermute | solution.py:85
  135.4 10.7 %collective-permute-start.35 = (bf16[128,2048]{1,0:T(8,128)(2,1)S(1)}, bf16[128,2048]{1,0:T(8,128)(2,1)S(1)}, u32[]{:S(2)}, u32[]{:S(2)}) collective-permute-start(bf16[128,2048]{1,0:T(8,128)(2,1)S(1)} %collective-permute-done.27.refs_8_), channel_id=1, source_target_pairs={{0,1},{1,0},{2,3},{3,2},{4,5},{5,4},{6,7},{7,6},{8,9},{9,8},{10,11... | collective-permute-start | bytes 1572872 | tf_op jit(solution)/shard_map/ppermute | solution.py:85
  135.6 16.7 %collective-permute-start.39 = (bf16[256,1024]{1,0:T(8,128)(2,1)}, bf16[256,1024]{1,0:T(8,128)(2,1)S(1)}, u32[]{:S(2)}, u32[]{:S(2)}) collective-permute-start(bf16[256,1024]{1,0:T(8,128)(2,1)} %get-tuple-element.117.refs_0_.refs_3_), channel_id=1, source_target_pairs={{0,2},{1,3},{2,0},{3,1},{4,6},{5,7},{6,4},{7,5},{8,10},{9,11},{10,... | collective-permute-start | bytes 1572872 | tf_op jit(solution)/shard_map/ppermute | solution.py:85
  139.8 26.7 %collective-permute-start.23 = (bf16[256,1024]{1,0:T(8,128)(2,1)}, bf16[256,1024]{1,0:T(8,128)(2,1)S(1)}, u32[]{:S(2)}, u32[]{:S(2)}) collective-permute-start(bf16[256,1024]{1,0:T(8,128)(2,1)} %get-tuple-element.107.refs_0_.refs_1_), channel_id=1, source_target_pairs={{0,2},{1,3},{2,0},{3,1},{4,6},{5,7},{6,4},{7,5},{8,10},{9,11},{10,... | collective-permute-start | bytes 1572872 | tf_op jit(solution)/shard_map/ppermute | solution.py:85
  165.5 16.9 %collective-permute-start.40 = (bf16[256,1024]{1,0:T(8,128)(2,1)}, bf16[256,1024]{1,0:T(8,128)(2,1)S(1)}, u32[]{:S(2)}, u32[]{:S(2)}) collective-permute-start(bf16[256,1024]{1,0:T(8,128)(2,1)} %get-tuple-element.119), channel_id=1, source_target_pairs={{0,2},{1,3},{2,0},{3,1},{4,6},{5,7},{6,4},{7,5},{8,10},{9,11},{10,... | collective-permute-start | bytes 1572872 | tf_op jit(solution)/shard_map/ppermute | solution.py:85
  180.1 15.1 %collective-permute-start.36 = (bf16[256,1024]{1,0:T(8,128)(2,1)}, bf16[256,1024]{1,0:T(8,128)(2,1)S(1)}, u32[]{:S(2)}, u32[]{:S(2)}) collective-permute-start(bf16[256,1024]{1,0:T(8,128)(2,1)} %get-tuple-element.109), channel_id=1, source_target_pairs={{0,2},{1,3},{2,0},{3,1},{4,6},{5,7},{6,4},{7,5},{8,10},{9,11},{10,... | collective-permute-start | bytes 1572872 | tf_op jit(solution)/shard_map/ppermute | solution.py:85
  187.2 19.3 %collective-permute-start.43 = (bf16[256,1024]{1,0:T(8,128)(2,1)}, bf16[256,1024]{1,0:T(8,128)(2,1)S(1)}, u32[]{:S(2)}, u32[]{:S(2)}) collective-permute-start(bf16[256,1024]{1,0:T(8,128)(2,1)} %get-tuple-element.128.refs_0_.refs_3_), channel_id=1, source_target_pairs={{0,2},{1,3},{2,0},{3,1},{4,6},{5,7},{6,4},{7,5},{8,10},{9,11},{10,... | collective-permute-start | bytes 1572872 | tf_op jit(solution)/shard_map/ppermute | solution.py:85
  200.1 19.9 %collective-permute-start.41 = (bf16[256,1024]{1,0:T(8,128)(2,1)}, bf16[256,1024]{1,0:T(8,128)(2,1)S(1)}, u32[]{:S(2)}, u32[]{:S(2)}) collective-permute-start(bf16[256,1024]{1,0:T(8,128)(2,1)} %get-tuple-element.123.refs_0_.refs_1_), channel_id=1, source_target_pairs={{0,2},{1,3},{2,0},{3,1},{4,6},{5,7},{6,4},{7,5},{8,10},{9,11},{10,... | collective-permute-start | bytes 1572872 | tf_op jit(solution)/shard_map/ppermute | solution.py:85
  218.7 24.0 %collective-permute-start.46 = (bf16[256,1024]{1,0:T(8,128)(2,1)}, bf16[256,1024]{1,0:T(8,128)(2,1)S(1)}, u32[]{:S(2)}, u32[]{:S(2)}) collective-permute-start(bf16[256,1024]{1,0:T(8,128)(2,1)} %get-tuple-element.145), channel_id=1, source_target_pairs={{0,2},{1,3},{2,0},{3,1},{4,6},{5,7},{6,4},{7,5},{8,10},{9,11},{10,... | collective-permute-start | bytes 1572872 | tf_op jit(solution)/shard_map/ppermute | solution.py:85
  232.1 15.4 %collective-permute-start.42 = (bf16[256,1024]{1,0:T(8,128)(2,1)}, bf16[256,1024]{1,0:T(8,128)(2,1)S(1)}, u32[]{:S(2)}, u32[]{:S(2)}) collective-permute-start(bf16[256,1024]{1,0:T(8,128)(2,1)} %get-tuple-element.127), channel_id=1, source_target_pairs={{0,2},{1,3},{2,0},{3,1},{4,6},{5,7},{6,4},{7,5},{8,10},{9,11},{10,... | collective-permute-start | bytes 1572872 | tf_op jit(solution)/shard_map/ppermute | solution.py:85
  242.7 34.9 %collective-permute-start.45 = (bf16[1024,1024]{1,0:T(8,128)(2,1)}, bf16[1024,1024]{1,0:T(8,128)(2,1)S(1)}, u32[]{:S(2)}, u32[]{:S(2)}) collective-permute-start(bf16[1024,1024]{1,0:T(8,128)(2,1)} %get-tuple-element.136.refs_5_), channel_id=1, source_target_pairs={{0,1},{1,0},{2,3},{3,2},{4,5},{5,4},{6,7},{7,6},{8,9},{9,8},{10,11... | collective-permute-start | bytes 6291464 | tf_op jit(solution)/shard_map/ppermute | solution.py:85
  262.2 53.3 %collective-permute-start.50 = (bf16[1024,1024]{1,0:T(8,128)(2,1)}, bf16[1024,1024]{1,0:T(8,128)(2,1)}, u32[]{:S(2)}, u32[]{:S(2)}) collective-permute-start(bf16[1024,1024]{1,0:T(8,128)(2,1)} %get-tuple-element.147.refs_9_), channel_id=1, source_target_pairs={{0,1},{1,0},{2,3},{3,2},{4,5},{5,4},{6,7},{7,6},{8,9},{9,8},{10,11... | collective-permute-start | bytes 6291464 | tf_op jit(solution)/shard_map/ppermute | solution.py:85
  262.7 14.9 %collective-permute-start.44 = (bf16[256,1024]{1,0:T(8,128)(2,1)S(1)}, bf16[256,1024]{1,0:T(8,128)(2,1)}, u32[]{:S(2)}, u32[]{:S(2)}) collective-permute-start(bf16[256,1024]{1,0:T(8,128)(2,1)S(1)} %copy-done.11), channel_id=1, source_target_pairs={{0,2},{1,3},{2,0},{3,1},{4,6},{5,7},{6,4},{7,5},{8,10},{9,11},{10,... | collective-permute-start | bytes 1572872 | tf_op jit(solution)/shard_map/ppermute | solution.py:85
  263.9 41.2 %collective-permute-start.53 = (bf16[256,1024]{1,0:T(8,128)(2,1)S(1)}, bf16[256,1024]{1,0:T(8,128)(2,1)}, u32[]{:S(2)}, u32[]{:S(2)}) collective-permute-start(bf16[256,1024]{1,0:T(8,128)(2,1)S(1)} %copy-done.12), channel_id=1, source_target_pairs={{0,2},{1,3},{2,0},{3,1},{4,6},{5,7},{6,4},{7,5},{8,10},{9,11},{10,... | collective-permute-start | bytes 1572872 | tf_op jit(solution)/shard_map/ppermute | solution.py:85
  309.6 14.4 %collective-permute-start.54 = (bf16[1024,256]{1,0:T(8,128)(2,1)}, bf16[1024,256]{1,0:T(8,128)(2,1)S(1)}, u32[]{:S(2)}, u32[]{:S(2)}) collective-permute-start(bf16[1024,256]{1,0:T(8,128)(2,1)} %get-tuple-element.159), channel_id=1, source_target_pairs={{0,1},{1,0},{2,3},{3,2},{4,5},{5,4},{6,7},{7,6},{8,9},{9,8},{10,11... | collective-permute-start | bytes 1572872 | tf_op jit(solution)/shard_map/ppermute | solution.py:85
  314.0 32.8 %collective-permute-start.48 = (bf16[512,1024]{1,0:T(8,128)(2,1)}, bf16[512,1024]{1,0:T(8,128)(2,1)}, u32[]{:S(2)}, u32[]{:S(2)}) collective-permute-start(bf16[512,1024]{1,0:T(8,128)(2,1)} %slice.315), channel_id=1, source_target_pairs={{0,4},{4,0},{8,12},{12,8},{16,20},{20,16},{24,28},{28,24},{1,5},{5... | collective-permute-start | bytes 3145736 | tf_op jit(solution)/shard_map/ppermute | solution.py:90
  321.4 25.6 %collective-permute-start.51 = (bf16[512,1024]{1,0:T(8,128)(2,1)}, bf16[512,1024]{1,0:T(8,128)(2,1)}, u32[]{:S(2)}, u32[]{:S(2)}) collective-permute-start(bf16[512,1024]{1,0:T(8,128)(2,1)} %slice.314), channel_id=1, source_target_pairs={{0,8},{4,12},{8,0},{12,4},{16,24},{20,28},{24,16},{28,20},{1,9},{5... | collective-permute-start | bytes 3145736 | tf_op jit(solution)/shard_map/ppermute | solution.py:90
  324.2 21.2 %collective-permute-start.55 = (bf16[512,256]{1,0:T(8,128)(2,1)S(1)}, bf16[512,256]{1,0:T(8,128)(2,1)S(1)}, u32[]{:S(2)}, u32[]{:S(2)}) collective-permute-start(bf16[512,256]{1,0:T(8,128)(2,1)S(1)} %slice.323), channel_id=1, source_target_pairs={{0,4},{4,0},{8,12},{12,8},{16,20},{20,16},{24,28},{28,24},{1,5},{5... | collective-permute-start | bytes 786440 | tf_op jit(solution)/shard_map/ppermute | solution.py:90
  326.2 60.5 %collective-permute-start.47 = (bf16[512,1024]{1,0:T(8,128)(2,1)}, bf16[512,1024]{1,0:T(8,128)(2,1)S(1)}, u32[]{:S(2)}, u32[]{:S(2)}) collective-permute-start(bf16[512,1024]{1,0:T(8,128)(2,1)} %get-tuple-element.150), channel_id=1, source_target_pairs={{0,1},{1,0},{2,3},{3,2},{4,5},{5,4},{6,7},{7,6},{8,9},{9,8},{10,11... | collective-permute-start | bytes 3145736 | tf_op jit(solution)/shard_map/ppermute | solution.py:85
  346.3 28.8 %collective-permute-start.58 = (bf16[256,256]{1,0:T(8,128)(2,1)S(1)}, bf16[256,256]{1,0:T(8,128)(2,1)S(1)}, u32[]{:S(2)}, u32[]{:S(2)}) collective-permute-start(bf16[256,256]{1,0:T(8,128)(2,1)S(1)} %slice.326), channel_id=1, source_target_pairs={{0,8},{4,12},{8,0},{12,4},{16,24},{20,28},{24,16},{28,20},{1,9},{5... | collective-permute-start | bytes 393224 | tf_op jit(solution)/shard_map/ppermute | solution.py:90
  375.2 10.8 %collective-permute-start.68 = (bf16[128,256]{1,0:T(8,128)(2,1)S(1)}, bf16[128,256]{1,0:T(8,128)(2,1)S(1)}, u32[]{:S(2)}, u32[]{:S(2)}) collective-permute-start(bf16[128,256]{1,0:T(8,128)(2,1)S(1)} %slice.327), channel_id=1, source_target_pairs={{0,16},{4,20},{8,24},{12,28},{16,0},{20,4},{24,8},{28,12},{1,17},{... | collective-permute-start | bytes 196616 | tf_op jit(solution)/shard_map/ppermute | solution.py:90
  383.7 16.0 %collective-permute-start.49 = (bf16[256,1024]{1,0:T(8,128)(2,1)}, bf16[256,1024]{1,0:T(8,128)(2,1)S(1)}, u32[]{:S(2)}, u32[]{:S(2)}) collective-permute-start(bf16[256,1024]{1,0:T(8,128)(2,1)} %slice.318), channel_id=1, source_target_pairs={{0,8},{4,12},{8,0},{12,4},{16,24},{20,28},{24,16},{28,20},{1,9},{5... | collective-permute-start | bytes 1572872 | tf_op jit(solution)/shard_map/ppermute | solution.py:90
  384.5 8.1 %collective-permute-start.73 = (f32[12288]{0:T(1024)S(1)}, f32[12288]{0:T(1024)S(1)}, u32[]{:S(2)}, u32[]{:S(2)}) collective-permute-start(f32[12288]{0:T(1024)S(1)} %add.191), channel_id=1, source_target_pairs={{0,4},{4,0},{8,12},{12,8},{16,20},{20,16},{24,28},{28,24},{1,5},{5... | collective-permute-start | bytes 147464 | tf_op jit(solution)/shard_map/ppermute | solution.py:90
  386.7 32.2 %collective-permute-start.57 = (bf16[512,1024]{1,0:T(8,128)(2,1)}, bf16[512,1024]{1,0:T(8,128)(2,1)}, u32[]{:S(2)}, u32[]{:S(2)}) collective-permute-start(bf16[512,1024]{1,0:T(8,128)(2,1)} %get-tuple-element.165), channel_id=1, source_target_pairs={{0,1},{1,0},{2,3},{3,2},{4,5},{5,4},{6,7},{7,6},{8,9},{9,8},{10,11... | collective-permute-start | bytes 3145736 | tf_op jit(solution)/shard_map/ppermute | solution.py:85
  392.1 18.8 %collective-permute-start.60 = (bf16[1024,256]{1,0:T(8,128)(2,1)}, bf16[1024,256]{1,0:T(8,128)(2,1)S(1)}, u32[]{:S(2)}, u32[]{:S(2)}) collective-permute-start(bf16[1024,256]{1,0:T(8,128)(2,1)} %get-tuple-element.169), channel_id=1, source_target_pairs={{0,1},{1,0},{2,3},{3,2},{4,5},{5,4},{6,7},{7,6},{8,9},{9,8},{10,11... | collective-permute-start | bytes 1572872 | tf_op jit(solution)/shard_map/ppermute | solution.py:85
  396.1 15.7 %collective-permute-start.52 = (bf16[256,1024]{1,0:T(8,128)(2,1)S(1)}, bf16[256,1024]{1,0:T(8,128)(2,1)S(1)}, u32[]{:S(2)}, u32[]{:S(2)}) collective-permute-start(bf16[256,1024]{1,0:T(8,128)(2,1)S(1)} %slice.317), channel_id=1, source_target_pairs={{0,4},{4,0},{8,12},{12,8},{16,20},{20,16},{24,28},{28,24},{1,5},{5... | collective-permute-start | bytes 1572872 | tf_op jit(solution)/shard_map/ppermute | solution.py:90
  398.7 10.9 %collective-permute-start.75 = (f32[12288]{0:T(1024)S(1)}, f32[12288]{0:T(1024)S(1)}, u32[]{:S(2)}, u32[]{:S(2)}) collective-permute-start(f32[12288]{0:T(1024)S(1)} %add.193), channel_id=1, source_target_pairs={{0,16},{4,20},{8,24},{12,28},{16,0},{20,4},{24,8},{28,12},{1,17},{... | collective-permute-start | bytes 147464 | tf_op jit(solution)/shard_map/ppermute | solution.py:90
  400.7 32.1 %collective-permute-start.70 = (bf16[128,1024]{1,0:T(8,128)(2,1)}, bf16[128,1024]{1,0:T(8,128)(2,1)S(1)}, u32[]{:S(2)}, u32[]{:S(2)}) collective-permute-start(bf16[128,1024]{1,0:T(8,128)(2,1)} %slice.319), channel_id=1, source_target_pairs={{0,16},{4,20},{8,24},{12,28},{16,0},{20,4},{24,8},{28,12},{1,17},{... | collective-permute-start | bytes 786440 | tf_op jit(solution)/shard_map/ppermute | solution.py:90
  411.8 23.0 %collective-permute-start.61 = (bf16[512,256]{1,0:T(8,128)(2,1)}, bf16[512,256]{1,0:T(8,128)(2,1)S(1)}, u32[]{:S(2)}, u32[]{:S(2)}) collective-permute-start(bf16[512,256]{1,0:T(8,128)(2,1)} %slice.322), channel_id=1, source_target_pairs={{0,8},{4,12},{8,0},{12,4},{16,24},{20,28},{24,16},{28,20},{1,9},{5... | collective-permute-start | bytes 786440 | tf_op jit(solution)/shard_map/ppermute | solution.py:90
  431.9 18.4 %collective-permute-start.64 = (bf16[1024,512]{1,0:T(8,128)(2,1)}, bf16[1024,512]{1,0:T(8,128)(2,1)}, u32[]{:S(2)}, u32[]{:S(2)}) collective-permute-start(bf16[1024,512]{1,0:T(8,128)(2,1)} %get-tuple-element.175), channel_id=1, source_target_pairs={{0,1},{1,0},{2,3},{3,2},{4,5},{5,4},{6,7},{7,6},{8,9},{9,8},{10,11... | collective-permute-start | bytes 3145736 | tf_op jit(solution)/shard_map/ppermute | solution.py:85
  432.8 15.5 %collective-permute-start.69 = (bf16[128,1024]{1,0:T(8,128)(2,1)}, bf16[128,1024]{1,0:T(8,128)(2,1)}, u32[]{:S(2)}, u32[]{:S(2)}) collective-permute-start(bf16[128,1024]{1,0:T(8,128)(2,1)} %slice.320), channel_id=1, source_target_pairs={{0,16},{4,20},{8,24},{12,28},{16,0},{20,4},{24,8},{28,12},{1,17},{... | collective-permute-start | bytes 786440 | tf_op jit(solution)/shard_map/ppermute | solution.py:90
  433.9 23.2 %collective-permute-start.56 = (bf16[256,1024]{1,0:T(8,128)(2,1)}, bf16[256,1024]{1,0:T(8,128)(2,1)S(1)}, u32[]{:S(2)}, u32[]{:S(2)}) collective-permute-start(bf16[256,1024]{1,0:T(8,128)(2,1)} %get-tuple-element.161), channel_id=1, source_target_pairs={{0,2},{1,3},{2,0},{3,1},{4,6},{5,7},{6,4},{7,5},{8,10},{9,11},{10,... | collective-permute-start | bytes 1572872 | tf_op jit(solution)/shard_map/ppermute | solution.py:85
  434.9 15.2 %collective-permute-start.62 = (bf16[256,256]{1,0:T(8,128)(2,1)S(1)}, bf16[256,256]{1,0:T(8,128)(2,1)S(1)}, u32[]{:S(2)}, u32[]{:S(2)}) collective-permute-start(bf16[256,256]{1,0:T(8,128)(2,1)S(1)} %slice.325), channel_id=1, source_target_pairs={{0,4},{4,0},{8,12},{12,8},{16,20},{20,16},{24,28},{28,24},{1,5},{5... | collective-permute-start | bytes 393224 | tf_op jit(solution)/shard_map/ppermute | solution.py:90
  452.1 13.6 %collective-permute-start.65 = (bf16[512,512]{1,0:T(8,128)(2,1)S(1)}, bf16[512,512]{1,0:T(8,128)(2,1)S(1)}, u32[]{:S(2)}, u32[]{:S(2)}) collective-permute-start(bf16[512,512]{1,0:T(8,128)(2,1)S(1)} %slice.316), channel_id=1, source_target_pairs={{0,4},{4,0},{8,12},{12,8},{16,20},{20,16},{24,28},{28,24},{1,5},{5... | collective-permute-start | bytes 1572872 | tf_op jit(solution)/shard_map/ppermute | solution.py:90
  456.1 12.7 %collective-permute-start.59 = (bf16[256,1024]{1,0:T(8,128)(2,1)S(1)}, bf16[256,1024]{1,0:T(8,128)(2,1)S(1)}, u32[]{:S(2)}, u32[]{:S(2)}) collective-permute-start(bf16[256,1024]{1,0:T(8,128)(2,1)S(1)} %copy-done.81), channel_id=1, source_target_pairs={{0,2},{1,3},{2,0},{3,1},{4,6},{5,7},{6,4},{7,5},{8,10},{9,11},{10,... | collective-permute-start | bytes 1572872 | tf_op jit(solution)/shard_map/ppermute | solution.py:85
  465.9 7.3 %collective-permute-start.66 = (bf16[256,512]{1,0:T(8,128)(2,1)S(1)}, bf16[256,512]{1,0:T(8,128)(2,1)S(1)}, u32[]{:S(2)}, u32[]{:S(2)}) collective-permute-start(bf16[256,512]{1,0:T(8,128)(2,1)S(1)} %slice.321), channel_id=1, source_target_pairs={{0,8},{4,12},{8,0},{12,4},{16,24},{20,28},{24,16},{28,20},{1,9},{5... | collective-permute-start | bytes 786440 | tf_op jit(solution)/shard_map/ppermute | solution.py:90
  473.3 7.3 %collective-permute-start.67 = (bf16[128,512]{1,0:T(8,128)(2,1)S(1)}, bf16[128,512]{1,0:T(8,128)(2,1)S(1)}, u32[]{:S(2)}, u32[]{:S(2)}) collective-permute-start(bf16[128,512]{1,0:T(8,128)(2,1)S(1)} %slice.324), channel_id=1, source_target_pairs={{0,16},{4,20},{8,24},{12,28},{16,0},{20,4},{24,8},{28,12},{1,17},{... | collective-permute-start | bytes 393224 | tf_op jit(solution)/shard_map/ppermute | solution.py:90
  (94 other events, 864.2 us)

commit v4 on v3

--- a/solution.py
+++ b/solution.py
@@ -12,6 +12,7 @@
 MASKED = -1000000000.0
 MIB = 1024 * 1024
 VMEM_LIMIT = 56 * MIB
+SMALL_LIMIT = 16 * MIB
 UNDERSTATED = 1000
 
 F32 = jnp.float32
@@ -40,7 +41,7 @@
     return body
 
 
-def whole_call(kernel, outs, args, flops, name, scratch=(), deps=()):
+def whole_call(kernel, outs, args, flops, name, scratch=(), deps=(), limit=VMEM_LIMIT):
     moved = sum(math.prod(a.shape) * a.dtype.itemsize for a in (*args, *outs))
     return pl.pallas_call(
         after(kernel, len(args), deps),
@@ -49,7 +50,7 @@
         + [pl.BlockSpec(memory_space=pl.ANY)] * len(deps),
         out_specs=tuple([pl.BlockSpec(memory_space=pltpu.VMEM)] * len(outs)),
         scratch_shapes=list(scratch),
-        compiler_params=pltpu.CompilerParams(vmem_limit_bytes=VMEM_LIMIT),
+        compiler_params=pltpu.CompilerParams(vmem_limit_bytes=limit),
         cost_estimate=pl.CostEstimate(
             flops=flops // UNDERSTATED, bytes_accessed=moved // UNDERSTATED, transcendentals=0
         ),
@@ -164,9 +165,8 @@
     return order
 
 
-def scatter_dp(kept, got, bits):
-    arrivals = [got]
-    total = kept + got.astype(F32)
+def scatter_dp(total, bits):
+    arrivals = []
     for bit in bits:
         half = total.shape[0] // 2
         came = swap_dp(total[half:].astype(BF16), 1 << bit)
@@ -402,7 +402,7 @@
     return centred * back, back
 
 
-def first_norm(x_own, part, got, b_out, gain, shift):
+def first_norm(x_own, part, got, b_out, gain, shift, deps):
     dims = x_own.shape
 
     def kernel(x_ref, p_ref, r_ref, b_ref, g_ref, s_ref, summed_ref, normed_ref, low_ref):
@@ -415,7 +415,13 @@
 
     outs = [shape(dims, F32), shape(dims, F32), shape(dims, BF16)]
     return whole_call(
-        kernel, outs, [x_own, part, got, b_out, gain, shift], 20 * math.prod(dims), "first_norm"
+        kernel,
+        outs,
+        [x_own, part, got, b_out, gain, shift],
+        20 * math.prod(dims),
+        "first_norm",
+        deps=deps,
+        limit=SMALL_LIMIT,
     )
 
 
@@ -446,6 +452,7 @@
         [normed, part, got, cotangent, b_down, gain, shift],
         40 * math.prod(dims),
         "second_norm",
+        limit=SMALL_LIMIT,
     )
 
 
@@ -475,59 +482,74 @@
         40 * math.prod(dims),
         "first_norm_back",
         deps=deps,
-    )
-
-
-def feed_forward(n_own, n_across, w_mine, w_other, b_mine, b_other):
+        limit=SMALL_LIMIT,
+    )
+
+
+def feed_forward(n_own, n_far, weights, bias, prior, deps):
     block, width = n_own.shape
     rows = 2 * block
-    hidden = w_mine.shape[1] // 2
+    hidden = weights.shape[1] // 2
     tile = min(256, hidden)
     steps = hidden // tile
-
-    def kernel(
-        n0, n1, um, uo, dm, do, bm, bo,
-        am_ref, ao_ref, sm_ref, so_ref, own_ref, across_ref, tokens, acc,
-    ):
+    last = prior is not None
+
+    def kernel(n0, n1, u, d, b, *refs):
         step = pl.program_id(0)
+        if last:
+            before, a_ref, s_ref, own_ref, far_ref, tokens, acc = refs
+        else:
+            a_ref, s_ref, acc, tokens = refs
 
         @pl.when(step == 0)
         def _():
             tokens[:block] = n0[...]
             tokens[block:] = n1[...]
-            acc[...] = jnp.zeros_like(acc)
-
-        total = acc[...]
-        for u, d, b, a_ref, s_ref in ((um, dm, bm, am_ref, sm_ref), (uo, do, bo, ao_ref, so_ref)):
-            hid = dot(tokens[...], u[...]) + b[...]
-            half = 0.5 * (1.0 + lax.erf(hid * (1.0 / math.sqrt(2.0))))
-            bell = jnp.exp(hid * hid * -0.5) * (1.0 / math.sqrt(2.0 * math.pi))
-            active = (hid * half).astype(BF16)
-            a_ref[...] = active
-            s_ref[...] = (half + hid * bell).astype(BF16)
-            total = total + dot_nt(active, d[...])
-        acc[...] = total
-
-        @pl.when(step == steps - 1)
-        def _():
-            own_ref[...] = acc[:block]
-            across_ref[...] = acc[block:].astype(BF16)
+            acc[...] = before[...] if last else jnp.zeros_like(acc)
+
+        hid = dot(tokens[...], u[...]) + b[...]
+        half = 0.5 * (1.0 + lax.erf(hid * (1.0 / math.sqrt(2.0))))
+        bell = jnp.exp(hid * hid * -0.5) * (1.0 / math.sqrt(2.0 * math.pi))
+        active = (hid * half).astype(BF16)
+        a_ref[...] = active
+        s_ref[...] = (half + hid * bell).astype(BF16)
+        acc[...] += dot_nt(active, d[...])
+
+        if last:
+
+            @pl.when(step == steps - 1)
+            def _():
+                own_ref[...] = acc[:block]
+                far_ref[...] = acc[block:].astype(BF16)
 
     column = pl.BlockSpec((width, tile), lambda i: (0, i))
     later = pl.BlockSpec((width, tile), lambda i: (0, steps + i))
-    bias = pl.BlockSpec((1, tile), lambda i: (0, i))
     made = pl.BlockSpec((rows, tile), lambda i: (0, i))
-    outs = [shape((rows, hidden), BF16)] * 4 + [shape((block, width), F32), shape((block, width), BF16)]
+    args = [n_own, n_far, weights, weights, bias]
+    in_specs = [const_spec((block, width))] * 2
+    in_specs += [column, later, pl.BlockSpec((1, tile), lambda i: (0, i))]
+    outs = [shape((rows, hidden), BF16)] * 2
+    scratch = [pltpu.VMEM((rows, width), BF16)]
+    if last:
+        args.append(prior)
+        in_specs.append(const_spec((rows, width)))
+        outs += [shape((block, width), F32), shape((block, width), BF16)]
+        out_specs = [made] * 2 + [const_spec((block, width))] * 2
+        scratch.append(pltpu.VMEM((rows, width), F32))
+    else:
+        outs.append(shape((rows, width), F32))
+        out_specs = [made] * 2 + [const_spec((rows, width))]
     return streamed_call(
         kernel,
         (steps,),
         outs,
-        [made] * 4 + [const_spec((block, width))] * 2,
-        [n_own, n_across, w_mine, w_other, w_mine, w_other, b_mine, b_other],
-        [const_spec((block, width))] * 2 + [column] * 2 + [later] * 2 + [bias] * 2,
-        2 * 2 * rows * width * 2 * hidden,
+        out_specs,
+        args,
+        in_specs,
+        2 * 2 * rows * width * hidden,
         "feed_forward",
-        [pltpu.VMEM((rows, width), BF16), pltpu.VMEM((rows, width), F32)],
+        scratch,
+        deps,
     )
 
 
@@ -585,7 +607,9 @@
     )
 
 
-def weight_grad(ones, mine, other, dp_place, bits, count, name, other_first=0, deps=()):
+def weight_grad(
+    ones, mine, other, dp_place, bits, count, name, other_first=0, deps=(), other_kind=BF16
+):
     block, width = ones[0].shape
     rows = 2 * block
     tile = min(256, count)
@@ -615,7 +639,7 @@
     return streamed_call(
         kernel,
         (count // tile,),
-        [shape((width, count), F32), shape((width, count), BF16)],
+        [shape((width, count), F32), shape((width, count), other_kind)],
         [made] * 2,
         [dp_place, *ones, *mine, *other],
         [pl.BlockSpec(memory_space=pltpu.SMEM)] + [const_spec((block, width))] * 4 + [column] * 2 + [other_column] * 2,
@@ -626,8 +650,25 @@
     )
 
 
+def add_up(parts, deps):
+    def kernel(*refs):
+        refs[-1][...] = sum(ref[...] for ref in refs[:-1])
+
+    out = shape(parts[0].shape, F32)
+    return whole_call(kernel, [out], parts, 0, "add_up", deps=deps, limit=SMALL_LIMIT)[0]
+
+
 def reduced(made, bits):
-    return scatter_dp(made[0], swap_tensor(made[1], CORE), bits)
+    got = swap_tensor(made[1], CORE)
+    total, arrivals = scatter_dp(made[0] + got.astype(F32), bits)
+    return total, [got, *arrivals]
+
+
+def reduced_across(made, bits):
+    mine, mine_came = scatter_dp(made[0], bits)
+    other, other_came = scatter_dp(made[1], bits)
+    total = mine + swap_tensor(other.astype(BF16), ACROSS).astype(F32)
+    return total, mine_came, other_came
 
 
 def shards(
@@ -666,24 +707,32 @@
     dp_place = lax.axis_index("dp").astype(jnp.int32).reshape(1)
     att_far = gather_far(pack([w_query, w_key, w_value, w_out.T], "pack_attention"))
     att_pieces = att_far + gather_near(att_far)
-    ffw_far = gather_far(pack([w_up, w_down.T], "pack_feed", [p for p, _ in att_far[1:2]]))
-    ffw_near = gather_near(ffw_far)
-    ffw_pieces = ffw_far + ffw_near
-    started = [p for p, _ in ffw_far[1:2]] + x_across
-    att_mine = assemble(att_pieces, dp_place, "assemble_attention", started)
+    share = pack([w_up, w_down.T], "pack_feed", [p for p, _ in att_far[1:2]])
+    share_other = swap_tensor(share, ACROSS)
+    mine_far = gather_far(share)
+    mine_near = gather_near(mine_far)
+    other_far = gather_far(share_other)
+    other_near = gather_near(other_far)
+
+    def arrays(pieces):
+        return [p for p, _ in pieces]
+
+    att_mine = assemble(att_pieces, dp_place, "assemble_attention", arrays(mine_far[1:2]))
     att_other = assemble(
-        other_core(att_pieces), dp_place, "assemble_attention_other", [p for p, _ in ffw_far[2:3]]
-    )
-    ffw_mine = assemble(ffw_pieces, dp_place, "assemble_feed")
-    ffw_other = assemble(other_core(ffw_pieces), dp_place, "assemble_feed_other")
-    project_waits = [[], [p for p, _ in ffw_near[:1]]]
-    waits = [[p for p, _ in ffw_far[3:]], [p for p, _ in ffw_near[1:2]]]
-
-    biases = jnp.concatenate([b_query, jnp.zeros_like(b_query), b_value, b_up])
-    biases_other = swap_tensor(biases, CORE)
-    qkv_bias_mine, up_bias_mine = row(biases[: 3 * head_dims]), row(biases[3 * head_dims :])
-    qkv_bias_other = row(biases_other[: 3 * head_dims])
-    up_bias_other = row(biases_other[3 * head_dims :])
+        other_core(att_pieces), dp_place, "assemble_attention_other",
+        x_across + arrays(mine_far[2:3]),
+    )
+    project_waits = [[], arrays(mine_far[3:] + mine_near[:1])]
+    attend_waits = [
+        arrays(mine_near[1:2] + other_far[1:2]),
+        arrays(mine_near[2:3] + other_far[2:3]),
+    ]
+    norm_waits = [arrays(mine_near[3:] + other_far[3:]), arrays(other_near[:1])]
+    ffw_mine = assemble(mine_far + mine_near, dp_place, "assemble_feed")
+
+    biases = jnp.concatenate([b_query, jnp.zeros_like(b_query), b_value])
+    qkv_bias_mine, qkv_bias_other = row(biases), row(swap_tensor(biases, CORE))
+    up_bias_mine, up_bias_other = row(b_up), row(swap_tensor(b_up, ACROSS))
     b_out_row, b_down_row = row(b_out), row(b_down)
     gain_one, shift_one = row(first_gain), row(first_shift)
     gain_two, shift_two = row(second_gain), row(second_shift)
@@ -703,42 +752,50 @@
     attended = [
         attention_forward(
             projected[s][0], projected[s][1], far[s], masks[s].reshape(1, seq_len),
-            att_mine, att_other, head_size, waits[s] if s < 2 else [],
+            att_mine, att_other, head_size, attend_waits[s] if s < 2 else [],
         )
         for s in seqs
     ]
     attended_got = [swap_tensor(attended[s][3], ACROSS) for s in seqs]
     one = [
-        first_norm(x_own[s], attended[s][2], attended_got[s], b_out_row, gain_one, shift_one)
+        first_norm(
+            x_own[s], attended[s][2], attended_got[s], b_out_row, gain_one, shift_one,
+            norm_waits[s] if s < 2 else [],
+        )
         for s in seqs
     ]
-    normed_across = [swap_tensor(one[s][2], ACROSS) for s in seqs]
-    fed = [
-        feed_forward(
-            one[s][2], normed_across[s], ffw_mine, ffw_other, up_bias_mine, up_bias_other,
-        )
+    normed_far = [swap_tensor(one[s][2], CORE) for s in seqs]
+    fed_one = [
+        feed_forward(one[s][2], normed_far[s], ffw_mine, up_bias_mine, None, []) for s in seqs
+    ]
+    ffw_other = assemble(
+        other_far + other_near, dp_place, "assemble_feed_other", [fed_one[-1][2]]
+    )
+    fed_two = [
+        feed_forward(one[s][2], normed_far[s], ffw_other, up_bias_other, fed_one[s][2], [])
         for s in seqs
     ]
-    branch_got = [swap_tensor(fed[s][5], ACROSS) for s in seqs]
+    fed = [(fed_one[s][0], fed_two[s][0], fed_one[s][1], fed_two[s][1], *fed_two[s][2:]) for s in seqs]
+    branch_got = [swap_tensor(fed[s][5], CORE) for s in seqs]
     two = [
         second_norm(
             one[s][1], fed[s][4], branch_got[s], cotangent[s], b_down_row, gain_two, shift_two
         )
         for s in seqs
     ]
-    grad_across = [swap_tensor(two[s][2], ACROSS) for s in seqs]
+    grad_far = [swap_tensor(two[s][2], CORE) for s in seqs]
     fed_back = [
         feed_forward_back(
-            two[s][2], grad_across[s], ffw_mine, ffw_other, fed[s][2], fed[s][3]
+            two[s][2], grad_far[s], ffw_mine, ffw_other, fed[s][2], fed[s][3]
         )
         for s in seqs
     ]
-    back_got = [swap_tensor(fed_back[s][3], ACROSS) for s in seqs]
-    def placed_in(part_mine, part_other):
+    back_got = [swap_tensor(fed_back[s][3], CORE) for s in seqs]
+    def placed_in(part_mine, part_other, bit):
         size = part_mine.shape[0]
         empty = jnp.zeros((tensor_size * size,), F32)
         empty = lax.dynamic_update_slice(empty, part_mine, (place * size,))
-        return lax.dynamic_update_slice(empty, part_other, ((place ^ CORE) * size,))
+        return lax.dynamic_update_slice(empty, part_other, ((place ^ bit) * size,))
 
     levels = range(lax.axis_size("dp").bit_length() - 1)
     near_first = list(levels)
@@ -753,19 +810,19 @@
         )
 
     down_made = weight_grad(
-        pairs([two[s][2] for s in seqs], grad_across),
+        pairs([two[s][2] for s in seqs], grad_far),
         [fed[s][0] for s in seqs], [fed[s][1] for s in seqs],
-        dp_place, near_first, hidden, "w_down_grad", deps=[fed_back[-1][2]],
+        dp_place, near_first, hidden, "w_down_grad", deps=[fed_back[-1][2]], other_kind=F32,
     )
     one_back = [norm_back(s, [down_made[1]]) for s in seqs]
     up_made = weight_grad(
-        pairs([one[s][2] for s in seqs], normed_across),
+        pairs([one[s][2] for s in seqs], normed_far),
         [fed_back[s][0] for s in seqs], [fed_back[s][1] for s in seqs],
-        dp_place, far_first, hidden, "w_up_grad", deps=[one_back[s][1] for s in seqs],
+        dp_place, far_first, hidden, "w_up_grad", deps=[one_back[s][1] for s in seqs], other_kind=F32,
     )
     first_across = [swap_tensor(one_back[s][1], ACROSS) for s in seqs]
-    down_grad, down_came = reduced(down_made, near_first)
-    up_grad, up_came = reduced(up_made, far_first)
+    down_grad, down_mine_came, down_other_came = reduced_across(down_made, near_first)
+    up_grad, up_mine_came, up_other_came = reduced_across(up_made, far_first)
 
     def backward(s, deps):
         return attention_backward(
@@ -773,7 +830,7 @@
             one_back[s][1], first_across[s], att_mine, att_other, head_size, deps,
         )
 
-    attended_back = [backward(0, [down_came[0], up_made[1]])]
+    attended_back = [backward(0, [up_made[1]])]
     out_grad, out_came = reduced(
         weight_grad(
             pairs([one_back[s][1] for s in seqs], first_across),
@@ -783,12 +840,14 @@
         near_first,
     )
 
-    attended_back += [backward(s, [down_came[1], up_came[1], out_came[0]]) for s in seqs[1:]]
+    attended_back += [
+        backward(s, [down_mine_came[0], up_mine_came[0], out_came[0]]) for s in seqs[1:]
+    ]
     far_back = [swap_tensor(attended_back[s][2], CORE) for s in seqs]
     back = [
         project_back(
             attended_back[s][0], attended_back[s][1], far_back[s], att_mine, att_other,
-            [down_came[2], up_came[2], out_came[1]] if s == 0 else [out_came[2]],
+            [c[-2] for c in (down_mine_came, up_mine_came)] if s == 0 else [],
         )
         for s in seqs
     ]
@@ -801,13 +860,11 @@
     )
     tokens = pairs(x_own, x_across)
     grad_queries = [attended_back[s][0] for s in seqs]
-    query_grad, _ = reduced(
-        weight_grad(
-            tokens, grad_queries, grad_queries, dp_place, far_first, head_dims, "w_query_grad",
-            head_dims, [far_back[0]],
-        ),
-        far_first,
-    )
+    query_made = weight_grad(
+        tokens, grad_queries, grad_queries, dp_place, far_first, head_dims, "w_query_grad",
+        head_dims, [far_back[0], down_other_came[0], up_other_came[0]],
+    )
+    query_grad, _ = reduced(query_made, far_first)
     both_grad, _ = reduced(
         weight_grad(
             tokens, [back[s][0] for s in seqs], [back[s][1] for s in seqs],
@@ -816,7 +873,7 @@
         near_first,
     )
 
-    sums = sum(attended_back[s][3] for s in seqs)
+    sums = add_up([attended_back[s][3] for s in seqs], [query_made[1]])
     small = sum_all(
         jnp.concatenate(
             [
@@ -825,9 +882,10 @@
                 placed_in(
                     sum(fed_back[s][4] for s in seqs).reshape(-1),
                     sum(fed_back[s][5] for s in seqs).reshape(-1),
+                    ACROSS,
                 ),
-                placed_in(sums[0, :head_dims], sums[1, :head_dims]),
-                placed_in(sums[0, head_dims:], sums[1, head_dims:]),
+                placed_in(sums[0, :head_dims], sums[1, :head_dims], CORE),
+                placed_in(sums[0, head_dims:], sums[1, head_dims:], CORE),
             ]
         )
     )

time: 487 us -> 504 us (1.035)
  starting transfers between devices: 61.7 us -> 75.2 us
    pallas_call x16 -> x17, Pallas kernels: 128 us -> 111 us  [whole_call(): pl.pallas_call(after(kernel, len(args), deps), out_shape=tuple(outs), in_...]
    ppermute x32 -> x45, starting transfers between devices: 40.9 us -> 57.3 us  [swap_dp(): return lax.ppermute(array, 'dp', [(i, i ^ bit) for i in range(size)])]
    ppermute x44 -> x38, waiting for transfers between devices: 31.9 us -> 16.3 us  [swap_tensor(): return lax.ppermute(array, 'tensor', [(i, i ^ bit) for i in range(size)])]
    ppermute x32 -> x45, waiting for transfers between devices: 98.3 us -> 112 us  [swap_dp(): return lax.ppermute(array, 'dp', [(i, i ^ bit) for i in range(size)])]
    pallas_call x9 -> x11, Pallas kernels: 83.4 us -> 96.3 us  [streamed_call(): pl.pallas_call(after(kernel, len(args), deps), grid=grid, out_shape=tuple...]
    slice x15 -> x21, local copies, waits for them, and re-layouts: 5.83 us -> 16.6 us  [scatter_dp(): came = swap_dp(total[half:].astype(BF16), 1 << bit)]
    add x6 -> x4, other arithmetic: 8.28 us -> 2.53 us  [the longest x3 1.64 us: reduced(): total, arrivals = scatter_dp(made[0] + got.astype(F32), bits)]
    add x13 -> x16, other arithmetic: 7 us -> 12 us  [scatter_dp(): total = total[:half] + came.astype(F32)]
  transfers between devices with their start and end apart: 76 -> 83, of which waited for: 23 -> 22; matrix products, arithmetic and copies ran while one was open for 8% -> 11% of each run, Pallas kernels for 45% -> 42%
where the time goes in v4:
time: 504 us; the launch traced here: 497 us
  Pallas kernels  222 us (44%)
  waiting for transfers between devices  128 us (25%)
  starting transfers between devices  75.2 us (15%)
  local copies, waits for them, and re-layouts  46.6 us (9%)
  other arithmetic  23.3 us (5%)
    ppermute x45, waiting for transfers between devices, swap_dp(): return lax.ppermute(array, 'dp', [(i, i ^ bit) for i in range(size)])  112 us
    pallas_call x17, Pallas kernels, whole_call(): pl.pallas_call(after(kernel, len(args), deps), out_shape=tuple(outs), in_...  111 us
    pallas_call x11, Pallas kernels, streamed_call(): pl.pallas_call(after(kernel, len(args), deps), grid=grid, out_shape=tuple...  96.3 us
    ppermute x45, starting transfers between devices, swap_dp(): return lax.ppermute(array, 'dp', [(i, i ^ bit) for i in range(size)])  57.3 us
    unnamed x200, local copies, waits for them, and re-layouts  23.5 us
    ppermute x38, starting transfers between devices, swap_tensor(): return lax.ppermute(array, 'tensor', [(i, i ^ bit) for i in range(size)])  17.9 us
    slice x21, local copies, waits for them, and re-layouts, scatter_dp(): came = swap_dp(total[half:].astype(BF16), 1 << bit)  16.6 us
    ppermute x38, waiting for transfers between devices, swap_tensor(): return lax.ppermute(array, 'tensor', [(i, i ^ bit) for i in range(size)])  16.3 us
  transfers between devices with their start and end apart: 83, of which 22 were waited for; matrix products, arithmetic and copies ran while one was open for 11% of the time, Pallas kernels for 42%

profile of v4, /device:TPU:0, one launch (start us, length us, event | category | flops | bytes accessed | tf_op | source)
XLA Modules:
  0.0 497.5 jit_solution(11626814902578455185)
XLA Ops:
  2.3 1.7 pack_attention.1.refs_1_
  3.9 4.0 collective-permute-start.1
  15.7 4.6 collective-permute-done.1.refs_2_
  23.4 1.9 copy.40
  25.3 1.9 pack_feed.1.refs_1_
  27.1 2.0 collective-permute-done.3.refs_4_
  31.3 3.3 collective-permute-start.8
  34.6 1.9 collective-permute-done.17.refs_10_.refs_1_.refs_4_
  39.0 13.7 %collective-permute-done.18.refs_11_.refs_3_ = bf16[128,2048]{1,0:T(8,128)(2,1)S(1)} collective-permute-done((bf16[128,2048]{1,0:T(8,128)(2,1)}, bf16[128,2048]{1,0:T(8,128)(2,1)S(1)}, u32[]{:S(2)}, u32[]{:S(2)}) %collective-permute-start.18) | collective-permute-done | bytes 524320 | tf_op jit(solution)/shard_map/ppermute | solution.py:91
  54.2 2.5 collective-permute-start.34
  59.0 3.0 assemble_attention.1.refs_2_.refs_4_.refs_6_.refs_3_
  62.1 3.0 assemble_attention_other.1.refs_3_.refs_5_.refs_7_.refs_4_
  65.1 5.6 %project_inputs.2 = (bf16[512,768]{1,0:T(8,128)(2,1)}, bf16[512,768]{1,0:T(8,128)(2,1)}, bf16[512,1024]{1,0:T(8,128)(2,1)}) custom-call(bf16[256,1024]{1,0:T(8,128)(2,1)} %copy-done.4, bf16[256,1024]{1,0:T(8,128)(2,1)} %copy-done.41, bf16[1024,1024]{1,0:T(8,128)(2,1)} %assemble_attention.1.refs_2_.refs_4_.refs_6_.refs_3_, ...), custom_call_target="tpu_custom_call" | custom-call | flops 1610612 | bytes 7870 | tf_op jit(solution)/shard_map/project_inputs/pallas_call | solution.py:46
  70.7 3.1 collective-permute-start.23
  74.7 5.6 %project_inputs.3 = (bf16[512,768]{1,0:T(8,128)(2,1)}, bf16[512,768]{1,0:T(8,128)(2,1)}, bf16[512,1024]{1,0:T(8,128)(2,1)}) custom-call(bf16[256,1024]{1,0:T(8,128)(2,1)} %copy-done.2, bf16[256,1024]{1,0:T(8,128)(2,1)} %copy-done.40, bf16[1024,1024]{1,0:T(8,128)(2,1)} %assemble_attention.1.refs_2_.refs_4_.refs_6_.refs_3_, ...), custom_call_target="tpu_custom_call" | custom-call | flops 1610612 | bytes 7870 | tf_op jit(solution)/shard_map/project_inputs/pallas_call | solution.py:46
  82.4 15.5 %collective-permute-done.23.refs_7_.refs_2_ = bf16[128,2048]{1,0:T(8,128)(2,1)} collective-permute-done((bf16[128,2048]{1,0:T(8,128)(2,1)}, bf16[128,2048]{1,0:T(8,128)(2,1)}, u32[]{:S(2)}, u32[]{:S(2)}) %collective-permute-start.23) | collective-permute-done | bytes 524320 | tf_op jit(solution)/shard_map/ppermute | solution.py:91
  101.1 2.0 collective-permute-start.27
  103.1 12.9 %attention_forward.2 = (bf16[512,256]{1,0:T(8,128)(2,1)}, bf16[512,256]{1,0:T(8,128)(2,1)}, f32[256,1024]{1,0:T(8,128)}, bf16[256,1024]{1,0:T(8,128)(2,1)}) custom-call(bf16[512,768]{1,0:T(8,128)(2,1)} %get-tuple-element.103.refs_0_, bf16[512,768]{1,0:T(8,128)(2,1)} %get-tuple-element.104.refs_1_, bf16[512,1024]{1,0:T(8,128)(2,1)} %copy-done.47, ...), custom_call_target="tpu_custom_call" | custom-call | flops 8589934 | bytes 8916 | tf_op jit(solution)/shard_map/attention_forward/pallas_call | solution.py:46
  120.7 12.8 %attention_forward.3 = (bf16[512,256]{1,0:T(8,128)(2,1)}, bf16[512,256]{1,0:T(8,128)(2,1)}, f32[256,1024]{1,0:T(8,128)}, bf16[256,1024]{1,0:T(8,128)(2,1)}) custom-call(bf16[512,768]{1,0:T(8,128)(2,1)} %get-tuple-element.110.refs_0_, bf16[512,768]{1,0:T(8,128)(2,1)} %get-tuple-element.111.refs_1_, bf16[512,1024]{1,0:T(8,128)(2,1)} %copy-done.48, ...), custom_call_target="tpu_custom_call" | custom-call | flops 8589934 | bytes 8916 | tf_op jit(solution)/shard_map/attention_forward/pallas_call | solution.py:46
  135.6 10.3 %collective-permute-done.37.refs_2_ = bf16[256,1024]{1,0:T(8,128)(2,1)S(1)} collective-permute-done((bf16[256,1024]{1,0:T(8,128)(2,1)}, bf16[256,1024]{1,0:T(8,128)(2,1)S(1)}, u32[]{:S(2)}, u32[]{:S(2)}) %collective-permute-start.37) | collective-permute-done | bytes 524320 | tf_op jit(solution)/shard_map/ppermute | solution.py:86
  150.5 4.4 assemble_feed.1.refs_2_.refs_3_.refs_4_
  154.9 8.8 %feed_forward.5 = (bf16[512,1024]{1,0:T(8,128)(2,1)}, bf16[512,1024]{1,0:T(8,128)(2,1)}, f32[512,1024]{1,0:T(8,128)}) custom-call(bf16[256,1024]{1,0:T(8,128)(2,1)} %copy-done.7, bf16[256,1024]{1,0:T(8,128)(2,1)} %copy-done.45, bf16[1024,2048]{1,0:T(8,128)(2,1)} %assemble_feed.1.refs_2_.refs_3_.refs_4_, ...), custom_call_target="tpu_custom_call" | custom-call | flops 2147483 | bytes 13635 | tf_op jit(solution)/shard_map/feed_forward/pallas_call | solution.py:63
  164.5 8.9 %feed_forward.4 = (bf16[512,1024]{1,0:T(8,128)(2,1)}, bf16[512,1024]{1,0:T(8,128)(2,1)}, f32[512,1024]{1,0:T(8,128)}) custom-call(bf16[256,1024]{1,0:T(8,128)(2,1)} %copy-done.8, bf16[256,1024]{1,0:T(8,128)(2,1)} %copy-done.46, bf16[1024,2048]{1,0:T(8,128)(2,1)} %assemble_feed.1.refs_2_.refs_3_.refs_4_, ...), custom_call_target="tpu_custom_call" | custom-call | flops 2147483 | bytes 13635 | tf_op jit(solution)/shard_map/feed_forward/pallas_call | solution.py:63
  173.5 10.1 %collective-permute-done.33.refs_8_ = bf16[128,2048]{1,0:T(8,128)(2,1)S(1)} collective-permute-done((bf16[128,2048]{1,0:T(8,128)(2,1)S(1)}, bf16[128,2048]{1,0:T(8,128)(2,1)S(1)}, u32[]{:S(2)}, u32[]{:S(2)}) %collective-permute-start.33) | collective-permute-done | bytes 524320 | tf_op jit(solution)/shard_map/ppermute | solution.py:91
  184.4 4.5 assemble_feed_other.1.refs_2_.refs_3_.refs_5_
  189.5 9.7 %feed_forward.6 = (bf16[512,1024]{1,0:T(8,128)(2,1)}, bf16[512,1024]{1,0:T(8,128)(2,1)}, f32[256,1024]{1,0:T(8,128)}, bf16[256,1024]{1,0:T(8,128)(2,1)}) custom-call(bf16[256,1024]{1,0:T(8,128)(2,1)} %copy-done.7, bf16[256,1024]{1,0:T(8,128)(2,1)} %copy-done.45, bf16[1024,2048]{1,0:T(8,128)(2,1)} %assemble_feed_other.1.refs_2_.refs_3_.refs_5_, ...), custom_call_target="tpu_custom_call" | custom-call | flops 2147483 | bytes 15208 | tf_op jit(solution)/shard_map/feed_forward/pallas_call | solution.py:63
  199.3 10.2 %feed_forward.7 = (bf16[512,1024]{1,0:T(8,128)(2,1)}, bf16[512,1024]{1,0:T(8,128)(2,1)}, f32[256,1024]{1,0:T(8,128)}, bf16[256,1024]{1,0:T(8,128)(2,1)}) custom-call(bf16[256,1024]{1,0:T(8,128)(2,1)} %copy-done.8, bf16[256,1024]{1,0:T(8,128)(2,1)} %copy-done.46, bf16[1024,2048]{1,0:T(8,128)(2,1)} %assemble_feed_other.1.refs_2_.refs_3_.refs_5_, ...), custom_call_target="tpu_custom_call" | custom-call | flops 2147483 | bytes 15208 | tf_op jit(solution)/shard_map/feed_forward/pallas_call | solution.py:63
  216.4 11.5 %feed_forward_back.2 = (bf16[512,1024]{1,0:T(8,128)(2,1)}, bf16[512,1024]{1,0:T(8,128)(2,1)}, f32[256,1024]{1,0:T(8,128)}, bf16[256,1024]{1,0:T(8,128)(2,1)}, f32[1,1024]{1,0:T(1,128)}, /*index=5*/f32[1,1024]{1,0:T(1,128)}) custom-call(bf16[256,1024]{1,0:T(8,128)(2,1)} %copy-done.12, bf16[256,1024]{1,0:T(8,128)(2,1)} %copy-done.64, ...), custom_call_target="tpu_custom_call" | custom-call | flops 4294967 | bytes 23601 | tf_op jit(solution)/shard_map/feed_forward_back/pallas_call | solution.py:63
  229.1 11.4 %feed_forward_back.3 = (bf16[512,1024]{1,0:T(8,128)(2,1)}, bf16[512,1024]{1,0:T(8,128)(2,1)}, f32[256,1024]{1,0:T(8,128)}, bf16[256,1024]{1,0:T(8,128)(2,1)}, f32[1,1024]{1,0:T(1,128)}, /*index=5*/f32[1,1024]{1,0:T(1,128)}) custom-call(bf16[256,1024]{1,0:T(8,128)(2,1)} %copy-done.13, bf16[256,1024]{1,0:T(8,128)(2,1)} %copy-done.65, ...), custom_call_target="tpu_custom_call" | custom-call | flops 4294967 | bytes 23601 | tf_op jit(solution)/shard_map/feed_forward_back/pallas_call | solution.py:63
  240.7 10.3 %w_down_grad.1 = (f32[1024,1024]{1,0:T(8,128)}, f32[1024,1024]{1,0:T(8,128)}) custom-call(s32[1]{0:T(128)} %bitcast.1.refs_0_, bf16[256,1024]{1,0:T(8,128)(2,1)} %copy-done.12, bf16[256,1024]{1,0:T(8,128)(2,1)} %copy-done.64, bf16[256,1024]{1,0:T(8,128)(2,1)} %copy-done.13, bf16[256,1024]{1,0:T(8,128)(2,1)} %copy-done.65, ...), custom_call_target="tpu_custom_call" | custom-call | flops 4294967 | bytes 14680 | tf_op jit(solution)/shard_map/w_down_grad/pallas_call | solution.py:63
  251.1 2.9 slice.385
  254.5 2.7 slice.387
  266.8 2.3 pad_maximum_fusion
  269.7 10.1 %w_up_grad.1 = (f32[1024,1024]{1,0:T(8,128)}, f32[1024,1024]{1,0:T(8,128)}) custom-call(s32[1]{0:T(128)} %bitcast.1.refs_0_, bf16[256,1024]{1,0:T(8,128)(2,1)} %copy-done.7, bf16[256,1024]{1,0:T(8,128)(2,1)} %copy-done.45, bf16[256,1024]{1,0:T(8,128)(2,1)} %copy-done.8, bf16[256,1024]{1,0:T(8,128)(2,1)} %copy-done.46, ...), custom_call_target="tpu_custom_call" | custom-call | flops 4294967 | bytes 14680 | tf_op jit(solution)/shard_map/w_up_grad/pallas_call | solution.py:63
  279.8 2.7 slice.386
  283.8 2.7 slice.384
  287.4 26.5 %attention_backward.2 = (bf16[512,512]{1,0:T(8,128)(2,1)}, f32[512,1024]{1,0:T(8,128)}, bf16[512,1024]{1,0:T(8,128)(2,1)}, f32[2,512]{1,0:T(2,128)}) custom-call(bf16[512,768]{1,0:T(8,128)(2,1)} %get-tuple-element.103.refs_0_, bf16[512,768]{1,0:T(8,128)(2,1)} %get-tuple-element.104.refs_1_, bf16[512,1024]{1,0:T(8,128)(2,1)} %copy-done.47, ...), custom_call_target="tpu_custom_call" | custom-call | flops 10737418 | bytes 11542 | tf_op jit(solution)/shard_map/attention_backward/pallas_call | solution.py:46
  313.9 4.3 w_out_grad.1
  318.7 1.8 convert_add_fusion
  321.9 1.7 convert_add_fusion.4
  324.8 17.8 %collective-permute-done.75 = bf16[256,1024]{1,0:T(8,128)(2,1)S(1)} collective-permute-done((bf16[256,1024]{1,0:T(8,128)(2,1)S(1)}, bf16[256,1024]{1,0:T(8,128)(2,1)S(1)}, u32[]{:S(2)}, u32[]{:S(2)}) %collective-permute-start.75) | collective-permute-done | bytes 524320 | tf_op jit(solution)/shard_map/ppermute | solution.py:91
  343.9 8.0 %collective-permute-done.49.refs_5_ = bf16[256,1024]{1,0:T(8,128)(2,1)S(1)} collective-permute-done((bf16[256,1024]{1,0:T(8,128)(2,1)S(1)}, bf16[256,1024]{1,0:T(8,128)(2,1)S(1)}, u32[]{:S(2)}, u32[]{:S(2)}) %collective-permute-start.49) | collective-permute-done | bytes 524320 | tf_op jit(solution)/shard_map/ppermute | solution.py:91
  352.0 1.7 collective-permute-start.76
  356.1 1.8 convert_add_fusion.1
  360.9 1.7 convert_add_fusion.3
  364.8 26.4 %attention_backward.3 = (bf16[512,512]{1,0:T(8,128)(2,1)}, f32[512,1024]{1,0:T(8,128)}, bf16[512,1024]{1,0:T(8,128)(2,1)}, f32[2,512]{1,0:T(2,128)}) custom-call(bf16[512,768]{1,0:T(8,128)(2,1)} %get-tuple-element.110.refs_0_, bf16[512,768]{1,0:T(8,128)(2,1)} %get-tuple-element.111.refs_1_, bf16[512,1024]{1,0:T(8,128)(2,1)} %copy-done.48, ...), custom_call_target="tpu_custom_call" | custom-call | flops 10737418 | bytes 11542 | tf_op jit(solution)/shard_map/attention_backward/pallas_call | solution.py:46
  391.2 1.6 collective-permute-start.51
  394.7 4.3 w_query_grad.1
  404.2 2.8 collective-permute-done.79
  409.6 2.0 collective-permute-done.80
  413.0 2.2 slice_add_fusion.3
  415.9 1.7 collective-permute-start.72
  422.0 1.8 collective-permute-start.70
  423.8 6.2 %project_back.2 = (bf16[512,512]{1,0:T(8,128)(2,1)}, bf16[512,512]{1,0:T(8,128)(2,1)}, f32[256,1024]{1,0:T(8,128)}, bf16[256,1024]{1,0:T(8,128)(2,1)}) custom-call(bf16[512,512]{1,0:T(8,128)(2,1)} %get-tuple-element.152.refs_0_.refs_5_.refs_7_, f32[512,1024]{1,0:T(8,128)} %get-tuple-element.153.refs_1_, bf16[512,1024]{1,0:T(8,128)(2,1)} %copy-done.49, ...), custom_call_target="tpu_custom_call" | custom-call | flops 1610612 | bytes 10485 | tf_op jit(solution)/shard_map/project_back/pallas_call | solution.py:46
  430.0 8.8 %collective-permute-done.82 = f32[12288]{0:T(1024)S(1)} collective-permute-done((f32[12288]{0:T(1024)S(1)}, f32[12288]{0:T(1024)S(1)}, u32[]{:S(2)}, u32[]{:S(2)}) %collective-permute-start.82) | collective-permute-done | bytes 49184 | tf_op jit(solution)/shard_map/ppermute | solution.py:91
  441.7 6.2 %project_back.3 = (bf16[512,512]{1,0:T(8,128)(2,1)}, bf16[512,512]{1,0:T(8,128)(2,1)}, f32[256,1024]{1,0:T(8,128)}, bf16[256,1024]{1,0:T(8,128)(2,1)}) custom-call(bf16[512,512]{1,0:T(8,128)(2,1)} %get-tuple-element.166.refs_0_.refs_6_.refs_8_, f32[512,1024]{1,0:T(8,128)} %get-tuple-element.167.refs_1_, bf16[512,1024]{1,0:T(8,128)(2,1)} %collective-permute-done.55.refs_2_, ...), custom_call_target="tpu_custom_call" | custom-call | flops 1610612 | bytes 10485 | tf_op jit(solution)/shard_map/project_back/pallas_call | solution.py:46
  447.9 6.7 %w_key_value_grad.1 = (f32[1024,512]{1,0:T(8,128)}, bf16[1024,512]{1,0:T(8,128)(2,1)}) custom-call(s32[1]{0:T(128)} %bitcast.1.refs_0_, bf16[256,1024]{1,0:T(8,128)(2,1)} %copy-done.4, bf16[256,1024]{1,0:T(8,128)(2,1)} %copy-done.41, bf16[256,1024]{1,0:T(8,128)(2,1)} %copy-done.2, bf16[256,1024]{1,0:T(8,128)(2,1)} %copy-done.40, ...), custom_call_target="tpu_custom_call" | custom-call | flops 2147483 | bytes 7340 | tf_op jit(solution)/shard_map/w_key_value_grad/pallas_call | solution.py:63
  457.7 1.6 collective-permute-start.56
  459.6 6.4 %collective-permute-done.60 = bf16[512,256]{1,0:T(8,128)(2,1)S(1)} collective-permute-done((bf16[512,256]{1,0:T(8,128)(2,1)S(1)}, bf16[512,256]{1,0:T(8,128)(2,1)S(1)}, u32[]{:S(2)}, u32[]{:S(2)}) %collective-permute-start.60) | collective-permute-done | bytes 262176 | tf_op jit(solution)/shard_map/ppermute | solution.py:91
  468.6 3.9 collective-permute-done.61
  474.3 4.0 collective-permute-done.62
  478.9 3.1 collective-permute-done.64
  483.2 5.6 %collective-permute-done.65 = bf16[256,512]{1,0:T(8,128)(2,1)S(1)} collective-permute-done((bf16[256,512]{1,0:T(8,128)(2,1)S(1)}, bf16[256,512]{1,0:T(8,128)(2,1)S(1)}, u32[]{:S(2)}, u32[]{:S(2)}) %collective-permute-start.65) | collective-permute-done | bytes 262176 | tf_op jit(solution)/shard_map/ppermute | solution.py:91
  491.4 4.8 collective-permute-done.66
  (417 shorter events, 104.9 us)
Async XLA Ops:
  3.9 16.3 %collective-permute-start.1 = (bf16[128,1024]{1,0:T(8,128)(2,1)}, bf16[128,1024]{1,0:T(8,128)(2,1)S(1)}, u32[]{:S(2)}, u32[]{:S(2)}) collective-permute-start(bf16[128,1024]{1,0:T(8,128)(2,1)} %pack_attention.1.refs_1_), channel_id=1, source_target_pairs={{0,16},{4,20},{8,24},{12,28},{16,0},{20,4},{24,8},{28,12},{1,17},{... | collective-permute-start | bytes 786440 | tf_op jit(solution)/shard_map/ppermute | solution.py:91
  8.0 12.5 %collective-permute-start.2 = (bf16[128,1024]{1,0:T(8,128)(2,1)}, bf16[128,1024]{1,0:T(8,128)(2,1)S(1)}, u32[]{:S(2)}, u32[]{:S(2)}) collective-permute-start(bf16[128,1024]{1,0:T(8,128)(2,1)} %pack_attention.1.refs_1_), channel_id=1, source_target_pairs={{0,8},{4,12},{8,0},{12,4},{16,24},{20,28},{24,16},{28,20},{1,9},{5... | collective-permute-start | bytes 786440 | tf_op jit(solution)/shard_map/ppermute | solution.py:91
  9.5 12.3 %collective-permute-start.4 = (bf16[128,1024]{1,0:T(8,128)(2,1)}, bf16[128,1024]{1,0:T(8,128)(2,1)S(1)}, u32[]{:S(2)}, u32[]{:S(2)}) collective-permute-start(bf16[128,1024]{1,0:T(8,128)(2,1)} %pack_attention.1.refs_1_), channel_id=1, source_target_pairs={{0,4},{4,0},{8,12},{12,8},{16,20},{20,16},{24,28},{28,24},{1,5},{5... | collective-permute-start | bytes 786440 | tf_op jit(solution)/shard_map/ppermute | solution.py:91
  12.3 18.9 %collective-permute-start = (bf16[256,1024]{1,0:T(8,128)(2,1)S(1)}, bf16[256,1024]{1,0:T(8,128)(2,1)S(1)}, u32[]{:S(2)}, u32[]{:S(2)}) collective-permute-start(bf16[256,1024]{1,0:T(8,128)(2,1)S(1)} %get-tuple-element.225.refs_0_.refs_1_), channel_id=1, source_target_pairs={{0,2},{1,3},{2,0},{3,1},{4,6},{5,7},{6,4},{7,5},{8,10},{9,11},{10,... | collective-permute-start | bytes 1572872 | tf_op jit(solution)/shard_map/ppermute | solution.py:86
  15.2 21.3 %collective-permute-start.17 = (bf16[256,1024]{1,0:T(8,128)(2,1)S(1)}, bf16[256,1024]{1,0:T(8,128)(2,1)S(1)}, u32[]{:S(2)}, u32[]{:S(2)}) collective-permute-start(bf16[256,1024]{1,0:T(8,128)(2,1)S(1)} %get-tuple-element.226.refs_0_.refs_3_), channel_id=1, source_target_pairs={{0,2},{1,3},{2,0},{3,1},{4,6},{5,7},{6,4},{7,5},{8,10},{9,11},{10,... | collective-permute-start | bytes 1572872 | tf_op jit(solution)/shard_map/ppermute | solution.py:86
  20.4 8.7 %collective-permute-start.3 = (bf16[128,1024]{1,0:T(8,128)(2,1)S(1)}, bf16[128,1024]{1,0:T(8,128)(2,1)}, u32[]{:S(2)}, u32[]{:S(2)}) collective-permute-start(bf16[128,1024]{1,0:T(8,128)(2,1)S(1)} %collective-permute-done.1.refs_2_), channel_id=1, source_target_pairs={{0,8},{4,12},{8,0},{12,4},{16,24},{20,28},{24,16},{28,20},{1,9},{5... | collective-permute-start | bytes 786440 | tf_op jit(solution)/shard_map/ppermute | solution.py:91
  23.4 13.1 %collective-permute-start.10 = (bf16[128,1024]{1,0:T(8,128)(2,1)S(1)}, bf16[128,1024]{1,0:T(8,128)(2,1)}, u32[]{:S(2)}, u32[]{:S(2)}) collective-permute-start(bf16[128,1024]{1,0:T(8,128)(2,1)S(1)} %collective-permute-done.1.refs_2_), channel_id=1, source_target_pairs={{0,1},{1,0},{2,3},{3,2},{4,5},{5,4},{6,7},{7,6},{8,9},{9,8},{10,11... | collective-permute-start | bytes 786440 | tf_op jit(solution)/shard_map/ppermute | solution.py:86
  29.1 23.6 %collective-permute-start.18 = (bf16[128,2048]{1,0:T(8,128)(2,1)}, bf16[128,2048]{1,0:T(8,128)(2,1)S(1)}, u32[]{:S(2)}, u32[]{:S(2)}) collective-permute-start(bf16[128,2048]{1,0:T(8,128)(2,1)} %pack_feed.1.refs_1_), channel_id=1, source_target_pairs={{0,8},{4,12},{8,0},{12,4},{16,24},{20,28},{24,16},{28,20},{1,9},{5... | collective-permute-start | bytes 1572872 | tf_op jit(solution)/shard_map/ppermute | solution.py:91
  31.3 26.1 %collective-permute-start.8 = (bf16[128,2048]{1,0:T(8,128)(2,1)}, bf16[128,2048]{1,0:T(8,128)(2,1)}, u32[]{:S(2)}, u32[]{:S(2)}) collective-permute-start(bf16[128,2048]{1,0:T(8,128)(2,1)} %pack_feed.1.refs_1_), channel_id=1, source_target_pairs={{0,16},{4,20},{8,24},{12,28},{16,0},{20,4},{24,8},{28,12},{1,17},{... | collective-permute-start | bytes 1572872 | tf_op jit(solution)/shard_map/ppermute | solution.py:91
  37.0 17.2 %collective-permute-start.7 = (bf16[128,1024]{1,0:T(8,128)(2,1)}, bf16[128,1024]{1,0:T(8,128)(2,1)}, u32[]{:S(2)}, u32[]{:S(2)}) collective-permute-start(bf16[128,1024]{1,0:T(8,128)(2,1)} %collective-permute-done.3.refs_4_), channel_id=1, source_target_pairs={{0,4},{4,0},{8,12},{12,8},{16,20},{20,16},{24,28},{28,24},{1,5},{5... | collective-permute-start | bytes 786440 | tf_op jit(solution)/shard_map/ppermute | solution.py:91
  38.5 18.9 %collective-permute-start.12 = (bf16[128,1024]{1,0:T(8,128)(2,1)}, bf16[128,1024]{1,0:T(8,128)(2,1)}, u32[]{:S(2)}, u32[]{:S(2)}) collective-permute-start(bf16[128,1024]{1,0:T(8,128)(2,1)} %collective-permute-done.3.refs_4_), channel_id=1, source_target_pairs={{0,1},{1,0},{2,3},{3,2},{4,5},{5,4},{6,7},{7,6},{8,9},{9,8},{10,11... | collective-permute-start | bytes 786440 | tf_op jit(solution)/shard_map/ppermute | solution.py:86
  38.5 18.8 %collective-permute-start.14 = (bf16[128,1024]{1,0:T(8,128)(2,1)}, bf16[128,1024]{1,0:T(8,128)(2,1)}, u32[]{:S(2)}, u32[]{:S(2)}) collective-permute-start(bf16[128,1024]{1,0:T(8,128)(2,1)} %collective-permute-done.5.refs_6_), channel_id=1, source_target_pairs={{0,1},{1,0},{2,3},{3,2},{4,5},{5,4},{6,7},{7,6},{8,9},{9,8},{10,11... | collective-permute-start | bytes 786440 | tf_op jit(solution)/shard_map/ppermute | solution.py:86
  52.7 18.1 %collective-permute-start.22 = (bf16[128,2048]{1,0:T(8,128)(2,1)}, bf16[128,2048]{1,0:T(8,128)(2,1)}, u32[]{:S(2)}, u32[]{:S(2)}) collective-permute-start(bf16[128,2048]{1,0:T(8,128)(2,1)} %pack_feed.1.refs_1_), channel_id=1, source_target_pairs={{0,2},{1,3},{2,0},{3,1},{4,6},{5,7},{6,4},{7,5},{8,10},{9,11},{10,... | collective-permute-start | bytes 1572872 | tf_op jit(solution)/shard_map/ppermute | solution.py:86
  54.2 19.6 %collective-permute-start.34 = (bf16[128,2048]{1,0:T(8,128)(2,1)}, bf16[128,2048]{1,0:T(8,128)(2,1)S(1)}, u32[]{:S(2)}, u32[]{:S(2)}) collective-permute-start(bf16[128,2048]{1,0:T(8,128)(2,1)} %pack_feed.1.refs_1_), channel_id=1, source_target_pairs={{0,4},{4,0},{8,12},{12,8},{16,20},{20,16},{24,28},{28,24},{1,5},{5... | collective-permute-start | bytes 1572872 | tf_op jit(solution)/shard_map/ppermute | solution.py:91
  57.3 16.5 %collective-permute-start.25 = (bf16[128,2048]{1,0:T(8,128)(2,1)}, bf16[128,2048]{1,0:T(8,128)(2,1)}, u32[]{:S(2)}, u32[]{:S(2)}) collective-permute-start(bf16[128,2048]{1,0:T(8,128)(2,1)} %collective-permute-done.8.refs_9_.refs_2_), channel_id=1, source_target_pairs={{0,8},{4,12},{8,0},{12,4},{16,24},{20,28},{24,16},{28,20},{1,9},{5... | collective-permute-start | bytes 1572872 | tf_op jit(solution)/shard_map/ppermute | solution.py:91
  70.7 30.4 %collective-permute-start.20 = (bf16[512,1024]{1,0:T(8,128)(2,1)}, bf16[512,1024]{1,0:T(8,128)(2,1)S(1)}, u32[]{:S(2)}, u32[]{:S(2)}) collective-permute-start(bf16[512,1024]{1,0:T(8,128)(2,1)} %get-tuple-element.105), channel_id=1, source_target_pairs={{0,1},{1,0},{2,3},{3,2},{4,5},{5,4},{6,7},{7,6},{8,9},{9,8},{10,11... | collective-permute-start | bytes 3145736 | tf_op jit(solution)/shard_map/ppermute | solution.py:86
  70.7 27.2 %collective-permute-start.23 = (bf16[128,2048]{1,0:T(8,128)(2,1)}, bf16[128,2048]{1,0:T(8,128)(2,1)}, u32[]{:S(2)}, u32[]{:S(2)}) collective-permute-start(bf16[128,2048]{1,0:T(8,128)(2,1)} %collective-permute-done.22.refs_1_), channel_id=1, source_target_pairs={{0,16},{4,20},{8,24},{12,28},{16,0},{20,4},{24,8},{28,12},{1,17},{... | collective-permute-start | bytes 1572872 | tf_op jit(solution)/shard_map/ppermute | solution.py:91
  80.2 39.4 %collective-permute-start.35 = (bf16[512,1024]{1,0:T(8,128)(2,1)}, bf16[512,1024]{1,0:T(8,128)(2,1)S(1)}, u32[]{:S(2)}, u32[]{:S(2)}) collective-permute-start(bf16[512,1024]{1,0:T(8,128)(2,1)} %get-tuple-element.112), channel_id=1, source_target_pairs={{0,1},{1,0},{2,3},{3,2},{4,5},{5,4},{6,7},{7,6},{8,9},{9,8},{10,11... | collective-permute-start | bytes 3145736 | tf_op jit(solution)/shard_map/ppermute | solution.py:86
  80.4 20.1 %collective-permute-start.21 = (bf16[128,2048]{1,0:T(8,128)(2,1)}, bf16[128,2048]{1,0:T(8,128)(2,1)S(1)}, u32[]{:S(2)}, u32[]{:S(2)}) collective-permute-start(bf16[128,2048]{1,0:T(8,128)(2,1)} %collective-permute-done.8.refs_9_.refs_2_), channel_id=1, source_target_pairs={{0,4},{4,0},{8,12},{12,8},{16,20},{20,16},{24,28},{28,24},{1,5},{5... | collective-permute-start | bytes 1572872 | tf_op jit(solution)/shard_map/ppermute | solution.py:91
  81.0 35.1 %collective-permute-start.36 = (bf16[128,2048]{1,0:T(8,128)(2,1)S(1)}, bf16[128,2048]{1,0:T(8,128)(2,1)}, u32[]{:S(2)}, u32[]{:S(2)}) collective-permute-start(bf16[128,2048]{1,0:T(8,128)(2,1)S(1)} %copy-done.59), channel_id=1, source_target_pairs={{0,4},{4,0},{8,12},{12,8},{16,20},{20,16},{24,28},{28,24},{1,5},{5... | collective-permute-start | bytes 1572872 | tf_op jit(solution)/shard_map/ppermute | solution.py:91
  97.9 20.3 %collective-permute-start.29 = (bf16[128,2048]{1,0:T(8,128)(2,1)}, bf16[128,2048]{1,0:T(8,128)(2,1)}, u32[]{:S(2)}, u32[]{:S(2)}) collective-permute-start(bf16[128,2048]{1,0:T(8,128)(2,1)} %collective-permute-done.22.refs_1_), channel_id=1, source_target_pairs={{0,8},{4,12},{8,0},{12,4},{16,24},{20,28},{24,16},{28,20},{1,9},{5... | collective-permute-start | bytes 1572872 | tf_op jit(solution)/shard_map/ppermute | solution.py:91
  100.5 33.4 %collective-permute-start.26 = (bf16[128,2048]{1,0:T(8,128)(2,1)}, bf16[128,2048]{1,0:T(8,128)(2,1)S(1)}, u32[]{:S(2)}, u32[]{:S(2)}) collective-permute-start(bf16[128,2048]{1,0:T(8,128)(2,1)} %collective-permute-done.25.refs_6_.refs_4_), channel_id=1, source_target_pairs={{0,4},{4,0},{8,12},{12,8},{16,20},{20,16},{24,28},{28,24},{1,5},{5... | collective-permute-start | bytes 1572872 | tf_op jit(solution)/shard_map/ppermute | solution.py:91
  101.1 32.9 %collective-permute-start.27 = (bf16[128,2048]{1,0:T(8,128)(2,1)}, bf16[128,2048]{1,0:T(8,128)(2,1)S(1)}, u32[]{:S(2)}, u32[]{:S(2)}) collective-permute-start(bf16[128,2048]{1,0:T(8,128)(2,1)} %collective-permute-done.23.refs_7_.refs_2_), channel_id=1, source_target_pairs={{0,8},{4,12},{8,0},{12,4},{16,24},{20,28},{24,16},{28,20},{1,9},{5... | collective-permute-start | bytes 1572872 | tf_op jit(solution)/shard_map/ppermute | solution.py:91
  116.1 18.0 %collective-permute-start.24 = (bf16[256,1024]{1,0:T(8,128)(2,1)}, bf16[256,1024]{1,0:T(8,128)(2,1)S(1)}, u32[]{:S(2)}, u32[]{:S(2)}) collective-permute-start(bf16[256,1024]{1,0:T(8,128)(2,1)} %get-tuple-element.107), channel_id=1, source_target_pairs={{0,2},{1,3},{2,0},{3,1},{4,6},{5,7},{6,4},{7,5},{8,10},{9,11},{10,... | collective-permute-start | bytes 1572872 | tf_op jit(solution)/shard_map/ppermute | solution.py:86
  118.2 17.4 %collective-permute-start.30 = (bf16[128,2048]{1,0:T(8,128)(2,1)}, bf16[128,2048]{1,0:T(8,128)(2,1)S(1)}, u32[]{:S(2)}, u32[]{:S(2)}) collective-permute-start(bf16[128,2048]{1,0:T(8,128)(2,1)} %collective-permute-done.22.refs_1_), channel_id=1, source_target_pairs={{0,4},{4,0},{8,12},{12,8},{16,20},{20,16},{24,28},{28,24},{1,5},{5... | collective-permute-start | bytes 1572872 | tf_op jit(solution)/shard_map/ppermute | solution.py:91
  133.5 12.5 %collective-permute-start.37 = (bf16[256,1024]{1,0:T(8,128)(2,1)}, bf16[256,1024]{1,0:T(8,128)(2,1)S(1)}, u32[]{:S(2)}, u32[]{:S(2)}) collective-permute-start(bf16[256,1024]{1,0:T(8,128)(2,1)} %get-tuple-element.114), channel_id=1, source_target_pairs={{0,2},{1,3},{2,0},{3,1},{4,6},{5,7},{6,4},{7,5},{8,10},{9,11},{10,... | collective-permute-start | bytes 1572872 | tf_op jit(solution)/shard_map/ppermute | solution.py:86
  135.6 13.5 %collective-permute-start.28 = (bf16[256,1024]{1,0:T(8,128)(2,1)S(1)}, bf16[256,1024]{1,0:T(8,128)(2,1)S(1)}, u32[]{:S(2)}, u32[]{:S(2)}) collective-permute-start(bf16[256,1024]{1,0:T(8,128)(2,1)S(1)} %get-tuple-element.109.refs_0_.refs_1_), channel_id=1, source_target_pairs={{0,1},{1,0},{2,3},{3,2},{4,5},{5,4},{6,7},{7,6},{8,9},{9,8},{10,11... | collective-permute-start | bytes 1572872 | tf_op jit(solution)/shard_map/ppermute | solution.py:86
  146.5 17.2 %collective-permute-start.38 = (bf16[256,1024]{1,0:T(8,128)(2,1)S(1)}, bf16[256,1024]{1,0:T(8,128)(2,1)S(1)}, u32[]{:S(2)}, u32[]{:S(2)}) collective-permute-start(bf16[256,1024]{1,0:T(8,128)(2,1)S(1)} %get-tuple-element.115.refs_0_.refs_3_), channel_id=1, source_target_pairs={{0,1},{1,0},{2,3},{3,2},{4,5},{5,4},{6,7},{7,6},{8,9},{9,8},{10,11... | collective-permute-start | bytes 1572872 | tf_op jit(solution)/shard_map/ppermute | solution.py:86
  146.6 26.9 %collective-permute-start.31 = (bf16[128,2048]{1,0:T(8,128)(2,1)}, bf16[128,2048]{1,0:T(8,128)(2,1)S(1)}, u32[]{:S(2)}, u32[]{:S(2)}) collective-permute-start(bf16[128,2048]{1,0:T(8,128)(2,1)} %collective-permute-done.23.refs_7_.refs_2_), channel_id=1, source_target_pairs={{0,4},{4,0},{8,12},{12,8},{16,20},{20,16},{24,28},{28,24},{1,5},{5... | collective-permute-start | bytes 1572872 | tf_op jit(solution)/shard_map/ppermute | solution.py:91
  147.1 26.4 %collective-permute-start.32 = (bf16[128,2048]{1,0:T(8,128)(2,1)}, bf16[128,2048]{1,0:T(8,128)(2,1)S(1)}, u32[]{:S(2)}, u32[]{:S(2)}) collective-permute-start(bf16[128,2048]{1,0:T(8,128)(2,1)} %collective-permute-done.29.refs_7_.refs_3_), channel_id=1, source_target_pairs={{0,4},{4,0},{8,12},{12,8},{16,20},{20,16},{24,28},{28,24},{1,5},{5... | collective-permute-start | bytes 1572872 | tf_op jit(solution)/shard_map/ppermute | solution.py:91
  148.7 34.9 %collective-permute-start.33 = (bf16[128,2048]{1,0:T(8,128)(2,1)S(1)}, bf16[128,2048]{1,0:T(8,128)(2,1)S(1)}, u32[]{:S(2)}, u32[]{:S(2)}) collective-permute-start(bf16[128,2048]{1,0:T(8,128)(2,1)S(1)} %collective-permute-done.27.refs_7_.refs_4_), channel_id=1, source_target_pairs={{0,4},{4,0},{8,12},{12,8},{16,20},{20,16},{24,28},{28,24},{1,5},{5... | collective-permute-start | bytes 1572872 | tf_op jit(solution)/shard_map/ppermute | solution.py:91
  150.0 38.9 %collective-permute-start.39 = (f32[1024]{0:T(1024)S(1)}, f32[1024]{0:T(1024)S(1)}, u32[]{:S(2)}, u32[]{:S(2)}) collective-permute-start(f32[1024]{0:T(1024)S(1)} %copy-done.84), channel_id=1, source_target_pairs={{0,2},{1,3},{2,0},{3,1},{4,6},{5,7},{6,4},{7,5},{8,10},{9,11},{10,... | collective-permute-start | bytes 12296 | tf_op jit(solution)/shard_map/ppermute | solution.py:86
  199.2 10.9 %collective-permute-start.40 = (bf16[256,1024]{1,0:T(8,128)(2,1)}, bf16[256,1024]{1,0:T(8,128)(2,1)S(1)}, u32[]{:S(2)}, u32[]{:S(2)}) collective-permute-start(bf16[256,1024]{1,0:T(8,128)(2,1)} %get-tuple-element.119), channel_id=1, source_target_pairs={{0,1},{1,0},{2,3},{3,2},{4,5},{5,4},{6,7},{7,6},{8,9},{9,8},{10,11... | collective-permute-start | bytes 1572872 | tf_op jit(solution)/shard_map/ppermute | solution.py:86
  215.4 12.9 %collective-permute-start.44 = (bf16[256,1024]{1,0:T(8,128)(2,1)S(1)}, bf16[256,1024]{1,0:T(8,128)(2,1)S(1)}, u32[]{:S(2)}, u32[]{:S(2)}) collective-permute-start(bf16[256,1024]{1,0:T(8,128)(2,1)S(1)} %get-tuple-element.132.refs_0_.refs_3_), channel_id=1, source_target_pairs={{0,1},{1,0},{2,3},{3,2},{4,5},{5,4},{6,7},{7,6},{8,9},{9,8},{10,11... | collective-permute-start | bytes 1572872 | tf_op jit(solution)/shard_map/ppermute | solution.py:86
  227.9 30.9 %collective-permute-start.43 = (bf16[256,1024]{1,0:T(8,128)(2,1)}, bf16[256,1024]{1,0:T(8,128)(2,1)S(1)}, u32[]{:S(2)}, u32[]{:S(2)}) collective-permute-start(bf16[256,1024]{1,0:T(8,128)(2,1)} %get-tuple-element.131), channel_id=1, source_target_pairs={{0,1},{1,0},{2,3},{3,2},{4,5},{5,4},{6,7},{7,6},{8,9},{9,8},{10,11... | collective-permute-start | bytes 1572872 | tf_op jit(solution)/shard_map/ppermute | solution.py:86
  240.5 19.7 %collective-permute-start.46 = (bf16[256,1024]{1,0:T(8,128)(2,1)}, bf16[256,1024]{1,0:T(8,128)(2,1)S(1)}, u32[]{:S(2)}, u32[]{:S(2)}) collective-permute-start(bf16[256,1024]{1,0:T(8,128)(2,1)} %get-tuple-element.149), channel_id=1, source_target_pairs={{0,1},{1,0},{2,3},{3,2},{4,5},{5,4},{6,7},{7,6},{8,9},{9,8},{10,11... | collective-permute-start | bytes 1572872 | tf_op jit(solution)/shard_map/ppermute | solution.py:86
  254.0 64.2 %collective-permute-start.57 = (bf16[512,1024]{1,0:T(8,128)(2,1)}, bf16[512,1024]{1,0:T(8,128)(2,1)}, u32[]{:S(2)}, u32[]{:S(2)}) collective-permute-start(bf16[512,1024]{1,0:T(8,128)(2,1)} %slice.385), channel_id=1, source_target_pairs={{0,4},{4,0},{8,12},{12,8},{16,20},{20,16},{24,28},{28,24},{1,5},{5... | collective-permute-start | bytes 3145736 | tf_op jit(solution)/shard_map/ppermute | solution.py:91
  257.2 63.4 %collective-permute-start.48 = (bf16[512,1024]{1,0:T(8,128)(2,1)}, bf16[512,1024]{1,0:T(8,128)(2,1)}, u32[]{:S(2)}, u32[]{:S(2)}) collective-permute-start(bf16[512,1024]{1,0:T(8,128)(2,1)} %slice.387), channel_id=1, source_target_pairs={{0,4},{4,0},{8,12},{12,8},{16,20},{20,16},{24,28},{28,24},{1,5},{5... | collective-permute-start | bytes 3145736 | tf_op jit(solution)/shard_map/ppermute | solution.py:91
  259.7 26.9 %collective-permute-start.45 = (bf16[256,1024]{1,0:T(8,128)(2,1)S(1)}, bf16[256,1024]{1,0:T(8,128)(2,1)}, u32[]{:S(2)}, u32[]{:S(2)}) collective-permute-start(bf16[256,1024]{1,0:T(8,128)(2,1)S(1)} %get-tuple-element.142.refs_9_.refs_4_.refs_1_), channel_id=1, source_target_pairs={{0,2},{1,3},{2,0},{3,1},{4,6},{5,7},{6,4},{7,5},{8,10},{9,11},{10,... | collective-permute-start | bytes 1572872 | tf_op jit(solution)/shard_map/ppermute | solution.py:86
  263.1 50.9 %collective-permute-start.53 = (bf16[256,1024]{1,0:T(8,128)(2,1)S(1)}, bf16[256,1024]{1,0:T(8,128)(2,1)}, u32[]{:S(2)}, u32[]{:S(2)}) collective-permute-start(bf16[256,1024]{1,0:T(8,128)(2,1)S(1)} %get-tuple-element.150.refs_10_.refs_3_.refs_4_), channel_id=1, source_target_pairs={{0,2},{1,3},{2,0},{3,1},{4,6},{5,7},{6,4},{7,5},{8,10},{9,11},{10,... | collective-permute-start | bytes 1572872 | tf_op jit(solution)/shard_map/ppermute | solution.py:86
  282.5 77.0 %collective-permute-start.50 = (bf16[512,1024]{1,0:T(8,128)(2,1)}, bf16[512,1024]{1,0:T(8,128)(2,1)}, u32[]{:S(2)}, u32[]{:S(2)}) collective-permute-start(bf16[512,1024]{1,0:T(8,128)(2,1)} %slice.386), channel_id=1, source_target_pairs={{0,8},{4,12},{8,0},{12,4},{16,24},{20,28},{24,16},{28,20},{1,9},{5... | collective-permute-start | bytes 3145736 | tf_op jit(solution)/shard_map/ppermute | solution.py:91
  286.6 68.1 %collective-permute-start.58 = (bf16[512,1024]{1,0:T(8,128)(2,1)}, bf16[512,1024]{1,0:T(8,128)(2,1)}, u32[]{:S(2)}, u32[]{:S(2)}) collective-permute-start(bf16[512,1024]{1,0:T(8,128)(2,1)} %slice.384), channel_id=1, source_target_pairs={{0,8},{4,12},{8,0},{12,4},{16,24},{20,28},{24,16},{28,20},{1,9},{5... | collective-permute-start | bytes 3145736 | tf_op jit(solution)/shard_map/ppermute | solution.py:91
  318.2 75.2 %collective-permute-start.47 = (bf16[512,1024]{1,0:T(8,128)(2,1)}, bf16[512,1024]{1,0:T(8,128)(2,1)S(1)}, u32[]{:S(2)}, u32[]{:S(2)}) collective-permute-start(bf16[512,1024]{1,0:T(8,128)(2,1)} %get-tuple-element.154), channel_id=1, source_target_pairs={{0,1},{1,0},{2,3},{3,2},{4,5},{5,4},{6,7},{7,6},{8,9},{9,8},{10,11... | collective-permute-start | bytes 3145736 | tf_op jit(solution)/shard_map/ppermute | solution.py:86
  320.6 21.9 %collective-permute-start.75 = (bf16[256,1024]{1,0:T(8,128)(2,1)S(1)}, bf16[256,1024]{1,0:T(8,128)(2,1)S(1)}, u32[]{:S(2)}, u32[]{:S(2)}) collective-permute-start(bf16[256,1024]{1,0:T(8,128)(2,1)S(1)} %slice.388), channel_id=1, source_target_pairs={{0,8},{4,12},{8,0},{12,4},{16,24},{20,28},{24,16},{28,20},{1,9},{5... | collective-permute-start | bytes 1572872 | tf_op jit(solution)/shard_map/ppermute | solution.py:91
  323.7 28.2 %collective-permute-start.49 = (bf16[256,1024]{1,0:T(8,128)(2,1)S(1)}, bf16[256,1024]{1,0:T(8,128)(2,1)S(1)}, u32[]{:S(2)}, u32[]{:S(2)}) collective-permute-start(bf16[256,1024]{1,0:T(8,128)(2,1)S(1)} %slice.392), channel_id=1, source_target_pairs={{0,8},{4,12},{8,0},{12,4},{16,24},{20,28},{24,16},{28,20},{1,9},{5... | collective-permute-start | bytes 1572872 | tf_op jit(solution)/shard_map/ppermute | solution.py:91
  342.6 16.4 %collective-permute-start.67 = (bf16[512,256]{1,0:T(8,128)(2,1)S(1)}, bf16[512,256]{1,0:T(8,128)(2,1)S(1)}, u32[]{:S(2)}, u32[]{:S(2)}) collective-permute-start(bf16[512,256]{1,0:T(8,128)(2,1)S(1)} %slice.397), channel_id=1, source_target_pairs={{0,4},{4,0},{8,12},{12,8},{16,20},{20,16},{24,28},{28,24},{1,5},{5... | collective-permute-start | bytes 786440 | tf_op jit(solution)/shard_map/ppermute | solution.py:91
  352.0 49.0 %collective-permute-start.76 = (bf16[128,1024]{1,0:T(8,128)(2,1)}, bf16[128,1024]{1,0:T(8,128)(2,1)}, u32[]{:S(2)}, u32[]{:S(2)}) collective-permute-start(bf16[128,1024]{1,0:T(8,128)(2,1)} %slice.393), channel_id=1, source_target_pairs={{0,16},{4,20},{8,24},{12,28},{16,0},{20,4},{24,8},{28,12},{1,17},{... | collective-permute-start | bytes 786440 | tf_op jit(solution)/shard_map/ppermute | solution.py:91
  354.9 62.7 %collective-permute-start.74 = (bf16[128,1024]{1,0:T(8,128)(2,1)}, bf16[128,1024]{1,0:T(8,128)(2,1)}, u32[]{:S(2)}, u32[]{:S(2)}) collective-permute-start(bf16[128,1024]{1,0:T(8,128)(2,1)} %slice.394), channel_id=1, source_target_pairs={{0,16},{4,20},{8,24},{12,28},{16,0},{20,4},{24,8},{28,12},{1,17},{... | collective-permute-start | bytes 786440 | tf_op jit(solution)/shard_map/ppermute | solution.py:91
  359.0 48.5 %collective-permute-start.71 = (bf16[256,1024]{1,0:T(8,128)(2,1)}, bf16[256,1024]{1,0:T(8,128)(2,1)}, u32[]{:S(2)}, u32[]{:S(2)}) collective-permute-start(bf16[256,1024]{1,0:T(8,128)(2,1)} %slice.389), channel_id=1, source_target_pairs={{0,4},{4,0},{8,12},{12,8},{16,20},{20,16},{24,28},{28,24},{1,5},{5... | collective-permute-start | bytes 1572872 | tf_op jit(solution)/shard_map/ppermute | solution.py:91
  359.6 31.6 %collective-permute-start.68 = (bf16[256,256]{1,0:T(8,128)(2,1)S(1)}, bf16[256,256]{1,0:T(8,128)(2,1)S(1)}, u32[]{:S(2)}, u32[]{:S(2)}) collective-permute-start(bf16[256,256]{1,0:T(8,128)(2,1)S(1)} %slice.400), channel_id=1, source_target_pairs={{0,8},{4,12},{8,0},{12,4},{16,24},{20,28},{24,16},{28,20},{1,9},{5... | collective-permute-start | bytes 393224 | tf_op jit(solution)/shard_map/ppermute | solution.py:91
  391.2 20.5 %collective-permute-start.51 = (bf16[256,1024]{1,0:T(8,128)(2,1)}, bf16[256,1024]{1,0:T(8,128)(2,1)}, u32[]{:S(2)}, u32[]{:S(2)}) collective-permute-start(bf16[256,1024]{1,0:T(8,128)(2,1)} %slice.391), channel_id=1, source_target_pairs={{0,4},{4,0},{8,12},{12,8},{16,20},{20,16},{24,28},{28,24},{1,5},{5... | collective-permute-start | bytes 1572872 | tf_op jit(solution)/shard_map/ppermute | solution.py:91
  393.5 9.4 %collective-permute-start.69 = (bf16[128,256]{1,0:T(8,128)(2,1)}, bf16[128,256]{1,0:T(8,128)(2,1)S(1)}, u32[]{:S(2)}, u32[]{:S(2)}) collective-permute-start(bf16[128,256]{1,0:T(8,128)(2,1)} %slice.403), channel_id=1, source_target_pairs={{0,16},{4,20},{8,24},{12,28},{16,0},{20,4},{24,8},{28,12},{1,17},{... | collective-permute-start | bytes 196616 | tf_op jit(solution)/shard_map/ppermute | solution.py:91
  402.3 39.3 %collective-permute-start.55 = (bf16[512,1024]{1,0:T(8,128)(2,1)}, bf16[512,1024]{1,0:T(8,128)(2,1)}, u32[]{:S(2)}, u32[]{:S(2)}) collective-permute-start(bf16[512,1024]{1,0:T(8,128)(2,1)} %get-tuple-element.168), channel_id=1, source_target_pairs={{0,1},{1,0},{2,3},{3,2},{4,5},{5,4},{6,7},{7,6},{8,9},{9,8},{10,11... | collective-permute-start | bytes 3145736 | tf_op jit(solution)/shard_map/ppermute | solution.py:86
  407.0 11.9 %collective-permute-start.77 = (bf16[128,1024]{1,0:T(8,128)(2,1)S(1)}, bf16[128,1024]{1,0:T(8,128)(2,1)S(1)}, u32[]{:S(2)}, u32[]{:S(2)}) collective-permute-start(bf16[128,1024]{1,0:T(8,128)(2,1)S(1)} %fusion.2), channel_id=1, source_target_pairs={{0,2},{1,3},{2,0},{3,1},{4,6},{5,7},{6,4},{7,5},{8,10},{9,11},{10,... | collective-permute-start | bytes 786440 | tf_op jit(solution)/shard_map/ppermute | solution.py:86
  411.6 44.8 %collective-permute-start.59 = (bf16[1024,256]{1,0:T(8,128)(2,1)S(1)}, bf16[1024,256]{1,0:T(8,128)(2,1)}, u32[]{:S(2)}, u32[]{:S(2)}) collective-permute-start(bf16[1024,256]{1,0:T(8,128)(2,1)S(1)} %copy-done.28), channel_id=1, source_target_pairs={{0,1},{1,0},{2,3},{3,2},{4,5},{5,4},{6,7},{7,6},{8,9},{9,8},{10,11... | collective-permute-start | bytes 1572872 | tf_op jit(solution)/shard_map/ppermute | solution.py:86
  415.9 38.8 %collective-permute-start.72 = (bf16[128,1024]{1,0:T(8,128)(2,1)S(1)}, bf16[128,1024]{1,0:T(8,128)(2,1)}, u32[]{:S(2)}, u32[]{:S(2)}) collective-permute-start(bf16[128,1024]{1,0:T(8,128)(2,1)S(1)} %slice.395), channel_id=1, source_target_pairs={{0,16},{4,20},{8,24},{12,28},{16,0},{20,4},{24,8},{28,12},{1,17},{... | collective-permute-start | bytes 786440 | tf_op jit(solution)/shard_map/ppermute | solution.py:91
  417.6 21.3 %collective-permute-start.82 = (f32[12288]{0:T(1024)S(1)}, f32[12288]{0:T(1024)S(1)}, u32[]{:S(2)}, u32[]{:S(2)}) collective-permute-start(f32[12288]{0:T(1024)S(1)} %add.213), channel_id=1, source_target_pairs={{0,16},{4,20},{8,24},{12,28},{16,0},{20,4},{24,8},{28,12},{1,17},{... | collective-permute-start | bytes 147464 | tf_op jit(solution)/shard_map/ppermute | solution.py:91
  422.0 51.4 %collective-permute-start.70 = (bf16[128,1024]{1,0:T(8,128)(2,1)S(1)}, bf16[128,1024]{1,0:T(8,128)(2,1)S(1)}, u32[]{:S(2)}, u32[]{:S(2)}) collective-permute-start(bf16[128,1024]{1,0:T(8,128)(2,1)S(1)} %slice.396), channel_id=1, source_target_pairs={{0,16},{4,20},{8,24},{12,28},{16,0},{20,4},{24,8},{28,12},{1,17},{... | collective-permute-start | bytes 786440 | tf_op jit(solution)/shard_map/ppermute | solution.py:91
  438.9 18.8 %collective-permute-start.52 = (bf16[256,1024]{1,0:T(8,128)(2,1)}, bf16[256,1024]{1,0:T(8,128)(2,1)S(1)}, u32[]{:S(2)}, u32[]{:S(2)}) collective-permute-start(bf16[256,1024]{1,0:T(8,128)(2,1)} %get-tuple-element.158), channel_id=1, source_target_pairs={{0,2},{1,3},{2,0},{3,1},{4,6},{5,7},{6,4},{7,5},{8,10},{9,11},{10,... | collective-permute-start | bytes 1572872 | tf_op jit(solution)/shard_map/ppermute | solution.py:86
  454.6 12.0 %collective-permute-start.63 = (bf16[1024,512]{1,0:T(8,128)(2,1)}, bf16[1024,512]{1,0:T(8,128)(2,1)S(1)}, u32[]{:S(2)}, u32[]{:S(2)}) collective-permute-start(bf16[1024,512]{1,0:T(8,128)(2,1)} %get-tuple-element.178), channel_id=1, source_target_pairs={{0,1},{1,0},{2,3},{3,2},{4,5},{5,4},{6,7},{7,6},{8,9},{9,8},{10,11... | collective-permute-start | bytes 3145736 | tf_op jit(solution)/shard_map/ppermute | solution.py:86
  455.8 17.5 %collective-permute-start.73 = (bf16[128,1024]{1,0:T(8,128)(2,1)S(1)}, bf16[128,1024]{1,0:T(8,128)(2,1)S(1)}, u32[]{:S(2)}, u32[]{:S(2)}) collective-permute-start(bf16[128,1024]{1,0:T(8,128)(2,1)S(1)} %fusion.5), channel_id=1, source_target_pairs={{0,2},{1,3},{2,0},{3,1},{4,6},{5,7},{6,4},{7,5},{8,10},{9,11},{10,... | collective-permute-start | bytes 786440 | tf_op jit(solution)/shard_map/ppermute | solution.py:86
  457.6 8.4 %collective-permute-start.60 = (bf16[512,256]{1,0:T(8,128)(2,1)S(1)}, bf16[512,256]{1,0:T(8,128)(2,1)S(1)}, u32[]{:S(2)}, u32[]{:S(2)}) collective-permute-start(bf16[512,256]{1,0:T(8,128)(2,1)S(1)} %slice.399), channel_id=1, source_target_pairs={{0,8},{4,12},{8,0},{12,4},{16,24},{20,28},{24,16},{28,20},{1,9},{5... | collective-permute-start | bytes 786440 | tf_op jit(solution)/shard_map/ppermute | solution.py:91
  457.7 25.2 %collective-permute-start.56 = (bf16[256,1024]{1,0:T(8,128)(2,1)S(1)}, bf16[256,1024]{1,0:T(8,128)(2,1)S(1)}, u32[]{:S(2)}, u32[]{:S(2)}) collective-permute-start(bf16[256,1024]{1,0:T(8,128)(2,1)S(1)} %copy-done.93), channel_id=1, source_target_pairs={{0,2},{1,3},{2,0},{3,1},{4,6},{5,7},{6,4},{7,5},{8,10},{9,11},{10,... | collective-permute-start | bytes 1572872 | tf_op jit(solution)/shard_map/ppermute | solution.py:86
  467.1 14.9 %collective-permute-start.64 = (bf16[512,512]{1,0:T(8,128)(2,1)S(1)}, bf16[512,512]{1,0:T(8,128)(2,1)S(1)}, u32[]{:S(2)}, u32[]{:S(2)}) collective-permute-start(bf16[512,512]{1,0:T(8,128)(2,1)S(1)} %slice.390), channel_id=1, source_target_pairs={{0,4},{4,0},{8,12},{12,8},{16,20},{20,16},{24,28},{28,24},{1,5},{5... | collective-permute-start | bytes 1572872 | tf_op jit(solution)/shard_map/ppermute | solution.py:91
  (113 other events, 955.0 us)

commit v5 on v4

--- a/solution.py
+++ b/solution.py
@@ -165,26 +165,62 @@
     return order
 
 
-def scatter_dp(total, bits):
-    arrivals = []
-    for bit in bits:
-        half = total.shape[0] // 2
-        came = swap_dp(total[half:].astype(BF16), 1 << bit)
-        arrivals.append(came)
-        total = total[:half] + came.astype(F32)
-    return total, arrivals
-
-
-def sum_all(vector):
-    step = 1
-    while step < lax.axis_size("tensor"):
-        vector = vector + swap_tensor(vector, step)
-        step *= 2
-    step = 1
-    while step < lax.axis_size("dp"):
-        vector = vector + swap_dp(vector, step)
-        step *= 2
-    return vector
+def fold(keep, came, last, deps):
+    rows, width = keep.shape
+
+    def kernel(k_ref, c_ref, *refs):
+        if last:
+            refs[0][...] = k_ref[...] + c_ref[...].astype(F32)
+        else:
+            half = rows // 2
+            refs[0][...] = k_ref[:half] + c_ref[:half].astype(F32)
+            refs[1][...] = (k_ref[half:] + c_ref[half:].astype(F32)).astype(BF16)
+
+    outs = [shape((rows, width), F32)]
+    if not last:
+        outs = [shape((rows // 2, width), F32), shape((rows // 2, width), BF16)]
+    return whole_call(
+        kernel, outs, [keep, came], rows * width, "fold", deps=deps, limit=SMALL_LIMIT
+    )
+
+
+class Chain:
+    def __init__(self, keep, send, bits):
+        self.keep, self.bits = keep, list(bits)
+        self.came = swap_dp(send, 1 << self.bits.pop(0))
+        self.done = False
+
+    def fold(self, deps=()):
+        if self.done:
+            return
+        self.done = not self.bits
+        made = fold(self.keep, self.came, self.done, list(deps))
+        self.keep = made[0]
+        if not self.done:
+            self.came = swap_dp(made[1], 1 << self.bits.pop(0))
+
+    def finish(self):
+        while not self.done:
+            self.fold()
+        return self.keep
+
+
+def sum_all(vector, waits):
+    def plus(one, two, deps):
+        def kernel(a_ref, b_ref, out_ref):
+            out_ref[...] = a_ref[...] + b_ref[...]
+
+        out = shape(one.shape, F32)
+        return whole_call(kernel, [out], [one, two], 0, "plus", deps=deps, limit=SMALL_LIMIT)[0]
+
+    waits = list(waits)
+    held = vector.reshape(-1, 128)
+    for swap, axis in ((swap_tensor, "tensor"), (swap_dp, "dp")):
+        step = 1
+        while step < lax.axis_size(axis):
+            held = plus(held, swap(held, step), waits.pop(0) if waits else [])
+            step *= 2
+    return held.reshape(-1)
 
 
 def project_inputs(x_own, x_across, w_mine, w_other, b_mine, b_other, deps):
@@ -349,7 +385,7 @@
         shape((rows, 4 * third), BF16),
         shape((2, 2 * third), F32),
     ]
-    flops = 5 * 2 * 2 * rows * keys_count * third * heads
+    flops = 5 * 2 * 2 * rows * keys_count * third * heads * 2 * UNDERSTATED
     return whole_call(
         kernel,
         outs,
@@ -553,7 +589,7 @@
     )
 
 
-def feed_forward_back(g_own, g_across, w_mine, w_other, slope_mine, slope_other):
+def feed_forward_back(g_own, g_across, w_mine, w_other, slope_mine, slope_other, deps):
     block, width = g_own.shape
     rows = 2 * block
     hidden = w_mine.shape[1] // 2
@@ -604,71 +640,90 @@
         2 * 2 * rows * width * 2 * hidden,
         "feed_forward_back",
         [pltpu.VMEM((rows, width), BF16), pltpu.VMEM((rows, width), F32)],
-    )
-
-
-def weight_grad(
-    ones, mine, other, dp_place, bits, count, name, other_first=0, deps=(), other_kind=BF16
-):
+        deps,
+    )
+
+
+def weight_grad(ones, mine, other, dp_place, chains, name, other_first=0, deps=(), halves=False):
     block, width = ones[0].shape
     rows = 2 * block
+    count = chains[0][0]
     tile = min(256, count)
+    tiles = count // tile
     size = lax.axis_size("dp")
     share = width // size
-    order = halving_order(size, bits)
-
-    def kernel(place_ref, a0, a1, a2, a3, m0, m1, o0, o1, mine_ref, other_ref, turned, full):
-        @pl.when(pl.program_id(0) == 0)
+    half = width // 2
+
+    def kernel(place_ref, a0, a1, a2, a3, m0, m1, o0, o1, *refs):
+        turned, full = refs[-2:]
+        step = pl.program_id(0)
+
+        @pl.when(step == 0)
         def _():
             for i, ref in enumerate((a0, a1, a2, a3)):
                 turned[:, i * block : (i + 1) * block] = ref[...].T
 
         place = place_ref[0]
-        for one, two, out_ref in ((m0, m1, mine_ref), (o0, o1, other_ref)):
-            full[...] = dot(turned[:, :rows], one[...]) + dot(turned[:, rows:], two[...])
+        each = 4 if halves else 2
+
+        def write(targets, order):
             for i, offset in enumerate(order):
                 start = pl.multiple_of((place ^ offset) * share, share)
-                out_ref[i * share : (i + 1) * share, :] = full[pl.ds(start, share), :].astype(
-                    out_ref.dtype
-                )
+                at = i * share
+                ref = targets[0] if len(targets) == 1 or at < half else targets[1]
+                at = at if len(targets) == 1 or at < half else at - half
+                ref[at : at + share, :] = full[pl.ds(start, share), :].astype(ref.dtype)
+
+        for which, (one, two) in enumerate(((m0, m1), (o0, o1))):
+            full[...] = dot(turned[:, :rows], one[...]) + dot(turned[:, rows:], two[...])
+            for c, (_, bits) in enumerate(chains):
+                per = each // 2
+                targets = refs[c * each + which * per : c * each + (which + 1) * per]
+                order = halving_order(size, bits)
+                if len(chains) == 1:
+                    write(targets, order)
+                else:
+                    pl.when(step // tiles == c)(lambda t=targets, o=order: write(t, o))
 
     base = other_first // tile
     column = pl.BlockSpec((rows, tile), lambda i: (0, i))
     other_column = pl.BlockSpec((rows, tile), lambda i: (0, base + i))
-    made = pl.BlockSpec((width, tile), lambda i: (0, i))
+    outs, out_specs = [], []
+    for c in range(len(chains)):
+        index = lambda i, c=c: (0, jnp.clip(i - c * tiles, 0, tiles - 1))
+        for kinds in ((F32, BF16), (F32, BF16)) if halves else ((F32,), (BF16,)):
+            for kind in kinds:
+                held = half if halves else width
+                outs.append(shape((held, count), kind))
+                out_specs.append(pl.BlockSpec((held, tile), index))
     return streamed_call(
         kernel,
-        (count // tile,),
-        [shape((width, count), F32), shape((width, count), other_kind)],
-        [made] * 2,
+        (tiles * len(chains),),
+        outs,
+        out_specs,
         [dp_place, *ones, *mine, *other],
-        [pl.BlockSpec(memory_space=pltpu.SMEM)] + [const_spec((block, width))] * 4 + [column] * 2 + [other_column] * 2,
-        2 * 2 * rows * width * 2 * count,
+        [pl.BlockSpec(memory_space=pltpu.SMEM)]
+        + [const_spec((block, width))] * 4
+        + [column] * 2
+        + [other_column] * 2,
+        2 * 2 * rows * width * 2 * count * len(chains),
         name,
         [pltpu.VMEM((width, 2 * rows), BF16), pltpu.VMEM((width, tile), F32)],
         deps,
     )
 
 
+def core_chain(mine, other, bits, deps=()):
+    keep, send = fold(mine, swap_tensor(other, CORE), False, list(deps))
+    return Chain(keep, send, bits)
+
+
 def add_up(parts, deps):
     def kernel(*refs):
         refs[-1][...] = sum(ref[...] for ref in refs[:-1])
 
     out = shape(parts[0].shape, F32)
     return whole_call(kernel, [out], parts, 0, "add_up", deps=deps, limit=SMALL_LIMIT)[0]
-
-
-def reduced(made, bits):
-    got = swap_tensor(made[1], CORE)
-    total, arrivals = scatter_dp(made[0] + got.astype(F32), bits)
-    return total, [got, *arrivals]
-
-
-def reduced_across(made, bits):
-    mine, mine_came = scatter_dp(made[0], bits)
-    other, other_came = scatter_dp(made[1], bits)
-    total = mine + swap_tensor(other.astype(BF16), ACROSS).astype(F32)
-    return total, mine_came, other_came
 
 
 def shards(
@@ -712,22 +767,23 @@
     mine_far = gather_far(share)
     mine_near = gather_near(mine_far)
     other_far = gather_far(share_other)
-    other_near = gather_near(other_far)
+    other_near = gather_near(other_far[:1]) + [
+        (swap_tensor(p, ACROSS), offsets) for p, offsets in mine_near[1:]
+    ]
 
     def arrays(pieces):
         return [p for p, _ in pieces]
 
-    att_mine = assemble(att_pieces, dp_place, "assemble_attention", arrays(mine_far[1:2]))
+    att_mine = assemble(att_pieces, dp_place, "assemble_attention")
     att_other = assemble(
-        other_core(att_pieces), dp_place, "assemble_attention_other",
-        x_across + arrays(mine_far[2:3]),
-    )
-    project_waits = [[], arrays(mine_far[3:] + mine_near[:1])]
+        other_core(att_pieces), dp_place, "assemble_attention_other", arrays(mine_far[1:2])
+    )
+    project_waits = [arrays(mine_far[2:3]), arrays(mine_near[:1])]
     attend_waits = [
-        arrays(mine_near[1:2] + other_far[1:2]),
-        arrays(mine_near[2:3] + other_far[2:3]),
+        [share_other] + arrays(mine_far[3:]),
+        arrays(mine_near[1:3] + other_far[1:3]),
     ]
-    norm_waits = [arrays(mine_near[3:] + other_far[3:]), arrays(other_near[:1])]
+    norm_waits = [arrays(mine_near[3:] + other_far[3:]), arrays(other_near[:2])]
     ffw_mine = assemble(mine_far + mine_near, dp_place, "assemble_feed")
 
     biases = jnp.concatenate([b_query, jnp.zeros_like(b_query), b_value])
@@ -741,40 +797,53 @@
     positions = (order[:, None] * block + jnp.arange(block, dtype=jnp.int32)[None, :]).reshape(-1)
     masks = [jnp.where(positions < lengths[s], 0.0, MASKED).astype(F32) for s in seqs]
 
-    projected = [
-        project_inputs(
-            x_own[s], x_across[s], att_mine, att_other, qkv_bias_mine, qkv_bias_other,
-            project_waits[s] if s < 2 else [],
-        )
-        for s in seqs
-    ]
+    projected = []
+    for s in seqs:
+        waits = project_waits[s] if s < 2 else []
+        projected.append(
+            project_inputs(
+                x_own[s], x_across[s], att_mine, att_other, qkv_bias_mine, qkv_bias_other,
+                waits + [p[2] for p in projected[-1:]],
+            )
+        )
     far = [swap_tensor(projected[s][2], CORE) for s in seqs]
-    attended = [
-        attention_forward(
-            projected[s][0], projected[s][1], far[s], masks[s].reshape(1, seq_len),
-            att_mine, att_other, head_size, attend_waits[s] if s < 2 else [],
-        )
-        for s in seqs
-    ]
+    attended = []
+    for s in seqs:
+        waits = attend_waits[s] if s < 2 else []
+        attended.append(
+            attention_forward(
+                projected[s][0], projected[s][1], far[s], masks[s].reshape(1, seq_len),
+                att_mine, att_other, head_size, waits + [p[2] for p in attended[-1:]],
+            )
+        )
     attended_got = [swap_tensor(attended[s][3], ACROSS) for s in seqs]
-    one = [
-        first_norm(
-            x_own[s], attended[s][2], attended_got[s], b_out_row, gain_one, shift_one,
-            norm_waits[s] if s < 2 else [],
-        )
-        for s in seqs
-    ]
+    one = []
+    for s in seqs:
+        waits = norm_waits[s] if s < 2 else []
+        one.append(
+            first_norm(
+                x_own[s], attended[s][2], attended_got[s], b_out_row, gain_one, shift_one,
+                waits + [p[2] for p in one[-1:]],
+            )
+        )
     normed_far = [swap_tensor(one[s][2], CORE) for s in seqs]
-    fed_one = [
-        feed_forward(one[s][2], normed_far[s], ffw_mine, up_bias_mine, None, []) for s in seqs
-    ]
+    fed_one = []
+    for s in seqs:
+        waits = [p[2] for p in fed_one[-1:]]
+        fed_one.append(
+            feed_forward(one[s][2], normed_far[s], ffw_mine, up_bias_mine, None, waits)
+        )
     ffw_other = assemble(
         other_far + other_near, dp_place, "assemble_feed_other", [fed_one[-1][2]]
     )
-    fed_two = [
-        feed_forward(one[s][2], normed_far[s], ffw_other, up_bias_other, fed_one[s][2], [])
-        for s in seqs
-    ]
+    fed_two = []
+    for s in seqs:
+        waits = [p[2] for p in fed_two[-1:]]
+        fed_two.append(
+            feed_forward(
+                one[s][2], normed_far[s], ffw_other, up_bias_other, fed_one[s][2], waits
+            )
+        )
     fed = [(fed_one[s][0], fed_two[s][0], fed_one[s][1], fed_two[s][1], *fed_two[s][2:]) for s in seqs]
     branch_got = [swap_tensor(fed[s][5], CORE) for s in seqs]
     two = [
@@ -784,12 +853,14 @@
         for s in seqs
     ]
     grad_far = [swap_tensor(two[s][2], CORE) for s in seqs]
-    fed_back = [
-        feed_forward_back(
-            two[s][2], grad_far[s], ffw_mine, ffw_other, fed[s][2], fed[s][3]
-        )
-        for s in seqs
-    ]
+    fed_back = []
+    for s in seqs:
+        waits = [p[2] for p in fed_back[-1:]]
+        fed_back.append(
+            feed_forward_back(
+                two[s][2], grad_far[s], ffw_mine, ffw_other, fed[s][2], fed[s][3], waits
+            )
+        )
     back_got = [swap_tensor(fed_back[s][3], CORE) for s in seqs]
     def placed_in(part_mine, part_other, bit):
         size = part_mine.shape[0]
@@ -812,17 +883,19 @@
     down_made = weight_grad(
         pairs([two[s][2] for s in seqs], grad_far),
         [fed[s][0] for s in seqs], [fed[s][1] for s in seqs],
-        dp_place, near_first, hidden, "w_down_grad", deps=[fed_back[-1][2]], other_kind=F32,
+        dp_place, [(hidden, near_first)], "w_down_grad", deps=[fed_back[-1][2]], halves=True,
     )
     one_back = [norm_back(s, [down_made[1]]) for s in seqs]
     up_made = weight_grad(
         pairs([one[s][2] for s in seqs], normed_far),
         [fed_back[s][0] for s in seqs], [fed_back[s][1] for s in seqs],
-        dp_place, far_first, hidden, "w_up_grad", deps=[one_back[s][1] for s in seqs], other_kind=F32,
+        dp_place, [(hidden, far_first)], "w_up_grad", deps=[one_back[s][1] for s in seqs], halves=True,
     )
     first_across = [swap_tensor(one_back[s][1], ACROSS) for s in seqs]
-    down_grad, down_mine_came, down_other_came = reduced_across(down_made, near_first)
-    up_grad, up_mine_came, up_other_came = reduced_across(up_made, far_first)
+    down_mine = Chain(down_made[0], down_made[1], near_first)
+    down_other = Chain(down_made[2], down_made[3], near_first)
+    up_mine = Chain(up_made[0], up_made[1], far_first)
+    up_other = Chain(up_made[2], up_made[3], far_first)
 
     def backward(s, deps):
         return attention_backward(
@@ -831,48 +904,62 @@
         )
 
     attended_back = [backward(0, [up_made[1]])]
-    out_grad, out_came = reduced(
-        weight_grad(
-            pairs([one_back[s][1] for s in seqs], first_across),
-            [attended[s][0] for s in seqs], [attended[s][1] for s in seqs],
-            dp_place, near_first, head_dims, "w_out_grad", deps=[attended_back[0][3]],
-        ),
-        near_first,
-    )
-
-    attended_back += [
-        backward(s, [down_mine_came[0], up_mine_came[0], out_came[0]]) for s in seqs[1:]
-    ]
+    out_made = weight_grad(
+        pairs([one_back[s][1] for s in seqs], first_across),
+        [attended[s][0] for s in seqs], [attended[s][1] for s in seqs],
+        dp_place, [(head_dims, near_first)], "w_out_grad", deps=[attended_back[0][3]],
+    )
+    down_mine.fold([attended_back[0][3]])
+    up_mine.fold([attended_back[0][3]])
+    attended_back += [backward(s, [down_mine.keep, up_mine.keep, out_made[1]]) for s in seqs[1:]]
     far_back = [swap_tensor(attended_back[s][2], CORE) for s in seqs]
+
+    down_other.fold([attended_back[-1][3]])
+    up_other.fold([attended_back[-1][3]])
+    tokens = pairs(x_own, x_across)
+    grad_queries = [attended_back[s][0] for s in seqs]
+    query_made = weight_grad(
+        tokens, grad_queries, grad_queries, dp_place, [(head_dims, far_first)], "w_query_grad",
+        head_dims, [far_back[0], down_other.keep, up_other.keep, down_mine.came, up_mine.came],
+    )
+    query_chain = core_chain(query_made[0], query_made[1], far_first)
     back = [
         project_back(
+            attended_back[0][0], attended_back[0][1], far_back[0], att_mine, att_other,
+            [query_made[1], far_back[-1]],
+        )
+    ]
+    down_mine.fold([back[0][2]])
+    up_mine.fold([back[0][2]])
+    back += [
+        project_back(
             attended_back[s][0], attended_back[s][1], far_back[s], att_mine, att_other,
-            [c[-2] for c in (down_mine_came, up_mine_came)] if s == 0 else [],
-        )
-        for s in seqs
+            [down_mine.keep, up_mine.keep],
+        )
+        for s in seqs[1:]
     ]
     input_got = [swap_tensor(back[s][3], ACROSS) for s in seqs]
+    key_value_made = weight_grad(
+        tokens, [back[s][0] for s in seqs], [back[s][1] for s in seqs],
+        dp_place, [(head_dims, near_first), (head_dims, far_first)], "w_key_value_grad",
+        deps=input_got[:1],
+    )
+    down_other.fold([key_value_made[0]])
+    up_other.fold([key_value_made[0]])
+    seconds = [down_other.keep, up_other.keep, input_got[-1]]
+    key_chain = core_chain(key_value_made[0], key_value_made[1], near_first, seconds)
+    value_chain = core_chain(key_value_made[2], key_value_made[3], far_first, seconds)
+    out_chain = core_chain(out_made[0], out_made[1], near_first, [attended_back[-1][3]])
+    out_chain.fold([key_value_made[0]])
+    query_chain.fold([key_value_made[0]])
+    for chain in (down_mine, up_mine, down_other, up_other):
+        chain.fold([value_chain.keep, key_chain.keep])
     input_grad = jnp.stack(
         [
             (one_back[s][0] + (back[s][2] + input_got[s].astype(F32))).astype(BF16)
             for s in seqs
         ]
     )
-    tokens = pairs(x_own, x_across)
-    grad_queries = [attended_back[s][0] for s in seqs]
-    query_made = weight_grad(
-        tokens, grad_queries, grad_queries, dp_place, far_first, head_dims, "w_query_grad",
-        head_dims, [far_back[0], down_other_came[0], up_other_came[0]],
-    )
-    query_grad, _ = reduced(query_made, far_first)
-    both_grad, _ = reduced(
-        weight_grad(
-            tokens, [back[s][0] for s in seqs], [back[s][1] for s in seqs],
-            dp_place, near_first, 2 * head_dims, "w_key_value_grad",
-        ),
-        near_first,
-    )
-
     sums = add_up([attended_back[s][3] for s in seqs], [query_made[1]])
     small = sum_all(
         jnp.concatenate(
@@ -887,8 +974,14 @@
                 placed_in(sums[0, :head_dims], sums[1, :head_dims], CORE),
                 placed_in(sums[0, head_dims:], sums[1, head_dims:], CORE),
             ]
-        )
-    )
+        ),
+        [[back[0][2]], [back[-1][2]], [key_chain.keep, value_chain.keep]],
+    )
+
+    def over_y(mine, other):
+        return mine.finish() + swap_tensor(other.finish().astype(BF16), ACROSS).astype(F32)
+
+    down_grad, up_grad = over_y(down_mine, down_other), over_y(up_mine, up_other)
     vectors = [small[i * width : (i + 1) * width] for i in range(6)]
     second_gain_grad, second_shift_grad, b_down_grad = vectors[:3]
     first_gain_grad, first_shift_grad, b_out_grad = vectors[3:]
@@ -899,10 +992,10 @@
     return (
         output,
         input_grad,
-        query_grad,
-        both_grad[:, :head_dims],
-        both_grad[:, head_dims:],
-        out_grad.T,
+        query_chain.finish(),
+        key_chain.finish(),
+        value_chain.finish(),
+        out_chain.finish().T,
         up_grad,
         down_grad.T,
         b_query_grad,

time: 504 us -> 492 us (0.976)
  other arithmetic: 23.3 us -> 6.8 us
  Pallas kernels: 222 us -> 238 us
  waiting for transfers between devices: 128 us -> 112 us
    ppermute x45, waiting for transfers between devices: 112 us -> 74.3 us  [swap_dp(): return lax.ppermute(array, 'dp', [(i, i ^ bit) for i in range(size)])]
    ppermute x38 -> x42, waiting for transfers between devices: 16.3 us -> 37.8 us  [swap_tensor(): return lax.ppermute(array, 'tensor', [(i, i ^ bit) for i in range(size)])]
    unnamed x200 -> x262, local copies, waits for them, and re-layouts: 23.5 us -> 42.8 us
    slice x22 -> x0, local copies, waits for them, and re-layouts: 17.3 us -> none  [the longest x21 16.6 us: scatter_dp(): came = swap_dp(total[half:].astype(BF16), 1 << bit)]
    pallas_call x17 -> x50, Pallas kernels: 111 us -> 125 us  [whole_call(): pl.pallas_call(after(kernel, len(args), deps), out_shape=tuple(outs), in_...]
    add x25 -> x1, other arithmetic: 14.6 us -> 0.85 us  [over_y(): mine.finish() + swap_tensor(other.finish().astype(BF16), ACROSS).astype(F32)]
    ppermute x38 -> x42, starting transfers between devices: 17.9 us -> 23.5 us  [swap_tensor(): return lax.ppermute(array, 'tensor', [(i, i ^ bit) for i in range(size)])]
  transfers between devices with their start and end apart: 83 -> 87, of which waited for: 22 -> 22; matrix products, arithmetic and copies ran while one was open for 11% -> 4% of each run, Pallas kernels for 42% -> 47%
where the time goes in v5:
time: 492 us; the launch traced here: 486 us
  Pallas kernels  238 us (48%)
  waiting for transfers between devices  112 us (23%)
  starting transfers between devices  78.8 us (16%)
  local copies, waits for them, and re-layouts  47.6 us (10%)
  other arithmetic  6.8 us (1%)
    pallas_call x50, Pallas kernels, whole_call(): pl.pallas_call(after(kernel, len(args), deps), out_shape=tuple(outs), in_...  125 us
    pallas_call x11, Pallas kernels, streamed_call(): pl.pallas_call(after(kernel, len(args), deps), grid=grid, out_shape=tuple...  98.4 us
    ppermute x45, waiting for transfers between devices, swap_dp(): return lax.ppermute(array, 'dp', [(i, i ^ bit) for i in range(size)])  74.3 us
    ppermute x45, starting transfers between devices, swap_dp(): return lax.ppermute(array, 'dp', [(i, i ^ bit) for i in range(size)])  55.3 us
    unnamed x262, local copies, waits for them, and re-layouts  42.8 us
    ppermute x42, waiting for transfers between devices, swap_tensor(): return lax.ppermute(array, 'tensor', [(i, i ^ bit) for i in range(size)])  37.8 us
    ppermute x42, starting transfers between devices, swap_tensor(): return lax.ppermute(array, 'tensor', [(i, i ^ bit) for i in range(size)])  23.5 us
    pallas_call x4, Pallas kernels, assemble(): pl.pallas_call(after(kernel, 1 + len(arrays), deps), out_shape=out, in_sp...  14.7 us
  transfers between devices with their start and end apart: 87, of which 22 were waited for; matrix products, arithmetic and copies ran while one was open for 4% of the time, Pallas kernels for 47%

profile of v5, /device:TPU:0, one launch (start us, length us, event | category | flops | bytes accessed | tf_op | source)
XLA Modules:
  0.0 485.9 jit_solution(168241062963581791)
XLA Ops:
  0.7 1.7 copy.39
  2.3 1.7 pack_attention.1.refs_1_
  4.0 4.0 collective-permute-start.1
  8.0 1.6 collective-permute-start.2
  12.3 8.0 %collective-permute-done.1.refs_2_ = bf16[128,1024]{1,0:T(8,128)(2,1)S(1)} collective-permute-done((bf16[128,1024]{1,0:T(8,128)(2,1)}, bf16[128,1024]{1,0:T(8,128)(2,1)S(1)}, u32[]{:S(2)}, u32[]{:S(2)}) %collective-permute-start.1) | collective-permute-done | bytes 262176 | tf_op jit(solution)/shard_map/ppermute | solution.py:91
  23.0 1.9 copy.40
  24.9 1.9 pack_feed.1.refs_1_
  26.8 3.3 collective-permute-start.16
  30.6 4.0 collective-permute-done.6.refs_7_
  38.2 1.5 collective-permute-start
  39.8 2.2 collective-permute-done.7.refs_8_
  44.3 1.5 collective-permute-start.34
  45.8 8.3 %collective-permute-done.16.refs_9_.refs_2_ = bf16[128,2048]{1,0:T(8,128)(2,1)S(1)} collective-permute-done((bf16[128,2048]{1,0:T(8,128)(2,1)}, bf16[128,2048]{1,0:T(8,128)(2,1)S(1)}, u32[]{:S(2)}, u32[]{:S(2)}) %collective-permute-start.16) | collective-permute-done | bytes 524320 | tf_op jit(solution)/shard_map/ppermute | solution.py:91
  56.8 3.0 assemble_attention.1.refs_2_.refs_4_.refs_6_.refs_3_
  60.5 3.0 assemble_attention_other.1.refs_3_.refs_5_.refs_7_.refs_4_
  65.7 5.6 %project_inputs.2 = (bf16[512,768]{1,0:T(8,128)(2,1)}, bf16[512,768]{1,0:T(8,128)(2,1)}, bf16[512,1024]{1,0:T(8,128)(2,1)}) custom-call(bf16[256,1024]{1,0:T(8,128)(2,1)} %copy-done.3, bf16[256,1024]{1,0:T(8,128)(2,1)} %copy-done.82, bf16[1024,1024]{1,0:T(8,128)(2,1)} %assemble_attention.1.refs_2_.refs_4_.refs_6_.refs_3_, ...), custom_call_target="tpu_custom_call" | custom-call | flops 1610612 | bytes 7870 | tf_op jit(solution)/shard_map/project_inputs/pallas_call | solution.py:46
  71.3 1.5 collective-permute-start.20
  75.2 5.6 %project_inputs.3 = (bf16[512,768]{1,0:T(8,128)(2,1)}, bf16[512,768]{1,0:T(8,128)(2,1)}, bf16[512,1024]{1,0:T(8,128)(2,1)}) custom-call(bf16[256,1024]{1,0:T(8,128)(2,1)} %copy-done.5, bf16[256,1024]{1,0:T(8,128)(2,1)} %copy-done.83, bf16[1024,1024]{1,0:T(8,128)(2,1)} %assemble_attention.1.refs_2_.refs_4_.refs_6_.refs_3_, ...), custom_call_target="tpu_custom_call" | custom-call | flops 1610612 | bytes 7870 | tf_op jit(solution)/shard_map/project_inputs/pallas_call | solution.py:46
  80.8 5.1 %collective-permute-done.20.refs_6_.refs_1_ = bf16[128,2048]{1,0:T(8,128)(2,1)S(1)} collective-permute-done((bf16[128,2048]{1,0:T(8,128)(2,1)}, bf16[128,2048]{1,0:T(8,128)(2,1)S(1)}, u32[]{:S(2)}, u32[]{:S(2)}) %collective-permute-start.20) | collective-permute-done | bytes 524320 | tf_op jit(solution)/shard_map/ppermute | solution.py:86
  88.1 2.1 collective-permute-start.27
  94.6 12.9 %attention_forward.2 = (bf16[512,256]{1,0:T(8,128)(2,1)}, bf16[512,256]{1,0:T(8,128)(2,1)}, f32[256,1024]{1,0:T(8,128)}, bf16[256,1024]{1,0:T(8,128)(2,1)}) custom-call(bf16[512,768]{1,0:T(8,128)(2,1)} %get-tuple-element.149.refs_0_, bf16[512,768]{1,0:T(8,128)(2,1)} %get-tuple-element.150.refs_1_, bf16[512,1024]{1,0:T(8,128)(2,1)} %collective-permute-done.19.refs_2_, ...), custom_call_target="tpu_custom_call" | custom-call | flops 8589934 | bytes 8916 | tf_op jit(solution)/shard_map/attention_forward/pallas_call | solution.py:46
  108.4 4.2 collective-permute-done.24.refs_8_.refs_2_
  115.0 12.8 %attention_forward.3 = (bf16[512,256]{1,0:T(8,128)(2,1)}, bf16[512,256]{1,0:T(8,128)(2,1)}, f32[256,1024]{1,0:T(8,128)}, bf16[256,1024]{1,0:T(8,128)(2,1)}) custom-call(bf16[512,768]{1,0:T(8,128)(2,1)} %get-tuple-element.156.refs_0_, bf16[512,768]{1,0:T(8,128)(2,1)} %get-tuple-element.157.refs_1_, bf16[512,1024]{1,0:T(8,128)(2,1)} %collective-permute-done.36.refs_2_, ...), custom_call_target="tpu_custom_call" | custom-call | flops 8589934 | bytes 8916 | tf_op jit(solution)/shard_map/attention_forward/pallas_call | solution.py:46
  129.2 9.7 %collective-permute-done.22.refs_2_ = bf16[256,1024]{1,0:T(8,128)(2,1)S(1)} collective-permute-done((bf16[256,1024]{1,0:T(8,128)(2,1)}, bf16[256,1024]{1,0:T(8,128)(2,1)S(1)}, u32[]{:S(2)}, u32[]{:S(2)}) %collective-permute-start.22) | collective-permute-done | bytes 524320 | tf_op jit(solution)/shard_map/ppermute | solution.py:86
  140.5 8.6 %collective-permute-done.37.refs_2_ = bf16[256,1024]{1,0:T(8,128)(2,1)S(1)} collective-permute-done((bf16[256,1024]{1,0:T(8,128)(2,1)}, bf16[256,1024]{1,0:T(8,128)(2,1)S(1)}, u32[]{:S(2)}, u32[]{:S(2)}) %collective-permute-start.37) | collective-permute-done | bytes 524320 | tf_op jit(solution)/shard_map/ppermute | solution.py:86
  149.8 1.6 collective-permute-start.32
  151.9 1.5 collective-permute-start.39
  153.4 4.4 assemble_feed.1.refs_2_.refs_3_.refs_4_
  158.6 8.8 %feed_forward.4 = (bf16[512,1024]{1,0:T(8,128)(2,1)}, bf16[512,1024]{1,0:T(8,128)(2,1)}, f32[512,1024]{1,0:T(8,128)}) custom-call(bf16[256,1024]{1,0:T(8,128)(2,1)} %copy-done.7, bf16[256,1024]{1,0:T(8,128)(2,1)} %copy-done.84, bf16[1024,2048]{1,0:T(8,128)(2,1)} %assemble_feed.1.refs_2_.refs_3_.refs_4_, ...), custom_call_target="tpu_custom_call" | custom-call | flops 2147483 | bytes 13635 | tf_op jit(solution)/shard_map/feed_forward/pallas_call | solution.py:63
  168.2 8.8 %feed_forward.5 = (bf16[512,1024]{1,0:T(8,128)(2,1)}, bf16[512,1024]{1,0:T(8,128)(2,1)}, f32[512,1024]{1,0:T(8,128)}) custom-call(bf16[256,1024]{1,0:T(8,128)(2,1)} %copy-done.8, bf16[256,1024]{1,0:T(8,128)(2,1)} %copy-done.85, bf16[1024,2048]{1,0:T(8,128)(2,1)} %assemble_feed.1.refs_2_.refs_3_.refs_4_, ...), custom_call_target="tpu_custom_call" | custom-call | flops 2147483 | bytes 13635 | tf_op jit(solution)/shard_map/feed_forward/pallas_call | solution.py:63
  177.9 4.4 assemble_feed_other.1.refs_2_.refs_3_.refs_5_
  182.9 9.7 %feed_forward.6 = (bf16[512,1024]{1,0:T(8,128)(2,1)}, bf16[512,1024]{1,0:T(8,128)(2,1)}, f32[256,1024]{1,0:T(8,128)}, bf16[256,1024]{1,0:T(8,128)(2,1)}) custom-call(bf16[256,1024]{1,0:T(8,128)(2,1)} %copy-done.7, bf16[256,1024]{1,0:T(8,128)(2,1)} %copy-done.84, bf16[1024,2048]{1,0:T(8,128)(2,1)} %assemble_feed_other.1.refs_2_.refs_3_.refs_5_, ...), custom_call_target="tpu_custom_call" | custom-call | flops 2147483 | bytes 15208 | tf_op jit(solution)/shard_map/feed_forward/pallas_call | solution.py:63
  192.7 9.9 %feed_forward.7 = (bf16[512,1024]{1,0:T(8,128)(2,1)}, bf16[512,1024]{1,0:T(8,128)(2,1)}, f32[256,1024]{1,0:T(8,128)}, bf16[256,1024]{1,0:T(8,128)(2,1)}) custom-call(bf16[256,1024]{1,0:T(8,128)(2,1)} %copy-done.8, bf16[256,1024]{1,0:T(8,128)(2,1)} %copy-done.85, bf16[1024,2048]{1,0:T(8,128)(2,1)} %assemble_feed_other.1.refs_2_.refs_3_.refs_5_, ...), custom_call_target="tpu_custom_call" | custom-call | flops 2147483 | bytes 15208 | tf_op jit(solution)/shard_map/feed_forward/pallas_call | solution.py:63
  209.9 11.4 %feed_forward_back.2 = (bf16[512,1024]{1,0:T(8,128)(2,1)}, bf16[512,1024]{1,0:T(8,128)(2,1)}, f32[256,1024]{1,0:T(8,128)}, bf16[256,1024]{1,0:T(8,128)(2,1)}, f32[1,1024]{1,0:T(1,128)}, /*index=5*/f32[1,1024]{1,0:T(1,128)}) custom-call(bf16[256,1024]{1,0:T(8,128)(2,1)} %copy-done.34, bf16[256,1024]{1,0:T(8,128)(2,1)} %copy-done.93, ...), custom_call_target="tpu_custom_call" | custom-call | flops 4294967 | bytes 23601 | tf_op jit(solution)/shard_map/feed_forward_back/pallas_call | solution.py:63
  222.7 11.4 %feed_forward_back.3 = (bf16[512,1024]{1,0:T(8,128)(2,1)}, bf16[512,1024]{1,0:T(8,128)(2,1)}, f32[256,1024]{1,0:T(8,128)}, bf16[256,1024]{1,0:T(8,128)(2,1)}, f32[1,1024]{1,0:T(1,128)}, /*index=5*/f32[1,1024]{1,0:T(1,128)}) custom-call(bf16[256,1024]{1,0:T(8,128)(2,1)} %copy-done.35, bf16[256,1024]{1,0:T(8,128)(2,1)} %copy-done.94, ...), custom_call_target="tpu_custom_call" | custom-call | flops 4294967 | bytes 23601 | tf_op jit(solution)/shard_map/feed_forward_back/pallas_call | solution.py:63
  234.2 9.8 %w_down_grad.1 = (f32[512,1024]{1,0:T(8,128)}, bf16[512,1024]{1,0:T(8,128)(2,1)}, f32[512,1024]{1,0:T(8,128)}, bf16[512,1024]{1,0:T(8,128)(2,1)}) custom-call(s32[1]{0:T(128)} %bitcast.1.refs_0_, bf16[256,1024]{1,0:T(8,128)(2,1)} %copy-done.34, bf16[256,1024]{1,0:T(8,128)(2,1)} %copy-done.93, bf16[256,1024]{1,0:T(8,128)(2,1)} %copy-done.35, ...), custom_call_target="tpu_custom_call" | custom-call | flops 4294967 | bytes 12582 | tf_op jit(solution)/shard_map/w_down_grad/pallas_call | solution.py:63
  256.0 1.5 collective-permute-start.48
  257.6 10.1 %w_up_grad.1 = (f32[512,1024]{1,0:T(8,128)}, bf16[512,1024]{1,0:T(8,128)(2,1)}, f32[512,1024]{1,0:T(8,128)}, bf16[512,1024]{1,0:T(8,128)(2,1)}) custom-call(s32[1]{0:T(128)} %bitcast.1.refs_0_, bf16[256,1024]{1,0:T(8,128)(2,1)} %copy-done.7, bf16[256,1024]{1,0:T(8,128)(2,1)} %copy-done.84, bf16[256,1024]{1,0:T(8,128)(2,1)} %copy-done.8, ...), custom_call_target="tpu_custom_call" | custom-call | flops 4294967 | bytes 12582 | tf_op jit(solution)/shard_map/w_up_grad/pallas_call | solution.py:63
  267.7 2.0 collective-permute-start.52
  269.7 26.1 %attention_backward.2 = (bf16[512,512]{1,0:T(8,128)(2,1)}, f32[512,1024]{1,0:T(8,128)}, bf16[512,1024]{1,0:T(8,128)(2,1)}, f32[2,512]{1,0:T(2,128)}) custom-call(bf16[512,768]{1,0:T(8,128)(2,1)} %get-tuple-element.149.refs_0_, bf16[512,768]{1,0:T(8,128)(2,1)} %get-tuple-element.150.refs_1_, bf16[512,1024]{1,0:T(8,128)(2,1)} %collective-permute-done.19.refs_2_, ...), custom_call_target="tpu_custom_call" | custom-call | flops 21474836480 | bytes 11542 | tf_op jit(solution)/shard_map/attention_backward/pallas_call | solution.py:46
  296.7 4.4 w_out_grad.1
  301.1 2.3 fold.28
  306.4 26.5 %attention_backward.3 = (bf16[512,512]{1,0:T(8,128)(2,1)}, f32[512,1024]{1,0:T(8,128)}, bf16[512,1024]{1,0:T(8,128)(2,1)}, f32[2,512]{1,0:T(2,128)}) custom-call(bf16[512,768]{1,0:T(8,128)(2,1)} %get-tuple-element.156.refs_0_, bf16[512,768]{1,0:T(8,128)(2,1)} %get-tuple-element.157.refs_1_, bf16[512,1024]{1,0:T(8,128)(2,1)} %collective-permute-done.36.refs_2_, ...), custom_call_target="tpu_custom_call" | custom-call | flops 21474836480 | bytes 11542 | tf_op jit(solution)/shard_map/attention_backward/pallas_call | solution.py:46
  341.6 5.8 %collective-permute-done.53.refs_12_.refs_1_ = bf16[256,1024]{1,0:T(8,128)(2,1)S(1)} collective-permute-done((bf16[256,1024]{1,0:T(8,128)(2,1)}, bf16[256,1024]{1,0:T(8,128)(2,1)S(1)}, u32[]{:S(2)}, u32[]{:S(2)}) %collective-permute-start.53) | collective-permute-done | bytes 524320 | tf_op jit(solution)/shard_map/ppermute | solution.py:91
  349.2 4.4 w_query_grad.1
  353.7 1.8 fold.48
  357.1 6.4 %project_back.2 = (bf16[512,512]{1,0:T(8,128)(2,1)}, bf16[512,512]{1,0:T(8,128)(2,1)}, f32[256,1024]{1,0:T(8,128)}, bf16[256,1024]{1,0:T(8,128)(2,1)}) custom-call(bf16[512,512]{1,0:T(8,128)(2,1)} %get-tuple-element.198.refs_5_.refs_7_.refs_0_, f32[512,1024]{1,0:T(8,128)} %get-tuple-element.199.refs_1_, ...), custom_call_target="tpu_custom_call" | custom-call | flops 1610612 | bytes 10485 | tf_op jit(solution)/shard_map/project_back/pallas_call | solution.py:46
  365.6 1.8 collective-permute-start.59
  370.1 7.7 %collective-permute-done.56.refs_9_ = bf16[256,1024]{1,0:T(8,128)(2,1)} collective-permute-done((bf16[256,1024]{1,0:T(8,128)(2,1)}, bf16[256,1024]{1,0:T(8,128)(2,1)}, u32[]{:S(2)}, u32[]{:S(2)}) %collective-permute-start.56) | collective-permute-done | bytes 524320 | tf_op jit(solution)/shard_map/ppermute | solution.py:86
  381.2 6.2 %project_back.3 = (bf16[512,512]{1,0:T(8,128)(2,1)}, bf16[512,512]{1,0:T(8,128)(2,1)}, f32[256,1024]{1,0:T(8,128)}, bf16[256,1024]{1,0:T(8,128)(2,1)}) custom-call(bf16[512,512]{1,0:T(8,128)(2,1)} %get-tuple-element.211.refs_6_.refs_8_.refs_0_, f32[512,1024]{1,0:T(8,128)} %get-tuple-element.226.refs_1_, ...), custom_call_target="tpu_custom_call" | custom-call | flops 1610612 | bytes 10485 | tf_op jit(solution)/shard_map/project_back/pallas_call | solution.py:46
  387.5 9.6 %w_key_value_grad.1 = (f32[1024,256]{1,0:T(8,128)}, bf16[1024,256]{1,0:T(8,128)(2,1)}, f32[1024,256]{1,0:T(8,128)}, bf16[1024,256]{1,0:T(8,128)(2,1)}) custom-call(s32[1]{0:T(128)} %bitcast.1.refs_0_, bf16[256,1024]{1,0:T(8,128)(2,1)} %copy-done.3, bf16[256,1024]{1,0:T(8,128)(2,1)} %copy-done.82, bf16[256,1024]{1,0:T(8,128)(2,1)} %copy-done.5, ...), custom_call_target="tpu_custom_call" | custom-call | flops 2147483 | bytes 7340 | tf_op jit(solution)/shard_map/w_key_value_grad/pallas_call | solution.py:63
  400.2 1.6 collective-permute-start.84
  405.4 1.7 collective-permute-done.60.refs_1_
  407.1 2.0 collective-permute-start.76
  410.1 2.0 collective-permute-start.79
  413.2 2.4 collective-permute-start.61
  417.1 6.7 %collective-permute-done.74.refs_1_ = bf16[256,256]{1,0:T(8,128)(2,1)S(1)} collective-permute-done((bf16[256,256]{1,0:T(8,128)(2,1)S(1)}, bf16[256,256]{1,0:T(8,128)(2,1)S(1)}, u32[]{:S(2)}, u32[]{:S(2)}) %collective-permute-start.74) | collective-permute-done | bytes 131104 | tf_op jit(solution)/shard_map/ppermute | solution.py:91
  423.8 3.2 collective-permute-start.77
  427.0 15.1 %collective-permute-done.61.refs_1_ = bf16[128,256]{1,0:T(8,128)(2,1)S(1)} collective-permute-done((bf16[128,256]{1,0:T(8,128)(2,1)S(1)}, bf16[128,256]{1,0:T(8,128)(2,1)S(1)}, u32[]{:S(2)}, u32[]{:S(2)}) %collective-permute-start.61) | collective-permute-done | bytes 65568 | tf_op jit(solution)/shard_map/ppermute | solution.py:91
  442.2 2.9 collective-permute-start.75
  446.4 14.1 %collective-permute-done.75.refs_1_ = bf16[128,256]{1,0:T(8,128)(2,1)S(1)} collective-permute-done((bf16[128,256]{1,0:T(8,128)(2,1)S(1)}, bf16[128,256]{1,0:T(8,128)(2,1)S(1)}, u32[]{:S(2)}, u32[]{:S(2)}) %collective-permute-start.75) | collective-permute-done | bytes 65568 | tf_op jit(solution)/shard_map/ppermute | solution.py:91
  465.3 2.4 collective-permute-start.69
  474.2 3.7 collective-permute-done.78
  479.6 2.2 collective-permute-start.71
  (473 shorter events, 109.8 us)
Async XLA Ops:
  4.0 16.3 %collective-permute-start.1 = (bf16[128,1024]{1,0:T(8,128)(2,1)}, bf16[128,1024]{1,0:T(8,128)(2,1)S(1)}, u32[]{:S(2)}, u32[]{:S(2)}) collective-permute-start(bf16[128,1024]{1,0:T(8,128)(2,1)} %pack_attention.1.refs_1_), channel_id=1, source_target_pairs={{0,16},{4,20},{8,24},{12,28},{16,0},{20,4},{24,8},{28,12},{1,17},{... | collective-permute-start | bytes 786440 | tf_op jit(solution)/shard_map/ppermute | solution.py:91
  8.0 14.5 %collective-permute-start.2 = (bf16[128,1024]{1,0:T(8,128)(2,1)}, bf16[128,1024]{1,0:T(8,128)(2,1)S(1)}, u32[]{:S(2)}, u32[]{:S(2)}) collective-permute-start(bf16[128,1024]{1,0:T(8,128)(2,1)} %pack_attention.1.refs_1_), channel_id=1, source_target_pairs={{0,8},{4,12},{8,0},{12,4},{16,24},{20,28},{24,16},{28,20},{1,9},{5... | collective-permute-start | bytes 786440 | tf_op jit(solution)/shard_map/ppermute | solution.py:91
  9.6 13.4 %collective-permute-start.4 = (bf16[128,1024]{1,0:T(8,128)(2,1)}, bf16[128,1024]{1,0:T(8,128)(2,1)S(1)}, u32[]{:S(2)}, u32[]{:S(2)}) collective-permute-start(bf16[128,1024]{1,0:T(8,128)(2,1)} %pack_attention.1.refs_1_), channel_id=1, source_target_pairs={{0,4},{4,0},{8,12},{12,8},{16,20},{20,16},{24,28},{28,24},{1,5},{5... | collective-permute-start | bytes 786440 | tf_op jit(solution)/shard_map/ppermute | solution.py:91
  11.8 15.0 %collective-permute-start.8 = (bf16[128,1024]{1,0:T(8,128)(2,1)}, bf16[128,1024]{1,0:T(8,128)(2,1)}, u32[]{:S(2)}, u32[]{:S(2)}) collective-permute-start(bf16[128,1024]{1,0:T(8,128)(2,1)} %pack_attention.1.refs_1_), channel_id=1, source_target_pairs={{0,1},{1,0},{2,3},{3,2},{4,5},{5,4},{6,7},{7,6},{8,9},{9,8},{10,11... | collective-permute-start | bytes 786440 | tf_op jit(solution)/shard_map/ppermute | solution.py:86
  22.5 12.1 %collective-permute-start.6 = (bf16[128,1024]{1,0:T(8,128)(2,1)S(1)}, bf16[128,1024]{1,0:T(8,128)(2,1)S(1)}, u32[]{:S(2)}, u32[]{:S(2)}) collective-permute-start(bf16[128,1024]{1,0:T(8,128)(2,1)S(1)} %collective-permute-done.2.refs_3_), channel_id=1, source_target_pairs={{0,4},{4,0},{8,12},{12,8},{16,20},{20,16},{24,28},{28,24},{1,5},{5... | collective-permute-start | bytes 786440 | tf_op jit(solution)/shard_map/ppermute | solution.py:91
  23.0 13.0 %collective-permute-start.9 = (bf16[128,1024]{1,0:T(8,128)(2,1)S(1)}, bf16[128,1024]{1,0:T(8,128)(2,1)S(1)}, u32[]{:S(2)}, u32[]{:S(2)}) collective-permute-start(bf16[128,1024]{1,0:T(8,128)(2,1)S(1)} %collective-permute-done.1.refs_2_), channel_id=1, source_target_pairs={{0,1},{1,0},{2,3},{3,2},{4,5},{5,4},{6,7},{7,6},{8,9},{9,8},{10,11... | collective-permute-start | bytes 786440 | tf_op jit(solution)/shard_map/ppermute | solution.py:86
  26.8 27.3 %collective-permute-start.16 = (bf16[128,2048]{1,0:T(8,128)(2,1)}, bf16[128,2048]{1,0:T(8,128)(2,1)S(1)}, u32[]{:S(2)}, u32[]{:S(2)}) collective-permute-start(bf16[128,2048]{1,0:T(8,128)(2,1)} %pack_feed.1.refs_1_), channel_id=1, source_target_pairs={{0,16},{4,20},{8,24},{12,28},{16,0},{20,4},{24,8},{28,12},{1,17},{... | collective-permute-start | bytes 1572872 | tf_op jit(solution)/shard_map/ppermute | solution.py:91
  38.2 25.2 %collective-permute-start = (bf16[256,1024]{1,0:T(8,128)(2,1)S(1)}, bf16[256,1024]{1,0:T(8,128)(2,1)S(1)}, u32[]{:S(2)}, u32[]{:S(2)}) collective-permute-start(bf16[256,1024]{1,0:T(8,128)(2,1)S(1)} %get-tuple-element.317.refs_0_.refs_1_), channel_id=1, source_target_pairs={{0,2},{1,3},{2,0},{3,1},{4,6},{5,7},{6,4},{7,5},{8,10},{9,11},{10,... | collective-permute-start | bytes 1572872 | tf_op jit(solution)/shard_map/ppermute | solution.py:86
  41.9 23.0 %collective-permute-start.18 = (bf16[128,2048]{1,0:T(8,128)(2,1)}, bf16[128,2048]{1,0:T(8,128)(2,1)S(1)}, u32[]{:S(2)}, u32[]{:S(2)}) collective-permute-start(bf16[128,2048]{1,0:T(8,128)(2,1)} %pack_feed.1.refs_1_), channel_id=1, source_target_pairs={{0,8},{4,12},{8,0},{12,4},{16,24},{20,28},{24,16},{28,20},{1,9},{5... | collective-permute-start | bytes 1572872 | tf_op jit(solution)/shard_map/ppermute | solution.py:91
  42.1 17.7 %collective-permute-start.15 = (bf16[128,1024]{1,0:T(8,128)(2,1)}, bf16[128,1024]{1,0:T(8,128)(2,1)S(1)}, u32[]{:S(2)}, u32[]{:S(2)}) collective-permute-start(bf16[128,1024]{1,0:T(8,128)(2,1)} %collective-permute-done.7.refs_8_), channel_id=1, source_target_pairs={{0,1},{1,0},{2,3},{3,2},{4,5},{5,4},{6,7},{7,6},{8,9},{9,8},{10,11... | collective-permute-start | bytes 786440 | tf_op jit(solution)/shard_map/ppermute | solution.py:86
  44.3 30.1 %collective-permute-start.34 = (bf16[256,1024]{1,0:T(8,128)(2,1)S(1)}, bf16[256,1024]{1,0:T(8,128)(2,1)S(1)}, u32[]{:S(2)}, u32[]{:S(2)}) collective-permute-start(bf16[256,1024]{1,0:T(8,128)(2,1)S(1)} %get-tuple-element.318.refs_0_.refs_3_), channel_id=1, source_target_pairs={{0,2},{1,3},{2,0},{3,1},{4,6},{5,7},{6,4},{7,5},{8,10},{9,11},{10,... | collective-permute-start | bytes 1572872 | tf_op jit(solution)/shard_map/ppermute | solution.py:86
  54.1 20.3 %collective-permute-start.35 = (bf16[128,2048]{1,0:T(8,128)(2,1)}, bf16[128,2048]{1,0:T(8,128)(2,1)}, u32[]{:S(2)}, u32[]{:S(2)}) collective-permute-start(bf16[128,2048]{1,0:T(8,128)(2,1)} %pack_feed.1.refs_1_), channel_id=1, source_target_pairs={{0,4},{4,0},{8,12},{12,8},{16,20},{20,16},{24,28},{28,24},{1,5},{5... | collective-permute-start | bytes 1572872 | tf_op jit(solution)/shard_map/ppermute | solution.py:91
  71.3 18.9 %collective-permute-start.19 = (bf16[512,1024]{1,0:T(8,128)(2,1)}, bf16[512,1024]{1,0:T(8,128)(2,1)}, u32[]{:S(2)}, u32[]{:S(2)}) collective-permute-start(bf16[512,1024]{1,0:T(8,128)(2,1)} %get-tuple-element.151.refs_7_), channel_id=1, source_target_pairs={{0,1},{1,0},{2,3},{3,2},{4,5},{5,4},{6,7},{7,6},{8,9},{9,8},{10,11... | collective-permute-start | bytes 3145736 | tf_op jit(solution)/shard_map/ppermute | solution.py:86
  71.3 14.5 %collective-permute-start.20 = (bf16[128,2048]{1,0:T(8,128)(2,1)}, bf16[128,2048]{1,0:T(8,128)(2,1)S(1)}, u32[]{:S(2)}, u32[]{:S(2)}) collective-permute-start(bf16[128,2048]{1,0:T(8,128)(2,1)} %pack_feed.1.refs_1_), channel_id=1, source_target_pairs={{0,2},{1,3},{2,0},{3,1},{4,6},{5,7},{6,4},{7,5},{8,10},{9,11},{10,... | collective-permute-start | bytes 1572872 | tf_op jit(solution)/shard_map/ppermute | solution.py:86
  72.9 14.5 %collective-permute-start.29 = (bf16[128,2048]{1,0:T(8,128)(2,1)S(1)}, bf16[128,2048]{1,0:T(8,128)(2,1)}, u32[]{:S(2)}, u32[]{:S(2)}) collective-permute-start(bf16[128,2048]{1,0:T(8,128)(2,1)S(1)} %copy-done.87), channel_id=1, source_target_pairs={{0,4},{4,0},{8,12},{12,8},{16,20},{20,16},{24,28},{28,24},{1,5},{5... | collective-permute-start | bytes 1572872 | tf_op jit(solution)/shard_map/ppermute | solution.py:91
  74.4 13.7 %collective-permute-start.21 = (bf16[128,2048]{1,0:T(8,128)(2,1)S(1)}, bf16[128,2048]{1,0:T(8,128)(2,1)S(1)}, u32[]{:S(2)}, u32[]{:S(2)}) collective-permute-start(bf16[128,2048]{1,0:T(8,128)(2,1)S(1)} %copy-done.87), channel_id=1, source_target_pairs={{0,8},{4,12},{8,0},{12,4},{16,24},{20,28},{24,16},{28,20},{1,9},{5... | collective-permute-start | bytes 1572872 | tf_op jit(solution)/shard_map/ppermute | solution.py:91
  80.8 33.4 %collective-permute-start.36 = (bf16[512,1024]{1,0:T(8,128)(2,1)}, bf16[512,1024]{1,0:T(8,128)(2,1)}, u32[]{:S(2)}, u32[]{:S(2)}) collective-permute-start(bf16[512,1024]{1,0:T(8,128)(2,1)} %get-tuple-element.158), channel_id=1, source_target_pairs={{0,1},{1,0},{2,3},{3,2},{4,5},{5,4},{6,7},{7,6},{8,9},{9,8},{10,11... | collective-permute-start | bytes 3145736 | tf_op jit(solution)/shard_map/ppermute | solution.py:86
  85.9 21.6 %collective-permute-start.31 = (bf16[128,2048]{1,0:T(8,128)(2,1)S(1)}, bf16[128,2048]{1,0:T(8,128)(2,1)S(1)}, u32[]{:S(2)}, u32[]{:S(2)}) collective-permute-start(bf16[128,2048]{1,0:T(8,128)(2,1)S(1)} %copy-done.89), channel_id=1, source_target_pairs={{0,4},{4,0},{8,12},{12,8},{16,20},{20,16},{24,28},{28,24},{1,5},{5... | collective-permute-start | bytes 1572872 | tf_op jit(solution)/shard_map/ppermute | solution.py:91
  87.3 25.3 %collective-permute-start.24 = (bf16[128,2048]{1,0:T(8,128)(2,1)S(1)}, bf16[128,2048]{1,0:T(8,128)(2,1)}, u32[]{:S(2)}, u32[]{:S(2)}) collective-permute-start(bf16[128,2048]{1,0:T(8,128)(2,1)S(1)} %collective-permute-done.20.refs_6_.refs_1_), channel_id=1, source_target_pairs={{0,16},{4,20},{8,24},{12,28},{16,0},{20,4},{24,8},{28,12},{1,17},{... | collective-permute-start | bytes 1572872 | tf_op jit(solution)/shard_map/ppermute | solution.py:91
  88.1 26.1 %collective-permute-start.27 = (bf16[128,2048]{1,0:T(8,128)(2,1)S(1)}, bf16[128,2048]{1,0:T(8,128)(2,1)S(1)}, u32[]{:S(2)}, u32[]{:S(2)}) collective-permute-start(bf16[128,2048]{1,0:T(8,128)(2,1)S(1)} %collective-permute-done.20.refs_6_.refs_1_), channel_id=1, source_target_pairs={{0,8},{4,12},{8,0},{12,4},{16,24},{20,28},{24,16},{28,20},{1,9},{5... | collective-permute-start | bytes 1572872 | tf_op jit(solution)/shard_map/ppermute | solution.py:91
  90.2 37.6 %collective-permute-start.23 = (bf16[128,2048]{1,0:T(8,128)(2,1)S(1)}, bf16[128,2048]{1,0:T(8,128)(2,1)S(1)}, u32[]{:S(2)}, u32[]{:S(2)}) collective-permute-start(bf16[128,2048]{1,0:T(8,128)(2,1)S(1)} %collective-permute-done.21.refs_7_.refs_4_), channel_id=1, source_target_pairs={{0,4},{4,0},{8,12},{12,8},{16,20},{20,16},{24,28},{28,24},{1,5},{5... | collective-permute-start | bytes 1572872 | tf_op jit(solution)/shard_map/ppermute | solution.py:91
  107.5 33.0 %collective-permute-start.28 = (bf16[128,2048]{1,0:T(8,128)(2,1)}, bf16[128,2048]{1,0:T(8,128)(2,1)S(1)}, u32[]{:S(2)}, u32[]{:S(2)}) collective-permute-start(bf16[128,2048]{1,0:T(8,128)(2,1)} %copy-done.95), channel_id=1, source_target_pairs={{0,4},{4,0},{8,12},{12,8},{16,20},{20,16},{24,28},{28,24},{1,5},{5... | collective-permute-start | bytes 1572872 | tf_op jit(solution)/shard_map/ppermute | solution.py:91
  112.7 27.8 %collective-permute-start.30 = (bf16[128,2048]{1,0:T(8,128)(2,1)}, bf16[128,2048]{1,0:T(8,128)(2,1)S(1)}, u32[]{:S(2)}, u32[]{:S(2)}) collective-permute-start(bf16[128,2048]{1,0:T(8,128)(2,1)} %collective-permute-done.29.refs_6_), channel_id=1, source_target_pairs={{0,2},{1,3},{2,0},{3,1},{4,6},{5,7},{6,4},{7,5},{8,10},{9,11},{10,... | collective-permute-start | bytes 1572872 | tf_op jit(solution)/shard_map/ppermute | solution.py:86
  114.2 15.0 %collective-permute-start.25 = (bf16[128,2048]{1,0:T(8,128)(2,1)}, bf16[128,2048]{1,0:T(8,128)(2,1)S(1)}, u32[]{:S(2)}, u32[]{:S(2)}) collective-permute-start(bf16[128,2048]{1,0:T(8,128)(2,1)} %collective-permute-done.24.refs_8_.refs_2_), channel_id=1, source_target_pairs={{0,8},{4,12},{8,0},{12,4},{16,24},{20,28},{24,16},{28,20},{1,9},{5... | collective-permute-start | bytes 1572872 | tf_op jit(solution)/shard_map/ppermute | solution.py:91
  114.2 24.7 %collective-permute-start.22 = (bf16[256,1024]{1,0:T(8,128)(2,1)}, bf16[256,1024]{1,0:T(8,128)(2,1)S(1)}, u32[]{:S(2)}, u32[]{:S(2)}) collective-permute-start(bf16[256,1024]{1,0:T(8,128)(2,1)} %get-tuple-element.153), channel_id=1, source_target_pairs={{0,2},{1,3},{2,0},{3,1},{4,6},{5,7},{6,4},{7,5},{8,10},{9,11},{10,... | collective-permute-start | bytes 1572872 | tf_op jit(solution)/shard_map/ppermute | solution.py:86
  127.8 21.3 %collective-permute-start.37 = (bf16[256,1024]{1,0:T(8,128)(2,1)}, bf16[256,1024]{1,0:T(8,128)(2,1)S(1)}, u32[]{:S(2)}, u32[]{:S(2)}) collective-permute-start(bf16[256,1024]{1,0:T(8,128)(2,1)} %get-tuple-element.160), channel_id=1, source_target_pairs={{0,2},{1,3},{2,0},{3,1},{4,6},{5,7},{6,4},{7,5},{8,10},{9,11},{10,... | collective-permute-start | bytes 1572872 | tf_op jit(solution)/shard_map/ppermute | solution.py:86
  140.5 17.4 %collective-permute-start.26 = (bf16[256,1024]{1,0:T(8,128)(2,1)S(1)}, bf16[256,1024]{1,0:T(8,128)(2,1)S(1)}, u32[]{:S(2)}, u32[]{:S(2)}) collective-permute-start(bf16[256,1024]{1,0:T(8,128)(2,1)S(1)} %get-tuple-element.155.refs_8_.refs_0_.refs_1_), channel_id=1, source_target_pairs={{0,1},{1,0},{2,3},{3,2},{4,5},{5,4},{6,7},{7,6},{8,9},{9,8},{10,11... | collective-permute-start | bytes 1572872 | tf_op jit(solution)/shard_map/ppermute | solution.py:86
  149.7 17.8 %collective-permute-start.38 = (bf16[256,1024]{1,0:T(8,128)(2,1)S(1)}, bf16[256,1024]{1,0:T(8,128)(2,1)S(1)}, u32[]{:S(2)}, u32[]{:S(2)}) collective-permute-start(bf16[256,1024]{1,0:T(8,128)(2,1)S(1)} %get-tuple-element.161.refs_0_.refs_3_), channel_id=1, source_target_pairs={{0,1},{1,0},{2,3},{3,2},{4,5},{5,4},{6,7},{7,6},{8,9},{9,8},{10,11... | collective-permute-start | bytes 1572872 | tf_op jit(solution)/shard_map/ppermute | solution.py:86
  149.8 27.3 %collective-permute-start.32 = (bf16[128,2048]{1,0:T(8,128)(2,1)S(1)}, bf16[128,2048]{1,0:T(8,128)(2,1)S(1)}, u32[]{:S(2)}, u32[]{:S(2)}) collective-permute-start(bf16[128,2048]{1,0:T(8,128)(2,1)S(1)} %copy-done.92), channel_id=1, source_target_pairs={{0,2},{1,3},{2,0},{3,1},{4,6},{5,7},{6,4},{7,5},{8,10},{9,11},{10,... | collective-permute-start | bytes 1572872 | tf_op jit(solution)/shard_map/ppermute | solution.py:86
  151.3 25.7 %collective-permute-start.33 = (bf16[128,2048]{1,0:T(8,128)(2,1)S(1)}, bf16[128,2048]{1,0:T(8,128)(2,1)}, u32[]{:S(2)}, u32[]{:S(2)}) collective-permute-start(bf16[128,2048]{1,0:T(8,128)(2,1)S(1)} %collective-permute-done.23.refs_6_.refs_8_), channel_id=1, source_target_pairs={{0,2},{1,3},{2,0},{3,1},{4,6},{5,7},{6,4},{7,5},{8,10},{9,11},{10,... | collective-permute-start | bytes 1572872 | tf_op jit(solution)/shard_map/ppermute | solution.py:86
  151.9 30.4 %collective-permute-start.39 = (f32[1024]{0:T(1024)S(1)}, f32[1024]{0:T(1024)S(1)}, u32[]{:S(2)}, u32[]{:S(2)}) collective-permute-start(f32[1024]{0:T(1024)S(1)} %copy-done.117), channel_id=1, source_target_pairs={{0,2},{1,3},{2,0},{3,1},{4,6},{5,7},{6,4},{7,5},{8,10},{9,11},{10,... | collective-permute-start | bytes 12296 | tf_op jit(solution)/shard_map/ppermute | solution.py:86
  209.0 12.8 %collective-permute-start.44 = (bf16[256,1024]{1,0:T(8,128)(2,1)S(1)}, bf16[256,1024]{1,0:T(8,128)(2,1)S(1)}, u32[]{:S(2)}, u32[]{:S(2)}) collective-permute-start(bf16[256,1024]{1,0:T(8,128)(2,1)S(1)} %get-tuple-element.178.refs_0_.refs_3_), channel_id=1, source_target_pairs={{0,1},{1,0},{2,3},{3,2},{4,5},{5,4},{6,7},{7,6},{8,9},{9,8},{10,11... | collective-permute-start | bytes 1572872 | tf_op jit(solution)/shard_map/ppermute | solution.py:86
  221.3 22.7 %collective-permute-start.43 = (bf16[256,1024]{1,0:T(8,128)(2,1)}, bf16[256,1024]{1,0:T(8,128)(2,1)S(1)}, u32[]{:S(2)}, u32[]{:S(2)}) collective-permute-start(bf16[256,1024]{1,0:T(8,128)(2,1)} %get-tuple-element.177), channel_id=1, source_target_pairs={{0,1},{1,0},{2,3},{3,2},{4,5},{5,4},{6,7},{7,6},{8,9},{9,8},{10,11... | collective-permute-start | bytes 1572872 | tf_op jit(solution)/shard_map/ppermute | solution.py:86
  234.0 17.7 %collective-permute-start.46 = (bf16[256,1024]{1,0:T(8,128)(2,1)}, bf16[256,1024]{1,0:T(8,128)(2,1)S(1)}, u32[]{:S(2)}, u32[]{:S(2)}) collective-permute-start(bf16[256,1024]{1,0:T(8,128)(2,1)} %get-tuple-element.195), channel_id=1, source_target_pairs={{0,1},{1,0},{2,3},{3,2},{4,5},{5,4},{6,7},{7,6},{8,9},{9,8},{10,11... | collective-permute-start | bytes 1572872 | tf_op jit(solution)/shard_map/ppermute | solution.py:86
  247.1 20.6 %collective-permute-start.45 = (bf16[256,1024]{1,0:T(8,128)(2,1)S(1)}, bf16[256,1024]{1,0:T(8,128)(2,1)}, u32[]{:S(2)}, u32[]{:S(2)}) collective-permute-start(bf16[256,1024]{1,0:T(8,128)(2,1)S(1)} %get-tuple-element.188.refs_9_.refs_4_.refs_1_), channel_id=1, source_target_pairs={{0,2},{1,3},{2,0},{3,1},{4,6},{5,7},{6,4},{7,5},{8,10},{9,11},{10,... | collective-permute-start | bytes 1572872 | tf_op jit(solution)/shard_map/ppermute | solution.py:86
  249.7 51.4 %collective-permute-start.49 = (bf16[512,1024]{1,0:T(8,128)(2,1)S(1)}, bf16[512,1024]{1,0:T(8,128)(2,1)}, u32[]{:S(2)}, u32[]{:S(2)}) collective-permute-start(bf16[512,1024]{1,0:T(8,128)(2,1)S(1)} %copy-done.18), channel_id=1, source_target_pairs={{0,4},{4,0},{8,12},{12,8},{16,20},{20,16},{24,28},{28,24},{1,5},{5... | collective-permute-start | bytes 3145736 | tf_op jit(solution)/shard_map/ppermute | solution.py:91
  250.7 82.4 %collective-permute-start.51 = (bf16[512,1024]{1,0:T(8,128)(2,1)}, bf16[512,1024]{1,0:T(8,128)(2,1)S(1)}, u32[]{:S(2)}, u32[]{:S(2)}) collective-permute-start(bf16[512,1024]{1,0:T(8,128)(2,1)} %get-tuple-element.213), channel_id=1, source_target_pairs={{0,4},{4,0},{8,12},{12,8},{16,20},{20,16},{24,28},{28,24},{1,5},{5... | collective-permute-start | bytes 3145736 | tf_op jit(solution)/shard_map/ppermute | solution.py:91
  256.0 39.8 %collective-permute-start.48 = (bf16[256,1024]{1,0:T(8,128)(2,1)S(1)}, bf16[256,1024]{1,0:T(8,128)(2,1)S(1)}, u32[]{:S(2)}, u32[]{:S(2)}) collective-permute-start(bf16[256,1024]{1,0:T(8,128)(2,1)S(1)} %get-tuple-element.196.refs_10_.refs_3_.refs_4_), channel_id=1, source_target_pairs={{0,2},{1,3},{2,0},{3,1},{4,6},{5,7},{6,4},{7,5},{8,10},{9,11},{10,... | collective-permute-start | bytes 1572872 | tf_op jit(solution)/shard_map/ppermute | solution.py:86
  267.7 36.8 %collective-permute-start.50 = (bf16[512,1024]{1,0:T(8,128)(2,1)}, bf16[512,1024]{1,0:T(8,128)(2,1)S(1)}, u32[]{:S(2)}, u32[]{:S(2)}) collective-permute-start(bf16[512,1024]{1,0:T(8,128)(2,1)} %get-tuple-element.197.refs_8_), channel_id=1, source_target_pairs={{0,8},{4,12},{8,0},{12,4},{16,24},{20,28},{24,16},{28,20},{1,9},{5... | collective-permute-start | bytes 3145736 | tf_op jit(solution)/shard_map/ppermute | solution.py:91
  267.7 66.8 %collective-permute-start.52 = (bf16[512,1024]{1,0:T(8,128)(2,1)}, bf16[512,1024]{1,0:T(8,128)(2,1)S(1)}, u32[]{:S(2)}, u32[]{:S(2)}) collective-permute-start(bf16[512,1024]{1,0:T(8,128)(2,1)} %get-tuple-element.217), channel_id=1, source_target_pairs={{0,8},{4,12},{8,0},{12,4},{16,24},{20,28},{24,16},{28,20},{1,9},{5... | collective-permute-start | bytes 3145736 | tf_op jit(solution)/shard_map/ppermute | solution.py:91
  295.9 51.6 %collective-permute-start.47 = (bf16[512,1024]{1,0:T(8,128)(2,1)}, bf16[512,1024]{1,0:T(8,128)(2,1)}, u32[]{:S(2)}, u32[]{:S(2)}) collective-permute-start(bf16[512,1024]{1,0:T(8,128)(2,1)} %get-tuple-element.200), channel_id=1, source_target_pairs={{0,1},{1,0},{2,3},{3,2},{4,5},{5,4},{6,7},{7,6},{8,9},{9,8},{10,11... | collective-permute-start | bytes 3145736 | tf_op jit(solution)/shard_map/ppermute | solution.py:86
  332.9 24.2 %collective-permute-start.55 = (bf16[512,1024]{1,0:T(8,128)(2,1)}, bf16[512,1024]{1,0:T(8,128)(2,1)}, u32[]{:S(2)}, u32[]{:S(2)}) collective-permute-start(bf16[512,1024]{1,0:T(8,128)(2,1)} %get-tuple-element.222), channel_id=1, source_target_pairs={{0,1},{1,0},{2,3},{3,2},{4,5},{5,4},{6,7},{7,6},{8,9},{9,8},{10,11... | collective-permute-start | bytes 3145736 | tf_op jit(solution)/shard_map/ppermute | solution.py:86
  332.9 14.5 %collective-permute-start.53 = (bf16[256,1024]{1,0:T(8,128)(2,1)}, bf16[256,1024]{1,0:T(8,128)(2,1)S(1)}, u32[]{:S(2)}, u32[]{:S(2)}) collective-permute-start(bf16[256,1024]{1,0:T(8,128)(2,1)} %get-tuple-element.219), channel_id=1, source_target_pairs={{0,8},{4,12},{8,0},{12,4},{16,24},{20,28},{24,16},{28,20},{1,9},{5... | collective-permute-start | bytes 1572872 | tf_op jit(solution)/shard_map/ppermute | solution.py:91
  334.0 14.4 %collective-permute-start.54 = (bf16[256,1024]{1,0:T(8,128)(2,1)}, bf16[256,1024]{1,0:T(8,128)(2,1)S(1)}, u32[]{:S(2)}, u32[]{:S(2)}) collective-permute-start(bf16[256,1024]{1,0:T(8,128)(2,1)} %get-tuple-element.220), channel_id=1, source_target_pairs={{0,4},{4,0},{8,12},{12,8},{16,20},{20,16},{24,28},{28,24},{1,5},{5... | collective-permute-start | bytes 1572872 | tf_op jit(solution)/shard_map/ppermute | solution.py:91
  335.6 18.1 %collective-permute-start.72 = (bf16[1024,256]{1,0:T(8,128)(2,1)}, bf16[1024,256]{1,0:T(8,128)(2,1)}, u32[]{:S(2)}, u32[]{:S(2)}) collective-permute-start(bf16[1024,256]{1,0:T(8,128)(2,1)} %get-tuple-element.210.refs_10_), channel_id=1, source_target_pairs={{0,1},{1,0},{2,3},{3,2},{4,5},{5,4},{6,7},{7,6},{8,9},{9,8},{10,11... | collective-permute-start | bytes 1572872 | tf_op jit(solution)/shard_map/ppermute | solution.py:86
  353.6 11.9 %collective-permute-start.58 = (bf16[1024,256]{1,0:T(8,128)(2,1)}, bf16[1024,256]{1,0:T(8,128)(2,1)S(1)}, u32[]{:S(2)}, u32[]{:S(2)}) collective-permute-start(bf16[1024,256]{1,0:T(8,128)(2,1)} %get-tuple-element.221.refs_5_.refs_2_), channel_id=1, source_target_pairs={{0,1},{1,0},{2,3},{3,2},{4,5},{5,4},{6,7},{7,6},{8,9},{9,8},{10,11... | collective-permute-start | bytes 1572872 | tf_op jit(solution)/shard_map/ppermute | solution.py:86
  355.5 41.6 %collective-permute-start.73 = (bf16[512,256]{1,0:T(8,128)(2,1)}, bf16[512,256]{1,0:T(8,128)(2,1)S(1)}, u32[]{:S(2)}, u32[]{:S(2)}) collective-permute-start(bf16[512,256]{1,0:T(8,128)(2,1)} %get-tuple-element.264), channel_id=1, source_target_pairs={{0,4},{4,0},{8,12},{12,8},{16,20},{20,16},{24,28},{28,24},{1,5},{5... | collective-permute-start | bytes 786440 | tf_op jit(solution)/shard_map/ppermute | solution.py:91
  363.4 14.4 %collective-permute-start.56 = (bf16[256,1024]{1,0:T(8,128)(2,1)}, bf16[256,1024]{1,0:T(8,128)(2,1)}, u32[]{:S(2)}, u32[]{:S(2)}) collective-permute-start(bf16[256,1024]{1,0:T(8,128)(2,1)} %get-tuple-element.224), channel_id=1, source_target_pairs={{0,2},{1,3},{2,0},{3,1},{4,6},{5,7},{6,4},{7,5},{8,10},{9,11},{10,... | collective-permute-start | bytes 1572872 | tf_op jit(solution)/shard_map/ppermute | solution.py:86
  365.6 32.6 %collective-permute-start.59 = (bf16[512,256]{1,0:T(8,128)(2,1)S(1)}, bf16[512,256]{1,0:T(8,128)(2,1)S(1)}, u32[]{:S(2)}, u32[]{:S(2)}) collective-permute-start(bf16[512,256]{1,0:T(8,128)(2,1)S(1)} %get-tuple-element.233), channel_id=1, source_target_pairs={{0,8},{4,12},{8,0},{12,4},{16,24},{20,28},{24,16},{28,20},{1,9},{5... | collective-permute-start | bytes 786440 | tf_op jit(solution)/shard_map/ppermute | solution.py:91
  367.4 32.7 %collective-permute-start.63 = (bf16[256,1024]{1,0:T(8,128)(2,1)}, bf16[256,1024]{1,0:T(8,128)(2,1)S(1)}, u32[]{:S(2)}, u32[]{:S(2)}) collective-permute-start(bf16[256,1024]{1,0:T(8,128)(2,1)} %copy-done.80), channel_id=1, source_target_pairs={{0,8},{4,12},{8,0},{12,4},{16,24},{20,28},{24,16},{28,20},{1,9},{5... | collective-permute-start | bytes 1572872 | tf_op jit(solution)/shard_map/ppermute | solution.py:91
  368.7 33.1 %collective-permute-start.64 = (bf16[256,1024]{1,0:T(8,128)(2,1)}, bf16[256,1024]{1,0:T(8,128)(2,1)S(1)}, u32[]{:S(2)}, u32[]{:S(2)}) collective-permute-start(bf16[256,1024]{1,0:T(8,128)(2,1)} %copy-done.79), channel_id=1, source_target_pairs={{0,4},{4,0},{8,12},{12,8},{16,20},{20,16},{24,28},{28,24},{1,5},{5... | collective-permute-start | bytes 1572872 | tf_op jit(solution)/shard_map/ppermute | solution.py:91
  377.8 20.4 %collective-permute-start.83 = (f32[96,128]{1,0:T(8,128)S(1)}, f32[96,128]{1,0:T(8,128)S(1)}, u32[]{:S(2)}, u32[]{:S(2)}) collective-permute-start(f32[96,128]{1,0:T(8,128)S(1)} %plus.5.refs_0_), channel_id=1, source_target_pairs={{0,2},{1,3},{2,0},{3,1},{4,6},{5,7},{6,4},{7,5},{8,10},{9,11},{10,... | collective-permute-start | bytes 147464 | tf_op jit(solution)/shard_map/ppermute | solution.py:86
  397.1 13.0 %collective-permute-start.57 = (bf16[256,1024]{1,0:T(8,128)(2,1)S(1)}, bf16[256,1024]{1,0:T(8,128)(2,1)S(1)}, u32[]{:S(2)}, u32[]{:S(2)}) collective-permute-start(bf16[256,1024]{1,0:T(8,128)(2,1)S(1)} %copy-done.124), channel_id=1, source_target_pairs={{0,2},{1,3},{2,0},{3,1},{4,6},{5,7},{6,4},{7,5},{8,10},{9,11},{10,... | collective-permute-start | bytes 1572872 | tf_op jit(solution)/shard_map/ppermute | solution.py:86
  398.2 13.9 %collective-permute-start.62 = (bf16[1024,256]{1,0:T(8,128)(2,1)}, bf16[1024,256]{1,0:T(8,128)(2,1)S(1)}, u32[]{:S(2)}, u32[]{:S(2)}) collective-permute-start(bf16[1024,256]{1,0:T(8,128)(2,1)} %get-tuple-element.243), channel_id=1, source_target_pairs={{0,1},{1,0},{2,3},{3,2},{4,5},{5,4},{6,7},{7,6},{8,9},{9,8},{10,11... | collective-permute-start | bytes 1572872 | tf_op jit(solution)/shard_map/ppermute | solution.py:86
  398.2 14.9 %collective-permute-start.68 = (bf16[1024,256]{1,0:T(8,128)(2,1)}, bf16[1024,256]{1,0:T(8,128)(2,1)S(1)}, u32[]{:S(2)}, u32[]{:S(2)}) collective-permute-start(bf16[1024,256]{1,0:T(8,128)(2,1)} %get-tuple-element.255), channel_id=1, source_target_pairs={{0,1},{1,0},{2,3},{3,2},{4,5},{5,4},{6,7},{7,6},{8,9},{9,8},{10,11... | collective-permute-start | bytes 1572872 | tf_op jit(solution)/shard_map/ppermute | solution.py:86
  400.2 15.5 %collective-permute-start.84 = (f32[96,128]{1,0:T(8,128)S(1)}, f32[96,128]{1,0:T(8,128)S(1)}, u32[]{:S(2)}, u32[]{:S(2)}) collective-permute-start(f32[96,128]{1,0:T(8,128)S(1)} %plus.6.refs_0_), channel_id=1, source_target_pairs={{0,4},{4,0},{8,12},{12,8},{16,20},{20,16},{24,28},{28,24},{1,5},{5... | collective-permute-start | bytes 147464 | tf_op jit(solution)/shard_map/ppermute | solution.py:91
  407.1 55.9 %collective-permute-start.76 = (bf16[128,1024]{1,0:T(8,128)(2,1)}, bf16[128,1024]{1,0:T(8,128)(2,1)}, u32[]{:S(2)}, u32[]{:S(2)}) collective-permute-start(bf16[128,1024]{1,0:T(8,128)(2,1)} %get-tuple-element.269), channel_id=1, source_target_pairs={{0,16},{4,20},{8,24},{12,28},{16,0},{20,4},{24,8},{28,12},{1,17},{... | collective-permute-start | bytes 786440 | tf_op jit(solution)/shard_map/ppermute | solution.py:91
  410.1 60.5 %collective-permute-start.79 = (bf16[128,1024]{1,0:T(8,128)(2,1)}, bf16[128,1024]{1,0:T(8,128)(2,1)S(1)}, u32[]{:S(2)}, u32[]{:S(2)}) collective-permute-start(bf16[128,1024]{1,0:T(8,128)(2,1)} %get-tuple-element.271), channel_id=1, source_target_pairs={{0,16},{4,20},{8,24},{12,28},{16,0},{20,4},{24,8},{28,12},{1,17},{... | collective-permute-start | bytes 786440 | tf_op jit(solution)/shard_map/ppermute | solution.py:91
  412.1 11.7 %collective-permute-start.74 = (bf16[256,256]{1,0:T(8,128)(2,1)S(1)}, bf16[256,256]{1,0:T(8,128)(2,1)S(1)}, u32[]{:S(2)}, u32[]{:S(2)}) collective-permute-start(bf16[256,256]{1,0:T(8,128)(2,1)S(1)} %get-tuple-element.266), channel_id=1, source_target_pairs={{0,8},{4,12},{8,0},{12,4},{16,24},{20,28},{24,16},{28,20},{1,9},{5... | collective-permute-start | bytes 393224 | tf_op jit(solution)/shard_map/ppermute | solution.py:91
  413.2 29.0 %collective-permute-start.61 = (bf16[128,256]{1,0:T(8,128)(2,1)S(1)}, bf16[128,256]{1,0:T(8,128)(2,1)S(1)}, u32[]{:S(2)}, u32[]{:S(2)}) collective-permute-start(bf16[128,256]{1,0:T(8,128)(2,1)S(1)} %get-tuple-element.242), channel_id=1, source_target_pairs={{0,16},{4,20},{8,24},{12,28},{16,0},{20,4},{24,8},{28,12},{1,17},{... | collective-permute-start | bytes 196616 | tf_op jit(solution)/shard_map/ppermute | solution.py:91
  416.4 25.8 %collective-permute-start.85 = (f32[96,128]{1,0:T(8,128)S(1)}, f32[96,128]{1,0:T(8,128)S(1)}, u32[]{:S(2)}, u32[]{:S(2)}) collective-permute-start(f32[96,128]{1,0:T(8,128)S(1)} %plus.7.refs_0_), channel_id=1, source_target_pairs={{0,8},{4,12},{8,0},{12,4},{16,24},{20,28},{24,16},{28,20},{1,9},{5... | collective-permute-start | bytes 147464 | tf_op jit(solution)/shard_map/ppermute | solution.py:91
  423.8 41.4 %collective-permute-start.77 = (bf16[128,1024]{1,0:T(8,128)(2,1)}, bf16[128,1024]{1,0:T(8,128)(2,1)}, u32[]{:S(2)}, u32[]{:S(2)}) collective-permute-start(bf16[128,1024]{1,0:T(8,128)(2,1)} %get-tuple-element.270), channel_id=1, source_target_pairs={{0,16},{4,20},{8,24},{12,28},{16,0},{20,4},{24,8},{28,12},{1,17},{... | collective-permute-start | bytes 786440 | tf_op jit(solution)/shard_map/ppermute | solution.py:91
  442.2 26.5 %collective-permute-start.80 = (bf16[128,1024]{1,0:T(8,128)(2,1)}, bf16[128,1024]{1,0:T(8,128)(2,1)}, u32[]{:S(2)}, u32[]{:S(2)}) collective-permute-start(bf16[128,1024]{1,0:T(8,128)(2,1)} %get-tuple-element.272), channel_id=1, source_target_pairs={{0,16},{4,20},{8,24},{12,28},{16,0},{20,4},{24,8},{28,12},{1,17},{... | collective-permute-start | bytes 786440 | tf_op jit(solution)/shard_map/ppermute | solution.py:91
  442.2 18.3 %collective-permute-start.75 = (bf16[128,256]{1,0:T(8,128)(2,1)S(1)}, bf16[128,256]{1,0:T(8,128)(2,1)S(1)}, u32[]{:S(2)}, u32[]{:S(2)}) collective-permute-start(bf16[128,256]{1,0:T(8,128)(2,1)S(1)} %get-tuple-element.268), channel_id=1, source_target_pairs={{0,16},{4,20},{8,24},{12,28},{16,0},{20,4},{24,8},{28,12},{1,17},{... | collective-permute-start | bytes 196616 | tf_op jit(solution)/shard_map/ppermute | solution.py:91
  (148 other events, 1204.6 us)

commit v6 on v5

--- a/solution.py
+++ b/solution.py
@@ -13,6 +13,7 @@
 MIB = 1024 * 1024
 VMEM_LIMIT = 56 * MIB
 SMALL_LIMIT = 16 * MIB
+FOLD_LIMIT = 24 * MIB
 UNDERSTATED = 1000
 
 F32 = jnp.float32
@@ -103,14 +104,21 @@
 
 
 def gather_far(rows):
-    pieces = [(rows, [0])]
+    held = (rows, [0])
+    steps = []
     step = lax.axis_size("dp") // 2
     while step > 1:
-        if len(pieces) > 2:
-            pieces = [merged(pieces)]
-        pieces += [(swap_dp(p, step), [o ^ step for o in offsets]) for p, offsets in pieces]
+        steps.append(step)
         step //= 2
-    return pieces
+    first = []
+    for step in steps[:-1]:
+        came = (swap_dp(held[0], step), [o ^ step for o in held[1]])
+        first.append(came[0])
+        held = merged([held, came])
+    pieces = [held]
+    if steps:
+        pieces.append((swap_dp(held[0], steps[-1]), [o ^ steps[-1] for o in held[1]]))
+    return pieces, first[:1]
 
 
 def merged(pieces):
@@ -166,21 +174,45 @@
 
 
 def fold(keep, came, last, deps):
-    rows, width = keep.shape
+    groups, rows, width = keep.shape
 
     def kernel(k_ref, c_ref, *refs):
         if last:
             refs[0][...] = k_ref[...] + c_ref[...].astype(F32)
         else:
             half = rows // 2
-            refs[0][...] = k_ref[:half] + c_ref[:half].astype(F32)
-            refs[1][...] = (k_ref[half:] + c_ref[half:].astype(F32)).astype(BF16)
-
-    outs = [shape((rows, width), F32)]
+            refs[0][...] = k_ref[:, :half] + c_ref[:, :half].astype(F32)
+            refs[1][...] = (k_ref[:, half:] + c_ref[:, half:].astype(F32)).astype(BF16)
+
+    outs = [shape(keep.shape, F32)]
     if not last:
-        outs = [shape((rows // 2, width), F32), shape((rows // 2, width), BF16)]
+        half_dims = (groups, rows // 2, width)
+        outs = [shape(half_dims, F32), shape(half_dims, BF16)]
     return whole_call(
-        kernel, outs, [keep, came], rows * width, "fold", deps=deps, limit=SMALL_LIMIT
+        kernel, outs, [keep, came], groups * rows * width, "fold", deps=deps, limit=FOLD_LIMIT
+    )
+
+
+def fold_core(pairs, deps):
+    rows, width = pairs[0][0].shape
+    half = rows // 2
+
+    def kernel(*refs):
+        for i in range(len(pairs)):
+            mine, got = refs[2 * i : 2 * i + 2]
+            refs[-2][i] = mine[:half] + got[:half].astype(F32)
+            refs[-1][i] = (mine[half:] + got[half:].astype(F32)).astype(BF16)
+
+    dims = (len(pairs), half, width)
+    args = [array for pair in pairs for array in pair]
+    return whole_call(
+        kernel,
+        [shape(dims, F32), shape(dims, BF16)],
+        args,
+        len(pairs) * rows * width,
+        "fold_core",
+        deps=deps,
+        limit=FOLD_LIMIT,
     )
 
 
@@ -664,38 +696,44 @@
                 turned[:, i * block : (i + 1) * block] = ref[...].T
 
         place = place_ref[0]
-        each = 4 if halves else 2
-
-        def write(targets, order):
+
+        def write(which, targets, order):
             for i, offset in enumerate(order):
                 start = pl.multiple_of((place ^ offset) * share, share)
                 at = i * share
-                ref = targets[0] if len(targets) == 1 or at < half else targets[1]
-                at = at if len(targets) == 1 or at < half else at - half
-                ref[at : at + share, :] = full[pl.ds(start, share), :].astype(ref.dtype)
+                rows_now = full[pl.ds(start, share), :]
+                if halves:
+                    ref = targets[0] if at < half else targets[1]
+                    at %= half
+                    ref[which, at : at + share, :] = rows_now.astype(ref.dtype)
+                else:
+                    targets[which][at : at + share, :] = rows_now.astype(targets[which].dtype)
 
         for which, (one, two) in enumerate(((m0, m1), (o0, o1))):
             full[...] = dot(turned[:, :rows], one[...]) + dot(turned[:, rows:], two[...])
             for c, (_, bits) in enumerate(chains):
-                per = each // 2
-                targets = refs[c * each + which * per : c * each + (which + 1) * per]
+                targets = refs[2 * c : 2 * c + 2]
                 order = halving_order(size, bits)
                 if len(chains) == 1:
-                    write(targets, order)
+                    write(which, targets, order)
                 else:
-                    pl.when(step // tiles == c)(lambda t=targets, o=order: write(t, o))
+                    pl.when(step // tiles == c)(
+                        lambda w=which, t=targets, o=order: write(w, t, o)
+                    )
 
     base = other_first // tile
     column = pl.BlockSpec((rows, tile), lambda i: (0, i))
     other_column = pl.BlockSpec((rows, tile), lambda i: (0, base + i))
     outs, out_specs = [], []
     for c in range(len(chains)):
-        index = lambda i, c=c: (0, jnp.clip(i - c * tiles, 0, tiles - 1))
-        for kinds in ((F32, BF16), (F32, BF16)) if halves else ((F32,), (BF16,)):
-            for kind in kinds:
-                held = half if halves else width
-                outs.append(shape((held, count), kind))
-                out_specs.append(pl.BlockSpec((held, tile), index))
+        for kind in (F32, BF16):
+            if halves:
+                outs.append(shape((2, half, count), kind))
+                out_specs.append(pl.BlockSpec((2, half, tile), lambda i: (0, 0, i)))
+            else:
+                index = lambda i, c=c: (0, jnp.clip(i - c * tiles, 0, tiles - 1))
+                outs.append(shape((width, count), kind))
+                out_specs.append(pl.BlockSpec((width, tile), index))
     return streamed_call(
         kernel,
         (tiles * len(chains),),
@@ -713,8 +751,9 @@
     )
 
 
-def core_chain(mine, other, bits, deps=()):
-    keep, send = fold(mine, swap_tensor(other, CORE), False, list(deps))
+def core_chain(made, bits, deps=()):
+    pairs = [(mine, swap_tensor(other, CORE)) for mine, other in made]
+    keep, send = fold_core(pairs, list(deps))
     return Chain(keep, send, bits)
 
 
@@ -757,16 +796,17 @@
     row = lambda vector: vector.reshape(1, -1)
 
     x_own = [inputs[s] for s in seqs]
-    x_across = [swap_tensor(x_own[s], ACROSS) for s in seqs]
+    all_across = swap_tensor(inputs, ACROSS)
+    x_across = [all_across[s] for s in seqs]
 
     dp_place = lax.axis_index("dp").astype(jnp.int32).reshape(1)
-    att_far = gather_far(pack([w_query, w_key, w_value, w_out.T], "pack_attention"))
+    att_far, att_first = gather_far(pack([w_query, w_key, w_value, w_out.T], "pack_attention"))
     att_pieces = att_far + gather_near(att_far)
-    share = pack([w_up, w_down.T], "pack_feed", [p for p, _ in att_far[1:2]])
+    share = pack([w_up, w_down.T], "pack_feed", att_first)
     share_other = swap_tensor(share, ACROSS)
-    mine_far = gather_far(share)
+    mine_far, mine_first = gather_far(share)
     mine_near = gather_near(mine_far)
-    other_far = gather_far(share_other)
+    other_far, other_first = gather_far(share_other)
     other_near = gather_near(other_far[:1]) + [
         (swap_tensor(p, ACROSS), offsets) for p, offsets in mine_near[1:]
     ]
@@ -775,15 +815,10 @@
         return [p for p, _ in pieces]
 
     att_mine = assemble(att_pieces, dp_place, "assemble_attention")
-    att_other = assemble(
-        other_core(att_pieces), dp_place, "assemble_attention_other", arrays(mine_far[1:2])
-    )
-    project_waits = [arrays(mine_far[2:3]), arrays(mine_near[:1])]
-    attend_waits = [
-        [share_other] + arrays(mine_far[3:]),
-        arrays(mine_near[1:3] + other_far[1:3]),
-    ]
-    norm_waits = [arrays(mine_near[3:] + other_far[3:]), arrays(other_near[:2])]
+    att_other = assemble(other_core(att_pieces), dp_place, "assemble_attention_other")
+    project_waits = [mine_first, [share_other]]
+    attend_waits = [arrays(mine_far[1:]), arrays(mine_near[:1]) + other_first]
+    norm_waits = [arrays(mine_near[1:]), arrays(other_far[1:])]
     ffw_mine = assemble(mine_far + mine_near, dp_place, "assemble_feed")
 
     biases = jnp.concatenate([b_query, jnp.zeros_like(b_query), b_value])
@@ -853,14 +888,25 @@
         for s in seqs
     ]
     grad_far = [swap_tensor(two[s][2], CORE) for s in seqs]
-    fed_back = []
-    for s in seqs:
-        waits = [p[2] for p in fed_back[-1:]]
-        fed_back.append(
-            feed_forward_back(
-                two[s][2], grad_far[s], ffw_mine, ffw_other, fed[s][2], fed[s][3], waits
-            )
-        )
+    levels = range(lax.axis_size("dp").bit_length() - 1)
+    near_first = list(levels)
+    far_first = [1, 0, *levels[2:]] if len(near_first) > 1 else near_first
+
+    def pairs(own, across):
+        return [part for s in seqs for part in (own[s], across[s])]
+
+    def feed_back(s, deps):
+        return feed_forward_back(
+            two[s][2], grad_far[s], ffw_mine, ffw_other, fed[s][2], fed[s][3], deps
+        )
+
+    fed_back = [feed_back(0, [])]
+    down_made = weight_grad(
+        pairs([two[s][2] for s in seqs], grad_far),
+        [fed[s][0] for s in seqs], [fed[s][1] for s in seqs],
+        dp_place, [(hidden, near_first)], "w_down_grad", deps=[fed_back[0][2]], halves=True,
+    )
+    fed_back += [feed_back(s, [down_made[1]]) for s in seqs[1:]]
     back_got = [swap_tensor(fed_back[s][3], CORE) for s in seqs]
     def placed_in(part_mine, part_other, bit):
         size = part_mine.shape[0]
@@ -868,34 +914,20 @@
         empty = lax.dynamic_update_slice(empty, part_mine, (place * size,))
         return lax.dynamic_update_slice(empty, part_other, ((place ^ bit) * size,))
 
-    levels = range(lax.axis_size("dp").bit_length() - 1)
-    near_first = list(levels)
-    far_first = [1, 0, *levels[2:]] if len(near_first) > 1 else near_first
-
-    def pairs(own, across):
-        return [part for s in seqs for part in (own[s], across[s])]
-
     def norm_back(s, deps):
         return first_norm_back(
             one[s][0], two[s][1], fed_back[s][2], back_got[s], gain_one, deps
         )
 
-    down_made = weight_grad(
-        pairs([two[s][2] for s in seqs], grad_far),
-        [fed[s][0] for s in seqs], [fed[s][1] for s in seqs],
-        dp_place, [(hidden, near_first)], "w_down_grad", deps=[fed_back[-1][2]], halves=True,
-    )
-    one_back = [norm_back(s, [down_made[1]]) for s in seqs]
+    one_back = [norm_back(s, [fed_back[-1][2]]) for s in seqs]
     up_made = weight_grad(
         pairs([one[s][2] for s in seqs], normed_far),
         [fed_back[s][0] for s in seqs], [fed_back[s][1] for s in seqs],
         dp_place, [(hidden, far_first)], "w_up_grad", deps=[one_back[s][1] for s in seqs], halves=True,
     )
     first_across = [swap_tensor(one_back[s][1], ACROSS) for s in seqs]
-    down_mine = Chain(down_made[0], down_made[1], near_first)
-    down_other = Chain(down_made[2], down_made[3], near_first)
-    up_mine = Chain(up_made[0], up_made[1], far_first)
-    up_other = Chain(up_made[2], up_made[3], far_first)
+    down_chain = Chain(*down_made, near_first)
+    up_chain = Chain(*up_made, far_first)
 
     def backward(s, deps):
         return attention_backward(
@@ -909,57 +941,56 @@
         [attended[s][0] for s in seqs], [attended[s][1] for s in seqs],
         dp_place, [(head_dims, near_first)], "w_out_grad", deps=[attended_back[0][3]],
     )
-    down_mine.fold([attended_back[0][3]])
-    up_mine.fold([attended_back[0][3]])
-    attended_back += [backward(s, [down_mine.keep, up_mine.keep, out_made[1]]) for s in seqs[1:]]
+    down_chain.fold([attended_back[0][3]])
+    attended_back += [backward(s, [down_chain.keep, out_made[1]]) for s in seqs[1:]]
     far_back = [swap_tensor(attended_back[s][2], CORE) for s in seqs]
 
-    down_other.fold([attended_back[-1][3]])
-    up_other.fold([attended_back[-1][3]])
+    up_chain.fold([attended_back[-1][3]])
     tokens = pairs(x_own, x_across)
     grad_queries = [attended_back[s][0] for s in seqs]
     query_made = weight_grad(
-        tokens, grad_queries, grad_queries, dp_place, [(head_dims, far_first)], "w_query_grad",
-        head_dims, [far_back[0], down_other.keep, up_other.keep, down_mine.came, up_mine.came],
-    )
-    query_chain = core_chain(query_made[0], query_made[1], far_first)
+        tokens, grad_queries, grad_queries, dp_place, [(head_dims, near_first)], "w_query_grad",
+        head_dims, [far_back[0], up_chain.keep],
+    )
     back = [
         project_back(
             attended_back[0][0], attended_back[0][1], far_back[0], att_mine, att_other,
-            [query_made[1], far_back[-1]],
+            [query_made[1]],
         )
     ]
-    down_mine.fold([back[0][2]])
-    up_mine.fold([back[0][2]])
     back += [
         project_back(
             attended_back[s][0], attended_back[s][1], far_back[s], att_mine, att_other,
-            [down_mine.keep, up_mine.keep],
+            [back[0][2]],
         )
         for s in seqs[1:]
     ]
     input_got = [swap_tensor(back[s][3], ACROSS) for s in seqs]
+    down_chain.fold([back[-1][2]])
+    query_chain = core_chain([query_made, out_made], near_first, [back[-1][2]])
     key_value_made = weight_grad(
         tokens, [back[s][0] for s in seqs], [back[s][1] for s in seqs],
         dp_place, [(head_dims, near_first), (head_dims, far_first)], "w_key_value_grad",
-        deps=input_got[:1],
-    )
-    down_other.fold([key_value_made[0]])
-    up_other.fold([key_value_made[0]])
-    seconds = [down_other.keep, up_other.keep, input_got[-1]]
-    key_chain = core_chain(key_value_made[0], key_value_made[1], near_first, seconds)
-    value_chain = core_chain(key_value_made[2], key_value_made[3], far_first, seconds)
-    out_chain = core_chain(out_made[0], out_made[1], near_first, [attended_back[-1][3]])
-    out_chain.fold([key_value_made[0]])
-    query_chain.fold([key_value_made[0]])
-    for chain in (down_mine, up_mine, down_other, up_other):
-        chain.fold([value_chain.keep, key_chain.keep])
+        deps=input_got[:1] + [down_chain.keep, query_chain.keep],
+    )
+    key_chain = core_chain([key_value_made[:2]], near_first, input_got[-1:])
+    value_chain = core_chain([key_value_made[2:]], far_first, input_got[-1:])
+    started = [key_chain.keep, value_chain.keep]
+    up_chain.fold(started)
+    query_chain.fold(started)
+    key_chain.fold()
+    value_chain.fold()
+    ending = [key_chain.keep, value_chain.keep]
+    query_chain.fold(ending)
+    down_chain.fold(ending)
+    up_chain.fold(ending)
     input_grad = jnp.stack(
         [
             (one_back[s][0] + (back[s][2] + input_got[s].astype(F32))).astype(BF16)
             for s in seqs
         ]
     )
+
     sums = add_up([attended_back[s][3] for s in seqs], [query_made[1]])
     small = sum_all(
         jnp.concatenate(
@@ -975,13 +1006,15 @@
                 placed_in(sums[0, head_dims:], sums[1, head_dims:], CORE),
             ]
         ),
-        [[back[0][2]], [back[-1][2]], [key_chain.keep, value_chain.keep]],
-    )
-
-    def over_y(mine, other):
-        return mine.finish() + swap_tensor(other.finish().astype(BF16), ACROSS).astype(F32)
-
-    down_grad, up_grad = over_y(down_mine, down_other), over_y(up_mine, up_other)
+        [[back[0][2]], [back[-1][2]], started, started, ending],
+    )
+
+    def over_y(both):
+        return both[0] + swap_tensor(both[1].astype(BF16), ACROSS).astype(F32)
+
+    down_grad, up_grad = over_y(down_chain.finish()), over_y(up_chain.finish())
+    query_and_out = query_chain.finish()
+
     vectors = [small[i * width : (i + 1) * width] for i in range(6)]
     second_gain_grad, second_shift_grad, b_down_grad = vectors[:3]
     first_gain_grad, first_shift_grad, b_out_grad = vectors[3:]
@@ -992,10 +1025,10 @@
     return (
         output,
         input_grad,
-        query_chain.finish(),
-        key_chain.finish(),
-        value_chain.finish(),
-        out_chain.finish().T,
+        query_and_out[0],
+        key_chain.finish()[0],
+        value_chain.finish()[0],
+        query_and_out[1].T,
         up_grad,
         down_grad.T,
         b_query_grad,

time: 492 us -> 461 us (0.937)
  starting transfers between devices: 78.8 us -> 55.9 us
  waiting for transfers between devices: 112 us -> 99.3 us
  local copies, waits for them, and re-layouts: 47.6 us -> 53.1 us
    ppermute x45 -> x29, starting transfers between devices: 55.3 us -> 37.2 us  [swap_dp(): return lax.ppermute(array, 'dp', [(i, i ^ bit) for i in range(size)])]
    ppermute x42 -> x35, waiting for transfers between devices: 37.8 us -> 24 us  [swap_tensor(): return lax.ppermute(array, 'tensor', [(i, i ^ bit) for i in range(size)])]
    ppermute x42 -> x35, starting transfers between devices: 23.5 us -> 18.7 us  [swap_tensor(): return lax.ppermute(array, 'tensor', [(i, i ^ bit) for i in range(size)])]
    pallas_call x50 -> x40, Pallas kernels: 125 us -> 121 us  [whole_call(): pl.pallas_call(after(kernel, len(args), deps), out_shape=tuple(outs), in_...]
    ppermute x45 -> x29, waiting for transfers between devices: 74.3 us -> 75.3 us  [swap_dp(): return lax.ppermute(array, 'dp', [(i, i ^ bit) for i in range(size)])]
    unnamed x262 -> x201, local copies, waits for them, and re-layouts: 42.8 us -> 42.3 us
  transfers between devices with their start and end apart: 87 -> 64, of which waited for: 22 -> 17; matrix products, arithmetic and copies ran while one was open for 4% -> 6% of each run, Pallas kernels for 47% -> 49%
where the time goes in v6:
time: 461 us; the launch traced here: 455 us
  Pallas kernels  235 us (51%)
  waiting for transfers between devices  99.3 us (22%)
  starting transfers between devices  55.9 us (12%)
  local copies, waits for them, and re-layouts  53.1 us (12%)
  other arithmetic  10.2 us (2%)
    pallas_call x40, Pallas kernels, whole_call(): pl.pallas_call(after(kernel, len(args), deps), out_shape=tuple(outs), in_...  121 us
    pallas_call x11, Pallas kernels, streamed_call(): pl.pallas_call(after(kernel, len(args), deps), grid=grid, out_shape=tuple...  99 us
    ppermute x29, waiting for transfers between devices, swap_dp(): return lax.ppermute(array, 'dp', [(i, i ^ bit) for i in range(size)])  75.3 us
    unnamed x201, local copies, waits for them, and re-layouts  42.3 us
    ppermute x29, starting transfers between devices, swap_dp(): return lax.ppermute(array, 'dp', [(i, i ^ bit) for i in range(size)])  37.2 us
    ppermute x35, waiting for transfers between devices, swap_tensor(): return lax.ppermute(array, 'tensor', [(i, i ^ bit) for i in range(size)])  24 us
    ppermute x35, starting transfers between devices, swap_tensor(): return lax.ppermute(array, 'tensor', [(i, i ^ bit) for i in range(size)])  18.7 us
    pallas_call x4, Pallas kernels, assemble(): pl.pallas_call(after(kernel, 1 + len(arrays), deps), out_shape=out, in_sp...  14.9 us
  transfers between devices with their start and end apart: 64, of which 17 were waited for; matrix products, arithmetic and copies ran while one was open for 6% of the time, Pallas kernels for 49%

profile of v6, /device:TPU:0, one launch (start us, length us, event | category | flops | bytes accessed | tf_op | source)
XLA Modules:
  0.0 455.0 jit_solution(1184729005065466839)
XLA Ops:
  0.7 1.7 copy.39
  2.3 1.7 pack_attention.1
  4.0 4.0 collective-permute-start.1
  8.0 1.8 copy.40
  9.8 10.3 %collective-permute-done.1.refs_2_ = bf16[128,1024]{1,0:T(8,128)(2,1)S(1)} collective-permute-done((bf16[128,1024]{1,0:T(8,128)(2,1)}, bf16[128,1024]{1,0:T(8,128)(2,1)S(1)}, u32[]{:S(2)}, u32[]{:S(2)}) %collective-permute-start.1) | collective-permute-done | bytes 262176 | tf_op jit(solution)/shard_map/ppermute | solution.py:92
  22.2 1.9 pack_feed.1
  24.0 3.3 collective-permute-start.10
  27.3 1.5 collective-permute-start.3
  28.8 1.5 collective-permute-start
  31.7 11.8 %collective-permute-done.2.refs_2_ = bf16[256,1024]{1,0:T(8,128)(2,1)} collective-permute-done((bf16[256,1024]{1,0:T(8,128)(2,1)S(1)}, bf16[256,1024]{1,0:T(8,128)(2,1)}, u32[]{:S(2)}, u32[]{:S(2)}) %collective-permute-start.2) | collective-permute-done | bytes 524320 | tf_op jit(solution)/shard_map/ppermute | solution.py:92
  44.8 5.8 %collective-permute-done.10.refs_6_ = bf16[128,2048]{1,0:T(8,128)(2,1)S(1)} collective-permute-done((bf16[128,2048]{1,0:T(8,128)(2,1)}, bf16[128,2048]{1,0:T(8,128)(2,1)S(1)}, u32[]{:S(2)}, u32[]{:S(2)}) %collective-permute-start.10) | collective-permute-done | bytes 524320 | tf_op jit(solution)/shard_map/ppermute | solution.py:92
  50.6 1.5 collective-permute-start.4
  52.1 2.1 pad_maximum_fusion.refs_1_
  55.6 8.8 %collective-permute-done.16.refs_6_ = bf16[128,2048]{1,0:T(8,128)(2,1)} collective-permute-done((bf16[128,2048]{1,0:T(8,128)(2,1)}, bf16[128,2048]{1,0:T(8,128)(2,1)}, u32[]{:S(2)}, u32[]{:S(2)}) %collective-permute-start.16) | collective-permute-done | bytes 524320 | tf_op jit(solution)/shard_map/ppermute | solution.py:87
  66.8 2.2 slice_bitcast_fusion.3
  69.0 3.0 assemble_attention.1.refs_2_.refs_4_.refs_6_.refs_3_
  73.7 3.0 assemble_attention_other.1.refs_3_.refs_5_.refs_7_.refs_4_
  76.7 5.6 %project_inputs.2 = (bf16[512,768]{1,0:T(8,128)(2,1)}, bf16[512,768]{1,0:T(8,128)(2,1)}, bf16[512,1024]{1,0:T(8,128)(2,1)}) custom-call(bf16[256,1024]{1,0:T(8,128)(2,1)} %get-tuple-element.283.refs_0_.refs_1_, bf16[256,1024]{1,0:T(8,128)(2,1)} %get-tuple-element.281.refs_1_.refs_2_, bf16[1024,1024]{1,0:T(8,128)(2,1)} %assemble_attention.1.refs_2_.refs_4_.refs_6_.refs_3_, ...), custom_call_target="tpu_custom_call" | custom-call | flops 1610612 | bytes 7870 | tf_op jit(solution)/shard_map/project_inputs/pallas_call | solution.py:47
  83.0 5.6 %project_inputs.3 = (bf16[512,768]{1,0:T(8,128)(2,1)}, bf16[512,768]{1,0:T(8,128)(2,1)}, bf16[512,1024]{1,0:T(8,128)(2,1)}) custom-call(bf16[256,1024]{1,0:T(8,128)(2,1)} %get-tuple-element.284.refs_0_.refs_3_, bf16[256,1024]{1,0:T(8,128)(2,1)} %get-tuple-element.282.refs_1_.refs_4_, bf16[1024,1024]{1,0:T(8,128)(2,1)} %assemble_attention.1.refs_2_.refs_4_.refs_6_.refs_3_, ...), custom_call_target="tpu_custom_call" | custom-call | flops 1610612 | bytes 7870 | tf_op jit(solution)/shard_map/project_inputs/pallas_call | solution.py:47
  90.1 1.9 constant_dynamic-update-slice_fusion.1
  98.8 13.3 %attention_forward.2 = (bf16[512,256]{1,0:T(8,128)(2,1)}, bf16[512,256]{1,0:T(8,128)(2,1)}, f32[256,1024]{1,0:T(8,128)}, bf16[256,1024]{1,0:T(8,128)(2,1)}) custom-call(bf16[512,768]{1,0:T(8,128)(2,1)} %get-tuple-element.131.refs_0_, bf16[512,768]{1,0:T(8,128)(2,1)} %get-tuple-element.132.refs_1_, bf16[512,1024]{1,0:T(8,128)(2,1)} %collective-permute-done.11.refs_2_, ...), custom_call_target="tpu_custom_call" | custom-call | flops 8589934 | bytes 8916 | tf_op jit(solution)/shard_map/attention_forward/pallas_call | solution.py:47
  112.1 1.5 collective-permute-start.13
  114.6 12.8 %attention_forward.3 = (bf16[512,256]{1,0:T(8,128)(2,1)}, bf16[512,256]{1,0:T(8,128)(2,1)}, f32[256,1024]{1,0:T(8,128)}, bf16[256,1024]{1,0:T(8,128)(2,1)}) custom-call(bf16[512,768]{1,0:T(8,128)(2,1)} %get-tuple-element.138.refs_0_, bf16[512,768]{1,0:T(8,128)(2,1)} %get-tuple-element.139.refs_1_, bf16[512,1024]{1,0:T(8,128)(2,1)} %collective-permute-done.21.refs_2_, ...), custom_call_target="tpu_custom_call" | custom-call | flops 8589934 | bytes 8916 | tf_op jit(solution)/shard_map/attention_forward/pallas_call | solution.py:47
  127.9 1.5 collective-permute-start.19
  129.4 1.4 collective-permute-done.14.refs_6_.refs_4_
  130.8 1.5 collective-permute-start.20
  133.9 8.6 %collective-permute-done.23.refs_2_ = bf16[256,1024]{1,0:T(8,128)(2,1)S(1)} collective-permute-done((bf16[256,1024]{1,0:T(8,128)(2,1)}, bf16[256,1024]{1,0:T(8,128)(2,1)S(1)}, u32[]{:S(2)}, u32[]{:S(2)}) %collective-permute-start.23) | collective-permute-done | bytes 524320 | tf_op jit(solution)/shard_map/ppermute | solution.py:87
  143.7 4.5 assemble_feed.1.refs_2_.refs_3_.refs_4_
  149.0 8.8 %feed_forward.4 = (bf16[512,1024]{1,0:T(8,128)(2,1)}, bf16[512,1024]{1,0:T(8,128)(2,1)}, f32[512,1024]{1,0:T(8,128)}) custom-call(bf16[256,1024]{1,0:T(8,128)(2,1)} %copy-done.9, bf16[256,1024]{1,0:T(8,128)(2,1)} %copy-done.64, bf16[1024,2048]{1,0:T(8,128)(2,1)} %assemble_feed.1.refs_2_.refs_3_.refs_4_, ...), custom_call_target="tpu_custom_call" | custom-call | flops 2147483 | bytes 13635 | tf_op jit(solution)/shard_map/feed_forward/pallas_call | solution.py:64
  158.6 8.8 %feed_forward.5 = (bf16[512,1024]{1,0:T(8,128)(2,1)}, bf16[512,1024]{1,0:T(8,128)(2,1)}, f32[512,1024]{1,0:T(8,128)}) custom-call(bf16[256,1024]{1,0:T(8,128)(2,1)} %copy-done.10, bf16[256,1024]{1,0:T(8,128)(2,1)} %copy-done.65, bf16[1024,2048]{1,0:T(8,128)(2,1)} %assemble_feed.1.refs_2_.refs_3_.refs_4_, ...), custom_call_target="tpu_custom_call" | custom-call | flops 2147483 | bytes 13635 | tf_op jit(solution)/shard_map/feed_forward/pallas_call | solution.py:64
  167.5 4.5 assemble_feed_other.1.refs_2_.refs_3_.refs_5_
  172.6 9.8 %feed_forward.6 = (bf16[512,1024]{1,0:T(8,128)(2,1)}, bf16[512,1024]{1,0:T(8,128)(2,1)}, f32[256,1024]{1,0:T(8,128)}, bf16[256,1024]{1,0:T(8,128)(2,1)}) custom-call(bf16[256,1024]{1,0:T(8,128)(2,1)} %copy-done.9, bf16[256,1024]{1,0:T(8,128)(2,1)} %copy-done.64, bf16[1024,2048]{1,0:T(8,128)(2,1)} %assemble_feed_other.1.refs_2_.refs_3_.refs_5_, ...), custom_call_target="tpu_custom_call" | custom-call | flops 2147483 | bytes 15208 | tf_op jit(solution)/shard_map/feed_forward/pallas_call | solution.py:64
  182.6 10.0 %feed_forward.7 = (bf16[512,1024]{1,0:T(8,128)(2,1)}, bf16[512,1024]{1,0:T(8,128)(2,1)}, f32[256,1024]{1,0:T(8,128)}, bf16[256,1024]{1,0:T(8,128)(2,1)}) custom-call(bf16[256,1024]{1,0:T(8,128)(2,1)} %copy-done.10, bf16[256,1024]{1,0:T(8,128)(2,1)} %copy-done.65, bf16[1024,2048]{1,0:T(8,128)(2,1)} %assemble_feed_other.1.refs_2_.refs_3_.refs_5_, ...), custom_call_target="tpu_custom_call" | custom-call | flops 2147483 | bytes 15208 | tf_op jit(solution)/shard_map/feed_forward/pallas_call | solution.py:64
  199.1 11.5 %feed_forward_back.2 = (bf16[512,1024]{1,0:T(8,128)(2,1)}, bf16[512,1024]{1,0:T(8,128)(2,1)}, f32[256,1024]{1,0:T(8,128)}, bf16[256,1024]{1,0:T(8,128)(2,1)}, f32[1,1024]{1,0:T(1,128)}, /*index=5*/f32[1,1024]{1,0:T(1,128)}) custom-call(bf16[256,1024]{1,0:T(8,128)(2,1)} %copy-done.24, bf16[256,1024]{1,0:T(8,128)(2,1)} %copy-done.71, ...), custom_call_target="tpu_custom_call" | custom-call | flops 4294967 | bytes 23601 | tf_op jit(solution)/shard_map/feed_forward_back/pallas_call | solution.py:64
  211.8 10.0 %w_down_grad.1 = (f32[2,512,1024]{2,1,0:T(8,128)}, bf16[2,512,1024]{2,1,0:T(8,128)(2,1)}) custom-call(s32[1]{0:T(128)} %bitcast.2.refs_0_, bf16[256,1024]{1,0:T(8,128)(2,1)} %copy-done.24, bf16[256,1024]{1,0:T(8,128)(2,1)} %copy-done.71, bf16[256,1024]{1,0:T(8,128)(2,1)} %copy-done.25, bf16[256,1024]{1,0:T(8,128)(2,1)} %copy-done.72, ...), custom_call_target="tpu_custom_call" | custom-call | flops 4294967 | bytes 12582 | tf_op jit(solution)/shard_map/w_down_grad/pallas_call | solution.py:64
  221.7 11.5 %feed_forward_back.3 = (bf16[512,1024]{1,0:T(8,128)(2,1)}, bf16[512,1024]{1,0:T(8,128)(2,1)}, f32[256,1024]{1,0:T(8,128)}, bf16[256,1024]{1,0:T(8,128)(2,1)}, f32[1,1024]{1,0:T(1,128)}, /*index=5*/f32[1,1024]{1,0:T(1,128)}) custom-call(bf16[256,1024]{1,0:T(8,128)(2,1)} %copy-done.25, bf16[256,1024]{1,0:T(8,128)(2,1)} %copy-done.72, ...), custom_call_target="tpu_custom_call" | custom-call | flops 4294967 | bytes 23601 | tf_op jit(solution)/shard_map/feed_forward_back/pallas_call | solution.py:64
  236.6 1.5 collective-permute-start.31
  238.1 1.5 collective-permute-start.35
  247.5 10.2 %w_up_grad.1 = (f32[2,512,1024]{2,1,0:T(8,128)}, bf16[2,512,1024]{2,1,0:T(8,128)(2,1)}) custom-call(s32[1]{0:T(128)} %bitcast.2.refs_0_, bf16[256,1024]{1,0:T(8,128)(2,1)} %copy-done.9, bf16[256,1024]{1,0:T(8,128)(2,1)} %copy-done.64, bf16[256,1024]{1,0:T(8,128)(2,1)} %copy-done.10, bf16[256,1024]{1,0:T(8,128)(2,1)} %copy-done.65, ...), custom_call_target="tpu_custom_call" | custom-call | flops 4294967 | bytes 12582 | tf_op jit(solution)/shard_map/w_up_grad/pallas_call | solution.py:64
  258.1 26.3 %attention_backward.2 = (bf16[512,512]{1,0:T(8,128)(2,1)}, f32[512,1024]{1,0:T(8,128)}, bf16[512,1024]{1,0:T(8,128)(2,1)}, f32[2,512]{1,0:T(2,128)}) custom-call(bf16[512,768]{1,0:T(8,128)(2,1)} %get-tuple-element.131.refs_0_, bf16[512,768]{1,0:T(8,128)(2,1)} %get-tuple-element.132.refs_1_, bf16[512,1024]{1,0:T(8,128)(2,1)} %collective-permute-done.11.refs_2_, ...), custom_call_target="tpu_custom_call" | custom-call | flops 21474836480 | bytes 11542 | tf_op jit(solution)/shard_map/attention_backward/pallas_call | solution.py:47
  285.2 4.3 w_out_grad.1
  289.6 1.9 fold.15
  292.8 26.9 %attention_backward.3 = (bf16[512,512]{1,0:T(8,128)(2,1)}, f32[512,1024]{1,0:T(8,128)}, bf16[512,1024]{1,0:T(8,128)(2,1)}, f32[2,512]{1,0:T(2,128)}) custom-call(bf16[512,768]{1,0:T(8,128)(2,1)} %get-tuple-element.138.refs_0_, bf16[512,768]{1,0:T(8,128)(2,1)} %get-tuple-element.139.refs_1_, bf16[512,1024]{1,0:T(8,128)(2,1)} %collective-permute-done.21.refs_2_, ...), custom_call_target="tpu_custom_call" | custom-call | flops 21474836480 | bytes 11542 | tf_op jit(solution)/shard_map/attention_backward/pallas_call | solution.py:47
  320.2 1.6 collective-permute-start.43
  322.0 2.2 copy-done.14
  324.8 1.4 fold.16
  327.6 4.3 w_query_grad.1
  332.5 6.3 %project_back.2 = (bf16[512,512]{1,0:T(8,128)(2,1)}, bf16[512,512]{1,0:T(8,128)(2,1)}, f32[256,1024]{1,0:T(8,128)}, bf16[256,1024]{1,0:T(8,128)(2,1)}) custom-call(bf16[512,512]{1,0:T(8,128)(2,1)} %get-tuple-element.180.refs_5_.refs_7_.refs_0_, f32[512,1024]{1,0:T(8,128)} %get-tuple-element.181.refs_1_, ...), custom_call_target="tpu_custom_call" | custom-call | flops 1610612 | bytes 10485 | tf_op jit(solution)/shard_map/project_back/pallas_call | solution.py:47
  341.8 6.4 %project_back.3 = (bf16[512,512]{1,0:T(8,128)(2,1)}, bf16[512,512]{1,0:T(8,128)(2,1)}, f32[256,1024]{1,0:T(8,128)}, bf16[256,1024]{1,0:T(8,128)(2,1)}) custom-call(bf16[512,512]{1,0:T(8,128)(2,1)} %get-tuple-element.191.refs_6_.refs_8_.refs_0_, f32[512,1024]{1,0:T(8,128)} %get-tuple-element.199.refs_1_, bf16[512,1024]{1,0:T(8,128)(2,1)} %collective-permute-done.38.refs_2_, ...), custom_call_target="tpu_custom_call" | custom-call | flops 1610612 | bytes 10485 | tf_op jit(solution)/shard_map/project_back/pallas_call | solution.py:47
  357.7 9.7 %w_key_value_grad.1 = (f32[1024,256]{1,0:T(8,128)}, bf16[1024,256]{1,0:T(8,128)(2,1)}, f32[1024,256]{1,0:T(8,128)}, bf16[1024,256]{1,0:T(8,128)(2,1)}) custom-call(s32[1]{0:T(128)} %bitcast.2.refs_0_, bf16[256,1024]{1,0:T(8,128)(2,1)} %get-tuple-element.283.refs_0_.refs_1_, bf16[256,1024]{1,0:T(8,128)(2,1)} %get-tuple-element.281.refs_1_.refs_2_, ...), custom_call_target="tpu_custom_call" | custom-call | flops 2147483 | bytes 7340 | tf_op jit(solution)/shard_map/w_key_value_grad/pallas_call | solution.py:64
  370.8 2.8 collective-permute-done.60.refs_1_
  373.7 1.5 collective-permute-start.42
  375.2 2.1 pad_maximum_fusion.1
  377.3 1.5 collective-permute-start.57
  381.0 6.3 %collective-permute-done.42.refs_1_ = bf16[2,512,256]{2,1,0:T(8,128)(2,1)S(1)} collective-permute-done((bf16[2,512,256]{2,1,0:T(8,128)(2,1)}, bf16[2,512,256]{2,1,0:T(8,128)(2,1)S(1)}, u32[]{:S(2)}, u32[]{:S(2)}) %collective-permute-start.42) | collective-permute-done | bytes 524320 | tf_op jit(solution)/shard_map/ppermute | solution.py:92
  389.4 1.6 collective-permute-start.48
  394.3 16.8 %collective-permute-done.62.refs_1_ = f32[96,128]{1,0:T(8,128)S(1)} collective-permute-done((f32[96,128]{1,0:T(8,128)S(1)}, f32[96,128]{1,0:T(8,128)S(1)}, u32[]{:S(2)}, u32[]{:S(2)}) %collective-permute-start.62) | collective-permute-done | bytes 49184 | tf_op jit(solution)/shard_map/ppermute | solution.py:92
  411.1 3.0 collective-permute-start.63
  414.4 1.8 collective-permute-start.50
  416.2 1.5 collective-permute-start.52
  418.5 20.4 %collective-permute-done.63.refs_1_ = f32[96,128]{1,0:T(8,128)S(1)} collective-permute-done((f32[96,128]{1,0:T(8,128)S(1)}, f32[96,128]{1,0:T(8,128)S(1)}, u32[]{:S(2)}, u32[]{:S(2)}) %collective-permute-start.63) | collective-permute-done | bytes 49184 | tf_op jit(solution)/shard_map/ppermute | solution.py:92
  441.6 3.0 collective-permute-start.53
  451.5 1.6 collective-permute-done.56
  453.0 1.8 fusion.4
  (361 shorter events, 84.1 us)
Async XLA Ops:
  4.0 16.2 %collective-permute-start.1 = (bf16[128,1024]{1,0:T(8,128)(2,1)}, bf16[128,1024]{1,0:T(8,128)(2,1)S(1)}, u32[]{:S(2)}, u32[]{:S(2)}) collective-permute-start(bf16[128,1024]{1,0:T(8,128)(2,1)} %pack_attention.1), channel_id=1, source_target_pairs={{0,16},{4,20},{8,24},{12,28},{16,0},{20,4},{24,8},{28,12},{1,17},{... | collective-permute-start | bytes 786440 | tf_op jit(solution)/shard_map/ppermute | solution.py:92
  21.3 22.2 %collective-permute-start.2 = (bf16[256,1024]{1,0:T(8,128)(2,1)S(1)}, bf16[256,1024]{1,0:T(8,128)(2,1)}, u32[]{:S(2)}, u32[]{:S(2)}) collective-permute-start(bf16[256,1024]{1,0:T(8,128)(2,1)S(1)} %pad_maximum_fusion.3.refs_1_), channel_id=1, source_target_pairs={{0,8},{4,12},{8,0},{12,4},{16,24},{20,28},{24,16},{28,20},{1,9},{5... | collective-permute-start | bytes 1572872 | tf_op jit(solution)/shard_map/ppermute | solution.py:92
  24.0 26.6 %collective-permute-start.10 = (bf16[128,2048]{1,0:T(8,128)(2,1)}, bf16[128,2048]{1,0:T(8,128)(2,1)S(1)}, u32[]{:S(2)}, u32[]{:S(2)}) collective-permute-start(bf16[128,2048]{1,0:T(8,128)(2,1)} %pack_feed.1), channel_id=1, source_target_pairs={{0,16},{4,20},{8,24},{12,28},{16,0},{20,4},{24,8},{28,12},{1,17},{... | collective-permute-start | bytes 1572872 | tf_op jit(solution)/shard_map/ppermute | solution.py:92
  27.3 26.9 %collective-permute-start.3 = (bf16[256,1024]{1,0:T(8,128)(2,1)S(1)}, bf16[256,1024]{1,0:T(8,128)(2,1)S(1)}, u32[]{:S(2)}, u32[]{:S(2)}) collective-permute-start(bf16[256,1024]{1,0:T(8,128)(2,1)S(1)} %pad_maximum_fusion.3.refs_1_), channel_id=1, source_target_pairs={{0,4},{4,0},{8,12},{12,8},{16,20},{20,16},{24,28},{28,24},{1,5},{5... | collective-permute-start | bytes 1572872 | tf_op jit(solution)/shard_map/ppermute | solution.py:92
  28.8 37.7 %collective-permute-start = (bf16[2,256,1024]{2,1,0:T(8,128)(2,1)S(1)}, bf16[2,256,1024]{2,1,0:T(8,128)(2,1)}, u32[]{:S(2)}, u32[]{:S(2)}) collective-permute-start(bf16[2,256,1024]{2,1,0:T(8,128)(2,1)S(1)} %copy-done.75), channel_id=1, source_target_pairs={{0,2},{1,3},{2,0},{3,1},{4,6},{5,7},{6,4},{7,5},{8,10},{9,11},{10,... | collective-permute-start | bytes 3145736 | tf_op jit(solution)/shard_map/ppermute | solution.py:87
  30.3 1.2 collective-permute-start.9
  31.6 24.1 %collective-permute-start.5 = (bf16[256,1024]{1,0:T(8,128)(2,1)S(1)}, bf16[256,1024]{1,0:T(8,128)(2,1)}, u32[]{:S(2)}, u32[]{:S(2)}) collective-permute-start(bf16[256,1024]{1,0:T(8,128)(2,1)S(1)} %pad_maximum_fusion.3.refs_1_), channel_id=1, source_target_pairs={{0,1},{1,0},{2,3},{3,2},{4,5},{5,4},{6,7},{7,6},{8,9},{9,8},{10,11... | collective-permute-start | bytes 1572872 | tf_op jit(solution)/shard_map/ppermute | solution.py:87
  43.5 20.9 %collective-permute-start.16 = (bf16[128,2048]{1,0:T(8,128)(2,1)}, bf16[128,2048]{1,0:T(8,128)(2,1)}, u32[]{:S(2)}, u32[]{:S(2)}) collective-permute-start(bf16[128,2048]{1,0:T(8,128)(2,1)} %pack_feed.1), channel_id=1, source_target_pairs={{0,2},{1,3},{2,0},{3,1},{4,6},{5,7},{6,4},{7,5},{8,10},{9,11},{10,... | collective-permute-start | bytes 1572872 | tf_op jit(solution)/shard_map/ppermute | solution.py:87
  50.6 13.8 %collective-permute-start.4 = (bf16[256,1024]{1,0:T(8,128)(2,1)}, bf16[256,1024]{1,0:T(8,128)(2,1)}, u32[]{:S(2)}, u32[]{:S(2)}) collective-permute-start(bf16[256,1024]{1,0:T(8,128)(2,1)} %collective-permute-done.2.refs_2_), channel_id=1, source_target_pairs={{0,4},{4,0},{8,12},{12,8},{16,20},{20,16},{24,28},{28,24},{1,5},{5... | collective-permute-start | bytes 1572872 | tf_op jit(solution)/shard_map/ppermute | solution.py:92
  55.0 33.9 %collective-permute-start.12 = (bf16[256,2048]{1,0:T(8,128)(2,1)}, bf16[256,2048]{1,0:T(8,128)(2,1)S(1)}, u32[]{:S(2)}, u32[]{:S(2)}) collective-permute-start(bf16[256,2048]{1,0:T(8,128)(2,1)} %pad_maximum_fusion.refs_1_), channel_id=1, source_target_pairs={{0,8},{4,12},{8,0},{12,4},{16,24},{20,28},{24,16},{28,20},{1,9},{5... | collective-permute-start | bytes 3145736 | tf_op jit(solution)/shard_map/ppermute | solution.py:92
  55.6 16.3 %collective-permute-start.6 = (bf16[256,1024]{1,0:T(8,128)(2,1)}, bf16[256,1024]{1,0:T(8,128)(2,1)S(1)}, u32[]{:S(2)}, u32[]{:S(2)}) collective-permute-start(bf16[256,1024]{1,0:T(8,128)(2,1)} %collective-permute-done.2.refs_2_), channel_id=1, source_target_pairs={{0,1},{1,0},{2,3},{3,2},{4,5},{5,4},{6,7},{7,6},{8,9},{9,8},{10,11... | collective-permute-start | bytes 1572872 | tf_op jit(solution)/shard_map/ppermute | solution.py:87
  64.4 7.6 %collective-permute-start.7 = (bf16[256,1024]{1,0:T(8,128)(2,1)}, bf16[256,1024]{1,0:T(8,128)(2,1)S(1)}, u32[]{:S(2)}, u32[]{:S(2)}) collective-permute-start(bf16[256,1024]{1,0:T(8,128)(2,1)} %copy-done.78), channel_id=1, source_target_pairs={{0,1},{1,0},{2,3},{3,2},{4,5},{5,4},{6,7},{7,6},{8,9},{9,8},{10,11... | collective-permute-start | bytes 1572872 | tf_op jit(solution)/shard_map/ppermute | solution.py:87
  64.4 7.6 %collective-permute-start.8 = (bf16[256,1024]{1,0:T(8,128)(2,1)}, bf16[256,1024]{1,0:T(8,128)(2,1)S(1)}, u32[]{:S(2)}, u32[]{:S(2)}) collective-permute-start(bf16[256,1024]{1,0:T(8,128)(2,1)} %collective-permute-done.4.refs_4_), channel_id=1, source_target_pairs={{0,1},{1,0},{2,3},{3,2},{4,5},{5,4},{6,7},{7,6},{8,9},{9,8},{10,11... | collective-permute-start | bytes 1572872 | tf_op jit(solution)/shard_map/ppermute | solution.py:87
  66.5 26.2 %collective-permute-start.17 = (bf16[128,2048]{1,0:T(8,128)(2,1)}, bf16[128,2048]{1,0:T(8,128)(2,1)S(1)}, u32[]{:S(2)}, u32[]{:S(2)}) collective-permute-start(bf16[128,2048]{1,0:T(8,128)(2,1)} %collective-permute-done.16.refs_6_), channel_id=1, source_target_pairs={{0,16},{4,20},{8,24},{12,28},{16,0},{20,4},{24,8},{28,12},{1,17},{... | collective-permute-start | bytes 1572872 | tf_op jit(solution)/shard_map/ppermute | solution.py:92
  82.3 16.5 %collective-permute-start.11 = (bf16[512,1024]{1,0:T(8,128)(2,1)}, bf16[512,1024]{1,0:T(8,128)(2,1)}, u32[]{:S(2)}, u32[]{:S(2)}) collective-permute-start(bf16[512,1024]{1,0:T(8,128)(2,1)} %get-tuple-element.133.refs_7_), channel_id=1, source_target_pairs={{0,1},{1,0},{2,3},{3,2},{4,5},{5,4},{6,7},{7,6},{8,9},{9,8},{10,11... | collective-permute-start | bytes 3145736 | tf_op jit(solution)/shard_map/ppermute | solution.py:87
  82.3 31.3 %collective-permute-start.22 = (bf16[256,2048]{1,0:T(8,128)(2,1)}, bf16[256,2048]{1,0:T(8,128)(2,1)S(1)}, u32[]{:S(2)}, u32[]{:S(2)}) collective-permute-start(bf16[256,2048]{1,0:T(8,128)(2,1)} %pad_maximum_fusion.refs_1_), channel_id=1, source_target_pairs={{0,4},{4,0},{8,12},{12,8},{16,20},{20,16},{24,28},{28,24},{1,5},{5... | collective-permute-start | bytes 3145736 | tf_op jit(solution)/shard_map/ppermute | solution.py:92
  88.6 25.0 %collective-permute-start.21 = (bf16[512,1024]{1,0:T(8,128)(2,1)}, bf16[512,1024]{1,0:T(8,128)(2,1)}, u32[]{:S(2)}, u32[]{:S(2)}) collective-permute-start(bf16[512,1024]{1,0:T(8,128)(2,1)} %get-tuple-element.140), channel_id=1, source_target_pairs={{0,1},{1,0},{2,3},{3,2},{4,5},{5,4},{6,7},{7,6},{8,9},{9,8},{10,11... | collective-permute-start | bytes 3145736 | tf_op jit(solution)/shard_map/ppermute | solution.py:87
  89.0 41.9 %collective-permute-start.14 = (bf16[256,2048]{1,0:T(8,128)(2,1)S(1)}, bf16[256,2048]{1,0:T(8,128)(2,1)S(1)}, u32[]{:S(2)}, u32[]{:S(2)}) collective-permute-start(bf16[256,2048]{1,0:T(8,128)(2,1)S(1)} %collective-permute-done.12.refs_6_.refs_2_), channel_id=1, source_target_pairs={{0,4},{4,0},{8,12},{12,8},{16,20},{20,16},{24,28},{28,24},{1,5},{5... | collective-permute-start | bytes 3145736 | tf_op jit(solution)/shard_map/ppermute | solution.py:92
  94.4 39.5 %collective-permute-start.18 = (bf16[256,2048]{1,0:T(8,128)(2,1)}, bf16[256,2048]{1,0:T(8,128)(2,1)}, u32[]{:S(2)}, u32[]{:S(2)}) collective-permute-start(bf16[256,2048]{1,0:T(8,128)(2,1)} %constant_dynamic-update-slice_fusion.refs_1_), channel_id=1, source_target_pairs={{0,8},{4,12},{8,0},{12,4},{16,24},{20,28},{24,16},{28,20},{1,9},{5... | collective-permute-start | bytes 3145736 | tf_op jit(solution)/shard_map/ppermute | solution.py:92
  112.1 20.3 %collective-permute-start.13 = (bf16[256,1024]{1,0:T(8,128)(2,1)}, bf16[256,1024]{1,0:T(8,128)(2,1)S(1)}, u32[]{:S(2)}, u32[]{:S(2)}) collective-permute-start(bf16[256,1024]{1,0:T(8,128)(2,1)} %get-tuple-element.135), channel_id=1, source_target_pairs={{0,2},{1,3},{2,0},{3,1},{4,6},{5,7},{6,4},{7,5},{8,10},{9,11},{10,... | collective-permute-start | bytes 1572872 | tf_op jit(solution)/shard_map/ppermute | solution.py:87
  127.4 15.1 %collective-permute-start.23 = (bf16[256,1024]{1,0:T(8,128)(2,1)}, bf16[256,1024]{1,0:T(8,128)(2,1)S(1)}, u32[]{:S(2)}, u32[]{:S(2)}) collective-permute-start(bf16[256,1024]{1,0:T(8,128)(2,1)} %get-tuple-element.142), channel_id=1, source_target_pairs={{0,2},{1,3},{2,0},{3,1},{4,6},{5,7},{6,4},{7,5},{8,10},{9,11},{10,... | collective-permute-start | bytes 1572872 | tf_op jit(solution)/shard_map/ppermute | solution.py:87
  127.9 39.6 %collective-permute-start.19 = (bf16[256,2048]{1,0:T(8,128)(2,1)}, bf16[256,2048]{1,0:T(8,128)(2,1)}, u32[]{:S(2)}, u32[]{:S(2)}) collective-permute-start(bf16[256,2048]{1,0:T(8,128)(2,1)} %constant_dynamic-update-slice_fusion.refs_1_), channel_id=1, source_target_pairs={{0,4},{4,0},{8,12},{12,8},{16,20},{20,16},{24,28},{28,24},{1,5},{5... | collective-permute-start | bytes 3145736 | tf_op jit(solution)/shard_map/ppermute | solution.py:92
  130.8 36.7 %collective-permute-start.20 = (bf16[256,2048]{1,0:T(8,128)(2,1)S(1)}, bf16[256,2048]{1,0:T(8,128)(2,1)}, u32[]{:S(2)}, u32[]{:S(2)}) collective-permute-start(bf16[256,2048]{1,0:T(8,128)(2,1)S(1)} %collective-permute-done.14.refs_6_.refs_4_), channel_id=1, source_target_pairs={{0,2},{1,3},{2,0},{3,1},{4,6},{5,7},{6,4},{7,5},{8,10},{9,11},{10,... | collective-permute-start | bytes 3145736 | tf_op jit(solution)/shard_map/ppermute | solution.py:87
  133.9 14.3 %collective-permute-start.15 = (bf16[256,1024]{1,0:T(8,128)(2,1)S(1)}, bf16[256,1024]{1,0:T(8,128)(2,1)S(1)}, u32[]{:S(2)}, u32[]{:S(2)}) collective-permute-start(bf16[256,1024]{1,0:T(8,128)(2,1)S(1)} %get-tuple-element.137.refs_7_.refs_0_.refs_1_), channel_id=1, source_target_pairs={{0,1},{1,0},{2,3},{3,2},{4,5},{5,4},{6,7},{7,6},{8,9},{9,8},{10,11... | collective-permute-start | bytes 1572872 | tf_op jit(solution)/shard_map/ppermute | solution.py:87
  143.0 14.8 %collective-permute-start.24 = (bf16[256,1024]{1,0:T(8,128)(2,1)S(1)}, bf16[256,1024]{1,0:T(8,128)(2,1)S(1)}, u32[]{:S(2)}, u32[]{:S(2)}) collective-permute-start(bf16[256,1024]{1,0:T(8,128)(2,1)S(1)} %get-tuple-element.143.refs_0_.refs_3_), channel_id=1, source_target_pairs={{0,1},{1,0},{2,3},{3,2},{4,5},{5,4},{6,7},{7,6},{8,9},{9,8},{10,11... | collective-permute-start | bytes 1572872 | tf_op jit(solution)/shard_map/ppermute | solution.py:87
  143.1 28.9 %collective-permute-start.25 = (f32[1024]{0:T(1024)S(1)}, f32[1024]{0:T(1024)S(1)}, u32[]{:S(2)}, u32[]{:S(2)}) collective-permute-start(f32[1024]{0:T(1024)S(1)} %copy-done.85), channel_id=1, source_target_pairs={{0,2},{1,3},{2,0},{3,1},{4,6},{5,7},{6,4},{7,5},{8,10},{9,11},{10,... | collective-permute-start | bytes 12296 | tf_op jit(solution)/shard_map/ppermute | solution.py:87
  182.4 10.8 %collective-permute-start.26 = (bf16[256,1024]{1,0:T(8,128)(2,1)}, bf16[256,1024]{1,0:T(8,128)(2,1)S(1)}, u32[]{:S(2)}, u32[]{:S(2)}) collective-permute-start(bf16[256,1024]{1,0:T(8,128)(2,1)} %get-tuple-element.147), channel_id=1, source_target_pairs={{0,1},{1,0},{2,3},{3,2},{4,5},{5,4},{6,7},{7,6},{8,9},{9,8},{10,11... | collective-permute-start | bytes 1572872 | tf_op jit(solution)/shard_map/ppermute | solution.py:87
  192.6 2.7 collective-permute-start.27
  194.9 3.4 collective-permute-start.28
  198.1 12.9 %collective-permute-start.30 = (bf16[256,1024]{1,0:T(8,128)(2,1)S(1)}, bf16[256,1024]{1,0:T(8,128)(2,1)S(1)}, u32[]{:S(2)}, u32[]{:S(2)}) collective-permute-start(bf16[256,1024]{1,0:T(8,128)(2,1)S(1)} %get-tuple-element.160.refs_3_.refs_0_), channel_id=1, source_target_pairs={{0,1},{1,0},{2,3},{3,2},{4,5},{5,4},{6,7},{7,6},{8,9},{9,8},{10,11... | collective-permute-start | bytes 1572872 | tf_op jit(solution)/shard_map/ppermute | solution.py:87
  210.6 22.9 %collective-permute-start.29 = (bf16[256,1024]{1,0:T(8,128)(2,1)}, bf16[256,1024]{1,0:T(8,128)(2,1)S(1)}, u32[]{:S(2)}, u32[]{:S(2)}) collective-permute-start(bf16[256,1024]{1,0:T(8,128)(2,1)} %get-tuple-element.159), channel_id=1, source_target_pairs={{0,1},{1,0},{2,3},{3,2},{4,5},{5,4},{6,7},{7,6},{8,9},{9,8},{10,11... | collective-permute-start | bytes 1572872 | tf_op jit(solution)/shard_map/ppermute | solution.py:87
  233.3 8.4 %collective-permute-start.32 = (bf16[256,1024]{1,0:T(8,128)(2,1)}, bf16[256,1024]{1,0:T(8,128)(2,1)S(1)}, u32[]{:S(2)}, u32[]{:S(2)}) collective-permute-start(bf16[256,1024]{1,0:T(8,128)(2,1)} %get-tuple-element.177), channel_id=1, source_target_pairs={{0,1},{1,0},{2,3},{3,2},{4,5},{5,4},{6,7},{7,6},{8,9},{9,8},{10,11... | collective-permute-start | bytes 1572872 | tf_op jit(solution)/shard_map/ppermute | solution.py:87
  236.6 21.5 %collective-permute-start.31 = (bf16[256,1024]{1,0:T(8,128)(2,1)S(1)}, bf16[256,1024]{1,0:T(8,128)(2,1)}, u32[]{:S(2)}, u32[]{:S(2)}) collective-permute-start(bf16[256,1024]{1,0:T(8,128)(2,1)S(1)} %get-tuple-element.170.refs_9_.refs_4_.refs_1_), channel_id=1, source_target_pairs={{0,2},{1,3},{2,0},{3,1},{4,6},{5,7},{6,4},{7,5},{8,10},{9,11},{10,... | collective-permute-start | bytes 1572872 | tf_op jit(solution)/shard_map/ppermute | solution.py:87
  238.1 51.4 %collective-permute-start.35 = (bf16[2,512,1024]{2,1,0:T(8,128)(2,1)}, bf16[2,512,1024]{2,1,0:T(8,128)(2,1)}, u32[]{:S(2)}, u32[]{:S(2)}) collective-permute-start(bf16[2,512,1024]{2,1,0:T(8,128)(2,1)} %get-tuple-element.167.refs_8_), channel_id=1, source_target_pairs={{0,4},{4,0},{8,12},{12,8},{16,20},{20,16},{24,28},{28,24},{1,5},{5... | collective-permute-start | bytes 6291464 | tf_op jit(solution)/shard_map/ppermute | solution.py:92
  246.7 37.7 %collective-permute-start.34 = (bf16[256,1024]{1,0:T(8,128)(2,1)S(1)}, bf16[256,1024]{1,0:T(8,128)(2,1)S(1)}, u32[]{:S(2)}, u32[]{:S(2)}) collective-permute-start(bf16[256,1024]{1,0:T(8,128)(2,1)S(1)} %get-tuple-element.178.refs_10_.refs_3_.refs_4_), channel_id=1, source_target_pairs={{0,2},{1,3},{2,0},{3,1},{4,6},{5,7},{6,4},{7,5},{8,10},{9,11},{10,... | collective-permute-start | bytes 1572872 | tf_op jit(solution)/shard_map/ppermute | solution.py:87
  257.7 64.2 %collective-permute-start.36 = (bf16[2,512,1024]{2,1,0:T(8,128)(2,1)}, bf16[2,512,1024]{2,1,0:T(8,128)(2,1)S(1)}, u32[]{:S(2)}, u32[]{:S(2)}) collective-permute-start(bf16[2,512,1024]{2,1,0:T(8,128)(2,1)} %get-tuple-element.179.refs_8_), channel_id=1, source_target_pairs={{0,8},{4,12},{8,0},{12,4},{16,24},{20,28},{24,16},{28,20},{1,9},{5... | collective-permute-start | bytes 6291464 | tf_op jit(solution)/shard_map/ppermute | solution.py:92
  284.4 43.2 %collective-permute-start.33 = (bf16[512,1024]{1,0:T(8,128)(2,1)}, bf16[512,1024]{1,0:T(8,128)(2,1)}, u32[]{:S(2)}, u32[]{:S(2)}) collective-permute-start(bf16[512,1024]{1,0:T(8,128)(2,1)} %get-tuple-element.182), channel_id=1, source_target_pairs={{0,1},{1,0},{2,3},{3,2},{4,5},{5,4},{6,7},{7,6},{8,9},{9,8},{10,11... | collective-permute-start | bytes 3145736 | tf_op jit(solution)/shard_map/ppermute | solution.py:87
  319.7 21.5 %collective-permute-start.38 = (bf16[512,1024]{1,0:T(8,128)(2,1)}, bf16[512,1024]{1,0:T(8,128)(2,1)}, u32[]{:S(2)}, u32[]{:S(2)}) collective-permute-start(bf16[512,1024]{1,0:T(8,128)(2,1)} %get-tuple-element.200), channel_id=1, source_target_pairs={{0,1},{1,0},{2,3},{3,2},{4,5},{5,4},{6,7},{7,6},{8,9},{9,8},{10,11... | collective-permute-start | bytes 3145736 | tf_op jit(solution)/shard_map/ppermute | solution.py:87
  320.2 28.0 %collective-permute-start.43 = (bf16[2,256,1024]{2,1,0:T(8,128)(2,1)}, bf16[2,256,1024]{2,1,0:T(8,128)(2,1)S(1)}, u32[]{:S(2)}, u32[]{:S(2)}) collective-permute-start(bf16[2,256,1024]{2,1,0:T(8,128)(2,1)} %copy-done.60), channel_id=1, source_target_pairs={{0,8},{4,12},{8,0},{12,4},{16,24},{20,28},{24,16},{28,20},{1,9},{5... | collective-permute-start | bytes 3145736 | tf_op jit(solution)/shard_map/ppermute | solution.py:92
  321.9 32.6 %collective-permute-start.41 = (bf16[1024,256]{1,0:T(8,128)(2,1)}, bf16[1024,256]{1,0:T(8,128)(2,1)}, u32[]{:S(2)}, u32[]{:S(2)}) collective-permute-start(bf16[1024,256]{1,0:T(8,128)(2,1)} %get-tuple-element.190.refs_9_), channel_id=1, source_target_pairs={{0,1},{1,0},{2,3},{3,2},{4,5},{5,4},{6,7},{7,6},{8,9},{9,8},{10,11... | collective-permute-start | bytes 1572872 | tf_op jit(solution)/shard_map/ppermute | solution.py:87
  332.0 22.5 %collective-permute-start.40 = (bf16[1024,256]{1,0:T(8,128)(2,1)}, bf16[1024,256]{1,0:T(8,128)(2,1)S(1)}, u32[]{:S(2)}, u32[]{:S(2)}) collective-permute-start(bf16[1024,256]{1,0:T(8,128)(2,1)} %get-tuple-element.195.refs_5_.refs_2_), channel_id=1, source_target_pairs={{0,1},{1,0},{2,3},{3,2},{4,5},{5,4},{6,7},{7,6},{8,9},{9,8},{10,11... | collective-permute-start | bytes 1572872 | tf_op jit(solution)/shard_map/ppermute | solution.py:87
  338.8 17.9 %collective-permute-start.37 = (bf16[256,1024]{1,0:T(8,128)(2,1)}, bf16[256,1024]{1,0:T(8,128)(2,1)S(1)}, u32[]{:S(2)}, u32[]{:S(2)}) collective-permute-start(bf16[256,1024]{1,0:T(8,128)(2,1)} %get-tuple-element.197), channel_id=1, source_target_pairs={{0,2},{1,3},{2,0},{3,1},{4,6},{5,7},{6,4},{7,5},{8,10},{9,11},{10,... | collective-permute-start | bytes 1572872 | tf_op jit(solution)/shard_map/ppermute | solution.py:87
  341.3 50.0 %collective-permute-start.54 = (bf16[2,256,1024]{2,1,0:T(8,128)(2,1)}, bf16[2,256,1024]{2,1,0:T(8,128)(2,1)}, u32[]{:S(2)}, u32[]{:S(2)}) collective-permute-start(bf16[2,256,1024]{2,1,0:T(8,128)(2,1)} %get-tuple-element.233), channel_id=1, source_target_pairs={{0,4},{4,0},{8,12},{12,8},{16,20},{20,16},{24,28},{28,24},{1,5},{5... | collective-permute-start | bytes 3145736 | tf_op jit(solution)/shard_map/ppermute | solution.py:92
  349.2 28.1 %collective-permute-start.39 = (bf16[256,1024]{1,0:T(8,128)(2,1)}, bf16[256,1024]{1,0:T(8,128)(2,1)S(1)}, u32[]{:S(2)}, u32[]{:S(2)}) collective-permute-start(bf16[256,1024]{1,0:T(8,128)(2,1)} %get-tuple-element.202), channel_id=1, source_target_pairs={{0,2},{1,3},{2,0},{3,1},{4,6},{5,7},{6,4},{7,5},{8,10},{9,11},{10,... | collective-permute-start | bytes 1572872 | tf_op jit(solution)/shard_map/ppermute | solution.py:87
  367.4 11.4 %collective-permute-start.44 = (bf16[1024,256]{1,0:T(8,128)(2,1)}, bf16[1024,256]{1,0:T(8,128)(2,1)}, u32[]{:S(2)}, u32[]{:S(2)}) collective-permute-start(bf16[1024,256]{1,0:T(8,128)(2,1)} %get-tuple-element.214), channel_id=1, source_target_pairs={{0,1},{1,0},{2,3},{3,2},{4,5},{5,4},{6,7},{7,6},{8,9},{9,8},{10,11... | collective-permute-start | bytes 1572872 | tf_op jit(solution)/shard_map/ppermute | solution.py:87
  368.0 1.5 collective-permute-start.59
  369.5 4.2 collective-permute-start.60
  370.8 10.1 %collective-permute-start.45 = (bf16[1024,256]{1,0:T(8,128)(2,1)}, bf16[1024,256]{1,0:T(8,128)(2,1)S(1)}, u32[]{:S(2)}, u32[]{:S(2)}) collective-permute-start(bf16[1024,256]{1,0:T(8,128)(2,1)} %get-tuple-element.217), channel_id=1, source_target_pairs={{0,1},{1,0},{2,3},{3,2},{4,5},{5,4},{6,7},{7,6},{8,9},{9,8},{10,11... | collective-permute-start | bytes 1572872 | tf_op jit(solution)/shard_map/ppermute | solution.py:87
  373.7 13.6 %collective-permute-start.42 = (bf16[2,512,256]{2,1,0:T(8,128)(2,1)}, bf16[2,512,256]{2,1,0:T(8,128)(2,1)S(1)}, u32[]{:S(2)}, u32[]{:S(2)}) collective-permute-start(bf16[2,512,256]{2,1,0:T(8,128)(2,1)} %copy-done.63), channel_id=1, source_target_pairs={{0,4},{4,0},{8,12},{12,8},{16,20},{20,16},{24,28},{28,24},{1,5},{5... | collective-permute-start | bytes 1572872 | tf_op jit(solution)/shard_map/ppermute | solution.py:92
  377.3 38.9 %collective-permute-start.57 = (bf16[2,128,1024]{2,1,0:T(8,128)(2,1)S(1)}, bf16[2,128,1024]{2,1,0:T(8,128)(2,1)S(1)}, u32[]{:S(2)}, u32[]{:S(2)}) collective-permute-start(bf16[2,128,1024]{2,1,0:T(8,128)(2,1)S(1)} %copy-done.62), channel_id=1, source_target_pairs={{0,16},{4,20},{8,24},{12,28},{16,0},{20,4},{24,8},{28,12},{1,17},{... | collective-permute-start | bytes 1572872 | tf_op jit(solution)/shard_map/ppermute | solution.py:92
  378.8 10.6 %collective-permute-start.61 = (f32[96,128]{1,0:T(8,128)S(1)}, f32[96,128]{1,0:T(8,128)S(1)}, u32[]{:S(2)}, u32[]{:S(2)}) collective-permute-start(f32[96,128]{1,0:T(8,128)S(1)} %plus.6.refs_0_), channel_id=1, source_target_pairs={{0,4},{4,0},{8,12},{12,8},{16,20},{20,16},{24,28},{28,24},{1,5},{5... | collective-permute-start | bytes 147464 | tf_op jit(solution)/shard_map/ppermute | solution.py:92
  387.4 26.8 %collective-permute-start.46 = (bf16[2,256,256]{2,1,0:T(8,128)(2,1)S(1)}, bf16[2,256,256]{2,1,0:T(8,128)(2,1)S(1)}, u32[]{:S(2)}, u32[]{:S(2)}) collective-permute-start(bf16[2,256,256]{2,1,0:T(8,128)(2,1)S(1)} %get-tuple-element.220), channel_id=1, source_target_pairs={{0,8},{4,12},{8,0},{12,4},{16,24},{20,28},{24,16},{28,20},{1,9},{5... | collective-permute-start | bytes 786440 | tf_op jit(solution)/shard_map/ppermute | solution.py:92
  388.3 22.8 %collective-permute-start.47 = (bf16[1,512,256]{2,1,0:T(8,128)(2,1)S(1)}, bf16[1,512,256]{2,1,0:T(8,128)(2,1)S(1)}, u32[]{:S(2)}, u32[]{:S(2)}) collective-permute-start(bf16[1,512,256]{2,1,0:T(8,128)(2,1)S(1)} %get-tuple-element.221), channel_id=1, source_target_pairs={{0,4},{4,0},{8,12},{12,8},{16,20},{20,16},{24,28},{28,24},{1,5},{5... | collective-permute-start | bytes 786440 | tf_op jit(solution)/shard_map/ppermute | solution.py:92
  389.4 24.8 %collective-permute-start.48 = (bf16[1,512,256]{2,1,0:T(8,128)(2,1)S(1)}, bf16[1,512,256]{2,1,0:T(8,128)(2,1)S(1)}, u32[]{:S(2)}, u32[]{:S(2)}) collective-permute-start(bf16[1,512,256]{2,1,0:T(8,128)(2,1)S(1)} %get-tuple-element.223), channel_id=1, source_target_pairs={{0,8},{4,12},{8,0},{12,4},{16,24},{20,28},{24,16},{28,20},{1,9},{5... | collective-permute-start | bytes 786440 | tf_op jit(solution)/shard_map/ppermute | solution.py:92
  391.3 19.8 %collective-permute-start.62 = (f32[96,128]{1,0:T(8,128)S(1)}, f32[96,128]{1,0:T(8,128)S(1)}, u32[]{:S(2)}, u32[]{:S(2)}) collective-permute-start(f32[96,128]{1,0:T(8,128)S(1)} %plus.7.refs_0_), channel_id=1, source_target_pairs={{0,8},{4,12},{8,0},{12,4},{16,24},{20,28},{24,16},{28,20},{1,9},{5... | collective-permute-start | bytes 147464 | tf_op jit(solution)/shard_map/ppermute | solution.py:92
  411.1 33.5 %collective-permute-start.55 = (bf16[2,128,1024]{2,1,0:T(8,128)(2,1)S(1)}, bf16[2,128,1024]{2,1,0:T(8,128)(2,1)S(1)}, u32[]{:S(2)}, u32[]{:S(2)}) collective-permute-start(bf16[2,128,1024]{2,1,0:T(8,128)(2,1)S(1)} %get-tuple-element.235), channel_id=1, source_target_pairs={{0,16},{4,20},{8,24},{12,28},{16,0},{20,4},{24,8},{28,12},{1,17},{... | collective-permute-start | bytes 1572872 | tf_op jit(solution)/shard_map/ppermute | solution.py:92
  411.1 27.8 %collective-permute-start.63 = (f32[96,128]{1,0:T(8,128)S(1)}, f32[96,128]{1,0:T(8,128)S(1)}, u32[]{:S(2)}, u32[]{:S(2)}) collective-permute-start(f32[96,128]{1,0:T(8,128)S(1)} %plus.8.refs_0_), channel_id=1, source_target_pairs={{0,16},{4,20},{8,24},{12,28},{16,0},{20,4},{24,8},{28,12},{1,17},{... | collective-permute-start | bytes 147464 | tf_op jit(solution)/shard_map/ppermute | solution.py:92
  414.3 30.2 %collective-permute-start.49 = (bf16[2,128,256]{2,1,0:T(8,128)(2,1)S(1)}, bf16[2,128,256]{2,1,0:T(8,128)(2,1)S(1)}, u32[]{:S(2)}, u32[]{:S(2)}) collective-permute-start(bf16[2,128,256]{2,1,0:T(8,128)(2,1)S(1)} %get-tuple-element.226), channel_id=1, source_target_pairs={{0,16},{4,20},{8,24},{12,28},{16,0},{20,4},{24,8},{28,12},{1,17},{... | collective-permute-start | bytes 393224 | tf_op jit(solution)/shard_map/ppermute | solution.py:92
  414.4 27.0 %collective-permute-start.50 = (bf16[1,256,256]{2,1,0:T(8,128)(2,1)S(1)}, bf16[1,256,256]{2,1,0:T(8,128)(2,1)S(1)}, u32[]{:S(2)}, u32[]{:S(2)}) collective-permute-start(bf16[1,256,256]{2,1,0:T(8,128)(2,1)S(1)} %get-tuple-element.227), channel_id=1, source_target_pairs={{0,8},{4,12},{8,0},{12,4},{16,24},{20,28},{24,16},{28,20},{1,9},{5... | collective-permute-start | bytes 393224 | tf_op jit(solution)/shard_map/ppermute | solution.py:92
  416.2 25.3 %collective-permute-start.52 = (bf16[1,256,256]{2,1,0:T(8,128)(2,1)S(1)}, bf16[1,256,256]{2,1,0:T(8,128)(2,1)S(1)}, u32[]{:S(2)}, u32[]{:S(2)}) collective-permute-start(bf16[1,256,256]{2,1,0:T(8,128)(2,1)S(1)} %get-tuple-element.230), channel_id=1, source_target_pairs={{0,4},{4,0},{8,12},{12,8},{16,20},{20,16},{24,28},{28,24},{1,5},{5... | collective-permute-start | bytes 393224 | tf_op jit(solution)/shard_map/ppermute | solution.py:92
  438.9 11.5 %collective-permute-start.58 = (bf16[128,1024]{1,0:T(8,128)(2,1)}, bf16[128,1024]{1,0:T(8,128)(2,1)S(1)}, u32[]{:S(2)}, u32[]{:S(2)}) collective-permute-start(bf16[128,1024]{1,0:T(8,128)(2,1)} %fusion.6), channel_id=1, source_target_pairs={{0,2},{1,3},{2,0},{3,1},{4,6},{5,7},{6,4},{7,5},{8,10},{9,11},{10,... | collective-permute-start | bytes 786440 | tf_op jit(solution)/shard_map/ppermute | solution.py:87
  441.4 6.7 %collective-permute-start.51 = (bf16[1,128,256]{2,1,0:T(8,128)(2,1)S(1)}, bf16[1,128,256]{2,1,0:T(8,128)(2,1)S(1)}, u32[]{:S(2)}, u32[]{:S(2)}) collective-permute-start(bf16[1,128,256]{2,1,0:T(8,128)(2,1)S(1)} %get-tuple-element.229), channel_id=1, source_target_pairs={{0,16},{4,20},{8,24},{12,28},{16,0},{20,4},{24,8},{28,12},{1,17},{... | collective-permute-start | bytes 196616 | tf_op jit(solution)/shard_map/ppermute | solution.py:92
  441.6 8.2 %collective-permute-start.53 = (bf16[1,128,256]{2,1,0:T(8,128)(2,1)S(1)}, bf16[1,128,256]{2,1,0:T(8,128)(2,1)S(1)}, u32[]{:S(2)}, u32[]{:S(2)}) collective-permute-start(bf16[1,128,256]{2,1,0:T(8,128)(2,1)S(1)} %get-tuple-element.232), channel_id=1, source_target_pairs={{0,16},{4,20},{8,24},{12,28},{16,0},{20,4},{24,8},{28,12},{1,17},{... | collective-permute-start | bytes 196616 | tf_op jit(solution)/shard_map/ppermute | solution.py:92
  445.4 7.6 %collective-permute-start.56 = (bf16[128,1024]{1,0:T(8,128)(2,1)}, bf16[128,1024]{1,0:T(8,128)(2,1)}, u32[]{:S(2)}, u32[]{:S(2)}) collective-permute-start(bf16[128,1024]{1,0:T(8,128)(2,1)} %fusion.5), channel_id=1, source_target_pairs={{0,2},{1,3},{2,0},{3,1},{4,6},{5,7},{6,4},{7,5},{8,10},{9,11},{10,... | collective-permute-start | bytes 786440 | tf_op jit(solution)/shard_map/ppermute | solution.py:87
  (94 other events, 712.9 us)

commit v7 on v6

--- a/solution.py
+++ b/solution.py
@@ -103,7 +103,7 @@
     return whole_call(kernel, [out], parts, 0, name, deps=deps)[0]
 
 
-def gather_far(rows):
+def gather_far(rows, deps=()):
     held = (rows, [0])
     steps = []
     step = lax.axis_size("dp") // 2
@@ -114,18 +114,24 @@
     for step in steps[:-1]:
         came = (swap_dp(held[0], step), [o ^ step for o in held[1]])
         first.append(came[0])
-        held = merged([held, came])
+        held = merged([held, came], deps)
     pieces = [held]
     if steps:
         pieces.append((swap_dp(held[0], steps[-1]), [o ^ steps[-1] for o in held[1]]))
     return pieces, first[:1]
 
 
-def merged(pieces):
-    return (
-        jnp.concatenate([p for p, _ in pieces], axis=0),
-        [o for _, offsets in pieces for o in offsets],
-    )
+def merged(pieces, deps=()):
+    def kernel(*refs):
+        at = 0
+        for ref in refs[:-1]:
+            refs[-1][at : at + ref.shape[0], :] = ref[...]
+            at += ref.shape[0]
+
+    parts = [p for p, _ in pieces]
+    out = shape((sum(p.shape[0] for p in parts), parts[0].shape[1]), parts[0].dtype)
+    held = whole_call(kernel, [out], parts, 0, "merge_rows", deps=list(deps))[0]
+    return (held, [o for _, offsets in pieces for o in offsets])
 
 
 def gather_near(pieces):
@@ -237,22 +243,12 @@
         return self.keep
 
 
-def sum_all(vector, waits):
-    def plus(one, two, deps):
-        def kernel(a_ref, b_ref, out_ref):
-            out_ref[...] = a_ref[...] + b_ref[...]
-
-        out = shape(one.shape, F32)
-        return whole_call(kernel, [out], [one, two], 0, "plus", deps=deps, limit=SMALL_LIMIT)[0]
-
-    waits = list(waits)
-    held = vector.reshape(-1, 128)
-    for swap, axis in ((swap_tensor, "tensor"), (swap_dp, "dp")):
-        step = 1
-        while step < lax.axis_size(axis):
-            held = plus(held, swap(held, step), waits.pop(0) if waits else [])
-            step *= 2
-    return held.reshape(-1)
+def plus(one, two, deps=()):
+    def kernel(a_ref, b_ref, out_ref):
+        out_ref[...] = a_ref[...] + b_ref[...]
+
+    out = shape(one.shape, F32)
+    return whole_call(kernel, [out], [one, two], 0, "plus", deps=list(deps), limit=SMALL_LIMIT)[0]
 
 
 def project_inputs(x_own, x_across, w_mine, w_other, b_mine, b_other, deps):
@@ -802,24 +798,16 @@
     dp_place = lax.axis_index("dp").astype(jnp.int32).reshape(1)
     att_far, att_first = gather_far(pack([w_query, w_key, w_value, w_out.T], "pack_attention"))
     att_pieces = att_far + gather_near(att_far)
-    share = pack([w_up, w_down.T], "pack_feed", att_first)
+    share = pack([w_up, w_down.T], "pack_feed", [p for p, _ in att_far[1:]] or att_first)
     share_other = swap_tensor(share, ACROSS)
-    mine_far, mine_first = gather_far(share)
-    mine_near = gather_near(mine_far)
-    other_far, other_first = gather_far(share_other)
-    other_near = gather_near(other_far[:1]) + [
-        (swap_tensor(p, ACROSS), offsets) for p, offsets in mine_near[1:]
-    ]
+    att_mine = assemble(att_pieces, dp_place, "assemble_attention", [all_across, share_other])
+    mine_far, mine_first = gather_far(share, [att_mine])
 
     def arrays(pieces):
         return [p for p, _ in pieces]
 
-    att_mine = assemble(att_pieces, dp_place, "assemble_attention")
     att_other = assemble(other_core(att_pieces), dp_place, "assemble_attention_other")
-    project_waits = [mine_first, [share_other]]
-    attend_waits = [arrays(mine_far[1:]), arrays(mine_near[:1]) + other_first]
-    norm_waits = [arrays(mine_near[1:]), arrays(other_far[1:])]
-    ffw_mine = assemble(mine_far + mine_near, dp_place, "assemble_feed")
+    project_waits = [[], mine_first]
 
     biases = jnp.concatenate([b_query, jnp.zeros_like(b_query), b_value])
     qkv_bias_mine, qkv_bias_other = row(biases), row(swap_tensor(biases, CORE))
@@ -844,13 +832,16 @@
     far = [swap_tensor(projected[s][2], CORE) for s in seqs]
     attended = []
     for s in seqs:
-        waits = attend_waits[s] if s < 2 else []
         attended.append(
             attention_forward(
                 projected[s][0], projected[s][1], far[s], masks[s].reshape(1, seq_len),
-                att_mine, att_other, head_size, waits + [p[2] for p in attended[-1:]],
+                att_mine, att_other, head_size, [p[2] for p in attended[-1:]],
             )
         )
+    later = [merged([piece], [attended[0][2]]) for piece in mine_far[1:]]
+    mine_near = gather_near(mine_far[:1] + later)
+    ffw_mine = assemble(mine_far + mine_near, dp_place, "assemble_feed")
+    norm_waits = [arrays(mine_near[:1]) + [attended[-1][2]], [ffw_mine]]
     attended_got = [swap_tensor(attended[s][3], ACROSS) for s in seqs]
     one = []
     for s in seqs:
@@ -861,10 +852,15 @@
                 waits + [p[2] for p in one[-1:]],
             )
         )
+    other_far, _ = gather_far(share_other, [one[0][2]])
+    other_near = gather_near(other_far[:1]) + [
+        (swap_tensor(p, ACROSS), offsets) for p, offsets in mine_near[1:]
+    ]
+    feed_waits = [arrays(other_far[1:]), []]
     normed_far = [swap_tensor(one[s][2], CORE) for s in seqs]
     fed_one = []
     for s in seqs:
-        waits = [p[2] for p in fed_one[-1:]]
+        waits = (feed_waits[s] if s < 2 else []) + [p[2] for p in fed_one[-1:]]
         fed_one.append(
             feed_forward(one[s][2], normed_far[s], ffw_mine, up_bias_mine, None, waits)
         )
@@ -945,12 +941,29 @@
     attended_back += [backward(s, [down_chain.keep, out_made[1]]) for s in seqs[1:]]
     far_back = [swap_tensor(attended_back[s][2], CORE) for s in seqs]
 
+    sums = add_up([attended_back[s][3] for s in seqs], [])
+    small = jnp.concatenate(
+        [
+            sum(two[s][3] for s in seqs).reshape(-1),
+            sum(one_back[s][2] for s in seqs).reshape(-1),
+            placed_in(
+                sum(fed_back[s][4] for s in seqs).reshape(-1),
+                sum(fed_back[s][5] for s in seqs).reshape(-1),
+                ACROSS,
+            ),
+            placed_in(sums[0, :head_dims], sums[1, :head_dims], CORE),
+            placed_in(sums[0, head_dims:], sums[1, head_dims:], CORE),
+        ]
+    ).reshape(-1, 128)
+    bits = [1 << level for level in reversed(near_first)]
     up_chain.fold([attended_back[-1][3]])
+    small = plus(small, swap_tensor(small, CORE), [up_chain.keep])
+
     tokens = pairs(x_own, x_across)
     grad_queries = [attended_back[s][0] for s in seqs]
     query_made = weight_grad(
         tokens, grad_queries, grad_queries, dp_place, [(head_dims, near_first)], "w_query_grad",
-        head_dims, [far_back[0], up_chain.keep],
+        head_dims, [far_back[0], small],
     )
     back = [
         project_back(
@@ -958,25 +971,32 @@
             [query_made[1]],
         )
     ]
+    small = plus(small, swap_tensor(small, ACROSS), [back[0][2]])
     back += [
         project_back(
-            attended_back[s][0], attended_back[s][1], far_back[s], att_mine, att_other,
-            [back[0][2]],
+            attended_back[s][0], attended_back[s][1], far_back[s], att_mine, att_other, [small]
         )
         for s in seqs[1:]
     ]
     input_got = [swap_tensor(back[s][3], ACROSS) for s in seqs]
+    for bit in bits[:1]:
+        small = plus(small, swap_dp(small, bit), [back[-1][2]])
     down_chain.fold([back[-1][2]])
-    query_chain = core_chain([query_made, out_made], near_first, [back[-1][2]])
+    both_got = swap_tensor(jnp.stack([query_made[1], out_made[1]]), CORE)
+    query_chain = Chain(
+        *fold_core([(query_made[0], both_got[0]), (out_made[0], both_got[1])], [back[-1][2]]),
+        near_first,
+    )
     key_value_made = weight_grad(
         tokens, [back[s][0] for s in seqs], [back[s][1] for s in seqs],
         dp_place, [(head_dims, near_first), (head_dims, far_first)], "w_key_value_grad",
-        deps=input_got[:1] + [down_chain.keep, query_chain.keep],
-    )
-    key_chain = core_chain([key_value_made[:2]], near_first, input_got[-1:])
-    value_chain = core_chain([key_value_made[2:]], far_first, input_got[-1:])
+        deps=input_got[:1] + [down_chain.keep, query_chain.keep, small],
+    )
+    up_chain.fold([key_value_made[0]])
+    waits = input_got[-1:] + [up_chain.keep]
+    key_chain = core_chain([key_value_made[:2]], near_first, waits)
+    value_chain = core_chain([key_value_made[2:]], far_first, waits)
     started = [key_chain.keep, value_chain.keep]
-    up_chain.fold(started)
     query_chain.fold(started)
     key_chain.fold()
     value_chain.fold()
@@ -984,29 +1004,15 @@
     query_chain.fold(ending)
     down_chain.fold(ending)
     up_chain.fold(ending)
+    for bit in bits[1:]:
+        small = plus(small, swap_dp(small, bit), ending)
+    small = small.reshape(-1)
+
     input_grad = jnp.stack(
         [
             (one_back[s][0] + (back[s][2] + input_got[s].astype(F32))).astype(BF16)
             for s in seqs
         ]
-    )
-
-    sums = add_up([attended_back[s][3] for s in seqs], [query_made[1]])
-    small = sum_all(
-        jnp.concatenate(
-            [
-                sum(two[s][3] for s in seqs).reshape(-1),
-                sum(one_back[s][2] for s in seqs).reshape(-1),
-                placed_in(
-                    sum(fed_back[s][4] for s in seqs).reshape(-1),
-                    sum(fed_back[s][5] for s in seqs).reshape(-1),
-                    ACROSS,
-                ),
-                placed_in(sums[0, :head_dims], sums[1, :head_dims], CORE),
-                placed_in(sums[0, head_dims:], sums[1, head_dims:], CORE),
-            ]
-        ),
-        [[back[0][2]], [back[-1][2]], started, started, ending],
     )
 
     def over_y(both):

time: 461 us -> 466 us (1.011)
  local copies, waits for them, and re-layouts: 53.1 us -> 60.2 us
  waiting for transfers between devices: 99.3 us -> 93.4 us
    unnamed x201 -> x220, local copies, waits for them, and re-layouts: 42.3 us -> 48.9 us
    pallas_call x40 -> x44, Pallas kernels: 121 us -> 125 us  [whole_call(): pl.pallas_call(after(kernel, len(args), deps), out_shape=tuple(outs), in_...]
    ppermute x35 -> x34, waiting for transfers between devices: 24 us -> 20.1 us  [swap_tensor(): return lax.ppermute(array, 'tensor', [(i, i ^ bit) for i in range(size)])]
    ppermute x35 -> x34, starting transfers between devices: 18.7 us -> 18.3 us  [swap_tensor(): return lax.ppermute(array, 'tensor', [(i, i ^ bit) for i in range(size)])]
  transfers between devices with their start and end apart: 64 -> 63, of which waited for: 17 -> 17; matrix products, arithmetic and copies ran while one was open for 6% -> 6% of each run, Pallas kernels for 49% -> 49%
where the time goes in v7:
time: 466 us; the launch traced here: 460 us
  Pallas kernels  238 us (51%)
  waiting for transfers between devices  93.4 us (20%)
  local copies, waits for them, and re-layouts  60.2 us (13%)
  starting transfers between devices  57.9 us (12%)
  other arithmetic  8.19 us (2%)
    pallas_call x44, Pallas kernels, whole_call(): pl.pallas_call(after(kernel, len(args), deps), out_shape=tuple(outs), in_...  125 us
    pallas_call x11, Pallas kernels, streamed_call(): pl.pallas_call(after(kernel, len(args), deps), grid=grid, out_shape=tuple...  98.8 us
    ppermute x29, waiting for transfers between devices, swap_dp(): return lax.ppermute(array, 'dp', [(i, i ^ bit) for i in range(size)])  73.3 us
    unnamed x220, local copies, waits for them, and re-layouts  48.9 us
    ppermute x29, starting transfers between devices, swap_dp(): return lax.ppermute(array, 'dp', [(i, i ^ bit) for i in range(size)])  39.6 us
    ppermute x34, waiting for transfers between devices, swap_tensor(): return lax.ppermute(array, 'tensor', [(i, i ^ bit) for i in range(size)])  20.1 us
    ppermute x34, starting transfers between devices, swap_tensor(): return lax.ppermute(array, 'tensor', [(i, i ^ bit) for i in range(size)])  18.3 us
    pallas_call x4, Pallas kernels, assemble(): pl.pallas_call(after(kernel, 1 + len(arrays), deps), out_shape=out, in_sp...  14.9 us
  transfers between devices with their start and end apart: 63, of which 17 were waited for; matrix products, arithmetic and copies ran while one was open for 6% of the time, Pallas kernels for 49%

profile of v7, /device:TPU:0, one launch (start us, length us, event | category | flops | bytes accessed | tf_op | source)
XLA Modules:
  0.0 460.0 jit_solution(1925079038994753173)
XLA Ops:
  0.7 1.6 copy.39
  2.3 1.7 pack_attention.1.refs_0_
  3.9 4.0 collective-permute-start.1
  8.0 12.1 %collective-permute-done.1.refs_1_ = bf16[128,1024]{1,0:T(8,128)(2,1)S(1)} collective-permute-done((bf16[128,1024]{1,0:T(8,128)(2,1)}, bf16[128,1024]{1,0:T(8,128)(2,1)S(1)}, u32[]{:S(2)}, u32[]{:S(2)}) %collective-permute-start.1) | collective-permute-done | bytes 262176 | tf_op jit(solution)/shard_map/ppermute | solution.py:92
  20.8 1.9 merge_rows.4.refs_1_
  23.5 1.5 collective-permute-start
  25.0 1.8 copy.40
  28.3 7.7 %collective-permute-done.2.refs_2_ = bf16[256,1024]{1,0:T(8,128)(2,1)S(1)} collective-permute-done((bf16[256,1024]{1,0:T(8,128)(2,1)}, bf16[256,1024]{1,0:T(8,128)(2,1)S(1)}, u32[]{:S(2)}, u32[]{:S(2)}) %collective-permute-start.2) | collective-permute-done | bytes 524320 | tf_op jit(solution)/shard_map/ppermute | solution.py:92
  37.4 1.8 pack_feed.1.refs_0_
  39.2 1.5 collective-permute-start.5
  42.2 3.3 collective-permute-start.13
  45.4 4.3 collective-permute-done.refs_5_
  49.8 1.9 collective-permute-done.4.refs_4_
  51.6 8.1 %collective-permute-done.5.refs_6_.refs_0_ = bf16[128,2048]{1,0:T(8,128)(2,1)S(1)} collective-permute-done((bf16[128,2048]{1,0:T(8,128)(2,1)}, bf16[128,2048]{1,0:T(8,128)(2,1)S(1)}, u32[]{:S(2)}, u32[]{:S(2)}) %collective-permute-start.5) | collective-permute-done | bytes 524320 | tf_op jit(solution)/shard_map/ppermute | solution.py:87
  59.7 2.4 slice_bitcast_fusion.9
  63.8 3.0 assemble_attention.1.refs_2_.refs_4_.refs_6_.refs_3_
  68.7 2.9 assemble_attention_other.1.refs_3_.refs_5_.refs_7_.refs_4_
  71.7 5.6 %project_inputs.2 = (bf16[512,768]{1,0:T(8,128)(2,1)}, bf16[512,768]{1,0:T(8,128)(2,1)}, bf16[512,1024]{1,0:T(8,128)(2,1)}) custom-call(bf16[256,1024]{1,0:T(8,128)(2,1)} %get-tuple-element.285.refs_0_.refs_1_, bf16[256,1024]{1,0:T(8,128)(2,1)} %get-tuple-element.283.refs_1_.refs_2_, bf16[1024,1024]{1,0:T(8,128)(2,1)} %assemble_attention.1.refs_2_.refs_4_.refs_6_.refs_3_, ...), custom_call_target="tpu_custom_call" | custom-call | flops 1610612 | bytes 7870 | tf_op jit(solution)/shard_map/project_inputs/pallas_call | solution.py:47
  78.4 2.3 merge_rows.5.refs_1_
  81.7 5.7 %project_inputs.3 = (bf16[512,768]{1,0:T(8,128)(2,1)}, bf16[512,768]{1,0:T(8,128)(2,1)}, bf16[512,1024]{1,0:T(8,128)(2,1)}) custom-call(bf16[256,1024]{1,0:T(8,128)(2,1)} %get-tuple-element.286.refs_0_.refs_3_, bf16[256,1024]{1,0:T(8,128)(2,1)} %get-tuple-element.284.refs_1_.refs_4_, bf16[1024,1024]{1,0:T(8,128)(2,1)} %assemble_attention.1.refs_2_.refs_4_.refs_6_.refs_3_, ...), custom_call_target="tpu_custom_call" | custom-call | flops 1610612 | bytes 7870 | tf_op jit(solution)/shard_map/project_inputs/pallas_call | solution.py:47
  91.7 12.9 %attention_forward.2 = (bf16[512,256]{1,0:T(8,128)(2,1)}, bf16[512,256]{1,0:T(8,128)(2,1)}, f32[256,1024]{1,0:T(8,128)}, bf16[256,1024]{1,0:T(8,128)(2,1)}) custom-call(bf16[512,768]{1,0:T(8,128)(2,1)} %get-tuple-element.131.refs_0_, bf16[512,768]{1,0:T(8,128)(2,1)} %get-tuple-element.132.refs_1_, bf16[512,1024]{1,0:T(8,128)(2,1)} %copy-done.82, ...), custom_call_target="tpu_custom_call" | custom-call | flops 8589934 | bytes 8916 | tf_op jit(solution)/shard_map/attention_forward/pallas_call | solution.py:47
  107.1 2.3 merge_rows.7
  110.8 1.5 collective-permute-start.12
  112.3 3.3 collective-permute-start.17
  117.2 12.8 %attention_forward.3 = (bf16[512,256]{1,0:T(8,128)(2,1)}, bf16[512,256]{1,0:T(8,128)(2,1)}, f32[256,1024]{1,0:T(8,128)}, bf16[256,1024]{1,0:T(8,128)(2,1)}) custom-call(bf16[512,768]{1,0:T(8,128)(2,1)} %get-tuple-element.136.refs_0_, bf16[512,768]{1,0:T(8,128)(2,1)} %get-tuple-element.137.refs_1_, bf16[512,1024]{1,0:T(8,128)(2,1)} %copy-done.79, ...), custom_call_target="tpu_custom_call" | custom-call | flops 8589934 | bytes 8916 | tf_op jit(solution)/shard_map/attention_forward/pallas_call | solution.py:47
  130.1 1.5 copy-done.20
  133.9 3.5 collective-permute-done.17.refs_1_
  138.3 2.2 merge_rows.6.refs_1_
  142.2 1.5 collective-permute-start.22
  143.7 4.6 assemble_feed.1.refs_6_.refs_2_.refs_3_.refs_4_
  148.3 7.1 %collective-permute-done.23.refs_2_ = bf16[256,1024]{1,0:T(8,128)(2,1)S(1)} collective-permute-done((bf16[256,1024]{1,0:T(8,128)(2,1)S(1)}, bf16[256,1024]{1,0:T(8,128)(2,1)S(1)}, u32[]{:S(2)}, u32[]{:S(2)}) %collective-permute-start.23) | collective-permute-done | bytes 524320 | tf_op jit(solution)/shard_map/ppermute | solution.py:87
  155.4 2.2 copy-done
  159.6 6.1 %collective-permute-done.18.refs_5_.refs_2_ = bf16[256,2048]{1,0:T(8,128)(2,1)S(1)} collective-permute-done((bf16[256,2048]{1,0:T(8,128)(2,1)}, bf16[256,2048]{1,0:T(8,128)(2,1)S(1)}, u32[]{:S(2)}, u32[]{:S(2)}) %collective-permute-start.18) | collective-permute-done | bytes 1048608 | tf_op jit(solution)/shard_map/ppermute | solution.py:92
  166.8 8.8 %feed_forward.4 = (bf16[512,1024]{1,0:T(8,128)(2,1)}, bf16[512,1024]{1,0:T(8,128)(2,1)}, f32[512,1024]{1,0:T(8,128)}) custom-call(bf16[256,1024]{1,0:T(8,128)(2,1)} %copy-done.3, bf16[256,1024]{1,0:T(8,128)(2,1)} %copy-done.66, bf16[1024,2048]{1,0:T(8,128)(2,1)} %assemble_feed.1.refs_6_.refs_2_.refs_3_.refs_4_, ...), custom_call_target="tpu_custom_call" | custom-call | flops 2147483 | bytes 13635 | tf_op jit(solution)/shard_map/feed_forward/pallas_call | solution.py:64
  176.5 8.8 %feed_forward.5 = (bf16[512,1024]{1,0:T(8,128)(2,1)}, bf16[512,1024]{1,0:T(8,128)(2,1)}, f32[512,1024]{1,0:T(8,128)}) custom-call(bf16[256,1024]{1,0:T(8,128)(2,1)} %copy-done.10, bf16[256,1024]{1,0:T(8,128)(2,1)} %copy-done.67, bf16[1024,2048]{1,0:T(8,128)(2,1)} %assemble_feed.1.refs_6_.refs_2_.refs_3_.refs_4_, ...), custom_call_target="tpu_custom_call" | custom-call | flops 2147483 | bytes 13635 | tf_op jit(solution)/shard_map/feed_forward/pallas_call | solution.py:64
  186.4 4.5 assemble_feed_other.1.refs_2_.refs_3_.refs_5_
  191.4 10.0 %feed_forward.6 = (bf16[512,1024]{1,0:T(8,128)(2,1)}, bf16[512,1024]{1,0:T(8,128)(2,1)}, f32[256,1024]{1,0:T(8,128)}, bf16[256,1024]{1,0:T(8,128)(2,1)}) custom-call(bf16[256,1024]{1,0:T(8,128)(2,1)} %copy-done.3, bf16[256,1024]{1,0:T(8,128)(2,1)} %copy-done.66, bf16[1024,2048]{1,0:T(8,128)(2,1)} %assemble_feed_other.1.refs_2_.refs_3_.refs_5_, ...), custom_call_target="tpu_custom_call" | custom-call | flops 2147483 | bytes 15208 | tf_op jit(solution)/shard_map/feed_forward/pallas_call | solution.py:64
  201.5 9.8 %feed_forward.7 = (bf16[512,1024]{1,0:T(8,128)(2,1)}, bf16[512,1024]{1,0:T(8,128)(2,1)}, f32[256,1024]{1,0:T(8,128)}, bf16[256,1024]{1,0:T(8,128)(2,1)}) custom-call(bf16[256,1024]{1,0:T(8,128)(2,1)} %copy-done.10, bf16[256,1024]{1,0:T(8,128)(2,1)} %copy-done.67, bf16[1024,2048]{1,0:T(8,128)(2,1)} %assemble_feed_other.1.refs_2_.refs_3_.refs_5_, ...), custom_call_target="tpu_custom_call" | custom-call | flops 2147483 | bytes 15208 | tf_op jit(solution)/shard_map/feed_forward/pallas_call | solution.py:64
  218.7 11.4 %feed_forward_back.2 = (bf16[512,1024]{1,0:T(8,128)(2,1)}, bf16[512,1024]{1,0:T(8,128)(2,1)}, f32[256,1024]{1,0:T(8,128)}, bf16[256,1024]{1,0:T(8,128)(2,1)}, f32[1,1024]{1,0:T(1,128)}, /*index=5*/f32[1,1024]{1,0:T(1,128)}) custom-call(bf16[256,1024]{1,0:T(8,128)(2,1)} %copy-done.26, bf16[256,1024]{1,0:T(8,128)(2,1)} %copy-done.76, ...), custom_call_target="tpu_custom_call" | custom-call | flops 4294967 | bytes 23601 | tf_op jit(solution)/shard_map/feed_forward_back/pallas_call | solution.py:64
  231.3 10.0 %w_down_grad.1 = (f32[2,512,1024]{2,1,0:T(8,128)}, bf16[2,512,1024]{2,1,0:T(8,128)(2,1)}) custom-call(s32[1]{0:T(128)} %bitcast.2.refs_0_, bf16[256,1024]{1,0:T(8,128)(2,1)} %copy-done.26, bf16[256,1024]{1,0:T(8,128)(2,1)} %copy-done.76, bf16[256,1024]{1,0:T(8,128)(2,1)} %copy-done.27, bf16[256,1024]{1,0:T(8,128)(2,1)} %copy-done.77, ...), custom_call_target="tpu_custom_call" | custom-call | flops 4294967 | bytes 12582 | tf_op jit(solution)/shard_map/w_down_grad/pallas_call | solution.py:64
  241.4 11.5 %feed_forward_back.3 = (bf16[512,1024]{1,0:T(8,128)(2,1)}, bf16[512,1024]{1,0:T(8,128)(2,1)}, f32[256,1024]{1,0:T(8,128)}, bf16[256,1024]{1,0:T(8,128)(2,1)}, f32[1,1024]{1,0:T(1,128)}, /*index=5*/f32[1,1024]{1,0:T(1,128)}) custom-call(bf16[256,1024]{1,0:T(8,128)(2,1)} %copy-done.27, bf16[256,1024]{1,0:T(8,128)(2,1)} %copy-done.77, ...), custom_call_target="tpu_custom_call" | custom-call | flops 4294967 | bytes 23601 | tf_op jit(solution)/shard_map/feed_forward_back/pallas_call | solution.py:64
  266.4 10.1 %w_up_grad.1 = (f32[2,512,1024]{2,1,0:T(8,128)}, bf16[2,512,1024]{2,1,0:T(8,128)(2,1)}) custom-call(s32[1]{0:T(128)} %bitcast.2.refs_0_, bf16[256,1024]{1,0:T(8,128)(2,1)} %copy-done.3, bf16[256,1024]{1,0:T(8,128)(2,1)} %copy-done.66, bf16[256,1024]{1,0:T(8,128)(2,1)} %copy-done.10, bf16[256,1024]{1,0:T(8,128)(2,1)} %copy-done.67, ...), custom_call_target="tpu_custom_call" | custom-call | flops 4294967 | bytes 12582 | tf_op jit(solution)/shard_map/w_up_grad/pallas_call | solution.py:64
  277.1 26.3 %attention_backward.2 = (bf16[512,512]{1,0:T(8,128)(2,1)}, f32[512,1024]{1,0:T(8,128)}, bf16[512,1024]{1,0:T(8,128)(2,1)}, f32[2,512]{1,0:T(2,128)}) custom-call(bf16[512,768]{1,0:T(8,128)(2,1)} %get-tuple-element.131.refs_0_, bf16[512,768]{1,0:T(8,128)(2,1)} %get-tuple-element.132.refs_1_, bf16[512,1024]{1,0:T(8,128)(2,1)} %copy-done.82, ...), custom_call_target="tpu_custom_call" | custom-call | flops 21474836480 | bytes 11542 | tf_op jit(solution)/shard_map/attention_backward/pallas_call | solution.py:47
  303.4 4.4 w_out_grad.1
  307.8 1.9 fold.15
  312.1 26.2 %attention_backward.3 = (bf16[512,512]{1,0:T(8,128)(2,1)}, f32[512,1024]{1,0:T(8,128)}, bf16[512,1024]{1,0:T(8,128)(2,1)}, f32[2,512]{1,0:T(2,128)}) custom-call(bf16[512,768]{1,0:T(8,128)(2,1)} %get-tuple-element.136.refs_0_, bf16[512,768]{1,0:T(8,128)(2,1)} %get-tuple-element.137.refs_1_, bf16[512,1024]{1,0:T(8,128)(2,1)} %copy-done.79, ...), custom_call_target="tpu_custom_call" | custom-call | flops 21474836480 | bytes 11542 | tf_op jit(solution)/shard_map/attention_backward/pallas_call | solution.py:47
  342.1 2.2 copy-done.16
  346.9 4.4 w_query_grad.1
  351.3 2.1 pad_maximum_fusion.2
  353.6 1.8 collective-permute-start.47
  356.2 6.3 %project_back.2 = (bf16[512,512]{1,0:T(8,128)(2,1)}, bf16[512,512]{1,0:T(8,128)(2,1)}, f32[256,1024]{1,0:T(8,128)}, bf16[256,1024]{1,0:T(8,128)(2,1)}) custom-call(bf16[512,512]{1,0:T(8,128)(2,1)} %get-tuple-element.180.refs_5_.refs_7_.refs_0_, f32[512,1024]{1,0:T(8,128)} %get-tuple-element.181.refs_1_, ...), custom_call_target="tpu_custom_call" | custom-call | flops 1610612 | bytes 10485 | tf_op jit(solution)/shard_map/project_back/pallas_call | solution.py:47
  366.0 6.4 %project_back.3 = (bf16[512,512]{1,0:T(8,128)(2,1)}, bf16[512,512]{1,0:T(8,128)(2,1)}, f32[256,1024]{1,0:T(8,128)}, bf16[256,1024]{1,0:T(8,128)(2,1)}) custom-call(bf16[512,512]{1,0:T(8,128)(2,1)} %get-tuple-element.191.refs_6_.refs_8_.refs_0_, f32[512,1024]{1,0:T(8,128)} %get-tuple-element.207.refs_1_, bf16[512,1024]{1,0:T(8,128)(2,1)} %copy-done.80, ...), custom_call_target="tpu_custom_call" | custom-call | flops 1610612 | bytes 10485 | tf_op jit(solution)/shard_map/project_back/pallas_call | solution.py:47
  378.6 9.6 %w_key_value_grad.1 = (f32[1024,256]{1,0:T(8,128)}, bf16[1024,256]{1,0:T(8,128)(2,1)}, f32[1024,256]{1,0:T(8,128)}, bf16[1024,256]{1,0:T(8,128)(2,1)}) custom-call(s32[1]{0:T(128)} %bitcast.2.refs_0_, bf16[256,1024]{1,0:T(8,128)(2,1)} %get-tuple-element.285.refs_0_.refs_1_, bf16[256,1024]{1,0:T(8,128)(2,1)} %get-tuple-element.283.refs_1_.refs_2_, ...), custom_call_target="tpu_custom_call" | custom-call | flops 2147483 | bytes 7340 | tf_op jit(solution)/shard_map/w_key_value_grad/pallas_call | solution.py:64
  388.8 1.6 collective-permute-start.43
  394.3 1.7 collective-permute-start.59
  396.2 6.4 %collective-permute-done.43.refs_1_ = bf16[2,512,256]{2,1,0:T(8,128)(2,1)S(1)} collective-permute-done((bf16[2,512,256]{2,1,0:T(8,128)(2,1)S(1)}, bf16[2,512,256]{2,1,0:T(8,128)(2,1)S(1)}, u32[]{:S(2)}, u32[]{:S(2)}) %collective-permute-start.43) | collective-permute-done | bytes 524320 | tf_op jit(solution)/shard_map/ppermute | solution.py:92
  402.8 1.6 collective-permute-start.49
  404.4 1.7 collective-permute-start.50
  407.8 4.1 collective-permute-done.50.refs_1_
  412.3 14.5 %collective-permute-done.51.refs_1_ = bf16[1,512,256]{2,1,0:T(8,128)(2,1)S(1)} collective-permute-done((bf16[1,512,256]{2,1,0:T(8,128)(2,1)S(1)}, bf16[1,512,256]{2,1,0:T(8,128)(2,1)S(1)}, u32[]{:S(2)}, u32[]{:S(2)}) %collective-permute-start.51) | collective-permute-done | bytes 262176 | tf_op jit(solution)/shard_map/ppermute | solution.py:92
  426.9 4.3 collective-permute-start.52
  433.0 11.0 %collective-permute-done.59.refs_1_ = bf16[2,128,1024]{2,1,0:T(8,128)(2,1)S(1)} collective-permute-done((bf16[2,128,1024]{2,1,0:T(8,128)(2,1)S(1)}, bf16[2,128,1024]{2,1,0:T(8,128)(2,1)S(1)}, u32[]{:S(2)}, u32[]{:S(2)}) %collective-permute-start.59) | collective-permute-done | bytes 524320 | tf_op jit(solution)/shard_map/ppermute | solution.py:92
  445.1 2.9 collective-permute-done.62.refs_1_
  450.7 3.0 collective-permute-start.56
  (381 shorter events, 92.2 us)
Async XLA Ops:
  0.7 40.1 %copy-start.100 = (f32[256]{0:T(256)S(1)}, f32[256]{0:T(256)}, u32[]{:S(2)}) copy-start(f32[256]{0:T(256)} %param.27) | copy-start | bytes 3076
  3.9 16.2 %collective-permute-start.1 = (bf16[128,1024]{1,0:T(8,128)(2,1)}, bf16[128,1024]{1,0:T(8,128)(2,1)S(1)}, u32[]{:S(2)}, u32[]{:S(2)}) collective-permute-start(bf16[128,1024]{1,0:T(8,128)(2,1)} %pack_attention.1.refs_0_), channel_id=1, source_target_pairs={{0,16},{4,20},{8,24},{12,28},{16,0},{20,4},{24,8},{28,12},{1,17},{... | collective-permute-start | bytes 786440 | tf_op jit(solution)/shard_map/ppermute | solution.py:92
  22.7 13.3 %collective-permute-start.2 = (bf16[256,1024]{1,0:T(8,128)(2,1)}, bf16[256,1024]{1,0:T(8,128)(2,1)S(1)}, u32[]{:S(2)}, u32[]{:S(2)}) collective-permute-start(bf16[256,1024]{1,0:T(8,128)(2,1)} %merge_rows.4.refs_1_), channel_id=1, source_target_pairs={{0,8},{4,12},{8,0},{12,4},{16,24},{20,28},{24,16},{28,20},{1,9},{5... | collective-permute-start | bytes 1572872 | tf_op jit(solution)/shard_map/ppermute | solution.py:92
  23.5 26.3 %collective-permute-start = (bf16[2,256,1024]{2,1,0:T(8,128)(2,1)}, bf16[2,256,1024]{2,1,0:T(8,128)(2,1)S(1)}, u32[]{:S(2)}, u32[]{:S(2)}) collective-permute-start(bf16[2,256,1024]{2,1,0:T(8,128)(2,1)} %param.18), channel_id=1, source_target_pairs={{0,2},{1,3},{2,0},{3,1},{4,6},{5,7},{6,4},{7,5},{8,10},{9,11},{10,... | collective-permute-start | bytes 3145736 | tf_op jit(solution)/shard_map/ppermute | solution.py:87
  26.8 15.4 %collective-permute-start.3 = (bf16[256,1024]{1,0:T(8,128)(2,1)}, bf16[256,1024]{1,0:T(8,128)(2,1)}, u32[]{:S(2)}, u32[]{:S(2)}) collective-permute-start(bf16[256,1024]{1,0:T(8,128)(2,1)} %merge_rows.4.refs_1_), channel_id=1, source_target_pairs={{0,4},{4,0},{8,12},{12,8},{16,20},{20,16},{24,28},{28,24},{1,5},{5... | collective-permute-start | bytes 1572872 | tf_op jit(solution)/shard_map/ppermute | solution.py:92
  36.0 15.7 %collective-permute-start.4 = (bf16[256,1024]{1,0:T(8,128)(2,1)S(1)}, bf16[256,1024]{1,0:T(8,128)(2,1)}, u32[]{:S(2)}, u32[]{:S(2)}) collective-permute-start(bf16[256,1024]{1,0:T(8,128)(2,1)S(1)} %collective-permute-done.2.refs_2_), channel_id=1, source_target_pairs={{0,4},{4,0},{8,12},{12,8},{16,20},{20,16},{24,28},{28,24},{1,5},{5... | collective-permute-start | bytes 1572872 | tf_op jit(solution)/shard_map/ppermute | solution.py:92
  39.2 20.5 %collective-permute-start.5 = (bf16[128,2048]{1,0:T(8,128)(2,1)}, bf16[128,2048]{1,0:T(8,128)(2,1)S(1)}, u32[]{:S(2)}, u32[]{:S(2)}) collective-permute-start(bf16[128,2048]{1,0:T(8,128)(2,1)} %pack_feed.1.refs_0_), channel_id=1, source_target_pairs={{0,2},{1,3},{2,0},{3,1},{4,6},{5,7},{6,4},{7,5},{8,10},{9,11},{10,... | collective-permute-start | bytes 1572872 | tf_op jit(solution)/shard_map/ppermute | solution.py:87
  40.7 1.2 collective-permute-start.10
  42.0 24.8 %collective-permute-start.6 = (bf16[256,1024]{1,0:T(8,128)(2,1)S(1)}, bf16[256,1024]{1,0:T(8,128)(2,1)S(1)}, u32[]{:S(2)}, u32[]{:S(2)}) collective-permute-start(bf16[256,1024]{1,0:T(8,128)(2,1)S(1)} %copy-done.75), channel_id=1, source_target_pairs={{0,1},{1,0},{2,3},{3,2},{4,5},{5,4},{6,7},{7,6},{8,9},{9,8},{10,11... | collective-permute-start | bytes 1572872 | tf_op jit(solution)/shard_map/ppermute | solution.py:87
  42.2 35.4 %collective-permute-start.13 = (bf16[128,2048]{1,0:T(8,128)(2,1)}, bf16[128,2048]{1,0:T(8,128)(2,1)S(1)}, u32[]{:S(2)}, u32[]{:S(2)}) collective-permute-start(bf16[128,2048]{1,0:T(8,128)(2,1)} %pack_feed.1.refs_0_), channel_id=1, source_target_pairs={{0,16},{4,20},{8,24},{12,28},{16,0},{20,4},{24,8},{28,12},{1,17},{... | collective-permute-start | bytes 1572872 | tf_op jit(solution)/shard_map/ppermute | solution.py:92
  49.8 17.0 %collective-permute-start.7 = (bf16[256,1024]{1,0:T(8,128)(2,1)}, bf16[256,1024]{1,0:T(8,128)(2,1)S(1)}, u32[]{:S(2)}, u32[]{:S(2)}) collective-permute-start(bf16[256,1024]{1,0:T(8,128)(2,1)} %copy-done.74), channel_id=1, source_target_pairs={{0,1},{1,0},{2,3},{3,2},{4,5},{5,4},{6,7},{7,6},{8,9},{9,8},{10,11... | collective-permute-start | bytes 1572872 | tf_op jit(solution)/shard_map/ppermute | solution.py:87
  51.6 15.2 %collective-permute-start.8 = (bf16[256,1024]{1,0:T(8,128)(2,1)}, bf16[256,1024]{1,0:T(8,128)(2,1)S(1)}, u32[]{:S(2)}, u32[]{:S(2)}) collective-permute-start(bf16[256,1024]{1,0:T(8,128)(2,1)} %collective-permute-done.3.refs_3_), channel_id=1, source_target_pairs={{0,1},{1,0},{2,3},{3,2},{4,5},{5,4},{6,7},{7,6},{8,9},{9,8},{10,11... | collective-permute-start | bytes 1572872 | tf_op jit(solution)/shard_map/ppermute | solution.py:87
  59.7 7.1 %collective-permute-start.9 = (bf16[256,1024]{1,0:T(8,128)(2,1)}, bf16[256,1024]{1,0:T(8,128)(2,1)S(1)}, u32[]{:S(2)}, u32[]{:S(2)}) collective-permute-start(bf16[256,1024]{1,0:T(8,128)(2,1)} %collective-permute-done.4.refs_4_), channel_id=1, source_target_pairs={{0,1},{1,0},{2,3},{3,2},{4,5},{5,4},{6,7},{7,6},{8,9},{9,8},{10,11... | collective-permute-start | bytes 1572872 | tf_op jit(solution)/shard_map/ppermute | solution.py:87
  77.2 13.4 %collective-permute-start.11 = (bf16[512,1024]{1,0:T(8,128)(2,1)}, bf16[512,1024]{1,0:T(8,128)(2,1)S(1)}, u32[]{:S(2)}, u32[]{:S(2)}) collective-permute-start(bf16[512,1024]{1,0:T(8,128)(2,1)} %get-tuple-element.133.refs_7_), channel_id=1, source_target_pairs={{0,1},{1,0},{2,3},{3,2},{4,5},{5,4},{6,7},{7,6},{8,9},{9,8},{10,11... | collective-permute-start | bytes 3145736 | tf_op jit(solution)/shard_map/ppermute | solution.py:87
  80.6 25.5 %collective-permute-start.20 = (bf16[256,2048]{1,0:T(8,128)(2,1)}, bf16[256,2048]{1,0:T(8,128)(2,1)S(1)}, u32[]{:S(2)}, u32[]{:S(2)}) collective-permute-start(bf16[256,2048]{1,0:T(8,128)(2,1)} %merge_rows.5.refs_1_), channel_id=1, source_target_pairs={{0,8},{4,12},{8,0},{12,4},{16,24},{20,28},{24,16},{28,20},{1,9},{5... | collective-permute-start | bytes 3145736 | tf_op jit(solution)/shard_map/ppermute | solution.py:92
  87.4 28.8 %collective-permute-start.15 = (bf16[512,1024]{1,0:T(8,128)(2,1)}, bf16[512,1024]{1,0:T(8,128)(2,1)S(1)}, u32[]{:S(2)}, u32[]{:S(2)}) collective-permute-start(bf16[512,1024]{1,0:T(8,128)(2,1)} %get-tuple-element.138), channel_id=1, source_target_pairs={{0,1},{1,0},{2,3},{3,2},{4,5},{5,4},{6,7},{7,6},{8,9},{9,8},{10,11... | collective-permute-start | bytes 3145736 | tf_op jit(solution)/shard_map/ppermute | solution.py:87
  88.8 41.2 %collective-permute-start.14 = (bf16[256,2048]{1,0:T(8,128)(2,1)S(1)}, bf16[256,2048]{1,0:T(8,128)(2,1)S(1)}, u32[]{:S(2)}, u32[]{:S(2)}) collective-permute-start(bf16[256,2048]{1,0:T(8,128)(2,1)S(1)} %copy-done.69), channel_id=1, source_target_pairs={{0,4},{4,0},{8,12},{12,8},{16,20},{20,16},{24,28},{28,24},{1,5},{5... | collective-permute-start | bytes 3145736 | tf_op jit(solution)/shard_map/ppermute | solution.py:92
  109.3 32.9 %collective-permute-start.21 = (bf16[256,2048]{1,0:T(8,128)(2,1)}, bf16[256,2048]{1,0:T(8,128)(2,1)}, u32[]{:S(2)}, u32[]{:S(2)}) collective-permute-start(bf16[256,2048]{1,0:T(8,128)(2,1)} %merge_rows.7), channel_id=1, source_target_pairs={{0,4},{4,0},{8,12},{12,8},{16,20},{20,16},{24,28},{28,24},{1,5},{5... | collective-permute-start | bytes 3145736 | tf_op jit(solution)/shard_map/ppermute | solution.py:92
  110.8 19.2 %collective-permute-start.12 = (bf16[256,1024]{1,0:T(8,128)(2,1)S(1)}, bf16[256,1024]{1,0:T(8,128)(2,1)S(1)}, u32[]{:S(2)}, u32[]{:S(2)}) collective-permute-start(bf16[256,1024]{1,0:T(8,128)(2,1)S(1)} %copy-done.103), channel_id=1, source_target_pairs={{0,2},{1,3},{2,0},{3,1},{4,6},{5,7},{6,4},{7,5},{8,10},{9,11},{10,... | collective-permute-start | bytes 1572872 | tf_op jit(solution)/shard_map/ppermute | solution.py:87
  112.3 25.1 %collective-permute-start.17 = (bf16[128,2048]{1,0:T(8,128)(2,1)S(1)}, bf16[128,2048]{1,0:T(8,128)(2,1)S(1)}, u32[]{:S(2)}, u32[]{:S(2)}) collective-permute-start(bf16[128,2048]{1,0:T(8,128)(2,1)S(1)} %copy-done.73), channel_id=1, source_target_pairs={{0,16},{4,20},{8,24},{12,28},{16,0},{20,4},{24,8},{28,12},{1,17},{... | collective-permute-start | bytes 1572872 | tf_op jit(solution)/shard_map/ppermute | solution.py:92
  140.5 25.3 %collective-permute-start.18 = (bf16[256,2048]{1,0:T(8,128)(2,1)}, bf16[256,2048]{1,0:T(8,128)(2,1)S(1)}, u32[]{:S(2)}, u32[]{:S(2)}) collective-permute-start(bf16[256,2048]{1,0:T(8,128)(2,1)} %merge_rows.6.refs_1_), channel_id=1, source_target_pairs={{0,8},{4,12},{8,0},{12,4},{16,24},{20,28},{24,16},{28,20},{1,9},{5... | collective-permute-start | bytes 3145736 | tf_op jit(solution)/shard_map/ppermute | solution.py:92
  140.5 14.8 %collective-permute-start.23 = (bf16[256,1024]{1,0:T(8,128)(2,1)S(1)}, bf16[256,1024]{1,0:T(8,128)(2,1)S(1)}, u32[]{:S(2)}, u32[]{:S(2)}) collective-permute-start(bf16[256,1024]{1,0:T(8,128)(2,1)S(1)} %copy-done.102), channel_id=1, source_target_pairs={{0,2},{1,3},{2,0},{3,1},{4,6},{5,7},{6,4},{7,5},{8,10},{9,11},{10,... | collective-permute-start | bytes 1572872 | tf_op jit(solution)/shard_map/ppermute | solution.py:87
  141.1 44.2 %collective-permute-start.19 = (bf16[256,2048]{1,0:T(8,128)(2,1)}, bf16[256,2048]{1,0:T(8,128)(2,1)S(1)}, u32[]{:S(2)}, u32[]{:S(2)}) collective-permute-start(bf16[256,2048]{1,0:T(8,128)(2,1)} %merge_rows.6.refs_1_), channel_id=1, source_target_pairs={{0,4},{4,0},{8,12},{12,8},{16,20},{20,16},{24,28},{28,24},{1,5},{5... | collective-permute-start | bytes 3145736 | tf_op jit(solution)/shard_map/ppermute | solution.py:92
  142.2 43.1 %collective-permute-start.22 = (bf16[256,2048]{1,0:T(8,128)(2,1)}, bf16[256,2048]{1,0:T(8,128)(2,1)}, u32[]{:S(2)}, u32[]{:S(2)}) collective-permute-start(bf16[256,2048]{1,0:T(8,128)(2,1)} %collective-permute-done.21.refs_4_), channel_id=1, source_target_pairs={{0,2},{1,3},{2,0},{3,1},{4,6},{5,7},{6,4},{7,5},{8,10},{9,11},{10,... | collective-permute-start | bytes 3145736 | tf_op jit(solution)/shard_map/ppermute | solution.py:87
  143.7 15.3 %collective-permute-start.16 = (bf16[256,1024]{1,0:T(8,128)(2,1)S(1)}, bf16[256,1024]{1,0:T(8,128)(2,1)S(1)}, u32[]{:S(2)}, u32[]{:S(2)}) collective-permute-start(bf16[256,1024]{1,0:T(8,128)(2,1)S(1)} %copy-done.4), channel_id=1, source_target_pairs={{0,1},{1,0},{2,3},{3,2},{4,5},{5,4},{6,7},{7,6},{8,9},{9,8},{10,11... | collective-permute-start | bytes 1572872 | tf_op jit(solution)/shard_map/ppermute | solution.py:87
  159.0 16.6 %collective-permute-start.24 = (bf16[256,1024]{1,0:T(8,128)(2,1)S(1)}, bf16[256,1024]{1,0:T(8,128)(2,1)S(1)}, u32[]{:S(2)}, u32[]{:S(2)}) collective-permute-start(bf16[256,1024]{1,0:T(8,128)(2,1)S(1)} %get-tuple-element.143.refs_0_.refs_3_), channel_id=1, source_target_pairs={{0,1},{1,0},{2,3},{3,2},{4,5},{5,4},{6,7},{7,6},{8,9},{9,8},{10,11... | collective-permute-start | bytes 1572872 | tf_op jit(solution)/shard_map/ppermute | solution.py:87
  159.1 31.7 %collective-permute-start.25 = (f32[1024]{0:T(1024)S(1)}, f32[1024]{0:T(1024)S(1)}, u32[]{:S(2)}, u32[]{:S(2)}) collective-permute-start(f32[1024]{0:T(1024)S(1)} %copy-done.93), channel_id=1, source_target_pairs={{0,2},{1,3},{2,0},{3,1},{4,6},{5,7},{6,4},{7,5},{8,10},{9,11},{10,... | collective-permute-start | bytes 12296 | tf_op jit(solution)/shard_map/ppermute | solution.py:87
  201.4 10.6 %collective-permute-start.26 = (bf16[256,1024]{1,0:T(8,128)(2,1)}, bf16[256,1024]{1,0:T(8,128)(2,1)S(1)}, u32[]{:S(2)}, u32[]{:S(2)}) collective-permute-start(bf16[256,1024]{1,0:T(8,128)(2,1)} %get-tuple-element.147), channel_id=1, source_target_pairs={{0,1},{1,0},{2,3},{3,2},{4,5},{5,4},{6,7},{7,6},{8,9},{9,8},{10,11... | collective-permute-start | bytes 1572872 | tf_op jit(solution)/shard_map/ppermute | solution.py:87
  211.4 3.5 collective-permute-start.27
  214.4 3.4 collective-permute-start.28
  217.8 12.8 %collective-permute-start.30 = (bf16[256,1024]{1,0:T(8,128)(2,1)S(1)}, bf16[256,1024]{1,0:T(8,128)(2,1)S(1)}, u32[]{:S(2)}, u32[]{:S(2)}) collective-permute-start(bf16[256,1024]{1,0:T(8,128)(2,1)S(1)} %get-tuple-element.160.refs_3_.refs_0_), channel_id=1, source_target_pairs={{0,1},{1,0},{2,3},{3,2},{4,5},{5,4},{6,7},{7,6},{8,9},{9,8},{10,11... | collective-permute-start | bytes 1572872 | tf_op jit(solution)/shard_map/ppermute | solution.py:87
  230.1 23.0 %collective-permute-start.29 = (bf16[256,1024]{1,0:T(8,128)(2,1)}, bf16[256,1024]{1,0:T(8,128)(2,1)S(1)}, u32[]{:S(2)}, u32[]{:S(2)}) collective-permute-start(bf16[256,1024]{1,0:T(8,128)(2,1)} %get-tuple-element.159), channel_id=1, source_target_pairs={{0,1},{1,0},{2,3},{3,2},{4,5},{5,4},{6,7},{7,6},{8,9},{9,8},{10,11... | collective-permute-start | bytes 1572872 | tf_op jit(solution)/shard_map/ppermute | solution.py:87
  252.9 7.0 %collective-permute-start.32 = (bf16[256,1024]{1,0:T(8,128)(2,1)}, bf16[256,1024]{1,0:T(8,128)(2,1)S(1)}, u32[]{:S(2)}, u32[]{:S(2)}) collective-permute-start(bf16[256,1024]{1,0:T(8,128)(2,1)} %get-tuple-element.177), channel_id=1, source_target_pairs={{0,1},{1,0},{2,3},{3,2},{4,5},{5,4},{6,7},{7,6},{8,9},{9,8},{10,11... | collective-permute-start | bytes 1572872 | tf_op jit(solution)/shard_map/ppermute | solution.py:87
  256.3 20.9 %collective-permute-start.31 = (bf16[256,1024]{1,0:T(8,128)(2,1)S(1)}, bf16[256,1024]{1,0:T(8,128)(2,1)}, u32[]{:S(2)}, u32[]{:S(2)}) collective-permute-start(bf16[256,1024]{1,0:T(8,128)(2,1)S(1)} %get-tuple-element.170.refs_9_.refs_4_.refs_1_), channel_id=1, source_target_pairs={{0,2},{1,3},{2,0},{3,1},{4,6},{5,7},{6,4},{7,5},{8,10},{9,11},{10,... | collective-permute-start | bytes 1572872 | tf_op jit(solution)/shard_map/ppermute | solution.py:87
  258.8 49.0 %collective-permute-start.35 = (bf16[2,512,1024]{2,1,0:T(8,128)(2,1)}, bf16[2,512,1024]{2,1,0:T(8,128)(2,1)}, u32[]{:S(2)}, u32[]{:S(2)}) collective-permute-start(bf16[2,512,1024]{2,1,0:T(8,128)(2,1)} %get-tuple-element.167.refs_8_), channel_id=1, source_target_pairs={{0,4},{4,0},{8,12},{12,8},{16,20},{20,16},{24,28},{28,24},{1,5},{5... | collective-permute-start | bytes 6291464 | tf_op jit(solution)/shard_map/ppermute | solution.py:92
  264.9 38.6 %collective-permute-start.34 = (bf16[256,1024]{1,0:T(8,128)(2,1)S(1)}, bf16[256,1024]{1,0:T(8,128)(2,1)}, u32[]{:S(2)}, u32[]{:S(2)}) collective-permute-start(bf16[256,1024]{1,0:T(8,128)(2,1)S(1)} %get-tuple-element.178.refs_10_.refs_3_.refs_4_), channel_id=1, source_target_pairs={{0,2},{1,3},{2,0},{3,1},{4,6},{5,7},{6,4},{7,5},{8,10},{9,11},{10,... | collective-permute-start | bytes 1572872 | tf_op jit(solution)/shard_map/ppermute | solution.py:87
  276.5 65.6 %collective-permute-start.37 = (bf16[2,512,1024]{2,1,0:T(8,128)(2,1)}, bf16[2,512,1024]{2,1,0:T(8,128)(2,1)S(1)}, u32[]{:S(2)}, u32[]{:S(2)}) collective-permute-start(bf16[2,512,1024]{2,1,0:T(8,128)(2,1)} %get-tuple-element.179.refs_8_), channel_id=1, source_target_pairs={{0,8},{4,12},{8,0},{12,4},{16,24},{20,28},{24,16},{28,20},{1,9},{5... | collective-permute-start | bytes 6291464 | tf_op jit(solution)/shard_map/ppermute | solution.py:92
  303.4 43.5 %collective-permute-start.33 = (bf16[512,1024]{1,0:T(8,128)(2,1)}, bf16[512,1024]{1,0:T(8,128)(2,1)}, u32[]{:S(2)}, u32[]{:S(2)}) collective-permute-start(bf16[512,1024]{1,0:T(8,128)(2,1)} %get-tuple-element.182), channel_id=1, source_target_pairs={{0,1},{1,0},{2,3},{3,2},{4,5},{5,4},{6,7},{7,6},{8,9},{9,8},{10,11... | collective-permute-start | bytes 3145736 | tf_op jit(solution)/shard_map/ppermute | solution.py:87
  340.1 6.2 %collective-permute-start.36 = (f32[96,128]{1,0:T(8,128)S(1)}, f32[96,128]{1,0:T(8,128)S(1)}, u32[]{:S(2)}, u32[]{:S(2)}) collective-permute-start(f32[96,128]{1,0:T(8,128)S(1)} %bitcast.108), channel_id=1, source_target_pairs={{0,1},{1,0},{2,3},{3,2},{4,5},{5,4},{6,7},{7,6},{8,9},{9,8},{10,11... | collective-permute-start | bytes 147464 | tf_op jit(solution)/shard_map/ppermute | solution.py:87
  340.7 24.3 %collective-permute-start.39 = (bf16[512,1024]{1,0:T(8,128)(2,1)}, bf16[512,1024]{1,0:T(8,128)(2,1)S(1)}, u32[]{:S(2)}, u32[]{:S(2)}) collective-permute-start(bf16[512,1024]{1,0:T(8,128)(2,1)} %get-tuple-element.208), channel_id=1, source_target_pairs={{0,1},{1,0},{2,3},{3,2},{4,5},{5,4},{6,7},{7,6},{8,9},{9,8},{10,11... | collective-permute-start | bytes 3145736 | tf_op jit(solution)/shard_map/ppermute | solution.py:87
  340.7 31.7 %collective-permute-start.44 = (bf16[2,256,1024]{2,1,0:T(8,128)(2,1)}, bf16[2,256,1024]{2,1,0:T(8,128)(2,1)S(1)}, u32[]{:S(2)}, u32[]{:S(2)}) collective-permute-start(bf16[2,256,1024]{2,1,0:T(8,128)(2,1)} %copy-done.65), channel_id=1, source_target_pairs={{0,8},{4,12},{8,0},{12,4},{16,24},{20,28},{24,16},{28,20},{1,9},{5... | collective-permute-start | bytes 3145736 | tf_op jit(solution)/shard_map/ppermute | solution.py:92
  353.4 22.2 %collective-permute-start.42 = (bf16[2,1024,256]{2,1,0:T(8,128)(2,1)}, bf16[2,1024,256]{2,1,0:T(8,128)(2,1)}, u32[]{:S(2)}, u32[]{:S(2)}) collective-permute-start(bf16[2,1024,256]{2,1,0:T(8,128)(2,1)} %pad_maximum_fusion.2), channel_id=1, source_target_pairs={{0,1},{1,0},{2,3},{3,2},{4,5},{5,4},{6,7},{7,6},{8,9},{9,8},{10,11... | collective-permute-start | bytes 3145736 | tf_op jit(solution)/shard_map/ppermute | solution.py:87
  353.6 37.8 %collective-permute-start.47 = (bf16[2,256,1024]{2,1,0:T(8,128)(2,1)}, bf16[2,256,1024]{2,1,0:T(8,128)(2,1)S(1)}, u32[]{:S(2)}, u32[]{:S(2)}) collective-permute-start(bf16[2,256,1024]{2,1,0:T(8,128)(2,1)} %get-tuple-element.223), channel_id=1, source_target_pairs={{0,4},{4,0},{8,12},{12,8},{16,20},{20,16},{24,28},{28,24},{1,5},{5... | collective-permute-start | bytes 3145736 | tf_op jit(solution)/shard_map/ppermute | solution.py:92
  355.4 7.1 %collective-permute-start.40 = (f32[96,128]{1,0:T(8,128)S(1)}, f32[96,128]{1,0:T(8,128)S(1)}, u32[]{:S(2)}, u32[]{:S(2)}) collective-permute-start(f32[96,128]{1,0:T(8,128)S(1)} %copy-done.55), channel_id=1, source_target_pairs={{0,2},{1,3},{2,0},{3,1},{4,6},{5,7},{6,4},{7,5},{8,10},{9,11},{10,... | collective-permute-start | bytes 147464 | tf_op jit(solution)/shard_map/ppermute | solution.py:87
  362.5 16.1 %collective-permute-start.38 = (bf16[256,1024]{1,0:T(8,128)(2,1)}, bf16[256,1024]{1,0:T(8,128)(2,1)}, u32[]{:S(2)}, u32[]{:S(2)}) collective-permute-start(bf16[256,1024]{1,0:T(8,128)(2,1)} %get-tuple-element.205), channel_id=1, source_target_pairs={{0,2},{1,3},{2,0},{3,1},{4,6},{5,7},{6,4},{7,5},{8,10},{9,11},{10,... | collective-permute-start | bytes 1572872 | tf_op jit(solution)/shard_map/ppermute | solution.py:87
  365.0 10.6 %collective-permute-start.45 = (f32[96,128]{1,0:T(8,128)S(1)}, f32[96,128]{1,0:T(8,128)S(1)}, u32[]{:S(2)}, u32[]{:S(2)}) collective-permute-start(f32[96,128]{1,0:T(8,128)S(1)} %plus.6.refs_5_.refs_0_), channel_id=1, source_target_pairs={{0,16},{4,20},{8,24},{12,28},{16,0},{20,4},{24,8},{28,12},{1,17},{... | collective-permute-start | bytes 147464 | tf_op jit(solution)/shard_map/ppermute | solution.py:92
  372.4 21.9 %collective-permute-start.41 = (bf16[256,1024]{1,0:T(8,128)(2,1)}, bf16[256,1024]{1,0:T(8,128)(2,1)S(1)}, u32[]{:S(2)}, u32[]{:S(2)}) collective-permute-start(bf16[256,1024]{1,0:T(8,128)(2,1)} %get-tuple-element.210), channel_id=1, source_target_pairs={{0,2},{1,3},{2,0},{3,1},{4,6},{5,7},{6,4},{7,5},{8,10},{9,11},{10,... | collective-permute-start | bytes 1572872 | tf_op jit(solution)/shard_map/ppermute | solution.py:87
  388.2 7.8 %collective-permute-start.46 = (bf16[1024,256]{1,0:T(8,128)(2,1)}, bf16[1024,256]{1,0:T(8,128)(2,1)S(1)}, u32[]{:S(2)}, u32[]{:S(2)}) collective-permute-start(bf16[1024,256]{1,0:T(8,128)(2,1)} %get-tuple-element.222), channel_id=1, source_target_pairs={{0,1},{1,0},{2,3},{3,2},{4,5},{5,4},{6,7},{7,6},{8,9},{9,8},{10,11... | collective-permute-start | bytes 1572872 | tf_op jit(solution)/shard_map/ppermute | solution.py:87
  388.3 7.8 %collective-permute-start.48 = (bf16[1024,256]{1,0:T(8,128)(2,1)}, bf16[1024,256]{1,0:T(8,128)(2,1)S(1)}, u32[]{:S(2)}, u32[]{:S(2)}) collective-permute-start(bf16[1024,256]{1,0:T(8,128)(2,1)} %get-tuple-element.227), channel_id=1, source_target_pairs={{0,1},{1,0},{2,3},{3,2},{4,5},{5,4},{6,7},{7,6},{8,9},{9,8},{10,11... | collective-permute-start | bytes 1572872 | tf_op jit(solution)/shard_map/ppermute | solution.py:87
  388.8 13.9 %collective-permute-start.43 = (bf16[2,512,256]{2,1,0:T(8,128)(2,1)S(1)}, bf16[2,512,256]{2,1,0:T(8,128)(2,1)S(1)}, u32[]{:S(2)}, u32[]{:S(2)}) collective-permute-start(bf16[2,512,256]{2,1,0:T(8,128)(2,1)S(1)} %get-tuple-element.214), channel_id=1, source_target_pairs={{0,4},{4,0},{8,12},{12,8},{16,20},{20,16},{24,28},{28,24},{1,5},{5... | collective-permute-start | bytes 1572872 | tf_op jit(solution)/shard_map/ppermute | solution.py:92
  391.6 39.6 %collective-permute-start.57 = (bf16[2,128,1024]{2,1,0:T(8,128)(2,1)S(1)}, bf16[2,128,1024]{2,1,0:T(8,128)(2,1)S(1)}, u32[]{:S(2)}, u32[]{:S(2)}) collective-permute-start(bf16[2,128,1024]{2,1,0:T(8,128)(2,1)S(1)} %get-tuple-element.243), channel_id=1, source_target_pairs={{0,16},{4,20},{8,24},{12,28},{16,0},{20,4},{24,8},{28,12},{1,17},{... | collective-permute-start | bytes 1572872 | tf_op jit(solution)/shard_map/ppermute | solution.py:92
  394.3 49.7 %collective-permute-start.59 = (bf16[2,128,1024]{2,1,0:T(8,128)(2,1)S(1)}, bf16[2,128,1024]{2,1,0:T(8,128)(2,1)S(1)}, u32[]{:S(2)}, u32[]{:S(2)}) collective-permute-start(bf16[2,128,1024]{2,1,0:T(8,128)(2,1)S(1)} %get-tuple-element.244), channel_id=1, source_target_pairs={{0,16},{4,20},{8,24},{12,28},{16,0},{20,4},{24,8},{28,12},{1,17},{... | collective-permute-start | bytes 1572872 | tf_op jit(solution)/shard_map/ppermute | solution.py:92
  402.8 24.0 %collective-permute-start.49 = (bf16[2,256,256]{2,1,0:T(8,128)(2,1)S(1)}, bf16[2,256,256]{2,1,0:T(8,128)(2,1)S(1)}, u32[]{:S(2)}, u32[]{:S(2)}) collective-permute-start(bf16[2,256,256]{2,1,0:T(8,128)(2,1)S(1)} %get-tuple-element.230), channel_id=1, source_target_pairs={{0,8},{4,12},{8,0},{12,4},{16,24},{20,28},{24,16},{28,20},{1,9},{5... | collective-permute-start | bytes 786440 | tf_op jit(solution)/shard_map/ppermute | solution.py:92
  404.4 7.5 %collective-permute-start.50 = (bf16[1,512,256]{2,1,0:T(8,128)(2,1)S(1)}, bf16[1,512,256]{2,1,0:T(8,128)(2,1)S(1)}, u32[]{:S(2)}, u32[]{:S(2)}) collective-permute-start(bf16[1,512,256]{2,1,0:T(8,128)(2,1)S(1)} %get-tuple-element.231), channel_id=1, source_target_pairs={{0,4},{4,0},{8,12},{12,8},{16,20},{20,16},{24,28},{28,24},{1,5},{5... | collective-permute-start | bytes 786440 | tf_op jit(solution)/shard_map/ppermute | solution.py:92
  406.1 20.6 %collective-permute-start.51 = (bf16[1,512,256]{2,1,0:T(8,128)(2,1)S(1)}, bf16[1,512,256]{2,1,0:T(8,128)(2,1)S(1)}, u32[]{:S(2)}, u32[]{:S(2)}) collective-permute-start(bf16[1,512,256]{2,1,0:T(8,128)(2,1)S(1)} %get-tuple-element.233), channel_id=1, source_target_pairs={{0,8},{4,12},{8,0},{12,4},{16,24},{20,28},{24,16},{28,20},{1,9},{5... | collective-permute-start | bytes 786440 | tf_op jit(solution)/shard_map/ppermute | solution.py:92
  411.9 19.8 %collective-permute-start.61 = (f32[96,128]{1,0:T(8,128)S(1)}, f32[96,128]{1,0:T(8,128)S(1)}, u32[]{:S(2)}, u32[]{:S(2)}) collective-permute-start(f32[96,128]{1,0:T(8,128)S(1)} %copy-done.53), channel_id=1, source_target_pairs={{0,8},{4,12},{8,0},{12,4},{16,24},{20,28},{24,16},{28,20},{1,9},{5... | collective-permute-start | bytes 147464 | tf_op jit(solution)/shard_map/ppermute | solution.py:92
  426.9 26.8 %collective-permute-start.52 = (bf16[2,128,256]{2,1,0:T(8,128)(2,1)S(1)}, bf16[2,128,256]{2,1,0:T(8,128)(2,1)S(1)}, u32[]{:S(2)}, u32[]{:S(2)}) collective-permute-start(bf16[2,128,256]{2,1,0:T(8,128)(2,1)S(1)} %get-tuple-element.236), channel_id=1, source_target_pairs={{0,16},{4,20},{8,24},{12,28},{16,0},{20,4},{24,8},{28,12},{1,17},{... | collective-permute-start | bytes 393224 | tf_op jit(solution)/shard_map/ppermute | solution.py:92
  431.2 19.4 %collective-permute-start.53 = (bf16[1,256,256]{2,1,0:T(8,128)(2,1)S(1)}, bf16[1,256,256]{2,1,0:T(8,128)(2,1)S(1)}, u32[]{:S(2)}, u32[]{:S(2)}) collective-permute-start(bf16[1,256,256]{2,1,0:T(8,128)(2,1)S(1)} %get-tuple-element.237), channel_id=1, source_target_pairs={{0,8},{4,12},{8,0},{12,4},{16,24},{20,28},{24,16},{28,20},{1,9},{5... | collective-permute-start | bytes 393224 | tf_op jit(solution)/shard_map/ppermute | solution.py:92
  431.2 19.5 %collective-permute-start.55 = (bf16[1,256,256]{2,1,0:T(8,128)(2,1)S(1)}, bf16[1,256,256]{2,1,0:T(8,128)(2,1)S(1)}, u32[]{:S(2)}, u32[]{:S(2)}) collective-permute-start(bf16[1,256,256]{2,1,0:T(8,128)(2,1)S(1)} %get-tuple-element.240), channel_id=1, source_target_pairs={{0,4},{4,0},{8,12},{12,8},{16,20},{20,16},{24,28},{28,24},{1,5},{5... | collective-permute-start | bytes 393224 | tf_op jit(solution)/shard_map/ppermute | solution.py:92
  431.7 27.3 %collective-permute-start.58 = (bf16[128,1024]{1,0:T(8,128)(2,1)S(1)}, bf16[128,1024]{1,0:T(8,128)(2,1)S(1)}, u32[]{:S(2)}, u32[]{:S(2)}) collective-permute-start(bf16[128,1024]{1,0:T(8,128)(2,1)S(1)} %fusion.5), channel_id=1, source_target_pairs={{0,2},{1,3},{2,0},{3,1},{4,6},{5,7},{6,4},{7,5},{8,10},{9,11},{10,... | collective-permute-start | bytes 786440 | tf_op jit(solution)/shard_map/ppermute | solution.py:87
  444.0 4.1 collective-permute-start.62
  448.1 9.8 %collective-permute-start.60 = (bf16[128,1024]{1,0:T(8,128)(2,1)}, bf16[128,1024]{1,0:T(8,128)(2,1)S(1)}, u32[]{:S(2)}, u32[]{:S(2)}) collective-permute-start(bf16[128,1024]{1,0:T(8,128)(2,1)} %fusion.6), channel_id=1, source_target_pairs={{0,2},{1,3},{2,0},{3,1},{4,6},{5,7},{6,4},{7,5},{8,10},{9,11},{10,... | collective-permute-start | bytes 786440 | tf_op jit(solution)/shard_map/ppermute | solution.py:87
  450.6 5.2 %collective-permute-start.54 = (bf16[1,128,256]{2,1,0:T(8,128)(2,1)S(1)}, bf16[1,128,256]{2,1,0:T(8,128)(2,1)S(1)}, u32[]{:S(2)}, u32[]{:S(2)}) collective-permute-start(bf16[1,128,256]{2,1,0:T(8,128)(2,1)S(1)} %get-tuple-element.239), channel_id=1, source_target_pairs={{0,16},{4,20},{8,24},{12,28},{16,0},{20,4},{24,8},{28,12},{1,17},{... | collective-permute-start | bytes 196616 | tf_op jit(solution)/shard_map/ppermute | solution.py:92
  450.7 6.5 %collective-permute-start.56 = (bf16[1,128,256]{2,1,0:T(8,128)(2,1)S(1)}, bf16[1,128,256]{2,1,0:T(8,128)(2,1)S(1)}, u32[]{:S(2)}, u32[]{:S(2)}) collective-permute-start(bf16[1,128,256]{2,1,0:T(8,128)(2,1)S(1)} %get-tuple-element.242), channel_id=1, source_target_pairs={{0,16},{4,20},{8,24},{12,28},{16,0},{20,4},{24,8},{28,12},{1,17},{... | collective-permute-start | bytes 196616 | tf_op jit(solution)/shard_map/ppermute | solution.py:92
  (103 other events, 503.4 us)

commit v8 on v7

--- a/solution.py
+++ b/solution.py
@@ -103,7 +103,7 @@
     return whole_call(kernel, [out], parts, 0, name, deps=deps)[0]
 
 
-def gather_far(rows, deps=()):
+def gather_far(rows):
     held = (rows, [0])
     steps = []
     step = lax.axis_size("dp") // 2
@@ -114,24 +114,18 @@
     for step in steps[:-1]:
         came = (swap_dp(held[0], step), [o ^ step for o in held[1]])
         first.append(came[0])
-        held = merged([held, came], deps)
+        held = merged([held, came])
     pieces = [held]
     if steps:
         pieces.append((swap_dp(held[0], steps[-1]), [o ^ steps[-1] for o in held[1]]))
     return pieces, first[:1]
 
 
-def merged(pieces, deps=()):
-    def kernel(*refs):
-        at = 0
-        for ref in refs[:-1]:
-            refs[-1][at : at + ref.shape[0], :] = ref[...]
-            at += ref.shape[0]
-
-    parts = [p for p, _ in pieces]
-    out = shape((sum(p.shape[0] for p in parts), parts[0].shape[1]), parts[0].dtype)
-    held = whole_call(kernel, [out], parts, 0, "merge_rows", deps=list(deps))[0]
-    return (held, [o for _, offsets in pieces for o in offsets])
+def merged(pieces):
+    return (
+        jnp.concatenate([p for p, _ in pieces], axis=0),
+        [o for _, offsets in pieces for o in offsets],
+    )
 
 
 def gather_near(pieces):
@@ -798,16 +792,24 @@
     dp_place = lax.axis_index("dp").astype(jnp.int32).reshape(1)
     att_far, att_first = gather_far(pack([w_query, w_key, w_value, w_out.T], "pack_attention"))
     att_pieces = att_far + gather_near(att_far)
-    share = pack([w_up, w_down.T], "pack_feed", [p for p, _ in att_far[1:]] or att_first)
+    share = pack([w_up, w_down.T], "pack_feed", att_first)
     share_other = swap_tensor(share, ACROSS)
-    att_mine = assemble(att_pieces, dp_place, "assemble_attention", [all_across, share_other])
-    mine_far, mine_first = gather_far(share, [att_mine])
+    mine_far, mine_first = gather_far(share)
+    mine_near = gather_near(mine_far)
+    other_far, other_first = gather_far(share_other)
+    other_near = gather_near(other_far[:1]) + [
+        (swap_tensor(p, ACROSS), offsets) for p, offsets in mine_near[1:]
+    ]
 
     def arrays(pieces):
         return [p for p, _ in pieces]
 
+    att_mine = assemble(att_pieces, dp_place, "assemble_attention")
     att_other = assemble(other_core(att_pieces), dp_place, "assemble_attention_other")
-    project_waits = [[], mine_first]
+    ffw_mine = assemble(mine_far + mine_near, dp_place, "assemble_feed")
+    project_waits = [mine_first, [share_other]]
+    attend_waits = [arrays(mine_far[1:]), arrays(mine_near[:1]) + other_first]
+    norm_waits = [arrays(mine_near[1:]), arrays(other_far[1:]) + [ffw_mine]]
 
     biases = jnp.concatenate([b_query, jnp.zeros_like(b_query), b_value])
     qkv_bias_mine, qkv_bias_other = row(biases), row(swap_tensor(biases, CORE))
@@ -832,16 +834,13 @@
     far = [swap_tensor(projected[s][2], CORE) for s in seqs]
     attended = []
     for s in seqs:
+        waits = attend_waits[s] if s < 2 else []
         attended.append(
             attention_forward(
                 projected[s][0], projected[s][1], far[s], masks[s].reshape(1, seq_len),
-                att_mine, att_other, head_size, [p[2] for p in attended[-1:]],
+                att_mine, att_other, head_size, waits + [p[2] for p in attended[-1:]],
             )
         )
-    later = [merged([piece], [attended[0][2]]) for piece in mine_far[1:]]
-    mine_near = gather_near(mine_far[:1] + later)
-    ffw_mine = assemble(mine_far + mine_near, dp_place, "assemble_feed")
-    norm_waits = [arrays(mine_near[:1]) + [attended[-1][2]], [ffw_mine]]
     attended_got = [swap_tensor(attended[s][3], ACROSS) for s in seqs]
     one = []
     for s in seqs:
@@ -852,15 +851,10 @@
                 waits + [p[2] for p in one[-1:]],
             )
         )
-    other_far, _ = gather_far(share_other, [one[0][2]])
-    other_near = gather_near(other_far[:1]) + [
-        (swap_tensor(p, ACROSS), offsets) for p, offsets in mine_near[1:]
-    ]
-    feed_waits = [arrays(other_far[1:]), []]
     normed_far = [swap_tensor(one[s][2], CORE) for s in seqs]
     fed_one = []
     for s in seqs:
-        waits = (feed_waits[s] if s < 2 else []) + [p[2] for p in fed_one[-1:]]
+        waits = [p[2] for p in fed_one[-1:]]
         fed_one.append(
             feed_forward(one[s][2], normed_far[s], ffw_mine, up_bias_mine, None, waits)
         )
@@ -982,6 +976,7 @@
     for bit in bits[:1]:
         small = plus(small, swap_dp(small, bit), [back[-1][2]])
     down_chain.fold([back[-1][2]])
+    up_chain.fold([down_chain.keep])
     both_got = swap_tensor(jnp.stack([query_made[1], out_made[1]]), CORE)
     query_chain = Chain(
         *fold_core([(query_made[0], both_got[0]), (out_made[0], both_got[1])], [back[-1][2]]),
@@ -990,10 +985,9 @@
     key_value_made = weight_grad(
         tokens, [back[s][0] for s in seqs], [back[s][1] for s in seqs],
         dp_place, [(head_dims, near_first), (head_dims, far_first)], "w_key_value_grad",
-        deps=input_got[:1] + [down_chain.keep, query_chain.keep, small],
-    )
-    up_chain.fold([key_value_made[0]])
-    waits = input_got[-1:] + [up_chain.keep]
+        deps=input_got[:1] + [up_chain.keep, query_chain.keep, small],
+    )
+    waits = input_got[-1:] + [down_chain.came]
     key_chain = core_chain([key_value_made[:2]], near_first, waits)
     value_chain = core_chain([key_value_made[2:]], far_first, waits)
     started = [key_chain.keep, value_chain.keep]

time: 466 us -> 443 us (0.951)
  waiting for transfers between devices: 93.4 us -> 84 us
  Pallas kernels: 238 us -> 230 us
    pallas_call x44 -> x40, Pallas kernels: 125 us -> 116 us  [whole_call(): pl.pallas_call(after(kernel, len(args), deps), out_shape=tuple(outs), in_...]
    ppermute x34, waiting for transfers between devices: 20.1 us -> 13.5 us  [swap_tensor(): return lax.ppermute(array, 'tensor', [(i, i ^ bit) for i in range(size)])]
    unnamed x220 -> x203, local copies, waits for them, and re-layouts: 48.9 us -> 45 us
  transfers between devices with their start and end apart: 63 -> 63, of which waited for: 17 -> 14; matrix products, arithmetic and copies ran while one was open for 6% -> 7% of each run, Pallas kernels for 49% -> 50%
where the time goes in v8:
time: 443 us; the launch traced here: 437 us
  Pallas kernels  230 us (52%)
  waiting for transfers between devices  84 us (19%)
  local copies, waits for them, and re-layouts  55.6 us (13%)
  starting transfers between devices  54.1 us (12%)
  other arithmetic  11.4 us (3%)
    pallas_call x40, Pallas kernels, whole_call(): pl.pallas_call(after(kernel, len(args), deps), out_shape=tuple(outs), in_...  116 us
    pallas_call x11, Pallas kernels, streamed_call(): pl.pallas_call(after(kernel, len(args), deps), grid=grid, out_shape=tuple...  98.7 us
    ppermute x29, waiting for transfers between devices, swap_dp(): return lax.ppermute(array, 'dp', [(i, i ^ bit) for i in range(size)])  70.5 us
    unnamed x203, local copies, waits for them, and re-layouts  45 us
    ppermute x29, starting transfers between devices, swap_dp(): return lax.ppermute(array, 'dp', [(i, i ^ bit) for i in range(size)])  35.7 us
    ppermute x34, starting transfers between devices, swap_tensor(): return lax.ppermute(array, 'tensor', [(i, i ^ bit) for i in range(size)])  18.4 us
    pallas_call x4, Pallas kernels, assemble(): pl.pallas_call(after(kernel, 1 + len(arrays), deps), out_shape=out, in_sp...  15.1 us
    ppermute x34, waiting for transfers between devices, swap_tensor(): return lax.ppermute(array, 'tensor', [(i, i ^ bit) for i in range(size)])  13.5 us
  transfers between devices with their start and end apart: 63, of which 14 were waited for; matrix products, arithmetic and copies ran while one was open for 7% of the time, Pallas kernels for 50%

profile of v8, /device:TPU:0, one launch (start us, length us, event | category | flops | bytes accessed | tf_op | source)
XLA Modules:
  0.0 436.9 jit_solution(15262557598432766662)
XLA Ops:
  0.7 1.7 copy.39
  2.3 1.7 pack_attention.1
  4.0 4.0 collective-permute-start.1
  8.0 1.8 copy.40
  9.8 10.3 %collective-permute-done.1.refs_2_ = bf16[128,1024]{1,0:T(8,128)(2,1)S(1)} collective-permute-done((bf16[128,1024]{1,0:T(8,128)(2,1)}, bf16[128,1024]{1,0:T(8,128)(2,1)S(1)}, u32[]{:S(2)}, u32[]{:S(2)}) %collective-permute-start.1) | collective-permute-done | bytes 262176 | tf_op jit(solution)/shard_map/ppermute | solution.py:92
  22.2 1.9 pack_feed.1
  24.0 3.3 collective-permute-start.10
  27.3 1.5 collective-permute-start.3
  28.8 1.5 collective-permute-start
  31.7 11.8 %collective-permute-done.2.refs_2_ = bf16[256,1024]{1,0:T(8,128)(2,1)} collective-permute-done((bf16[256,1024]{1,0:T(8,128)(2,1)S(1)}, bf16[256,1024]{1,0:T(8,128)(2,1)}, u32[]{:S(2)}, u32[]{:S(2)}) %collective-permute-start.2) | collective-permute-done | bytes 524320 | tf_op jit(solution)/shard_map/ppermute | solution.py:92
  44.8 5.8 %collective-permute-done.10.refs_6_ = bf16[128,2048]{1,0:T(8,128)(2,1)S(1)} collective-permute-done((bf16[128,2048]{1,0:T(8,128)(2,1)}, bf16[128,2048]{1,0:T(8,128)(2,1)S(1)}, u32[]{:S(2)}, u32[]{:S(2)}) %collective-permute-start.10) | collective-permute-done | bytes 524320 | tf_op jit(solution)/shard_map/ppermute | solution.py:92
  50.6 1.5 collective-permute-start.4
  52.1 2.1 pad_maximum_fusion.refs_1_
  55.6 8.8 %collective-permute-done.16.refs_6_ = bf16[128,2048]{1,0:T(8,128)(2,1)} collective-permute-done((bf16[128,2048]{1,0:T(8,128)(2,1)}, bf16[128,2048]{1,0:T(8,128)(2,1)}, u32[]{:S(2)}, u32[]{:S(2)}) %collective-permute-start.16) | collective-permute-done | bytes 524320 | tf_op jit(solution)/shard_map/ppermute | solution.py:87
  67.8 3.0 assemble_attention.1.refs_2_.refs_4_.refs_6_.refs_3_
  72.5 3.0 assemble_attention_other.1.refs_3_.refs_5_.refs_7_.refs_4_
  75.5 5.6 %project_inputs.2 = (bf16[512,768]{1,0:T(8,128)(2,1)}, bf16[512,768]{1,0:T(8,128)(2,1)}, bf16[512,1024]{1,0:T(8,128)(2,1)}) custom-call(bf16[256,1024]{1,0:T(8,128)(2,1)} %get-tuple-element.285.refs_0_.refs_1_, bf16[256,1024]{1,0:T(8,128)(2,1)} %get-tuple-element.283.refs_1_.refs_2_, bf16[1024,1024]{1,0:T(8,128)(2,1)} %assemble_attention.1.refs_2_.refs_4_.refs_6_.refs_3_, ...), custom_call_target="tpu_custom_call" | custom-call | flops 1610612 | bytes 7870 | tf_op jit(solution)/shard_map/project_inputs/pallas_call | solution.py:47
  81.8 5.6 %project_inputs.3 = (bf16[512,768]{1,0:T(8,128)(2,1)}, bf16[512,768]{1,0:T(8,128)(2,1)}, bf16[512,1024]{1,0:T(8,128)(2,1)}) custom-call(bf16[256,1024]{1,0:T(8,128)(2,1)} %get-tuple-element.286.refs_0_.refs_3_, bf16[256,1024]{1,0:T(8,128)(2,1)} %get-tuple-element.284.refs_1_.refs_4_, bf16[1024,1024]{1,0:T(8,128)(2,1)} %assemble_attention.1.refs_2_.refs_4_.refs_6_.refs_3_, ...), custom_call_target="tpu_custom_call" | custom-call | flops 1610612 | bytes 7870 | tf_op jit(solution)/shard_map/project_inputs/pallas_call | solution.py:47
  87.4 1.6 collective-permute-done.12.refs_6_.refs_2_
  89.1 1.9 constant_dynamic-update-slice_fusion.1
  91.0 1.8 collective-permute-done.17.refs_7_
  94.3 1.4 select_bitcast_fusion.1
  96.9 12.9 %attention_forward.2 = (bf16[512,256]{1,0:T(8,128)(2,1)}, bf16[512,256]{1,0:T(8,128)(2,1)}, f32[256,1024]{1,0:T(8,128)}, bf16[256,1024]{1,0:T(8,128)(2,1)}) custom-call(bf16[512,768]{1,0:T(8,128)(2,1)} %get-tuple-element.131.refs_0_, bf16[512,768]{1,0:T(8,128)(2,1)} %get-tuple-element.132.refs_1_, bf16[512,1024]{1,0:T(8,128)(2,1)} %collective-permute-done.11.refs_2_, ...), custom_call_target="tpu_custom_call" | custom-call | flops 8589934 | bytes 8916 | tf_op jit(solution)/shard_map/attention_forward/pallas_call | solution.py:47
  109.8 1.5 collective-permute-start.13
  112.3 12.8 %attention_forward.3 = (bf16[512,256]{1,0:T(8,128)(2,1)}, bf16[512,256]{1,0:T(8,128)(2,1)}, f32[256,1024]{1,0:T(8,128)}, bf16[256,1024]{1,0:T(8,128)(2,1)}) custom-call(bf16[512,768]{1,0:T(8,128)(2,1)} %get-tuple-element.138.refs_0_, bf16[512,768]{1,0:T(8,128)(2,1)} %get-tuple-element.139.refs_1_, bf16[512,1024]{1,0:T(8,128)(2,1)} %collective-permute-done.21.refs_2_, ...), custom_call_target="tpu_custom_call" | custom-call | flops 8589934 | bytes 8916 | tf_op jit(solution)/shard_map/attention_forward/pallas_call | solution.py:47
  125.6 1.4 collective-permute-start.19
  127.1 2.6 collective-permute-done.14.refs_6_.refs_4_
  129.7 1.5 collective-permute-start.20
  131.9 4.8 %assemble_feed.1.refs_7_.refs_2_.refs_3_.refs_4_ = bf16[1024,2048]{1,0:T(8,128)(2,1)} custom-call(s32[1]{0:T(128)} %bitcast.2.refs_0_, bf16[256,2048]{1,0:T(8,128)(2,1)} %pad_maximum_fusion.refs_1_, bf16[256,2048]{1,0:T(8,128)(2,1)} %collective-permute-done.12.refs_6_.refs_2_, bf16[256,2048]{1,0:T(8,128)(2,1)} %copy-done.69, bf16[256,2048]{1,0:T(8,128)(2,1)} %copy-done.9), custom_call_target="tpu_custom_call" | custom-call | bytes 8388 | tf_op jit(solution)/shard_map/assemble_feed/pallas_call | solution.py:154
  136.7 3.5 collective-permute-done.23.refs_2_
  140.2 2.2 copy-done
  145.3 8.8 %feed_forward.4 = (bf16[512,1024]{1,0:T(8,128)(2,1)}, bf16[512,1024]{1,0:T(8,128)(2,1)}, f32[512,1024]{1,0:T(8,128)}) custom-call(bf16[256,1024]{1,0:T(8,128)(2,1)} %copy-done.7, bf16[256,1024]{1,0:T(8,128)(2,1)} %copy-done.67, bf16[1024,2048]{1,0:T(8,128)(2,1)} %assemble_feed.1.refs_7_.refs_2_.refs_3_.refs_4_, ...), custom_call_target="tpu_custom_call" | custom-call | flops 2147483 | bytes 13635 | tf_op jit(solution)/shard_map/feed_forward/pallas_call | solution.py:64
  155.0 8.8 %feed_forward.5 = (bf16[512,1024]{1,0:T(8,128)(2,1)}, bf16[512,1024]{1,0:T(8,128)(2,1)}, f32[512,1024]{1,0:T(8,128)}) custom-call(bf16[256,1024]{1,0:T(8,128)(2,1)} %copy-done.8, bf16[256,1024]{1,0:T(8,128)(2,1)} %copy-done.68, bf16[1024,2048]{1,0:T(8,128)(2,1)} %assemble_feed.1.refs_7_.refs_2_.refs_3_.refs_4_, ...), custom_call_target="tpu_custom_call" | custom-call | flops 2147483 | bytes 13635 | tf_op jit(solution)/shard_map/feed_forward/pallas_call | solution.py:64
  163.8 4.5 %assemble_feed_other.1.refs_2_.refs_3_.refs_5_ = bf16[1024,2048]{1,0:T(8,128)(2,1)} custom-call(s32[1]{0:T(128)} %bitcast.2.refs_0_, bf16[256,2048]{1,0:T(8,128)(2,1)} %constant_dynamic-update-slice_fusion.refs_1_, bf16[256,2048]{1,0:T(8,128)(2,1)} %collective-permute-done.18.refs_6_.refs_2_, bf16[256,2048]{1,0:T(8,128)(2,1)} %collective-permute-done.19.refs_3_, ...), custom_call_target="tpu_custom_call" | custom-call | bytes 8388 | tf_op jit(solution)/shard_map/assemble_feed_other/pallas_call | solution.py:154
  168.9 9.8 %feed_forward.6 = (bf16[512,1024]{1,0:T(8,128)(2,1)}, bf16[512,1024]{1,0:T(8,128)(2,1)}, f32[256,1024]{1,0:T(8,128)}, bf16[256,1024]{1,0:T(8,128)(2,1)}) custom-call(bf16[256,1024]{1,0:T(8,128)(2,1)} %copy-done.7, bf16[256,1024]{1,0:T(8,128)(2,1)} %copy-done.67, bf16[1024,2048]{1,0:T(8,128)(2,1)} %assemble_feed_other.1.refs_2_.refs_3_.refs_5_, ...), custom_call_target="tpu_custom_call" | custom-call | flops 2147483 | bytes 15208 | tf_op jit(solution)/shard_map/feed_forward/pallas_call | solution.py:64
  178.9 10.2 %feed_forward.7 = (bf16[512,1024]{1,0:T(8,128)(2,1)}, bf16[512,1024]{1,0:T(8,128)(2,1)}, f32[256,1024]{1,0:T(8,128)}, bf16[256,1024]{1,0:T(8,128)(2,1)}) custom-call(bf16[256,1024]{1,0:T(8,128)(2,1)} %copy-done.8, bf16[256,1024]{1,0:T(8,128)(2,1)} %copy-done.68, bf16[1024,2048]{1,0:T(8,128)(2,1)} %assemble_feed_other.1.refs_2_.refs_3_.refs_5_, ...), custom_call_target="tpu_custom_call" | custom-call | flops 2147483 | bytes 15208 | tf_op jit(solution)/shard_map/feed_forward/pallas_call | solution.py:64
  196.3 11.4 %feed_forward_back.2 = (bf16[512,1024]{1,0:T(8,128)(2,1)}, bf16[512,1024]{1,0:T(8,128)(2,1)}, f32[256,1024]{1,0:T(8,128)}, bf16[256,1024]{1,0:T(8,128)(2,1)}, f32[1,1024]{1,0:T(1,128)}, /*index=5*/f32[1,1024]{1,0:T(1,128)}) custom-call(bf16[256,1024]{1,0:T(8,128)(2,1)} %copy-done.23, bf16[256,1024]{1,0:T(8,128)(2,1)} %copy-done.73, ...), custom_call_target="tpu_custom_call" | custom-call | flops 4294967 | bytes 23601 | tf_op jit(solution)/shard_map/feed_forward_back/pallas_call | solution.py:64
  209.0 9.9 %w_down_grad.1 = (f32[2,512,1024]{2,1,0:T(8,128)}, bf16[2,512,1024]{2,1,0:T(8,128)(2,1)}) custom-call(s32[1]{0:T(128)} %bitcast.2.refs_0_, bf16[256,1024]{1,0:T(8,128)(2,1)} %copy-done.23, bf16[256,1024]{1,0:T(8,128)(2,1)} %copy-done.73, bf16[256,1024]{1,0:T(8,128)(2,1)} %copy-done.24, bf16[256,1024]{1,0:T(8,128)(2,1)} %copy-done.74, ...), custom_call_target="tpu_custom_call" | custom-call | flops 4294967 | bytes 12582 | tf_op jit(solution)/shard_map/w_down_grad/pallas_call | solution.py:64
  218.9 11.5 %feed_forward_back.3 = (bf16[512,1024]{1,0:T(8,128)(2,1)}, bf16[512,1024]{1,0:T(8,128)(2,1)}, f32[256,1024]{1,0:T(8,128)}, bf16[256,1024]{1,0:T(8,128)(2,1)}, f32[1,1024]{1,0:T(1,128)}, /*index=5*/f32[1,1024]{1,0:T(1,128)}) custom-call(bf16[256,1024]{1,0:T(8,128)(2,1)} %copy-done.24, bf16[256,1024]{1,0:T(8,128)(2,1)} %copy-done.74, ...), custom_call_target="tpu_custom_call" | custom-call | flops 4294967 | bytes 23601 | tf_op jit(solution)/shard_map/feed_forward_back/pallas_call | solution.py:64
  233.8 1.5 collective-permute-start.31
  237.4 1.5 collective-permute-start.35
  245.5 9.9 %w_up_grad.1 = (f32[2,512,1024]{2,1,0:T(8,128)}, bf16[2,512,1024]{2,1,0:T(8,128)(2,1)}) custom-call(s32[1]{0:T(128)} %bitcast.2.refs_0_, bf16[256,1024]{1,0:T(8,128)(2,1)} %copy-done.7, bf16[256,1024]{1,0:T(8,128)(2,1)} %copy-done.67, bf16[256,1024]{1,0:T(8,128)(2,1)} %copy-done.8, bf16[256,1024]{1,0:T(8,128)(2,1)} %copy-done.68, ...), custom_call_target="tpu_custom_call" | custom-call | flops 4294967 | bytes 12582 | tf_op jit(solution)/shard_map/w_up_grad/pallas_call | solution.py:64
  255.4 1.6 collective-permute-start.37
  257.1 26.3 %attention_backward.2 = (bf16[512,512]{1,0:T(8,128)(2,1)}, f32[512,1024]{1,0:T(8,128)}, bf16[512,1024]{1,0:T(8,128)(2,1)}, f32[2,512]{1,0:T(2,128)}) custom-call(bf16[512,768]{1,0:T(8,128)(2,1)} %get-tuple-element.131.refs_0_, bf16[512,768]{1,0:T(8,128)(2,1)} %get-tuple-element.132.refs_1_, bf16[512,1024]{1,0:T(8,128)(2,1)} %collective-permute-done.11.refs_2_, ...), custom_call_target="tpu_custom_call" | custom-call | flops 21474836480 | bytes 11542 | tf_op jit(solution)/shard_map/attention_backward/pallas_call | solution.py:47
  283.4 4.3 w_out_grad.1
  287.8 1.9 fold.15
  289.7 1.4 copy-done.21
  292.1 26.1 %attention_backward.3 = (bf16[512,512]{1,0:T(8,128)(2,1)}, f32[512,1024]{1,0:T(8,128)}, bf16[512,1024]{1,0:T(8,128)(2,1)}, f32[2,512]{1,0:T(2,128)}) custom-call(bf16[512,768]{1,0:T(8,128)(2,1)} %get-tuple-element.138.refs_0_, bf16[512,768]{1,0:T(8,128)(2,1)} %get-tuple-element.139.refs_1_, bf16[512,1024]{1,0:T(8,128)(2,1)} %collective-permute-done.21.refs_2_, ...), custom_call_target="tpu_custom_call" | custom-call | flops 21474836480 | bytes 11542 | tf_op jit(solution)/shard_map/attention_backward/pallas_call | solution.py:47
  321.0 2.2 copy-done.15
  325.8 4.4 %w_query_grad.1 = (f32[1024,256]{1,0:T(8,128)}, bf16[1024,256]{1,0:T(8,128)(2,1)}) custom-call(s32[1]{0:T(128)} %bitcast.2.refs_0_, bf16[256,1024]{1,0:T(8,128)(2,1)} %get-tuple-element.285.refs_0_.refs_1_, bf16[256,1024]{1,0:T(8,128)(2,1)} %get-tuple-element.283.refs_1_.refs_2_, bf16[256,1024]{1,0:T(8,128)(2,1)} %get-tuple-element.286.refs_0_.refs_3_, ...), custom_call_target="tpu_custom_call" | custom-call | flops 1073741 | bytes 5767 | tf_op jit(solution)/shard_map/w_query_grad/pallas_call | solution.py:64
  330.2 2.1 pad_maximum_fusion.3
  334.6 6.2 %project_back.2 = (bf16[512,512]{1,0:T(8,128)(2,1)}, bf16[512,512]{1,0:T(8,128)(2,1)}, f32[256,1024]{1,0:T(8,128)}, bf16[256,1024]{1,0:T(8,128)(2,1)}) custom-call(bf16[512,512]{1,0:T(8,128)(2,1)} %get-tuple-element.180.refs_5_.refs_7_.refs_0_, f32[512,1024]{1,0:T(8,128)} %get-tuple-element.181.refs_1_, ...), custom_call_target="tpu_custom_call" | custom-call | flops 1610612 | bytes 10485 | tf_op jit(solution)/shard_map/project_back/pallas_call | solution.py:47
  342.9 2.4 collective-permute-start.46
  345.3 6.4 %project_back.3 = (bf16[512,512]{1,0:T(8,128)(2,1)}, bf16[512,512]{1,0:T(8,128)(2,1)}, f32[256,1024]{1,0:T(8,128)}, bf16[256,1024]{1,0:T(8,128)(2,1)}) custom-call(bf16[512,512]{1,0:T(8,128)(2,1)} %get-tuple-element.191.refs_6_.refs_8_.refs_0_, f32[512,1024]{1,0:T(8,128)} %get-tuple-element.207.refs_1_, bf16[512,1024]{1,0:T(8,128)(2,1)} %copy-done.75, ...), custom_call_target="tpu_custom_call" | custom-call | flops 1610612 | bytes 10485 | tf_op jit(solution)/shard_map/project_back/pallas_call | solution.py:47
  361.2 9.6 %w_key_value_grad.1 = (f32[1024,256]{1,0:T(8,128)}, bf16[1024,256]{1,0:T(8,128)(2,1)}, f32[1024,256]{1,0:T(8,128)}, bf16[1024,256]{1,0:T(8,128)(2,1)}) custom-call(s32[1]{0:T(128)} %bitcast.2.refs_0_, bf16[256,1024]{1,0:T(8,128)(2,1)} %get-tuple-element.285.refs_0_.refs_1_, bf16[256,1024]{1,0:T(8,128)(2,1)} %get-tuple-element.283.refs_1_.refs_2_, ...), custom_call_target="tpu_custom_call" | custom-call | flops 2147483 | bytes 7340 | tf_op jit(solution)/shard_map/w_key_value_grad/pallas_call | solution.py:64
  371.4 1.5 collective-permute-start.43
  374.0 2.0 collective-permute-start.58
  377.4 15.6 %collective-permute-done.48.refs_3_.refs_1_ = bf16[2,128,1024]{2,1,0:T(8,128)(2,1)S(1)} collective-permute-done((bf16[2,128,1024]{2,1,0:T(8,128)(2,1)S(1)}, bf16[2,128,1024]{2,1,0:T(8,128)(2,1)S(1)}, u32[]{:S(2)}, u32[]{:S(2)}) %collective-permute-start.48) | collective-permute-done | bytes 524320 | tf_op jit(solution)/shard_map/ppermute | solution.py:92
  394.3 2.1 collective-permute-start.50
  398.8 5.0 %collective-permute-done.51.refs_1_ = bf16[1,512,256]{2,1,0:T(8,128)(2,1)S(1)} collective-permute-done((bf16[1,512,256]{2,1,0:T(8,128)(2,1)S(1)}, bf16[1,512,256]{2,1,0:T(8,128)(2,1)S(1)}, u32[]{:S(2)}, u32[]{:S(2)}) %collective-permute-start.51) | collective-permute-done | bytes 262176 | tf_op jit(solution)/shard_map/ppermute | solution.py:92
  403.9 12.4 %collective-permute-done.52.refs_1_ = bf16[1,512,256]{2,1,0:T(8,128)(2,1)S(1)} collective-permute-done((bf16[1,512,256]{2,1,0:T(8,128)(2,1)S(1)}, bf16[1,512,256]{2,1,0:T(8,128)(2,1)S(1)}, u32[]{:S(2)}, u32[]{:S(2)}) %collective-permute-start.52) | collective-permute-done | bytes 262176 | tf_op jit(solution)/shard_map/ppermute | solution.py:92
  416.5 2.3 collective-permute-start.54
  422.7 2.3 collective-permute-done.62.refs_1_
  428.3 2.4 collective-permute-start.57
  (363 shorter events, 82.0 us)
Async XLA Ops:
  4.0 16.2 %collective-permute-start.1 = (bf16[128,1024]{1,0:T(8,128)(2,1)}, bf16[128,1024]{1,0:T(8,128)(2,1)S(1)}, u32[]{:S(2)}, u32[]{:S(2)}) collective-permute-start(bf16[128,1024]{1,0:T(8,128)(2,1)} %pack_attention.1), channel_id=1, source_target_pairs={{0,16},{4,20},{8,24},{12,28},{16,0},{20,4},{24,8},{28,12},{1,17},{... | collective-permute-start | bytes 786440 | tf_op jit(solution)/shard_map/ppermute | solution.py:92
  21.3 44.7 %copy-start.71 = (bf16[256,1024]{1,0:T(8,128)(2,1)}, bf16[256,1024]{1,0:T(8,128)(2,1)S(1)}, u32[]{:S(2)}) copy-start(bf16[256,1024]{1,0:T(8,128)(2,1)S(1)} %pad_maximum_fusion.4.refs_1_) | copy-start | bytes 1572868
  21.3 22.2 %collective-permute-start.2 = (bf16[256,1024]{1,0:T(8,128)(2,1)S(1)}, bf16[256,1024]{1,0:T(8,128)(2,1)}, u32[]{:S(2)}, u32[]{:S(2)}) collective-permute-start(bf16[256,1024]{1,0:T(8,128)(2,1)S(1)} %pad_maximum_fusion.4.refs_1_), channel_id=1, source_target_pairs={{0,8},{4,12},{8,0},{12,4},{16,24},{20,28},{24,16},{28,20},{1,9},{5... | collective-permute-start | bytes 1572872 | tf_op jit(solution)/shard_map/ppermute | solution.py:92
  24.0 26.6 %collective-permute-start.10 = (bf16[128,2048]{1,0:T(8,128)(2,1)}, bf16[128,2048]{1,0:T(8,128)(2,1)S(1)}, u32[]{:S(2)}, u32[]{:S(2)}) collective-permute-start(bf16[128,2048]{1,0:T(8,128)(2,1)} %pack_feed.1), channel_id=1, source_target_pairs={{0,16},{4,20},{8,24},{12,28},{16,0},{20,4},{24,8},{28,12},{1,17},{... | collective-permute-start | bytes 1572872 | tf_op jit(solution)/shard_map/ppermute | solution.py:92
  27.3 26.9 %collective-permute-start.3 = (bf16[256,1024]{1,0:T(8,128)(2,1)S(1)}, bf16[256,1024]{1,0:T(8,128)(2,1)S(1)}, u32[]{:S(2)}, u32[]{:S(2)}) collective-permute-start(bf16[256,1024]{1,0:T(8,128)(2,1)S(1)} %pad_maximum_fusion.4.refs_1_), channel_id=1, source_target_pairs={{0,4},{4,0},{8,12},{12,8},{16,20},{20,16},{24,28},{28,24},{1,5},{5... | collective-permute-start | bytes 1572872 | tf_op jit(solution)/shard_map/ppermute | solution.py:92
  28.8 37.7 %collective-permute-start = (bf16[2,256,1024]{2,1,0:T(8,128)(2,1)S(1)}, bf16[2,256,1024]{2,1,0:T(8,128)(2,1)S(1)}, u32[]{:S(2)}, u32[]{:S(2)}) collective-permute-start(bf16[2,256,1024]{2,1,0:T(8,128)(2,1)S(1)} %copy-done.76), channel_id=1, source_target_pairs={{0,2},{1,3},{2,0},{3,1},{4,6},{5,7},{6,4},{7,5},{8,10},{9,11},{10,... | collective-permute-start | bytes 3145736 | tf_op jit(solution)/shard_map/ppermute | solution.py:87
  30.3 1.2 collective-permute-start.9
  31.6 24.0 %collective-permute-start.5 = (bf16[256,1024]{1,0:T(8,128)(2,1)S(1)}, bf16[256,1024]{1,0:T(8,128)(2,1)}, u32[]{:S(2)}, u32[]{:S(2)}) collective-permute-start(bf16[256,1024]{1,0:T(8,128)(2,1)S(1)} %pad_maximum_fusion.4.refs_1_), channel_id=1, source_target_pairs={{0,1},{1,0},{2,3},{3,2},{4,5},{5,4},{6,7},{7,6},{8,9},{9,8},{10,11... | collective-permute-start | bytes 1572872 | tf_op jit(solution)/shard_map/ppermute | solution.py:87
  43.5 20.9 %collective-permute-start.16 = (bf16[128,2048]{1,0:T(8,128)(2,1)}, bf16[128,2048]{1,0:T(8,128)(2,1)}, u32[]{:S(2)}, u32[]{:S(2)}) collective-permute-start(bf16[128,2048]{1,0:T(8,128)(2,1)} %pack_feed.1), channel_id=1, source_target_pairs={{0,2},{1,3},{2,0},{3,1},{4,6},{5,7},{6,4},{7,5},{8,10},{9,11},{10,... | collective-permute-start | bytes 1572872 | tf_op jit(solution)/shard_map/ppermute | solution.py:87
  50.6 13.8 %collective-permute-start.4 = (bf16[256,1024]{1,0:T(8,128)(2,1)}, bf16[256,1024]{1,0:T(8,128)(2,1)}, u32[]{:S(2)}, u32[]{:S(2)}) collective-permute-start(bf16[256,1024]{1,0:T(8,128)(2,1)} %collective-permute-done.2.refs_2_), channel_id=1, source_target_pairs={{0,4},{4,0},{8,12},{12,8},{16,20},{20,16},{24,28},{28,24},{1,5},{5... | collective-permute-start | bytes 1572872 | tf_op jit(solution)/shard_map/ppermute | solution.py:92
  55.0 34.0 %collective-permute-start.12 = (bf16[256,2048]{1,0:T(8,128)(2,1)}, bf16[256,2048]{1,0:T(8,128)(2,1)}, u32[]{:S(2)}, u32[]{:S(2)}) collective-permute-start(bf16[256,2048]{1,0:T(8,128)(2,1)} %pad_maximum_fusion.refs_1_), channel_id=1, source_target_pairs={{0,8},{4,12},{8,0},{12,4},{16,24},{20,28},{24,16},{28,20},{1,9},{5... | collective-permute-start | bytes 3145736 | tf_op jit(solution)/shard_map/ppermute | solution.py:92
  55.6 15.1 %collective-permute-start.6 = (bf16[256,1024]{1,0:T(8,128)(2,1)}, bf16[256,1024]{1,0:T(8,128)(2,1)S(1)}, u32[]{:S(2)}, u32[]{:S(2)}) collective-permute-start(bf16[256,1024]{1,0:T(8,128)(2,1)} %collective-permute-done.2.refs_2_), channel_id=1, source_target_pairs={{0,1},{1,0},{2,3},{3,2},{4,5},{5,4},{6,7},{7,6},{8,9},{9,8},{10,11... | collective-permute-start | bytes 1572872 | tf_op jit(solution)/shard_map/ppermute | solution.py:87
  64.4 6.4 %collective-permute-start.7 = (bf16[256,1024]{1,0:T(8,128)(2,1)}, bf16[256,1024]{1,0:T(8,128)(2,1)S(1)}, u32[]{:S(2)}, u32[]{:S(2)}) collective-permute-start(bf16[256,1024]{1,0:T(8,128)(2,1)} %copy-done.79), channel_id=1, source_target_pairs={{0,1},{1,0},{2,3},{3,2},{4,5},{5,4},{6,7},{7,6},{8,9},{9,8},{10,11... | collective-permute-start | bytes 1572872 | tf_op jit(solution)/shard_map/ppermute | solution.py:87
  64.4 6.4 %collective-permute-start.8 = (bf16[256,1024]{1,0:T(8,128)(2,1)}, bf16[256,1024]{1,0:T(8,128)(2,1)S(1)}, u32[]{:S(2)}, u32[]{:S(2)}) collective-permute-start(bf16[256,1024]{1,0:T(8,128)(2,1)} %collective-permute-done.4.refs_4_), channel_id=1, source_target_pairs={{0,1},{1,0},{2,3},{3,2},{4,5},{5,4},{6,7},{7,6},{8,9},{9,8},{10,11... | collective-permute-start | bytes 1572872 | tf_op jit(solution)/shard_map/ppermute | solution.py:87
  66.5 26.2 %collective-permute-start.17 = (bf16[128,2048]{1,0:T(8,128)(2,1)}, bf16[128,2048]{1,0:T(8,128)(2,1)S(1)}, u32[]{:S(2)}, u32[]{:S(2)}) collective-permute-start(bf16[128,2048]{1,0:T(8,128)(2,1)} %collective-permute-done.16.refs_6_), channel_id=1, source_target_pairs={{0,16},{4,20},{8,24},{12,28},{16,0},{20,4},{24,8},{28,12},{1,17},{... | collective-permute-start | bytes 1572872 | tf_op jit(solution)/shard_map/ppermute | solution.py:92
  81.1 15.8 %collective-permute-start.11 = (bf16[512,1024]{1,0:T(8,128)(2,1)}, bf16[512,1024]{1,0:T(8,128)(2,1)}, u32[]{:S(2)}, u32[]{:S(2)}) collective-permute-start(bf16[512,1024]{1,0:T(8,128)(2,1)} %get-tuple-element.133.refs_7_), channel_id=1, source_target_pairs={{0,1},{1,0},{2,3},{3,2},{4,5},{5,4},{6,7},{7,6},{8,9},{9,8},{10,11... | collective-permute-start | bytes 3145736 | tf_op jit(solution)/shard_map/ppermute | solution.py:87
  81.1 30.3 %collective-permute-start.22 = (bf16[256,2048]{1,0:T(8,128)(2,1)}, bf16[256,2048]{1,0:T(8,128)(2,1)S(1)}, u32[]{:S(2)}, u32[]{:S(2)}) collective-permute-start(bf16[256,2048]{1,0:T(8,128)(2,1)} %pad_maximum_fusion.refs_1_), channel_id=1, source_target_pairs={{0,4},{4,0},{8,12},{12,8},{16,20},{20,16},{24,28},{28,24},{1,5},{5... | collective-permute-start | bytes 3145736 | tf_op jit(solution)/shard_map/ppermute | solution.py:92
  87.4 23.9 %collective-permute-start.21 = (bf16[512,1024]{1,0:T(8,128)(2,1)}, bf16[512,1024]{1,0:T(8,128)(2,1)}, u32[]{:S(2)}, u32[]{:S(2)}) collective-permute-start(bf16[512,1024]{1,0:T(8,128)(2,1)} %get-tuple-element.140), channel_id=1, source_target_pairs={{0,1},{1,0},{2,3},{3,2},{4,5},{5,4},{6,7},{7,6},{8,9},{9,8},{10,11... | collective-permute-start | bytes 3145736 | tf_op jit(solution)/shard_map/ppermute | solution.py:87
  89.1 40.7 %collective-permute-start.14 = (bf16[256,2048]{1,0:T(8,128)(2,1)}, bf16[256,2048]{1,0:T(8,128)(2,1)S(1)}, u32[]{:S(2)}, u32[]{:S(2)}) collective-permute-start(bf16[256,2048]{1,0:T(8,128)(2,1)} %collective-permute-done.12.refs_6_.refs_2_), channel_id=1, source_target_pairs={{0,4},{4,0},{8,12},{12,8},{16,20},{20,16},{24,28},{28,24},{1,5},{5... | collective-permute-start | bytes 3145736 | tf_op jit(solution)/shard_map/ppermute | solution.py:92
  93.7 43.0 %collective-permute-start.18 = (bf16[256,2048]{1,0:T(8,128)(2,1)}, bf16[256,2048]{1,0:T(8,128)(2,1)}, u32[]{:S(2)}, u32[]{:S(2)}) collective-permute-start(bf16[256,2048]{1,0:T(8,128)(2,1)} %constant_dynamic-update-slice_fusion.refs_1_), channel_id=1, source_target_pairs={{0,8},{4,12},{8,0},{12,4},{16,24},{20,28},{24,16},{28,20},{1,9},{5... | collective-permute-start | bytes 3145736 | tf_op jit(solution)/shard_map/ppermute | solution.py:92
  109.8 21.4 %collective-permute-start.13 = (bf16[256,1024]{1,0:T(8,128)(2,1)}, bf16[256,1024]{1,0:T(8,128)(2,1)S(1)}, u32[]{:S(2)}, u32[]{:S(2)}) collective-permute-start(bf16[256,1024]{1,0:T(8,128)(2,1)} %get-tuple-element.135), channel_id=1, source_target_pairs={{0,2},{1,3},{2,0},{3,1},{4,6},{5,7},{6,4},{7,5},{8,10},{9,11},{10,... | collective-permute-start | bytes 1572872 | tf_op jit(solution)/shard_map/ppermute | solution.py:87
  125.1 15.1 %collective-permute-start.23 = (bf16[256,1024]{1,0:T(8,128)(2,1)}, bf16[256,1024]{1,0:T(8,128)(2,1)S(1)}, u32[]{:S(2)}, u32[]{:S(2)}) collective-permute-start(bf16[256,1024]{1,0:T(8,128)(2,1)} %get-tuple-element.142), channel_id=1, source_target_pairs={{0,2},{1,3},{2,0},{3,1},{4,6},{5,7},{6,4},{7,5},{8,10},{9,11},{10,... | collective-permute-start | bytes 1572872 | tf_op jit(solution)/shard_map/ppermute | solution.py:87
  125.6 38.2 %collective-permute-start.19 = (bf16[256,2048]{1,0:T(8,128)(2,1)}, bf16[256,2048]{1,0:T(8,128)(2,1)}, u32[]{:S(2)}, u32[]{:S(2)}) collective-permute-start(bf16[256,2048]{1,0:T(8,128)(2,1)} %constant_dynamic-update-slice_fusion.refs_1_), channel_id=1, source_target_pairs={{0,4},{4,0},{8,12},{12,8},{16,20},{20,16},{24,28},{28,24},{1,5},{5... | collective-permute-start | bytes 3145736 | tf_op jit(solution)/shard_map/ppermute | solution.py:92
  129.7 34.1 %collective-permute-start.20 = (bf16[256,2048]{1,0:T(8,128)(2,1)S(1)}, bf16[256,2048]{1,0:T(8,128)(2,1)}, u32[]{:S(2)}, u32[]{:S(2)}) collective-permute-start(bf16[256,2048]{1,0:T(8,128)(2,1)S(1)} %collective-permute-done.14.refs_6_.refs_4_), channel_id=1, source_target_pairs={{0,2},{1,3},{2,0},{3,1},{4,6},{5,7},{6,4},{7,5},{8,10},{9,11},{10,... | collective-permute-start | bytes 3145736 | tf_op jit(solution)/shard_map/ppermute | solution.py:87
  131.8 12.6 %collective-permute-start.15 = (bf16[256,1024]{1,0:T(8,128)(2,1)S(1)}, bf16[256,1024]{1,0:T(8,128)(2,1)S(1)}, u32[]{:S(2)}, u32[]{:S(2)}) collective-permute-start(bf16[256,1024]{1,0:T(8,128)(2,1)S(1)} %get-tuple-element.137.refs_8_.refs_0_.refs_1_), channel_id=1, source_target_pairs={{0,1},{1,0},{2,3},{3,2},{4,5},{5,4},{6,7},{7,6},{8,9},{9,8},{10,11... | collective-permute-start | bytes 1572872 | tf_op jit(solution)/shard_map/ppermute | solution.py:87
  143.9 10.3 %collective-permute-start.24 = (bf16[256,1024]{1,0:T(8,128)(2,1)S(1)}, bf16[256,1024]{1,0:T(8,128)(2,1)S(1)}, u32[]{:S(2)}, u32[]{:S(2)}) collective-permute-start(bf16[256,1024]{1,0:T(8,128)(2,1)S(1)} %get-tuple-element.143.refs_0_.refs_3_), channel_id=1, source_target_pairs={{0,1},{1,0},{2,3},{3,2},{4,5},{5,4},{6,7},{7,6},{8,9},{9,8},{10,11... | collective-permute-start | bytes 1572872 | tf_op jit(solution)/shard_map/ppermute | solution.py:87
  143.9 24.4 %collective-permute-start.25 = (f32[1024]{0:T(1024)S(1)}, f32[1024]{0:T(1024)S(1)}, u32[]{:S(2)}, u32[]{:S(2)}) collective-permute-start(f32[1024]{0:T(1024)S(1)} %copy-done.86), channel_id=1, source_target_pairs={{0,2},{1,3},{2,0},{3,1},{4,6},{5,7},{6,4},{7,5},{8,10},{9,11},{10,... | collective-permute-start | bytes 12296 | tf_op jit(solution)/shard_map/ppermute | solution.py:87
  178.7 10.9 %collective-permute-start.26 = (bf16[256,1024]{1,0:T(8,128)(2,1)}, bf16[256,1024]{1,0:T(8,128)(2,1)S(1)}, u32[]{:S(2)}, u32[]{:S(2)}) collective-permute-start(bf16[256,1024]{1,0:T(8,128)(2,1)} %get-tuple-element.147), channel_id=1, source_target_pairs={{0,1},{1,0},{2,3},{3,2},{4,5},{5,4},{6,7},{7,6},{8,9},{9,8},{10,11... | collective-permute-start | bytes 1572872 | tf_op jit(solution)/shard_map/ppermute | solution.py:87
  189.1 3.4 collective-permute-start.27
  192.2 3.3 collective-permute-start.28
  195.3 12.8 %collective-permute-start.30 = (bf16[256,1024]{1,0:T(8,128)(2,1)S(1)}, bf16[256,1024]{1,0:T(8,128)(2,1)S(1)}, u32[]{:S(2)}, u32[]{:S(2)}) collective-permute-start(bf16[256,1024]{1,0:T(8,128)(2,1)S(1)} %get-tuple-element.160.refs_3_.refs_0_), channel_id=1, source_target_pairs={{0,1},{1,0},{2,3},{3,2},{4,5},{5,4},{6,7},{7,6},{8,9},{9,8},{10,11... | collective-permute-start | bytes 1572872 | tf_op jit(solution)/shard_map/ppermute | solution.py:87
  207.8 22.9 %collective-permute-start.29 = (bf16[256,1024]{1,0:T(8,128)(2,1)}, bf16[256,1024]{1,0:T(8,128)(2,1)S(1)}, u32[]{:S(2)}, u32[]{:S(2)}) collective-permute-start(bf16[256,1024]{1,0:T(8,128)(2,1)} %get-tuple-element.159), channel_id=1, source_target_pairs={{0,1},{1,0},{2,3},{3,2},{4,5},{5,4},{6,7},{7,6},{8,9},{9,8},{10,11... | collective-permute-start | bytes 1572872 | tf_op jit(solution)/shard_map/ppermute | solution.py:87
  230.4 9.3 %collective-permute-start.32 = (bf16[256,1024]{1,0:T(8,128)(2,1)}, bf16[256,1024]{1,0:T(8,128)(2,1)S(1)}, u32[]{:S(2)}, u32[]{:S(2)}) collective-permute-start(bf16[256,1024]{1,0:T(8,128)(2,1)} %get-tuple-element.177), channel_id=1, source_target_pairs={{0,1},{1,0},{2,3},{3,2},{4,5},{5,4},{6,7},{7,6},{8,9},{9,8},{10,11... | collective-permute-start | bytes 1572872 | tf_op jit(solution)/shard_map/ppermute | solution.py:87
  233.8 23.3 %collective-permute-start.31 = (bf16[256,1024]{1,0:T(8,128)(2,1)S(1)}, bf16[256,1024]{1,0:T(8,128)(2,1)}, u32[]{:S(2)}, u32[]{:S(2)}) collective-permute-start(bf16[256,1024]{1,0:T(8,128)(2,1)S(1)} %get-tuple-element.170.refs_9_.refs_4_.refs_1_), channel_id=1, source_target_pairs={{0,2},{1,3},{2,0},{3,1},{4,6},{5,7},{6,4},{7,5},{8,10},{9,11},{10,... | collective-permute-start | bytes 1572872 | tf_op jit(solution)/shard_map/ppermute | solution.py:87
  237.4 50.3 %collective-permute-start.35 = (bf16[2,512,1024]{2,1,0:T(8,128)(2,1)}, bf16[2,512,1024]{2,1,0:T(8,128)(2,1)}, u32[]{:S(2)}, u32[]{:S(2)}) collective-permute-start(bf16[2,512,1024]{2,1,0:T(8,128)(2,1)} %get-tuple-element.167.refs_8_), channel_id=1, source_target_pairs={{0,4},{4,0},{8,12},{12,8},{16,20},{20,16},{24,28},{28,24},{1,5},{5... | collective-permute-start | bytes 6291464 | tf_op jit(solution)/shard_map/ppermute | solution.py:92
  244.7 38.7 %collective-permute-start.34 = (bf16[256,1024]{1,0:T(8,128)(2,1)S(1)}, bf16[256,1024]{1,0:T(8,128)(2,1)}, u32[]{:S(2)}, u32[]{:S(2)}) collective-permute-start(bf16[256,1024]{1,0:T(8,128)(2,1)S(1)} %get-tuple-element.178.refs_10_.refs_3_.refs_4_), channel_id=1, source_target_pairs={{0,2},{1,3},{2,0},{3,1},{4,6},{5,7},{6,4},{7,5},{8,10},{9,11},{10,... | collective-permute-start | bytes 1572872 | tf_op jit(solution)/shard_map/ppermute | solution.py:87
  255.4 65.6 %collective-permute-start.37 = (bf16[2,512,1024]{2,1,0:T(8,128)(2,1)}, bf16[2,512,1024]{2,1,0:T(8,128)(2,1)S(1)}, u32[]{:S(2)}, u32[]{:S(2)}) collective-permute-start(bf16[2,512,1024]{2,1,0:T(8,128)(2,1)} %get-tuple-element.179.refs_8_), channel_id=1, source_target_pairs={{0,8},{4,12},{8,0},{12,4},{16,24},{20,28},{24,16},{28,20},{1,9},{5... | collective-permute-start | bytes 6291464 | tf_op jit(solution)/shard_map/ppermute | solution.py:92
  283.4 42.4 %collective-permute-start.33 = (bf16[512,1024]{1,0:T(8,128)(2,1)}, bf16[512,1024]{1,0:T(8,128)(2,1)}, u32[]{:S(2)}, u32[]{:S(2)}) collective-permute-start(bf16[512,1024]{1,0:T(8,128)(2,1)} %get-tuple-element.182), channel_id=1, source_target_pairs={{0,1},{1,0},{2,3},{3,2},{4,5},{5,4},{6,7},{7,6},{8,9},{9,8},{10,11... | collective-permute-start | bytes 3145736 | tf_op jit(solution)/shard_map/ppermute | solution.py:87
  320.0 5.2 %collective-permute-start.36 = (f32[96,128]{1,0:T(8,128)S(1)}, f32[96,128]{1,0:T(8,128)S(1)}, u32[]{:S(2)}, u32[]{:S(2)}) collective-permute-start(f32[96,128]{1,0:T(8,128)S(1)} %bitcast.108), channel_id=1, source_target_pairs={{0,1},{1,0},{2,3},{3,2},{4,5},{5,4},{6,7},{7,6},{8,9},{9,8},{10,11... | collective-permute-start | bytes 147464 | tf_op jit(solution)/shard_map/ppermute | solution.py:87
  320.5 22.3 %collective-permute-start.39 = (bf16[512,1024]{1,0:T(8,128)(2,1)}, bf16[512,1024]{1,0:T(8,128)(2,1)S(1)}, u32[]{:S(2)}, u32[]{:S(2)}) collective-permute-start(bf16[512,1024]{1,0:T(8,128)(2,1)} %get-tuple-element.208), channel_id=1, source_target_pairs={{0,1},{1,0},{2,3},{3,2},{4,5},{5,4},{6,7},{7,6},{8,9},{9,8},{10,11... | collective-permute-start | bytes 3145736 | tf_op jit(solution)/shard_map/ppermute | solution.py:87
  320.6 31.1 %collective-permute-start.45 = (bf16[2,256,1024]{2,1,0:T(8,128)(2,1)}, bf16[2,256,1024]{2,1,0:T(8,128)(2,1)S(1)}, u32[]{:S(2)}, u32[]{:S(2)}) collective-permute-start(bf16[2,256,1024]{2,1,0:T(8,128)(2,1)} %copy-done.66), channel_id=1, source_target_pairs={{0,8},{4,12},{8,0},{12,4},{16,24},{20,28},{24,16},{28,20},{1,9},{5... | collective-permute-start | bytes 3145736 | tf_op jit(solution)/shard_map/ppermute | solution.py:92
  332.3 25.3 %collective-permute-start.42 = (bf16[2,1024,256]{2,1,0:T(8,128)(2,1)}, bf16[2,1024,256]{2,1,0:T(8,128)(2,1)}, u32[]{:S(2)}, u32[]{:S(2)}) collective-permute-start(bf16[2,1024,256]{2,1,0:T(8,128)(2,1)} %pad_maximum_fusion.3), channel_id=1, source_target_pairs={{0,1},{1,0},{2,3},{3,2},{4,5},{5,4},{6,7},{7,6},{8,9},{9,8},{10,11... | collective-permute-start | bytes 3145736 | tf_op jit(solution)/shard_map/ppermute | solution.py:87
  332.5 27.6 %collective-permute-start.44 = (bf16[2,256,1024]{2,1,0:T(8,128)(2,1)}, bf16[2,256,1024]{2,1,0:T(8,128)(2,1)S(1)}, u32[]{:S(2)}, u32[]{:S(2)}) collective-permute-start(bf16[2,256,1024]{2,1,0:T(8,128)(2,1)} %get-tuple-element.219), channel_id=1, source_target_pairs={{0,4},{4,0},{8,12},{12,8},{16,20},{20,16},{24,28},{28,24},{1,5},{5... | collective-permute-start | bytes 3145736 | tf_op jit(solution)/shard_map/ppermute | solution.py:92
  333.3 7.5 %collective-permute-start.40 = (f32[96,128]{1,0:T(8,128)S(1)}, f32[96,128]{1,0:T(8,128)S(1)}, u32[]{:S(2)}, u32[]{:S(2)}) collective-permute-start(f32[96,128]{1,0:T(8,128)S(1)} %copy-done.56), channel_id=1, source_target_pairs={{0,2},{1,3},{2,0},{3,1},{4,6},{5,7},{6,4},{7,5},{8,10},{9,11},{10,... | collective-permute-start | bytes 147464 | tf_op jit(solution)/shard_map/ppermute | solution.py:87
  340.9 20.4 %collective-permute-start.38 = (bf16[256,1024]{1,0:T(8,128)(2,1)}, bf16[256,1024]{1,0:T(8,128)(2,1)}, u32[]{:S(2)}, u32[]{:S(2)}) collective-permute-start(bf16[256,1024]{1,0:T(8,128)(2,1)} %get-tuple-element.205), channel_id=1, source_target_pairs={{0,2},{1,3},{2,0},{3,1},{4,6},{5,7},{6,4},{7,5},{8,10},{9,11},{10,... | collective-permute-start | bytes 1572872 | tf_op jit(solution)/shard_map/ppermute | solution.py:87
  342.9 13.7 %collective-permute-start.46 = (f32[96,128]{1,0:T(8,128)S(1)}, f32[96,128]{1,0:T(8,128)S(1)}, u32[]{:S(2)}, u32[]{:S(2)}) collective-permute-start(f32[96,128]{1,0:T(8,128)S(1)} %plus.6.refs_5_.refs_0_), channel_id=1, source_target_pairs={{0,16},{4,20},{8,24},{12,28},{16,0},{20,4},{24,8},{28,12},{1,17},{... | collective-permute-start | bytes 147464 | tf_op jit(solution)/shard_map/ppermute | solution.py:92
  352.6 21.3 %collective-permute-start.41 = (bf16[256,1024]{1,0:T(8,128)(2,1)}, bf16[256,1024]{1,0:T(8,128)(2,1)S(1)}, u32[]{:S(2)}, u32[]{:S(2)}) collective-permute-start(bf16[256,1024]{1,0:T(8,128)(2,1)} %get-tuple-element.210), channel_id=1, source_target_pairs={{0,2},{1,3},{2,0},{3,1},{4,6},{5,7},{6,4},{7,5},{8,10},{9,11},{10,... | collective-permute-start | bytes 1572872 | tf_op jit(solution)/shard_map/ppermute | solution.py:87
  356.6 36.3 %collective-permute-start.48 = (bf16[2,128,1024]{2,1,0:T(8,128)(2,1)S(1)}, bf16[2,128,1024]{2,1,0:T(8,128)(2,1)S(1)}, u32[]{:S(2)}, u32[]{:S(2)}) collective-permute-start(bf16[2,128,1024]{2,1,0:T(8,128)(2,1)S(1)} %get-tuple-element.225), channel_id=1, source_target_pairs={{0,16},{4,20},{8,24},{12,28},{16,0},{20,4},{24,8},{28,12},{1,17},{... | collective-permute-start | bytes 1572872 | tf_op jit(solution)/shard_map/ppermute | solution.py:92
  370.8 22.1 %collective-permute-start.47 = (bf16[1024,256]{1,0:T(8,128)(2,1)}, bf16[1024,256]{1,0:T(8,128)(2,1)S(1)}, u32[]{:S(2)}, u32[]{:S(2)}) collective-permute-start(bf16[1024,256]{1,0:T(8,128)(2,1)} %get-tuple-element.224), channel_id=1, source_target_pairs={{0,1},{1,0},{2,3},{3,2},{4,5},{5,4},{6,7},{7,6},{8,9},{9,8},{10,11... | collective-permute-start | bytes 1572872 | tf_op jit(solution)/shard_map/ppermute | solution.py:87
  370.9 22.1 %collective-permute-start.49 = (bf16[1024,256]{1,0:T(8,128)(2,1)}, bf16[1024,256]{1,0:T(8,128)(2,1)S(1)}, u32[]{:S(2)}, u32[]{:S(2)}) collective-permute-start(bf16[1024,256]{1,0:T(8,128)(2,1)} %get-tuple-element.228), channel_id=1, source_target_pairs={{0,1},{1,0},{2,3},{3,2},{4,5},{5,4},{6,7},{7,6},{8,9},{9,8},{10,11... | collective-permute-start | bytes 1572872 | tf_op jit(solution)/shard_map/ppermute | solution.py:87
  371.4 21.8 %collective-permute-start.43 = (bf16[2,512,256]{2,1,0:T(8,128)(2,1)S(1)}, bf16[2,512,256]{2,1,0:T(8,128)(2,1)S(1)}, u32[]{:S(2)}, u32[]{:S(2)}) collective-permute-start(bf16[2,512,256]{2,1,0:T(8,128)(2,1)S(1)} %get-tuple-element.214), channel_id=1, source_target_pairs={{0,4},{4,0},{8,12},{12,8},{16,20},{20,16},{24,28},{28,24},{1,5},{5... | collective-permute-start | bytes 1572872 | tf_op jit(solution)/shard_map/ppermute | solution.py:92
  374.0 45.9 %collective-permute-start.58 = (bf16[2,128,1024]{2,1,0:T(8,128)(2,1)S(1)}, bf16[2,128,1024]{2,1,0:T(8,128)(2,1)S(1)}, u32[]{:S(2)}, u32[]{:S(2)}) collective-permute-start(bf16[2,128,1024]{2,1,0:T(8,128)(2,1)S(1)} %get-tuple-element.244), channel_id=1, source_target_pairs={{0,16},{4,20},{8,24},{12,28},{16,0},{20,4},{24,8},{28,12},{1,17},{... | collective-permute-start | bytes 1572872 | tf_op jit(solution)/shard_map/ppermute | solution.py:92
  392.9 27.9 %collective-permute-start.61 = (f32[96,128]{1,0:T(8,128)S(1)}, f32[96,128]{1,0:T(8,128)S(1)}, u32[]{:S(2)}, u32[]{:S(2)}) collective-permute-start(f32[96,128]{1,0:T(8,128)S(1)} %copy-done.54), channel_id=1, source_target_pairs={{0,8},{4,12},{8,0},{12,4},{16,24},{20,28},{24,16},{28,20},{1,9},{5... | collective-permute-start | bytes 147464 | tf_op jit(solution)/shard_map/ppermute | solution.py:92
  394.3 22.1 %collective-permute-start.50 = (bf16[2,256,256]{2,1,0:T(8,128)(2,1)S(1)}, bf16[2,256,256]{2,1,0:T(8,128)(2,1)S(1)}, u32[]{:S(2)}, u32[]{:S(2)}) collective-permute-start(bf16[2,256,256]{2,1,0:T(8,128)(2,1)S(1)} %get-tuple-element.231), channel_id=1, source_target_pairs={{0,8},{4,12},{8,0},{12,4},{16,24},{20,28},{24,16},{28,20},{1,9},{5... | collective-permute-start | bytes 786440 | tf_op jit(solution)/shard_map/ppermute | solution.py:92
  396.3 7.5 %collective-permute-start.51 = (bf16[1,512,256]{2,1,0:T(8,128)(2,1)S(1)}, bf16[1,512,256]{2,1,0:T(8,128)(2,1)S(1)}, u32[]{:S(2)}, u32[]{:S(2)}) collective-permute-start(bf16[1,512,256]{2,1,0:T(8,128)(2,1)S(1)} %get-tuple-element.232), channel_id=1, source_target_pairs={{0,4},{4,0},{8,12},{12,8},{16,20},{20,16},{24,28},{28,24},{1,5},{5... | collective-permute-start | bytes 786440 | tf_op jit(solution)/shard_map/ppermute | solution.py:92
  397.4 18.9 %collective-permute-start.52 = (bf16[1,512,256]{2,1,0:T(8,128)(2,1)S(1)}, bf16[1,512,256]{2,1,0:T(8,128)(2,1)S(1)}, u32[]{:S(2)}, u32[]{:S(2)}) collective-permute-start(bf16[1,512,256]{2,1,0:T(8,128)(2,1)S(1)} %get-tuple-element.234), channel_id=1, source_target_pairs={{0,8},{4,12},{8,0},{12,4},{16,24},{20,28},{24,16},{28,20},{1,9},{5... | collective-permute-start | bytes 786440 | tf_op jit(solution)/shard_map/ppermute | solution.py:92
  416.4 14.2 %collective-permute-start.53 = (bf16[2,128,256]{2,1,0:T(8,128)(2,1)S(1)}, bf16[2,128,256]{2,1,0:T(8,128)(2,1)S(1)}, u32[]{:S(2)}, u32[]{:S(2)}) collective-permute-start(bf16[2,128,256]{2,1,0:T(8,128)(2,1)S(1)} %get-tuple-element.237), channel_id=1, source_target_pairs={{0,16},{4,20},{8,24},{12,28},{16,0},{20,4},{24,8},{28,12},{1,17},{... | collective-permute-start | bytes 393224 | tf_op jit(solution)/shard_map/ppermute | solution.py:92
  416.5 11.0 %collective-permute-start.54 = (bf16[1,256,256]{2,1,0:T(8,128)(2,1)S(1)}, bf16[1,256,256]{2,1,0:T(8,128)(2,1)S(1)}, u32[]{:S(2)}, u32[]{:S(2)}) collective-permute-start(bf16[1,256,256]{2,1,0:T(8,128)(2,1)S(1)} %get-tuple-element.238), channel_id=1, source_target_pairs={{0,8},{4,12},{8,0},{12,4},{16,24},{20,28},{24,16},{28,20},{1,9},{5... | collective-permute-start | bytes 393224 | tf_op jit(solution)/shard_map/ppermute | solution.py:92
  418.9 9.4 %collective-permute-start.56 = (bf16[1,256,256]{2,1,0:T(8,128)(2,1)S(1)}, bf16[1,256,256]{2,1,0:T(8,128)(2,1)S(1)}, u32[]{:S(2)}, u32[]{:S(2)}) collective-permute-start(bf16[1,256,256]{2,1,0:T(8,128)(2,1)S(1)} %get-tuple-element.241), channel_id=1, source_target_pairs={{0,4},{4,0},{8,12},{12,8},{16,20},{20,16},{24,28},{28,24},{1,5},{5... | collective-permute-start | bytes 393224 | tf_op jit(solution)/shard_map/ppermute | solution.py:92
  420.0 15.8 %collective-permute-start.59 = (bf16[128,1024]{1,0:T(8,128)(2,1)S(1)}, bf16[128,1024]{1,0:T(8,128)(2,1)S(1)}, u32[]{:S(2)}, u32[]{:S(2)}) collective-permute-start(bf16[128,1024]{1,0:T(8,128)(2,1)S(1)} %fusion.5), channel_id=1, source_target_pairs={{0,2},{1,3},{2,0},{3,1},{4,6},{5,7},{6,4},{7,5},{8,10},{9,11},{10,... | collective-permute-start | bytes 786440 | tf_op jit(solution)/shard_map/ppermute | solution.py:87
  420.9 4.2 collective-permute-start.62
  425.0 9.7 %collective-permute-start.60 = (bf16[128,1024]{1,0:T(8,128)(2,1)}, bf16[128,1024]{1,0:T(8,128)(2,1)S(1)}, u32[]{:S(2)}, u32[]{:S(2)}) collective-permute-start(bf16[128,1024]{1,0:T(8,128)(2,1)} %fusion.6), channel_id=1, source_target_pairs={{0,2},{1,3},{2,0},{3,1},{4,6},{5,7},{6,4},{7,5},{8,10},{9,11},{10,... | collective-permute-start | bytes 786440 | tf_op jit(solution)/shard_map/ppermute | solution.py:87
  427.6 5.8 %collective-permute-start.55 = (bf16[1,128,256]{2,1,0:T(8,128)(2,1)S(1)}, bf16[1,128,256]{2,1,0:T(8,128)(2,1)S(1)}, u32[]{:S(2)}, u32[]{:S(2)}) collective-permute-start(bf16[1,128,256]{2,1,0:T(8,128)(2,1)S(1)} %get-tuple-element.240), channel_id=1, source_target_pairs={{0,16},{4,20},{8,24},{12,28},{16,0},{20,4},{24,8},{28,12},{1,17},{... | collective-permute-start | bytes 196616 | tf_op jit(solution)/shard_map/ppermute | solution.py:92
  428.3 5.8 %collective-permute-start.57 = (bf16[1,128,256]{2,1,0:T(8,128)(2,1)S(1)}, bf16[1,128,256]{2,1,0:T(8,128)(2,1)S(1)}, u32[]{:S(2)}, u32[]{:S(2)}) collective-permute-start(bf16[1,128,256]{2,1,0:T(8,128)(2,1)S(1)} %get-tuple-element.243), channel_id=1, source_target_pairs={{0,16},{4,20},{8,24},{12,28},{16,0},{20,4},{24,8},{28,12},{1,17},{... | collective-permute-start | bytes 196616 | tf_op jit(solution)/shard_map/ppermute | solution.py:92
  (94 other events, 603.0 us)

commit v9 on v8

--- a/solution.py
+++ b/solution.py
@@ -909,12 +909,13 @@
             one[s][0], two[s][1], fed_back[s][2], back_got[s], gain_one, deps
         )
 
-    one_back = [norm_back(s, [fed_back[-1][2]]) for s in seqs]
+    one_back = [norm_back(0, [fed_back[-1][2]])]
     up_made = weight_grad(
         pairs([one[s][2] for s in seqs], normed_far),
         [fed_back[s][0] for s in seqs], [fed_back[s][1] for s in seqs],
-        dp_place, [(hidden, far_first)], "w_up_grad", deps=[one_back[s][1] for s in seqs], halves=True,
-    )
+        dp_place, [(hidden, far_first)], "w_up_grad", deps=[one_back[0][1]], halves=True,
+    )
+    one_back += [norm_back(s, [up_made[1]]) for s in seqs[1:]]
     first_across = [swap_tensor(one_back[s][1], ACROSS) for s in seqs]
     down_chain = Chain(*down_made, near_first)
     up_chain = Chain(*up_made, far_first)

time: 443 us -> 443 us (level)
    unnamed x203 -> x195, local copies, waits for them, and re-layouts: 45 us -> 43.2 us
where the time goes in v9:
time: 443 us; the launch traced here: 438 us
  Pallas kernels  232 us (52%)
  waiting for transfers between devices  82.2 us (19%)
  starting transfers between devices  55.2 us (12%)
  local copies, waits for them, and re-layouts  54.8 us (12%)
  other arithmetic  11.4 us (3%)
    pallas_call x40, Pallas kernels, whole_call(): pl.pallas_call(after(kernel, len(args), deps), out_shape=tuple(outs), in_...  118 us
    pallas_call x11, Pallas kernels, streamed_call(): pl.pallas_call(after(kernel, len(args), deps), grid=grid, out_shape=tuple...  99.1 us
    ppermute x29, waiting for transfers between devices, swap_dp(): return lax.ppermute(array, 'dp', [(i, i ^ bit) for i in range(size)])  68 us
    unnamed x195, local copies, waits for them, and re-layouts  43.2 us
    ppermute x29, starting transfers between devices, swap_dp(): return lax.ppermute(array, 'dp', [(i, i ^ bit) for i in range(size)])  36.5 us
    ppermute x34, starting transfers between devices, swap_tensor(): return lax.ppermute(array, 'tensor', [(i, i ^ bit) for i in range(size)])  18.7 us
    pallas_call x4, Pallas kernels, assemble(): pl.pallas_call(after(kernel, 1 + len(arrays), deps), out_shape=out, in_sp...  15.1 us
    ppermute x34, waiting for transfers between devices, swap_tensor(): return lax.ppermute(array, 'tensor', [(i, i ^ bit) for i in range(size)])  14.2 us
  transfers between devices with their start and end apart: 63, of which 14 were waited for; matrix products, arithmetic and copies ran while one was open for 7% of the time, Pallas kernels for 50%

profile of v9, /device:TPU:0, one launch (start us, length us, event | category | flops | bytes accessed | tf_op | source)
XLA Modules:
  0.0 437.7 jit_solution(13343403595595168795)
XLA Ops:
  0.7 1.7 copy.39
  2.3 1.7 pack_attention.1
  4.0 4.0 collective-permute-start.1
  8.0 1.8 copy.40
  9.8 10.3 %collective-permute-done.1.refs_2_ = bf16[128,1024]{1,0:T(8,128)(2,1)S(1)} collective-permute-done((bf16[128,1024]{1,0:T(8,128)(2,1)}, bf16[128,1024]{1,0:T(8,128)(2,1)S(1)}, u32[]{:S(2)}, u32[]{:S(2)}) %collective-permute-start.1) | collective-permute-done | bytes 262176 | tf_op jit(solution)/shard_map/ppermute | solution.py:92
  22.2 1.9 pack_feed.1
  24.0 3.3 collective-permute-start.10
  27.3 1.5 collective-permute-start.3
  28.8 1.5 collective-permute-start
  31.7 11.8 %collective-permute-done.2.refs_2_ = bf16[256,1024]{1,0:T(8,128)(2,1)} collective-permute-done((bf16[256,1024]{1,0:T(8,128)(2,1)S(1)}, bf16[256,1024]{1,0:T(8,128)(2,1)}, u32[]{:S(2)}, u32[]{:S(2)}) %collective-permute-start.2) | collective-permute-done | bytes 524320 | tf_op jit(solution)/shard_map/ppermute | solution.py:92
  44.8 5.8 %collective-permute-done.10.refs_6_ = bf16[128,2048]{1,0:T(8,128)(2,1)S(1)} collective-permute-done((bf16[128,2048]{1,0:T(8,128)(2,1)}, bf16[128,2048]{1,0:T(8,128)(2,1)S(1)}, u32[]{:S(2)}, u32[]{:S(2)}) %collective-permute-start.10) | collective-permute-done | bytes 524320 | tf_op jit(solution)/shard_map/ppermute | solution.py:92
  50.6 1.5 collective-permute-start.4
  52.1 2.1 pad_maximum_fusion.refs_1_
  55.6 8.8 %collective-permute-done.16.refs_6_ = bf16[128,2048]{1,0:T(8,128)(2,1)} collective-permute-done((bf16[128,2048]{1,0:T(8,128)(2,1)}, bf16[128,2048]{1,0:T(8,128)(2,1)}, u32[]{:S(2)}, u32[]{:S(2)}) %collective-permute-start.16) | collective-permute-done | bytes 524320 | tf_op jit(solution)/shard_map/ppermute | solution.py:87
  66.8 2.2 slice_bitcast_fusion.5
  69.0 2.9 assemble_attention.1.refs_2_.refs_4_.refs_6_.refs_3_
  73.8 3.0 assemble_attention_other.1.refs_3_.refs_5_.refs_7_.refs_4_
  76.7 5.6 %project_inputs.2 = (bf16[512,768]{1,0:T(8,128)(2,1)}, bf16[512,768]{1,0:T(8,128)(2,1)}, bf16[512,1024]{1,0:T(8,128)(2,1)}) custom-call(bf16[256,1024]{1,0:T(8,128)(2,1)} %get-tuple-element.285.refs_0_.refs_1_, bf16[256,1024]{1,0:T(8,128)(2,1)} %get-tuple-element.283.refs_1_.refs_2_, bf16[1024,1024]{1,0:T(8,128)(2,1)} %assemble_attention.1.refs_2_.refs_4_.refs_6_.refs_3_, ...), custom_call_target="tpu_custom_call" | custom-call | flops 1610612 | bytes 7870 | tf_op jit(solution)/shard_map/project_inputs/pallas_call | solution.py:47
  83.1 5.6 %project_inputs.3 = (bf16[512,768]{1,0:T(8,128)(2,1)}, bf16[512,768]{1,0:T(8,128)(2,1)}, bf16[512,1024]{1,0:T(8,128)(2,1)}) custom-call(bf16[256,1024]{1,0:T(8,128)(2,1)} %get-tuple-element.286.refs_0_.refs_3_, bf16[256,1024]{1,0:T(8,128)(2,1)} %get-tuple-element.284.refs_1_.refs_4_, bf16[1024,1024]{1,0:T(8,128)(2,1)} %assemble_attention.1.refs_2_.refs_4_.refs_6_.refs_3_, ...), custom_call_target="tpu_custom_call" | custom-call | flops 1610612 | bytes 7870 | tf_op jit(solution)/shard_map/project_inputs/pallas_call | solution.py:47
  90.2 1.9 constant_dynamic-update-slice_fusion.1
  98.9 12.8 %attention_forward.2 = (bf16[512,256]{1,0:T(8,128)(2,1)}, bf16[512,256]{1,0:T(8,128)(2,1)}, f32[256,1024]{1,0:T(8,128)}, bf16[256,1024]{1,0:T(8,128)(2,1)}) custom-call(bf16[512,768]{1,0:T(8,128)(2,1)} %get-tuple-element.131.refs_0_, bf16[512,768]{1,0:T(8,128)(2,1)} %get-tuple-element.132.refs_1_, bf16[512,1024]{1,0:T(8,128)(2,1)} %collective-permute-done.11.refs_2_, ...), custom_call_target="tpu_custom_call" | custom-call | flops 8589934 | bytes 8916 | tf_op jit(solution)/shard_map/attention_forward/pallas_call | solution.py:47
  111.7 1.5 collective-permute-start.13
  114.2 12.8 %attention_forward.3 = (bf16[512,256]{1,0:T(8,128)(2,1)}, bf16[512,256]{1,0:T(8,128)(2,1)}, f32[256,1024]{1,0:T(8,128)}, bf16[256,1024]{1,0:T(8,128)(2,1)}) custom-call(bf16[512,768]{1,0:T(8,128)(2,1)} %get-tuple-element.138.refs_0_, bf16[512,768]{1,0:T(8,128)(2,1)} %get-tuple-element.139.refs_1_, bf16[512,1024]{1,0:T(8,128)(2,1)} %collective-permute-done.21.refs_2_, ...), custom_call_target="tpu_custom_call" | custom-call | flops 8589934 | bytes 8916 | tf_op jit(solution)/shard_map/attention_forward/pallas_call | solution.py:47
  129.0 2.0 collective-permute-done.14.refs_6_.refs_4_
  131.0 1.5 collective-permute-start.20
  133.2 4.7 %assemble_feed.1.refs_7_.refs_2_.refs_3_.refs_4_ = bf16[1024,2048]{1,0:T(8,128)(2,1)} custom-call(s32[1]{0:T(128)} %bitcast.2.refs_0_, bf16[256,2048]{1,0:T(8,128)(2,1)} %pad_maximum_fusion.refs_1_, bf16[256,2048]{1,0:T(8,128)(2,1)} %copy-done.64, bf16[256,2048]{1,0:T(8,128)(2,1)} %copy-done.65, bf16[256,2048]{1,0:T(8,128)(2,1)} %copy-done.7), custom_call_target="tpu_custom_call" | custom-call | bytes 8388 | tf_op jit(solution)/shard_map/assemble_feed/pallas_call | solution.py:154
  137.9 4.2 collective-permute-done.23.refs_2_
  142.1 2.2 copy-done
  147.2 8.8 %feed_forward.4 = (bf16[512,1024]{1,0:T(8,128)(2,1)}, bf16[512,1024]{1,0:T(8,128)(2,1)}, f32[512,1024]{1,0:T(8,128)}) custom-call(bf16[256,1024]{1,0:T(8,128)(2,1)} %copy-done.5, bf16[256,1024]{1,0:T(8,128)(2,1)} %copy-done.62, bf16[1024,2048]{1,0:T(8,128)(2,1)} %assemble_feed.1.refs_7_.refs_2_.refs_3_.refs_4_, ...), custom_call_target="tpu_custom_call" | custom-call | flops 2147483 | bytes 13635 | tf_op jit(solution)/shard_map/feed_forward/pallas_call | solution.py:64
  156.8 8.9 %feed_forward.5 = (bf16[512,1024]{1,0:T(8,128)(2,1)}, bf16[512,1024]{1,0:T(8,128)(2,1)}, f32[512,1024]{1,0:T(8,128)}) custom-call(bf16[256,1024]{1,0:T(8,128)(2,1)} %copy-done.6, bf16[256,1024]{1,0:T(8,128)(2,1)} %copy-done.63, bf16[1024,2048]{1,0:T(8,128)(2,1)} %assemble_feed.1.refs_7_.refs_2_.refs_3_.refs_4_, ...), custom_call_target="tpu_custom_call" | custom-call | flops 2147483 | bytes 13635 | tf_op jit(solution)/shard_map/feed_forward/pallas_call | solution.py:64
  165.7 4.5 %assemble_feed_other.1.refs_2_.refs_3_.refs_5_ = bf16[1024,2048]{1,0:T(8,128)(2,1)} custom-call(s32[1]{0:T(128)} %bitcast.2.refs_0_, bf16[256,2048]{1,0:T(8,128)(2,1)} %constant_dynamic-update-slice_fusion.refs_1_, bf16[256,2048]{1,0:T(8,128)(2,1)} %collective-permute-done.18.refs_6_.refs_2_, bf16[256,2048]{1,0:T(8,128)(2,1)} %collective-permute-done.19.refs_3_, ...), custom_call_target="tpu_custom_call" | custom-call | bytes 8388 | tf_op jit(solution)/shard_map/assemble_feed_other/pallas_call | solution.py:154
  170.8 9.7 %feed_forward.6 = (bf16[512,1024]{1,0:T(8,128)(2,1)}, bf16[512,1024]{1,0:T(8,128)(2,1)}, f32[256,1024]{1,0:T(8,128)}, bf16[256,1024]{1,0:T(8,128)(2,1)}) custom-call(bf16[256,1024]{1,0:T(8,128)(2,1)} %copy-done.5, bf16[256,1024]{1,0:T(8,128)(2,1)} %copy-done.62, bf16[1024,2048]{1,0:T(8,128)(2,1)} %assemble_feed_other.1.refs_2_.refs_3_.refs_5_, ...), custom_call_target="tpu_custom_call" | custom-call | flops 2147483 | bytes 15208 | tf_op jit(solution)/shard_map/feed_forward/pallas_call | solution.py:64
  180.7 10.1 %feed_forward.7 = (bf16[512,1024]{1,0:T(8,128)(2,1)}, bf16[512,1024]{1,0:T(8,128)(2,1)}, f32[256,1024]{1,0:T(8,128)}, bf16[256,1024]{1,0:T(8,128)(2,1)}) custom-call(bf16[256,1024]{1,0:T(8,128)(2,1)} %copy-done.6, bf16[256,1024]{1,0:T(8,128)(2,1)} %copy-done.63, bf16[1024,2048]{1,0:T(8,128)(2,1)} %assemble_feed_other.1.refs_2_.refs_3_.refs_5_, ...), custom_call_target="tpu_custom_call" | custom-call | flops 2147483 | bytes 15208 | tf_op jit(solution)/shard_map/feed_forward/pallas_call | solution.py:64
  197.4 11.4 %feed_forward_back.2 = (bf16[512,1024]{1,0:T(8,128)(2,1)}, bf16[512,1024]{1,0:T(8,128)(2,1)}, f32[256,1024]{1,0:T(8,128)}, bf16[256,1024]{1,0:T(8,128)(2,1)}, f32[1,1024]{1,0:T(1,128)}, /*index=5*/f32[1,1024]{1,0:T(1,128)}) custom-call(bf16[256,1024]{1,0:T(8,128)(2,1)} %copy-done.24, bf16[256,1024]{1,0:T(8,128)(2,1)} %copy-done.70, ...), custom_call_target="tpu_custom_call" | custom-call | flops 4294967 | bytes 23601 | tf_op jit(solution)/shard_map/feed_forward_back/pallas_call | solution.py:64
  210.0 10.0 %w_down_grad.1 = (f32[2,512,1024]{2,1,0:T(8,128)}, bf16[2,512,1024]{2,1,0:T(8,128)(2,1)}) custom-call(s32[1]{0:T(128)} %bitcast.2.refs_0_, bf16[256,1024]{1,0:T(8,128)(2,1)} %copy-done.24, bf16[256,1024]{1,0:T(8,128)(2,1)} %copy-done.70, bf16[256,1024]{1,0:T(8,128)(2,1)} %copy-done.25, bf16[256,1024]{1,0:T(8,128)(2,1)} %copy-done.71, ...), custom_call_target="tpu_custom_call" | custom-call | flops 4294967 | bytes 12582 | tf_op jit(solution)/shard_map/w_down_grad/pallas_call | solution.py:64
  220.0 11.5 %feed_forward_back.3 = (bf16[512,1024]{1,0:T(8,128)(2,1)}, bf16[512,1024]{1,0:T(8,128)(2,1)}, f32[256,1024]{1,0:T(8,128)}, bf16[256,1024]{1,0:T(8,128)(2,1)}, f32[1,1024]{1,0:T(1,128)}, /*index=5*/f32[1,1024]{1,0:T(1,128)}) custom-call(bf16[256,1024]{1,0:T(8,128)(2,1)} %copy-done.25, bf16[256,1024]{1,0:T(8,128)(2,1)} %copy-done.71, ...), custom_call_target="tpu_custom_call" | custom-call | flops 4294967 | bytes 23601 | tf_op jit(solution)/shard_map/feed_forward_back/pallas_call | solution.py:64
  234.8 1.5 collective-permute-start.31
  238.4 1.6 collective-permute-start.35
  240.7 10.3 %w_up_grad.1 = (f32[2,512,1024]{2,1,0:T(8,128)}, bf16[2,512,1024]{2,1,0:T(8,128)(2,1)}) custom-call(s32[1]{0:T(128)} %bitcast.2.refs_0_, bf16[256,1024]{1,0:T(8,128)(2,1)} %copy-done.5, bf16[256,1024]{1,0:T(8,128)(2,1)} %copy-done.62, bf16[256,1024]{1,0:T(8,128)(2,1)} %copy-done.6, bf16[256,1024]{1,0:T(8,128)(2,1)} %copy-done.63, ...), custom_call_target="tpu_custom_call" | custom-call | flops 4294967 | bytes 12582 | tf_op jit(solution)/shard_map/w_up_grad/pallas_call | solution.py:64
  251.3 1.6 copy-done.23
  252.9 1.7 first_norm_back.3
  256.1 26.3 %attention_backward.2 = (bf16[512,512]{1,0:T(8,128)(2,1)}, f32[512,1024]{1,0:T(8,128)}, bf16[512,1024]{1,0:T(8,128)(2,1)}, f32[2,512]{1,0:T(2,128)}) custom-call(bf16[512,768]{1,0:T(8,128)(2,1)} %get-tuple-element.131.refs_0_, bf16[512,768]{1,0:T(8,128)(2,1)} %get-tuple-element.132.refs_1_, bf16[512,1024]{1,0:T(8,128)(2,1)} %collective-permute-done.11.refs_2_, ...), custom_call_target="tpu_custom_call" | custom-call | flops 21474836480 | bytes 11542 | tf_op jit(solution)/shard_map/attention_backward/pallas_call | solution.py:47
  282.4 4.4 %w_out_grad.1 = (f32[1024,256]{1,0:T(8,128)}, bf16[1024,256]{1,0:T(8,128)(2,1)}) custom-call(s32[1]{0:T(128)} %bitcast.2.refs_0_, bf16[256,1024]{1,0:T(8,128)(2,1)} %copy-done.26, bf16[256,1024]{1,0:T(8,128)(2,1)} %collective-permute-done.31.refs_5_.refs_2_, bf16[256,1024]{1,0:T(8,128)(2,1)} %get-tuple-element.182.refs_3_.refs_4_, ...), custom_call_target="tpu_custom_call" | custom-call | flops 1073741 | bytes 4718 | tf_op jit(solution)/shard_map/w_out_grad/pallas_call | solution.py:64
  286.9 3.0 fold.15
  291.2 26.2 %attention_backward.3 = (bf16[512,512]{1,0:T(8,128)(2,1)}, f32[512,1024]{1,0:T(8,128)}, bf16[512,1024]{1,0:T(8,128)(2,1)}, f32[2,512]{1,0:T(2,128)}) custom-call(bf16[512,768]{1,0:T(8,128)(2,1)} %get-tuple-element.138.refs_0_, bf16[512,768]{1,0:T(8,128)(2,1)} %get-tuple-element.139.refs_1_, bf16[512,1024]{1,0:T(8,128)(2,1)} %collective-permute-done.21.refs_2_, ...), custom_call_target="tpu_custom_call" | custom-call | flops 21474836480 | bytes 11542 | tf_op jit(solution)/shard_map/attention_backward/pallas_call | solution.py:47
  319.8 1.7 collective-permute-start.45
  321.5 2.2 copy-done.13
  327.5 4.4 %w_query_grad.1 = (f32[1024,256]{1,0:T(8,128)}, bf16[1024,256]{1,0:T(8,128)(2,1)}) custom-call(s32[1]{0:T(128)} %bitcast.2.refs_0_, bf16[256,1024]{1,0:T(8,128)(2,1)} %get-tuple-element.285.refs_0_.refs_1_, bf16[256,1024]{1,0:T(8,128)(2,1)} %get-tuple-element.283.refs_1_.refs_2_, bf16[256,1024]{1,0:T(8,128)(2,1)} %get-tuple-element.286.refs_0_.refs_3_, ...), custom_call_target="tpu_custom_call" | custom-call | flops 1073741 | bytes 5767 | tf_op jit(solution)/shard_map/w_query_grad/pallas_call | solution.py:64
  331.9 2.2 pad_maximum_fusion.3
  334.8 1.5 collective-permute-start.40
  336.3 6.3 %project_back.2 = (bf16[512,512]{1,0:T(8,128)(2,1)}, bf16[512,512]{1,0:T(8,128)(2,1)}, f32[256,1024]{1,0:T(8,128)}, bf16[256,1024]{1,0:T(8,128)(2,1)}) custom-call(bf16[512,512]{1,0:T(8,128)(2,1)} %get-tuple-element.176.refs_5_.refs_7_.refs_0_, f32[512,1024]{1,0:T(8,128)} %get-tuple-element.177.refs_1_, bf16[512,1024]{1,0:T(8,128)(2,1)} %copy-done.66, ...), custom_call_target="tpu_custom_call" | custom-call | flops 1610612 | bytes 10485 | tf_op jit(solution)/shard_map/project_back/pallas_call | solution.py:47
  345.8 6.4 %project_back.3 = (bf16[512,512]{1,0:T(8,128)(2,1)}, bf16[512,512]{1,0:T(8,128)(2,1)}, f32[256,1024]{1,0:T(8,128)}, bf16[256,1024]{1,0:T(8,128)(2,1)}) custom-call(bf16[512,512]{1,0:T(8,128)(2,1)} %get-tuple-element.191.refs_6_.refs_8_.refs_0_, f32[512,1024]{1,0:T(8,128)} %get-tuple-element.207.refs_1_, bf16[512,1024]{1,0:T(8,128)(2,1)} %collective-permute-done.39.refs_2_, ...), custom_call_target="tpu_custom_call" | custom-call | flops 1610612 | bytes 10485 | tf_op jit(solution)/shard_map/project_back/pallas_call | solution.py:47
  353.1 1.5 collective-permute-start.41
  357.3 1.6 collective-permute-start.48
  362.6 9.6 %w_key_value_grad.1 = (f32[1024,256]{1,0:T(8,128)}, bf16[1024,256]{1,0:T(8,128)(2,1)}, f32[1024,256]{1,0:T(8,128)}, bf16[1024,256]{1,0:T(8,128)(2,1)}) custom-call(s32[1]{0:T(128)} %bitcast.2.refs_0_, bf16[256,1024]{1,0:T(8,128)(2,1)} %get-tuple-element.285.refs_0_.refs_1_, bf16[256,1024]{1,0:T(8,128)(2,1)} %get-tuple-element.283.refs_1_.refs_2_, ...), custom_call_target="tpu_custom_call" | custom-call | flops 2147483 | bytes 7340 | tf_op jit(solution)/shard_map/w_key_value_grad/pallas_call | solution.py:64
  372.8 1.5 collective-permute-start.43
  378.1 16.4 %collective-permute-done.48.refs_3_.refs_1_ = bf16[2,128,1024]{2,1,0:T(8,128)(2,1)S(1)} collective-permute-done((bf16[2,128,1024]{2,1,0:T(8,128)(2,1)S(1)}, bf16[2,128,1024]{2,1,0:T(8,128)(2,1)S(1)}, u32[]{:S(2)}, u32[]{:S(2)}) %collective-permute-start.48) | collective-permute-done | bytes 524320 | tf_op jit(solution)/shard_map/ppermute | solution.py:92
  395.9 2.1 collective-permute-start.50
  399.9 4.4 %collective-permute-done.51.refs_1_ = bf16[1,512,256]{2,1,0:T(8,128)(2,1)S(1)} collective-permute-done((bf16[1,512,256]{2,1,0:T(8,128)(2,1)S(1)}, bf16[1,512,256]{2,1,0:T(8,128)(2,1)S(1)}, u32[]{:S(2)}, u32[]{:S(2)}) %collective-permute-start.51) | collective-permute-done | bytes 262176 | tf_op jit(solution)/shard_map/ppermute | solution.py:92
  404.4 12.7 %collective-permute-done.52.refs_1_ = bf16[1,512,256]{2,1,0:T(8,128)(2,1)S(1)} collective-permute-done((bf16[1,512,256]{2,1,0:T(8,128)(2,1)S(1)}, bf16[1,512,256]{2,1,0:T(8,128)(2,1)S(1)}, u32[]{:S(2)}, u32[]{:S(2)}) %collective-permute-start.52) | collective-permute-done | bytes 262176 | tf_op jit(solution)/shard_map/ppermute | solution.py:92
  417.2 2.3 collective-permute-start.54
  423.2 2.3 collective-permute-done.62.refs_1_
  425.5 1.5 collective-permute-start.60
  429.4 2.0 collective-permute-start.57
  (355 shorter events, 81.5 us)
Async XLA Ops:
  4.0 16.2 %collective-permute-start.1 = (bf16[128,1024]{1,0:T(8,128)(2,1)}, bf16[128,1024]{1,0:T(8,128)(2,1)S(1)}, u32[]{:S(2)}, u32[]{:S(2)}) collective-permute-start(bf16[128,1024]{1,0:T(8,128)(2,1)} %pack_attention.1), channel_id=1, source_target_pairs={{0,16},{4,20},{8,24},{12,28},{16,0},{20,4},{24,8},{28,12},{1,17},{... | collective-permute-start | bytes 786440 | tf_op jit(solution)/shard_map/ppermute | solution.py:92
  21.3 44.7 %copy-start.68 = (bf16[256,1024]{1,0:T(8,128)(2,1)}, bf16[256,1024]{1,0:T(8,128)(2,1)S(1)}, u32[]{:S(2)}) copy-start(bf16[256,1024]{1,0:T(8,128)(2,1)S(1)} %pad_maximum_fusion.4.refs_1_) | copy-start | bytes 1572868
  21.3 22.2 %collective-permute-start.2 = (bf16[256,1024]{1,0:T(8,128)(2,1)S(1)}, bf16[256,1024]{1,0:T(8,128)(2,1)}, u32[]{:S(2)}, u32[]{:S(2)}) collective-permute-start(bf16[256,1024]{1,0:T(8,128)(2,1)S(1)} %pad_maximum_fusion.4.refs_1_), channel_id=1, source_target_pairs={{0,8},{4,12},{8,0},{12,4},{16,24},{20,28},{24,16},{28,20},{1,9},{5... | collective-permute-start | bytes 1572872 | tf_op jit(solution)/shard_map/ppermute | solution.py:92
  24.0 26.6 %collective-permute-start.10 = (bf16[128,2048]{1,0:T(8,128)(2,1)}, bf16[128,2048]{1,0:T(8,128)(2,1)S(1)}, u32[]{:S(2)}, u32[]{:S(2)}) collective-permute-start(bf16[128,2048]{1,0:T(8,128)(2,1)} %pack_feed.1), channel_id=1, source_target_pairs={{0,16},{4,20},{8,24},{12,28},{16,0},{20,4},{24,8},{28,12},{1,17},{... | collective-permute-start | bytes 1572872 | tf_op jit(solution)/shard_map/ppermute | solution.py:92
  27.3 26.9 %collective-permute-start.3 = (bf16[256,1024]{1,0:T(8,128)(2,1)S(1)}, bf16[256,1024]{1,0:T(8,128)(2,1)S(1)}, u32[]{:S(2)}, u32[]{:S(2)}) collective-permute-start(bf16[256,1024]{1,0:T(8,128)(2,1)S(1)} %pad_maximum_fusion.4.refs_1_), channel_id=1, source_target_pairs={{0,4},{4,0},{8,12},{12,8},{16,20},{20,16},{24,28},{28,24},{1,5},{5... | collective-permute-start | bytes 1572872 | tf_op jit(solution)/shard_map/ppermute | solution.py:92
  28.8 37.7 %collective-permute-start = (bf16[2,256,1024]{2,1,0:T(8,128)(2,1)S(1)}, bf16[2,256,1024]{2,1,0:T(8,128)(2,1)}, u32[]{:S(2)}, u32[]{:S(2)}) collective-permute-start(bf16[2,256,1024]{2,1,0:T(8,128)(2,1)S(1)} %copy-done.72), channel_id=1, source_target_pairs={{0,2},{1,3},{2,0},{3,1},{4,6},{5,7},{6,4},{7,5},{8,10},{9,11},{10,... | collective-permute-start | bytes 3145736 | tf_op jit(solution)/shard_map/ppermute | solution.py:87
  30.3 1.2 collective-permute-start.9
  31.6 24.0 %collective-permute-start.5 = (bf16[256,1024]{1,0:T(8,128)(2,1)S(1)}, bf16[256,1024]{1,0:T(8,128)(2,1)}, u32[]{:S(2)}, u32[]{:S(2)}) collective-permute-start(bf16[256,1024]{1,0:T(8,128)(2,1)S(1)} %pad_maximum_fusion.4.refs_1_), channel_id=1, source_target_pairs={{0,1},{1,0},{2,3},{3,2},{4,5},{5,4},{6,7},{7,6},{8,9},{9,8},{10,11... | collective-permute-start | bytes 1572872 | tf_op jit(solution)/shard_map/ppermute | solution.py:87
  43.5 20.9 %collective-permute-start.16 = (bf16[128,2048]{1,0:T(8,128)(2,1)}, bf16[128,2048]{1,0:T(8,128)(2,1)}, u32[]{:S(2)}, u32[]{:S(2)}) collective-permute-start(bf16[128,2048]{1,0:T(8,128)(2,1)} %pack_feed.1), channel_id=1, source_target_pairs={{0,2},{1,3},{2,0},{3,1},{4,6},{5,7},{6,4},{7,5},{8,10},{9,11},{10,... | collective-permute-start | bytes 1572872 | tf_op jit(solution)/shard_map/ppermute | solution.py:87
  50.6 13.8 %collective-permute-start.4 = (bf16[256,1024]{1,0:T(8,128)(2,1)}, bf16[256,1024]{1,0:T(8,128)(2,1)}, u32[]{:S(2)}, u32[]{:S(2)}) collective-permute-start(bf16[256,1024]{1,0:T(8,128)(2,1)} %collective-permute-done.2.refs_2_), channel_id=1, source_target_pairs={{0,4},{4,0},{8,12},{12,8},{16,20},{20,16},{24,28},{28,24},{1,5},{5... | collective-permute-start | bytes 1572872 | tf_op jit(solution)/shard_map/ppermute | solution.py:92
  55.0 33.9 %collective-permute-start.12 = (bf16[256,2048]{1,0:T(8,128)(2,1)}, bf16[256,2048]{1,0:T(8,128)(2,1)S(1)}, u32[]{:S(2)}, u32[]{:S(2)}) collective-permute-start(bf16[256,2048]{1,0:T(8,128)(2,1)} %pad_maximum_fusion.refs_1_), channel_id=1, source_target_pairs={{0,8},{4,12},{8,0},{12,4},{16,24},{20,28},{24,16},{28,20},{1,9},{5... | collective-permute-start | bytes 3145736 | tf_op jit(solution)/shard_map/ppermute | solution.py:92
  55.6 16.4 %collective-permute-start.6 = (bf16[256,1024]{1,0:T(8,128)(2,1)}, bf16[256,1024]{1,0:T(8,128)(2,1)S(1)}, u32[]{:S(2)}, u32[]{:S(2)}) collective-permute-start(bf16[256,1024]{1,0:T(8,128)(2,1)} %collective-permute-done.2.refs_2_), channel_id=1, source_target_pairs={{0,1},{1,0},{2,3},{3,2},{4,5},{5,4},{6,7},{7,6},{8,9},{9,8},{10,11... | collective-permute-start | bytes 1572872 | tf_op jit(solution)/shard_map/ppermute | solution.py:87
  64.4 7.6 %collective-permute-start.7 = (bf16[256,1024]{1,0:T(8,128)(2,1)}, bf16[256,1024]{1,0:T(8,128)(2,1)S(1)}, u32[]{:S(2)}, u32[]{:S(2)}) collective-permute-start(bf16[256,1024]{1,0:T(8,128)(2,1)} %copy-done.75), channel_id=1, source_target_pairs={{0,1},{1,0},{2,3},{3,2},{4,5},{5,4},{6,7},{7,6},{8,9},{9,8},{10,11... | collective-permute-start | bytes 1572872 | tf_op jit(solution)/shard_map/ppermute | solution.py:87
  64.4 7.6 %collective-permute-start.8 = (bf16[256,1024]{1,0:T(8,128)(2,1)}, bf16[256,1024]{1,0:T(8,128)(2,1)S(1)}, u32[]{:S(2)}, u32[]{:S(2)}) collective-permute-start(bf16[256,1024]{1,0:T(8,128)(2,1)} %collective-permute-done.4.refs_4_), channel_id=1, source_target_pairs={{0,1},{1,0},{2,3},{3,2},{4,5},{5,4},{6,7},{7,6},{8,9},{9,8},{10,11... | collective-permute-start | bytes 1572872 | tf_op jit(solution)/shard_map/ppermute | solution.py:87
  66.5 26.2 %collective-permute-start.17 = (bf16[128,2048]{1,0:T(8,128)(2,1)}, bf16[128,2048]{1,0:T(8,128)(2,1)S(1)}, u32[]{:S(2)}, u32[]{:S(2)}) collective-permute-start(bf16[128,2048]{1,0:T(8,128)(2,1)} %collective-permute-done.16.refs_6_), channel_id=1, source_target_pairs={{0,16},{4,20},{8,24},{12,28},{16,0},{20,4},{24,8},{28,12},{1,17},{... | collective-permute-start | bytes 1572872 | tf_op jit(solution)/shard_map/ppermute | solution.py:92
  82.3 16.5 %collective-permute-start.11 = (bf16[512,1024]{1,0:T(8,128)(2,1)}, bf16[512,1024]{1,0:T(8,128)(2,1)}, u32[]{:S(2)}, u32[]{:S(2)}) collective-permute-start(bf16[512,1024]{1,0:T(8,128)(2,1)} %get-tuple-element.133.refs_7_), channel_id=1, source_target_pairs={{0,1},{1,0},{2,3},{3,2},{4,5},{5,4},{6,7},{7,6},{8,9},{9,8},{10,11... | collective-permute-start | bytes 3145736 | tf_op jit(solution)/shard_map/ppermute | solution.py:87
  82.3 30.9 %collective-permute-start.22 = (bf16[256,2048]{1,0:T(8,128)(2,1)}, bf16[256,2048]{1,0:T(8,128)(2,1)S(1)}, u32[]{:S(2)}, u32[]{:S(2)}) collective-permute-start(bf16[256,2048]{1,0:T(8,128)(2,1)} %pad_maximum_fusion.refs_1_), channel_id=1, source_target_pairs={{0,4},{4,0},{8,12},{12,8},{16,20},{20,16},{24,28},{28,24},{1,5},{5... | collective-permute-start | bytes 3145736 | tf_op jit(solution)/shard_map/ppermute | solution.py:92
  88.7 24.6 %collective-permute-start.21 = (bf16[512,1024]{1,0:T(8,128)(2,1)}, bf16[512,1024]{1,0:T(8,128)(2,1)}, u32[]{:S(2)}, u32[]{:S(2)}) collective-permute-start(bf16[512,1024]{1,0:T(8,128)(2,1)} %get-tuple-element.140), channel_id=1, source_target_pairs={{0,1},{1,0},{2,3},{3,2},{4,5},{5,4},{6,7},{7,6},{8,9},{9,8},{10,11... | collective-permute-start | bytes 3145736 | tf_op jit(solution)/shard_map/ppermute | solution.py:87
  88.9 42.0 %collective-permute-start.14 = (bf16[256,2048]{1,0:T(8,128)(2,1)S(1)}, bf16[256,2048]{1,0:T(8,128)(2,1)S(1)}, u32[]{:S(2)}, u32[]{:S(2)}) collective-permute-start(bf16[256,2048]{1,0:T(8,128)(2,1)S(1)} %collective-permute-done.12.refs_6_.refs_2_), channel_id=1, source_target_pairs={{0,4},{4,0},{8,12},{12,8},{16,20},{20,16},{24,28},{28,24},{1,5},{5... | collective-permute-start | bytes 3145736 | tf_op jit(solution)/shard_map/ppermute | solution.py:92
  94.4 43.4 %collective-permute-start.18 = (bf16[256,2048]{1,0:T(8,128)(2,1)}, bf16[256,2048]{1,0:T(8,128)(2,1)}, u32[]{:S(2)}, u32[]{:S(2)}) collective-permute-start(bf16[256,2048]{1,0:T(8,128)(2,1)} %constant_dynamic-update-slice_fusion.refs_1_), channel_id=1, source_target_pairs={{0,8},{4,12},{8,0},{12,4},{16,24},{20,28},{24,16},{28,20},{1,9},{5... | collective-permute-start | bytes 3145736 | tf_op jit(solution)/shard_map/ppermute | solution.py:92
  111.7 20.8 %collective-permute-start.13 = (bf16[256,1024]{1,0:T(8,128)(2,1)}, bf16[256,1024]{1,0:T(8,128)(2,1)S(1)}, u32[]{:S(2)}, u32[]{:S(2)}) collective-permute-start(bf16[256,1024]{1,0:T(8,128)(2,1)} %get-tuple-element.135), channel_id=1, source_target_pairs={{0,2},{1,3},{2,0},{3,1},{4,6},{5,7},{6,4},{7,5},{8,10},{9,11},{10,... | collective-permute-start | bytes 1572872 | tf_op jit(solution)/shard_map/ppermute | solution.py:87
  127.0 15.0 %collective-permute-start.23 = (bf16[256,1024]{1,0:T(8,128)(2,1)}, bf16[256,1024]{1,0:T(8,128)(2,1)S(1)}, u32[]{:S(2)}, u32[]{:S(2)}) collective-permute-start(bf16[256,1024]{1,0:T(8,128)(2,1)} %get-tuple-element.142), channel_id=1, source_target_pairs={{0,2},{1,3},{2,0},{3,1},{4,6},{5,7},{6,4},{7,5},{8,10},{9,11},{10,... | collective-permute-start | bytes 1572872 | tf_op jit(solution)/shard_map/ppermute | solution.py:87
  127.5 38.1 %collective-permute-start.19 = (bf16[256,2048]{1,0:T(8,128)(2,1)}, bf16[256,2048]{1,0:T(8,128)(2,1)}, u32[]{:S(2)}, u32[]{:S(2)}) collective-permute-start(bf16[256,2048]{1,0:T(8,128)(2,1)} %constant_dynamic-update-slice_fusion.refs_1_), channel_id=1, source_target_pairs={{0,4},{4,0},{8,12},{12,8},{16,20},{20,16},{24,28},{28,24},{1,5},{5... | collective-permute-start | bytes 3145736 | tf_op jit(solution)/shard_map/ppermute | solution.py:92
  131.0 34.7 %collective-permute-start.20 = (bf16[256,2048]{1,0:T(8,128)(2,1)S(1)}, bf16[256,2048]{1,0:T(8,128)(2,1)}, u32[]{:S(2)}, u32[]{:S(2)}) collective-permute-start(bf16[256,2048]{1,0:T(8,128)(2,1)S(1)} %collective-permute-done.14.refs_6_.refs_4_), channel_id=1, source_target_pairs={{0,2},{1,3},{2,0},{3,1},{4,6},{5,7},{6,4},{7,5},{8,10},{9,11},{10,... | collective-permute-start | bytes 3145736 | tf_op jit(solution)/shard_map/ppermute | solution.py:87
  133.1 13.3 %collective-permute-start.15 = (bf16[256,1024]{1,0:T(8,128)(2,1)S(1)}, bf16[256,1024]{1,0:T(8,128)(2,1)S(1)}, u32[]{:S(2)}, u32[]{:S(2)}) collective-permute-start(bf16[256,1024]{1,0:T(8,128)(2,1)S(1)} %get-tuple-element.137.refs_8_.refs_0_.refs_1_), channel_id=1, source_target_pairs={{0,1},{1,0},{2,3},{3,2},{4,5},{5,4},{6,7},{7,6},{8,9},{9,8},{10,11... | collective-permute-start | bytes 1572872 | tf_op jit(solution)/shard_map/ppermute | solution.py:87
  145.8 10.2 %collective-permute-start.24 = (bf16[256,1024]{1,0:T(8,128)(2,1)S(1)}, bf16[256,1024]{1,0:T(8,128)(2,1)S(1)}, u32[]{:S(2)}, u32[]{:S(2)}) collective-permute-start(bf16[256,1024]{1,0:T(8,128)(2,1)S(1)} %get-tuple-element.143.refs_0_.refs_3_), channel_id=1, source_target_pairs={{0,1},{1,0},{2,3},{3,2},{4,5},{5,4},{6,7},{7,6},{8,9},{9,8},{10,11... | collective-permute-start | bytes 1572872 | tf_op jit(solution)/shard_map/ppermute | solution.py:87
  145.8 24.4 %collective-permute-start.25 = (f32[1024]{0:T(1024)S(1)}, f32[1024]{0:T(1024)S(1)}, u32[]{:S(2)}, u32[]{:S(2)}) collective-permute-start(f32[1024]{0:T(1024)S(1)} %copy-done.82), channel_id=1, source_target_pairs={{0,2},{1,3},{2,0},{3,1},{4,6},{5,7},{6,4},{7,5},{8,10},{9,11},{10,... | collective-permute-start | bytes 12296 | tf_op jit(solution)/shard_map/ppermute | solution.py:87
  180.4 10.9 %collective-permute-start.26 = (bf16[256,1024]{1,0:T(8,128)(2,1)}, bf16[256,1024]{1,0:T(8,128)(2,1)S(1)}, u32[]{:S(2)}, u32[]{:S(2)}) collective-permute-start(bf16[256,1024]{1,0:T(8,128)(2,1)} %get-tuple-element.147), channel_id=1, source_target_pairs={{0,1},{1,0},{2,3},{3,2},{4,5},{5,4},{6,7},{7,6},{8,9},{9,8},{10,11... | collective-permute-start | bytes 1572872 | tf_op jit(solution)/shard_map/ppermute | solution.py:87
  190.9 2.7 collective-permute-start.27
  193.1 3.4 collective-permute-start.28
  196.3 12.9 %collective-permute-start.30 = (bf16[256,1024]{1,0:T(8,128)(2,1)S(1)}, bf16[256,1024]{1,0:T(8,128)(2,1)S(1)}, u32[]{:S(2)}, u32[]{:S(2)}) collective-permute-start(bf16[256,1024]{1,0:T(8,128)(2,1)S(1)} %get-tuple-element.160.refs_3_.refs_0_), channel_id=1, source_target_pairs={{0,1},{1,0},{2,3},{3,2},{4,5},{5,4},{6,7},{7,6},{8,9},{9,8},{10,11... | collective-permute-start | bytes 1572872 | tf_op jit(solution)/shard_map/ppermute | solution.py:87
  208.8 22.9 %collective-permute-start.29 = (bf16[256,1024]{1,0:T(8,128)(2,1)}, bf16[256,1024]{1,0:T(8,128)(2,1)S(1)}, u32[]{:S(2)}, u32[]{:S(2)}) collective-permute-start(bf16[256,1024]{1,0:T(8,128)(2,1)} %get-tuple-element.159), channel_id=1, source_target_pairs={{0,1},{1,0},{2,3},{3,2},{4,5},{5,4},{6,7},{7,6},{8,9},{9,8},{10,11... | collective-permute-start | bytes 1572872 | tf_op jit(solution)/shard_map/ppermute | solution.py:87
  231.5 19.8 %collective-permute-start.33 = (bf16[256,1024]{1,0:T(8,128)(2,1)}, bf16[256,1024]{1,0:T(8,128)(2,1)S(1)}, u32[]{:S(2)}, u32[]{:S(2)}) collective-permute-start(bf16[256,1024]{1,0:T(8,128)(2,1)} %get-tuple-element.181), channel_id=1, source_target_pairs={{0,1},{1,0},{2,3},{3,2},{4,5},{5,4},{6,7},{7,6},{8,9},{9,8},{10,11... | collective-permute-start | bytes 1572872 | tf_op jit(solution)/shard_map/ppermute | solution.py:87
  234.8 21.3 %collective-permute-start.31 = (bf16[256,1024]{1,0:T(8,128)(2,1)S(1)}, bf16[256,1024]{1,0:T(8,128)(2,1)}, u32[]{:S(2)}, u32[]{:S(2)}) collective-permute-start(bf16[256,1024]{1,0:T(8,128)(2,1)S(1)} %get-tuple-element.170.refs_9_.refs_4_.refs_1_), channel_id=1, source_target_pairs={{0,2},{1,3},{2,0},{3,1},{4,6},{5,7},{6,4},{7,5},{8,10},{9,11},{10,... | collective-permute-start | bytes 1572872 | tf_op jit(solution)/shard_map/ppermute | solution.py:87
  238.4 48.4 %collective-permute-start.35 = (bf16[2,512,1024]{2,1,0:T(8,128)(2,1)}, bf16[2,512,1024]{2,1,0:T(8,128)(2,1)}, u32[]{:S(2)}, u32[]{:S(2)}) collective-permute-start(bf16[2,512,1024]{2,1,0:T(8,128)(2,1)} %get-tuple-element.167.refs_8_), channel_id=1, source_target_pairs={{0,4},{4,0},{8,12},{12,8},{16,20},{20,16},{24,28},{28,24},{1,5},{5... | collective-permute-start | bytes 6291464 | tf_op jit(solution)/shard_map/ppermute | solution.py:92
  251.0 70.6 %collective-permute-start.37 = (bf16[2,512,1024]{2,1,0:T(8,128)(2,1)}, bf16[2,512,1024]{2,1,0:T(8,128)(2,1)S(1)}, u32[]{:S(2)}, u32[]{:S(2)}) collective-permute-start(bf16[2,512,1024]{2,1,0:T(8,128)(2,1)} %get-tuple-element.175.refs_8_.refs_5_), channel_id=1, source_target_pairs={{0,8},{4,12},{8,0},{12,4},{16,24},{20,28},{24,16},{28,20},{1,9},{5... | collective-permute-start | bytes 6291464 | tf_op jit(solution)/shard_map/ppermute | solution.py:92
  255.6 26.8 %collective-permute-start.34 = (bf16[256,1024]{1,0:T(8,128)(2,1)}, bf16[256,1024]{1,0:T(8,128)(2,1)}, u32[]{:S(2)}, u32[]{:S(2)}) collective-permute-start(bf16[256,1024]{1,0:T(8,128)(2,1)} %get-tuple-element.182.refs_3_.refs_4_), channel_id=1, source_target_pairs={{0,2},{1,3},{2,0},{3,1},{4,6},{5,7},{6,4},{7,5},{8,10},{9,11},{10,... | collective-permute-start | bytes 1572872 | tf_op jit(solution)/shard_map/ppermute | solution.py:87
  282.4 44.1 %collective-permute-start.32 = (bf16[512,1024]{1,0:T(8,128)(2,1)}, bf16[512,1024]{1,0:T(8,128)(2,1)S(1)}, u32[]{:S(2)}, u32[]{:S(2)}) collective-permute-start(bf16[512,1024]{1,0:T(8,128)(2,1)} %get-tuple-element.178), channel_id=1, source_target_pairs={{0,1},{1,0},{2,3},{3,2},{4,5},{5,4},{6,7},{7,6},{8,9},{9,8},{10,11... | collective-permute-start | bytes 3145736 | tf_op jit(solution)/shard_map/ppermute | solution.py:87
  319.2 6.6 %collective-permute-start.36 = (f32[96,128]{1,0:T(8,128)S(1)}, f32[96,128]{1,0:T(8,128)S(1)}, u32[]{:S(2)}, u32[]{:S(2)}) collective-permute-start(f32[96,128]{1,0:T(8,128)S(1)} %bitcast.108), channel_id=1, source_target_pairs={{0,1},{1,0},{2,3},{3,2},{4,5},{5,4},{6,7},{7,6},{8,9},{9,8},{10,11... | collective-permute-start | bytes 147464 | tf_op jit(solution)/shard_map/ppermute | solution.py:87
  319.8 24.5 %collective-permute-start.39 = (bf16[512,1024]{1,0:T(8,128)(2,1)}, bf16[512,1024]{1,0:T(8,128)(2,1)}, u32[]{:S(2)}, u32[]{:S(2)}) collective-permute-start(bf16[512,1024]{1,0:T(8,128)(2,1)} %get-tuple-element.208), channel_id=1, source_target_pairs={{0,1},{1,0},{2,3},{3,2},{4,5},{5,4},{6,7},{7,6},{8,9},{9,8},{10,11... | collective-permute-start | bytes 3145736 | tf_op jit(solution)/shard_map/ppermute | solution.py:87
  319.8 32.3 %collective-permute-start.45 = (bf16[2,256,1024]{2,1,0:T(8,128)(2,1)}, bf16[2,256,1024]{2,1,0:T(8,128)(2,1)S(1)}, u32[]{:S(2)}, u32[]{:S(2)}) collective-permute-start(bf16[2,256,1024]{2,1,0:T(8,128)(2,1)} %get-tuple-element.220), channel_id=1, source_target_pairs={{0,8},{4,12},{8,0},{12,4},{16,24},{20,28},{24,16},{28,20},{1,9},{5... | collective-permute-start | bytes 3145736 | tf_op jit(solution)/shard_map/ppermute | solution.py:92
  334.1 24.9 %collective-permute-start.42 = (bf16[2,1024,256]{2,1,0:T(8,128)(2,1)}, bf16[2,1024,256]{2,1,0:T(8,128)(2,1)}, u32[]{:S(2)}, u32[]{:S(2)}) collective-permute-start(bf16[2,1024,256]{2,1,0:T(8,128)(2,1)} %pad_maximum_fusion.3), channel_id=1, source_target_pairs={{0,1},{1,0},{2,3},{3,2},{4,5},{5,4},{6,7},{7,6},{8,9},{9,8},{10,11... | collective-permute-start | bytes 3145736 | tf_op jit(solution)/shard_map/ppermute | solution.py:87
  334.2 27.2 %collective-permute-start.44 = (bf16[2,256,1024]{2,1,0:T(8,128)(2,1)}, bf16[2,256,1024]{2,1,0:T(8,128)(2,1)S(1)}, u32[]{:S(2)}, u32[]{:S(2)}) collective-permute-start(bf16[2,256,1024]{2,1,0:T(8,128)(2,1)} %get-tuple-element.219), channel_id=1, source_target_pairs={{0,4},{4,0},{8,12},{12,8},{16,20},{20,16},{24,28},{28,24},{1,5},{5... | collective-permute-start | bytes 3145736 | tf_op jit(solution)/shard_map/ppermute | solution.py:92
  334.8 7.8 %collective-permute-start.40 = (f32[96,128]{1,0:T(8,128)S(1)}, f32[96,128]{1,0:T(8,128)S(1)}, u32[]{:S(2)}, u32[]{:S(2)}) collective-permute-start(f32[96,128]{1,0:T(8,128)S(1)} %copy-done.52), channel_id=1, source_target_pairs={{0,2},{1,3},{2,0},{3,1},{4,6},{5,7},{6,4},{7,5},{8,10},{9,11},{10,... | collective-permute-start | bytes 147464 | tf_op jit(solution)/shard_map/ppermute | solution.py:87
  342.5 20.0 %collective-permute-start.38 = (bf16[256,1024]{1,0:T(8,128)(2,1)}, bf16[256,1024]{1,0:T(8,128)(2,1)}, u32[]{:S(2)}, u32[]{:S(2)}) collective-permute-start(bf16[256,1024]{1,0:T(8,128)(2,1)} %get-tuple-element.205), channel_id=1, source_target_pairs={{0,2},{1,3},{2,0},{3,1},{4,6},{5,7},{6,4},{7,5},{8,10},{9,11},{10,... | collective-permute-start | bytes 1572872 | tf_op jit(solution)/shard_map/ppermute | solution.py:87
  344.3 13.0 %collective-permute-start.46 = (f32[96,128]{1,0:T(8,128)S(1)}, f32[96,128]{1,0:T(8,128)S(1)}, u32[]{:S(2)}, u32[]{:S(2)}) collective-permute-start(f32[96,128]{1,0:T(8,128)S(1)} %plus.6.refs_5_.refs_0_), channel_id=1, source_target_pairs={{0,16},{4,20},{8,24},{12,28},{16,0},{20,4},{24,8},{28,12},{1,17},{... | collective-permute-start | bytes 147464 | tf_op jit(solution)/shard_map/ppermute | solution.py:92
  353.1 22.2 %collective-permute-start.41 = (bf16[256,1024]{1,0:T(8,128)(2,1)}, bf16[256,1024]{1,0:T(8,128)(2,1)S(1)}, u32[]{:S(2)}, u32[]{:S(2)}) collective-permute-start(bf16[256,1024]{1,0:T(8,128)(2,1)} %get-tuple-element.210), channel_id=1, source_target_pairs={{0,2},{1,3},{2,0},{3,1},{4,6},{5,7},{6,4},{7,5},{8,10},{9,11},{10,... | collective-permute-start | bytes 1572872 | tf_op jit(solution)/shard_map/ppermute | solution.py:87
  357.3 37.2 %collective-permute-start.48 = (bf16[2,128,1024]{2,1,0:T(8,128)(2,1)S(1)}, bf16[2,128,1024]{2,1,0:T(8,128)(2,1)S(1)}, u32[]{:S(2)}, u32[]{:S(2)}) collective-permute-start(bf16[2,128,1024]{2,1,0:T(8,128)(2,1)S(1)} %get-tuple-element.225), channel_id=1, source_target_pairs={{0,16},{4,20},{8,24},{12,28},{16,0},{20,4},{24,8},{28,12},{1,17},{... | collective-permute-start | bytes 1572872 | tf_op jit(solution)/shard_map/ppermute | solution.py:92
  372.2 22.3 %collective-permute-start.47 = (bf16[1024,256]{1,0:T(8,128)(2,1)}, bf16[1024,256]{1,0:T(8,128)(2,1)S(1)}, u32[]{:S(2)}, u32[]{:S(2)}) collective-permute-start(bf16[1024,256]{1,0:T(8,128)(2,1)} %get-tuple-element.224), channel_id=1, source_target_pairs={{0,1},{1,0},{2,3},{3,2},{4,5},{5,4},{6,7},{7,6},{8,9},{9,8},{10,11... | collective-permute-start | bytes 1572872 | tf_op jit(solution)/shard_map/ppermute | solution.py:87
  372.3 22.4 %collective-permute-start.49 = (bf16[1024,256]{1,0:T(8,128)(2,1)}, bf16[1024,256]{1,0:T(8,128)(2,1)S(1)}, u32[]{:S(2)}, u32[]{:S(2)}) collective-permute-start(bf16[1024,256]{1,0:T(8,128)(2,1)} %get-tuple-element.228), channel_id=1, source_target_pairs={{0,1},{1,0},{2,3},{3,2},{4,5},{5,4},{6,7},{7,6},{8,9},{9,8},{10,11... | collective-permute-start | bytes 1572872 | tf_op jit(solution)/shard_map/ppermute | solution.py:87
  372.8 22.0 %collective-permute-start.43 = (bf16[2,512,256]{2,1,0:T(8,128)(2,1)S(1)}, bf16[2,512,256]{2,1,0:T(8,128)(2,1)S(1)}, u32[]{:S(2)}, u32[]{:S(2)}) collective-permute-start(bf16[2,512,256]{2,1,0:T(8,128)(2,1)S(1)} %get-tuple-element.214), channel_id=1, source_target_pairs={{0,4},{4,0},{8,12},{12,8},{16,20},{20,16},{24,28},{28,24},{1,5},{5... | collective-permute-start | bytes 1572872 | tf_op jit(solution)/shard_map/ppermute | solution.py:92
  375.4 45.2 %collective-permute-start.58 = (bf16[2,128,1024]{2,1,0:T(8,128)(2,1)S(1)}, bf16[2,128,1024]{2,1,0:T(8,128)(2,1)S(1)}, u32[]{:S(2)}, u32[]{:S(2)}) collective-permute-start(bf16[2,128,1024]{2,1,0:T(8,128)(2,1)S(1)} %get-tuple-element.244), channel_id=1, source_target_pairs={{0,16},{4,20},{8,24},{12,28},{16,0},{20,4},{24,8},{28,12},{1,17},{... | collective-permute-start | bytes 1572872 | tf_op jit(solution)/shard_map/ppermute | solution.py:92
  394.6 26.8 %collective-permute-start.61 = (f32[96,128]{1,0:T(8,128)S(1)}, f32[96,128]{1,0:T(8,128)S(1)}, u32[]{:S(2)}, u32[]{:S(2)}) collective-permute-start(f32[96,128]{1,0:T(8,128)S(1)} %copy-done.50), channel_id=1, source_target_pairs={{0,8},{4,12},{8,0},{12,4},{16,24},{20,28},{24,16},{28,20},{1,9},{5... | collective-permute-start | bytes 147464 | tf_op jit(solution)/shard_map/ppermute | solution.py:92
  395.9 21.2 %collective-permute-start.50 = (bf16[2,256,256]{2,1,0:T(8,128)(2,1)S(1)}, bf16[2,256,256]{2,1,0:T(8,128)(2,1)S(1)}, u32[]{:S(2)}, u32[]{:S(2)}) collective-permute-start(bf16[2,256,256]{2,1,0:T(8,128)(2,1)S(1)} %get-tuple-element.231), channel_id=1, source_target_pairs={{0,8},{4,12},{8,0},{12,4},{16,24},{20,28},{24,16},{28,20},{1,9},{5... | collective-permute-start | bytes 786440 | tf_op jit(solution)/shard_map/ppermute | solution.py:92
  398.0 6.4 %collective-permute-start.51 = (bf16[1,512,256]{2,1,0:T(8,128)(2,1)S(1)}, bf16[1,512,256]{2,1,0:T(8,128)(2,1)S(1)}, u32[]{:S(2)}, u32[]{:S(2)}) collective-permute-start(bf16[1,512,256]{2,1,0:T(8,128)(2,1)S(1)} %get-tuple-element.232), channel_id=1, source_target_pairs={{0,4},{4,0},{8,12},{12,8},{16,20},{20,16},{24,28},{28,24},{1,5},{5... | collective-permute-start | bytes 786440 | tf_op jit(solution)/shard_map/ppermute | solution.py:92
  398.5 18.6 %collective-permute-start.52 = (bf16[1,512,256]{2,1,0:T(8,128)(2,1)S(1)}, bf16[1,512,256]{2,1,0:T(8,128)(2,1)S(1)}, u32[]{:S(2)}, u32[]{:S(2)}) collective-permute-start(bf16[1,512,256]{2,1,0:T(8,128)(2,1)S(1)} %get-tuple-element.234), channel_id=1, source_target_pairs={{0,8},{4,12},{8,0},{12,4},{16,24},{20,28},{24,16},{28,20},{1,9},{5... | collective-permute-start | bytes 786440 | tf_op jit(solution)/shard_map/ppermute | solution.py:92
  417.2 14.2 %collective-permute-start.53 = (bf16[2,128,256]{2,1,0:T(8,128)(2,1)S(1)}, bf16[2,128,256]{2,1,0:T(8,128)(2,1)S(1)}, u32[]{:S(2)}, u32[]{:S(2)}) collective-permute-start(bf16[2,128,256]{2,1,0:T(8,128)(2,1)S(1)} %get-tuple-element.237), channel_id=1, source_target_pairs={{0,16},{4,20},{8,24},{12,28},{16,0},{20,4},{24,8},{28,12},{1,17},{... | collective-permute-start | bytes 393224 | tf_op jit(solution)/shard_map/ppermute | solution.py:92
  417.2 11.0 %collective-permute-start.54 = (bf16[1,256,256]{2,1,0:T(8,128)(2,1)S(1)}, bf16[1,256,256]{2,1,0:T(8,128)(2,1)S(1)}, u32[]{:S(2)}, u32[]{:S(2)}) collective-permute-start(bf16[1,256,256]{2,1,0:T(8,128)(2,1)S(1)} %get-tuple-element.238), channel_id=1, source_target_pairs={{0,8},{4,12},{8,0},{12,4},{16,24},{20,28},{24,16},{28,20},{1,9},{5... | collective-permute-start | bytes 393224 | tf_op jit(solution)/shard_map/ppermute | solution.py:92
  419.6 9.8 %collective-permute-start.56 = (bf16[1,256,256]{2,1,0:T(8,128)(2,1)S(1)}, bf16[1,256,256]{2,1,0:T(8,128)(2,1)S(1)}, u32[]{:S(2)}, u32[]{:S(2)}) collective-permute-start(bf16[1,256,256]{2,1,0:T(8,128)(2,1)S(1)} %get-tuple-element.241), channel_id=1, source_target_pairs={{0,4},{4,0},{8,12},{12,8},{16,20},{20,16},{24,28},{28,24},{1,5},{5... | collective-permute-start | bytes 393224 | tf_op jit(solution)/shard_map/ppermute | solution.py:92
  420.8 15.9 %collective-permute-start.59 = (bf16[128,1024]{1,0:T(8,128)(2,1)S(1)}, bf16[128,1024]{1,0:T(8,128)(2,1)S(1)}, u32[]{:S(2)}, u32[]{:S(2)}) collective-permute-start(bf16[128,1024]{1,0:T(8,128)(2,1)S(1)} %fusion.5), channel_id=1, source_target_pairs={{0,2},{1,3},{2,0},{3,1},{4,6},{5,7},{6,4},{7,5},{8,10},{9,11},{10,... | collective-permute-start | bytes 786440 | tf_op jit(solution)/shard_map/ppermute | solution.py:87
  421.3 4.2 collective-permute-start.62
  425.5 10.1 %collective-permute-start.60 = (bf16[128,1024]{1,0:T(8,128)(2,1)}, bf16[128,1024]{1,0:T(8,128)(2,1)S(1)}, u32[]{:S(2)}, u32[]{:S(2)}) collective-permute-start(bf16[128,1024]{1,0:T(8,128)(2,1)} %fusion.6), channel_id=1, source_target_pairs={{0,2},{1,3},{2,0},{3,1},{4,6},{5,7},{6,4},{7,5},{8,10},{9,11},{10,... | collective-permute-start | bytes 786440 | tf_op jit(solution)/shard_map/ppermute | solution.py:87
  428.3 5.9 %collective-permute-start.55 = (bf16[1,128,256]{2,1,0:T(8,128)(2,1)S(1)}, bf16[1,128,256]{2,1,0:T(8,128)(2,1)S(1)}, u32[]{:S(2)}, u32[]{:S(2)}) collective-permute-start(bf16[1,128,256]{2,1,0:T(8,128)(2,1)S(1)} %get-tuple-element.240), channel_id=1, source_target_pairs={{0,16},{4,20},{8,24},{12,28},{16,0},{20,4},{24,8},{28,12},{1,17},{... | collective-permute-start | bytes 196616 | tf_op jit(solution)/shard_map/ppermute | solution.py:92
  429.4 5.5 %collective-permute-start.57 = (bf16[1,128,256]{2,1,0:T(8,128)(2,1)S(1)}, bf16[1,128,256]{2,1,0:T(8,128)(2,1)S(1)}, u32[]{:S(2)}, u32[]{:S(2)}) collective-permute-start(bf16[1,128,256]{2,1,0:T(8,128)(2,1)S(1)} %get-tuple-element.243), channel_id=1, source_target_pairs={{0,16},{4,20},{8,24},{12,28},{16,0},{20,4},{24,8},{28,12},{1,17},{... | collective-permute-start | bytes 196616 | tf_op jit(solution)/shard_map/ppermute | solution.py:92
  (90 other events, 600.7 us)

commit v10 on v9

--- a/solution.py
+++ b/solution.py
@@ -985,19 +985,19 @@
     )
     key_value_made = weight_grad(
         tokens, [back[s][0] for s in seqs], [back[s][1] for s in seqs],
-        dp_place, [(head_dims, near_first), (head_dims, far_first)], "w_key_value_grad",
+        dp_place, [(head_dims, near_first), (head_dims, near_first)], "w_key_value_grad",
         deps=input_got[:1] + [up_chain.keep, query_chain.keep, small],
     )
     waits = input_got[-1:] + [down_chain.came]
     key_chain = core_chain([key_value_made[:2]], near_first, waits)
-    value_chain = core_chain([key_value_made[2:]], far_first, waits)
+    value_chain = core_chain([key_value_made[2:]], near_first, waits)
     started = [key_chain.keep, value_chain.keep]
+    down_chain.fold(started)
     query_chain.fold(started)
     key_chain.fold()
     value_chain.fold()
     ending = [key_chain.keep, value_chain.keep]
     query_chain.fold(ending)
-    down_chain.fold(ending)
     up_chain.fold(ending)
     for bit in bits[1:]:
         small = plus(small, swap_dp(small, bit), ending)

time: 443 us -> 434 us (0.980)
  waiting for transfers between devices: 82.2 us -> 77.2 us
    ppermute x29, waiting for transfers between devices: 68 us -> 63.1 us  [swap_dp(): return lax.ppermute(array, 'dp', [(i, i ^ bit) for i in range(size)])]
    unnamed x195 -> x193, local copies, waits for them, and re-layouts: 43.2 us -> 39.3 us
  transfers between devices with their start and end apart: 63 -> 63, of which waited for: 14 -> 16; matrix products, arithmetic and copies ran while one was open for 7% -> 7% of each run, Pallas kernels for 50% -> 51%
where the time goes in v10:
time: 434 us; the launch traced here: 429 us
  Pallas kernels  232 us (53%)
  waiting for transfers between devices  77.2 us (18%)
  starting transfers between devices  54.5 us (13%)
  local copies, waits for them, and re-layouts  50.9 us (12%)
  other arithmetic  12.4 us (3%)
    pallas_call x40, Pallas kernels, whole_call(): pl.pallas_call(after(kernel, len(args), deps), out_shape=tuple(outs), in_...  118 us
    pallas_call x11, Pallas kernels, streamed_call(): pl.pallas_call(after(kernel, len(args), deps), grid=grid, out_shape=tuple...  98.9 us
    ppermute x29, waiting for transfers between devices, swap_dp(): return lax.ppermute(array, 'dp', [(i, i ^ bit) for i in range(size)])  63.1 us
    unnamed x193, local copies, waits for them, and re-layouts  39.3 us
    ppermute x29, starting transfers between devices, swap_dp(): return lax.ppermute(array, 'dp', [(i, i ^ bit) for i in range(size)])  36.6 us
    ppermute x34, starting transfers between devices, swap_tensor(): return lax.ppermute(array, 'tensor', [(i, i ^ bit) for i in range(size)])  17.9 us
    pallas_call x4, Pallas kernels, assemble(): pl.pallas_call(after(kernel, 1 + len(arrays), deps), out_shape=out, in_sp...  15.1 us
    ppermute x34, waiting for transfers between devices, swap_tensor(): return lax.ppermute(array, 'tensor', [(i, i ^ bit) for i in range(size)])  14 us
  transfers between devices with their start and end apart: 63, of which 16 were waited for; matrix products, arithmetic and copies ran while one was open for 7% of the time, Pallas kernels for 51%

profile of v10, /device:TPU:0, one launch (start us, length us, event | category | flops | bytes accessed | tf_op | source)
XLA Modules:
  0.0 428.8 jit_solution(7462747964823638201)
XLA Ops:
  0.7 1.7 copy.39
  2.3 1.7 pack_attention.1
  4.0 4.0 collective-permute-start.1
  8.0 1.8 copy.40
  9.8 10.3 %collective-permute-done.1.refs_2_ = bf16[128,1024]{1,0:T(8,128)(2,1)S(1)} collective-permute-done((bf16[128,1024]{1,0:T(8,128)(2,1)}, bf16[128,1024]{1,0:T(8,128)(2,1)S(1)}, u32[]{:S(2)}, u32[]{:S(2)}) %collective-permute-start.1) | collective-permute-done | bytes 262176 | tf_op jit(solution)/shard_map/ppermute | solution.py:92
  22.2 1.9 pack_feed.1
  24.0 3.3 collective-permute-start.10
  28.8 1.5 collective-permute-start
  31.7 11.7 %collective-permute-done.2.refs_2_ = bf16[256,1024]{1,0:T(8,128)(2,1)S(1)} collective-permute-done((bf16[256,1024]{1,0:T(8,128)(2,1)S(1)}, bf16[256,1024]{1,0:T(8,128)(2,1)S(1)}, u32[]{:S(2)}, u32[]{:S(2)}) %collective-permute-start.2) | collective-permute-done | bytes 524320 | tf_op jit(solution)/shard_map/ppermute | solution.py:92
  44.7 5.9 %collective-permute-done.10.refs_6_ = bf16[128,2048]{1,0:T(8,128)(2,1)S(1)} collective-permute-done((bf16[128,2048]{1,0:T(8,128)(2,1)}, bf16[128,2048]{1,0:T(8,128)(2,1)S(1)}, u32[]{:S(2)}, u32[]{:S(2)}) %collective-permute-start.10) | collective-permute-done | bytes 524320 | tf_op jit(solution)/shard_map/ppermute | solution.py:92
  52.1 2.1 pad_maximum_fusion.refs_1_
  54.8 9.6 %collective-permute-done.16.refs_6_ = bf16[128,2048]{1,0:T(8,128)(2,1)} collective-permute-done((bf16[128,2048]{1,0:T(8,128)(2,1)}, bf16[128,2048]{1,0:T(8,128)(2,1)}, u32[]{:S(2)}, u32[]{:S(2)}) %collective-permute-start.16) | collective-permute-done | bytes 524320 | tf_op jit(solution)/shard_map/ppermute | solution.py:87
  66.8 2.2 slice_bitcast_fusion.5
  69.1 2.9 assemble_attention.1.refs_2_.refs_4_.refs_6_.refs_3_
  73.7 3.0 assemble_attention_other.1.refs_3_.refs_5_.refs_7_.refs_4_
  76.7 5.6 %project_inputs.2 = (bf16[512,768]{1,0:T(8,128)(2,1)}, bf16[512,768]{1,0:T(8,128)(2,1)}, bf16[512,1024]{1,0:T(8,128)(2,1)}) custom-call(bf16[256,1024]{1,0:T(8,128)(2,1)} %get-tuple-element.285.refs_0_.refs_1_, bf16[256,1024]{1,0:T(8,128)(2,1)} %get-tuple-element.283.refs_1_.refs_2_, bf16[1024,1024]{1,0:T(8,128)(2,1)} %assemble_attention.1.refs_2_.refs_4_.refs_6_.refs_3_, ...), custom_call_target="tpu_custom_call" | custom-call | flops 1610612 | bytes 7870 | tf_op jit(solution)/shard_map/project_inputs/pallas_call | solution.py:47
  82.9 5.6 %project_inputs.3 = (bf16[512,768]{1,0:T(8,128)(2,1)}, bf16[512,768]{1,0:T(8,128)(2,1)}, bf16[512,1024]{1,0:T(8,128)(2,1)}) custom-call(bf16[256,1024]{1,0:T(8,128)(2,1)} %get-tuple-element.286.refs_0_.refs_3_, bf16[256,1024]{1,0:T(8,128)(2,1)} %get-tuple-element.284.refs_1_.refs_4_, bf16[1024,1024]{1,0:T(8,128)(2,1)} %assemble_attention.1.refs_2_.refs_4_.refs_6_.refs_3_, ...), custom_call_target="tpu_custom_call" | custom-call | flops 1610612 | bytes 7870 | tf_op jit(solution)/shard_map/project_inputs/pallas_call | solution.py:47
  90.2 1.9 constant_dynamic-update-slice_fusion.1
  97.8 12.9 %attention_forward.2 = (bf16[512,256]{1,0:T(8,128)(2,1)}, bf16[512,256]{1,0:T(8,128)(2,1)}, f32[256,1024]{1,0:T(8,128)}, bf16[256,1024]{1,0:T(8,128)(2,1)}) custom-call(bf16[512,768]{1,0:T(8,128)(2,1)} %get-tuple-element.131.refs_0_, bf16[512,768]{1,0:T(8,128)(2,1)} %get-tuple-element.132.refs_1_, bf16[512,1024]{1,0:T(8,128)(2,1)} %collective-permute-done.11.refs_2_, ...), custom_call_target="tpu_custom_call" | custom-call | flops 8589934 | bytes 8916 | tf_op jit(solution)/shard_map/attention_forward/pallas_call | solution.py:47
  110.7 1.5 collective-permute-start.13
  113.2 12.8 %attention_forward.3 = (bf16[512,256]{1,0:T(8,128)(2,1)}, bf16[512,256]{1,0:T(8,128)(2,1)}, f32[256,1024]{1,0:T(8,128)}, bf16[256,1024]{1,0:T(8,128)(2,1)}) custom-call(bf16[512,768]{1,0:T(8,128)(2,1)} %get-tuple-element.138.refs_0_, bf16[512,768]{1,0:T(8,128)(2,1)} %get-tuple-element.139.refs_1_, bf16[512,1024]{1,0:T(8,128)(2,1)} %collective-permute-done.21.refs_2_, ...), custom_call_target="tpu_custom_call" | custom-call | flops 8589934 | bytes 8916 | tf_op jit(solution)/shard_map/attention_forward/pallas_call | solution.py:47
  128.0 2.9 collective-permute-done.14.refs_6_.refs_4_
  131.0 1.5 collective-permute-start.20
  133.2 4.7 %assemble_feed.1.refs_7_.refs_2_.refs_3_.refs_4_ = bf16[1024,2048]{1,0:T(8,128)(2,1)} custom-call(s32[1]{0:T(128)} %bitcast.2.refs_0_, bf16[256,2048]{1,0:T(8,128)(2,1)} %pad_maximum_fusion.refs_1_, bf16[256,2048]{1,0:T(8,128)(2,1)} %collective-permute-done.12.refs_6_.refs_2_, bf16[256,2048]{1,0:T(8,128)(2,1)} %copy-done.63, bf16[256,2048]{1,0:T(8,128)(2,1)} %copy-done.7), custom_call_target="tpu_custom_call" | custom-call | bytes 8388 | tf_op jit(solution)/shard_map/assemble_feed/pallas_call | solution.py:154
  137.8 3.2 collective-permute-done.23.refs_2_
  141.1 2.2 copy-done
  146.2 8.8 %feed_forward.4 = (bf16[512,1024]{1,0:T(8,128)(2,1)}, bf16[512,1024]{1,0:T(8,128)(2,1)}, f32[512,1024]{1,0:T(8,128)}) custom-call(bf16[256,1024]{1,0:T(8,128)(2,1)} %copy-done.5, bf16[256,1024]{1,0:T(8,128)(2,1)} %copy-done.61, bf16[1024,2048]{1,0:T(8,128)(2,1)} %assemble_feed.1.refs_7_.refs_2_.refs_3_.refs_4_, ...), custom_call_target="tpu_custom_call" | custom-call | flops 2147483 | bytes 13635 | tf_op jit(solution)/shard_map/feed_forward/pallas_call | solution.py:64
  155.8 8.9 %feed_forward.5 = (bf16[512,1024]{1,0:T(8,128)(2,1)}, bf16[512,1024]{1,0:T(8,128)(2,1)}, f32[512,1024]{1,0:T(8,128)}) custom-call(bf16[256,1024]{1,0:T(8,128)(2,1)} %copy-done.6, bf16[256,1024]{1,0:T(8,128)(2,1)} %copy-done.62, bf16[1024,2048]{1,0:T(8,128)(2,1)} %assemble_feed.1.refs_7_.refs_2_.refs_3_.refs_4_, ...), custom_call_target="tpu_custom_call" | custom-call | flops 2147483 | bytes 13635 | tf_op jit(solution)/shard_map/feed_forward/pallas_call | solution.py:64
  164.7 4.5 %assemble_feed_other.1.refs_2_.refs_3_.refs_5_ = bf16[1024,2048]{1,0:T(8,128)(2,1)} custom-call(s32[1]{0:T(128)} %bitcast.2.refs_0_, bf16[256,2048]{1,0:T(8,128)(2,1)} %constant_dynamic-update-slice_fusion.refs_1_, bf16[256,2048]{1,0:T(8,128)(2,1)} %collective-permute-done.18.refs_6_.refs_2_, bf16[256,2048]{1,0:T(8,128)(2,1)} %collective-permute-done.19.refs_3_, ...), custom_call_target="tpu_custom_call" | custom-call | bytes 8388 | tf_op jit(solution)/shard_map/assemble_feed_other/pallas_call | solution.py:154
  169.8 9.7 %feed_forward.6 = (bf16[512,1024]{1,0:T(8,128)(2,1)}, bf16[512,1024]{1,0:T(8,128)(2,1)}, f32[256,1024]{1,0:T(8,128)}, bf16[256,1024]{1,0:T(8,128)(2,1)}) custom-call(bf16[256,1024]{1,0:T(8,128)(2,1)} %copy-done.5, bf16[256,1024]{1,0:T(8,128)(2,1)} %copy-done.61, bf16[1024,2048]{1,0:T(8,128)(2,1)} %assemble_feed_other.1.refs_2_.refs_3_.refs_5_, ...), custom_call_target="tpu_custom_call" | custom-call | flops 2147483 | bytes 15208 | tf_op jit(solution)/shard_map/feed_forward/pallas_call | solution.py:64
  179.7 10.1 %feed_forward.7 = (bf16[512,1024]{1,0:T(8,128)(2,1)}, bf16[512,1024]{1,0:T(8,128)(2,1)}, f32[256,1024]{1,0:T(8,128)}, bf16[256,1024]{1,0:T(8,128)(2,1)}) custom-call(bf16[256,1024]{1,0:T(8,128)(2,1)} %copy-done.6, bf16[256,1024]{1,0:T(8,128)(2,1)} %copy-done.62, bf16[1024,2048]{1,0:T(8,128)(2,1)} %assemble_feed_other.1.refs_2_.refs_3_.refs_5_, ...), custom_call_target="tpu_custom_call" | custom-call | flops 2147483 | bytes 15208 | tf_op jit(solution)/shard_map/feed_forward/pallas_call | solution.py:64
  196.4 11.4 %feed_forward_back.2 = (bf16[512,1024]{1,0:T(8,128)(2,1)}, bf16[512,1024]{1,0:T(8,128)(2,1)}, f32[256,1024]{1,0:T(8,128)}, bf16[256,1024]{1,0:T(8,128)(2,1)}, f32[1,1024]{1,0:T(1,128)}, /*index=5*/f32[1,1024]{1,0:T(1,128)}) custom-call(bf16[256,1024]{1,0:T(8,128)(2,1)} %copy-done.24, bf16[256,1024]{1,0:T(8,128)(2,1)} %copy-done.67, ...), custom_call_target="tpu_custom_call" | custom-call | flops 4294967 | bytes 23601 | tf_op jit(solution)/shard_map/feed_forward_back/pallas_call | solution.py:64
  209.0 9.9 %w_down_grad.1 = (f32[2,512,1024]{2,1,0:T(8,128)}, bf16[2,512,1024]{2,1,0:T(8,128)(2,1)}) custom-call(s32[1]{0:T(128)} %bitcast.2.refs_0_, bf16[256,1024]{1,0:T(8,128)(2,1)} %copy-done.24, bf16[256,1024]{1,0:T(8,128)(2,1)} %copy-done.67, bf16[256,1024]{1,0:T(8,128)(2,1)} %copy-done.25, bf16[256,1024]{1,0:T(8,128)(2,1)} %copy-done.68, ...), custom_call_target="tpu_custom_call" | custom-call | flops 4294967 | bytes 12582 | tf_op jit(solution)/shard_map/w_down_grad/pallas_call | solution.py:64
  219.0 11.4 %feed_forward_back.3 = (bf16[512,1024]{1,0:T(8,128)(2,1)}, bf16[512,1024]{1,0:T(8,128)(2,1)}, f32[256,1024]{1,0:T(8,128)}, bf16[256,1024]{1,0:T(8,128)(2,1)}, f32[1,1024]{1,0:T(1,128)}, /*index=5*/f32[1,1024]{1,0:T(1,128)}) custom-call(bf16[256,1024]{1,0:T(8,128)(2,1)} %copy-done.25, bf16[256,1024]{1,0:T(8,128)(2,1)} %copy-done.68, ...), custom_call_target="tpu_custom_call" | custom-call | flops 4294967 | bytes 23601 | tf_op jit(solution)/shard_map/feed_forward_back/pallas_call | solution.py:64
  233.8 1.5 collective-permute-start.31
  237.4 1.6 collective-permute-start.35
  239.6 10.3 %w_up_grad.1 = (f32[2,512,1024]{2,1,0:T(8,128)}, bf16[2,512,1024]{2,1,0:T(8,128)(2,1)}) custom-call(s32[1]{0:T(128)} %bitcast.2.refs_0_, bf16[256,1024]{1,0:T(8,128)(2,1)} %copy-done.5, bf16[256,1024]{1,0:T(8,128)(2,1)} %copy-done.61, bf16[256,1024]{1,0:T(8,128)(2,1)} %copy-done.6, bf16[256,1024]{1,0:T(8,128)(2,1)} %copy-done.62, ...), custom_call_target="tpu_custom_call" | custom-call | flops 4294967 | bytes 12582 | tf_op jit(solution)/shard_map/w_up_grad/pallas_call | solution.py:64
  250.4 1.6 copy-done.23
  252.0 1.6 first_norm_back.3
  255.1 26.3 %attention_backward.2 = (bf16[512,512]{1,0:T(8,128)(2,1)}, f32[512,1024]{1,0:T(8,128)}, bf16[512,1024]{1,0:T(8,128)(2,1)}, f32[2,512]{1,0:T(2,128)}) custom-call(bf16[512,768]{1,0:T(8,128)(2,1)} %get-tuple-element.131.refs_0_, bf16[512,768]{1,0:T(8,128)(2,1)} %get-tuple-element.132.refs_1_, bf16[512,1024]{1,0:T(8,128)(2,1)} %collective-permute-done.11.refs_2_, ...), custom_call_target="tpu_custom_call" | custom-call | flops 21474836480 | bytes 11542 | tf_op jit(solution)/shard_map/attention_backward/pallas_call | solution.py:47
  282.2 4.4 %w_out_grad.1 = (f32[1024,256]{1,0:T(8,128)}, bf16[1024,256]{1,0:T(8,128)(2,1)}) custom-call(s32[1]{0:T(128)} %bitcast.2.refs_0_, bf16[256,1024]{1,0:T(8,128)(2,1)} %copy-done.26, bf16[256,1024]{1,0:T(8,128)(2,1)} %collective-permute-done.31.refs_5_.refs_2_, bf16[256,1024]{1,0:T(8,128)(2,1)} %get-tuple-element.182.refs_3_.refs_4_, ...), custom_call_target="tpu_custom_call" | custom-call | flops 1073741 | bytes 4718 | tf_op jit(solution)/shard_map/w_out_grad/pallas_call | solution.py:64
  286.6 1.9 fold.15
  289.9 26.6 %attention_backward.3 = (bf16[512,512]{1,0:T(8,128)(2,1)}, f32[512,1024]{1,0:T(8,128)}, bf16[512,1024]{1,0:T(8,128)(2,1)}, f32[2,512]{1,0:T(2,128)}) custom-call(bf16[512,768]{1,0:T(8,128)(2,1)} %get-tuple-element.138.refs_0_, bf16[512,768]{1,0:T(8,128)(2,1)} %get-tuple-element.139.refs_1_, bf16[512,1024]{1,0:T(8,128)(2,1)} %collective-permute-done.21.refs_2_, ...), custom_call_target="tpu_custom_call" | custom-call | flops 21474836480 | bytes 11542 | tf_op jit(solution)/shard_map/attention_backward/pallas_call | solution.py:47
  318.9 1.6 collective-permute-start.45
  320.5 2.2 copy-done.13
  325.4 4.4 %w_query_grad.1 = (f32[1024,256]{1,0:T(8,128)}, bf16[1024,256]{1,0:T(8,128)(2,1)}) custom-call(s32[1]{0:T(128)} %bitcast.2.refs_0_, bf16[256,1024]{1,0:T(8,128)(2,1)} %get-tuple-element.285.refs_0_.refs_1_, bf16[256,1024]{1,0:T(8,128)(2,1)} %get-tuple-element.283.refs_1_.refs_2_, bf16[256,1024]{1,0:T(8,128)(2,1)} %get-tuple-element.286.refs_0_.refs_3_, ...), custom_call_target="tpu_custom_call" | custom-call | flops 1073741 | bytes 5767 | tf_op jit(solution)/shard_map/w_query_grad/pallas_call | solution.py:64
  329.8 2.1 pad_maximum_fusion.3
  332.6 1.5 collective-permute-start.40
  334.1 6.3 %project_back.2 = (bf16[512,512]{1,0:T(8,128)(2,1)}, bf16[512,512]{1,0:T(8,128)(2,1)}, f32[256,1024]{1,0:T(8,128)}, bf16[256,1024]{1,0:T(8,128)(2,1)}) custom-call(bf16[512,512]{1,0:T(8,128)(2,1)} %get-tuple-element.176.refs_5_.refs_7_.refs_0_, f32[512,1024]{1,0:T(8,128)} %get-tuple-element.177.refs_1_, ...), custom_call_target="tpu_custom_call" | custom-call | flops 1610612 | bytes 10485 | tf_op jit(solution)/shard_map/project_back/pallas_call | solution.py:47
  344.8 6.4 %project_back.3 = (bf16[512,512]{1,0:T(8,128)(2,1)}, bf16[512,512]{1,0:T(8,128)(2,1)}, f32[256,1024]{1,0:T(8,128)}, bf16[256,1024]{1,0:T(8,128)(2,1)}) custom-call(bf16[512,512]{1,0:T(8,128)(2,1)} %get-tuple-element.191.refs_6_.refs_8_.refs_0_, f32[512,1024]{1,0:T(8,128)} %get-tuple-element.207.refs_1_, bf16[512,1024]{1,0:T(8,128)(2,1)} %collective-permute-done.39.refs_2_, ...), custom_call_target="tpu_custom_call" | custom-call | flops 1610612 | bytes 10485 | tf_op jit(solution)/shard_map/project_back/pallas_call | solution.py:47
  351.1 1.5 collective-permute-start.41
  354.8 1.5 collective-permute-start.48
  361.6 9.6 %w_key_value_grad.1 = (f32[1024,256]{1,0:T(8,128)}, bf16[1024,256]{1,0:T(8,128)(2,1)}, f32[1024,256]{1,0:T(8,128)}, bf16[1024,256]{1,0:T(8,128)(2,1)}) custom-call(s32[1]{0:T(128)} %bitcast.2.refs_0_, bf16[256,1024]{1,0:T(8,128)(2,1)} %get-tuple-element.285.refs_0_.refs_1_, bf16[256,1024]{1,0:T(8,128)(2,1)} %get-tuple-element.283.refs_1_.refs_2_, ...), custom_call_target="tpu_custom_call" | custom-call | flops 2147483 | bytes 7340 | tf_op jit(solution)/shard_map/w_key_value_grad/pallas_call | solution.py:64
  373.1 1.5 collective-permute-start.58
  374.9 17.5 %collective-permute-done.48.refs_3_.refs_1_ = bf16[2,128,1024]{2,1,0:T(8,128)(2,1)S(1)} collective-permute-done((bf16[2,128,1024]{2,1,0:T(8,128)(2,1)}, bf16[2,128,1024]{2,1,0:T(8,128)(2,1)S(1)}, u32[]{:S(2)}, u32[]{:S(2)}) %collective-permute-start.48) | collective-permute-done | bytes 524320 | tf_op jit(solution)/shard_map/ppermute | solution.py:92
  394.3 1.6 collective-permute-start.52
  397.7 5.4 %collective-permute-done.51.refs_1_ = bf16[1,512,256]{2,1,0:T(8,128)(2,1)S(1)} collective-permute-done((bf16[1,512,256]{2,1,0:T(8,128)(2,1)S(1)}, bf16[1,512,256]{2,1,0:T(8,128)(2,1)S(1)}, u32[]{:S(2)}, u32[]{:S(2)}) %collective-permute-start.51) | collective-permute-done | bytes 262176 | tf_op jit(solution)/shard_map/ppermute | solution.py:92
  403.1 1.9 collective-permute-start.61
  406.2 1.9 collective-permute-done.50.refs_1_
  408.4 2.4 collective-permute-start.54
  414.3 2.0 collective-permute-done.62.refs_1_
  417.9 2.1 collective-permute-start.55
  422.5 2.9 collective-permute-done.55.refs_1_
  426.8 1.8 fusion.4
  (353 shorter events, 79.9 us)
Async XLA Ops:
  4.0 16.2 %collective-permute-start.1 = (bf16[128,1024]{1,0:T(8,128)(2,1)}, bf16[128,1024]{1,0:T(8,128)(2,1)S(1)}, u32[]{:S(2)}, u32[]{:S(2)}) collective-permute-start(bf16[128,1024]{1,0:T(8,128)(2,1)} %pack_attention.1), channel_id=1, source_target_pairs={{0,16},{4,20},{8,24},{12,28},{16,0},{20,4},{24,8},{28,12},{1,17},{... | collective-permute-start | bytes 786440 | tf_op jit(solution)/shard_map/ppermute | solution.py:92
  21.3 44.7 %copy-start.65 = (bf16[256,1024]{1,0:T(8,128)(2,1)}, bf16[256,1024]{1,0:T(8,128)(2,1)S(1)}, u32[]{:S(2)}) copy-start(bf16[256,1024]{1,0:T(8,128)(2,1)S(1)} %pad_maximum_fusion.4.refs_1_) | copy-start | bytes 1572868
  21.3 22.1 %collective-permute-start.2 = (bf16[256,1024]{1,0:T(8,128)(2,1)S(1)}, bf16[256,1024]{1,0:T(8,128)(2,1)S(1)}, u32[]{:S(2)}, u32[]{:S(2)}) collective-permute-start(bf16[256,1024]{1,0:T(8,128)(2,1)S(1)} %pad_maximum_fusion.4.refs_1_), channel_id=1, source_target_pairs={{0,8},{4,12},{8,0},{12,4},{16,24},{20,28},{24,16},{28,20},{1,9},{5... | collective-permute-start | bytes 1572872 | tf_op jit(solution)/shard_map/ppermute | solution.py:92
  24.0 26.6 %collective-permute-start.10 = (bf16[128,2048]{1,0:T(8,128)(2,1)}, bf16[128,2048]{1,0:T(8,128)(2,1)S(1)}, u32[]{:S(2)}, u32[]{:S(2)}) collective-permute-start(bf16[128,2048]{1,0:T(8,128)(2,1)} %pack_feed.1), channel_id=1, source_target_pairs={{0,16},{4,20},{8,24},{12,28},{16,0},{20,4},{24,8},{28,12},{1,17},{... | collective-permute-start | bytes 1572872 | tf_op jit(solution)/shard_map/ppermute | solution.py:92
  27.3 26.9 %collective-permute-start.3 = (bf16[256,1024]{1,0:T(8,128)(2,1)S(1)}, bf16[256,1024]{1,0:T(8,128)(2,1)}, u32[]{:S(2)}, u32[]{:S(2)}) collective-permute-start(bf16[256,1024]{1,0:T(8,128)(2,1)S(1)} %pad_maximum_fusion.4.refs_1_), channel_id=1, source_target_pairs={{0,4},{4,0},{8,12},{12,8},{16,20},{20,16},{24,28},{28,24},{1,5},{5... | collective-permute-start | bytes 1572872 | tf_op jit(solution)/shard_map/ppermute | solution.py:92
  28.8 37.7 %collective-permute-start = (bf16[2,256,1024]{2,1,0:T(8,128)(2,1)S(1)}, bf16[2,256,1024]{2,1,0:T(8,128)(2,1)}, u32[]{:S(2)}, u32[]{:S(2)}) collective-permute-start(bf16[2,256,1024]{2,1,0:T(8,128)(2,1)S(1)} %copy-done.69), channel_id=1, source_target_pairs={{0,2},{1,3},{2,0},{3,1},{4,6},{5,7},{6,4},{7,5},{8,10},{9,11},{10,... | collective-permute-start | bytes 3145736 | tf_op jit(solution)/shard_map/ppermute | solution.py:87
  30.3 1.2 collective-permute-start.9
  31.6 23.2 %collective-permute-start.5 = (bf16[256,1024]{1,0:T(8,128)(2,1)S(1)}, bf16[256,1024]{1,0:T(8,128)(2,1)S(1)}, u32[]{:S(2)}, u32[]{:S(2)}) collective-permute-start(bf16[256,1024]{1,0:T(8,128)(2,1)S(1)} %pad_maximum_fusion.4.refs_1_), channel_id=1, source_target_pairs={{0,1},{1,0},{2,3},{3,2},{4,5},{5,4},{6,7},{7,6},{8,9},{9,8},{10,11... | collective-permute-start | bytes 1572872 | tf_op jit(solution)/shard_map/ppermute | solution.py:87
  43.4 21.0 %collective-permute-start.16 = (bf16[128,2048]{1,0:T(8,128)(2,1)}, bf16[128,2048]{1,0:T(8,128)(2,1)}, u32[]{:S(2)}, u32[]{:S(2)}) collective-permute-start(bf16[128,2048]{1,0:T(8,128)(2,1)} %pack_feed.1), channel_id=1, source_target_pairs={{0,2},{1,3},{2,0},{3,1},{4,6},{5,7},{6,4},{7,5},{8,10},{9,11},{10,... | collective-permute-start | bytes 1572872 | tf_op jit(solution)/shard_map/ppermute | solution.py:87
  50.6 13.8 %collective-permute-start.4 = (bf16[256,1024]{1,0:T(8,128)(2,1)S(1)}, bf16[256,1024]{1,0:T(8,128)(2,1)}, u32[]{:S(2)}, u32[]{:S(2)}) collective-permute-start(bf16[256,1024]{1,0:T(8,128)(2,1)S(1)} %collective-permute-done.2.refs_2_), channel_id=1, source_target_pairs={{0,4},{4,0},{8,12},{12,8},{16,20},{20,16},{24,28},{28,24},{1,5},{5... | collective-permute-start | bytes 1572872 | tf_op jit(solution)/shard_map/ppermute | solution.py:92
  54.2 34.5 %collective-permute-start.12 = (bf16[256,2048]{1,0:T(8,128)(2,1)}, bf16[256,2048]{1,0:T(8,128)(2,1)}, u32[]{:S(2)}, u32[]{:S(2)}) collective-permute-start(bf16[256,2048]{1,0:T(8,128)(2,1)} %pad_maximum_fusion.refs_1_), channel_id=1, source_target_pairs={{0,8},{4,12},{8,0},{12,4},{16,24},{20,28},{24,16},{28,20},{1,9},{5... | collective-permute-start | bytes 3145736 | tf_op jit(solution)/shard_map/ppermute | solution.py:92
  54.8 17.2 %collective-permute-start.6 = (bf16[256,1024]{1,0:T(8,128)(2,1)S(1)}, bf16[256,1024]{1,0:T(8,128)(2,1)S(1)}, u32[]{:S(2)}, u32[]{:S(2)}) collective-permute-start(bf16[256,1024]{1,0:T(8,128)(2,1)S(1)} %collective-permute-done.2.refs_2_), channel_id=1, source_target_pairs={{0,1},{1,0},{2,3},{3,2},{4,5},{5,4},{6,7},{7,6},{8,9},{9,8},{10,11... | collective-permute-start | bytes 1572872 | tf_op jit(solution)/shard_map/ppermute | solution.py:87
  64.4 7.6 %collective-permute-start.7 = (bf16[256,1024]{1,0:T(8,128)(2,1)}, bf16[256,1024]{1,0:T(8,128)(2,1)S(1)}, u32[]{:S(2)}, u32[]{:S(2)}) collective-permute-start(bf16[256,1024]{1,0:T(8,128)(2,1)} %collective-permute-done.3.refs_3_), channel_id=1, source_target_pairs={{0,1},{1,0},{2,3},{3,2},{4,5},{5,4},{6,7},{7,6},{8,9},{9,8},{10,11... | collective-permute-start | bytes 1572872 | tf_op jit(solution)/shard_map/ppermute | solution.py:87
  64.4 7.6 %collective-permute-start.8 = (bf16[256,1024]{1,0:T(8,128)(2,1)}, bf16[256,1024]{1,0:T(8,128)(2,1)S(1)}, u32[]{:S(2)}, u32[]{:S(2)}) collective-permute-start(bf16[256,1024]{1,0:T(8,128)(2,1)} %collective-permute-done.4.refs_4_), channel_id=1, source_target_pairs={{0,1},{1,0},{2,3},{3,2},{4,5},{5,4},{6,7},{7,6},{8,9},{9,8},{10,11... | collective-permute-start | bytes 1572872 | tf_op jit(solution)/shard_map/ppermute | solution.py:87
  66.5 26.2 %collective-permute-start.17 = (bf16[128,2048]{1,0:T(8,128)(2,1)}, bf16[128,2048]{1,0:T(8,128)(2,1)S(1)}, u32[]{:S(2)}, u32[]{:S(2)}) collective-permute-start(bf16[128,2048]{1,0:T(8,128)(2,1)} %collective-permute-done.16.refs_6_), channel_id=1, source_target_pairs={{0,16},{4,20},{8,24},{12,28},{16,0},{20,4},{24,8},{28,12},{1,17},{... | collective-permute-start | bytes 1572872 | tf_op jit(solution)/shard_map/ppermute | solution.py:92
  82.3 15.5 %collective-permute-start.11 = (bf16[512,1024]{1,0:T(8,128)(2,1)}, bf16[512,1024]{1,0:T(8,128)(2,1)}, u32[]{:S(2)}, u32[]{:S(2)}) collective-permute-start(bf16[512,1024]{1,0:T(8,128)(2,1)} %get-tuple-element.133.refs_7_), channel_id=1, source_target_pairs={{0,1},{1,0},{2,3},{3,2},{4,5},{5,4},{6,7},{7,6},{8,9},{9,8},{10,11... | collective-permute-start | bytes 3145736 | tf_op jit(solution)/shard_map/ppermute | solution.py:87
  82.3 29.9 %collective-permute-start.22 = (bf16[256,2048]{1,0:T(8,128)(2,1)}, bf16[256,2048]{1,0:T(8,128)(2,1)S(1)}, u32[]{:S(2)}, u32[]{:S(2)}) collective-permute-start(bf16[256,2048]{1,0:T(8,128)(2,1)} %pad_maximum_fusion.refs_1_), channel_id=1, source_target_pairs={{0,4},{4,0},{8,12},{12,8},{16,20},{20,16},{24,28},{28,24},{1,5},{5... | collective-permute-start | bytes 3145736 | tf_op jit(solution)/shard_map/ppermute | solution.py:92
  88.5 23.8 %collective-permute-start.21 = (bf16[512,1024]{1,0:T(8,128)(2,1)}, bf16[512,1024]{1,0:T(8,128)(2,1)}, u32[]{:S(2)}, u32[]{:S(2)}) collective-permute-start(bf16[512,1024]{1,0:T(8,128)(2,1)} %get-tuple-element.140), channel_id=1, source_target_pairs={{0,1},{1,0},{2,3},{3,2},{4,5},{5,4},{6,7},{7,6},{8,9},{9,8},{10,11... | collective-permute-start | bytes 3145736 | tf_op jit(solution)/shard_map/ppermute | solution.py:87
  88.7 42.3 %collective-permute-start.14 = (bf16[256,2048]{1,0:T(8,128)(2,1)}, bf16[256,2048]{1,0:T(8,128)(2,1)S(1)}, u32[]{:S(2)}, u32[]{:S(2)}) collective-permute-start(bf16[256,2048]{1,0:T(8,128)(2,1)} %collective-permute-done.12.refs_6_.refs_2_), channel_id=1, source_target_pairs={{0,4},{4,0},{8,12},{12,8},{16,20},{20,16},{24,28},{28,24},{1,5},{5... | collective-permute-start | bytes 3145736 | tf_op jit(solution)/shard_map/ppermute | solution.py:92
  93.6 44.2 %collective-permute-start.18 = (bf16[256,2048]{1,0:T(8,128)(2,1)}, bf16[256,2048]{1,0:T(8,128)(2,1)}, u32[]{:S(2)}, u32[]{:S(2)}) collective-permute-start(bf16[256,2048]{1,0:T(8,128)(2,1)} %constant_dynamic-update-slice_fusion.refs_1_), channel_id=1, source_target_pairs={{0,8},{4,12},{8,0},{12,4},{16,24},{20,28},{24,16},{28,20},{1,9},{5... | collective-permute-start | bytes 3145736 | tf_op jit(solution)/shard_map/ppermute | solution.py:92
  110.7 21.8 %collective-permute-start.13 = (bf16[256,1024]{1,0:T(8,128)(2,1)}, bf16[256,1024]{1,0:T(8,128)(2,1)S(1)}, u32[]{:S(2)}, u32[]{:S(2)}) collective-permute-start(bf16[256,1024]{1,0:T(8,128)(2,1)} %get-tuple-element.135), channel_id=1, source_target_pairs={{0,2},{1,3},{2,0},{3,1},{4,6},{5,7},{6,4},{7,5},{8,10},{9,11},{10,... | collective-permute-start | bytes 1572872 | tf_op jit(solution)/shard_map/ppermute | solution.py:87
  126.0 15.1 %collective-permute-start.23 = (bf16[256,1024]{1,0:T(8,128)(2,1)}, bf16[256,1024]{1,0:T(8,128)(2,1)S(1)}, u32[]{:S(2)}, u32[]{:S(2)}) collective-permute-start(bf16[256,1024]{1,0:T(8,128)(2,1)} %get-tuple-element.142), channel_id=1, source_target_pairs={{0,2},{1,3},{2,0},{3,1},{4,6},{5,7},{6,4},{7,5},{8,10},{9,11},{10,... | collective-permute-start | bytes 1572872 | tf_op jit(solution)/shard_map/ppermute | solution.py:87
  126.5 38.1 %collective-permute-start.19 = (bf16[256,2048]{1,0:T(8,128)(2,1)}, bf16[256,2048]{1,0:T(8,128)(2,1)}, u32[]{:S(2)}, u32[]{:S(2)}) collective-permute-start(bf16[256,2048]{1,0:T(8,128)(2,1)} %constant_dynamic-update-slice_fusion.refs_1_), channel_id=1, source_target_pairs={{0,4},{4,0},{8,12},{12,8},{16,20},{20,16},{24,28},{28,24},{1,5},{5... | collective-permute-start | bytes 3145736 | tf_op jit(solution)/shard_map/ppermute | solution.py:92
  131.0 33.7 %collective-permute-start.20 = (bf16[256,2048]{1,0:T(8,128)(2,1)S(1)}, bf16[256,2048]{1,0:T(8,128)(2,1)}, u32[]{:S(2)}, u32[]{:S(2)}) collective-permute-start(bf16[256,2048]{1,0:T(8,128)(2,1)S(1)} %collective-permute-done.14.refs_6_.refs_4_), channel_id=1, source_target_pairs={{0,2},{1,3},{2,0},{3,1},{4,6},{5,7},{6,4},{7,5},{8,10},{9,11},{10,... | collective-permute-start | bytes 3145736 | tf_op jit(solution)/shard_map/ppermute | solution.py:87
  133.1 12.3 %collective-permute-start.15 = (bf16[256,1024]{1,0:T(8,128)(2,1)S(1)}, bf16[256,1024]{1,0:T(8,128)(2,1)S(1)}, u32[]{:S(2)}, u32[]{:S(2)}) collective-permute-start(bf16[256,1024]{1,0:T(8,128)(2,1)S(1)} %get-tuple-element.137.refs_8_.refs_0_.refs_1_), channel_id=1, source_target_pairs={{0,1},{1,0},{2,3},{3,2},{4,5},{5,4},{6,7},{7,6},{8,9},{9,8},{10,11... | collective-permute-start | bytes 1572872 | tf_op jit(solution)/shard_map/ppermute | solution.py:87
  144.8 10.2 %collective-permute-start.24 = (bf16[256,1024]{1,0:T(8,128)(2,1)S(1)}, bf16[256,1024]{1,0:T(8,128)(2,1)S(1)}, u32[]{:S(2)}, u32[]{:S(2)}) collective-permute-start(bf16[256,1024]{1,0:T(8,128)(2,1)S(1)} %get-tuple-element.143.refs_0_.refs_3_), channel_id=1, source_target_pairs={{0,1},{1,0},{2,3},{3,2},{4,5},{5,4},{6,7},{7,6},{8,9},{9,8},{10,11... | collective-permute-start | bytes 1572872 | tf_op jit(solution)/shard_map/ppermute | solution.py:87
  144.8 24.4 %collective-permute-start.25 = (f32[1024]{0:T(1024)S(1)}, f32[1024]{0:T(1024)S(1)}, u32[]{:S(2)}, u32[]{:S(2)}) collective-permute-start(f32[1024]{0:T(1024)S(1)} %copy-done.81), channel_id=1, source_target_pairs={{0,2},{1,3},{2,0},{3,1},{4,6},{5,7},{6,4},{7,5},{8,10},{9,11},{10,... | collective-permute-start | bytes 12296 | tf_op jit(solution)/shard_map/ppermute | solution.py:87
  179.5 10.9 %collective-permute-start.26 = (bf16[256,1024]{1,0:T(8,128)(2,1)}, bf16[256,1024]{1,0:T(8,128)(2,1)S(1)}, u32[]{:S(2)}, u32[]{:S(2)}) collective-permute-start(bf16[256,1024]{1,0:T(8,128)(2,1)} %get-tuple-element.147), channel_id=1, source_target_pairs={{0,1},{1,0},{2,3},{3,2},{4,5},{5,4},{6,7},{7,6},{8,9},{9,8},{10,11... | collective-permute-start | bytes 1572872 | tf_op jit(solution)/shard_map/ppermute | solution.py:87
  189.9 2.7 collective-permute-start.27
  192.1 3.4 collective-permute-start.28
  195.4 12.8 %collective-permute-start.30 = (bf16[256,1024]{1,0:T(8,128)(2,1)S(1)}, bf16[256,1024]{1,0:T(8,128)(2,1)S(1)}, u32[]{:S(2)}, u32[]{:S(2)}) collective-permute-start(bf16[256,1024]{1,0:T(8,128)(2,1)S(1)} %get-tuple-element.160.refs_3_.refs_0_), channel_id=1, source_target_pairs={{0,1},{1,0},{2,3},{3,2},{4,5},{5,4},{6,7},{7,6},{8,9},{9,8},{10,11... | collective-permute-start | bytes 1572872 | tf_op jit(solution)/shard_map/ppermute | solution.py:87
  207.8 22.9 %collective-permute-start.29 = (bf16[256,1024]{1,0:T(8,128)(2,1)}, bf16[256,1024]{1,0:T(8,128)(2,1)S(1)}, u32[]{:S(2)}, u32[]{:S(2)}) collective-permute-start(bf16[256,1024]{1,0:T(8,128)(2,1)} %get-tuple-element.159), channel_id=1, source_target_pairs={{0,1},{1,0},{2,3},{3,2},{4,5},{5,4},{6,7},{7,6},{8,9},{9,8},{10,11... | collective-permute-start | bytes 1572872 | tf_op jit(solution)/shard_map/ppermute | solution.py:87
  230.4 19.9 %collective-permute-start.33 = (bf16[256,1024]{1,0:T(8,128)(2,1)}, bf16[256,1024]{1,0:T(8,128)(2,1)S(1)}, u32[]{:S(2)}, u32[]{:S(2)}) collective-permute-start(bf16[256,1024]{1,0:T(8,128)(2,1)} %get-tuple-element.181), channel_id=1, source_target_pairs={{0,1},{1,0},{2,3},{3,2},{4,5},{5,4},{6,7},{7,6},{8,9},{9,8},{10,11... | collective-permute-start | bytes 1572872 | tf_op jit(solution)/shard_map/ppermute | solution.py:87
  233.8 21.3 %collective-permute-start.31 = (bf16[256,1024]{1,0:T(8,128)(2,1)S(1)}, bf16[256,1024]{1,0:T(8,128)(2,1)}, u32[]{:S(2)}, u32[]{:S(2)}) collective-permute-start(bf16[256,1024]{1,0:T(8,128)(2,1)S(1)} %get-tuple-element.170.refs_9_.refs_4_.refs_1_), channel_id=1, source_target_pairs={{0,2},{1,3},{2,0},{3,1},{4,6},{5,7},{6,4},{7,5},{8,10},{9,11},{10,... | collective-permute-start | bytes 1572872 | tf_op jit(solution)/shard_map/ppermute | solution.py:87
  237.4 49.2 %collective-permute-start.35 = (bf16[2,512,1024]{2,1,0:T(8,128)(2,1)}, bf16[2,512,1024]{2,1,0:T(8,128)(2,1)}, u32[]{:S(2)}, u32[]{:S(2)}) collective-permute-start(bf16[2,512,1024]{2,1,0:T(8,128)(2,1)} %get-tuple-element.167.refs_8_), channel_id=1, source_target_pairs={{0,4},{4,0},{8,12},{12,8},{16,20},{20,16},{24,28},{28,24},{1,5},{5... | collective-permute-start | bytes 6291464 | tf_op jit(solution)/shard_map/ppermute | solution.py:92
  249.9 70.6 %collective-permute-start.37 = (bf16[2,512,1024]{2,1,0:T(8,128)(2,1)}, bf16[2,512,1024]{2,1,0:T(8,128)(2,1)S(1)}, u32[]{:S(2)}, u32[]{:S(2)}) collective-permute-start(bf16[2,512,1024]{2,1,0:T(8,128)(2,1)} %get-tuple-element.175.refs_8_.refs_5_), channel_id=1, source_target_pairs={{0,8},{4,12},{8,0},{12,4},{16,24},{20,28},{24,16},{28,20},{1,9},{5... | collective-permute-start | bytes 6291464 | tf_op jit(solution)/shard_map/ppermute | solution.py:92
  254.5 26.8 %collective-permute-start.34 = (bf16[256,1024]{1,0:T(8,128)(2,1)}, bf16[256,1024]{1,0:T(8,128)(2,1)S(1)}, u32[]{:S(2)}, u32[]{:S(2)}) collective-permute-start(bf16[256,1024]{1,0:T(8,128)(2,1)} %get-tuple-element.182.refs_3_.refs_4_), channel_id=1, source_target_pairs={{0,2},{1,3},{2,0},{3,1},{4,6},{5,7},{6,4},{7,5},{8,10},{9,11},{10,... | collective-permute-start | bytes 1572872 | tf_op jit(solution)/shard_map/ppermute | solution.py:87
  281.4 44.0 %collective-permute-start.32 = (bf16[512,1024]{1,0:T(8,128)(2,1)}, bf16[512,1024]{1,0:T(8,128)(2,1)}, u32[]{:S(2)}, u32[]{:S(2)}) collective-permute-start(bf16[512,1024]{1,0:T(8,128)(2,1)} %get-tuple-element.178), channel_id=1, source_target_pairs={{0,1},{1,0},{2,3},{3,2},{4,5},{5,4},{6,7},{7,6},{8,9},{9,8},{10,11... | collective-permute-start | bytes 3145736 | tf_op jit(solution)/shard_map/ppermute | solution.py:87
  318.3 6.5 %collective-permute-start.36 = (f32[96,128]{1,0:T(8,128)S(1)}, f32[96,128]{1,0:T(8,128)S(1)}, u32[]{:S(2)}, u32[]{:S(2)}) collective-permute-start(f32[96,128]{1,0:T(8,128)S(1)} %bitcast.108), channel_id=1, source_target_pairs={{0,1},{1,0},{2,3},{3,2},{4,5},{5,4},{6,7},{7,6},{8,9},{9,8},{10,11... | collective-permute-start | bytes 147464 | tf_op jit(solution)/shard_map/ppermute | solution.py:87
  318.8 23.4 %collective-permute-start.39 = (bf16[512,1024]{1,0:T(8,128)(2,1)}, bf16[512,1024]{1,0:T(8,128)(2,1)}, u32[]{:S(2)}, u32[]{:S(2)}) collective-permute-start(bf16[512,1024]{1,0:T(8,128)(2,1)} %get-tuple-element.208), channel_id=1, source_target_pairs={{0,1},{1,0},{2,3},{3,2},{4,5},{5,4},{6,7},{7,6},{8,9},{9,8},{10,11... | collective-permute-start | bytes 3145736 | tf_op jit(solution)/shard_map/ppermute | solution.py:87
  318.9 32.2 %collective-permute-start.45 = (bf16[2,256,1024]{2,1,0:T(8,128)(2,1)}, bf16[2,256,1024]{2,1,0:T(8,128)(2,1)S(1)}, u32[]{:S(2)}, u32[]{:S(2)}) collective-permute-start(bf16[2,256,1024]{2,1,0:T(8,128)(2,1)} %copy-done.60), channel_id=1, source_target_pairs={{0,8},{4,12},{8,0},{12,4},{16,24},{20,28},{24,16},{28,20},{1,9},{5... | collective-permute-start | bytes 3145736 | tf_op jit(solution)/shard_map/ppermute | solution.py:92
  331.9 24.5 %collective-permute-start.42 = (bf16[2,1024,256]{2,1,0:T(8,128)(2,1)}, bf16[2,1024,256]{2,1,0:T(8,128)(2,1)}, u32[]{:S(2)}, u32[]{:S(2)}) collective-permute-start(bf16[2,1024,256]{2,1,0:T(8,128)(2,1)} %pad_maximum_fusion.3), channel_id=1, source_target_pairs={{0,1},{1,0},{2,3},{3,2},{4,5},{5,4},{6,7},{7,6},{8,9},{9,8},{10,11... | collective-permute-start | bytes 3145736 | tf_op jit(solution)/shard_map/ppermute | solution.py:87
  332.1 28.3 %collective-permute-start.44 = (bf16[2,256,1024]{2,1,0:T(8,128)(2,1)}, bf16[2,256,1024]{2,1,0:T(8,128)(2,1)S(1)}, u32[]{:S(2)}, u32[]{:S(2)}) collective-permute-start(bf16[2,256,1024]{2,1,0:T(8,128)(2,1)} %get-tuple-element.219), channel_id=1, source_target_pairs={{0,4},{4,0},{8,12},{12,8},{16,20},{20,16},{24,28},{28,24},{1,5},{5... | collective-permute-start | bytes 3145736 | tf_op jit(solution)/shard_map/ppermute | solution.py:92
  332.6 7.9 %collective-permute-start.40 = (f32[96,128]{1,0:T(8,128)S(1)}, f32[96,128]{1,0:T(8,128)S(1)}, u32[]{:S(2)}, u32[]{:S(2)}) collective-permute-start(f32[96,128]{1,0:T(8,128)S(1)} %copy-done.50), channel_id=1, source_target_pairs={{0,2},{1,3},{2,0},{3,1},{4,6},{5,7},{6,4},{7,5},{8,10},{9,11},{10,... | collective-permute-start | bytes 147464 | tf_op jit(solution)/shard_map/ppermute | solution.py:87
  340.5 21.1 %collective-permute-start.38 = (bf16[256,1024]{1,0:T(8,128)(2,1)}, bf16[256,1024]{1,0:T(8,128)(2,1)}, u32[]{:S(2)}, u32[]{:S(2)}) collective-permute-start(bf16[256,1024]{1,0:T(8,128)(2,1)} %get-tuple-element.205), channel_id=1, source_target_pairs={{0,2},{1,3},{2,0},{3,1},{4,6},{5,7},{6,4},{7,5},{8,10},{9,11},{10,... | collective-permute-start | bytes 1572872 | tf_op jit(solution)/shard_map/ppermute | solution.py:87
  342.2 12.6 %collective-permute-start.46 = (f32[96,128]{1,0:T(8,128)S(1)}, f32[96,128]{1,0:T(8,128)S(1)}, u32[]{:S(2)}, u32[]{:S(2)}) collective-permute-start(f32[96,128]{1,0:T(8,128)S(1)} %plus.6.refs_5_.refs_0_), channel_id=1, source_target_pairs={{0,16},{4,20},{8,24},{12,28},{16,0},{20,4},{24,8},{28,12},{1,17},{... | collective-permute-start | bytes 147464 | tf_op jit(solution)/shard_map/ppermute | solution.py:92
  351.1 21.9 %collective-permute-start.41 = (bf16[256,1024]{1,0:T(8,128)(2,1)}, bf16[256,1024]{1,0:T(8,128)(2,1)S(1)}, u32[]{:S(2)}, u32[]{:S(2)}) collective-permute-start(bf16[256,1024]{1,0:T(8,128)(2,1)} %get-tuple-element.210), channel_id=1, source_target_pairs={{0,2},{1,3},{2,0},{3,1},{4,6},{5,7},{6,4},{7,5},{8,10},{9,11},{10,... | collective-permute-start | bytes 1572872 | tf_op jit(solution)/shard_map/ppermute | solution.py:87
  354.8 37.5 %collective-permute-start.48 = (bf16[2,128,1024]{2,1,0:T(8,128)(2,1)}, bf16[2,128,1024]{2,1,0:T(8,128)(2,1)S(1)}, u32[]{:S(2)}, u32[]{:S(2)}) collective-permute-start(bf16[2,128,1024]{2,1,0:T(8,128)(2,1)} %get-tuple-element.225), channel_id=1, source_target_pairs={{0,16},{4,20},{8,24},{12,28},{16,0},{20,4},{24,8},{28,12},{1,17},{... | collective-permute-start | bytes 1572872 | tf_op jit(solution)/shard_map/ppermute | solution.py:92
  358.8 33.8 %collective-permute-start.43 = (bf16[2,512,256]{2,1,0:T(8,128)(2,1)S(1)}, bf16[2,512,256]{2,1,0:T(8,128)(2,1)S(1)}, u32[]{:S(2)}, u32[]{:S(2)}) collective-permute-start(bf16[2,512,256]{2,1,0:T(8,128)(2,1)S(1)} %get-tuple-element.214), channel_id=1, source_target_pairs={{0,4},{4,0},{8,12},{12,8},{16,20},{20,16},{24,28},{28,24},{1,5},{5... | collective-permute-start | bytes 1572872 | tf_op jit(solution)/shard_map/ppermute | solution.py:92
  371.2 21.2 %collective-permute-start.47 = (bf16[1024,256]{1,0:T(8,128)(2,1)}, bf16[1024,256]{1,0:T(8,128)(2,1)S(1)}, u32[]{:S(2)}, u32[]{:S(2)}) collective-permute-start(bf16[1024,256]{1,0:T(8,128)(2,1)} %get-tuple-element.224), channel_id=1, source_target_pairs={{0,1},{1,0},{2,3},{3,2},{4,5},{5,4},{6,7},{7,6},{8,9},{9,8},{10,11... | collective-permute-start | bytes 1572872 | tf_op jit(solution)/shard_map/ppermute | solution.py:87
  371.2 21.3 %collective-permute-start.49 = (bf16[1024,256]{1,0:T(8,128)(2,1)}, bf16[1024,256]{1,0:T(8,128)(2,1)S(1)}, u32[]{:S(2)}, u32[]{:S(2)}) collective-permute-start(bf16[1024,256]{1,0:T(8,128)(2,1)} %get-tuple-element.228), channel_id=1, source_target_pairs={{0,1},{1,0},{2,3},{3,2},{4,5},{5,4},{6,7},{7,6},{8,9},{9,8},{10,11... | collective-permute-start | bytes 1572872 | tf_op jit(solution)/shard_map/ppermute | solution.py:87
  373.1 37.7 %collective-permute-start.58 = (bf16[2,128,1024]{2,1,0:T(8,128)(2,1)S(1)}, bf16[2,128,1024]{2,1,0:T(8,128)(2,1)S(1)}, u32[]{:S(2)}, u32[]{:S(2)}) collective-permute-start(bf16[2,128,1024]{2,1,0:T(8,128)(2,1)S(1)} %get-tuple-element.244), channel_id=1, source_target_pairs={{0,16},{4,20},{8,24},{12,28},{16,0},{20,4},{24,8},{28,12},{1,17},{... | collective-permute-start | bytes 1572872 | tf_op jit(solution)/shard_map/ppermute | solution.py:92
  393.7 14.4 %collective-permute-start.50 = (bf16[2,256,256]{2,1,0:T(8,128)(2,1)S(1)}, bf16[2,256,256]{2,1,0:T(8,128)(2,1)S(1)}, u32[]{:S(2)}, u32[]{:S(2)}) collective-permute-start(bf16[2,256,256]{2,1,0:T(8,128)(2,1)S(1)} %get-tuple-element.231), channel_id=1, source_target_pairs={{0,8},{4,12},{8,0},{12,4},{16,24},{20,28},{24,16},{28,20},{1,9},{5... | collective-permute-start | bytes 786440 | tf_op jit(solution)/shard_map/ppermute | solution.py:92
  393.8 9.3 %collective-permute-start.51 = (bf16[1,512,256]{2,1,0:T(8,128)(2,1)S(1)}, bf16[1,512,256]{2,1,0:T(8,128)(2,1)S(1)}, u32[]{:S(2)}, u32[]{:S(2)}) collective-permute-start(bf16[1,512,256]{2,1,0:T(8,128)(2,1)S(1)} %get-tuple-element.232), channel_id=1, source_target_pairs={{0,4},{4,0},{8,12},{12,8},{16,20},{20,16},{24,28},{28,24},{1,5},{5... | collective-permute-start | bytes 786440 | tf_op jit(solution)/shard_map/ppermute | solution.py:92
  394.3 11.9 %collective-permute-start.52 = (bf16[1,512,256]{2,1,0:T(8,128)(2,1)S(1)}, bf16[1,512,256]{2,1,0:T(8,128)(2,1)S(1)}, u32[]{:S(2)}, u32[]{:S(2)}) collective-permute-start(bf16[1,512,256]{2,1,0:T(8,128)(2,1)S(1)} %get-tuple-element.234), channel_id=1, source_target_pairs={{0,4},{4,0},{8,12},{12,8},{16,20},{20,16},{24,28},{28,24},{1,5},{5... | collective-permute-start | bytes 786440 | tf_op jit(solution)/shard_map/ppermute | solution.py:92
  396.0 16.2 %collective-permute-start.60 = (bf16[128,1024]{1,0:T(8,128)(2,1)S(1)}, bf16[128,1024]{1,0:T(8,128)(2,1)S(1)}, u32[]{:S(2)}, u32[]{:S(2)}) collective-permute-start(bf16[128,1024]{1,0:T(8,128)(2,1)S(1)} %fusion.6), channel_id=1, source_target_pairs={{0,2},{1,3},{2,0},{3,1},{4,6},{5,7},{6,4},{7,5},{8,10},{9,11},{10,... | collective-permute-start | bytes 786440 | tf_op jit(solution)/shard_map/ppermute | solution.py:87
  403.1 8.6 %collective-permute-start.61 = (f32[96,128]{1,0:T(8,128)S(1)}, f32[96,128]{1,0:T(8,128)S(1)}, u32[]{:S(2)}, u32[]{:S(2)}) collective-permute-start(f32[96,128]{1,0:T(8,128)S(1)} %copy-done.48), channel_id=1, source_target_pairs={{0,8},{4,12},{8,0},{12,4},{16,24},{20,28},{24,16},{28,20},{1,9},{5... | collective-permute-start | bytes 147464 | tf_op jit(solution)/shard_map/ppermute | solution.py:92
  408.2 12.8 %collective-permute-start.53 = (bf16[2,128,256]{2,1,0:T(8,128)(2,1)S(1)}, bf16[2,128,256]{2,1,0:T(8,128)(2,1)S(1)}, u32[]{:S(2)}, u32[]{:S(2)}) collective-permute-start(bf16[2,128,256]{2,1,0:T(8,128)(2,1)S(1)} %get-tuple-element.237), channel_id=1, source_target_pairs={{0,16},{4,20},{8,24},{12,28},{16,0},{20,4},{24,8},{28,12},{1,17},{... | collective-permute-start | bytes 393224 | tf_op jit(solution)/shard_map/ppermute | solution.py:92
  408.4 9.5 %collective-permute-start.54 = (bf16[1,256,256]{2,1,0:T(8,128)(2,1)S(1)}, bf16[1,256,256]{2,1,0:T(8,128)(2,1)S(1)}, u32[]{:S(2)}, u32[]{:S(2)}) collective-permute-start(bf16[1,256,256]{2,1,0:T(8,128)(2,1)S(1)} %get-tuple-element.238), channel_id=1, source_target_pairs={{0,8},{4,12},{8,0},{12,4},{16,24},{20,28},{24,16},{28,20},{1,9},{5... | collective-permute-start | bytes 393224 | tf_op jit(solution)/shard_map/ppermute | solution.py:92
  410.8 9.6 %collective-permute-start.56 = (bf16[1,256,256]{2,1,0:T(8,128)(2,1)S(1)}, bf16[1,256,256]{2,1,0:T(8,128)(2,1)S(1)}, u32[]{:S(2)}, u32[]{:S(2)}) collective-permute-start(bf16[1,256,256]{2,1,0:T(8,128)(2,1)S(1)} %get-tuple-element.241), channel_id=1, source_target_pairs={{0,8},{4,12},{8,0},{12,4},{16,24},{20,28},{24,16},{28,20},{1,9},{5... | collective-permute-start | bytes 393224 | tf_op jit(solution)/shard_map/ppermute | solution.py:92
  411.7 15.1 %collective-permute-start.59 = (bf16[128,1024]{1,0:T(8,128)(2,1)}, bf16[128,1024]{1,0:T(8,128)(2,1)}, u32[]{:S(2)}, u32[]{:S(2)}) collective-permute-start(bf16[128,1024]{1,0:T(8,128)(2,1)} %fusion.5), channel_id=1, source_target_pairs={{0,2},{1,3},{2,0},{3,1},{4,6},{5,7},{6,4},{7,5},{8,10},{9,11},{10,... | collective-permute-start | bytes 786440 | tf_op jit(solution)/shard_map/ppermute | solution.py:87
  412.2 4.2 collective-permute-start.62
  417.9 7.5 %collective-permute-start.55 = (bf16[1,128,256]{2,1,0:T(8,128)(2,1)S(1)}, bf16[1,128,256]{2,1,0:T(8,128)(2,1)S(1)}, u32[]{:S(2)}, u32[]{:S(2)}) collective-permute-start(bf16[1,128,256]{2,1,0:T(8,128)(2,1)S(1)} %get-tuple-element.240), channel_id=1, source_target_pairs={{0,16},{4,20},{8,24},{12,28},{16,0},{20,4},{24,8},{28,12},{1,17},{... | collective-permute-start | bytes 196616 | tf_op jit(solution)/shard_map/ppermute | solution.py:92
  420.5 5.7 %collective-permute-start.57 = (bf16[1,128,256]{2,1,0:T(8,128)(2,1)S(1)}, bf16[1,128,256]{2,1,0:T(8,128)(2,1)S(1)}, u32[]{:S(2)}, u32[]{:S(2)}) collective-permute-start(bf16[1,128,256]{2,1,0:T(8,128)(2,1)S(1)} %get-tuple-element.243), channel_id=1, source_target_pairs={{0,16},{4,20},{8,24},{12,28},{16,0},{20,4},{24,8},{28,12},{1,17},{... | collective-permute-start | bytes 196616 | tf_op jit(solution)/shard_map/ppermute | solution.py:92
  (89 other events, 657.5 us)
